TPU v7x, 32 devices: a whole 2x2x4 slice. The times are simulated.
32 devices in a mesh: groups: 2 (over y), seq: 4 (over z), batch: 2 (over x), tp: 2 (over core).
Axes of the slice: x: 2, y: 2, z: 4, core: 2. Of those that a mesh axis runs over, the one named last changes fastest.
Arguments:
- tokens: bfloat16 [4, 1024, 7168], P(('groups', 'batch'), 'seq', 'tp'), parts along dimension 0, may hold values from -24 to 24
- frozen_qkv_matrix: bfloat16 [768, 7168], P('seq', 'tp'), as said below
- adapter_down_weight: bfloat16 [64, 64, 2, 3584], P(None, None, 'tp', ('seq', 'batch')), may hold values from -0.0625 to 0.0625
- adapter_up_weight: bfloat16 [64, 32, 640], P(None, None, ('seq', 'batch')), may hold values from -0.5 to 0.5
- adapter_bank_row: int32 [64], replicated, may hold values from 0 to 63, each once
- document_lengths: int32 [4, 3], P('groups'), parts along dimension 0, may hold values from 1 to 512, 1024 in all within a row
- document_adapter: int32 [4, 3], P('groups'), parts along dimension 0, may hold values from 0 to 63
- output_gradient: bfloat16 [4, 1024, 512], P(('groups', 'batch'), ('seq', 'tp')), parts along dimension 0, may hold values from -6 to 6
Outputs:
- attn_out: bfloat16 [4, 1024, 512], P(('groups', 'batch'), ('seq', 'tp')), parts along dimension 0
- token_grad: bfloat16 [4, 1024, 7168], P(('groups', 'batch'), 'seq', 'tp'), parts along dimension 0
- down_grad: float32 [128, 64, 2, 3584], P('groups', None, 'tp', ('seq', 'batch')), parts along dimension 0
- up_grad: float32 [128, 32, 640], P('groups', None, ('seq', 'batch')), parts along dimension 0
There are 2 independent parts, one for each index of `groups`. A program takes and returns all parts, laid end to end along the dimension named above; an argument that names none is the same for every part. Nothing has to cross between parts.
Inputs may be any that keep to these rules, and one draw needn't show every extreme that they name: Entries of frozen_qkv_matrix are at most 18 / sqrt(7168) in magnitude.
All inputs are finite; a program needn't handle non-finite values.
Results may differ from a plain program's by a relative error of at most 0.0075.
The roundings to bfloat16 on the way count: a program that leaves them out, or rounds other values in their place, can miss the bound.
Values may be sent and summed in bfloat16 or wider, within the bound.
No kernel may reach another device: no remote copies, remote signals or barrier semaphores. Data moves between devices by JAX's collectives and lax.ppermute only.
A program may use at most 128 MiB of HBM per device.

v0:
```python
import jax
import jax.numpy as jnp
from jax import lax
from jax.sharding import PartitionSpec as P

QHEADS = 4
HEAD_WIDTH = 128
ADAPTER_RANK = 32


adapter_scale = 2.0
rope_base = 5000000.0
start_floor = -1e30


def from_behind(value, axis, steps):
    count = lax.axis_size(axis)
    pairs = [(source, (source + steps) % count) for source in range(count)]
    return lax.ppermute(value, axis, pairs)


def segment_info(lengths, positions):
    segment_ends = jnp.cumsum(lengths)
    starts = segment_ends - lengths
    crossed = positions[:, None] >= segment_ends[None, :-1]
    segment = jnp.sum(crossed.astype(jnp.int32), axis=1)
    member = segment[:, None] == jnp.arange(lengths.shape[0], dtype=jnp.int32)[None, :]
    inside = positions - jnp.sum(jnp.where(member, starts[None, :], 0), axis=1)
    return (segment, member, inside)


def rope_tables(inside, head_width):
    exponent = jnp.arange(head_width // 2, dtype=jnp.float32) * (2.0 / head_width)
    inverse = jnp.power(jnp.float32(rope_base), -exponent)
    angles = inside.astype(jnp.float32)[:, None] * inverse[None, :]
    return (jnp.cos(angles), jnp.sin(angles))


def rotate(values, cosine_table, sine_table):
    half_dim = values.shape[-1] // 2
    front_half = values[..., :half_dim]
    back_half = values[..., half_dim:]
    cosine_wide = cosine_table[:, None, :]
    sine_wide = sine_table[:, None, :]
    return jnp.concatenate(
        [
            front_half * cosine_wide - back_half * sine_wide,
            back_half * cosine_wide + front_half * sine_wide,
        ],
        axis=-1,
    )


def unrotate(gradients, cosine_table, sine_table):
    half_dim = gradients.shape[-1] // 2
    front_half = gradients[..., :half_dim]
    back_half = gradients[..., half_dim:]
    cosine_wide = cosine_table[:, None, :]
    sine_wide = sine_table[:, None, :]
    return jnp.concatenate(
        [
            front_half * cosine_wide + back_half * sine_wide,
            back_half * cosine_wide - front_half * sine_wide,
        ],
        axis=-1,
    )


def lookup_rows(adapter_bank_row, document_adapter):
    matches = document_adapter[..., None] == jnp.arange(adapter_bank_row.shape[0], dtype=jnp.int32)
    return jnp.sum(jnp.where(matches, adapter_bank_row, 0), axis=-1)


def keep_same(carry):
    return carry


def allowed_block(query_pos, query_seg, key_seg, offset, key_block):
    block_pos = offset + jnp.arange(key_block, dtype=jnp.int32)
    block_seg = lax.dynamic_slice_in_dim(key_seg, offset, key_block)
    return (block_pos[None, :] <= query_pos[:, None]) & (block_seg[None, :] == query_seg[:, None])


def block_scores(queries, keys_all, allowed, offset, key_block):
    score_scale = queries.shape[2] ** (-0.5)
    key_rows = lax.dynamic_slice_in_dim(keys_all, offset, key_block)
    scores = (
        jnp.einsum("chd,kd->hck", queries, key_rows, preferred_element_type=jnp.float32)
        * score_scale
    )
    return jnp.where(allowed[None], scores, -jnp.inf)


def attend_rows(queries, query_pos, query_seg, keys_all, values_all, key_seg, key_block):
    row_total_count, head_count, head_width = queries.shape
    block_count = keys_all.shape[0] // key_block

    def gather_stats(block_id, stats):
        offset = block_id * key_block
        allowed = allowed_block(query_pos, query_seg, key_seg, offset, key_block)

        def gather_compute(stats):
            running_max, running_total = stats
            scores = block_scores(queries, keys_all, allowed, offset, key_block)
            new_max = jnp.maximum(running_max, jnp.max(scores, axis=2))
            new_total = running_total * jnp.exp(running_max - new_max) + jnp.sum(
                jnp.exp(scores - new_max[:, :, None]), axis=2
            )
            return (new_max, new_total)

        return lax.cond(jnp.any(allowed), gather_compute, keep_same, stats)

    start_stats = (
        jnp.full((head_count, row_total_count), start_floor, jnp.float32),
        jnp.zeros((head_count, row_total_count), jnp.float32),
    )
    row_max, row_total = lax.fori_loop(0, block_count, gather_stats, start_stats)

    def add_values(block_id, weighted):
        offset = block_id * key_block
        allowed = allowed_block(query_pos, query_seg, key_seg, offset, key_block)

        def add_compute(weighted):
            scores = block_scores(queries, keys_all, allowed, offset, key_block)
            block_low = (jnp.exp(scores - row_max[:, :, None]) / row_total[:, :, None]).astype(
                jnp.bfloat16
            )
            value_rows = lax.dynamic_slice_in_dim(values_all, offset, key_block)
            return weighted + jnp.einsum(
                "hck,kd->chd", block_low, value_rows, preferred_element_type=jnp.float32
            )

        return lax.cond(jnp.any(allowed), add_compute, keep_same, weighted)

    weighted = lax.fori_loop(
        0,
        block_count,
        add_values,
        jnp.zeros((row_total_count, head_count, values_all.shape[1]), jnp.float32),
    )
    return (lax.optimization_barrier(weighted.astype(jnp.bfloat16)), row_max, row_total)


def attend_grad(
    queries,
    output_rows,
    incoming,
    row_max,
    row_total,
    query_pos,
    query_seg,
    keys_all,
    values_all,
    key_seg,
    key_block,
):
    row_total_count, head_count, head_width = queries.shape
    block_count = keys_all.shape[0] // key_block
    score_scale = head_width ** (-0.5)
    row_delta = jnp.transpose(
        jnp.sum(incoming.astype(jnp.float32) * output_rows.astype(jnp.float32), axis=2)
    )

    def backward_step(query_grad, block_id):
        offset = block_id * key_block
        allowed = allowed_block(query_pos, query_seg, key_seg, offset, key_block)

        def backward_compute(query_grad):
            scores = block_scores(queries, keys_all, allowed, offset, key_block)
            prob_block = jnp.exp(scores - row_max[:, :, None]) / row_total[:, :, None]
            low_block = prob_block.astype(jnp.bfloat16)
            key_rows = lax.dynamic_slice_in_dim(keys_all, offset, key_block)
            value_rows = lax.dynamic_slice_in_dim(values_all, offset, key_block)
            prob_grad = jnp.einsum(
                "chd,kd->hck", incoming, value_rows, preferred_element_type=jnp.float32
            )
            score_grad = (prob_block * (prob_grad - row_delta[:, :, None])).astype(jnp.bfloat16)
            query_grad = query_grad + jnp.einsum(
                "hck,kd->chd", score_grad, key_rows, preferred_element_type=jnp.float32
            )
            key_part = (
                jnp.einsum("hck,chd->kd", score_grad, queries, preferred_element_type=jnp.float32)
                * score_scale
            )
            value_part = jnp.einsum(
                "hck,chd->kd", low_block, incoming, preferred_element_type=jnp.float32
            )
            return (query_grad, jnp.concatenate([key_part, value_part], axis=1))

        def skip(query_grad):
            return (query_grad, jnp.zeros((key_block, 2 * head_width), jnp.float32))

        return lax.cond(jnp.any(allowed), backward_compute, skip, query_grad)

    start_grad = jnp.zeros((row_total_count, head_count, head_width), jnp.float32)
    query_grad, block_grads = lax.scan(
        backward_step, start_grad, jnp.arange(block_count, dtype=jnp.int32)
    )
    return (query_grad * score_scale, block_grads.reshape(block_count * key_block, 2 * head_width))


def shards(
    tokens,
    frozen_qkv_matrix,
    adapter_down_weight,
    adapter_up_weight,
    adapter_bank_row,
    document_lengths,
    document_adapter,
    output_gradient,
):
    cycle_size = lax.axis_size(("seq", "tp"))
    cycle_index = lax.axis_index(("seq", "tp"))
    chip_size = lax.axis_size("tp")
    seq_count = lax.axis_size("seq")
    owner_count = lax.axis_size(("seq", "batch"))
    batch_index = lax.axis_index("batch")
    seq_index = lax.axis_index("seq")
    local_tokens = tokens[0]
    tok_count = local_tokens.shape[0]
    row_count = tok_count // chip_size
    half_rows = row_count // 2
    length = cycle_size * row_count
    key_block = min(512, length)
    head_width = HEAD_WIDTH
    query_columns = QHEADS * HEAD_WIDTH
    low_width = ADAPTER_RANK
    adapters = adapter_bank_row.shape[0]
    sample_rows = lookup_rows(adapter_bank_row, document_adapter)
    own_lengths = lax.dynamic_index_in_dim(document_lengths, batch_index, 0, keepdims=False)
    neighbor_rows = jnp.tile(sample_rows, (seq_count, 1))
    outgoing_down = adapter_down_weight[:, :, 0, :][neighbor_rows]
    outgoing_up = adapter_up_weight[neighbor_rows]
    got_down, got_up = (
        lax.all_to_all(outgoing_down, ("seq", "batch"), split_axis=0, concat_axis=0, tiled=True),
        lax.all_to_all(outgoing_up, ("seq", "batch"), split_axis=0, concat_axis=0, tiled=True),
    )
    frozen = lax.all_gather(frozen_qkv_matrix, "seq", axis=0, tiled=True)
    base_part = lax.dot_general(
        local_tokens, frozen, (((1,), (1,)), ((), ())), preferred_element_type=jnp.float32
    )
    split_tokens = local_tokens.reshape(tok_count, owner_count, -1)
    token_pos = seq_index * tok_count + jnp.arange(tok_count, dtype=jnp.int32)
    token_seg, token_member, token_inside = segment_info(own_lengths, token_pos)
    low_all = jnp.einsum(
        "tpd,psrd->tsr", split_tokens, got_down, preferred_element_type=jnp.float32
    )
    low_part = jnp.sum(jnp.where(token_member[:, :, None], low_all, 0.0), axis=1)
    base_row_values, low_rows = (
        lax.psum_scatter(base_part, "tp", scatter_dimension=0, tiled=True),
        lax.psum_scatter(low_part, "tp", scatter_dimension=0, tiled=True),
    )
    row_pos = cycle_index * row_count + jnp.arange(row_count, dtype=jnp.int32)
    row_seg, row_member, row_inside = segment_info(own_lengths, row_pos)
    low_rank = low_rows.astype(jnp.bfloat16)
    query_rank_rows = jnp.where(row_member[:, :, None], low_rank[:, None, :low_width], 0)
    value_rank_rows = jnp.where(row_member[:, :, None], low_rank[:, None, low_width:], 0)
    query_delta = jnp.einsum(
        "tsr,psrc->tpc", query_rank_rows, got_up, preferred_element_type=jnp.float32
    ).reshape(row_count, -1)
    value_delta = jnp.einsum(
        "tsr,psrc->tpc", value_rank_rows, got_up, preferred_element_type=jnp.float32
    ).reshape(row_count, -1)
    projected_query = (
        base_row_values[:, :query_columns] + adapter_scale * query_delta[:, :query_columns]
    )
    proj_key = base_row_values[:, query_columns : query_columns + head_width]
    projected_value = (
        base_row_values[:, query_columns + head_width :]
        + adapter_scale * value_delta[:, query_columns:]
    )
    cosine_table, sine_table = rope_tables(row_inside, head_width)
    queries = rotate(
        projected_query.reshape(row_count, -1, head_width), cosine_table, sine_table
    ).astype(jnp.bfloat16)
    keys_own = rotate(proj_key[:, None, :], cosine_table, sine_table)[:, 0].astype(jnp.bfloat16)
    values_own = projected_value.astype(jnp.bfloat16)
    incoming = output_gradient[0]
    early_pos = cycle_index * row_count + jnp.arange(half_rows, dtype=jnp.int32)
    late_pos = early_pos + half_rows
    current_pos = jnp.concatenate([early_pos, late_pos], axis=0)
    current_seg, current_member, current_inside = segment_info(own_lengths, current_pos)
    keys_all, values_all = (
        lax.all_gather(keys_own, ("seq", "tp"), axis=0, tiled=True),
        lax.all_gather(values_own, ("seq", "tp"), axis=0, tiled=True),
    )
    key_seg, key_member, key_inside = segment_info(own_lengths, jnp.arange(length, dtype=jnp.int32))
    incoming_heads = incoming.reshape(row_count, -1, head_width)
    output_rows, row_max, row_total = attend_rows(
        queries, current_pos, current_seg, keys_all, values_all, key_seg, key_block
    )
    query_grad, key_grads = attend_grad(
        queries,
        output_rows,
        incoming_heads,
        row_max,
        row_total,
        current_pos,
        current_seg,
        keys_all,
        values_all,
        key_seg,
        key_block,
    )

    def cycle_add(step, running):
        running = from_behind(running, ("seq", "tp"), 1)
        block_id = jnp.remainder(cycle_index - 1 - step, cycle_size)
        return running + lax.dynamic_slice_in_dim(key_grads, block_id * row_count, row_count)

    first_block = jnp.remainder(cycle_index - 1, cycle_size)
    first_terms = lax.dynamic_slice_in_dim(key_grads, first_block * row_count, row_count)
    own_key_grads = lax.fori_loop(1, cycle_size, cycle_add, first_terms)
    current_cos, current_sin = rope_tables(current_inside, head_width)
    grad_query = (
        unrotate(query_grad, current_cos, current_sin).reshape(row_count, -1).astype(jnp.bfloat16)
    )
    grad_key = unrotate(own_key_grads[:, None, :head_width], current_cos, current_sin)[:, 0].astype(
        jnp.bfloat16
    )
    grad_value = own_key_grads[:, head_width:].astype(jnp.bfloat16)
    grad_rows = jnp.concatenate([grad_query, grad_key, grad_value], axis=1)
    attention = output_rows.reshape(row_count, -1)
    all_grad, all_low = (
        lax.all_gather(grad_rows, "tp", axis=0, tiled=True),
        lax.all_gather(low_rank, "tp", axis=0, tiled=True),
    )
    qv_grad = jnp.concatenate(
        [all_grad[:, :query_columns], all_grad[:, query_columns + head_width :]], axis=1
    )
    is_query = jnp.arange(qv_grad.shape[1]) < query_columns
    query_gradient_part = jnp.where(is_query[None, :], qv_grad, 0).reshape(
        tok_count, owner_count, -1
    )
    value_gradient_part = jnp.where(is_query[None, :], 0, qv_grad).reshape(
        tok_count, owner_count, -1
    )
    token_query_low = jnp.where(token_member[:, :, None], all_low[:, None, :low_width], 0)
    token_value_low = jnp.where(token_member[:, :, None], all_low[:, None, low_width:], 0)
    low_query_grad = jnp.einsum(
        "tpc,psrc->tsr", query_gradient_part, got_up, preferred_element_type=jnp.float32
    )
    low_value_grad = jnp.einsum(
        "tpc,psrc->tsr", value_gradient_part, got_up, preferred_element_type=jnp.float32
    )
    rank_gradient = adapter_scale * jnp.concatenate(
        [
            jnp.sum(jnp.where(token_member[:, :, None], low_query_grad, 0.0), axis=1),
            jnp.sum(jnp.where(token_member[:, :, None], low_value_grad, 0.0), axis=1),
        ],
        axis=1,
    )
    rank_gradient = rank_gradient.astype(jnp.bfloat16)
    up_outgoing = adapter_scale * (
        jnp.einsum(
            "tsr,tpc->psrc",
            token_query_low,
            query_gradient_part,
            preferred_element_type=jnp.float32,
        )
        + jnp.einsum(
            "tsr,tpc->psrc",
            token_value_low,
            value_gradient_part,
            preferred_element_type=jnp.float32,
        )
    )
    low_tokens = jnp.where(token_member[:, :, None], rank_gradient[:, None, :], 0)
    token_part = jnp.dot(all_grad, frozen, preferred_element_type=jnp.float32)
    token_part = token_part + jnp.einsum(
        "tsr,psrd->tpd", low_tokens, got_down, preferred_element_type=jnp.float32
    ).reshape(tok_count, -1)
    token_grad = token_part.astype(jnp.bfloat16)[None]
    down_send = jnp.einsum(
        "tsr,tpd->psrd", low_tokens, split_tokens, preferred_element_type=jnp.float32
    )
    back_down, back_up = (
        lax.all_to_all(down_send, ("seq", "batch"), split_axis=0, concat_axis=0, tiled=True),
        lax.all_to_all(up_outgoing, ("seq", "batch"), split_axis=0, concat_axis=0, tiled=True),
    )
    flat_rows = neighbor_rows.reshape(-1)
    bank_hot = (flat_rows[:, None] == jnp.arange(adapters, dtype=jnp.int32)[None, :]).astype(
        jnp.float32
    )
    down_grad = jnp.einsum(
        "na,nx->ax",
        bank_hot,
        back_down.reshape(flat_rows.shape[0], -1),
        precision=lax.Precision.HIGHEST,
    )
    up_grad = jnp.einsum(
        "na,nx->ax",
        bank_hot,
        back_up.reshape(flat_rows.shape[0], -1),
        precision=lax.Precision.HIGHEST,
    )
    down_grad = down_grad.reshape(adapters, down_send.shape[2], 1, down_send.shape[3])
    up_grad = up_grad.reshape(adapters, low_width, up_outgoing.shape[3])
    return (attention[None], token_grad, down_grad, up_grad)


def solution(mesh):
    in_specs = (
        P(("groups", "batch"), "seq", "tp"),
        P("seq", "tp"),
        P(None, None, "tp", ("seq", "batch")),
        P(None, None, ("seq", "batch")),
        P(),
        P("groups", None),
        P("groups", None),
        P(("groups", "batch"), ("seq", "tp"), None),
    )
    out_specs = (
        P(("groups", "batch"), ("seq", "tp"), None),
        P(("groups", "batch"), "seq", "tp"),
        P("groups", None, "tp", ("seq", "batch")),
        P("groups", None, ("seq", "batch")),
    )
    return jax.shard_map(shards, mesh=mesh, in_specs=in_specs, out_specs=out_specs, check_vma=False)
```

profile of v0, /device:TPU:0, one launch (start us, length us, event | category | flops | bytes accessed | tf_op | source)
XLA Modules:
  0.0 388.6 jit_solution(15445309512948781283)
XLA Ops:
  10.6 4.0 %gather_fusion = bf16[24,64,448]{2,1,0:T(8,128)(2,1)} fusion(bf16[64,64,448]{2,1,0:T(8,128)(2,1)} %bitcast.253, s32[1024]{0:T(1024)S(1)} %pad_clamp_fusion), kind=kCustom, calls=%fused_computation | custom fusion | bytes 2752608 | tf_op jit(solution)/shard_map/gather | solution.py:232
  14.6 7.4 %all-to-all-start = ((bf16[8,3,64,448]{3,2,1,0:T(8,128)(2,1)}), bf16[8,3,64,448]{3,2,1,0:T(8,128)(2,1)}, u32[]{:S(2)}, u32[]{:S(2)}) async-start(bf16[8,3,64,448]{3,2,1,0:T(8,128)(2,1)} %bitcast.24), calls=%async_computation.1 | async-start | bytes 3145728 | tf_op jit(solution)/shard_map/all_to_all | solution.py:235
  27.1 74.9 %all-to-all-done = bf16[8,3,64,448]{3,2,1,0:T(8,128)(2,1)} async-done(((bf16[8,3,64,448]{3,2,1,0:T(8,128)(2,1)}), bf16[8,3,64,448]{3,2,1,0:T(8,128)(2,1)}, u32[]{:S(2)}, u32[]{:S(2)}) %all-to-all-start) | async-done | bytes 1376288 | tf_op jit(solution)/shard_map/all_to_all | solution.py:235
  108.2 44.0 %all-gather.3.cloned.1.call-done = bf16[768,3584]{1,0:T(8,128)(2,1)} async-done(((bf16[192,3584]{1,0:T(8,128)(2,1)}), bf16[768,3584]{1,0:T(8,128)(2,1)}) %all-gather.3.cloned.1.call-update) | async-done | bytes 5505040 | tf_op jit(solution)/shard_map/all_gather | solution.py:238
  152.3 5.6 %fusion.52 = f32[256,768]{0,1:T(8,128)} fusion(bf16[768,3584]{1,0:T(8,128)(2,1)} %all-gather.3.cloned.1.call-done, bf16[1,256,3584]{2,1,0:T(8,128)(2,1)} %param.22), kind=kOutput, calls=%fused_computation.72 | convolution fusion | flops 1409286144 | bytes 8126464 | tf_op jit(solution)/shard_map/dot_general | solution.py:239
  166.1 13.4 %all_gather.16 = bf16[1024,128]{0,1:T(8,128)(2,1)S(1)} all-gather(bf16[128,128]{0,1:T(8,128)(2,1)S(1)} %get-tuple-element.809), channel_id=1, replica_groups=mesh['groups'=2,'seq'=4,'batch'=2,'tp'=2] {'seq','tp'}, dimensions={0}, use_global_device_ids=true | all-gather | bytes 294912 | tf_op jit(solution)/shard_map/all_gather | solution.py:285
  179.7 13.1 %all-gather = bf16[1024,1,128]{0,2,1:T(8,128)(2,1)S(1)} all-gather(bf16[128,1,128]{0,2,1:T(8,128)(2,1)S(1)} %pad_maximum_fusion.4), channel_id=2, replica_groups=mesh['groups'=2,'seq'=4,'batch'=2,'tp'=2] {'seq','tp'}, dimensions={0}, use_global_device_ids=true | all-gather | bytes 294912 | tf_op jit(solution)/shard_map/all_gather | solution.py:284
  202.1 9.5 %while.63 = (s32[]{:T(128)}, f32[128,4,128]{0,2,1:T(8,128)S(1)}, f32[2,512,256]{2,1,0:T(8,128)}, s32[2]{0:T(128)S(1)}, s32[128]{0:T(128)S(1)}, /*index=5*/s32[10...) while((s32[]{:T(128)}, f32[128,4,128]{0,2,1:T(8,128)S(1)}, ...), condition=%wide.region_27.28_spmd, body=%wide.region_23.27_spmd.sunk | while | flops 338166272 | bytes 9979271 | solution.py:196
  212.5 50.2 %while.64 = (s32[]{:T(128)}, f32[128,256]{1,0:T(8,128)S(1)}, s32[]{:T(128)}, f32[1024,256]{1,0:T(8,128)}, s32[]{:T(128)}, /*index=5*/s32[]{:T(128)}, s32[]{:T(128)}, s32[]{:T(128)}, s32[]{:T(128)}, s32[]{:T(128)}) while((s32[]{:T(128)}, f32[128,256]{1,0:T(8,128)S(1)}, s32[]{:T(128)}, f32[1024,256]{1,0:T(8,128)}, s32[]{:T(128)}, ...), condition=%wide.region_30.31_spmd, body=%wide.region_29.30_spmd.sunk | while | flops 32786 | bytes 917816 | solution.py:313
  212.9 5.8 %collective-permute-done = f32[128,256]{1,0:T(8,128)S(1)} collective-permute-done((f32[128,256]{1,0:T(8,128)S(1)}, f32[128,256]{1,0:T(8,128)S(1)}, u32[]{:S(2)}, u32[]{:S(2)}) %collective-permute-start) | collective-permute-done | bytes 131104 | tf_op jit(solution)/shard_map/while/body/eval_jaxpr/ppermute | solution.py:19
  219.8 6.2 %collective-permute-done = f32[128,256]{1,0:T(8,128)S(1)} collective-permute-done((f32[128,256]{1,0:T(8,128)S(1)}, f32[128,256]{1,0:T(8,128)S(1)}, u32[]{:S(2)}, u32[]{:S(2)}) %collective-permute-start) | collective-permute-done | bytes 131104 | tf_op jit(solution)/shard_map/while/body/eval_jaxpr/ppermute | solution.py:19
  226.9 6.2 %collective-permute-done = f32[128,256]{1,0:T(8,128)S(1)} collective-permute-done((f32[128,256]{1,0:T(8,128)S(1)}, f32[128,256]{1,0:T(8,128)S(1)}, u32[]{:S(2)}, u32[]{:S(2)}) %collective-permute-start) | collective-permute-done | bytes 131104 | tf_op jit(solution)/shard_map/while/body/eval_jaxpr/ppermute | solution.py:19
  234.1 6.2 %collective-permute-done = f32[128,256]{1,0:T(8,128)S(1)} collective-permute-done((f32[128,256]{1,0:T(8,128)S(1)}, f32[128,256]{1,0:T(8,128)S(1)}, u32[]{:S(2)}, u32[]{:S(2)}) %collective-permute-start) | collective-permute-done | bytes 131104 | tf_op jit(solution)/shard_map/while/body/eval_jaxpr/ppermute | solution.py:19
  241.3 6.2 %collective-permute-done = f32[128,256]{1,0:T(8,128)S(1)} collective-permute-done((f32[128,256]{1,0:T(8,128)S(1)}, f32[128,256]{1,0:T(8,128)S(1)}, u32[]{:S(2)}, u32[]{:S(2)}) %collective-permute-start) | collective-permute-done | bytes 131104 | tf_op jit(solution)/shard_map/while/body/eval_jaxpr/ppermute | solution.py:19
  248.5 6.2 %collective-permute-done = f32[128,256]{1,0:T(8,128)S(1)} collective-permute-done((f32[128,256]{1,0:T(8,128)S(1)}, f32[128,256]{1,0:T(8,128)S(1)}, u32[]{:S(2)}, u32[]{:S(2)}) %collective-permute-start) | collective-permute-done | bytes 131104 | tf_op jit(solution)/shard_map/while/body/eval_jaxpr/ppermute | solution.py:19
  255.6 6.2 %collective-permute-done = f32[128,256]{1,0:T(8,128)S(1)} collective-permute-done((f32[128,256]{1,0:T(8,128)S(1)}, f32[128,256]{1,0:T(8,128)S(1)}, u32[]{:S(2)}, u32[]{:S(2)}) %collective-permute-start) | collective-permute-done | bytes 131104 | tf_op jit(solution)/shard_map/while/body/eval_jaxpr/ppermute | solution.py:19
  273.7 8.8 %all-to-all-done.3 = f32[8,3,32,80]{3,2,1,0:T(8,128)S(1)} async-done(((f32[8,3,32,80]{3,2,1,0:T(8,128)}), f32[8,3,32,80]{3,2,1,0:T(8,128)S(1)}, u32[]{:S(2)}, u32[]{:S(2)}) %all-to-all-start.3) | async-done | bytes 245792 | tf_op jit(solution)/shard_map/all_to_all | solution.py:379
  282.6 4.7 %all-to-all-start.2 = ((f32[8,3,64,448]{3,2,1,0:T(8,128)}), f32[8,3,64,448]{3,2,1,0:T(8,128)}, u32[]{:S(2)}, u32[]{:S(2)}) async-start(f32[8,3,64,448]{3,2,1,0:T(8,128)} %copy.153), calls=%async_computation.4 | async-start | bytes 6291456 | tf_op jit(solution)/shard_map/all_to_all | solution.py:378
  288.1 4.1 %fusion.74 = f32[256,8,448,1]{0,2,3,1:T(8,128)} fusion(bf16[8,3,64,448]{3,2,1,0:T(8,128)(2,1)} %all-to-all-done, pred[256,3]{0,1:T(4,128)(4,1)S(1)} %iota_compare_fusion.1, bf16[256,64]{0,1:T(8,128)(2,1)S(1)} %fusion.79), kind=kOutput, calls=%fused_computation.113 | convolution fusion | flops 352370688 | bytes 5079808 | tf_op jit(solution)/shard_map/tsr,psrd->tpd/dot_general | solution.py:370
  292.2 5.2 %copy.151 = f32[256,3584]{1,0:T(8,128)} copy(f32[256,3584]{0,1:T(8,128)} %bitcast.240) | data formatting | bytes 7340032 | tf_op jit(solution)/shard_map/reshape | solution.py:372
  297.4 6.5 %fusion.50 = bf16[1,256,3584]{2,1,0:T(8,128)(2,1)} fusion(f32[256,3584]{1,0:T(8,128)} %copy.151, bf16[256,768]{0,1:T(8,128)(2,1)S(1)} %all_gather.18, bf16[768,3584]{1,0:T(8,128)(2,1)} %all-gather.3.cloned.1.call-done), kind=kOutput, calls=%fused_computation.68 | convolution fusion | flops 1411121152 | bytes 11403264 | tf_op jit(solution)/shard_map/dot_general | solution.py:369
  306.8 50.7 %all-to-all-done.2 = f32[8,3,64,448]{3,2,1,0:T(8,128)} async-done(((f32[8,3,64,448]{3,2,1,0:T(8,128)}), f32[8,3,64,448]{3,2,1,0:T(8,128)}, u32[]{:S(2)}, u32[]{:S(2)}) %all-to-all-start.2) | async-done | bytes 2752544 | tf_op jit(solution)/shard_map/all_to_all | solution.py:378
  363.9 7.4 %convolution_bitcast_fusion.4 = f32[64,64,1,448]{3,0,1,2:T(8,128)S(1)} fusion(f32[64,448,24]{1,0,2:T(8,128)} %reshape.432, s32[24]{0:T(128)S(1)} %eq.175), kind=kOutput, calls=%fused_computation.69 | convolution fusion | flops 528483840 | bytes 10092640 | tf_op jit(solution)/shard_map/na,nx->ax/dot_general | solution.py:385
  371.3 9.9 %copy.156 = f32[64,64,1,448]{3,2,1,0:T(1,128)} copy(f32[64,64,1,448]{3,0,1,2:T(8,128)S(1)} %convolution_bitcast_fusion.4) | data formatting | bytes 14680064
  (166 shorter events, 74.7 us)
Async XLA Ops:
  8.0 14.2 %copy-start = (bf16[64,32,80]{2,1,0:T(8,128)(2,1)S(1)}, bf16[64,32,80]{2,1,0:T(8,128)(2,1)}, u32[]{:S(2)}) copy-start(bf16[64,32,80]{2,1,0:T(8,128)(2,1)} %param.25) | copy-start | bytes 983044
  8.0 144.2 %all-gather.3.cloned.1.call-start = ((), (), s32[]{:S(2)}) async-start(), calls=%async_computation.6 | async-start | bytes 6881280 | tf_op jit(solution)/shard_map/all_gather | solution.py:238
  10.6 11.4 %copy-start.5 = (s32[2,3]{1,0:T(2,128)S(1)}, s32[2,3]{1,0:T(2,128)}, u32[]{:S(2)}) copy-start(s32[2,3]{1,0:T(2,128)} %param.27) | copy-start | bytes 76
  14.6 11.8 %copy-start.4 = (bf16[1,128,512]{2,1,0:T(8,128)(2,1)S(1)}, bf16[1,128,512]{2,1,0:T(8,128)(2,1)}, u32[]{:S(2)}) copy-start(bf16[1,128,512]{2,1,0:T(8,128)(2,1)} %param.29) | copy-start | bytes 393220
  14.6 87.4 %all-to-all-start = ((bf16[8,3,64,448]{3,2,1,0:T(8,128)(2,1)}), bf16[8,3,64,448]{3,2,1,0:T(8,128)(2,1)}, u32[]{:S(2)}, u32[]{:S(2)}) async-start(bf16[8,3,64,448]{3,2,1,0:T(8,128)(2,1)} %bitcast.24), calls=%async_computation.1 | async-start | bytes 3145728 | tf_op jit(solution)/shard_map/all_to_all | solution.py:235
  26.4 131.5 %copy-start.2 = (bf16[1,256,3584]{1,2,0:T(8,128)(2,1)}, bf16[1,256,3584]{1,2,0:T(8,128)(2,1)S(1)}, u32[]{:S(2)}) copy-start(bf16[1,256,3584]{1,2,0:T(8,128)(2,1)S(1)} %copy.137) | copy-start | bytes 5505028
  102.0 58.9 %all-to-all-start.1 = ((bf16[8,3,32,80]{3,2,1,0:T(8,128)(2,1)}), bf16[8,3,32,80]{3,2,1,0:T(8,128)(2,1)S(1)}, u32[]{:S(2)}, u32[]{:S(2)}) async-start(bf16[8,3,32,80]{3,2,1,0:T(8,128)(2,1)} %bitcast.17), calls=%async_computation.3 | async-start | bytes 393216 | tf_op jit(solution)/shard_map/all_to_all | solution.py:236
  105.5 52.7 %reduce-scatter.5.cloned.1.call-start = ((), (), s32[]{:S(2)}) async-start(), calls=%async_computation.8 | async-start | bytes 98304 | tf_op jit(solution)/shard_map/reduce_scatter | solution.py:251
  108.2 57.1 %reduce-scatter.3.cloned.1.call-start = ((), (), s32[]{:S(2)}) async-start(), calls=%async_computation.7 | async-start | bytes 1179648 | tf_op jit(solution)/shard_map/reduce_scatter | solution.py:250
  212.5 6.2 %collective-permute-start = (f32[128,256]{1,0:T(8,128)S(1)}, f32[128,256]{1,0:T(8,128)S(1)}, u32[]{:S(2)}, u32[]{:S(2)}) collective-permute-start(f32[128,256]{1,0:T(8,128)S(1)} %get-tuple-element.1221), channel_id=1, source_target_pairs={{0,1},{1,4},{4,5},{5,8},{8,9},{9,12},{12,13},{13,0},{2,3},{3,6},{6... | collective-permute-start | bytes 393224 | tf_op jit(solution)/shard_map/while/body/eval_jaxpr/ppermute | solution.py:19
  219.7 6.2 %collective-permute-start = (f32[128,256]{1,0:T(8,128)S(1)}, f32[128,256]{1,0:T(8,128)S(1)}, u32[]{:S(2)}, u32[]{:S(2)}) collective-permute-start(f32[128,256]{1,0:T(8,128)S(1)} %get-tuple-element.1221), channel_id=1, source_target_pairs={{0,1},{1,4},{4,5},{5,8},{8,9},{9,12},{12,13},{13,0},{2,3},{3,6},{6... | collective-permute-start | bytes 393224 | tf_op jit(solution)/shard_map/while/body/eval_jaxpr/ppermute | solution.py:19
  226.8 6.2 %collective-permute-start = (f32[128,256]{1,0:T(8,128)S(1)}, f32[128,256]{1,0:T(8,128)S(1)}, u32[]{:S(2)}, u32[]{:S(2)}) collective-permute-start(f32[128,256]{1,0:T(8,128)S(1)} %get-tuple-element.1221), channel_id=1, source_target_pairs={{0,1},{1,4},{4,5},{5,8},{8,9},{9,12},{12,13},{13,0},{2,3},{3,6},{6... | collective-permute-start | bytes 393224 | tf_op jit(solution)/shard_map/while/body/eval_jaxpr/ppermute | solution.py:19
  234.0 6.2 %collective-permute-start = (f32[128,256]{1,0:T(8,128)S(1)}, f32[128,256]{1,0:T(8,128)S(1)}, u32[]{:S(2)}, u32[]{:S(2)}) collective-permute-start(f32[128,256]{1,0:T(8,128)S(1)} %get-tuple-element.1221), channel_id=1, source_target_pairs={{0,1},{1,4},{4,5},{5,8},{8,9},{9,12},{12,13},{13,0},{2,3},{3,6},{6... | collective-permute-start | bytes 393224 | tf_op jit(solution)/shard_map/while/body/eval_jaxpr/ppermute | solution.py:19
  241.2 6.2 %collective-permute-start = (f32[128,256]{1,0:T(8,128)S(1)}, f32[128,256]{1,0:T(8,128)S(1)}, u32[]{:S(2)}, u32[]{:S(2)}) collective-permute-start(f32[128,256]{1,0:T(8,128)S(1)} %get-tuple-element.1221), channel_id=1, source_target_pairs={{0,1},{1,4},{4,5},{5,8},{8,9},{9,12},{12,13},{13,0},{2,3},{3,6},{6... | collective-permute-start | bytes 393224 | tf_op jit(solution)/shard_map/while/body/eval_jaxpr/ppermute | solution.py:19
  248.4 6.2 %collective-permute-start = (f32[128,256]{1,0:T(8,128)S(1)}, f32[128,256]{1,0:T(8,128)S(1)}, u32[]{:S(2)}, u32[]{:S(2)}) collective-permute-start(f32[128,256]{1,0:T(8,128)S(1)} %get-tuple-element.1221), channel_id=1, source_target_pairs={{0,1},{1,4},{4,5},{5,8},{8,9},{9,12},{12,13},{13,0},{2,3},{3,6},{6... | collective-permute-start | bytes 393224 | tf_op jit(solution)/shard_map/while/body/eval_jaxpr/ppermute | solution.py:19
  255.6 6.2 %collective-permute-start = (f32[128,256]{1,0:T(8,128)S(1)}, f32[128,256]{1,0:T(8,128)S(1)}, u32[]{:S(2)}, u32[]{:S(2)}) collective-permute-start(f32[128,256]{1,0:T(8,128)S(1)} %get-tuple-element.1221), channel_id=1, source_target_pairs={{0,1},{1,4},{4,5},{5,8},{8,9},{9,12},{12,13},{13,0},{2,3},{3,6},{6... | collective-permute-start | bytes 393224 | tf_op jit(solution)/shard_map/while/body/eval_jaxpr/ppermute | solution.py:19
  265.4 5.7 %copy-start.3 = (bf16[1,256,3584]{1,2,0:T(8,128)(2,1)S(1)}, bf16[1,256,3584]{1,2,0:T(8,128)(2,1)}, u32[]{:S(2)}) copy-start(bf16[1,256,3584]{1,2,0:T(8,128)(2,1)} %copy-done.2) | copy-start | bytes 5505028
  266.9 15.6 %all-to-all-start.3 = ((f32[8,3,32,80]{3,2,1,0:T(8,128)}), f32[8,3,32,80]{3,2,1,0:T(8,128)S(1)}, u32[]{:S(2)}, u32[]{:S(2)}) async-start(f32[8,3,32,80]{3,2,1,0:T(8,128)} %fusion.55), calls=%async_computation.5 | async-start | bytes 786432 | tf_op jit(solution)/shard_map/all_to_all | solution.py:379
  282.6 74.9 %all-to-all-start.2 = ((f32[8,3,64,448]{3,2,1,0:T(8,128)}), f32[8,3,64,448]{3,2,1,0:T(8,128)}, u32[]{:S(2)}, u32[]{:S(2)}) async-start(f32[8,3,64,448]{3,2,1,0:T(8,128)} %copy.153), calls=%async_computation.4 | async-start | bytes 6291456 | tf_op jit(solution)/shard_map/all_to_all | solution.py:378
  371.3 9.9 %copy-start.1 = (bf16[64,32,80]{2,1,0:T(8,128)(2,1)S(1)}, bf16[64,32,80]{2,1,0:T(8,128)(2,1)}, u32[]{:S(2)}) copy-start(bf16[64,32,80]{2,1,0:T(8,128)(2,1)} %param.25) | copy-start | bytes 983044
Sparse Core Ops, SparseCore 0:
  10.4 141.7 all-gather.2
Sparse Core Ops, SparseCore 1:
  108.8 8.8 reduce-scatter.4
  158.0 7.2 reduce-scatter.2
where the time goes:
time: 390 us; the launch traced here: 389 us
  waiting for transfers between devices  226 us (58%)
  local copies, waits for them, and re-layouts  41.1 us (11%)
  matrix products  32.7 us (8%)
  blocking collectives  30.4 us (8%)
  starting transfers between devices  19.9 us (5%)
  other arithmetic  16.8 us (4%)
  between operations  16 us (4%)
  loops' own time  5.89 us (2%)
    all_to_all x1, waiting for transfers between devices, shards(): lax.all_to_all(outgoing_down, ('seq', 'batch'), split_axis=0, concat_axis...  74.9 us
    all_to_all x1, waiting for transfers between devices, shards(): lax.all_to_all(down_send, ('seq', 'batch'), split_axis=0, concat_axis=0,...  50.7 us
    all_gather x1, waiting for transfers between devices, shards(): frozen = lax.all_gather(frozen_qkv_matrix, 'seq', axis=0, tiled=True)  44 us
    ppermute x7, waiting for transfers between devices, from_behind(): return lax.ppermute(value, axis, pairs)  42.8 us
    unnamed x17, local copies, waits for them, and re-layouts  15.3 us
    all_gather x1, blocking collectives, shards(): lax.all_gather(values_own, ('seq', 'tp'), axis=0, tiled=True)  13.4 us
    all_gather x1, blocking collectives, shards(): lax.all_gather(keys_own, ('seq', 'tp'), axis=0, tiled=True)  13.1 us
    all_to_all x1, waiting for transfers between devices, shards(): lax.all_to_all(up_outgoing, ('seq', 'batch'), split_axis=0, concat_axis=0...  8.82 us
  transfers between devices with their start and end apart: 14, of which 12 were waited for; matrix products, arithmetic and copies ran while one was open for 11% of the time, Pallas kernels for 0%

commit v1 on v0

--- a/solution.py
+++ b/solution.py
@@ -11,12 +11,6 @@
 adapter_scale = 2.0
 rope_base = 5000000.0
 start_floor = -1e30
-
-
-def from_behind(value, axis, steps):
-    count = lax.axis_size(axis)
-    pairs = [(source, (source + steps) % count) for source in range(count)]
-    return lax.ppermute(value, axis, pairs)
 
 
 def segment_info(lengths, positions):
@@ -213,7 +207,6 @@
     cycle_index = lax.axis_index(("seq", "tp"))
     chip_size = lax.axis_size("tp")
     seq_count = lax.axis_size("seq")
-    owner_count = lax.axis_size(("seq", "batch"))
     batch_index = lax.axis_index("batch")
     seq_index = lax.axis_index("seq")
     local_tokens = tokens[0]
@@ -228,39 +221,60 @@
     adapters = adapter_bank_row.shape[0]
     sample_rows = lookup_rows(adapter_bank_row, document_adapter)
     own_lengths = lax.dynamic_index_in_dim(document_lengths, batch_index, 0, keepdims=False)
-    neighbor_rows = jnp.tile(sample_rows, (seq_count, 1))
-    outgoing_down = adapter_down_weight[:, :, 0, :][neighbor_rows]
-    outgoing_up = adapter_up_weight[neighbor_rows]
-    got_down, got_up = (
-        lax.all_to_all(outgoing_down, ("seq", "batch"), split_axis=0, concat_axis=0, tiled=True),
-        lax.all_to_all(outgoing_up, ("seq", "batch"), split_axis=0, concat_axis=0, tiled=True),
-    )
-    frozen = lax.all_gather(frozen_qkv_matrix, "seq", axis=0, tiled=True)
+    batch_count = lax.axis_size("batch")
+    group_count = lax.axis_size("groups")
+    segment_count = document_lengths.shape[1]
+    plane_index = lax.axis_index(("groups", "batch"))
+    plane_count = group_count * batch_count
+    flat_rows = sample_rows.reshape(-1)
+    frozen_rows = frozen_qkv_matrix.shape[0] // plane_count
+    frozen_piece = lax.dynamic_slice_in_dim(
+        frozen_qkv_matrix, plane_index * frozen_rows, frozen_rows
+    )
+    frozen = lax.all_gather(frozen_piece, ("seq", "groups", "batch"), axis=0, tiled=True)
+    joint_rank = adapter_down_weight.shape[1]
+    outgoing_down = adapter_down_weight[:, :, 0, :][sample_rows]
+    outgoing_up = adapter_up_weight[sample_rows]
+    got_down = lax.all_to_all(outgoing_down, "batch", split_axis=0, concat_axis=0, tiled=True)
+    got_up = lax.all_to_all(outgoing_up, "batch", split_axis=0, concat_axis=0, tiled=True)
+    got_down = jnp.transpose(got_down, (1, 2, 0, 3)).reshape(segment_count * joint_rank, -1)
+    got_up = jnp.transpose(got_up, (1, 2, 0, 3)).reshape(segment_count * low_width, -1)
+    down_all = lax.all_gather(got_down, "seq", axis=0)
+    up_all = lax.all_gather(got_up, "seq", axis=0)
+    down_width = got_down.shape[1]
+    up_rows = jnp.transpose(up_all, (1, 0, 2)).reshape(segment_count, low_width, -1)
     base_part = lax.dot_general(
         local_tokens, frozen, (((1,), (1,)), ((), ())), preferred_element_type=jnp.float32
     )
-    split_tokens = local_tokens.reshape(tok_count, owner_count, -1)
     token_pos = seq_index * tok_count + jnp.arange(tok_count, dtype=jnp.int32)
     token_seg, token_member, token_inside = segment_info(own_lengths, token_pos)
-    low_all = jnp.einsum(
-        "tpd,psrd->tsr", split_tokens, got_down, preferred_element_type=jnp.float32
-    )
+    low_all = sum(
+        lax.dot_general(
+            local_tokens[:, owner * down_width : (owner + 1) * down_width],
+            down_all[owner],
+            (((1,), (1,)), ((), ())),
+            preferred_element_type=jnp.float32,
+        )
+        for owner in range(seq_count)
+    ).reshape(tok_count, segment_count, joint_rank)
     low_part = jnp.sum(jnp.where(token_member[:, :, None], low_all, 0.0), axis=1)
-    base_row_values, low_rows = (
-        lax.psum_scatter(base_part, "tp", scatter_dimension=0, tiled=True),
-        lax.psum_scatter(low_part, "tp", scatter_dimension=0, tiled=True),
-    )
+    summed_rows = lax.psum_scatter(
+        jnp.concatenate([base_part, low_part], axis=1), "tp", scatter_dimension=0, tiled=True
+    )
+    qkv_width = base_part.shape[1]
+    base_row_values = summed_rows[:, :qkv_width]
+    low_rows = summed_rows[:, qkv_width:]
     row_pos = cycle_index * row_count + jnp.arange(row_count, dtype=jnp.int32)
     row_seg, row_member, row_inside = segment_info(own_lengths, row_pos)
     low_rank = low_rows.astype(jnp.bfloat16)
     query_rank_rows = jnp.where(row_member[:, :, None], low_rank[:, None, :low_width], 0)
     value_rank_rows = jnp.where(row_member[:, :, None], low_rank[:, None, low_width:], 0)
     query_delta = jnp.einsum(
-        "tsr,psrc->tpc", query_rank_rows, got_up, preferred_element_type=jnp.float32
-    ).reshape(row_count, -1)
+        "tsr,src->tc", query_rank_rows, up_rows, preferred_element_type=jnp.float32
+    )
     value_delta = jnp.einsum(
-        "tsr,psrc->tpc", value_rank_rows, got_up, preferred_element_type=jnp.float32
-    ).reshape(row_count, -1)
+        "tsr,src->tc", value_rank_rows, up_rows, preferred_element_type=jnp.float32
+    )
     projected_query = (
         base_row_values[:, :query_columns] + adapter_scale * query_delta[:, :query_columns]
     )
@@ -280,10 +294,11 @@
     late_pos = early_pos + half_rows
     current_pos = jnp.concatenate([early_pos, late_pos], axis=0)
     current_seg, current_member, current_inside = segment_info(own_lengths, current_pos)
-    keys_all, values_all = (
-        lax.all_gather(keys_own, ("seq", "tp"), axis=0, tiled=True),
-        lax.all_gather(values_own, ("seq", "tp"), axis=0, tiled=True),
-    )
+    pairs_all = lax.all_gather(
+        jnp.concatenate([keys_own, values_own], axis=1), ("seq", "tp"), axis=0, tiled=True
+    )
+    keys_all = pairs_all[:, :head_width]
+    values_all = pairs_all[:, head_width:]
     key_seg, key_member, key_inside = segment_info(own_lengths, jnp.arange(length, dtype=jnp.int32))
     incoming_heads = incoming.reshape(row_count, -1, head_width)
     output_rows, row_max, row_total = attend_rows(
@@ -303,14 +318,7 @@
         key_block,
     )
 
-    def cycle_add(step, running):
-        running = from_behind(running, ("seq", "tp"), 1)
-        block_id = jnp.remainder(cycle_index - 1 - step, cycle_size)
-        return running + lax.dynamic_slice_in_dim(key_grads, block_id * row_count, row_count)
-
-    first_block = jnp.remainder(cycle_index - 1, cycle_size)
-    first_terms = lax.dynamic_slice_in_dim(key_grads, first_block * row_count, row_count)
-    own_key_grads = lax.fori_loop(1, cycle_size, cycle_add, first_terms)
+    own_key_grads = lax.psum_scatter(key_grads, ("seq", "tp"), scatter_dimension=0, tiled=True)
     current_cos, current_sin = rope_tables(current_inside, head_width)
     grad_query = (
         unrotate(query_grad, current_cos, current_sin).reshape(row_count, -1).astype(jnp.bfloat16)
@@ -321,27 +329,26 @@
     grad_value = own_key_grads[:, head_width:].astype(jnp.bfloat16)
     grad_rows = jnp.concatenate([grad_query, grad_key, grad_value], axis=1)
     attention = output_rows.reshape(row_count, -1)
-    all_grad, all_low = (
-        lax.all_gather(grad_rows, "tp", axis=0, tiled=True),
-        lax.all_gather(low_rank, "tp", axis=0, tiled=True),
-    )
-    qv_grad = jnp.concatenate(
-        [all_grad[:, :query_columns], all_grad[:, query_columns + head_width :]], axis=1
-    )
-    is_query = jnp.arange(qv_grad.shape[1]) < query_columns
-    query_gradient_part = jnp.where(is_query[None, :], qv_grad, 0).reshape(
-        tok_count, owner_count, -1
-    )
-    value_gradient_part = jnp.where(is_query[None, :], 0, qv_grad).reshape(
-        tok_count, owner_count, -1
-    )
+    both_rows = lax.all_gather(
+        jnp.concatenate([grad_rows, low_rank], axis=1), "tp", axis=0, tiled=True
+    )
+    all_grad = both_rows[:, :qkv_width]
+    all_low = both_rows[:, qkv_width:]
+    query_gradient_part = all_grad[:, :query_columns]
+    value_gradient_part = all_grad[:, query_columns + head_width :]
     token_query_low = jnp.where(token_member[:, :, None], all_low[:, None, :low_width], 0)
     token_value_low = jnp.where(token_member[:, :, None], all_low[:, None, low_width:], 0)
     low_query_grad = jnp.einsum(
-        "tpc,psrc->tsr", query_gradient_part, got_up, preferred_element_type=jnp.float32
+        "tc,src->tsr",
+        query_gradient_part,
+        up_rows[:, :, :query_columns],
+        preferred_element_type=jnp.float32,
     )
     low_value_grad = jnp.einsum(
-        "tpc,psrc->tsr", value_gradient_part, got_up, preferred_element_type=jnp.float32
+        "tc,src->tsr",
+        value_gradient_part,
+        up_rows[:, :, query_columns:],
+        preferred_element_type=jnp.float32,
     )
     rank_gradient = adapter_scale * jnp.concatenate(
         [
@@ -351,34 +358,59 @@
         axis=1,
     )
     rank_gradient = rank_gradient.astype(jnp.bfloat16)
-    up_outgoing = adapter_scale * (
-        jnp.einsum(
-            "tsr,tpc->psrc",
-            token_query_low,
-            query_gradient_part,
-            preferred_element_type=jnp.float32,
-        )
-        + jnp.einsum(
-            "tsr,tpc->psrc",
-            token_value_low,
-            value_gradient_part,
-            preferred_element_type=jnp.float32,
-        )
-    )
-    low_tokens = jnp.where(token_member[:, :, None], rank_gradient[:, None, :], 0)
+    up_terms = adapter_scale * jnp.concatenate(
+        [
+            jnp.einsum(
+                "tsr,tc->src",
+                token_query_low,
+                query_gradient_part,
+                preferred_element_type=jnp.float32,
+            ),
+            jnp.einsum(
+                "tsr,tc->src",
+                token_value_low,
+                value_gradient_part,
+                preferred_element_type=jnp.float32,
+            ),
+        ],
+        axis=2,
+    )
+    low_tokens = jnp.where(token_member[:, :, None], rank_gradient[:, None, :], 0).reshape(
+        tok_count, -1
+    )
+    down_terms = jnp.stack(
+        [
+            lax.dot_general(
+                low_tokens,
+                local_tokens[:, owner * down_width : (owner + 1) * down_width],
+                (((0,), (0,)), ((), ())),
+                preferred_element_type=jnp.float32,
+            )
+            for owner in range(seq_count)
+        ]
+    )
+    down_sums = lax.psum_scatter(down_terms, "seq", scatter_dimension=0, tiled=False)
+    up_split = jnp.transpose(
+        up_terms.reshape(segment_count * low_width, seq_count, -1), (1, 0, 2)
+    )
+    up_sums = lax.psum_scatter(up_split, "seq", scatter_dimension=0, tiled=False)
     token_part = jnp.dot(all_grad, frozen, preferred_element_type=jnp.float32)
-    token_part = token_part + jnp.einsum(
-        "tsr,psrd->tpd", low_tokens, got_down, preferred_element_type=jnp.float32
-    ).reshape(tok_count, -1)
+    token_part = token_part + jnp.concatenate(
+        [
+            jnp.dot(low_tokens, down_all[owner], preferred_element_type=jnp.float32)
+            for owner in range(seq_count)
+        ],
+        axis=1,
+    )
     token_grad = token_part.astype(jnp.bfloat16)[None]
-    down_send = jnp.einsum(
-        "tsr,tpd->psrd", low_tokens, split_tokens, preferred_element_type=jnp.float32
-    )
-    back_down, back_up = (
-        lax.all_to_all(down_send, ("seq", "batch"), split_axis=0, concat_axis=0, tiled=True),
-        lax.all_to_all(up_outgoing, ("seq", "batch"), split_axis=0, concat_axis=0, tiled=True),
-    )
-    flat_rows = neighbor_rows.reshape(-1)
+    down_send = jnp.transpose(
+        down_sums.reshape(segment_count, joint_rank, batch_count, -1), (2, 0, 1, 3)
+    )
+    up_send = jnp.transpose(
+        up_sums.reshape(segment_count, low_width, batch_count, -1), (2, 0, 1, 3)
+    )
+    back_down = lax.all_to_all(down_send, "batch", split_axis=0, concat_axis=0, tiled=True)
+    back_up = lax.all_to_all(up_send, "batch", split_axis=0, concat_axis=0, tiled=True)
     bank_hot = (flat_rows[:, None] == jnp.arange(adapters, dtype=jnp.int32)[None, :]).astype(
         jnp.float32
     )
@@ -394,8 +426,8 @@
         back_up.reshape(flat_rows.shape[0], -1),
         precision=lax.Precision.HIGHEST,
     )
-    down_grad = down_grad.reshape(adapters, down_send.shape[2], 1, down_send.shape[3])
-    up_grad = up_grad.reshape(adapters, low_width, up_outgoing.shape[3])
+    down_grad = down_grad.reshape(adapters, joint_rank, 1, -1)
+    up_grad = up_grad.reshape(adapters, low_width, -1)
     return (attention[None], token_grad, down_grad, up_grad)
 
 

time: 390 us -> 386 us (0.990)
  local copies, waits for them, and re-layouts: 41.1 us -> 62.5 us
  waiting for transfers between devices: 226 us -> 208 us
  blocking collectives: 30.4 us -> 41.2 us
  starting transfers between devices: 19.9 us -> 10.6 us
  matrix products: 32.7 us -> 27.4 us
    all_to_all x4 -> x3, waiting for transfers between devices: 134 us -> 2.47 us  [the longest x1 2.46 us: shards(): lax.all_to_all(down_send, 'batch', split_axis=0, concat_axis=0, tiled=True)]
    reduce_scatter x2 -> x4, waiting for transfers between devices: 3.88 us -> 91.9 us  [the longest x1 49 us: shards(): lax.psum_scatter(down_terms, 'seq', scatter_dimension=0, tiled=False)]
    all_gather x1 -> x2, waiting for transfers between devices: 44 us -> 114 us  [the longest x1 86.2 us: shards(): lax.all_gather(frozen_piece, ('seq', 'groups', 'batch'), axis=0, tiled=True)]
    ppermute x7 -> x0, waiting for transfers between devices: 42.8 us -> none  [from_behind(): return lax.ppermute(value, axis, pairs)]
    dynamic_update_slice x4, local copies, waits for them, and re-layouts: 2.06 us -> 21.8 us  [attend_grad(): lax.scan(backward_step, start_grad, jnp.arange(block_count, dtype=jnp.int...]
    all_to_all x0 -> x1, blocking collectives: none -> 11.6 us  [shards(): lax.all_to_all(outgoing_down, 'batch', split_axis=0, concat_axis=0, tiled...]
    all_to_all x4 -> x3, starting transfers between devices: 19 us -> 10.1 us  [the longest x1 3.54 us: shards(): lax.all_to_all(down_send, 'batch', split_axis=0, concat_axis=0, tiled=True)]
    add x7 -> x0, other arithmetic: 6.44 us -> none  [cycle_add(): running + lax.dynamic_slice_in_dim(key_grads, block_id * row_count, row_c...]
  transfers between devices with their start and end apart: 14 -> 9, of which waited for: 12 -> 6; matrix products, arithmetic and copies ran while one was open for 11% -> 9% of each run, Pallas kernels for 0% -> 0%
where the time goes in v1:
time: 386 us; the launch traced here: 384 us
  waiting for transfers between devices  208 us (54%)
  local copies, waits for them, and re-layouts  62.5 us (16%)
  blocking collectives  41.2 us (11%)
  matrix products  27.4 us (7%)
  between operations  14.8 us (4%)
  other arithmetic  13.1 us (3%)
  starting transfers between devices  10.6 us (3%)
  loops' own time  5.59 us (1%)
    all_gather x1, waiting for transfers between devices, shards(): lax.all_gather(frozen_piece, ('seq', 'groups', 'batch'), axis=0, tiled=True)  86.2 us
    reduce_scatter x1, waiting for transfers between devices, shards(): lax.psum_scatter(down_terms, 'seq', scatter_dimension=0, tiled=False)  49 us
    reduce_scatter x1, waiting for transfers between devices, shards(): lax.psum_scatter(key_grads, ('seq', 'tp'), scatter_dimension=0, tiled=True)  32.3 us
    all_gather x1, waiting for transfers between devices, shards(): down_all = lax.all_gather(got_down, 'seq', axis=0)  27.8 us
    dynamic_update_slice x4, local copies, waits for them, and re-layouts, attend_grad(): lax.scan(backward_step, start_grad, jnp.arange(block_count, dtype=jnp.int...  21.8 us
    unnamed x27, local copies, waits for them, and re-layouts  15.4 us
    all_gather x1, blocking collectives, shards(): lax.all_gather(jnp.concatenate([keys_own, values_own], axis=1), ('seq', '...  14 us
    all_gather x1, blocking collectives, shards(): up_all = lax.all_gather(got_up, 'seq', axis=0)  13.5 us
  transfers between devices with their start and end apart: 9, of which 6 were waited for; matrix products, arithmetic and copies ran while one was open for 9% of the time, Pallas kernels for 0%

profile of v1, /device:TPU:0, one launch (start us, length us, event | category | flops | bytes accessed | tf_op | source)
XLA Modules:
  0.0 383.7 jit_solution(15517372045462022364)
XLA Ops:
  9.2 3.5 gather_fusion
  12.7 11.6 %all_to_all.20 = bf16[2,3,64,448]{3,2,1,0:T(8,128)(2,1)S(1)} all-to-all(bf16[2,3,64,448]{3,2,1,0:T(8,128)(2,1)} %bitcast.226), channel_id=1, replica_groups=mesh['groups'=2,'seq'=4,'batch'=2,'tp'=2] {'batch'}, dimensions={0} | all-to-all | bytes 688128 | tf_op jit(solution)/shard_map/all_to_all | solution.py:238
  28.4 2.2 gather_fusion.1
  30.6 3.3 all-to-all-start.1
  34.3 27.8 %all-gather.5.cloned.1.call-done = bf16[4,192,896]{2,1,0:T(8,128)(2,1)} async-done(((bf16[1,192,896]{2,1,0:T(8,128)(2,1)}), bf16[4,192,896]{2,1,0:T(8,128)(2,1)}) %all-gather.5.cloned.1.call-update) | async-done | bytes 1376272 | tf_op jit(solution)/shard_map/all_gather | solution.py:242
  65.5 86.2 %all-gather.3.cloned.1.call-done = bf16[768,3584]{1,0:T(8,128)(2,1)} async-done(((bf16[48,3584]{1,0:T(8,128)(2,1)}), bf16[768,3584]{1,0:T(8,128)(2,1)}) %all-gather.3.cloned.1.call-update) | async-done | bytes 5505040 | tf_op jit(solution)/shard_map/all_gather | solution.py:234
  151.6 4.2 %convolution_bitcast_fusion.5 = f32[256,768]{0,1:T(8,128)S(1)} fusion(bf16[768,3584]{1,0:T(8,128)(2,1)} %all-gather.3.cloned.1.call-done, bf16[1,256,3584]{2,1,0:T(8,128)(2,1)S(1)} %copy-done.2), kind=kOutput, calls=%fused_computation.69 | convolution fusion | flops 1409286144 | bytes 8126464 | tf_op jit(solution)/shard_map/dot_general | solution.py:246
  158.0 13.5 %all_gather.17 = bf16[4,96,160]{1,2,0:T(8,128)(2,1)S(1)} all-gather(bf16[1,96,160]{1,2,0:T(8,128)(2,1)S(1)} %copy.117), channel_id=1, replica_groups=mesh['groups'=2,'seq'=4,'batch'=2,'tp'=2] {'seq'}, dimensions={0}, use_global_device_ids=true | all-gather | bytes 153600 | tf_op jit(solution)/shard_map/all_gather | solution.py:243
  174.2 14.0 %all_gather.18 = bf16[1024,256]{0,1:T(8,128)(2,1)S(1)} all-gather(bf16[128,256]{0,1:T(8,128)(2,1)S(1)} %pad_maximum_fusion.5), channel_id=1, replica_groups=mesh['groups'=2,'seq'=4,'batch'=2,'tp'=2] {'seq','tp'}, dimensions={0}, use_global_device_ids=true | all-gather | bytes 589824 | tf_op jit(solution)/shard_map/all_gather | solution.py:297
  189.0 3.8 while.46
  193.0 3.8 while.47
  196.9 29.2 %while.48 = (s32[]{:T(128)}, f32[128,4,128]{0,2,1:T(8,128)S(1)}, f32[2,512,256]{1,0,2:T(2,128)}, s32[2]{0:T(128)S(1)}, s32[128]{0:T(128)S(1)}, /*index=5*/s32[10...) while((s32[]{:T(128)}, f32[128,4,128]{0,2,1:T(8,128)S(1)}, ...), condition=%wide.region_26.27_spmd, body=%wide.region_22.26_spmd.sunk | while | flops 338166272 | bytes 9979271 | solution.py:190
  202.0 10.3 %dynamic_update_slice.5 = f32[2,512,256]{1,0,2:T(2,128)} dynamic-update-slice(f32[2,512,256]{1,0,2:T(2,128)} %get-tuple-element.1050, f32[1,512,256]{1,0,2:T(1,128)S(1)} %copy.173, s32[]{:T(128)S(6)} %copy.203, s32[]{:T(128)} %constant.155.clone.1..sunk.2, s32[]{:T(128)} %constant.155.clone.1..sunk.2) | dynamic-update-slice | bytes 1048580 | tf_op jit(solution)/shard_map/while/body/jit(dynamic_update_index_in_dim)/dynamic_update_slice | solution.py:190
  215.7 10.3 %dynamic_update_slice.5 = f32[2,512,256]{1,0,2:T(2,128)} dynamic-update-slice(f32[2,512,256]{1,0,2:T(2,128)} %get-tuple-element.1050, f32[1,512,256]{1,0,2:T(1,128)S(1)} %copy.173, s32[]{:T(128)S(6)} %copy.203, s32[]{:T(128)} %constant.155.clone.1..sunk.2, s32[]{:T(128)} %constant.155.clone.1..sunk.2) | dynamic-update-slice | bytes 1048580 | tf_op jit(solution)/shard_map/while/body/jit(dynamic_update_index_in_dim)/dynamic_update_slice | solution.py:190
  226.1 2.4 copy.165
  228.9 32.3 %reduce-scatter.7.cloned.1.call-done = f32[128,256]{0,1:T(8,128)} async-done(((f32[1024,256]{0,1:T(8,128)}), f32[128,256]{0,1:T(8,128)}) %reduce-scatter.7.cloned.1.call-update) | async-done | bytes 131088 | tf_op jit(solution)/shard_map/reduce_scatter | solution.py:321
  279.3 10.7 %reduce-scatter.11.cloned.1.call-done = f32[1,96,160]{1,2,0:T(8,128)} async-done(((f32[4,96,160]{1,2,0:T(8,128)}), f32[1,96,160]{1,2,0:T(8,128)}) %reduce-scatter.11.cloned.1.call-update) | async-done | bytes 61456 | tf_op jit(solution)/shard_map/reduce_scatter | solution.py:396
  291.7 3.3 all-to-all-start.3
  296.4 49.0 %reduce-scatter.9.cloned.1.call-done = f32[1,192,896]{2,1,0:T(8,128)} async-done(((f32[4,192,896]{2,1,0:T(8,128)}), f32[1,192,896]{2,1,0:T(8,128)}) %reduce-scatter.9.cloned.1.call-update) | async-done | bytes 688144 | tf_op jit(solution)/shard_map/reduce_scatter | solution.py:392
  348.2 3.5 all-to-all-start.2
  351.8 5.9 %fusion.50 = bf16[1,256,3584]{2,1,0:T(8,128)(2,1)} fusion(bf16[768,3584]{1,0:T(8,128)(2,1)} %all-gather.3.cloned.1.call-done, f32[256,896]{1,0:T(8,128)S(1)} %copy-done.7, f32[256,896]{1,0:T(8,128)S(1)} %copy-done.8, f32[256,896]{1,0:T(8,128)} %fusion.65, f32[256,896]{1,0:T(8,128)} %fusion.64, bf16[256,832]{1,0:T(8,128)(2,1)S(1)} %all_gather.19), kind=kOutput, calls=%fused_computation.66 | convolution fusion | flops 1413873664 | bytes 11403264 | tf_op jit(solution)/shard_map/dot_general | solution.py:397
  360.2 2.5 all-to-all-done.2
  363.4 3.6 convolution_bitcast_fusion.4
  367.0 9.9 %copy.143 = f32[64,64,1,448]{3,2,1,0:T(1,128)} copy(f32[64,64,1,448]{3,0,1,2:T(8,128)S(1)} %convolution_bitcast_fusion.4) | data formatting | bytes 14680064
  (188 shorter events, 56.3 us)
Async XLA Ops:
  7.2 20.4 %copy-start = (bf16[192,3584]{1,0:T(8,128)(2,1)S(1)}, bf16[192,3584]{1,0:T(8,128)(2,1)}, u32[]{:S(2)}) copy-start(bf16[192,3584]{1,0:T(8,128)(2,1)} %param.21) | copy-start | bytes 4128772
  7.2 54.9 %all-gather.5.cloned.1.call-start = ((), (), s32[]{:S(2)}) async-start(), calls=%async_computation.9 | async-start | bytes 1720320 | tf_op jit(solution)/shard_map/all_gather | solution.py:242
  12.7 21.3 %copy-start.10 = (s32[2,3]{1,0:T(2,128)S(1)}, s32[2,3]{1,0:T(2,128)}, u32[]{:S(2)}) copy-start(s32[2,3]{1,0:T(2,128)} %param.25) | copy-start | bytes 76
  12.7 49.4 %copy-start.2 = (bf16[1,256,3584]{2,1,0:T(8,128)(2,1)S(1)}, bf16[1,256,3584]{2,1,0:T(8,128)(2,1)}, u32[]{:S(2)}) copy-start(bf16[1,256,3584]{2,1,0:T(8,128)(2,1)} %param.20) | copy-start | bytes 5505028
  27.5 124.1 %all-gather.3.cloned.1.call-start = ((), (), s32[]{:S(2)}) async-start(), calls=%async_computation.8 | async-start | bytes 5849088 | tf_op jit(solution)/shard_map/all_gather | solution.py:234
  30.6 127.1 %all-to-all-start.1 = ((bf16[2,3,32,80]{3,2,1,0:T(8,128)(2,1)}), bf16[2,3,32,80]{3,2,1,0:T(8,128)(2,1)S(1)}, u32[]{:S(2)}, u32[]{:S(2)}) async-start(bf16[2,3,32,80]{3,2,1,0:T(8,128)(2,1)} %bitcast.34), calls=%async_computation.2 | async-start | bytes 98304 | tf_op jit(solution)/shard_map/all_to_all | solution.py:239
  33.9 137.9 %reduce-scatter.5.cloned.1.call-start = ((), (), s32[]{:S(2)}) async-start(), calls=%async_computation.10 | async-start | bytes 1277952 | tf_op jit(solution)/shard_map/reduce_scatter | solution.py:261
  62.1 2.7 copy-start.4
  155.8 1.8 copy-start.9
  156.8 104.4 %reduce-scatter.7.cloned.1.call-start = ((), (), s32[]{:S(2)}) async-start(), calls=%async_computation.11 | async-start | bytes 1179648 | tf_op jit(solution)/shard_map/reduce_scatter | solution.py:321
  172.9 15.9 %copy-start.6 = (f32[128,832]{0,1:T(8,128)S(1)}, f32[128,832]{0,1:T(8,128)}, u32[]{:S(2)}) copy-start(f32[128,832]{0,1:T(8,128)} %reduce-scatter.5.cloned.1.call-done) | copy-start | bytes 1277956
  228.5 61.5 %reduce-scatter.11.cloned.1.call-start = ((), (), s32[]{:S(2)}) async-start(), calls=%async_computation.13 | async-start | bytes 409600 | tf_op jit(solution)/shard_map/reduce_scatter | solution.py:396
  228.7 37.3 %copy-start.3 = (bf16[1,256,3584]{2,1,0:T(8,128)(2,1)S(1)}, bf16[1,256,3584]{2,1,0:T(8,128)(2,1)}, u32[]{:S(2)}) copy-start(bf16[1,256,3584]{2,1,0:T(8,128)(2,1)} %param.20) | copy-start | bytes 5505028
  271.4 73.9 %reduce-scatter.9.cloned.1.call-start = ((), (), s32[]{:S(2)}) async-start(), calls=%async_computation.12 | async-start | bytes 3440640 | tf_op jit(solution)/shard_map/reduce_scatter | solution.py:392
  274.2 1.4 copy-start.5
  291.7 56.5 %all-to-all-start.3 = ((f32[2,3,32,80]{3,2,1,0:T(8,128)}), f32[2,3,32,80]{3,2,1,0:T(8,128)S(1)}, u32[]{:S(2)}, u32[]{:S(2)}) async-start(f32[2,3,32,80]{3,2,1,0:T(8,128)} %copy.141), calls=%async_computation.7 | async-start | bytes 196608 | tf_op jit(solution)/shard_map/all_to_all | solution.py:413
  347.2 4.6 %copy-start.7 = (f32[256,896]{1,0:T(8,128)S(1)}, f32[256,896]{1,0:T(8,128)}, u32[]{:S(2)}) copy-start(f32[256,896]{1,0:T(8,128)} %fusion.67) | copy-start | bytes 2752516
  347.2 4.6 %copy-start.8 = (f32[256,896]{1,0:T(8,128)S(1)}, f32[256,896]{1,0:T(8,128)}, u32[]{:S(2)}) copy-start(f32[256,896]{1,0:T(8,128)} %fusion.66) | copy-start | bytes 2752516
  348.2 14.4 %all-to-all-start.2 = ((f32[2,3,64,448]{3,2,1,0:T(8,128)}), f32[2,3,64,448]{3,2,1,0:T(8,128)S(1)}, u32[]{:S(2)}, u32[]{:S(2)}) async-start(f32[2,3,64,448]{3,2,1,0:T(8,128)} %bitcast.202), calls=%async_computation.5 | async-start | bytes 1572864 | tf_op jit(solution)/shard_map/all_to_all | solution.py:412
  367.0 9.9 %copy-start.1 = (bf16[192,3584]{1,0:T(8,128)(2,1)S(1)}, bf16[192,3584]{1,0:T(8,128)(2,1)}, u32[]{:S(2)}) copy-start(bf16[192,3584]{1,0:T(8,128)(2,1)} %param.21) | copy-start | bytes 4128772
Sparse Core Ops, SparseCore 0:
  27.6 34.3 all-gather.4
  65.4 86.1 all-gather.2
  156.9 6.7 reduce-scatter.4
  228.6 32.5 reduce-scatter.6
  271.5 18.4 reduce-scatter.10
  292.8 52.4 reduce-scatter.8

commit v2 on v0

v2 whole, which is shorter than its diff:
```python
import functools

import jax
import jax.numpy as jnp
from jax import lax
from jax.experimental import pallas as pl
from jax.experimental.pallas import tpu as pltpu
from jax.sharding import PartitionSpec as P

QHEADS = 4
HEAD_WIDTH = 128
ADAPTER_RANK = 32
SEGS = 3

adapter_scale = 2.0
rope_base = 5000000.0
masked_score = -1e30
vmem_limit = 48 * 1024 * 1024


def shift(value, axis, steps):
    count = lax.axis_size(axis)
    return lax.ppermute(value, axis, [(at, (at + steps) % count) for at in range(count)])


def push(value, axis, steps):
    count = lax.axis_size(axis)
    pairs = [(at, at + steps) for at in range(count) if 0 <= at + steps < count]
    return lax.ppermute(value, axis, pairs)


def dot_nt(left, right):
    return lax.dot_general(
        left, right, (((1,), (1,)), ((), ())), preferred_element_type=jnp.float32
    )


def dot_nn(left, right):
    return jnp.dot(left, right, preferred_element_type=jnp.float32)


def dot_tn(left, right):
    return lax.dot_general(
        left, right, (((0,), (0,)), ((), ())), preferred_element_type=jnp.float32
    )


def lookup_rows(adapter_bank_row, document_adapter):
    matches = document_adapter[..., None] == jnp.arange(adapter_bank_row.shape[0], dtype=jnp.int32)
    return jnp.sum(jnp.where(matches, adapter_bank_row, 0), axis=-1)


def row_positions(first, count):
    return first + lax.broadcasted_iota(jnp.int32, (count, 1), 0)


def row_segments(marks, positions):
    return (positions >= marks[0]).astype(jnp.int32) + (positions >= marks[1]).astype(jnp.int32)


def cost(flops, bytes_accessed, transcendentals=0):
    return pl.CostEstimate(
        flops=flops, bytes_accessed=bytes_accessed, transcendentals=transcendentals
    )


def in_vmem():
    return pl.BlockSpec(memory_space=pltpu.VMEM)


def in_smem():
    return pl.BlockSpec(memory_space=pltpu.SMEM)


def in_place():
    return pl.BlockSpec(memory_space=pl.ANY)


def fetch_pieces(offsets, pieces, target, semaphore, first):
    copies = []
    for number, piece in enumerate(pieces):
        height, width = piece.shape
        row = pl.multiple_of(offsets[first + number, 0], 16)
        column = pl.multiple_of(offsets[first + number, 1], 128)
        copy = pltpu.make_async_copy(
            piece,
            target.at[pl.ds(row, height), pl.ds(column, width)],
            semaphore.at[first + number],
        )
        copy.start()
        copies.append(copy)
    return copies


def project_kernel(frozen_count, down_count, marks, offsets, tokens, *refs):
    frozen_pieces = refs[:frozen_count]
    down_pieces = refs[frozen_count : frozen_count + down_count]
    part, frozen, down, semaphore = refs[frozen_count + down_count :]
    copies = fetch_pieces(offsets, frozen_pieces, frozen, semaphore, 0)
    copies += fetch_pieces(offsets, down_pieces, down, semaphore, frozen_count)
    for copy in copies:
        copy.wait()
    rows = tokens.shape[0]
    features = frozen.shape[0]
    joint_rank = down.shape[0] // 2
    positions = row_positions(marks[2] * rows, rows)
    second = row_segments(marks, positions) != marks[6]
    values = tokens[...]
    part[:, :features] = dot_nt(values, frozen[...])
    first_low = dot_nt(values, down[:joint_rank])
    second_low = dot_nt(values, down[joint_rank:])
    part[:, features:] = jnp.where(second, second_low, first_low)


def rotated(values, cosines, sines):
    return values * cosines + pltpu.roll(values, values.shape[1] // 2, 1) * sines


def qkv_kernel(marks, mine, theirs, up_blocks, cosines, sines, queries, pairs, low_rank):
    rows = mine.shape[0]
    own_rows = queries.shape[0] // QHEADS
    query_columns = QHEADS * HEAD_WIDTH
    value_start = query_columns + HEAD_WIDTH
    features = value_start + HEAD_WIDTH
    segments = row_segments(marks, row_positions(marks[2] * rows, rows))
    low = (mine[:, features:] + theirs[:, features:]).astype(jnp.bfloat16)
    low_rank[...] = low
    value_delta = jnp.zeros((rows, HEAD_WIDTH), jnp.float32)
    for document in range(SEGS):
        chosen = jnp.where(segments == document, low, jnp.zeros_like(low))
        value_delta += dot_nn(chosen, up_blocks[document, :, query_columns:])
    keys = mine[:, query_columns:value_start] + theirs[:, query_columns:value_start]
    pairs[:, :HEAD_WIDTH] = rotated(keys, cosines[...], sines[...]).astype(jnp.bfloat16)
    values = mine[:, value_start:features] + theirs[:, value_start:features]
    pairs[:, HEAD_WIDTH:] = (values + adapter_scale * value_delta).astype(jnp.bfloat16)
    start = pl.multiple_of(marks[3] * own_rows, own_rows)
    own = pl.ds(start, own_rows)
    own_segments = row_segments(marks, row_positions(marks[2] * rows + start, own_rows))
    own_low = (mine[own, features:] + theirs[own, features:]).astype(jnp.bfloat16)
    query_delta = jnp.zeros((own_rows, query_columns), jnp.float32)
    for document in range(SEGS):
        chosen = jnp.where(own_segments == document, own_low, jnp.zeros_like(own_low))
        query_delta += dot_nn(chosen, up_blocks[document, :, :query_columns])
    projected = mine[own, :query_columns] + theirs[own, :query_columns]
    projected = projected + adapter_scale * query_delta
    for head in range(QHEADS):
        turned = rotated(
            projected[:, head * HEAD_WIDTH : (head + 1) * HEAD_WIDTH], cosines[own], sines[own]
        )
        queries[head * own_rows : (head + 1) * own_rows] = turned.astype(jnp.bfloat16)


def attention_kernel(block_count, marks, queries, incoming, cosines, sines, *refs):
    blocks = refs[:block_count]
    output, query_grad, kept, sent, low_probs = refs[block_count:]
    own_rows, query_columns = incoming.shape
    rows = blocks[0].shape[0]
    score_scale = HEAD_WIDTH ** (-0.5)
    first = marks[2] * rows + marks[3] * own_rows
    positions = row_positions(first, own_rows)
    positions = jnp.concatenate([positions] * QHEADS, axis=0)
    segments = row_segments(marks, positions)
    starts = jnp.where(segments == 0, 0, jnp.where(segments == 1, marks[0], marks[1]))
    scores = []
    for back, block in enumerate(blocks):
        key_positions = (marks[2] - back) * rows + lax.broadcasted_iota(jnp.int32, (1, rows), 1)
        allowed = (key_positions <= positions) & (key_positions >= starts)
        block_scores = dot_nt(queries[...], block[:, :HEAD_WIDTH]) * score_scale
        scores.append(jnp.where(allowed, block_scores, masked_score))
    row_max = functools.reduce(
        jnp.maximum, [jnp.max(part, axis=1, keepdims=True) for part in scores]
    )
    raised = [jnp.exp(part - row_max) for part in scores]
    row_total = sum(jnp.sum(part, axis=1, keepdims=True) for part in raised)
    inverse = 1.0 / row_total
    probs = [part * inverse for part in raised]
    weighted = jnp.zeros((QHEADS * own_rows, HEAD_WIDTH), jnp.float32)
    for back, block in enumerate(blocks):
        low_probs[back] = probs[back].astype(jnp.bfloat16)
        weighted += dot_nn(low_probs[back], block[:, HEAD_WIDTH:])
    attended = weighted.astype(jnp.bfloat16)
    gradients = jnp.concatenate(
        [incoming[:, head * HEAD_WIDTH : (head + 1) * HEAD_WIDTH] for head in range(QHEADS)],
        axis=0,
    )
    row_delta = jnp.sum(
        gradients.astype(jnp.float32) * attended.astype(jnp.float32), axis=1, keepdims=True
    )
    start = pl.multiple_of(marks[3] * own_rows, own_rows)
    other = pl.multiple_of(own_rows - start, own_rows)
    total = jnp.zeros((QHEADS * own_rows, HEAD_WIDTH), jnp.float32)
    for back, block in enumerate(blocks):
        prob_grad = dot_nt(gradients, block[:, HEAD_WIDTH:])
        score_grad = (probs[back] * (prob_grad - row_delta)).astype(jnp.bfloat16)
        total += dot_nn(score_grad, block[:, :HEAD_WIDTH])
        key_part = dot_tn(score_grad, queries[...]) * score_scale
        value_part = dot_tn(low_probs[back], gradients)
        mine = marks[3] == 0
        kept[back, :, :HEAD_WIDTH] = jnp.where(mine, key_part[:own_rows], key_part[own_rows:])
        sent[back, :, :HEAD_WIDTH] = jnp.where(mine, key_part[own_rows:], key_part[:own_rows])
        kept[back, :, HEAD_WIDTH:] = jnp.where(mine, value_part[:own_rows], value_part[own_rows:])
        sent[back, :, HEAD_WIDTH:] = jnp.where(mine, value_part[own_rows:], value_part[:own_rows])
    own = pl.ds(start, own_rows)
    for head in range(QHEADS):
        picked = slice(head * own_rows, (head + 1) * own_rows)
        columns = slice(head * HEAD_WIDTH, (head + 1) * HEAD_WIDTH)
        output[:, columns] = attended[picked]
        query_grad[:, columns] = rotated(
            total[picked] * score_scale, cosines[own], -sines[own]
        ).astype(jnp.bfloat16)


def rank_kernel(
    marks, own_query, other_query, own_pair, other_pair, low_rank, up_blocks,
    gradients, rank_grad, up_terms,
):
    own_rows, query_columns = own_query.shape
    rows = low_rank.shape[0]
    start = pl.multiple_of(marks[3] * own_rows, own_rows)
    other = pl.multiple_of(own_rows - start, own_rows)
    gradients[pl.ds(start, own_rows), :query_columns] = own_query[...]
    gradients[pl.ds(other, own_rows), :query_columns] = other_query[...]
    gradients[pl.ds(start, own_rows), query_columns:] = own_pair[...]
    gradients[pl.ds(other, own_rows), query_columns:] = other_pair[...]
    query_grad = gradients[:, :query_columns]
    value_grad = gradients[:, query_columns + HEAD_WIDTH :]
    low = low_rank[...]
    rank = low.shape[1] // 2
    segments = row_segments(marks, row_positions(marks[2] * rows, rows))
    total = jnp.zeros((rows, low.shape[1]), jnp.float32)
    for document in range(SEGS):
        member = segments == document
        terms = dot_nt(query_grad, up_blocks[document, :, :query_columns])
        terms += dot_nt(value_grad, up_blocks[document, :, query_columns:])
        total = jnp.where(member, terms, total)
        chosen = jnp.where(member, low, jnp.zeros_like(low))
        query_terms = dot_tn(chosen, query_grad)
        value_terms = dot_tn(chosen, value_grad)
        place = slice(document * rank, (document + 1) * rank)
        up_terms[place, :query_columns] = adapter_scale * query_terms[:rank]
        up_terms[place, query_columns:] = adapter_scale * value_terms[rank:]
    rank_grad[...] = (adapter_scale * total).astype(jnp.bfloat16)


def token_kernel(frozen_count, down_count, marks, offsets, gradients, rank_grad, *refs):
    frozen_pieces = refs[:frozen_count]
    down_pieces = refs[frozen_count : frozen_count + down_count]
    token_grad, frozen, down, semaphore = refs[frozen_count + down_count :]
    copies = fetch_pieces(offsets, frozen_pieces, frozen, semaphore, 0)
    copies += fetch_pieces(offsets, down_pieces, down, semaphore, frozen_count)
    for copy in copies:
        copy.wait()
    rows = gradients.shape[0]
    joint_rank = down.shape[0] // 2
    second = row_segments(marks, row_positions(marks[2] * rows, rows)) != marks[6]
    low = rank_grad[...]
    nothing = jnp.zeros_like(low)
    first_low = jnp.where(second, nothing, low)
    second_low = jnp.where(second, low, nothing)
    chunk = 512
    for column in range(0, token_grad.shape[1], chunk):
        columns = slice(column, column + chunk)
        total = dot_nn(gradients[...], frozen[:, columns])
        total += dot_nn(first_low, down[:joint_rank, columns])
        total += dot_nn(second_low, down[joint_rank:, columns])
        token_grad[:, columns] = total.astype(jnp.bfloat16)


def down_kernel(block_count, marks, *refs):
    ranks = refs[:block_count]
    columns = refs[block_count : 2 * block_count]
    terms = refs[2 * block_count]
    rows, joint_rank = ranks[0].shape
    for document in range(SEGS):
        total = jnp.zeros((joint_rank, terms.shape[1]), jnp.float32)
        for behind in range(block_count):
            holder = marks[2] - behind
            holder = jnp.where(holder < 0, holder + block_count, holder)
            segments = row_segments(marks, row_positions(holder * rows, rows))
            low = ranks[behind][...]
            chosen = jnp.where(segments == document, low, jnp.zeros_like(low))
            total += dot_tn(chosen, columns[behind][...])
        terms[document * joint_rank : (document + 1) * joint_rank] = total


def bank_kernel(block_count, bank_rows, *refs):
    down_terms = refs[:block_count]
    up_terms = refs[block_count : 2 * block_count]
    down_out, up_out = refs[2 * block_count + 2 :]
    step = pl.program_id(0)
    joint_rank = down_out.shape[1]
    low_width = up_out.shape[1]
    down_total = jnp.zeros((joint_rank, down_out.shape[3]), jnp.float32)
    up_total = jnp.zeros((low_width, up_out.shape[2]), jnp.float32)
    for block in range(block_count):
        for document in range(SEGS):
            same = bank_rows[block * SEGS + document] == bank_rows[step]
            down_rows = down_terms[block][document * joint_rank : (document + 1) * joint_rank]
            up_rows = up_terms[block][document * low_width : (document + 1) * low_width]
            down_total += jnp.where(same, down_rows, 0.0)
            up_total += jnp.where(same, up_rows, 0.0)
    down_out[0, :, 0, :] = down_total
    up_out[0] = up_total


def shards(
    tokens,
    frozen_qkv_matrix,
    adapter_down_weight,
    adapter_up_weight,
    adapter_bank_row,
    document_lengths,
    document_adapter,
    output_gradient,
):
    seq_count = lax.axis_size("seq")
    batch_count = lax.axis_size("batch")
    group_count = lax.axis_size("groups")
    chip_size = lax.axis_size("tp")
    seq_index = lax.axis_index("seq")
    batch_index = lax.axis_index("batch")
    group_index = lax.axis_index("groups")
    tp_index = lax.axis_index("tp")
    local_tokens = tokens[0]
    rows, width = local_tokens.shape
    own_rows = rows // chip_size
    query_columns = QHEADS * HEAD_WIDTH
    frozen_rows = frozen_qkv_matrix.shape[0]
    features = frozen_rows * seq_count
    low_width = ADAPTER_RANK
    joint_rank = adapter_down_weight.shape[1]
    adapters = adapter_bank_row.shape[0]
    bf16 = jnp.bfloat16
    f32 = jnp.float32

    sample_rows = lookup_rows(adapter_bank_row, document_adapter)
    lengths = lax.dynamic_index_in_dim(document_lengths, batch_index, 0, keepdims=False)
    ends = jnp.cumsum(lengths)
    half_count = seq_count // 2

    def first_document(holder):
        return (holder >= half_count).astype(jnp.int32)

    marks = jnp.stack(
        [
            ends[0],
            ends[1],
            seq_index,
            tp_index,
            batch_index,
            group_index,
            first_document(seq_index),
            jnp.int32(0),
        ]
    ).astype(jnp.int32)

    plane_count = group_count * batch_count
    share = width // plane_count
    pieces, places = [], []
    direct = group_count == 2 and batch_count == 2 and share % 128 == 0 and frozen_rows % 16 == 0
    if direct:
        own_share = lax.dynamic_slice_in_dim(
            frozen_qkv_matrix, (group_index * batch_count + batch_index) * share, share, axis=1
        )
        pieces.append(frozen_qkv_matrix)
        places.append((seq_index * frozen_rows, 0))
        for steps in range(1, seq_count):
            holder = jnp.remainder(seq_index - steps, seq_count)
            here = shift(own_share, "seq", steps)
            if steps % 2 == 1:
                over_batch = shift(here, "batch", 1)
                over_groups = shift(here, "groups", 1)
                over_both = shift(over_batch, "groups", 1)
            else:
                over_groups = shift(here, "groups", 1)
                over_batch = shift(here, "batch", 1)
                over_both = shift(over_groups, "batch", 1)
            for value, group, batch in (
                (here, group_index, batch_index),
                (over_batch, group_index, 1 - batch_index),
                (over_groups, 1 - group_index, batch_index),
                (over_both, 1 - group_index, 1 - batch_index),
            ):
                pieces.append(value)
                places.append((holder * frozen_rows, (group * batch_count + batch) * share))
    else:
        pieces.append(lax.all_gather(frozen_qkv_matrix, "seq", axis=0, tiled=True))
        places.append((0, 0))
    frozen_count = len(pieces)

    down_bank = adapter_down_weight[:, :, 0, :]
    if batch_count == 2:
        own_bank = lax.dynamic_index_in_dim(sample_rows, batch_index, 0, keepdims=False)
        other_bank = lax.dynamic_index_in_dim(sample_rows, 1 - batch_index, 0, keepdims=False)
        own_down, own_up = down_bank[own_bank], adapter_up_weight[own_bank]
        far_down = shift(down_bank[other_bank], "batch", 1)
        far_up = shift(adapter_up_weight[other_bank], "batch", 1)
        ahead = batch_index == 0
        down_block = jnp.concatenate(
            [jnp.where(ahead, own_down, far_down), jnp.where(ahead, far_down, own_down)], axis=2
        )
        up_block = jnp.concatenate(
            [jnp.where(ahead, own_up, far_up), jnp.where(ahead, far_up, own_up)], axis=2
        )
    else:
        got_down = lax.all_to_all(
            down_bank[sample_rows], "batch", split_axis=0, concat_axis=0, tiled=True
        )
        got_up = lax.all_to_all(
            adapter_up_weight[sample_rows], "batch", split_axis=0, concat_axis=0, tiled=True
        )
        down_block = jnp.transpose(got_down, (1, 2, 0, 3)).reshape(SEGS, joint_rank, -1)
        up_block = jnp.transpose(got_up, (1, 2, 0, 3)).reshape(SEGS, low_width, -1)
    down_block = down_block.reshape(SEGS * joint_rank, -1)
    up_block = up_block.reshape(SEGS * low_width, -1)
    down_width = down_block.shape[1]
    down_parts, down_places, up_parts = [], [], []
    for steps in range(seq_count):
        target = jnp.remainder(seq_index + steps, seq_count)
        holder = jnp.remainder(seq_index - steps, seq_count)
        part = lax.dynamic_slice_in_dim(
            down_block, first_document(target) * joint_rank, 2 * joint_rank
        )
        down_parts.append(shift(part, "seq", steps) if steps else part)
        down_places.append((0, holder * down_width))
        up_parts.append(shift(up_block, "seq", steps) if steps else up_block)
    relative = jnp.remainder(seq_index - jnp.arange(seq_count, dtype=jnp.int32), seq_count)
    up_rows = jnp.stack(up_parts)[relative]
    up_rows = jnp.transpose(up_rows, (1, 0, 2)).reshape(SEGS, low_width, -1)
    is_query = jnp.arange(up_rows.shape[2]) < query_columns
    up_blocks = jnp.concatenate(
        [
            jnp.where(is_query[None, None, :], up_rows, 0),
            jnp.where(is_query[None, None, :], 0, up_rows),
        ],
        axis=1,
    )
    if down_width % 128 != 0:
        merged = jnp.stack(down_parts)[relative]
        merged = jnp.transpose(merged, (1, 0, 2)).reshape(2 * joint_rank, -1)
        down_parts, down_places = [merged], [(0, 0)]
    down_count = len(down_parts)
    offsets = jnp.stack(
        [jnp.stack([jnp.int32(0) + row, jnp.int32(0) + column]) for row, column in places + down_places]
    ).astype(jnp.int32)

    positions = seq_index * rows + jnp.arange(rows, dtype=jnp.int32)
    inside = positions - jnp.where(
        positions >= ends[1], ends[1], jnp.where(positions >= ends[0], ends[0], 0)
    )
    exponent = jnp.arange(HEAD_WIDTH // 2, dtype=f32) * (2.0 / HEAD_WIDTH)
    angles = inside.astype(f32)[:, None] * jnp.power(jnp.float32(rope_base), -exponent)[None, :]
    cosines = jnp.tile(jnp.cos(angles), (1, 2))
    sines = jnp.concatenate([-jnp.sin(angles), jnp.sin(angles)], axis=1)

    scratch = [
        pltpu.VMEM((features, width), bf16),
        pltpu.VMEM((2 * joint_rank, width), bf16),
        pltpu.SemaphoreType.DMA((frozen_count + down_count,)),
    ]
    weight_bytes = 2 * width * (features + 2 * joint_rank)
    part = pl.pallas_call(
        functools.partial(project_kernel, frozen_count, down_count),
        out_shape=jax.ShapeDtypeStruct((rows, features + joint_rank), f32),
        in_specs=[in_smem(), in_smem(), in_vmem()] + [in_place()] * (frozen_count + down_count),
        out_specs=in_vmem(),
        scratch_shapes=scratch,
        compiler_params=pltpu.CompilerParams(vmem_limit_bytes=vmem_limit),
        cost_estimate=cost(
            2 * rows * width * (features + 2 * joint_rank), weight_bytes + 2 * rows * width
        ),
        name="project",
    )(marks, offsets, local_tokens, *pieces, *down_parts)

    part, late_tokens = lax.optimization_barrier((part, local_tokens))
    column_parts = []
    for steps in range(seq_count):
        target = jnp.remainder(seq_index + steps, seq_count)
        part_columns = lax.dynamic_slice_in_dim(
            late_tokens, target * down_width, down_width, axis=1
        )
        column_parts.append(shift(part_columns, "seq", steps) if steps else part_columns)

    other_part = shift(part, "tp", 1)
    queries, pairs, low_rank = pl.pallas_call(
        qkv_kernel,
        out_shape=(
            jax.ShapeDtypeStruct((QHEADS * own_rows, HEAD_WIDTH), bf16),
            jax.ShapeDtypeStruct((rows, 2 * HEAD_WIDTH), bf16),
            jax.ShapeDtypeStruct((rows, joint_rank), bf16),
        ),
        in_specs=[in_smem()] + [in_vmem()] * 5,
        out_specs=(in_vmem(),) * 3,
        compiler_params=pltpu.CompilerParams(vmem_limit_bytes=vmem_limit),
        cost_estimate=cost(2 * rows * 3 * 64 * 640, 8 * rows * features),
        name="qkv",
    )(marks, part, other_part, up_blocks, cosines, sines)

    blocks = [pairs] + [push(pairs, "seq", back) for back in range(1, half_count + 1)]
    block_count = len(blocks)
    incoming = output_gradient[0]
    attention, query_grad, kept, sent = pl.pallas_call(
        functools.partial(attention_kernel, block_count),
        out_shape=(
            jax.ShapeDtypeStruct((own_rows, query_columns), bf16),
            jax.ShapeDtypeStruct((own_rows, query_columns), bf16),
            jax.ShapeDtypeStruct((block_count, own_rows, 2 * HEAD_WIDTH), f32),
            jax.ShapeDtypeStruct((block_count, own_rows, 2 * HEAD_WIDTH), f32),
        ),
        in_specs=[in_smem()] + [in_vmem()] * (4 + block_count),
        out_specs=(in_vmem(),) * 4,
        scratch_shapes=[pltpu.VMEM((block_count, QHEADS * own_rows, rows), bf16)],
        compiler_params=pltpu.CompilerParams(vmem_limit_bytes=vmem_limit),
        cost_estimate=cost(
            10 * block_count * QHEADS * own_rows * rows * HEAD_WIDTH,
            4 * rows * features,
            block_count * QHEADS * own_rows * rows,
        ),
        name="attention",
    )(marks, queries, incoming, cosines, sines, *blocks)

    other_query = shift(query_grad, "tp", 1)
    pair_sums = kept + shift(sent, "tp", 1)
    own_sum = pair_sums[0]
    for back in range(1, block_count):
        own_sum = own_sum + push(pair_sums[back], "seq", -back)
    own_place = tp_index * own_rows
    own_cosines = lax.dynamic_slice_in_dim(cosines, own_place, own_rows)
    own_sines = lax.dynamic_slice_in_dim(sines, own_place, own_rows)
    key_grad = own_sum[:, :HEAD_WIDTH]
    key_grad = key_grad * own_cosines - jnp.roll(key_grad, HEAD_WIDTH // 2, axis=1) * own_sines
    pair_grad = jnp.concatenate([key_grad, own_sum[:, HEAD_WIDTH:]], axis=1).astype(bf16)
    other_pair = shift(pair_grad, "tp", 1)

    gradients, rank_grad, up_terms = pl.pallas_call(
        rank_kernel,
        out_shape=(
            jax.ShapeDtypeStruct((rows, features), bf16),
            jax.ShapeDtypeStruct((rows, joint_rank), bf16),
            jax.ShapeDtypeStruct((SEGS * low_width, features - HEAD_WIDTH), f32),
        ),
        in_specs=[in_smem()] + [in_vmem()] * 6,
        out_specs=(in_vmem(),) * 3,
        compiler_params=pltpu.CompilerParams(vmem_limit_bytes=vmem_limit),
        cost_estimate=cost(4 * rows * 3 * 64 * 640, 4 * rows * features),
        name="rank_gradients",
    )(marks, query_grad, other_query, pair_grad, other_pair, low_rank, up_blocks)

    rank_parts = [rank_grad] + [shift(rank_grad, "seq", steps) for steps in range(1, seq_count)]
    up_split = jnp.transpose(
        up_terms.reshape(SEGS * low_width, seq_count, -1), (1, 0, 2)
    )
    up_sum = lax.dynamic_index_in_dim(up_split, seq_index, 0, keepdims=False)
    for steps in range(1, seq_count):
        target = jnp.remainder(seq_index + steps, seq_count)
        up_sum = up_sum + shift(
            lax.dynamic_index_in_dim(up_split, target, 0, keepdims=False), "seq", steps
        )

    token_grad = pl.pallas_call(
        functools.partial(token_kernel, frozen_count, down_count),
        out_shape=jax.ShapeDtypeStruct((rows, width), bf16),
        in_specs=[in_smem(), in_smem(), in_vmem(), in_vmem()]
        + [in_place()] * (frozen_count + down_count),
        out_specs=in_vmem(),
        scratch_shapes=scratch,
        compiler_params=pltpu.CompilerParams(vmem_limit_bytes=vmem_limit),
        cost_estimate=cost(
            2 * rows * width * (features + 2 * joint_rank), weight_bytes + 2 * rows * width
        ),
        name="token_gradient",
    )(marks, offsets, gradients, rank_grad, *pieces, *down_parts)

    down_terms = pl.pallas_call(
        functools.partial(down_kernel, seq_count),
        out_shape=jax.ShapeDtypeStruct((SEGS * joint_rank, down_width), f32),
        in_specs=[in_smem()] + [in_vmem()] * (2 * seq_count),
        out_specs=in_vmem(),
        compiler_params=pltpu.CompilerParams(vmem_limit_bytes=vmem_limit),
        cost_estimate=cost(
            2 * seq_count * rows * SEGS * joint_rank * down_width, 2 * seq_count * rows * down_width
        ),
        name="down_terms",
    )(marks, *rank_parts, *column_parts)

    held_down = down_width // batch_count
    held_up = up_sum.shape[1] // batch_count
    if batch_count == 2:
        ahead = batch_index == 0
        own_terms = jnp.where(ahead, down_terms[:, :held_down], down_terms[:, held_down:])
        far_terms = jnp.where(ahead, down_terms[:, held_down:], down_terms[:, :held_down])
        own_ups = jnp.where(ahead, up_sum[:, :held_up], up_sum[:, held_up:])
        far_ups = jnp.where(ahead, up_sum[:, held_up:], up_sum[:, :held_up])
        bank_downs = [own_terms, shift(far_terms, "batch", 1)]
        bank_ups = [own_ups, shift(far_ups, "batch", 1)]
        bank_rows = jnp.concatenate([own_bank, other_bank])
    else:
        down_send = jnp.transpose(
            down_terms.reshape(SEGS * joint_rank, batch_count, held_down), (1, 0, 2)
        )
        up_send = jnp.transpose(
            up_sum.reshape(SEGS * low_width, batch_count, held_up), (1, 0, 2)
        )
        back_down = lax.all_to_all(down_send, "batch", split_axis=0, concat_axis=0, tiled=True)
        back_up = lax.all_to_all(up_send, "batch", split_axis=0, concat_axis=0, tiled=True)
        bank_downs = [back_down[batch] for batch in range(batch_count)]
        bank_ups = [back_up[batch] for batch in range(batch_count)]
        bank_rows = sample_rows.reshape(-1)
    down_zeros = jnp.zeros((adapters, joint_rank, 1, held_down), f32)
    up_zeros = jnp.zeros((adapters, low_width, held_up), f32)

    def whole(array):
        return pl.BlockSpec(array.shape, lambda step, bank: (0,) * array.ndim)

    down_grad, up_grad = pl.pallas_call(
        functools.partial(bank_kernel, batch_count),
        out_shape=(
            jax.ShapeDtypeStruct(down_zeros.shape, f32),
            jax.ShapeDtypeStruct(up_zeros.shape, f32),
        ),
        grid_spec=pltpu.PrefetchScalarGridSpec(
            num_scalar_prefetch=1,
            grid=(batch_count * SEGS,),
            in_specs=[whole(array) for array in bank_downs + bank_ups] + [in_place()] * 2,
            out_specs=(
                pl.BlockSpec(
                    (1, joint_rank, 1, held_down), lambda step, bank: (bank[step], 0, 0, 0)
                ),
                pl.BlockSpec((1, low_width, held_up), lambda step, bank: (bank[step], 0, 0)),
            ),
        ),
        input_output_aliases={1 + 2 * batch_count: 0, 2 + 2 * batch_count: 1},
        compiler_params=pltpu.CompilerParams(vmem_limit_bytes=vmem_limit),
        name="bank_rows",
    )(bank_rows, *bank_downs, *bank_ups, down_zeros, up_zeros)
    return (attention[None], token_grad[None], down_grad, up_grad)


def solution(mesh):
    in_specs = (
        P(("groups", "batch"), "seq", "tp"),
        P("seq", "tp"),
        P(None, None, "tp", ("seq", "batch")),
        P(None, None, ("seq", "batch")),
        P(),
        P("groups", None),
        P("groups", None),
        P(("groups", "batch"), ("seq", "tp"), None),
    )
    out_specs = (
        P(("groups", "batch"), ("seq", "tp"), None),
        P(("groups", "batch"), "seq", "tp"),
        P("groups", None, "tp", ("seq", "batch")),
        P("groups", None, ("seq", "batch")),
    )
    return jax.shard_map(shards, mesh=mesh, in_specs=in_specs, out_specs=out_specs, check_vma=False)
```

time: 390 us -> 223 us (0.57)
  waiting for transfers between devices: 226 us -> 48.2 us
  starting transfers between devices: 19.9 us -> 75.6 us
  matrix products: 32.7 us -> 0 us
  blocking collectives: 30.4 us -> 0 us
  Pallas kernels: 0 us -> 23.5 us
  local copies, waits for them, and re-layouts: 41.1 us -> 60.6 us
  between operations: 16 us -> 1.25 us
  loops' own time: 5.89 us -> 0 us
  other arithmetic: 16.8 us -> 12.8 us
    all_to_all x4 -> x0, waiting for transfers between devices: 134 us -> none  [the longest x1 74.9 us: shards(): lax.all_to_all(outgoing_down, ('seq', 'batch'), split_axis=0, concat_axis...]
    ppermute x7 -> x39, starting transfers between devices: 0.74 us -> 75.6 us  [the longest x35 67.2 us: shift(): lax.ppermute(value, axis, [(at, (at + steps) % count) for at in range(cou...]
    all_gather x1 -> x0, waiting for transfers between devices: 44 us -> none  [shards(): frozen = lax.all_gather(frozen_qkv_matrix, 'seq', axis=0, tiled=True)]
    dot_general x20 -> x0, matrix products: 32.7 us -> none  [the longest x1 7.37 us: shards(): jnp.einsum('na,nx->ax', bank_hot, back_down.reshape(flat_rows.shape[0], -...]
    all_gather x4 -> x0, blocking collectives: 30.4 us -> none  [the longest x1 13.4 us: shards(): lax.all_gather(values_own, ('seq', 'tp'), axis=0, tiled=True)]
    pallas_call x0 -> x7, Pallas kernels: none -> 23.5 us  [the longest x1 6.11 us: shards(): pl.pallas_call(functools.partial(token_kernel, frozen_count, down_count),...]
    all_to_all x4 -> x0, starting transfers between devices: 19 us -> none  [the longest x1 7.38 us: shards(): lax.all_to_all(outgoing_down, ('seq', 'batch'), split_axis=0, concat_axis...]
    another operation x6 -> x10, local copies, waits for them, and re-layouts: 3.98 us -> 12.4 us
  transfers between devices with their start and end apart: 14 -> 39, of which waited for: 12 -> 16; matrix products, arithmetic and copies ran while one was open for 11% -> 19% of each run, Pallas kernels for 0% -> 7%
where the time goes in v2:
time: 223 us; the launch traced here: 222 us
  starting transfers between devices  75.6 us (34%)
  local copies, waits for them, and re-layouts  60.6 us (27%)
  waiting for transfers between devices  48.2 us (22%)
  Pallas kernels  23.5 us (11%)
  other arithmetic  12.8 us (6%)
    ppermute x35, starting transfers between devices, shift(): lax.ppermute(value, axis, [(at, (at + steps) % count) for at in range(cou...  67.2 us
    ppermute x35, waiting for transfers between devices, shift(): lax.ppermute(value, axis, [(at, (at + steps) % count) for at in range(cou...  41 us
    unnamed x93, local copies, waits for them, and re-layouts  21.2 us
    ppermute x4, starting transfers between devices, push(): return lax.ppermute(value, axis, pairs)  8.39 us
    another operation x5, local copies, waits for them, and re-layouts  8.16 us
    ppermute x4, waiting for transfers between devices, push(): return lax.ppermute(value, axis, pairs)  7.2 us
    pallas_call x1, Pallas kernels, shards(): pl.pallas_call(functools.partial(token_kernel, frozen_count, down_count),...  6.11 us
    pallas_call x1, Pallas kernels, shards(): pl.pallas_call(functools.partial(project_kernel, frozen_count, down_count...  5.59 us
  transfers between devices with their start and end apart: 39, of which 16 were waited for; matrix products, arithmetic and copies ran while one was open for 19% of the time, Pallas kernels for 7%

profile of v2, /device:TPU:0, one launch (start us, length us, event | category | flops | bytes accessed | tf_op | source)
XLA Modules:
  0.0 222.0 jit_solution(13498257805438499004)
XLA Ops:
  2.5 5.0 %collective-permute-start.8 = (bf16[192,896]{1,0:T(8,128)(2,1)}, bf16[192,896]{1,0:T(8,128)(2,1)S(1)}, u32[]{:S(2)}, u32[]{:S(2)}) collective-permute-start(bf16[192,896]{1,0:T(8,128)(2,1)} %constant_dynamic-slice_fusion.14), channel_id=1, source_target_pairs={{0,12},{4,0},{8,4},{12,8},{1,13},{5,1},{9,5},{13,9},{2,14},{6,2},{... | collective-permute-start | bytes 1032200 | tf_op jit(solution)/shard_map/ppermute | solution.py:23
  10.4 2.7 %gather_fusion.1 = bf16[3,64,448]{2,1,0:T(8,128)(2,1)S(1)} fusion(bf16[64,64,448]{2,1,0:T(8,128)(2,1)} %bitcast.116, s32[1024]{0:T(1024)S(1)} %pad_clamp_fusion.1), kind=kCustom, calls=%fused_computation.1 | custom fusion | bytes 344076 | tf_op jit(solution)/shard_map/gather | solution.py:396
  17.4 2.7 %gather_fusion = bf16[3,64,448]{2,1,0:T(8,128)(2,1)S(1)} fusion(bf16[64,64,448]{2,1,0:T(8,128)(2,1)} %bitcast.117, s32[1024]{0:T(1024)S(1)} %pad_clamp_fusion.2), kind=kCustom, calls=%fused_computation | custom fusion | bytes 344076 | tf_op jit(solution)/shard_map/gather | solution.py:395
  23.2 2.8 %collective-permute-start.15 = (bf16[128,896]{1,0:T(8,128)(2,1)}, bf16[128,896]{1,0:T(8,128)(2,1)S(1)}, u32[]{:S(2)}, u32[]{:S(2)}) collective-permute-start(bf16[128,896]{1,0:T(8,128)(2,1)} %get-tuple-element.44), channel_id=1, source_target_pairs={{0,12},{4,0},{8,4},{12,8},{1,13},{5,1},{9,5},{13,9},{2,14},{6,2},{... | collective-permute-start | bytes 688136 | tf_op jit(solution)/shard_map/ppermute | solution.py:23
  29.5 13.7 %collective-permute-done.4.refs_5_ = bf16[192,896]{1,0:T(8,128)(2,1)S(1)} collective-permute-done((bf16[192,896]{1,0:T(8,128)(2,1)}, bf16[192,896]{1,0:T(8,128)(2,1)S(1)}, u32[]{:S(2)}, u32[]{:S(2)}) %collective-permute-start.4) | collective-permute-done | bytes 344096 | tf_op jit(solution)/shard_map/ppermute | solution.py:23
  47.4 4.4 %collective-permute-done.14.refs_15_ = bf16[128,896]{1,0:T(8,128)(2,1)S(1)} collective-permute-done((bf16[128,896]{1,0:T(8,128)(2,1)}, bf16[128,896]{1,0:T(8,128)(2,1)S(1)}, u32[]{:S(2)}, u32[]{:S(2)}) %collective-permute-start.14) | collective-permute-done | bytes 229408 | tf_op jit(solution)/shard_map/ppermute | solution.py:23
  74.6 7.4 %collective-permute-done.11.refs_12_ = bf16[192,896]{1,0:T(8,128)(2,1)S(1)} collective-permute-done((bf16[192,896]{1,0:T(8,128)(2,1)S(1)}, bf16[192,896]{1,0:T(8,128)(2,1)S(1)}, u32[]{:S(2)}, u32[]{:S(2)}) %collective-permute-start.11) | collective-permute-done | bytes 344096 | tf_op jit(solution)/shard_map/ppermute | solution.py:23
  82.0 4.6 %collective-permute-done.3.refs_4_ = bf16[192,896]{1,0:T(8,128)(2,1)S(1)} collective-permute-done((bf16[192,896]{1,0:T(8,128)(2,1)S(1)}, bf16[192,896]{1,0:T(8,128)(2,1)S(1)}, u32[]{:S(2)}, u32[]{:S(2)}) %collective-permute-start.3) | collective-permute-done | bytes 344096 | tf_op jit(solution)/shard_map/ppermute | solution.py:23
  91.3 5.6 %project.1.mine = f32[256,832]{1,0:T(8,128)S(1)} custom-call(s32[8]{0:T(128)S(1)} %stack.197.marks, s32[17,2]{1,0:T(8,128)S(1)} %stack.244.offsets, bf16[256,3584]{1,0:T(8,128)(2,1)} %bitcast.101, bf16[192,3584]{1,0:T(8,128)(2,1)} %refs_0_.3, bf16[192,896]{1,0:T(8,128)(2,1)S(1)} %collective-permute-done.refs_1_, bf16[192,896]{1,0:T(8,128)(2,1)S(1)} %copy-done.11, ...), custom_call_target="tpu_custom_call" | custom-call | flops 1644167168 | bytes 8257536 | tf_op jit(solution)/shard_map/project/pallas_call | solution.py:462
  102.8 3.0 %collective-permute-start.20 = (bf16[96,160]{0,1:T(8,128)(2,1)S(1)}, bf16[96,160]{0,1:T(8,128)(2,1)S(1)}, u32[]{:S(2)}, u32[]{:S(2)}) collective-permute-start(bf16[96,160]{0,1:T(8,128)(2,1)S(1)} %copy.115), channel_id=1, source_target_pairs={{0,12},{4,0},{8,4},{12,8},{1,13},{5,1},{9,5},{13,9},{2,14},{6,2},{... | collective-permute-start | bytes 92168 | tf_op jit(solution)/shard_map/ppermute | solution.py:23
  117.9 3.2 %collective-permute-start.22 = (bf16[256,256]{1,0:T(8,128)(2,1)S(1)}, bf16[256,256]{1,0:T(8,128)(2,1)S(1)}, u32[]{:S(2)}, u32[]{:S(2)}) collective-permute-start(bf16[256,256]{1,0:T(8,128)(2,1)S(1)} %get-tuple-element.20.refs_0_), channel_id=1, source_target_pairs={{0,8},{4,12},{1,9},{5,13},{2,10},{6,14},{3,11},{7,15},{16,24},{20,... | collective-permute-start | bytes 393224 | tf_op jit(solution)/shard_map/ppermute | solution.py:29
  121.2 2.6 %collective-permute-start.21 = (bf16[256,256]{1,0:T(8,128)(2,1)S(1)}, bf16[256,256]{1,0:T(8,128)(2,1)S(1)}, u32[]{:S(2)}, u32[]{:S(2)}) collective-permute-start(bf16[256,256]{1,0:T(8,128)(2,1)S(1)} %get-tuple-element.20.refs_0_), channel_id=1, source_target_pairs={{0,4},{4,8},{8,12},{1,5},{5,9},{9,13},{2,6},{6,10},{10,14},{3,7},{... | collective-permute-start | bytes 393224 | tf_op jit(solution)/shard_map/ppermute | solution.py:29
  124.8 2.2 %collective-permute-done.21.refs_1_ = bf16[256,256]{1,0:T(8,128)(2,1)S(1)} collective-permute-done((bf16[256,256]{1,0:T(8,128)(2,1)S(1)}, bf16[256,256]{1,0:T(8,128)(2,1)S(1)}, u32[]{:S(2)}, u32[]{:S(2)}) %collective-permute-start.21) | collective-permute-done | bytes 131104 | tf_op jit(solution)/shard_map/ppermute | solution.py:29
  127.9 3.6 %attention.1 = (bf16[128,512]{1,0:T(8,128)(2,1)}, bf16[128,512]{1,0:T(8,128)(2,1)}, f32[3,128,256]{2,1,0:T(8,128)S(1)}, f32[3,128,256]{2,1,0:T(8,128)S(1)}) custom-call(s32[8]{0:T(128)S(1)} %stack.197.marks, bf16[512,128]{1,0:T(8,128)(2,1)S(1)} %get-tuple-element.19.queries, bf16[128,512]{1,0:T(8,128)(2,1)S(1)} %bitcast.100, f32[256,128]{1,0:T(8,128)S(1)} %copy-done.32, ...), custom_call_target="tpu_custom_call" | custom-call | flops 503316480 | bytes 786432 | tf_op jit(solution)/shard_map/attention/pallas_call | solution.py:502
  135.9 2.6 %constant_dynamic-slice_fusion.4 = (bf16[256,896]{1,0:T(8,128)(2,1)}, bf16[256,896]{1,0:T(8,128)(2,1)}, bf16[256,896]{1,0:T(8,128)(2,1)}, bf16[256,896]{1,0:T(8,128)(2,1)S(1)}) fusion(bf16[256,3584]{1,0:T(8,128)(2,1)} %bitcast.102, s32[]{:T(128)S(6)} %select_n.248, s32[]{:T(128)S(6)} %select_n.247, s32[]{:T(128)S(6)} %select_n.246, s32[]{:T(128)S(6)} %select_n.245), kind=kLoop, calls=%fused_computation.45 | loop fusion | bytes 3670032 | tf_op jit(solution)/shard_map/dynamic_slice | solution.py:479
  138.5 7.4 %collective-permute-start.33 = (bf16[256,896]{1,0:T(8,128)(2,1)}, bf16[256,896]{1,0:T(8,128)(2,1)}, u32[]{:S(2)}, u32[]{:S(2)}) collective-permute-start(bf16[256,896]{1,0:T(8,128)(2,1)} %get-tuple-element.34), channel_id=1, source_target_pairs={{0,12},{4,0},{8,4},{12,8},{1,13},{5,1},{9,5},{13,9},{2,14},{6,2},{... | collective-permute-start | bytes 1376264 | tf_op jit(solution)/shard_map/ppermute | solution.py:23
  146.4 4.0 %collective-permute-done.26 = f32[128,256]{1,0:T(8,128)S(1)} collective-permute-done((f32[128,256]{1,0:T(8,128)S(1)}, f32[128,256]{1,0:T(8,128)S(1)}, u32[]{:S(2)}, u32[]{:S(2)}) %collective-permute-start.26) | collective-permute-done | bytes 131104 | tf_op jit(solution)/shard_map/ppermute | solution.py:29
  159.9 23.4 %collective-permute-start.28 = (bf16[256,64]{1,0:T(8,128)(2,1)}, bf16[256,64]{1,0:T(8,128)(2,1)S(1)}, u32[]{:S(2)}, u32[]{:S(2)}) collective-permute-start(bf16[256,64]{1,0:T(8,128)(2,1)} %get-tuple-element.27.rank_grad.refs_0_), channel_id=1, source_target_pairs={{0,4},{4,8},{8,12},{12,0},{1,5},{5,9},{9,13},{13,1},{2,6},{6,10},{... | collective-permute-start | bytes 98312 | tf_op jit(solution)/shard_map/ppermute | solution.py:23
  192.6 3.9 %collective-permute-start.37 = (f32[96,160]{1,0:T(8,128)}, f32[96,160]{1,0:T(8,128)S(1)}, u32[]{:S(2)}, u32[]{:S(2)}) collective-permute-start(f32[96,160]{1,0:T(8,128)} %bitcast.110), channel_id=1, source_target_pairs={{0,12},{4,0},{8,4},{12,8},{1,13},{5,1},{9,5},{13,9},{2,14},{6,2},{... | collective-permute-start | bytes 184328 | tf_op jit(solution)/shard_map/ppermute | solution.py:23
  196.5 2.3 %down_terms.1 = f32[192,896]{1,0:T(8,128)S(1)} custom-call(s32[8]{0:T(128)S(1)} %stack.197.marks, bf16[256,64]{1,0:T(8,128)(2,1)} %get-tuple-element.27.rank_grad.refs_0_, bf16[256,64]{1,0:T(8,128)(2,1)S(1)} %collective-permute-done.28.refs_1_, bf16[256,64]{1,0:T(8,128)(2,1)S(1)} %collective-permute-done.29.refs_2_, ...), custom_call_target="tpu_custom_call" | custom-call | flops 352321536 | bytes 1835008 | tf_op jit(solution)/shard_map/down_terms/pallas_call | solution.py:574
  200.4 2.5 %collective-permute-done.36 = f32[96,160]{1,0:T(8,128)S(1)} collective-permute-done((f32[96,160]{1,0:T(8,128)}, f32[96,160]{1,0:T(8,128)S(1)}, u32[]{:S(2)}, u32[]{:S(2)}) %collective-permute-start.36) | collective-permute-done | bytes 61472 | tf_op jit(solution)/shard_map/ppermute | solution.py:23
  206.5 6.1 %token_gradient.1 = bf16[256,3584]{1,0:T(8,128)(2,1)} custom-call(s32[8]{0:T(128)S(1)} %stack.197.marks, s32[17,2]{1,0:T(8,128)S(1)} %stack.244.offsets, bf16[256,768]{1,0:T(8,128)(2,1)S(1)} %copy-done.35, bf16[256,64]{1,0:T(8,128)(2,1)} %get-tuple-element.27.rank_grad.refs_0_, bf16[192,3584]{1,0:T(8,128)(2,1)} %refs_0_.3, bf16[192,896]{1,0:T(8,128)(2,1)S(1)} %copy-done.2, ...), custom_call_target="tpu_custom_call" | custom-call | flops 1644167168 | bytes 8257536 | tf_op jit(solution)/shard_map/token_gradient/pallas_call | solution.py:560
  213.7 5.4 %broadcast_in_dim.68.clone.refs_4_ = f32[64,64,1,448]{3,2,1,0:T(1,128)} broadcast(f32[]{:T(128)} %constant.152.clone.1), dimensions={} | broadcast | bytes 7340036 | tf_op jit(solution)/shard_map/broadcast_in_dim | solution.py:609
  219.1 2.9 %bank_rows.1 = (f32[64,64,1,448]{3,2,1,0:T(1,128)}, f32[64,32,80]{2,1,0:T(8,128)}) custom-call(s32[6]{0:T(128)S(1)} %pad_add_fusion.4.bank_rows, f32[192,448]{1,0:T(8,128)S(1)} %get-tuple-element.39.refs_0_, f32[192,448]{1,0:T(8,128)S(1)} %collective-permute-done.34.refs_1_, ...), custom_call_target="tpu_custom_call", output_to_operand_aliasing={{0}: (5, {}), {1}: (6, {})} | custom-call | tf_op jit(solution)/shard_map/bank_rows/pallas_call | solution.py:615
  (223 shorter events, 96.7 us)
Async XLA Ops:
  2.5 25.5 %collective-permute-start.8 = (bf16[192,896]{1,0:T(8,128)(2,1)}, bf16[192,896]{1,0:T(8,128)(2,1)S(1)}, u32[]{:S(2)}, u32[]{:S(2)}) collective-permute-start(bf16[192,896]{1,0:T(8,128)(2,1)} %constant_dynamic-slice_fusion.14), channel_id=1, source_target_pairs={{0,12},{4,0},{8,4},{12,8},{1,13},{5,1},{9,5},{13,9},{2,14},{6,2},{... | collective-permute-start | bytes 1032200 | tf_op jit(solution)/shard_map/ppermute | solution.py:23
  7.5 35.6 %collective-permute-start.4 = (bf16[192,896]{1,0:T(8,128)(2,1)}, bf16[192,896]{1,0:T(8,128)(2,1)S(1)}, u32[]{:S(2)}, u32[]{:S(2)}) collective-permute-start(bf16[192,896]{1,0:T(8,128)(2,1)} %constant_dynamic-slice_fusion.14), channel_id=1, source_target_pairs={{0,8},{4,12},{8,0},{12,4},{1,9},{5,13},{9,1},{13,5},{2,10},{6,14},... | collective-permute-start | bytes 1032200 | tf_op jit(solution)/shard_map/ppermute | solution.py:23
  7.5 37.1 %collective-permute-start = (bf16[192,896]{1,0:T(8,128)(2,1)}, bf16[192,896]{1,0:T(8,128)(2,1)S(1)}, u32[]{:S(2)}, u32[]{:S(2)}) collective-permute-start(bf16[192,896]{1,0:T(8,128)(2,1)} %constant_dynamic-slice_fusion.14), channel_id=1, source_target_pairs={{0,4},{4,8},{8,12},{12,0},{1,5},{5,9},{9,13},{13,1},{2,6},{6,10},{... | collective-permute-start | bytes 1032200 | tf_op jit(solution)/shard_map/ppermute | solution.py:23
  23.2 23.0 %collective-permute-start.15 = (bf16[128,896]{1,0:T(8,128)(2,1)}, bf16[128,896]{1,0:T(8,128)(2,1)S(1)}, u32[]{:S(2)}, u32[]{:S(2)}) collective-permute-start(bf16[128,896]{1,0:T(8,128)(2,1)} %get-tuple-element.44), channel_id=1, source_target_pairs={{0,12},{4,0},{8,4},{12,8},{1,13},{5,1},{9,5},{13,9},{2,14},{6,2},{... | collective-permute-start | bytes 688136 | tf_op jit(solution)/shard_map/ppermute | solution.py:23
  26.0 25.8 %collective-permute-start.14 = (bf16[128,896]{1,0:T(8,128)(2,1)}, bf16[128,896]{1,0:T(8,128)(2,1)S(1)}, u32[]{:S(2)}, u32[]{:S(2)}) collective-permute-start(bf16[128,896]{1,0:T(8,128)(2,1)} %get-tuple-element.45), channel_id=1, source_target_pairs={{0,8},{4,12},{8,0},{12,4},{1,9},{5,13},{9,1},{13,5},{2,10},{6,14},... | collective-permute-start | bytes 688136 | tf_op jit(solution)/shard_map/ppermute | solution.py:23
  28.0 35.6 %collective-permute-start.10 = (bf16[192,896]{1,0:T(8,128)(2,1)S(1)}, bf16[192,896]{1,0:T(8,128)(2,1)S(1)}, u32[]{:S(2)}, u32[]{:S(2)}) collective-permute-start(bf16[192,896]{1,0:T(8,128)(2,1)S(1)} %collective-permute-done.8.refs_9_), channel_id=1, source_target_pairs={{0,16},{16,0},{1,17},{17,1},{2,18},{18,2},{3,19},{19,3},{4,20},{20... | collective-permute-start | bytes 1032200 | tf_op jit(solution)/shard_map/ppermute | solution.py:23
  43.2 22.0 %collective-permute-start.9 = (bf16[192,896]{1,0:T(8,128)(2,1)S(1)}, bf16[192,896]{1,0:T(8,128)(2,1)S(1)}, u32[]{:S(2)}, u32[]{:S(2)}) collective-permute-start(bf16[192,896]{1,0:T(8,128)(2,1)S(1)} %collective-permute-done.8.refs_9_), channel_id=1, source_target_pairs={{0,2},{2,0},{1,3},{3,1},{4,6},{6,4},{5,7},{7,5},{8,10},{10,8},{9,1... | collective-permute-start | bytes 1032200 | tf_op jit(solution)/shard_map/ppermute | solution.py:23
  44.7 21.0 %collective-permute-start.6 = (bf16[192,896]{1,0:T(8,128)(2,1)S(1)}, bf16[192,896]{1,0:T(8,128)(2,1)S(1)}, u32[]{:S(2)}, u32[]{:S(2)}) collective-permute-start(bf16[192,896]{1,0:T(8,128)(2,1)S(1)} %collective-permute-done.4.refs_5_), channel_id=1, source_target_pairs={{0,16},{16,0},{1,17},{17,1},{2,18},{18,2},{3,19},{19,3},{4,20},{20... | collective-permute-start | bytes 1032200 | tf_op jit(solution)/shard_map/ppermute | solution.py:23
  46.9 20.0 %collective-permute-start.1 = (bf16[192,896]{1,0:T(8,128)(2,1)S(1)}, bf16[192,896]{1,0:T(8,128)(2,1)S(1)}, u32[]{:S(2)}, u32[]{:S(2)}) collective-permute-start(bf16[192,896]{1,0:T(8,128)(2,1)S(1)} %collective-permute-done.refs_1_), channel_id=1, source_target_pairs={{0,2},{2,0},{1,3},{3,1},{4,6},{6,4},{5,7},{7,5},{8,10},{10,8},{9,1... | collective-permute-start | bytes 1032200 | tf_op jit(solution)/shard_map/ppermute | solution.py:23
  62.1 11.0 %collective-permute-start.5 = (bf16[192,896]{1,0:T(8,128)(2,1)S(1)}, bf16[192,896]{1,0:T(8,128)(2,1)S(1)}, u32[]{:S(2)}, u32[]{:S(2)}) collective-permute-start(bf16[192,896]{1,0:T(8,128)(2,1)S(1)} %collective-permute-done.4.refs_5_), channel_id=1, source_target_pairs={{0,2},{2,0},{1,3},{3,1},{4,6},{6,4},{5,7},{7,5},{8,10},{10,8},{9,1... | collective-permute-start | bytes 1032200 | tf_op jit(solution)/shard_map/ppermute | solution.py:23
  65.1 16.8 %collective-permute-start.11 = (bf16[192,896]{1,0:T(8,128)(2,1)S(1)}, bf16[192,896]{1,0:T(8,128)(2,1)S(1)}, u32[]{:S(2)}, u32[]{:S(2)}) collective-permute-start(bf16[192,896]{1,0:T(8,128)(2,1)S(1)} %collective-permute-done.9.refs_10_), channel_id=1, source_target_pairs={{0,16},{16,0},{1,17},{17,1},{2,18},{18,2},{3,19},{19,3},{4,20},{20... | collective-permute-start | bytes 1032200 | tf_op jit(solution)/shard_map/ppermute | solution.py:23
  65.6 16.3 %collective-permute-start.7 = (bf16[192,896]{1,0:T(8,128)(2,1)S(1)}, bf16[192,896]{1,0:T(8,128)(2,1)S(1)}, u32[]{:S(2)}, u32[]{:S(2)}) collective-permute-start(bf16[192,896]{1,0:T(8,128)(2,1)S(1)} %collective-permute-done.6.refs_7_), channel_id=1, source_target_pairs={{0,2},{2,0},{1,3},{3,1},{4,6},{6,4},{5,7},{7,5},{8,10},{10,8},{9,1... | collective-permute-start | bytes 1032200 | tf_op jit(solution)/shard_map/ppermute | solution.py:23
  66.9 19.7 %collective-permute-start.3 = (bf16[192,896]{1,0:T(8,128)(2,1)S(1)}, bf16[192,896]{1,0:T(8,128)(2,1)S(1)}, u32[]{:S(2)}, u32[]{:S(2)}) collective-permute-start(bf16[192,896]{1,0:T(8,128)(2,1)S(1)} %collective-permute-done.1.refs_2_), channel_id=1, source_target_pairs={{0,16},{16,0},{1,17},{17,1},{2,18},{18,2},{3,19},{19,3},{4,20},{20... | collective-permute-start | bytes 1032200 | tf_op jit(solution)/shard_map/ppermute | solution.py:23
  73.1 28.8 %collective-permute-start.17 = (bf16[3,32,80]{2,1,0:T(8,128)(2,1)}, bf16[3,32,80]{2,1,0:T(8,128)(2,1)}, u32[]{:S(2)}, u32[]{:S(2)}) collective-permute-start(bf16[3,32,80]{2,1,0:T(8,128)(2,1)} %gather_fusion.3), channel_id=1, source_target_pairs={{0,2},{2,0},{1,3},{3,1},{4,6},{6,4},{5,7},{7,5},{8,10},{10,8},{9,1... | collective-permute-start | bytes 46088 | tf_op jit(solution)/shard_map/ppermute | solution.py:23
  101.8 11.2 %collective-permute-start.16 = (f32[256,832]{0,1:T(8,128)}, f32[256,832]{0,1:T(8,128)}, u32[]{:S(2)}, u32[]{:S(2)}) collective-permute-start(f32[256,832]{0,1:T(8,128)} %copy.114), channel_id=1, source_target_pairs={{0,1},{1,0},{2,3},{3,2},{4,5},{5,4},{6,7},{7,6},{8,9},{9,8},{10,11... | collective-permute-start | bytes 2555912 | tf_op jit(solution)/shard_map/ppermute | solution.py:23
  133.3 13.1 %collective-permute-start.25 = (f32[128,256]{1,0:T(8,128)S(1)}, f32[128,256]{1,0:T(8,128)S(1)}, u32[]{:S(2)}, u32[]{:S(2)}) collective-permute-start(f32[128,256]{1,0:T(8,128)S(1)} %get-tuple-element.40), channel_id=1, source_target_pairs={{4,0},{8,4},{12,8},{5,1},{9,5},{13,9},{6,2},{10,6},{14,10},{7,3},{... | collective-permute-start | bytes 393224 | tf_op jit(solution)/shard_map/ppermute | solution.py:29
  134.6 15.8 %collective-permute-start.26 = (f32[128,256]{1,0:T(8,128)S(1)}, f32[128,256]{1,0:T(8,128)S(1)}, u32[]{:S(2)}, u32[]{:S(2)}) collective-permute-start(f32[128,256]{1,0:T(8,128)S(1)} %get-tuple-element.41), channel_id=1, source_target_pairs={{8,0},{12,4},{9,1},{13,5},{10,2},{14,6},{11,3},{15,7},{24,16},{28,... | collective-permute-start | bytes 393224 | tf_op jit(solution)/shard_map/ppermute | solution.py:29
  138.5 21.5 %collective-permute-start.33 = (bf16[256,896]{1,0:T(8,128)(2,1)}, bf16[256,896]{1,0:T(8,128)(2,1)}, u32[]{:S(2)}, u32[]{:S(2)}) collective-permute-start(bf16[256,896]{1,0:T(8,128)(2,1)} %get-tuple-element.34), channel_id=1, source_target_pairs={{0,12},{4,0},{8,4},{12,8},{1,13},{5,1},{9,5},{13,9},{2,14},{6,2},{... | collective-permute-start | bytes 1376264 | tf_op jit(solution)/shard_map/ppermute | solution.py:23
  145.8 46.8 %collective-permute-start.32 = (bf16[256,896]{1,0:T(8,128)(2,1)}, bf16[256,896]{1,0:T(8,128)(2,1)}, u32[]{:S(2)}, u32[]{:S(2)}) collective-permute-start(bf16[256,896]{1,0:T(8,128)(2,1)} %get-tuple-element.35), channel_id=1, source_target_pairs={{0,8},{4,12},{8,0},{12,4},{1,9},{5,13},{9,1},{13,5},{2,10},{6,14},... | collective-permute-start | bytes 1376264 | tf_op jit(solution)/shard_map/ppermute | solution.py:23
  145.8 46.8 %collective-permute-start.31 = (bf16[256,896]{1,0:T(8,128)(2,1)}, bf16[256,896]{1,0:T(8,128)(2,1)}, u32[]{:S(2)}, u32[]{:S(2)}) collective-permute-start(bf16[256,896]{1,0:T(8,128)(2,1)} %get-tuple-element.36), channel_id=1, source_target_pairs={{0,4},{4,8},{8,12},{12,0},{1,5},{5,9},{9,13},{13,1},{2,6},{6,10},{... | collective-permute-start | bytes 1376264 | tf_op jit(solution)/shard_map/ppermute | solution.py:23
  157.3 35.3 %collective-permute-start.30 = (bf16[256,64]{1,0:T(8,128)(2,1)}, bf16[256,64]{1,0:T(8,128)(2,1)S(1)}, u32[]{:S(2)}, u32[]{:S(2)}) collective-permute-start(bf16[256,64]{1,0:T(8,128)(2,1)} %get-tuple-element.27.rank_grad.refs_0_), channel_id=1, source_target_pairs={{0,12},{4,0},{8,4},{12,8},{1,13},{5,1},{9,5},{13,9},{2,14},{6,2},{... | collective-permute-start | bytes 98312 | tf_op jit(solution)/shard_map/ppermute | solution.py:23
  157.3 39.2 %collective-permute-start.29 = (bf16[256,64]{1,0:T(8,128)(2,1)}, bf16[256,64]{1,0:T(8,128)(2,1)S(1)}, u32[]{:S(2)}, u32[]{:S(2)}) collective-permute-start(bf16[256,64]{1,0:T(8,128)(2,1)} %get-tuple-element.27.rank_grad.refs_0_), channel_id=1, source_target_pairs={{0,8},{4,12},{8,0},{12,4},{1,9},{5,13},{9,1},{13,5},{2,10},{6,14},... | collective-permute-start | bytes 98312 | tf_op jit(solution)/shard_map/ppermute | solution.py:23
  159.9 36.6 %collective-permute-start.28 = (bf16[256,64]{1,0:T(8,128)(2,1)}, bf16[256,64]{1,0:T(8,128)(2,1)S(1)}, u32[]{:S(2)}, u32[]{:S(2)}) collective-permute-start(bf16[256,64]{1,0:T(8,128)(2,1)} %get-tuple-element.27.rank_grad.refs_0_), channel_id=1, source_target_pairs={{0,4},{4,8},{8,12},{12,0},{1,5},{5,9},{9,13},{13,1},{2,6},{6,10},{... | collective-permute-start | bytes 98312 | tf_op jit(solution)/shard_map/ppermute | solution.py:23
  199.1 13.6 %collective-permute-start.34 = (f32[192,448]{1,0:T(8,128)S(1)}, f32[192,448]{1,0:T(8,128)S(1)}, u32[]{:S(2)}, u32[]{:S(2)}) collective-permute-start(f32[192,448]{1,0:T(8,128)S(1)} %get-tuple-element.38), channel_id=1, source_target_pairs={{0,2},{2,0},{1,3},{3,1},{4,6},{6,4},{5,7},{7,5},{8,10},{10,8},{9,1... | collective-permute-start | bytes 1032200 | tf_op jit(solution)/shard_map/ppermute | solution.py:23
  (61 other events, 711.9 us)

commit v3 on v2

--- a/solution.py
+++ b/solution.py
@@ -15,7 +15,7 @@
 adapter_scale = 2.0
 rope_base = 5000000.0
 masked_score = -1e30
-vmem_limit = 48 * 1024 * 1024
+mebibyte = 1024 * 1024
 
 
 def shift(value, axis, steps):
@@ -54,8 +54,18 @@
     return first + lax.broadcasted_iota(jnp.int32, (count, 1), 0)
 
 
-def row_segments(marks, positions):
-    return (positions >= marks[0]).astype(jnp.int32) + (positions >= marks[1]).astype(jnp.int32)
+def ring_index(index, count):
+    return lax.rem(index + count, count)
+
+
+def kernel_marks(lengths):
+    batch = lax.axis_index("batch")
+    first_end = lengths[batch, 0]
+    return first_end, first_end + lengths[batch, 1]
+
+
+def row_segments(ends, positions):
+    return (positions >= ends[0]).astype(jnp.int32) + (positions >= ends[1]).astype(jnp.int32)
 
 
 def cost(flops, bytes_accessed, transcendentals=0):
@@ -76,15 +86,16 @@
     return pl.BlockSpec(memory_space=pl.ANY)
 
 
-def fetch_pieces(offsets, pieces, target, semaphore, first):
+def fetch_pieces(places, pieces, target, semaphore, first):
     copies = []
-    for number, piece in enumerate(pieces):
+    for number, (place, piece) in enumerate(zip(places, pieces)):
         height, width = piece.shape
-        row = pl.multiple_of(offsets[first + number, 0], 16)
-        column = pl.multiple_of(offsets[first + number, 1], 128)
+        row, column = place()
         copy = pltpu.make_async_copy(
             piece,
-            target.at[pl.ds(row, height), pl.ds(column, width)],
+            target.at[
+                pl.ds(pl.multiple_of(row, 16), height), pl.ds(pl.multiple_of(column, 128), width)
+            ],
             semaphore.at[first + number],
         )
         copy.start()
@@ -92,38 +103,75 @@
     return copies
 
 
-def project_kernel(frozen_count, down_count, marks, offsets, tokens, *refs):
+def frozen_place(seq_count, rows, share, behind, batch_step, group_step):
+    def place():
+        holder = ring_index(lax.axis_index("seq") - behind, seq_count)
+        if share is None:
+            return holder * rows, 0
+        batch = lax.rem(lax.axis_index("batch") + batch_step, 2)
+        group = lax.rem(lax.axis_index("groups") + group_step, 2)
+        return holder * rows, (group * 2 + batch) * share
+
+    return place
+
+
+def down_place(seq_count, width, behind):
+    def place():
+        return 0, ring_index(lax.axis_index("seq") - behind, seq_count) * width
+
+    return place
+
+
+def whole_place():
+    return 0, 0
+
+
+def second_document(ends, rows, seq_count):
+    seq_index = lax.axis_index("seq")
+    first = (seq_index >= seq_count // 2).astype(jnp.int32)
+    return row_segments(ends, row_positions(seq_index * rows, rows)) != first
+
+
+def project_kernel(frozen_places, down_places, unused, seq_count, lengths, tokens, *refs):
+    frozen_count, down_count = len(frozen_places), len(down_places)
     frozen_pieces = refs[:frozen_count]
     down_pieces = refs[frozen_count : frozen_count + down_count]
-    part, frozen, down, semaphore = refs[frozen_count + down_count :]
-    copies = fetch_pieces(offsets, frozen_pieces, frozen, semaphore, 0)
-    copies += fetch_pieces(offsets, down_pieces, down, semaphore, frozen_count)
+    refs = refs[frozen_count + down_count + unused :]
+    part, columns, (frozen, down, semaphore) = refs[0], refs[1:-3], refs[-3:]
+    copies = fetch_pieces(frozen_places, frozen_pieces, frozen, semaphore, 0)
+    copies += fetch_pieces(down_places, down_pieces, down, semaphore, frozen_count)
+    rows, width = tokens.shape
+    for steps, block in enumerate(columns):
+        target = ring_index(lax.axis_index("seq") + steps - seq_count, seq_count)
+        held = block.shape[1]
+        block[...] = tokens[:, pl.ds(pl.multiple_of(target * held, 128), held)]
     for copy in copies:
         copy.wait()
-    rows = tokens.shape[0]
     features = frozen.shape[0]
     joint_rank = down.shape[0] // 2
-    positions = row_positions(marks[2] * rows, rows)
-    second = row_segments(marks, positions) != marks[6]
+    second = second_document(kernel_marks(lengths), rows, seq_count)
     values = tokens[...]
     part[:, :features] = dot_nt(values, frozen[...])
     first_low = dot_nt(values, down[:joint_rank])
     second_low = dot_nt(values, down[joint_rank:])
-    part[:, features:] = jnp.where(second, second_low, first_low)
+    part[:, features : features + joint_rank] = jnp.where(second, second_low, first_low)
 
 
 def rotated(values, cosines, sines):
     return values * cosines + pltpu.roll(values, values.shape[1] // 2, 1) * sines
 
 
-def qkv_kernel(marks, mine, theirs, up_blocks, cosines, sines, queries, pairs, low_rank):
+def qkv_kernel(lengths, mine, theirs, up_blocks, cosines, sines, queries, pairs, low_rank):
     rows = mine.shape[0]
     own_rows = queries.shape[0] // QHEADS
     query_columns = QHEADS * HEAD_WIDTH
     value_start = query_columns + HEAD_WIDTH
     features = value_start + HEAD_WIDTH
-    segments = row_segments(marks, row_positions(marks[2] * rows, rows))
-    low = (mine[:, features:] + theirs[:, features:]).astype(jnp.bfloat16)
+    low_columns = slice(features, features + low_rank.shape[1])
+    ends = kernel_marks(lengths)
+    first_row = lax.axis_index("seq") * rows
+    segments = row_segments(ends, row_positions(first_row, rows))
+    low = (mine[:, low_columns] + theirs[:, low_columns]).astype(jnp.bfloat16)
     low_rank[...] = low
     value_delta = jnp.zeros((rows, HEAD_WIDTH), jnp.float32)
     for document in range(SEGS):
@@ -133,10 +181,10 @@
     pairs[:, :HEAD_WIDTH] = rotated(keys, cosines[...], sines[...]).astype(jnp.bfloat16)
     values = mine[:, value_start:features] + theirs[:, value_start:features]
     pairs[:, HEAD_WIDTH:] = (values + adapter_scale * value_delta).astype(jnp.bfloat16)
-    start = pl.multiple_of(marks[3] * own_rows, own_rows)
+    start = pl.multiple_of(lax.axis_index("tp") * own_rows, own_rows)
     own = pl.ds(start, own_rows)
-    own_segments = row_segments(marks, row_positions(marks[2] * rows + start, own_rows))
-    own_low = (mine[own, features:] + theirs[own, features:]).astype(jnp.bfloat16)
+    own_segments = row_segments(ends, row_positions(first_row + start, own_rows))
+    own_low = (mine[own, low_columns] + theirs[own, low_columns]).astype(jnp.bfloat16)
     query_delta = jnp.zeros((own_rows, query_columns), jnp.float32)
     for document in range(SEGS):
         chosen = jnp.where(own_segments == document, own_low, jnp.zeros_like(own_low))
@@ -150,20 +198,21 @@
         queries[head * own_rows : (head + 1) * own_rows] = turned.astype(jnp.bfloat16)
 
 
-def attention_kernel(block_count, marks, queries, incoming, cosines, sines, *refs):
+def attention_kernel(block_count, lengths, queries, incoming, cosines, sines, *refs):
     blocks = refs[:block_count]
     output, query_grad, kept, sent, low_probs = refs[block_count:]
     own_rows, query_columns = incoming.shape
     rows = blocks[0].shape[0]
     score_scale = HEAD_WIDTH ** (-0.5)
-    first = marks[2] * rows + marks[3] * own_rows
-    positions = row_positions(first, own_rows)
+    ends = kernel_marks(lengths)
+    seq_index, tp_index = lax.axis_index("seq"), lax.axis_index("tp")
+    positions = row_positions(seq_index * rows + tp_index * own_rows, own_rows)
     positions = jnp.concatenate([positions] * QHEADS, axis=0)
-    segments = row_segments(marks, positions)
-    starts = jnp.where(segments == 0, 0, jnp.where(segments == 1, marks[0], marks[1]))
+    segments = row_segments(ends, positions)
+    starts = jnp.where(segments == 0, 0, jnp.where(segments == 1, ends[0], ends[1]))
     scores = []
     for back, block in enumerate(blocks):
-        key_positions = (marks[2] - back) * rows + lax.broadcasted_iota(jnp.int32, (1, rows), 1)
+        key_positions = (seq_index - back) * rows + lax.broadcasted_iota(jnp.int32, (1, rows), 1)
         allowed = (key_positions <= positions) & (key_positions >= starts)
         block_scores = dot_nt(queries[...], block[:, :HEAD_WIDTH]) * score_scale
         scores.append(jnp.where(allowed, block_scores, masked_score))
@@ -186,8 +235,7 @@
     row_delta = jnp.sum(
         gradients.astype(jnp.float32) * attended.astype(jnp.float32), axis=1, keepdims=True
     )
-    start = pl.multiple_of(marks[3] * own_rows, own_rows)
-    other = pl.multiple_of(own_rows - start, own_rows)
+    start = pl.multiple_of(tp_index * own_rows, own_rows)
     total = jnp.zeros((QHEADS * own_rows, HEAD_WIDTH), jnp.float32)
     for back, block in enumerate(blocks):
         prob_grad = dot_nt(gradients, block[:, HEAD_WIDTH:])
@@ -195,7 +243,7 @@
         total += dot_nn(score_grad, block[:, :HEAD_WIDTH])
         key_part = dot_tn(score_grad, queries[...]) * score_scale
         value_part = dot_tn(low_probs[back], gradients)
-        mine = marks[3] == 0
+        mine = tp_index == 0
         kept[back, :, :HEAD_WIDTH] = jnp.where(mine, key_part[:own_rows], key_part[own_rows:])
         sent[back, :, :HEAD_WIDTH] = jnp.where(mine, key_part[own_rows:], key_part[:own_rows])
         kept[back, :, HEAD_WIDTH:] = jnp.where(mine, value_part[:own_rows], value_part[own_rows:])
@@ -211,12 +259,15 @@
 
 
 def rank_kernel(
-    marks, own_query, other_query, own_pair, other_pair, low_rank, up_blocks,
-    gradients, rank_grad, up_terms,
+    unused, seq_count, lengths, own_query, other_query, own_pair, other_pair, low_rank, up_blocks, *refs
 ):
+    refs = refs[unused:]
+    gradients, rank_grad = refs[:2]
+    split_terms, (terms, blocks) = refs[2:-2], refs[-2:]
     own_rows, query_columns = own_query.shape
     rows = low_rank.shape[0]
-    start = pl.multiple_of(marks[3] * own_rows, own_rows)
+    seq_index = lax.axis_index("seq")
+    start = pl.multiple_of(lax.axis_index("tp") * own_rows, own_rows)
     other = pl.multiple_of(own_rows - start, own_rows)
     gradients[pl.ds(start, own_rows), :query_columns] = own_query[...]
     gradients[pl.ds(other, own_rows), :query_columns] = other_query[...]
@@ -226,33 +277,39 @@
     value_grad = gradients[:, query_columns + HEAD_WIDTH :]
     low = low_rank[...]
     rank = low.shape[1] // 2
-    segments = row_segments(marks, row_positions(marks[2] * rows, rows))
+    segments = row_segments(kernel_marks(lengths), row_positions(seq_index * rows, rows))
     total = jnp.zeros((rows, low.shape[1]), jnp.float32)
     for document in range(SEGS):
         member = segments == document
-        terms = dot_nt(query_grad, up_blocks[document, :, :query_columns])
-        terms += dot_nt(value_grad, up_blocks[document, :, query_columns:])
-        total = jnp.where(member, terms, total)
+        parts = dot_nt(query_grad, up_blocks[document, :, :query_columns])
+        parts += dot_nt(value_grad, up_blocks[document, :, query_columns:])
+        total = jnp.where(member, parts, total)
         chosen = jnp.where(member, low, jnp.zeros_like(low))
         query_terms = dot_tn(chosen, query_grad)
         value_terms = dot_tn(chosen, value_grad)
         place = slice(document * rank, (document + 1) * rank)
-        up_terms[place, :query_columns] = adapter_scale * query_terms[:rank]
-        up_terms[place, query_columns:] = adapter_scale * value_terms[rank:]
+        terms[place, :query_columns] = adapter_scale * query_terms[:rank]
+        terms[place, query_columns:] = adapter_scale * value_terms[rank:]
     rank_grad[...] = (adapter_scale * total).astype(jnp.bfloat16)
-
-
-def token_kernel(frozen_count, down_count, marks, offsets, gradients, rank_grad, *refs):
+    held = blocks.shape[2]
+    for holder in range(seq_count):
+        blocks[holder] = terms[:, holder * held : (holder + 1) * held]
+    for steps, block in enumerate(split_terms):
+        block[...] = blocks[ring_index(seq_index + steps - seq_count, seq_count)]
+
+
+def token_kernel(frozen_places, down_places, seq_count, lengths, gradients, rank_grad, *refs):
+    frozen_count, down_count = len(frozen_places), len(down_places)
     frozen_pieces = refs[:frozen_count]
     down_pieces = refs[frozen_count : frozen_count + down_count]
     token_grad, frozen, down, semaphore = refs[frozen_count + down_count :]
-    copies = fetch_pieces(offsets, frozen_pieces, frozen, semaphore, 0)
-    copies += fetch_pieces(offsets, down_pieces, down, semaphore, frozen_count)
+    copies = fetch_pieces(frozen_places, frozen_pieces, frozen, semaphore, 0)
+    copies += fetch_pieces(down_places, down_pieces, down, semaphore, frozen_count)
     for copy in copies:
         copy.wait()
     rows = gradients.shape[0]
     joint_rank = down.shape[0] // 2
-    second = row_segments(marks, row_positions(marks[2] * rows, rows)) != marks[6]
+    second = second_document(kernel_marks(lengths), rows, seq_count)
     low = rank_grad[...]
     nothing = jnp.zeros_like(low)
     first_low = jnp.where(second, nothing, low)
@@ -266,21 +323,39 @@
         token_grad[:, columns] = total.astype(jnp.bfloat16)
 
 
-def down_kernel(block_count, marks, *refs):
+def split_halves(terms, own, far):
+    held = own.shape[1]
+    left, right = terms[:, :held], terms[:, held:]
+    ahead = lax.axis_index("batch") == 0
+    own[...] = jnp.where(ahead, left, right)
+    far[...] = jnp.where(ahead, right, left)
+
+
+def down_kernel(block_count, lengths, *refs):
     ranks = refs[:block_count]
     columns = refs[block_count : 2 * block_count]
-    terms = refs[2 * block_count]
+    up_parts = refs[2 * block_count : 3 * block_count]
+    outputs = refs[3 * block_count :]
     rows, joint_rank = ranks[0].shape
+    ends = kernel_marks(lengths)
+    all_terms = []
     for document in range(SEGS):
-        total = jnp.zeros((joint_rank, terms.shape[1]), jnp.float32)
+        total = jnp.zeros((joint_rank, columns[0].shape[1]), jnp.float32)
         for behind in range(block_count):
-            holder = marks[2] - behind
-            holder = jnp.where(holder < 0, holder + block_count, holder)
-            segments = row_segments(marks, row_positions(holder * rows, rows))
+            holder = ring_index(lax.axis_index("seq") - behind, block_count)
+            segments = row_segments(ends, row_positions(holder * rows, rows))
             low = ranks[behind][...]
             chosen = jnp.where(segments == document, low, jnp.zeros_like(low))
             total += dot_tn(chosen, columns[behind][...])
-        terms[document * joint_rank : (document + 1) * joint_rank] = total
+        all_terms.append(total)
+    down_terms = jnp.concatenate(all_terms, axis=0)
+    up_terms = sum(part[...] for part in up_parts)
+    if len(outputs) == 2:
+        outputs[0][...] = down_terms
+        outputs[1][...] = up_terms
+    else:
+        split_halves(down_terms, *outputs[:2])
+        split_halves(up_terms, *outputs[2:])
 
 
 def bank_kernel(block_count, bank_rows, *refs):
@@ -341,19 +416,6 @@
     def first_document(holder):
         return (holder >= half_count).astype(jnp.int32)
 
-    marks = jnp.stack(
-        [
-            ends[0],
-            ends[1],
-            seq_index,
-            tp_index,
-            batch_index,
-            group_index,
-            first_document(seq_index),
-            jnp.int32(0),
-        ]
-    ).astype(jnp.int32)
-
     plane_count = group_count * batch_count
     share = width // plane_count
     pieces, places = [], []
@@ -363,11 +425,15 @@
             frozen_qkv_matrix, (group_index * batch_count + batch_index) * share, share, axis=1
         )
         pieces.append(frozen_qkv_matrix)
-        places.append((seq_index * frozen_rows, 0))
-        for steps in range(1, seq_count):
-            holder = jnp.remainder(seq_index - steps, seq_count)
-            here = shift(own_share, "seq", steps)
-            if steps % 2 == 1:
+        places.append(frozen_place(seq_count, frozen_rows, None, 0, 0, 0))
+        before = shift(own_share, "seq", 1)
+        after = shift(own_share, "seq", seq_count - 1)
+        arrivals = [(1, before), (seq_count - 1, after)]
+        for steps in range(2, seq_count - 1):
+            before = shift(before, "seq", 1)
+            arrivals.append((steps, before))
+        for steps, here in arrivals:
+            if steps < seq_count - 1:
                 over_batch = shift(here, "batch", 1)
                 over_groups = shift(here, "groups", 1)
                 over_both = shift(over_batch, "groups", 1)
@@ -375,18 +441,19 @@
                 over_groups = shift(here, "groups", 1)
                 over_batch = shift(here, "batch", 1)
                 over_both = shift(over_groups, "batch", 1)
-            for value, group, batch in (
-                (here, group_index, batch_index),
-                (over_batch, group_index, 1 - batch_index),
-                (over_groups, 1 - group_index, batch_index),
-                (over_both, 1 - group_index, 1 - batch_index),
+            for value, batch_step, group_step in (
+                (here, 0, 0),
+                (over_batch, 1, 0),
+                (over_groups, 0, 1),
+                (over_both, 1, 1),
             ):
                 pieces.append(value)
-                places.append((holder * frozen_rows, (group * batch_count + batch) * share))
+                places.append(
+                    frozen_place(seq_count, frozen_rows, share, steps, batch_step, group_step)
+                )
     else:
         pieces.append(lax.all_gather(frozen_qkv_matrix, "seq", axis=0, tiled=True))
-        places.append((0, 0))
-    frozen_count = len(pieces)
+        places.append(whole_place)
 
     down_bank = adapter_down_weight[:, :, 0, :]
     if batch_count == 2:
@@ -417,12 +484,11 @@
     down_parts, down_places, up_parts = [], [], []
     for steps in range(seq_count):
         target = jnp.remainder(seq_index + steps, seq_count)
-        holder = jnp.remainder(seq_index - steps, seq_count)
         part = lax.dynamic_slice_in_dim(
             down_block, first_document(target) * joint_rank, 2 * joint_rank
         )
         down_parts.append(shift(part, "seq", steps) if steps else part)
-        down_places.append((0, holder * down_width))
+        down_places.append(down_place(seq_count, down_width, steps))
         up_parts.append(shift(up_block, "seq", steps) if steps else up_block)
     relative = jnp.remainder(seq_index - jnp.arange(seq_count, dtype=jnp.int32), seq_count)
     up_rows = jnp.stack(up_parts)[relative]
@@ -438,11 +504,7 @@
     if down_width % 128 != 0:
         merged = jnp.stack(down_parts)[relative]
         merged = jnp.transpose(merged, (1, 0, 2)).reshape(2 * joint_rank, -1)
-        down_parts, down_places = [merged], [(0, 0)]
-    down_count = len(down_parts)
-    offsets = jnp.stack(
-        [jnp.stack([jnp.int32(0) + row, jnp.int32(0) + column]) for row, column in places + down_places]
-    ).astype(jnp.int32)
+        down_parts, down_places = [merged], [whole_place]
 
     positions = seq_index * rows + jnp.arange(rows, dtype=jnp.int32)
     inside = positions - jnp.where(
@@ -456,30 +518,45 @@
     scratch = [
         pltpu.VMEM((features, width), bf16),
         pltpu.VMEM((2 * joint_rank, width), bf16),
-        pltpu.SemaphoreType.DMA((frozen_count + down_count,)),
+        pltpu.SemaphoreType.DMA((len(pieces) + len(down_parts),)),
     ]
     weight_bytes = 2 * width * (features + 2 * joint_rank)
-    part = pl.pallas_call(
-        functools.partial(project_kernel, frozen_count, down_count),
-        out_shape=jax.ShapeDtypeStruct((rows, features + joint_rank), f32),
-        in_specs=[in_smem(), in_smem(), in_vmem()] + [in_place()] * (frozen_count + down_count),
-        out_specs=in_vmem(),
+    held_down = down_width // batch_count
+    held_up = up_blocks.shape[2] // (seq_count * batch_count)
+    down_zeros = jnp.zeros((adapters, joint_rank, 1, held_down), f32)
+    up_zeros = jnp.zeros((adapters, low_width, held_up), f32)
+    early = [down_zeros, up_zeros, cosines, sines, up_blocks]
+    part_width = features + 128
+    column_count = seq_count if down_width % 128 == 0 else 0
+    part, *column_blocks = pl.pallas_call(
+        functools.partial(project_kernel, places, down_places, len(early), seq_count),
+        out_shape=[jax.ShapeDtypeStruct((rows, part_width), f32)]
+        + [jax.ShapeDtypeStruct((rows, down_width), bf16)] * column_count,
+        in_specs=[in_smem(), in_vmem()]
+        + [in_place()] * (len(pieces) + len(down_parts) + len(early)),
+        out_specs=[in_vmem()] * (1 + column_count),
         scratch_shapes=scratch,
-        compiler_params=pltpu.CompilerParams(vmem_limit_bytes=vmem_limit),
+        compiler_params=pltpu.CompilerParams(vmem_limit_bytes=20 * mebibyte),
         cost_estimate=cost(
             2 * rows * width * (features + 2 * joint_rank), weight_bytes + 2 * rows * width
         ),
         name="project",
-    )(marks, offsets, local_tokens, *pieces, *down_parts)
-
-    part, late_tokens = lax.optimization_barrier((part, local_tokens))
-    column_parts = []
-    for steps in range(seq_count):
-        target = jnp.remainder(seq_index + steps, seq_count)
-        part_columns = lax.dynamic_slice_in_dim(
-            late_tokens, target * down_width, down_width, axis=1
-        )
-        column_parts.append(shift(part_columns, "seq", steps) if steps else part_columns)
+    )(document_lengths, local_tokens, *pieces, *down_parts, *early)
+
+    if column_count == 0:
+        column_blocks = [
+            lax.dynamic_slice_in_dim(
+                local_tokens,
+                jnp.remainder(seq_index + steps, seq_count) * down_width,
+                down_width,
+                axis=1,
+            )
+            for steps in range(seq_count)
+        ]
+    column_parts = [
+        shift(block, "seq", steps) if steps else block
+        for steps, block in enumerate(column_blocks)
+    ]
 
     other_part = shift(part, "tp", 1)
     queries, pairs, low_rank = pl.pallas_call(
@@ -491,10 +568,10 @@
         ),
         in_specs=[in_smem()] + [in_vmem()] * 5,
         out_specs=(in_vmem(),) * 3,
-        compiler_params=pltpu.CompilerParams(vmem_limit_bytes=vmem_limit),
+        compiler_params=pltpu.CompilerParams(vmem_limit_bytes=8 * mebibyte),
         cost_estimate=cost(2 * rows * 3 * 64 * 640, 8 * rows * features),
         name="qkv",
-    )(marks, part, other_part, up_blocks, cosines, sines)
+    )(document_lengths, part, other_part, up_blocks, cosines, sines)
 
     blocks = [pairs] + [push(pairs, "seq", back) for back in range(1, half_count + 1)]
     block_count = len(blocks)
@@ -510,14 +587,14 @@
         in_specs=[in_smem()] + [in_vmem()] * (4 + block_count),
         out_specs=(in_vmem(),) * 4,
         scratch_shapes=[pltpu.VMEM((block_count, QHEADS * own_rows, rows), bf16)],
-        compiler_params=pltpu.CompilerParams(vmem_limit_bytes=vmem_limit),
+        compiler_params=pltpu.CompilerParams(vmem_limit_bytes=(4 + 4 * block_count) * mebibyte),
         cost_estimate=cost(
             10 * block_count * QHEADS * own_rows * rows * HEAD_WIDTH,
             4 * rows * features,
             block_count * QHEADS * own_rows * rows,
         ),
         name="attention",
-    )(marks, queries, incoming, cosines, sines, *blocks)
+    )(document_lengths, queries, incoming, cosines, sines, *blocks)
 
     other_query = shift(query_grad, "tp", 1)
     pair_sums = kept + shift(sent, "tp", 1)
@@ -532,82 +609,78 @@
     pair_grad = jnp.concatenate([key_grad, own_sum[:, HEAD_WIDTH:]], axis=1).astype(bf16)
     other_pair = shift(pair_grad, "tp", 1)
 
-    gradients, rank_grad, up_terms = pl.pallas_call(
-        rank_kernel,
-        out_shape=(
+    gradients, rank_grad, *up_split = pl.pallas_call(
+        functools.partial(rank_kernel, seq_count - 1, seq_count),
+        out_shape=[
             jax.ShapeDtypeStruct((rows, features), bf16),
             jax.ShapeDtypeStruct((rows, joint_rank), bf16),
-            jax.ShapeDtypeStruct((SEGS * low_width, features - HEAD_WIDTH), f32),
-        ),
-        in_specs=[in_smem()] + [in_vmem()] * 6,
-        out_specs=(in_vmem(),) * 3,
-        compiler_params=pltpu.CompilerParams(vmem_limit_bytes=vmem_limit),
+        ]
+        + [jax.ShapeDtypeStruct((SEGS * low_width, held_up * batch_count), f32)] * seq_count,
+        in_specs=[in_smem()] + [in_vmem()] * 6 + [in_place()] * (seq_count - 1),
+        out_specs=[in_vmem()] * (2 + seq_count),
+        scratch_shapes=[
+            pltpu.VMEM((SEGS * low_width, features - HEAD_WIDTH), f32),
+            pltpu.VMEM((seq_count, SEGS * low_width, held_up * batch_count), f32),
+        ],
+        compiler_params=pltpu.CompilerParams(vmem_limit_bytes=8 * mebibyte),
         cost_estimate=cost(4 * rows * 3 * 64 * 640, 4 * rows * features),
         name="rank_gradients",
-    )(marks, query_grad, other_query, pair_grad, other_pair, low_rank, up_blocks)
+    )(
+        document_lengths, query_grad, other_query, pair_grad, other_pair, low_rank, up_blocks,
+        *column_parts[1:],
+    )
 
     rank_parts = [rank_grad] + [shift(rank_grad, "seq", steps) for steps in range(1, seq_count)]
-    up_split = jnp.transpose(
-        up_terms.reshape(SEGS * low_width, seq_count, -1), (1, 0, 2)
-    )
-    up_sum = lax.dynamic_index_in_dim(up_split, seq_index, 0, keepdims=False)
-    for steps in range(1, seq_count):
-        target = jnp.remainder(seq_index + steps, seq_count)
-        up_sum = up_sum + shift(
-            lax.dynamic_index_in_dim(up_split, target, 0, keepdims=False), "seq", steps
-        )
+    up_sums = [
+        shift(block, "seq", steps) if steps else block for steps, block in enumerate(up_split)
+    ]
 
     token_grad = pl.pallas_call(
-        functools.partial(token_kernel, frozen_count, down_count),
+        functools.partial(token_kernel, places, down_places, seq_count),
         out_shape=jax.ShapeDtypeStruct((rows, width), bf16),
-        in_specs=[in_smem(), in_smem(), in_vmem(), in_vmem()]
-        + [in_place()] * (frozen_count + down_count),
+        in_specs=[in_smem(), in_vmem(), in_vmem()]
+        + [in_place()] * (len(pieces) + len(down_parts)),
         out_specs=in_vmem(),
         scratch_shapes=scratch,
-        compiler_params=pltpu.CompilerParams(vmem_limit_bytes=vmem_limit),
+        compiler_params=pltpu.CompilerParams(vmem_limit_bytes=20 * mebibyte),
         cost_estimate=cost(
             2 * rows * width * (features + 2 * joint_rank), weight_bytes + 2 * rows * width
         ),
         name="token_gradient",
-    )(marks, offsets, gradients, rank_grad, *pieces, *down_parts)
-
-    down_terms = pl.pallas_call(
+    )(document_lengths, gradients, rank_grad, *pieces, *down_parts)
+
+    if batch_count == 2:
+        term_shapes = [(SEGS * joint_rank, held_down)] * 2 + [(SEGS * low_width, held_up)] * 2
+    else:
+        term_shapes = [(SEGS * joint_rank, down_width), (SEGS * low_width, held_up * batch_count)]
+    terms = pl.pallas_call(
         functools.partial(down_kernel, seq_count),
-        out_shape=jax.ShapeDtypeStruct((SEGS * joint_rank, down_width), f32),
-        in_specs=[in_smem()] + [in_vmem()] * (2 * seq_count),
-        out_specs=in_vmem(),
-        compiler_params=pltpu.CompilerParams(vmem_limit_bytes=vmem_limit),
+        out_shape=[jax.ShapeDtypeStruct(shape, f32) for shape in term_shapes],
+        in_specs=[in_smem()] + [in_vmem()] * (3 * seq_count),
+        out_specs=[in_vmem()] * len(term_shapes),
+        compiler_params=pltpu.CompilerParams(vmem_limit_bytes=8 * mebibyte),
         cost_estimate=cost(
             2 * seq_count * rows * SEGS * joint_rank * down_width, 2 * seq_count * rows * down_width
         ),
         name="down_terms",
-    )(marks, *rank_parts, *column_parts)
-
-    held_down = down_width // batch_count
-    held_up = up_sum.shape[1] // batch_count
+    )(document_lengths, *rank_parts, *column_parts, *up_sums)
+
     if batch_count == 2:
-        ahead = batch_index == 0
-        own_terms = jnp.where(ahead, down_terms[:, :held_down], down_terms[:, held_down:])
-        far_terms = jnp.where(ahead, down_terms[:, held_down:], down_terms[:, :held_down])
-        own_ups = jnp.where(ahead, up_sum[:, :held_up], up_sum[:, held_up:])
-        far_ups = jnp.where(ahead, up_sum[:, held_up:], up_sum[:, :held_up])
-        bank_downs = [own_terms, shift(far_terms, "batch", 1)]
-        bank_ups = [own_ups, shift(far_ups, "batch", 1)]
+        bank_downs = [terms[0], shift(terms[1], "batch", 1)]
+        bank_ups = [terms[2], shift(terms[3], "batch", 1)]
         bank_rows = jnp.concatenate([own_bank, other_bank])
     else:
         down_send = jnp.transpose(
-            down_terms.reshape(SEGS * joint_rank, batch_count, held_down), (1, 0, 2)
+            terms[0].reshape(SEGS * joint_rank, batch_count, held_down), (1, 0, 2)
         )
         up_send = jnp.transpose(
-            up_sum.reshape(SEGS * low_width, batch_count, held_up), (1, 0, 2)
+            terms[1].reshape(SEGS * low_width, batch_count, held_up), (1, 0, 2)
         )
         back_down = lax.all_to_all(down_send, "batch", split_axis=0, concat_axis=0, tiled=True)
         back_up = lax.all_to_all(up_send, "batch", split_axis=0, concat_axis=0, tiled=True)
         bank_downs = [back_down[batch] for batch in range(batch_count)]
         bank_ups = [back_up[batch] for batch in range(batch_count)]
         bank_rows = sample_rows.reshape(-1)
-    down_zeros = jnp.zeros((adapters, joint_rank, 1, held_down), f32)
-    up_zeros = jnp.zeros((adapters, low_width, held_up), f32)
 
     def whole(array):
         return pl.BlockSpec(array.shape, lambda step, bank: (0,) * array.ndim)
@@ -630,7 +703,7 @@
             ),
         ),
         input_output_aliases={1 + 2 * batch_count: 0, 2 + 2 * batch_count: 1},
-        compiler_params=pltpu.CompilerParams(vmem_limit_bytes=vmem_limit),
+        compiler_params=pltpu.CompilerParams(vmem_limit_bytes=16 * mebibyte),
         name="bank_rows",
     )(bank_rows, *bank_downs, *bank_ups, down_zeros, up_zeros)
     return (attention[None], token_grad[None], down_grad, up_grad)

time: 223 us -> 232 us (1.040)
  waiting for transfers between devices: 48.2 us -> 79.8 us
  local copies, waits for them, and re-layouts: 60.6 us -> 45.1 us
  other arithmetic: 12.8 us -> 9.23 us
  starting transfers between devices: 75.6 us -> 72.7 us
    ppermute x4, waiting for transfers between devices: 7.2 us -> 29.3 us  [push(): return lax.ppermute(value, axis, pairs)]
    another operation x7 -> x0, local copies, waits for them, and re-layouts: 11.6 us -> none
    ppermute x35, waiting for transfers between devices: 41 us -> 50.5 us  [shift(): lax.ppermute(value, axis, [(at, (at + steps) % count) for at in range(cou...]
    another operation x11 -> x2, other arithmetic: 5.94 us -> 1.16 us  [the longest x9 4.71 us: shards(): jnp.stack([jnp.stack([jnp.int32(0) + row, jnp.int32(0) + column]) for row...]
    ppermute x35, starting transfers between devices: 67.2 us -> 64.4 us  [shift(): lax.ppermute(value, axis, [(at, (at + steps) % count) for at in range(cou...]
    dynamic_slice x1 -> x0, local copies, waits for them, and re-layouts: 2.56 us -> none  [shards(): lax.dynamic_slice_in_dim(late_tokens, target * down_width, down_width, ax...]
    unnamed x93 -> x123, local copies, waits for them, and re-layouts: 21.2 us -> 19.1 us
  transfers between devices with their start and end apart: 39 -> 39, of which waited for: 16 -> 13; matrix products, arithmetic and copies ran while one was open for 19% -> 13% of each run, Pallas kernels for 7% -> 3%
where the time goes in v3:
time: 232 us; the launch traced here: 231 us
  waiting for transfers between devices  79.8 us (34%)
  starting transfers between devices  72.7 us (31%)
  local copies, waits for them, and re-layouts  45.1 us (19%)
  Pallas kernels  22.1 us (10%)
  other arithmetic  9.23 us (4%)
    ppermute x35, starting transfers between devices, shift(): lax.ppermute(value, axis, [(at, (at + steps) % count) for at in range(cou...  64.4 us
    ppermute x35, waiting for transfers between devices, shift(): lax.ppermute(value, axis, [(at, (at + steps) % count) for at in range(cou...  50.5 us
    ppermute x4, waiting for transfers between devices, push(): return lax.ppermute(value, axis, pairs)  29.3 us
    unnamed x123, local copies, waits for them, and re-layouts  19.1 us
    ppermute x4, starting transfers between devices, push(): return lax.ppermute(value, axis, pairs)  8.26 us
    pallas_call x1, Pallas kernels, shards(): pl.pallas_call(functools.partial(token_kernel, places, down_places, seq_c...  6.03 us
    pallas_call x1, Pallas kernels, shards(): pl.pallas_call(functools.partial(project_kernel, places, down_places, len...  5.15 us
  transfers between devices with their start and end apart: 39, of which 13 were waited for; matrix products, arithmetic and copies ran while one was open for 13% of the time, Pallas kernels for 3%

profile of v3, /device:TPU:0, one launch (start us, length us, event | category | flops | bytes accessed | tf_op | source)
XLA Modules:
  0.0 230.5 jit_solution(3210682830897270365)
XLA Ops:
  1.7 5.1 %collective-permute-start.4 = (bf16[192,896]{1,0:T(8,128)(2,1)S(1)}, bf16[192,896]{1,0:T(8,128)(2,1)S(1)}, u32[]{:S(2)}, u32[]{:S(2)}) collective-permute-start(bf16[192,896]{1,0:T(8,128)(2,1)S(1)} %constant_dynamic-slice_fusion.7), channel_id=1, source_target_pairs={{0,12},{4,0},{8,4},{12,8},{1,13},{5,1},{9,5},{13,9},{2,14},{6,2},{... | collective-permute-start | bytes 1032200 | tf_op jit(solution)/shard_map/ppermute | solution.py:23
  20.6 3.9 %collective-permute-start.19 = (bf16[96,160]{0,1:T(8,128)(2,1)S(1)}, bf16[96,160]{0,1:T(8,128)(2,1)S(1)}, u32[]{:S(2)}, u32[]{:S(2)}) collective-permute-start(bf16[96,160]{0,1:T(8,128)(2,1)S(1)} %copy.57), channel_id=1, source_target_pairs={{0,12},{4,0},{8,4},{12,8},{1,13},{5,1},{9,5},{13,9},{2,14},{6,2},{... | collective-permute-start | bytes 92168 | tf_op jit(solution)/shard_map/ppermute | solution.py:23
  28.5 3.0 %collective-permute-start.8 = (bf16[192,896]{1,0:T(8,128)(2,1)S(1)}, bf16[192,896]{1,0:T(8,128)(2,1)S(1)}, u32[]{:S(2)}, u32[]{:S(2)}) collective-permute-start(bf16[192,896]{1,0:T(8,128)(2,1)S(1)} %collective-permute-done.refs_1_), channel_id=1, source_target_pairs={{0,4},{4,8},{8,12},{12,0},{1,5},{5,9},{9,13},{13,1},{2,6},{6,10},{... | collective-permute-start | bytes 1032200 | tf_op jit(solution)/shard_map/ppermute | solution.py:23
  32.0 4.1 %collective-permute-start.17 = (bf16[96,160]{0,1:T(8,128)(2,1)S(1)}, bf16[96,160]{0,1:T(8,128)(2,1)S(1)}, u32[]{:S(2)}, u32[]{:S(2)}) collective-permute-start(bf16[96,160]{0,1:T(8,128)(2,1)S(1)} %copy.57), channel_id=1, source_target_pairs={{0,4},{4,8},{8,12},{12,0},{1,5},{5,9},{9,13},{13,1},{2,6},{6,10},{... | collective-permute-start | bytes 92168 | tf_op jit(solution)/shard_map/ppermute | solution.py:23
  38.5 8.2 %collective-permute-done.17 = bf16[96,160]{0,1:T(8,128)(2,1)S(1)} collective-permute-done((bf16[96,160]{0,1:T(8,128)(2,1)S(1)}, bf16[96,160]{0,1:T(8,128)(2,1)S(1)}, u32[]{:S(2)}, u32[]{:S(2)}) %collective-permute-start.17) | collective-permute-done | bytes 30752 | tf_op jit(solution)/shard_map/ppermute | solution.py:23
  51.0 3.9 %collective-permute-start.13 = (bf16[128,896]{1,0:T(8,128)(2,1)}, bf16[128,896]{1,0:T(8,128)(2,1)}, u32[]{:S(2)}, u32[]{:S(2)}) collective-permute-start(bf16[128,896]{1,0:T(8,128)(2,1)} %get-tuple-element.60), channel_id=1, source_target_pairs={{0,4},{4,8},{8,12},{12,0},{1,5},{5,9},{9,13},{13,1},{2,6},{6,10},{... | collective-permute-start | bytes 688136 | tf_op jit(solution)/shard_map/ppermute | solution.py:23
  74.0 4.0 %collective-permute-done.2.refs_3_ = bf16[192,896]{1,0:T(8,128)(2,1)S(1)} collective-permute-done((bf16[192,896]{1,0:T(8,128)(2,1)S(1)}, bf16[192,896]{1,0:T(8,128)(2,1)S(1)}, u32[]{:S(2)}, u32[]{:S(2)}) %collective-permute-start.2) | collective-permute-done | bytes 344096 | tf_op jit(solution)/shard_map/ppermute | solution.py:23
  78.0 7.4 %collective-permute-done.10.refs_11_ = bf16[192,896]{1,0:T(8,128)(2,1)S(1)} collective-permute-done((bf16[192,896]{1,0:T(8,128)(2,1)S(1)}, bf16[192,896]{1,0:T(8,128)(2,1)S(1)}, u32[]{:S(2)}, u32[]{:S(2)}) %collective-permute-start.10) | collective-permute-done | bytes 344096 | tf_op jit(solution)/shard_map/ppermute | solution.py:23
  85.3 7.4 %collective-permute-done.3.refs_4_ = bf16[192,896]{1,0:T(8,128)(2,1)S(1)} collective-permute-done((bf16[192,896]{1,0:T(8,128)(2,1)S(1)}, bf16[192,896]{1,0:T(8,128)(2,1)S(1)}, u32[]{:S(2)}, u32[]{:S(2)}) %collective-permute-start.3) | collective-permute-done | bytes 344096 | tf_op jit(solution)/shard_map/ppermute | solution.py:23
  92.7 5.0 %collective-permute-done.11.refs_12_ = bf16[192,896]{1,0:T(8,128)(2,1)S(1)} collective-permute-done((bf16[192,896]{1,0:T(8,128)(2,1)S(1)}, bf16[192,896]{1,0:T(8,128)(2,1)S(1)}, u32[]{:S(2)}, u32[]{:S(2)}) %collective-permute-start.11) | collective-permute-done | bytes 344096 | tf_op jit(solution)/shard_map/ppermute | solution.py:23
  98.0 4.5 %broadcast_in_dim.63.refs_17_.refs_4_ = f32[64,64,1,448]{3,2,1,0:T(1,128)S(1)} broadcast(f32[]{:T(128)} %constant.93.clone.1), dimensions={} | broadcast | bytes 7340036 | tf_op jit(solution)/shard_map/broadcast_in_dim | solution.py:526
  102.7 5.1 %project.1 = (f32[256,896]{1,0:T(8,128)S(1)}, bf16[256,896]{1,0:T(8,128)(2,1)S(1)}, bf16[256,896]{1,0:T(8,128)(2,1)S(1)}, bf16[256,896]{1,0:T(8,128)(2,1)S(1)}, bf16[256,896]{1,0:T(8,128)(2,1)S(1)}) custom-call(s32[2,3]{1,0:T(2,128)S(1)} %copy-done.45, bf16[256,3584]{1,0:T(8,128)(2,1)S(1)} %bitcast.37, bf16[192,3584]{1,0:T(8,128)(2,1)S(1)} %copy-done.3, ...), custom_call_target="tpu_custom_call" | custom-call | flops 1644167168 | bytes 8257536 | tf_op jit(solution)/shard_map/project/pallas_call | solution.py:531
  111.5 4.1 %collective-permute-start.22 = (bf16[256,256]{1,0:T(8,128)(2,1)S(1)}, bf16[256,256]{1,0:T(8,128)(2,1)S(1)}, u32[]{:S(2)}, u32[]{:S(2)}) collective-permute-start(bf16[256,256]{1,0:T(8,128)(2,1)S(1)} %get-tuple-element.30.refs_0_), channel_id=1, source_target_pairs={{0,8},{4,12},{1,9},{5,13},{2,10},{6,14},{3,11},{7,15},{16,24},{20,... | collective-permute-start | bytes 393224 | tf_op jit(solution)/shard_map/ppermute | solution.py:29
  121.5 3.6 %attention.1 = (bf16[128,512]{1,0:T(8,128)(2,1)}, bf16[128,512]{1,0:T(8,128)(2,1)}, f32[3,128,256]{2,1,0:T(8,128)S(1)}, f32[3,128,256]{2,1,0:T(8,128)S(1)}) custom-call(s32[2,3]{1,0:T(2,128)S(1)} %copy-done.45, bf16[512,128]{1,0:T(8,128)(2,1)S(1)} %get-tuple-element.29.queries, bf16[128,512]{1,0:T(8,128)(2,1)S(1)} %bitcast.38, ...), custom_call_target="tpu_custom_call" | custom-call | flops 503316480 | bytes 786432 | tf_op jit(solution)/shard_map/attention/pallas_call | solution.py:579
  130.3 3.4 %collective-permute-start.28 = (bf16[256,896]{1,0:T(8,128)(2,1)}, bf16[256,896]{1,0:T(8,128)(2,1)S(1)}, u32[]{:S(2)}, u32[]{:S(2)}) collective-permute-start(bf16[256,896]{1,0:T(8,128)(2,1)} %copy-done.50), channel_id=1, source_target_pairs={{0,4},{4,8},{8,12},{12,0},{1,5},{5,9},{9,13},{13,1},{2,6},{6,10},{... | collective-permute-start | bytes 1376264 | tf_op jit(solution)/shard_map/ppermute | solution.py:23
  133.7 5.2 %collective-permute-start.29 = (bf16[256,896]{1,0:T(8,128)(2,1)}, bf16[256,896]{1,0:T(8,128)(2,1)S(1)}, u32[]{:S(2)}, u32[]{:S(2)}) collective-permute-start(bf16[256,896]{1,0:T(8,128)(2,1)} %copy-done.49), channel_id=1, source_target_pairs={{0,8},{4,12},{8,0},{12,4},{1,9},{5,13},{9,1},{13,5},{2,10},{6,14},... | collective-permute-start | bytes 1376264 | tf_op jit(solution)/shard_map/ppermute | solution.py:23
  139.1 25.0 %collective-permute-done.26 = f32[128,256]{1,0:T(8,128)} collective-permute-done((f32[128,256]{1,0:T(8,128)}, f32[128,256]{1,0:T(8,128)}, u32[]{:S(2)}, u32[]{:S(2)}) %collective-permute-start.26) | collective-permute-done | bytes 131104 | tf_op jit(solution)/shard_map/ppermute | solution.py:29
  166.4 7.5 %collective-permute-done.29.refs_1_.refs_6_ = bf16[256,896]{1,0:T(8,128)(2,1)S(1)} collective-permute-done((bf16[256,896]{1,0:T(8,128)(2,1)}, bf16[256,896]{1,0:T(8,128)(2,1)S(1)}, u32[]{:S(2)}, u32[]{:S(2)}) %collective-permute-start.29) | collective-permute-done | bytes 458784 | tf_op jit(solution)/shard_map/ppermute | solution.py:23
  176.2 5.6 %collective-permute-start.33 = (bf16[256,64]{1,0:T(8,128)(2,1)S(1)}, bf16[256,64]{1,0:T(8,128)(2,1)S(1)}, u32[]{:S(2)}, u32[]{:S(2)}) collective-permute-start(bf16[256,64]{1,0:T(8,128)(2,1)S(1)} %get-tuple-element.40.rank_grad.refs_0_), channel_id=1, source_target_pairs={{0,12},{4,0},{8,4},{12,8},{1,13},{5,1},{9,5},{13,9},{2,14},{6,2},{... | collective-permute-start | bytes 98312 | tf_op jit(solution)/shard_map/ppermute | solution.py:23
  181.7 4.5 %collective-permute-start.34 = (f32[96,160]{1,0:T(8,128)S(1)}, f32[96,160]{1,0:T(8,128)S(1)}, u32[]{:S(2)}, u32[]{:S(2)}) collective-permute-start(f32[96,160]{1,0:T(8,128)S(1)} %get-tuple-element.43), channel_id=1, source_target_pairs={{0,4},{4,8},{8,12},{12,0},{1,5},{5,9},{9,13},{13,1},{2,6},{6,10},{... | collective-permute-start | bytes 184328 | tf_op jit(solution)/shard_map/ppermute | solution.py:23
  187.6 2.9 %collective-permute-start.36 = (f32[96,160]{1,0:T(8,128)S(1)}, f32[96,160]{1,0:T(8,128)S(1)}, u32[]{:S(2)}, u32[]{:S(2)}) collective-permute-start(f32[96,160]{1,0:T(8,128)S(1)} %get-tuple-element.45), channel_id=1, source_target_pairs={{0,12},{4,0},{8,4},{12,8},{1,13},{5,1},{9,5},{13,9},{2,14},{6,2},{... | collective-permute-start | bytes 184328 | tf_op jit(solution)/shard_map/ppermute | solution.py:23
  190.5 4.6 %collective-permute-start.31 = (bf16[256,64]{1,0:T(8,128)(2,1)S(1)}, bf16[256,64]{1,0:T(8,128)(2,1)S(1)}, u32[]{:S(2)}, u32[]{:S(2)}) collective-permute-start(bf16[256,64]{1,0:T(8,128)(2,1)S(1)} %get-tuple-element.40.rank_grad.refs_0_), channel_id=1, source_target_pairs={{0,4},{4,8},{8,12},{12,0},{1,5},{5,9},{9,13},{13,1},{2,6},{6,10},{... | collective-permute-start | bytes 98312 | tf_op jit(solution)/shard_map/ppermute | solution.py:23
  195.1 6.5 %collective-permute-done.32.refs_2_ = bf16[256,64]{1,0:T(8,128)(2,1)S(1)} collective-permute-done((bf16[256,64]{1,0:T(8,128)(2,1)S(1)}, bf16[256,64]{1,0:T(8,128)(2,1)S(1)}, u32[]{:S(2)}, u32[]{:S(2)}) %collective-permute-start.32) | collective-permute-done | bytes 32800 | tf_op jit(solution)/shard_map/ppermute | solution.py:23
  221.6 6.0 %token_gradient.1 = bf16[256,3584]{1,0:T(8,128)(2,1)} custom-call(s32[2,3]{1,0:T(2,128)S(1)} %copy-done.47, bf16[256,768]{1,0:T(8,128)(2,1)S(1)} %get-tuple-element.39.gradients, bf16[256,64]{1,0:T(8,128)(2,1)S(1)} %get-tuple-element.40.rank_grad.refs_0_, bf16[192,3584]{1,0:T(8,128)(2,1)S(1)} %copy-done.3, bf16[192,896]{1,0:T(8,128)(2,1)S(1)} %copy-done.10, ...), custom_call_target="tpu_custom_call" | custom-call | flops 1644167168 | bytes 8257536 | tf_op jit(solution)/shard_map/token_gradient/pallas_call | solution.py:638
  (230 shorter events, 88.6 us)
Async XLA Ops:
  1.7 35.2 %collective-permute-start.4 = (bf16[192,896]{1,0:T(8,128)(2,1)S(1)}, bf16[192,896]{1,0:T(8,128)(2,1)S(1)}, u32[]{:S(2)}, u32[]{:S(2)}) collective-permute-start(bf16[192,896]{1,0:T(8,128)(2,1)S(1)} %constant_dynamic-slice_fusion.7), channel_id=1, source_target_pairs={{0,12},{4,0},{8,4},{12,8},{1,13},{5,1},{9,5},{13,9},{2,14},{6,2},{... | collective-permute-start | bytes 1032200 | tf_op jit(solution)/shard_map/ppermute | solution.py:23
  6.8 21.7 %collective-permute-start = (bf16[192,896]{1,0:T(8,128)(2,1)S(1)}, bf16[192,896]{1,0:T(8,128)(2,1)S(1)}, u32[]{:S(2)}, u32[]{:S(2)}) collective-permute-start(bf16[192,896]{1,0:T(8,128)(2,1)S(1)} %constant_dynamic-slice_fusion.7), channel_id=1, source_target_pairs={{0,4},{4,8},{8,12},{12,0},{1,5},{5,9},{9,13},{13,1},{2,6},{6,10},{... | collective-permute-start | bytes 1032200 | tf_op jit(solution)/shard_map/ppermute | solution.py:23
  25.5 22.7 %collective-permute-start.15 = (bf16[128,896]{1,0:T(8,128)(2,1)S(1)}, bf16[128,896]{1,0:T(8,128)(2,1)S(1)}, u32[]{:S(2)}, u32[]{:S(2)}) collective-permute-start(bf16[128,896]{1,0:T(8,128)(2,1)S(1)} %get-tuple-element.58), channel_id=1, source_target_pairs={{0,12},{4,0},{8,4},{12,8},{1,13},{5,1},{9,5},{13,9},{2,14},{6,2},{... | collective-permute-start | bytes 688136 | tf_op jit(solution)/shard_map/ppermute | solution.py:23
  26.5 24.5 %collective-permute-start.14 = (bf16[128,896]{1,0:T(8,128)(2,1)S(1)}, bf16[128,896]{1,0:T(8,128)(2,1)S(1)}, u32[]{:S(2)}, u32[]{:S(2)}) collective-permute-start(bf16[128,896]{1,0:T(8,128)(2,1)S(1)} %get-tuple-element.59), channel_id=1, source_target_pairs={{0,8},{4,12},{8,0},{12,4},{1,9},{5,13},{9,1},{13,5},{2,10},{6,14},... | collective-permute-start | bytes 688136 | tf_op jit(solution)/shard_map/ppermute | solution.py:23
  28.5 20.9 %collective-permute-start.8 = (bf16[192,896]{1,0:T(8,128)(2,1)S(1)}, bf16[192,896]{1,0:T(8,128)(2,1)S(1)}, u32[]{:S(2)}, u32[]{:S(2)}) collective-permute-start(bf16[192,896]{1,0:T(8,128)(2,1)S(1)} %collective-permute-done.refs_1_), channel_id=1, source_target_pairs={{0,4},{4,8},{8,12},{12,0},{1,5},{5,9},{9,13},{13,1},{2,6},{6,10},{... | collective-permute-start | bytes 1032200 | tf_op jit(solution)/shard_map/ppermute | solution.py:23
  32.0 14.6 %collective-permute-start.17 = (bf16[96,160]{0,1:T(8,128)(2,1)S(1)}, bf16[96,160]{0,1:T(8,128)(2,1)S(1)}, u32[]{:S(2)}, u32[]{:S(2)}) collective-permute-start(bf16[96,160]{0,1:T(8,128)(2,1)S(1)} %copy.57), channel_id=1, source_target_pairs={{0,4},{4,8},{8,12},{12,0},{1,5},{5,9},{9,13},{13,1},{2,6},{6,10},{... | collective-permute-start | bytes 92168 | tf_op jit(solution)/shard_map/ppermute | solution.py:23
  37.0 31.5 %collective-permute-start.6 = (bf16[192,896]{1,0:T(8,128)(2,1)S(1)}, bf16[192,896]{1,0:T(8,128)(2,1)S(1)}, u32[]{:S(2)}, u32[]{:S(2)}) collective-permute-start(bf16[192,896]{1,0:T(8,128)(2,1)S(1)} %collective-permute-done.4.refs_5_), channel_id=1, source_target_pairs={{0,16},{16,0},{1,17},{17,1},{2,18},{18,2},{3,19},{19,3},{4,20},{20... | collective-permute-start | bytes 1032200 | tf_op jit(solution)/shard_map/ppermute | solution.py:23
  46.7 22.3 %collective-permute-start.5 = (bf16[192,896]{1,0:T(8,128)(2,1)S(1)}, bf16[192,896]{1,0:T(8,128)(2,1)S(1)}, u32[]{:S(2)}, u32[]{:S(2)}) collective-permute-start(bf16[192,896]{1,0:T(8,128)(2,1)S(1)} %collective-permute-done.4.refs_5_), channel_id=1, source_target_pairs={{0,2},{2,0},{1,3},{3,1},{4,6},{6,4},{5,7},{7,5},{8,10},{10,8},{9,1... | collective-permute-start | bytes 1032200 | tf_op jit(solution)/shard_map/ppermute | solution.py:23
  48.9 20.6 %collective-permute-start.1 = (bf16[192,896]{1,0:T(8,128)(2,1)S(1)}, bf16[192,896]{1,0:T(8,128)(2,1)S(1)}, u32[]{:S(2)}, u32[]{:S(2)}) collective-permute-start(bf16[192,896]{1,0:T(8,128)(2,1)S(1)} %collective-permute-done.refs_1_), channel_id=1, source_target_pairs={{0,2},{2,0},{1,3},{3,1},{4,6},{6,4},{5,7},{7,5},{8,10},{10,8},{9,1... | collective-permute-start | bytes 1032200 | tf_op jit(solution)/shard_map/ppermute | solution.py:23
  49.4 22.4 %collective-permute-start.9 = (bf16[192,896]{1,0:T(8,128)(2,1)S(1)}, bf16[192,896]{1,0:T(8,128)(2,1)S(1)}, u32[]{:S(2)}, u32[]{:S(2)}) collective-permute-start(bf16[192,896]{1,0:T(8,128)(2,1)S(1)} %collective-permute-done.8.refs_9_), channel_id=1, source_target_pairs={{0,2},{2,0},{1,3},{3,1},{4,6},{6,4},{5,7},{7,5},{8,10},{10,8},{9,1... | collective-permute-start | bytes 1032200 | tf_op jit(solution)/shard_map/ppermute | solution.py:23
  51.0 15.9 %collective-permute-start.13 = (bf16[128,896]{1,0:T(8,128)(2,1)}, bf16[128,896]{1,0:T(8,128)(2,1)}, u32[]{:S(2)}, u32[]{:S(2)}) collective-permute-start(bf16[128,896]{1,0:T(8,128)(2,1)} %get-tuple-element.60), channel_id=1, source_target_pairs={{0,4},{4,8},{8,12},{12,0},{1,5},{5,9},{9,13},{13,1},{2,6},{6,10},{... | collective-permute-start | bytes 688136 | tf_op jit(solution)/shard_map/ppermute | solution.py:23
  68.5 16.8 %collective-permute-start.10 = (bf16[192,896]{1,0:T(8,128)(2,1)S(1)}, bf16[192,896]{1,0:T(8,128)(2,1)S(1)}, u32[]{:S(2)}, u32[]{:S(2)}) collective-permute-start(bf16[192,896]{1,0:T(8,128)(2,1)S(1)} %collective-permute-done.8.refs_9_), channel_id=1, source_target_pairs={{0,16},{16,0},{1,17},{17,1},{2,18},{18,2},{3,19},{19,3},{4,20},{20... | collective-permute-start | bytes 1032200 | tf_op jit(solution)/shard_map/ppermute | solution.py:23
  69.5 23.2 %collective-permute-start.3 = (bf16[192,896]{1,0:T(8,128)(2,1)S(1)}, bf16[192,896]{1,0:T(8,128)(2,1)S(1)}, u32[]{:S(2)}, u32[]{:S(2)}) collective-permute-start(bf16[192,896]{1,0:T(8,128)(2,1)S(1)} %collective-permute-done.1.refs_2_), channel_id=1, source_target_pairs={{0,16},{16,0},{1,17},{17,1},{2,18},{18,2},{3,19},{19,3},{4,20},{20... | collective-permute-start | bytes 1032200 | tf_op jit(solution)/shard_map/ppermute | solution.py:23
  71.8 25.9 %collective-permute-start.11 = (bf16[192,896]{1,0:T(8,128)(2,1)S(1)}, bf16[192,896]{1,0:T(8,128)(2,1)S(1)}, u32[]{:S(2)}, u32[]{:S(2)}) collective-permute-start(bf16[192,896]{1,0:T(8,128)(2,1)S(1)} %collective-permute-done.9.refs_10_), channel_id=1, source_target_pairs={{0,16},{16,0},{1,17},{17,1},{2,18},{18,2},{3,19},{19,3},{4,20},{20... | collective-permute-start | bytes 1032200 | tf_op jit(solution)/shard_map/ppermute | solution.py:23
  129.0 35.1 %collective-permute-start.26 = (f32[128,256]{1,0:T(8,128)}, f32[128,256]{1,0:T(8,128)}, u32[]{:S(2)}, u32[]{:S(2)}) collective-permute-start(f32[128,256]{1,0:T(8,128)} %get-tuple-element.55), channel_id=1, source_target_pairs={{8,0},{12,4},{9,1},{13,5},{10,2},{14,6},{11,3},{15,7},{24,16},{28,... | collective-permute-start | bytes 393224 | tf_op jit(solution)/shard_map/ppermute | solution.py:29
  130.3 36.1 %collective-permute-start.28 = (bf16[256,896]{1,0:T(8,128)(2,1)}, bf16[256,896]{1,0:T(8,128)(2,1)S(1)}, u32[]{:S(2)}, u32[]{:S(2)}) collective-permute-start(bf16[256,896]{1,0:T(8,128)(2,1)} %copy-done.50), channel_id=1, source_target_pairs={{0,4},{4,8},{8,12},{12,0},{1,5},{5,9},{9,13},{13,1},{2,6},{6,10},{... | collective-permute-start | bytes 1376264 | tf_op jit(solution)/shard_map/ppermute | solution.py:23
  133.7 40.2 %collective-permute-start.29 = (bf16[256,896]{1,0:T(8,128)(2,1)}, bf16[256,896]{1,0:T(8,128)(2,1)S(1)}, u32[]{:S(2)}, u32[]{:S(2)}) collective-permute-start(bf16[256,896]{1,0:T(8,128)(2,1)} %copy-done.49), channel_id=1, source_target_pairs={{0,8},{4,12},{8,0},{12,4},{1,9},{5,13},{9,1},{13,5},{2,10},{6,14},... | collective-permute-start | bytes 1376264 | tf_op jit(solution)/shard_map/ppermute | solution.py:23
  138.9 35.0 %collective-permute-start.30 = (bf16[256,896]{1,0:T(8,128)(2,1)}, bf16[256,896]{1,0:T(8,128)(2,1)S(1)}, u32[]{:S(2)}, u32[]{:S(2)}) collective-permute-start(bf16[256,896]{1,0:T(8,128)(2,1)} %copy-done.48), channel_id=1, source_target_pairs={{0,12},{4,0},{8,4},{12,8},{1,13},{5,1},{9,5},{13,9},{2,14},{6,2},{... | collective-permute-start | bytes 1376264 | tf_op jit(solution)/shard_map/ppermute | solution.py:23
  139.1 34.7 %collective-permute-start.23 = (bf16[128,512]{1,0:T(8,128)(2,1)}, bf16[128,512]{1,0:T(8,128)(2,1)S(1)}, u32[]{:S(2)}, u32[]{:S(2)}) collective-permute-start(bf16[128,512]{1,0:T(8,128)(2,1)} %get-tuple-element.32.own_query), channel_id=1, source_target_pairs={{0,1},{1,0},{2,3},{3,2},{4,5},{5,4},{6,7},{7,6},{8,9},{9,8},{10,11... | collective-permute-start | bytes 393224 | tf_op jit(solution)/shard_map/ppermute | solution.py:23
  176.2 14.4 %collective-permute-start.33 = (bf16[256,64]{1,0:T(8,128)(2,1)S(1)}, bf16[256,64]{1,0:T(8,128)(2,1)S(1)}, u32[]{:S(2)}, u32[]{:S(2)}) collective-permute-start(bf16[256,64]{1,0:T(8,128)(2,1)S(1)} %get-tuple-element.40.rank_grad.refs_0_), channel_id=1, source_target_pairs={{0,12},{4,0},{8,4},{12,8},{1,13},{5,1},{9,5},{13,9},{2,14},{6,2},{... | collective-permute-start | bytes 98312 | tf_op jit(solution)/shard_map/ppermute | solution.py:23
  181.7 19.9 %collective-permute-start.34 = (f32[96,160]{1,0:T(8,128)S(1)}, f32[96,160]{1,0:T(8,128)S(1)}, u32[]{:S(2)}, u32[]{:S(2)}) collective-permute-start(f32[96,160]{1,0:T(8,128)S(1)} %get-tuple-element.43), channel_id=1, source_target_pairs={{0,4},{4,8},{8,12},{12,0},{1,5},{5,9},{9,13},{13,1},{2,6},{6,10},{... | collective-permute-start | bytes 184328 | tf_op jit(solution)/shard_map/ppermute | solution.py:23
  186.2 15.4 %collective-permute-start.35 = (f32[96,160]{1,0:T(8,128)S(1)}, f32[96,160]{1,0:T(8,128)S(1)}, u32[]{:S(2)}, u32[]{:S(2)}) collective-permute-start(f32[96,160]{1,0:T(8,128)S(1)} %get-tuple-element.44), channel_id=1, source_target_pairs={{0,8},{4,12},{8,0},{12,4},{1,9},{5,13},{9,1},{13,5},{2,10},{6,14},... | collective-permute-start | bytes 184328 | tf_op jit(solution)/shard_map/ppermute | solution.py:23
  204.5 23.1 %collective-permute-start.37 = (f32[192,448]{1,0:T(8,128)S(1)}, f32[192,448]{1,0:T(8,128)S(1)}, u32[]{:S(2)}, u32[]{:S(2)}) collective-permute-start(f32[192,448]{1,0:T(8,128)S(1)} %get-tuple-element.47), channel_id=1, source_target_pairs={{0,2},{2,0},{1,3},{3,1},{4,6},{6,4},{5,7},{7,5},{8,10},{10,8},{9,1... | collective-permute-start | bytes 1032200 | tf_op jit(solution)/shard_map/ppermute | solution.py:23
  205.8 21.8 %collective-permute-start.38 = (f32[96,80]{1,0:T(8,128)S(1)}, f32[96,80]{1,0:T(8,128)S(1)}, u32[]{:S(2)}, u32[]{:S(2)}) collective-permute-start(f32[96,80]{1,0:T(8,128)S(1)} %get-tuple-element.49), channel_id=1, source_target_pairs={{0,2},{2,0},{1,3},{3,1},{4,6},{6,4},{5,7},{7,5},{8,10},{10,8},{9,1... | collective-permute-start | bytes 92168 | tf_op jit(solution)/shard_map/ppermute | solution.py:23
  (76 other events, 739.6 us)

commit v4 on v3

--- a/solution.py
+++ b/solution.py
@@ -86,21 +86,18 @@
     return pl.BlockSpec(memory_space=pl.ANY)
 
 
-def fetch_pieces(places, pieces, target, semaphore, first):
-    copies = []
-    for number, (place, piece) in enumerate(zip(places, pieces)):
-        height, width = piece.shape
-        row, column = place()
-        copy = pltpu.make_async_copy(
-            piece,
-            target.at[
-                pl.ds(pl.multiple_of(row, 16), height), pl.ds(pl.multiple_of(column, 128), width)
-            ],
-            semaphore.at[first + number],
-        )
-        copy.start()
-        copies.append(copy)
-    return copies
+def fetch(piece, target, place, semaphore):
+    height, width = piece.shape
+    row, column = place()
+    copy = pltpu.make_async_copy(
+        piece,
+        target.at[
+            pl.ds(pl.multiple_of(row, 16), height), pl.ds(pl.multiple_of(column, 128), width)
+        ],
+        semaphore,
+    )
+    copy.start()
+    return copy
 
 
 def frozen_place(seq_count, rows, share, behind, batch_step, group_step):
@@ -132,29 +129,116 @@
     return row_segments(ends, row_positions(seq_index * rows, rows)) != first
 
 
+def select_kernel(bank_row, adapters, down_bank, up_bank, *refs):
+    outputs, semaphore = refs[:4], refs[4]
+    batch = lax.axis_index("batch")
+    copies = []
+    for which, sample in enumerate((batch, 1 - batch)):
+        for document in range(SEGS):
+            row = bank_row[adapters[sample, document]]
+            for source, target in ((down_bank, outputs[which]), (up_bank, outputs[2 + which])):
+                copy = pltpu.make_async_copy(
+                    source.at[row], target.at[document], semaphore.at[len(copies)]
+                )
+                copy.start()
+                copies.append(copy)
+    for copy in copies:
+        copy.wait()
+
+
+def pack_kernel(unused, seq_count, own_down, far_down, own_up, far_up, tokens, *refs):
+    refs = refs[unused:]
+    payloads, columns = refs[:seq_count], refs[seq_count : 2 * seq_count]
+    down, up = refs[2 * seq_count :]
+    ahead = lax.axis_index("batch") == 0
+    joint_rank, held = own_down.shape[1:]
+    low_width, held_up = own_up.shape[1:]
+    for document in range(SEGS):
+        rows = slice(document * joint_rank, (document + 1) * joint_rank)
+        down[rows, :held] = jnp.where(ahead, own_down[document], far_down[document])
+        down[rows, held:] = jnp.where(ahead, far_down[document], own_down[document])
+        up[document, :, :held_up] = jnp.where(ahead, own_up[document], far_up[document])
+        up[document, :, held_up:] = jnp.where(ahead, far_up[document], own_up[document])
+    half, slot = low_width // 2, down.shape[1] // 4
+    for steps in range(seq_count):
+        target = ring_index(lax.axis_index("seq") + steps - seq_count, seq_count)
+        first = (target >= seq_count // 2).astype(jnp.int32)
+        start = pl.multiple_of(first * joint_rank, joint_rank)
+        payload = payloads[steps]
+        payload[: 2 * joint_rank] = down[pl.ds(start, 2 * joint_rank)]
+        for index in range(2):
+            block = up[first + index]
+            for part in range(2):
+                column = (2 * index + part) * slot
+                payload[2 * joint_rank :, column : column + 2 * held_up] = block[
+                    part * half : (part + 1) * half
+                ]
+        width = columns[steps].shape[1]
+        columns[steps][...] = tokens[:, pl.ds(pl.multiple_of(target * width, 128), width)]
+
+
+def assemble_up(seq_count, arrived, up_blocks):
+    low_width = up_blocks.shape[1] // 2
+    query_columns = QHEADS * HEAD_WIDTH
+    seq_index = lax.axis_index("seq")
+    first = (seq_index >= seq_count // 2).astype(jnp.int32)
+    held = up_blocks.shape[2] // seq_count
+    half, slot = low_width // 2, arrived.shape[2] // 4
+    up_blocks[...] = jnp.zeros_like(up_blocks)
+    for holder in range(seq_count):
+        block = arrived[ring_index(seq_index - holder, seq_count)]
+        start, stop = holder * held, (holder + 1) * held
+        middle = min(max(query_columns, start), stop)
+        for index in range(2):
+            for part in range(2):
+                offset = (2 * index + part) * slot
+                if middle > start:
+                    up_blocks[first + index, part * half : (part + 1) * half, start:middle] = block[
+                        :, offset : offset + middle - start
+                    ]
+                if stop > middle:
+                    low = low_width + part * half
+                    up_blocks[first + index, low : low + half, middle:stop] = block[
+                        :, offset + middle - start : offset + held
+                    ]
+
+
 def project_kernel(frozen_places, down_places, unused, seq_count, lengths, tokens, *refs):
     frozen_count, down_count = len(frozen_places), len(down_places)
     frozen_pieces = refs[:frozen_count]
     down_pieces = refs[frozen_count : frozen_count + down_count]
     refs = refs[frozen_count + down_count + unused :]
-    part, columns, (frozen, down, semaphore) = refs[0], refs[1:-3], refs[-3:]
-    copies = fetch_pieces(frozen_places, frozen_pieces, frozen, semaphore, 0)
-    copies += fetch_pieces(down_places, down_pieces, down, semaphore, frozen_count)
-    rows, width = tokens.shape
-    for steps, block in enumerate(columns):
-        target = ring_index(lax.axis_index("seq") + steps - seq_count, seq_count)
-        held = block.shape[1]
-        block[...] = tokens[:, pl.ds(pl.multiple_of(target * held, 128), held)]
+    packed = down_count > 1
+    part, frozen, down = refs[:3]
+    semaphore = refs[-1]
+    copies = []
+    for piece, place in zip(frozen_pieces, frozen_places):
+        copies.append(fetch(piece, frozen, place, semaphore.at[len(copies)]))
+    joint_rank = down.shape[0] // 2
+    for number, (piece, place) in enumerate(zip(down_pieces, down_places)):
+        rows = piece.at[pl.ds(0, 2 * joint_rank)] if packed else piece
+        copies.append(fetch(rows, down, place, semaphore.at[len(copies)]))
+        if packed:
+            extra = piece.shape[0] - 2 * joint_rank
+            copy = pltpu.make_async_copy(
+                piece.at[pl.ds(2 * joint_rank, extra)],
+                refs[4].at[number],
+                semaphore.at[len(copies)],
+            )
+            copy.start()
+            copies.append(copy)
     for copy in copies:
         copy.wait()
+    rows = tokens.shape[0]
     features = frozen.shape[0]
-    joint_rank = down.shape[0] // 2
     second = second_document(kernel_marks(lengths), rows, seq_count)
     values = tokens[...]
     part[:, :features] = dot_nt(values, frozen[...])
     first_low = dot_nt(values, down[:joint_rank])
     second_low = dot_nt(values, down[joint_rank:])
     part[:, features : features + joint_rank] = jnp.where(second, second_low, first_low)
+    if packed:
+        assemble_up(seq_count, refs[4], refs[3])
 
 
 def rotated(values, cosines, sines):
@@ -198,9 +282,9 @@
         queries[head * own_rows : (head + 1) * own_rows] = turned.astype(jnp.bfloat16)
 
 
-def attention_kernel(block_count, lengths, queries, incoming, cosines, sines, *refs):
+def attention_kernel(block_count, unused, lengths, queries, incoming, cosines, sines, *refs):
     blocks = refs[:block_count]
-    output, query_grad, kept, sent, low_probs = refs[block_count:]
+    output, query_grad, kept, sent, low_probs = refs[block_count + unused :]
     own_rows, query_columns = incoming.shape
     rows = blocks[0].shape[0]
     score_scale = HEAD_WIDTH ** (-0.5)
@@ -298,15 +382,7 @@
         block[...] = blocks[ring_index(seq_index + steps - seq_count, seq_count)]
 
 
-def token_kernel(frozen_places, down_places, seq_count, lengths, gradients, rank_grad, *refs):
-    frozen_count, down_count = len(frozen_places), len(down_places)
-    frozen_pieces = refs[:frozen_count]
-    down_pieces = refs[frozen_count : frozen_count + down_count]
-    token_grad, frozen, down, semaphore = refs[frozen_count + down_count :]
-    copies = fetch_pieces(frozen_places, frozen_pieces, frozen, semaphore, 0)
-    copies += fetch_pieces(down_places, down_pieces, down, semaphore, frozen_count)
-    for copy in copies:
-        copy.wait()
+def token_kernel(seq_count, lengths, gradients, rank_grad, frozen, down, token_grad):
     rows = gradients.shape[0]
     joint_rank = down.shape[0] // 2
     second = second_document(kernel_marks(lengths), rows, seq_count)
@@ -363,13 +439,14 @@
     up_terms = refs[block_count : 2 * block_count]
     down_out, up_out = refs[2 * block_count + 2 :]
     step = pl.program_id(0)
+    row = bank_rows[step]
     joint_rank = down_out.shape[1]
     low_width = up_out.shape[1]
     down_total = jnp.zeros((joint_rank, down_out.shape[3]), jnp.float32)
     up_total = jnp.zeros((low_width, up_out.shape[2]), jnp.float32)
     for block in range(block_count):
         for document in range(SEGS):
-            same = bank_rows[block * SEGS + document] == bank_rows[step]
+            same = bank_rows[block * SEGS + document] == row
             down_rows = down_terms[block][document * joint_rank : (document + 1) * joint_rank]
             up_rows = up_terms[block][document * low_width : (document + 1) * low_width]
             down_total += jnp.where(same, down_rows, 0.0)
@@ -408,18 +485,25 @@
     bf16 = jnp.bfloat16
     f32 = jnp.float32
 
-    sample_rows = lookup_rows(adapter_bank_row, document_adapter)
     lengths = lax.dynamic_index_in_dim(document_lengths, batch_index, 0, keepdims=False)
-    ends = jnp.cumsum(lengths)
+    first_end = lengths[0]
+    second_end = first_end + lengths[1]
     half_count = seq_count // 2
-
-    def first_document(holder):
-        return (holder >= half_count).astype(jnp.int32)
 
     plane_count = group_count * batch_count
     share = width // plane_count
     pieces, places = [], []
-    direct = group_count == 2 and batch_count == 2 and share % 128 == 0 and frozen_rows % 16 == 0
+    held_down = adapter_down_weight.shape[3]
+    held_up = adapter_up_weight.shape[2]
+    down_width = held_down * batch_count
+    direct = (
+        group_count == 2
+        and batch_count == 2
+        and share % 128 == 0
+        and down_width % 128 == 0
+        and frozen_rows % 16 == 0
+        and 4 * 2 * held_up <= down_width
+    )
     if direct:
         own_share = lax.dynamic_slice_in_dim(
             frozen_qkv_matrix, (group_index * batch_count + batch_index) * share, share, axis=1
@@ -456,94 +540,66 @@
         places.append(whole_place)
 
     down_bank = adapter_down_weight[:, :, 0, :]
-    if batch_count == 2:
-        own_bank = lax.dynamic_index_in_dim(sample_rows, batch_index, 0, keepdims=False)
-        other_bank = lax.dynamic_index_in_dim(sample_rows, 1 - batch_index, 0, keepdims=False)
-        own_down, own_up = down_bank[own_bank], adapter_up_weight[own_bank]
-        far_down = shift(down_bank[other_bank], "batch", 1)
-        far_up = shift(adapter_up_weight[other_bank], "batch", 1)
-        ahead = batch_index == 0
-        down_block = jnp.concatenate(
-            [jnp.where(ahead, own_down, far_down), jnp.where(ahead, far_down, own_down)], axis=2
-        )
-        up_block = jnp.concatenate(
-            [jnp.where(ahead, own_up, far_up), jnp.where(ahead, far_up, own_up)], axis=2
-        )
+    column_blocks, up_blocks = None, None
+    if direct:
+        row_shapes = [(SEGS, joint_rank, held_down)] * 2 + [(SEGS, low_width, held_up)] * 2
+        own_down, far_down, own_up, far_up = pl.pallas_call(
+            select_kernel,
+            out_shape=[jax.ShapeDtypeStruct(shape, bf16) for shape in row_shapes],
+            in_specs=[in_smem()] * 2 + [in_place()] * 2,
+            out_specs=[in_place()] * 4,
+            scratch_shapes=[pltpu.SemaphoreType.DMA((4 * SEGS,))],
+            cost_estimate=cost(0, 4 * SEGS * joint_rank * held_down * 2),
+            name="select",
+        )(adapter_bank_row, document_adapter, down_bank, adapter_up_weight)
+        far_down = shift(far_down, "batch", 1)
+        far_up = shift(far_up, "batch", 1)
+        payload_rows = 2 * joint_rank + low_width // 2
+        packed = pl.pallas_call(
+            functools.partial(pack_kernel, 1, seq_count),
+            out_shape=[jax.ShapeDtypeStruct((payload_rows, down_width), bf16)] * seq_count
+            + [jax.ShapeDtypeStruct((rows, down_width), bf16)] * seq_count,
+            in_specs=[in_vmem()] * 5 + [in_place()],
+            out_specs=[in_vmem()] * (2 * seq_count),
+            scratch_shapes=[
+                pltpu.VMEM((SEGS * joint_rank, down_width), bf16),
+                pltpu.VMEM((SEGS, low_width, 2 * held_up), bf16),
+            ],
+            compiler_params=pltpu.CompilerParams(vmem_limit_bytes=8 * mebibyte),
+            cost_estimate=cost(0, 4 * rows * width),
+            name="pack",
+        )(own_down, far_down, own_up, far_up, local_tokens, before)
+        column_blocks = packed[seq_count:]
+        down_parts = [
+            shift(part, "seq", steps) if steps else part
+            for steps, part in enumerate(packed[:seq_count])
+        ]
+        down_places = [down_place(seq_count, down_width, steps) for steps in range(seq_count)]
     else:
+        sample_rows = lookup_rows(adapter_bank_row, document_adapter)
         got_down = lax.all_to_all(
             down_bank[sample_rows], "batch", split_axis=0, concat_axis=0, tiled=True
         )
         got_up = lax.all_to_all(
             adapter_up_weight[sample_rows], "batch", split_axis=0, concat_axis=0, tiled=True
         )
-        down_block = jnp.transpose(got_down, (1, 2, 0, 3)).reshape(SEGS, joint_rank, -1)
-        up_block = jnp.transpose(got_up, (1, 2, 0, 3)).reshape(SEGS, low_width, -1)
-    down_block = down_block.reshape(SEGS * joint_rank, -1)
-    up_block = up_block.reshape(SEGS * low_width, -1)
-    down_width = down_block.shape[1]
-    down_parts, down_places, up_parts = [], [], []
-    for steps in range(seq_count):
-        target = jnp.remainder(seq_index + steps, seq_count)
-        part = lax.dynamic_slice_in_dim(
-            down_block, first_document(target) * joint_rank, 2 * joint_rank
+        down_block = jnp.transpose(got_down, (1, 2, 0, 3)).reshape(SEGS * joint_rank, -1)
+        up_block = jnp.transpose(got_up, (1, 2, 0, 3)).reshape(SEGS * low_width, -1)
+        all_down = lax.all_gather(down_block, "seq", axis=0)
+        all_up = lax.all_gather(up_block, "seq", axis=0)
+        first = (seq_index >= half_count).astype(jnp.int32)
+        merged = jnp.transpose(all_down, (1, 0, 2)).reshape(SEGS * joint_rank, -1)
+        down_parts = [lax.dynamic_slice_in_dim(merged, first * joint_rank, 2 * joint_rank)]
+        down_places = [whole_place]
+        up_rows = jnp.transpose(all_up, (1, 0, 2)).reshape(SEGS, low_width, -1)
+        is_query = jnp.arange(up_rows.shape[2]) < query_columns
+        up_blocks = jnp.concatenate(
+            [
+                jnp.where(is_query[None, None, :], up_rows, 0),
+                jnp.where(is_query[None, None, :], 0, up_rows),
+            ],
+            axis=1,
         )
-        down_parts.append(shift(part, "seq", steps) if steps else part)
-        down_places.append(down_place(seq_count, down_width, steps))
-        up_parts.append(shift(up_block, "seq", steps) if steps else up_block)
-    relative = jnp.remainder(seq_index - jnp.arange(seq_count, dtype=jnp.int32), seq_count)
-    up_rows = jnp.stack(up_parts)[relative]
-    up_rows = jnp.transpose(up_rows, (1, 0, 2)).reshape(SEGS, low_width, -1)
-    is_query = jnp.arange(up_rows.shape[2]) < query_columns
-    up_blocks = jnp.concatenate(
-        [
-            jnp.where(is_query[None, None, :], up_rows, 0),
-            jnp.where(is_query[None, None, :], 0, up_rows),
-        ],
-        axis=1,
-    )
-    if down_width % 128 != 0:
-        merged = jnp.stack(down_parts)[relative]
-        merged = jnp.transpose(merged, (1, 0, 2)).reshape(2 * joint_rank, -1)
-        down_parts, down_places = [merged], [whole_place]
-
-    positions = seq_index * rows + jnp.arange(rows, dtype=jnp.int32)
-    inside = positions - jnp.where(
-        positions >= ends[1], ends[1], jnp.where(positions >= ends[0], ends[0], 0)
-    )
-    exponent = jnp.arange(HEAD_WIDTH // 2, dtype=f32) * (2.0 / HEAD_WIDTH)
-    angles = inside.astype(f32)[:, None] * jnp.power(jnp.float32(rope_base), -exponent)[None, :]
-    cosines = jnp.tile(jnp.cos(angles), (1, 2))
-    sines = jnp.concatenate([-jnp.sin(angles), jnp.sin(angles)], axis=1)
-
-    scratch = [
-        pltpu.VMEM((features, width), bf16),
-        pltpu.VMEM((2 * joint_rank, width), bf16),
-        pltpu.SemaphoreType.DMA((len(pieces) + len(down_parts),)),
-    ]
-    weight_bytes = 2 * width * (features + 2 * joint_rank)
-    held_down = down_width // batch_count
-    held_up = up_blocks.shape[2] // (seq_count * batch_count)
-    down_zeros = jnp.zeros((adapters, joint_rank, 1, held_down), f32)
-    up_zeros = jnp.zeros((adapters, low_width, held_up), f32)
-    early = [down_zeros, up_zeros, cosines, sines, up_blocks]
-    part_width = features + 128
-    column_count = seq_count if down_width % 128 == 0 else 0
-    part, *column_blocks = pl.pallas_call(
-        functools.partial(project_kernel, places, down_places, len(early), seq_count),
-        out_shape=[jax.ShapeDtypeStruct((rows, part_width), f32)]
-        + [jax.ShapeDtypeStruct((rows, down_width), bf16)] * column_count,
-        in_specs=[in_smem(), in_vmem()]
-        + [in_place()] * (len(pieces) + len(down_parts) + len(early)),
-        out_specs=[in_vmem()] * (1 + column_count),
-        scratch_shapes=scratch,
-        compiler_params=pltpu.CompilerParams(vmem_limit_bytes=20 * mebibyte),
-        cost_estimate=cost(
-            2 * rows * width * (features + 2 * joint_rank), weight_bytes + 2 * rows * width
-        ),
-        name="project",
-    )(document_lengths, local_tokens, *pieces, *down_parts, *early)
-
-    if column_count == 0:
         column_blocks = [
             lax.dynamic_slice_in_dim(
                 local_tokens,
@@ -553,6 +609,47 @@
             )
             for steps in range(seq_count)
         ]
+
+    positions = seq_index * rows + jnp.arange(rows, dtype=jnp.int32)
+    inside = positions - jnp.where(
+        positions >= second_end, second_end, jnp.where(positions >= first_end, first_end, 0)
+    )
+    exponent = jnp.arange(HEAD_WIDTH // 2, dtype=f32) * (2.0 / HEAD_WIDTH)
+    inverse = jnp.power(jnp.float32(rope_base), -exponent)
+    angles = inside.astype(f32)[:, None] * jnp.concatenate([inverse, inverse])[None, :]
+    signs = jnp.where(jnp.arange(HEAD_WIDTH) < HEAD_WIDTH // 2, -1.0, 1.0).astype(f32)
+    cosines = jnp.cos(angles)
+    sines = jnp.sin(angles) * signs[None, :]
+
+    sample_rows = lookup_rows(adapter_bank_row, document_adapter)
+    down_zeros = jnp.zeros((adapters, joint_rank, 1, held_down), f32)
+    up_zeros = jnp.zeros((adapters, low_width, held_up), f32)
+    early = [down_zeros, up_zeros, cosines, sines]
+    up_shape = jax.ShapeDtypeStruct((SEGS, joint_rank, query_columns + HEAD_WIDTH), bf16)
+    arrived = [pltpu.VMEM((seq_count, low_width // 2, down_width), bf16)] if direct else []
+    weight_bytes = 2 * width * (features + 2 * joint_rank)
+    part, frozen, down, *built = pl.pallas_call(
+        functools.partial(project_kernel, places, down_places, len(early), seq_count),
+        out_shape=[
+            jax.ShapeDtypeStruct((rows, features + 128), f32),
+            jax.ShapeDtypeStruct((features, width), bf16),
+            jax.ShapeDtypeStruct((2 * joint_rank, width), bf16),
+        ]
+        + ([up_shape] if direct else []),
+        in_specs=[in_smem(), in_vmem()]
+        + [in_place()] * (len(pieces) + len(down_parts) + len(early)),
+        out_specs=[in_vmem()] * (4 if direct else 3),
+        scratch_shapes=arrived
+        + [pltpu.SemaphoreType.DMA((len(pieces) + 2 * len(down_parts),))],
+        compiler_params=pltpu.CompilerParams(vmem_limit_bytes=12 * mebibyte),
+        cost_estimate=cost(
+            2 * rows * width * (features + 2 * joint_rank), weight_bytes + 2 * rows * width
+        ),
+        name="project",
+    )(document_lengths, local_tokens, *pieces, *down_parts, *early)
+    if direct:
+        up_blocks = built[0]
+
     column_parts = [
         shift(block, "seq", steps) if steps else block
         for steps, block in enumerate(column_blocks)
@@ -576,15 +673,18 @@
     blocks = [pairs] + [push(pairs, "seq", back) for back in range(1, half_count + 1)]
     block_count = len(blocks)
     incoming = output_gradient[0]
+    early_columns = [column_parts[1], column_parts[-1]]
     attention, query_grad, kept, sent = pl.pallas_call(
-        functools.partial(attention_kernel, block_count),
+        functools.partial(attention_kernel, block_count, len(early_columns)),
         out_shape=(
             jax.ShapeDtypeStruct((own_rows, query_columns), bf16),
             jax.ShapeDtypeStruct((own_rows, query_columns), bf16),
             jax.ShapeDtypeStruct((block_count, own_rows, 2 * HEAD_WIDTH), f32),
             jax.ShapeDtypeStruct((block_count, own_rows, 2 * HEAD_WIDTH), f32),
         ),
-        in_specs=[in_smem()] + [in_vmem()] * (4 + block_count),
+        in_specs=[in_smem()]
+        + [in_vmem()] * (4 + block_count)
+        + [in_place()] * len(early_columns),
         out_specs=(in_vmem(),) * 4,
         scratch_shapes=[pltpu.VMEM((block_count, QHEADS * own_rows, rows), bf16)],
         compiler_params=pltpu.CompilerParams(vmem_limit_bytes=(4 + 4 * block_count) * mebibyte),
@@ -594,7 +694,7 @@
             block_count * QHEADS * own_rows * rows,
         ),
         name="attention",
-    )(document_lengths, queries, incoming, cosines, sines, *blocks)
+    )(document_lengths, queries, incoming, cosines, sines, *blocks, *early_columns)
 
     other_query = shift(query_grad, "tp", 1)
     pair_sums = kept + shift(sent, "tp", 1)
@@ -610,13 +710,13 @@
     other_pair = shift(pair_grad, "tp", 1)
 
     gradients, rank_grad, *up_split = pl.pallas_call(
-        functools.partial(rank_kernel, seq_count - 1, seq_count),
+        functools.partial(rank_kernel, 0, seq_count),
         out_shape=[
             jax.ShapeDtypeStruct((rows, features), bf16),
             jax.ShapeDtypeStruct((rows, joint_rank), bf16),
         ]
         + [jax.ShapeDtypeStruct((SEGS * low_width, held_up * batch_count), f32)] * seq_count,
-        in_specs=[in_smem()] + [in_vmem()] * 6 + [in_place()] * (seq_count - 1),
+        in_specs=[in_smem()] + [in_vmem()] * 6,
         out_specs=[in_vmem()] * (2 + seq_count),
         scratch_shapes=[
             pltpu.VMEM((SEGS * low_width, features - HEAD_WIDTH), f32),
@@ -626,8 +726,7 @@
         cost_estimate=cost(4 * rows * 3 * 64 * 640, 4 * rows * features),
         name="rank_gradients",
     )(
-        document_lengths, query_grad, other_query, pair_grad, other_pair, low_rank, up_blocks,
-        *column_parts[1:],
+        document_lengths, query_grad, other_query, pair_grad, other_pair, low_rank, up_blocks
     )
 
     rank_parts = [rank_grad] + [shift(rank_grad, "seq", steps) for steps in range(1, seq_count)]
@@ -636,18 +735,16 @@
     ]
 
     token_grad = pl.pallas_call(
-        functools.partial(token_kernel, places, down_places, seq_count),
+        functools.partial(token_kernel, seq_count),
         out_shape=jax.ShapeDtypeStruct((rows, width), bf16),
-        in_specs=[in_smem(), in_vmem(), in_vmem()]
-        + [in_place()] * (len(pieces) + len(down_parts)),
+        in_specs=[in_smem()] + [in_vmem()] * 4,
         out_specs=in_vmem(),
-        scratch_shapes=scratch,
-        compiler_params=pltpu.CompilerParams(vmem_limit_bytes=20 * mebibyte),
+        compiler_params=pltpu.CompilerParams(vmem_limit_bytes=8 * mebibyte),
         cost_estimate=cost(
             2 * rows * width * (features + 2 * joint_rank), weight_bytes + 2 * rows * width
         ),
         name="token_gradient",
-    )(document_lengths, gradients, rank_grad, *pieces, *down_parts)
+    )(document_lengths, gradients, rank_grad, frozen, down)
 
     if batch_count == 2:
         term_shapes = [(SEGS * joint_rank, held_down)] * 2 + [(SEGS * low_width, held_up)] * 2
@@ -668,7 +765,7 @@
     if batch_count == 2:
         bank_downs = [terms[0], shift(terms[1], "batch", 1)]
         bank_ups = [terms[2], shift(terms[3], "batch", 1)]
-        bank_rows = jnp.concatenate([own_bank, other_bank])
+        sample_rows = jnp.where(batch_index == 0, sample_rows, sample_rows[::-1])
     else:
         down_send = jnp.transpose(
             terms[0].reshape(SEGS * joint_rank, batch_count, held_down), (1, 0, 2)
@@ -680,7 +777,8 @@
         back_up = lax.all_to_all(up_send, "batch", split_axis=0, concat_axis=0, tiled=True)
         bank_downs = [back_down[batch] for batch in range(batch_count)]
         bank_ups = [back_up[batch] for batch in range(batch_count)]
-        bank_rows = sample_rows.reshape(-1)
+
+    bank_rows = sample_rows.reshape(-1)
 
     def whole(array):
         return pl.BlockSpec(array.shape, lambda step, bank: (0,) * array.ndim)
@@ -697,15 +795,25 @@
             in_specs=[whole(array) for array in bank_downs + bank_ups] + [in_place()] * 2,
             out_specs=(
                 pl.BlockSpec(
-                    (1, joint_rank, 1, held_down), lambda step, bank: (bank[step], 0, 0, 0)
+                    (1, joint_rank, 1, held_down),
+                    lambda step, bank: (bank[step], 0, 0, 0),
                 ),
-                pl.BlockSpec((1, low_width, held_up), lambda step, bank: (bank[step], 0, 0)),
+                pl.BlockSpec(
+                    (1, low_width, held_up),
+                    lambda step, bank: (bank[step], 0, 0),
+                ),
             ),
         ),
         input_output_aliases={1 + 2 * batch_count: 0, 2 + 2 * batch_count: 1},
         compiler_params=pltpu.CompilerParams(vmem_limit_bytes=16 * mebibyte),
         name="bank_rows",
-    )(bank_rows, *bank_downs, *bank_ups, down_zeros, up_zeros)
+    )(
+        bank_rows,
+        *bank_downs,
+        *bank_ups,
+        down_zeros,
+        up_zeros,
+    )
     return (attention[None], token_grad[None], down_grad, up_grad)
 
 

time: 232 us -> 204 us (0.88)
  starting transfers between devices: 72.7 us -> 53.1 us
  Pallas kernels: 22.1 us -> 40.2 us
  local copies, waits for them, and re-layouts: 45.1 us -> 28.6 us
  other arithmetic: 9.23 us -> 3.35 us
  waiting for transfers between devices: 79.8 us -> 75.5 us
    ppermute x35 -> x32, starting transfers between devices: 64.4 us -> 44.9 us  [shift(): lax.ppermute(value, axis, [(at, (at + steps) % count) for at in range(cou...]
    pallas_call x3 -> x5, Pallas kernels: 11.2 us -> 25.3 us  [the longest x1 15.3 us: shards(): pl.pallas_call(select_kernel, out_shape=[jax.ShapeDtypeStruct(shape, bf16...]
    gather x5 -> x0, local copies, waits for them, and re-layouts: 8.76 us -> none  [the longest x2 3.31 us: shards(): own_down, own_up = (down_bank[own_bank], adapter_up_weight[own_bank])]
    ppermute x4, waiting for transfers between devices: 29.3 us -> 21.5 us  [push(): return lax.ppermute(value, axis, pairs)]
    another operation x3 -> x0, local copies, waits for them, and re-layouts: 4.01 us -> none  [the longest x2 2.49 us: shards(): cosines = jnp.tile(jnp.cos(angles), (1, 2))]
    ppermute x35 -> x32, waiting for transfers between devices: 50.5 us -> 54 us  [shift(): lax.ppermute(value, axis, [(at, (at + steps) % count) for at in range(cou...]
    pallas_call x1, Pallas kernels: 5.15 us -> 8.03 us  [shards(): pl.pallas_call(functools.partial(project_kernel, places, down_places, len...]
    another operation x3 -> x1, other arithmetic: 2.71 us -> 0.09 us  [the longest x1 1.55 us: shards(): up_rows = jnp.stack(up_parts)[relative]]
  transfers between devices with their start and end apart: 39 -> 36, of which waited for: 13 -> 20; matrix products, arithmetic and copies ran while one was open for 13% -> 2% of each run, Pallas kernels for 3% -> 11%
where the time goes in v4:
time: 204 us; the launch traced here: 203 us
  waiting for transfers between devices  75.5 us (37%)
  starting transfers between devices  53.1 us (26%)
  Pallas kernels  40.2 us (20%)
  local copies, waits for them, and re-layouts  28.6 us (14%)
  other arithmetic  3.35 us (2%)
  between operations  2.37 us (1%)
    ppermute x32, waiting for transfers between devices, shift(): lax.ppermute(value, axis, [(at, (at + steps) % count) for at in range(cou...  54 us
    ppermute x32, starting transfers between devices, shift(): lax.ppermute(value, axis, [(at, (at + steps) % count) for at in range(cou...  44.9 us
    ppermute x4, waiting for transfers between devices, push(): return lax.ppermute(value, axis, pairs)  21.5 us
    unnamed x79, local copies, waits for them, and re-layouts  20.6 us
    pallas_call x1, Pallas kernels, shards(): pl.pallas_call(select_kernel, out_shape=[jax.ShapeDtypeStruct(shape, bf16...  15.3 us
    ppermute x4, starting transfers between devices, push(): return lax.ppermute(value, axis, pairs)  8.15 us
    pallas_call x1, Pallas kernels, shards(): pl.pallas_call(functools.partial(project_kernel, places, down_places, len...  8.03 us
    broadcast_in_dim x1, local copies, waits for them, and re-layouts, shards(): down_zeros = jnp.zeros((adapters, joint_rank, 1, held_down), f32)  4.53 us
  transfers between devices with their start and end apart: 36, of which 20 were waited for; matrix products, arithmetic and copies ran while one was open for 2% of the time, Pallas kernels for 11%

profile of v4, /device:TPU:0, one launch (start us, length us, event | category | flops | bytes accessed | tf_op | source)
XLA Modules:
  0.0 203.1 jit_solution(13178015552918902930)
XLA Ops:
  1.8 3.1 %collective-permute-start = (bf16[192,896]{1,0:T(8,128)(2,1)S(1)}, bf16[192,896]{1,0:T(8,128)(2,1)S(1)}, u32[]{:S(2)}, u32[]{:S(2)}) collective-permute-start(bf16[192,896]{1,0:T(8,128)(2,1)S(1)} %constant_dynamic-slice_fusion.1), channel_id=1, source_target_pairs={{0,4},{4,8},{8,12},{12,0},{1,5},{5,9},{9,13},{13,1},{2,6},{6,10},{... | collective-permute-start | bytes 1032200 | tf_op jit(solution)/shard_map/ppermute | solution.py:23
  7.0 8.9 %collective-permute-done.refs_1_ = bf16[192,896]{1,0:T(8,128)(2,1)S(1)} collective-permute-done((bf16[192,896]{1,0:T(8,128)(2,1)S(1)}, bf16[192,896]{1,0:T(8,128)(2,1)S(1)}, u32[]{:S(2)}, u32[]{:S(2)}) %collective-permute-start) | collective-permute-done | bytes 344096 | tf_op jit(solution)/shard_map/ppermute | solution.py:23
  15.8 6.3 %collective-permute-done.4.refs_5_ = bf16[192,896]{1,0:T(8,128)(2,1)} collective-permute-done((bf16[192,896]{1,0:T(8,128)(2,1)S(1)}, bf16[192,896]{1,0:T(8,128)(2,1)}, u32[]{:S(2)}, u32[]{:S(2)}) %collective-permute-start.4) | collective-permute-done | bytes 344096 | tf_op jit(solution)/shard_map/ppermute | solution.py:23
  25.4 15.3 %select.1 = (bf16[3,64,448]{2,1,0:T(8,128)(2,1)}, bf16[3,64,448]{2,1,0:T(8,128)(2,1)}, bf16[3,32,80]{2,1,0:T(8,128)(2,1)}, bf16[3,32,80]{2,1,0:T(8,128)(2,1)}) custom-call(s32[64]{0:T(128)} %bank_row.1, s32[2,3]{1,0:T(2,128)} %adapters.1, bf16[64,64,448]{2,1,0:T(8,128)(2,1)} %bitcast.20, bf16[64,32,80]{2,1,0:T(8,128)(2,1)} %up_bank.1), custom_call_target="tpu_custom_call" | custom-call | bytes 688128 | tf_op jit(solution)/shard_map/select/pallas_call | solution.py:546
  42.8 4.1 %collective-permute-done.13.far_up = bf16[3,32,80]{2,1,0:T(8,128)(2,1)S(1)} collective-permute-done((bf16[3,32,80]{2,1,0:T(8,128)(2,1)}, bf16[3,32,80]{2,1,0:T(8,128)(2,1)S(1)}, u32[]{:S(2)}, u32[]{:S(2)}) %collective-permute-start.13) | collective-permute-done | bytes 15392 | tf_op jit(solution)/shard_map/ppermute | solution.py:23
  68.8 4.2 %collective-permute-done.15.refs_15_ = bf16[144,896]{1,0:T(8,128)(2,1)} collective-permute-done((bf16[144,896]{1,0:T(8,128)(2,1)}, bf16[144,896]{1,0:T(8,128)(2,1)}, u32[]{:S(2)}, u32[]{:S(2)}) %collective-permute-start.15) | collective-permute-done | bytes 258080 | tf_op jit(solution)/shard_map/ppermute | solution.py:23
  73.0 2.5 %collective-permute-start.16 = (bf16[144,896]{1,0:T(8,128)(2,1)}, bf16[144,896]{1,0:T(8,128)(2,1)S(1)}, u32[]{:S(2)}, u32[]{:S(2)}) collective-permute-start(bf16[144,896]{1,0:T(8,128)(2,1)} %copy-done.28), channel_id=1, source_target_pairs={{0,12},{4,0},{8,4},{12,8},{1,13},{5,1},{9,5},{13,9},{2,14},{6,2},{... | collective-permute-start | bytes 774152 | tf_op jit(solution)/shard_map/ppermute | solution.py:23
  76.7 4.6 %collective-permute-done.16.refs_16_ = bf16[144,896]{1,0:T(8,128)(2,1)S(1)} collective-permute-done((bf16[144,896]{1,0:T(8,128)(2,1)}, bf16[144,896]{1,0:T(8,128)(2,1)S(1)}, u32[]{:S(2)}, u32[]{:S(2)}) %collective-permute-start.16) | collective-permute-done | bytes 258080 | tf_op jit(solution)/shard_map/ppermute | solution.py:23
  81.5 4.5 %broadcast_in_dim.41.refs_17_.refs_4_ = f32[64,64,1,448]{3,2,1,0:T(1,128)S(1)} broadcast(f32[]{:T(128)} %constant.12.clone.1), dimensions={} | broadcast | bytes 7340036 | tf_op jit(solution)/shard_map/broadcast_in_dim | solution.py:625
  86.1 8.0 %project.1 = (f32[256,896]{1,0:T(8,128)S(1)}, bf16[768,3584]{1,0:T(8,128)(2,1)S(1)}, bf16[128,3584]{1,0:T(8,128)(2,1)S(1)}, bf16[3,64,640]{2,1,0:T(8,128)(2,1)S(1)}) custom-call(s32[2,3]{1,0:T(2,128)S(1)} %copy-done.19, bf16[256,3584]{1,0:T(8,128)(2,1)S(1)} %bitcast.18, bf16[192,3584]{1,0:T(8,128)(2,1)S(1)} %copy-done.5, ...), custom_call_target="tpu_custom_call" | custom-call | flops 1644167168 | bytes 8257536 | tf_op jit(solution)/shard_map/project/pallas_call | solution.py:631
  98.7 2.7 %collective-permute-start.21 = (bf16[256,896]{1,0:T(8,128)(2,1)S(1)}, bf16[256,896]{1,0:T(8,128)(2,1)S(1)}, u32[]{:S(2)}, u32[]{:S(2)}) collective-permute-start(bf16[256,896]{1,0:T(8,128)(2,1)S(1)} %copy-done.25), channel_id=1, source_target_pairs={{0,12},{4,0},{8,4},{12,8},{1,13},{5,1},{9,5},{13,9},{2,14},{6,2},{... | collective-permute-start | bytes 1376264 | tf_op jit(solution)/shard_map/ppermute | solution.py:23
  102.4 2.9 %collective-permute-start.19 = (bf16[256,256]{1,0:T(8,128)(2,1)S(1)}, bf16[256,256]{1,0:T(8,128)(2,1)S(1)}, u32[]{:S(2)}, u32[]{:S(2)}) collective-permute-start(bf16[256,256]{1,0:T(8,128)(2,1)S(1)} %get-tuple-element.50.refs_0_), channel_id=1, source_target_pairs={{0,8},{4,12},{1,9},{5,13},{2,10},{6,14},{3,11},{7,15},{16,24},{20,... | collective-permute-start | bytes 393224 | tf_op jit(solution)/shard_map/ppermute | solution.py:29
  105.3 2.7 %collective-permute-start.18 = (bf16[256,256]{1,0:T(8,128)(2,1)S(1)}, bf16[256,256]{1,0:T(8,128)(2,1)S(1)}, u32[]{:S(2)}, u32[]{:S(2)}) collective-permute-start(bf16[256,256]{1,0:T(8,128)(2,1)S(1)} %get-tuple-element.50.refs_0_), channel_id=1, source_target_pairs={{0,4},{4,8},{8,12},{1,5},{5,9},{9,13},{2,6},{6,10},{10,14},{3,7},{... | collective-permute-start | bytes 393224 | tf_op jit(solution)/shard_map/ppermute | solution.py:29
  108.0 4.7 %collective-permute-done.20.refs_3_.refs_5_ = bf16[256,896]{1,0:T(8,128)(2,1)S(1)} collective-permute-done((bf16[256,896]{1,0:T(8,128)(2,1)S(1)}, bf16[256,896]{1,0:T(8,128)(2,1)S(1)}, u32[]{:S(2)}, u32[]{:S(2)}) %collective-permute-start.20) | collective-permute-done | bytes 458784 | tf_op jit(solution)/shard_map/ppermute | solution.py:23
  112.7 8.4 %collective-permute-done.21.refs_4_.refs_7_ = bf16[256,896]{1,0:T(8,128)(2,1)S(1)} collective-permute-done((bf16[256,896]{1,0:T(8,128)(2,1)S(1)}, bf16[256,896]{1,0:T(8,128)(2,1)S(1)}, u32[]{:S(2)}, u32[]{:S(2)}) %collective-permute-start.21) | collective-permute-done | bytes 458784 | tf_op jit(solution)/shard_map/ppermute | solution.py:23
  124.6 3.4 %attention.1 = (bf16[128,512]{1,0:T(8,128)(2,1)}, bf16[128,512]{1,0:T(8,128)(2,1)S(1)}, f32[3,128,256]{2,1,0:T(8,128)S(1)}, f32[3,128,256]{2,1,0:T(8,128)S(1)}) custom-call(s32[2,3]{1,0:T(2,128)S(1)} %copy-done.19, bf16[512,128]{1,0:T(8,128)(2,1)S(1)} %get-tuple-element.49.queries, bf16[128,512]{1,0:T(8,128)(2,1)S(1)} %bitcast.19, ...), custom_call_target="tpu_custom_call" | custom-call | flops 503316480 | bytes 786432 | tf_op jit(solution)/shard_map/attention/pallas_call | solution.py:677
  133.8 7.7 %collective-permute-start.30 = (bf16[256,896]{1,0:T(8,128)(2,1)}, bf16[256,896]{1,0:T(8,128)(2,1)}, u32[]{:S(2)}, u32[]{:S(2)}) collective-permute-start(bf16[256,896]{1,0:T(8,128)(2,1)} %copy-done.23), channel_id=1, source_target_pairs={{0,8},{4,12},{8,0},{12,4},{1,9},{5,13},{9,1},{13,5},{2,10},{6,14},... | collective-permute-start | bytes 1376264 | tf_op jit(solution)/shard_map/ppermute | solution.py:23
  141.6 18.0 %collective-permute-done.25 = f32[128,256]{1,0:T(8,128)} collective-permute-done((f32[128,256]{1,0:T(8,128)S(1)}, f32[128,256]{1,0:T(8,128)}, u32[]{:S(2)}, u32[]{:S(2)}) %collective-permute-start.25) | collective-permute-done | bytes 131104 | tf_op jit(solution)/shard_map/ppermute | solution.py:29
  170.5 2.7 %collective-permute-start.33 = (f32[96,160]{1,0:T(8,128)}, f32[96,160]{1,0:T(8,128)S(1)}, u32[]{:S(2)}, u32[]{:S(2)}) collective-permute-start(f32[96,160]{1,0:T(8,128)} %copy-done.31), channel_id=1, source_target_pairs={{0,12},{4,0},{8,4},{12,8},{1,13},{5,1},{9,5},{13,9},{2,14},{6,2},{... | collective-permute-start | bytes 184328 | tf_op jit(solution)/shard_map/ppermute | solution.py:23
  174.1 5.0 %collective-permute-done.28.refs_2_ = bf16[256,64]{1,0:T(8,128)(2,1)S(1)} collective-permute-done((bf16[256,64]{1,0:T(8,128)(2,1)S(1)}, bf16[256,64]{1,0:T(8,128)(2,1)S(1)}, u32[]{:S(2)}, u32[]{:S(2)}) %collective-permute-start.28) | collective-permute-done | bytes 32800 | tf_op jit(solution)/shard_map/ppermute | solution.py:23
  185.7 3.0 %down_terms.1 = (f32[192,448]{1,0:T(8,128)S(1)}, f32[192,448]{1,0:T(8,128)}, f32[96,80]{1,0:T(8,128)S(1)}, f32[96,80]{1,0:T(8,128)S(1)}) custom-call(s32[2,3]{1,0:T(2,128)S(1)} %copy-done.20, bf16[256,64]{1,0:T(8,128)(2,1)S(1)} %get-tuple-element.59.rank_grad.refs_0_, bf16[256,64]{1,0:T(8,128)(2,1)S(1)} %copy-done.18, bf16[256,64]{1,0:T(8,128)(2,1)S(1)} %copy-done.16, ...), custom_call_target="tpu_custom_call" | custom-call | flops 352321536 | bytes 1835008 | tf_op jit(solution)/shard_map/down_terms/pallas_call | solution.py:753
  192.3 2.6 %copy-done.4 = bf16[768,3584]{1,0:T(8,128)(2,1)S(1)} copy-done((bf16[768,3584]{1,0:T(8,128)(2,1)S(1)}, bf16[768,3584]{1,0:T(8,128)(2,1)}, u32[]{:S(2)}) %copy-start.4) | copy-done | bytes 5505048
  195.5 4.3 %token_gradient.1 = bf16[256,3584]{1,0:T(8,128)(2,1)} custom-call(s32[2,3]{1,0:T(2,128)S(1)} %copy-done.21, bf16[256,768]{1,0:T(8,128)(2,1)S(1)} %get-tuple-element.58.gradients, bf16[256,64]{1,0:T(8,128)(2,1)S(1)} %get-tuple-element.59.rank_grad.refs_0_, bf16[768,3584]{1,0:T(8,128)(2,1)S(1)} %copy-done.4, bf16[128,3584]{1,0:T(8,128)(2,1)S(1)} %copy-done.7), custom_call_target="tpu_custom_call" | custom-call | flops 1644167168 | bytes 8257536 | tf_op jit(solution)/shard_map/token_gradient/pallas_call | solution.py:737
  200.2 2.9 %bank_rows.1 = (f32[64,64,1,448]{3,2,1,0:T(1,128)}, f32[64,32,80]{2,1,0:T(8,128)}) custom-call(s32[6]{0:T(128)S(1)} %reshape.32.bank_rows, f32[192,448]{1,0:T(8,128)S(1)} %get-tuple-element.68.refs_0_, f32[192,448]{1,0:T(8,128)S(1)} %collective-permute-done.34.refs_1_, ...), custom_call_target="tpu_custom_call", output_to_operand_aliasing={{0}: (5, {}), {1}: (6, {})} | custom-call | tf_op jit(solution)/shard_map/bank_rows/pallas_call | solution.py:786
  (157 shorter events, 68.3 us)
Async XLA Ops:
  1.8 14.0 %collective-permute-start = (bf16[192,896]{1,0:T(8,128)(2,1)S(1)}, bf16[192,896]{1,0:T(8,128)(2,1)S(1)}, u32[]{:S(2)}, u32[]{:S(2)}) collective-permute-start(bf16[192,896]{1,0:T(8,128)(2,1)S(1)} %constant_dynamic-slice_fusion.1), channel_id=1, source_target_pairs={{0,4},{4,8},{8,12},{12,0},{1,5},{5,9},{9,13},{13,1},{2,6},{6,10},{... | collective-permute-start | bytes 1032200 | tf_op jit(solution)/shard_map/ppermute | solution.py:23
  4.9 17.2 %collective-permute-start.4 = (bf16[192,896]{1,0:T(8,128)(2,1)S(1)}, bf16[192,896]{1,0:T(8,128)(2,1)}, u32[]{:S(2)}, u32[]{:S(2)}) collective-permute-start(bf16[192,896]{1,0:T(8,128)(2,1)S(1)} %constant_dynamic-slice_fusion.1), channel_id=1, source_target_pairs={{0,12},{4,0},{8,4},{12,8},{1,13},{5,1},{9,5},{13,9},{2,14},{6,2},{... | collective-permute-start | bytes 1032200 | tf_op jit(solution)/shard_map/ppermute | solution.py:23
  15.8 31.9 %collective-permute-start.8 = (bf16[192,896]{1,0:T(8,128)(2,1)S(1)}, bf16[192,896]{1,0:T(8,128)(2,1)S(1)}, u32[]{:S(2)}, u32[]{:S(2)}) collective-permute-start(bf16[192,896]{1,0:T(8,128)(2,1)S(1)} %collective-permute-done.refs_1_), channel_id=1, source_target_pairs={{0,4},{4,8},{8,12},{12,0},{1,5},{5,9},{9,13},{13,1},{2,6},{6,10},{... | collective-permute-start | bytes 1032200 | tf_op jit(solution)/shard_map/ppermute | solution.py:23
  22.1 32.3 %collective-permute-start.6 = (bf16[192,896]{1,0:T(8,128)(2,1)}, bf16[192,896]{1,0:T(8,128)(2,1)}, u32[]{:S(2)}, u32[]{:S(2)}) collective-permute-start(bf16[192,896]{1,0:T(8,128)(2,1)} %collective-permute-done.4.refs_5_), channel_id=1, source_target_pairs={{0,16},{16,0},{1,17},{17,1},{2,18},{18,2},{3,19},{19,3},{4,20},{20... | collective-permute-start | bytes 1032200 | tf_op jit(solution)/shard_map/ppermute | solution.py:23
  23.9 33.9 %collective-permute-start.5 = (bf16[192,896]{1,0:T(8,128)(2,1)}, bf16[192,896]{1,0:T(8,128)(2,1)}, u32[]{:S(2)}, u32[]{:S(2)}) collective-permute-start(bf16[192,896]{1,0:T(8,128)(2,1)} %collective-permute-done.4.refs_5_), channel_id=1, source_target_pairs={{0,2},{2,0},{1,3},{3,1},{4,6},{6,4},{5,7},{7,5},{8,10},{10,8},{9,1... | collective-permute-start | bytes 1032200 | tf_op jit(solution)/shard_map/ppermute | solution.py:23
  46.9 13.0 %collective-permute-start.2 = (bf16[192,896]{1,0:T(8,128)(2,1)S(1)}, bf16[192,896]{1,0:T(8,128)(2,1)}, u32[]{:S(2)}, u32[]{:S(2)}) collective-permute-start(bf16[192,896]{1,0:T(8,128)(2,1)S(1)} %collective-permute-done.refs_1_), channel_id=1, source_target_pairs={{0,16},{16,0},{1,17},{17,1},{2,18},{18,2},{3,19},{19,3},{4,20},{20... | collective-permute-start | bytes 1032200 | tf_op jit(solution)/shard_map/ppermute | solution.py:23
  47.4 14.5 %collective-permute-start.1 = (bf16[192,896]{1,0:T(8,128)(2,1)S(1)}, bf16[192,896]{1,0:T(8,128)(2,1)}, u32[]{:S(2)}, u32[]{:S(2)}) collective-permute-start(bf16[192,896]{1,0:T(8,128)(2,1)S(1)} %collective-permute-done.refs_1_), channel_id=1, source_target_pairs={{0,2},{2,0},{1,3},{3,1},{4,6},{6,4},{5,7},{7,5},{8,10},{10,8},{9,1... | collective-permute-start | bytes 1032200 | tf_op jit(solution)/shard_map/ppermute | solution.py:23
  47.7 19.2 %collective-permute-start.9 = (bf16[192,896]{1,0:T(8,128)(2,1)S(1)}, bf16[192,896]{1,0:T(8,128)(2,1)}, u32[]{:S(2)}, u32[]{:S(2)}) collective-permute-start(bf16[192,896]{1,0:T(8,128)(2,1)S(1)} %collective-permute-done.8.refs_0_.refs_9_), channel_id=1, source_target_pairs={{0,2},{2,0},{1,3},{3,1},{4,6},{6,4},{5,7},{7,5},{8,10},{10,8},{9,1... | collective-permute-start | bytes 1032200 | tf_op jit(solution)/shard_map/ppermute | solution.py:23
  57.8 15.2 %collective-permute-start.15 = (bf16[144,896]{1,0:T(8,128)(2,1)}, bf16[144,896]{1,0:T(8,128)(2,1)}, u32[]{:S(2)}, u32[]{:S(2)}) collective-permute-start(bf16[144,896]{1,0:T(8,128)(2,1)} %copy-done.29), channel_id=1, source_target_pairs={{0,8},{4,12},{8,0},{12,4},{1,9},{5,13},{9,1},{13,5},{2,10},{6,14},... | collective-permute-start | bytes 774152 | tf_op jit(solution)/shard_map/ppermute | solution.py:23
  59.9 21.4 %collective-permute-start.10 = (bf16[192,896]{1,0:T(8,128)(2,1)S(1)}, bf16[192,896]{1,0:T(8,128)(2,1)}, u32[]{:S(2)}, u32[]{:S(2)}) collective-permute-start(bf16[192,896]{1,0:T(8,128)(2,1)S(1)} %collective-permute-done.8.refs_0_.refs_9_), channel_id=1, source_target_pairs={{0,16},{16,0},{1,17},{17,1},{2,18},{18,2},{3,19},{19,3},{4,20},{20... | collective-permute-start | bytes 1032200 | tf_op jit(solution)/shard_map/ppermute | solution.py:23
  61.9 19.4 %collective-permute-start.7 = (bf16[192,896]{1,0:T(8,128)(2,1)}, bf16[192,896]{1,0:T(8,128)(2,1)}, u32[]{:S(2)}, u32[]{:S(2)}) collective-permute-start(bf16[192,896]{1,0:T(8,128)(2,1)} %collective-permute-done.6.refs_7_), channel_id=1, source_target_pairs={{0,2},{2,0},{1,3},{3,1},{4,6},{6,4},{5,7},{7,5},{8,10},{10,8},{9,1... | collective-permute-start | bytes 1032200 | tf_op jit(solution)/shard_map/ppermute | solution.py:23
  65.4 16.0 %collective-permute-start.3 = (bf16[192,896]{1,0:T(8,128)(2,1)}, bf16[192,896]{1,0:T(8,128)(2,1)}, u32[]{:S(2)}, u32[]{:S(2)}) collective-permute-start(bf16[192,896]{1,0:T(8,128)(2,1)} %collective-permute-done.1.refs_2_), channel_id=1, source_target_pairs={{0,16},{16,0},{1,17},{17,1},{2,18},{18,2},{3,19},{19,3},{4,20},{20... | collective-permute-start | bytes 1032200 | tf_op jit(solution)/shard_map/ppermute | solution.py:23
  66.9 14.4 %collective-permute-start.11 = (bf16[192,896]{1,0:T(8,128)(2,1)}, bf16[192,896]{1,0:T(8,128)(2,1)}, u32[]{:S(2)}, u32[]{:S(2)}) collective-permute-start(bf16[192,896]{1,0:T(8,128)(2,1)} %collective-permute-done.9.refs_10_), channel_id=1, source_target_pairs={{0,16},{16,0},{1,17},{17,1},{2,18},{18,2},{3,19},{19,3},{4,20},{20... | collective-permute-start | bytes 1032200 | tf_op jit(solution)/shard_map/ppermute | solution.py:23
  97.5 15.2 %collective-permute-start.20 = (bf16[256,896]{1,0:T(8,128)(2,1)S(1)}, bf16[256,896]{1,0:T(8,128)(2,1)S(1)}, u32[]{:S(2)}, u32[]{:S(2)}) collective-permute-start(bf16[256,896]{1,0:T(8,128)(2,1)S(1)} %copy-done.27), channel_id=1, source_target_pairs={{0,4},{4,8},{8,12},{12,0},{1,5},{5,9},{9,13},{13,1},{2,6},{6,10},{... | collective-permute-start | bytes 1376264 | tf_op jit(solution)/shard_map/ppermute | solution.py:23
  98.7 22.4 %collective-permute-start.21 = (bf16[256,896]{1,0:T(8,128)(2,1)S(1)}, bf16[256,896]{1,0:T(8,128)(2,1)S(1)}, u32[]{:S(2)}, u32[]{:S(2)}) collective-permute-start(bf16[256,896]{1,0:T(8,128)(2,1)S(1)} %copy-done.25), channel_id=1, source_target_pairs={{0,12},{4,0},{8,4},{12,8},{1,13},{5,1},{9,5},{13,9},{2,14},{6,2},{... | collective-permute-start | bytes 1376264 | tf_op jit(solution)/shard_map/ppermute | solution.py:23
  102.4 19.8 %collective-permute-start.19 = (bf16[256,256]{1,0:T(8,128)(2,1)S(1)}, bf16[256,256]{1,0:T(8,128)(2,1)S(1)}, u32[]{:S(2)}, u32[]{:S(2)}) collective-permute-start(bf16[256,256]{1,0:T(8,128)(2,1)S(1)} %get-tuple-element.50.refs_0_), channel_id=1, source_target_pairs={{0,8},{4,12},{1,9},{5,13},{2,10},{6,14},{3,11},{7,15},{16,24},{20,... | collective-permute-start | bytes 393224 | tf_op jit(solution)/shard_map/ppermute | solution.py:29
  105.3 19.3 %collective-permute-start.18 = (bf16[256,256]{1,0:T(8,128)(2,1)S(1)}, bf16[256,256]{1,0:T(8,128)(2,1)S(1)}, u32[]{:S(2)}, u32[]{:S(2)}) collective-permute-start(bf16[256,256]{1,0:T(8,128)(2,1)S(1)} %get-tuple-element.50.refs_0_), channel_id=1, source_target_pairs={{0,4},{4,8},{8,12},{1,5},{5,9},{9,13},{2,6},{6,10},{10,14},{3,7},{... | collective-permute-start | bytes 393224 | tf_op jit(solution)/shard_map/ppermute | solution.py:29
  132.5 27.1 %collective-permute-start.25 = (f32[128,256]{1,0:T(8,128)S(1)}, f32[128,256]{1,0:T(8,128)}, u32[]{:S(2)}, u32[]{:S(2)}) collective-permute-start(f32[128,256]{1,0:T(8,128)S(1)} %get-tuple-element.75), channel_id=1, source_target_pairs={{8,0},{12,4},{9,1},{13,5},{10,2},{14,6},{11,3},{15,7},{24,16},{28,... | collective-permute-start | bytes 393224 | tf_op jit(solution)/shard_map/ppermute | solution.py:29
  133.8 35.6 %collective-permute-start.30 = (bf16[256,896]{1,0:T(8,128)(2,1)}, bf16[256,896]{1,0:T(8,128)(2,1)}, u32[]{:S(2)}, u32[]{:S(2)}) collective-permute-start(bf16[256,896]{1,0:T(8,128)(2,1)} %copy-done.23), channel_id=1, source_target_pairs={{0,8},{4,12},{8,0},{12,4},{1,9},{5,13},{9,1},{13,5},{2,10},{6,14},... | collective-permute-start | bytes 1376264 | tf_op jit(solution)/shard_map/ppermute | solution.py:23
  141.5 19.3 %collective-permute-start.22 = (bf16[128,512]{1,0:T(8,128)(2,1)S(1)}, bf16[128,512]{1,0:T(8,128)(2,1)S(1)}, u32[]{:S(2)}, u32[]{:S(2)}) collective-permute-start(bf16[128,512]{1,0:T(8,128)(2,1)S(1)} %get-tuple-element.54.own_query), channel_id=1, source_target_pairs={{0,1},{1,0},{2,3},{3,2},{4,5},{5,4},{6,7},{7,6},{8,9},{9,8},{10,11... | collective-permute-start | bytes 393224 | tf_op jit(solution)/shard_map/ppermute | solution.py:23
  165.3 13.8 %collective-permute-start.28 = (bf16[256,64]{1,0:T(8,128)(2,1)S(1)}, bf16[256,64]{1,0:T(8,128)(2,1)S(1)}, u32[]{:S(2)}, u32[]{:S(2)}) collective-permute-start(bf16[256,64]{1,0:T(8,128)(2,1)S(1)} %get-tuple-element.59.rank_grad.refs_0_), channel_id=1, source_target_pairs={{0,8},{4,12},{8,0},{12,4},{1,9},{5,13},{9,1},{13,5},{2,10},{6,14},... | collective-permute-start | bytes 98312 | tf_op jit(solution)/shard_map/ppermute | solution.py:23
  165.3 14.4 %collective-permute-start.27 = (bf16[256,64]{1,0:T(8,128)(2,1)S(1)}, bf16[256,64]{1,0:T(8,128)(2,1)S(1)}, u32[]{:S(2)}, u32[]{:S(2)}) collective-permute-start(bf16[256,64]{1,0:T(8,128)(2,1)S(1)} %get-tuple-element.59.rank_grad.refs_0_), channel_id=1, source_target_pairs={{0,4},{4,8},{8,12},{12,0},{1,5},{5,9},{9,13},{13,1},{2,6},{6,10},{... | collective-permute-start | bytes 98312 | tf_op jit(solution)/shard_map/ppermute | solution.py:23
  167.4 12.9 %collective-permute-start.31 = (f32[96,160]{1,0:T(8,128)}, f32[96,160]{1,0:T(8,128)S(1)}, u32[]{:S(2)}, u32[]{:S(2)}) collective-permute-start(f32[96,160]{1,0:T(8,128)} %copy-done.33), channel_id=1, source_target_pairs={{0,4},{4,8},{8,12},{12,0},{1,5},{5,9},{9,13},{13,1},{2,6},{6,10},{... | collective-permute-start | bytes 184328 | tf_op jit(solution)/shard_map/ppermute | solution.py:23
  169.4 11.8 %collective-permute-start.32 = (f32[96,160]{1,0:T(8,128)}, f32[96,160]{1,0:T(8,128)S(1)}, u32[]{:S(2)}, u32[]{:S(2)}) collective-permute-start(f32[96,160]{1,0:T(8,128)} %copy-done.32), channel_id=1, source_target_pairs={{0,8},{4,12},{8,0},{12,4},{1,9},{5,13},{9,1},{13,5},{2,10},{6,14},... | collective-permute-start | bytes 184328 | tf_op jit(solution)/shard_map/ppermute | solution.py:23
  (51 other events, 545.3 us)

commit v5 on v4

--- a/solution.py
+++ b/solution.py
@@ -80,6 +80,10 @@
 
 def in_smem():
     return pl.BlockSpec(memory_space=pltpu.SMEM)
+
+
+def by_block(shape):
+    return pl.BlockSpec(shape, lambda: (0,) * len(shape))
 
 
 def in_place():
@@ -112,30 +116,35 @@
     return place
 
 
-def down_place(seq_count, width, behind):
+def down_place(seq_count, features, width, behind):
     def place():
-        return 0, ring_index(lax.axis_index("seq") - behind, seq_count) * width
+        return features, ring_index(lax.axis_index("seq") - behind, seq_count) * width
 
     return place
 
 
-def whole_place():
-    return 0, 0
-
-
-def second_document(ends, rows, seq_count):
-    seq_index = lax.axis_index("seq")
-    first = (seq_index >= seq_count // 2).astype(jnp.int32)
-    return row_segments(ends, row_positions(seq_index * rows, rows)) != first
-
-
-def select_kernel(bank_row, adapters, down_bank, up_bank, *refs):
-    outputs, semaphore = refs[:4], refs[4]
+def whole_place(row):
+    def place():
+        return row, 0
+
+    return place
+
+
+def select_kernel(bank_row, adapters, frozen, down_bank, up_bank, *refs):
+    share, outputs, rows, semaphore = refs[0], refs[1:5], refs[5], refs[6]
     batch = lax.axis_index("batch")
-    copies = []
+    width = share.shape[1]
+    place = (lax.axis_index("groups") * 2 + batch) * width
+    copies = [
+        pltpu.make_async_copy(
+            frozen.at[:, pl.ds(pl.multiple_of(place, 128), width)], share, semaphore.at[0]
+        )
+    ]
+    copies[0].start()
     for which, sample in enumerate((batch, 1 - batch)):
         for document in range(SEGS):
             row = bank_row[adapters[sample, document]]
+            rows[which * SEGS + document] = row
             for source, target in ((down_bank, outputs[which]), (up_bank, outputs[2 + which])):
                 copy = pltpu.make_async_copy(
                     source.at[row], target.at[document], semaphore.at[len(copies)]
@@ -203,59 +212,64 @@
                     ]
 
 
-def project_kernel(frozen_places, down_places, unused, seq_count, lengths, tokens, *refs):
+def project_kernel(frozen_places, down_places, unused, seq_count, tokens, *refs):
     frozen_count, down_count = len(frozen_places), len(down_places)
     frozen_pieces = refs[:frozen_count]
     down_pieces = refs[frozen_count : frozen_count + down_count]
     refs = refs[frozen_count + down_count + unused :]
     packed = down_count > 1
-    part, frozen, down = refs[:3]
-    semaphore = refs[-1]
+    part, matrix = refs[:2]
+    weights, semaphore = refs[-2:]
+    features = part.shape[1] - 2 * ADAPTER_RANK * 2
     copies = []
     for piece, place in zip(frozen_pieces, frozen_places):
-        copies.append(fetch(piece, frozen, place, semaphore.at[len(copies)]))
-    joint_rank = down.shape[0] // 2
+        copies.append(fetch(piece, weights, place, semaphore.at[len(copies)]))
+    joint_rank = 2 * ADAPTER_RANK
     for number, (piece, place) in enumerate(zip(down_pieces, down_places)):
         rows = piece.at[pl.ds(0, 2 * joint_rank)] if packed else piece
-        copies.append(fetch(rows, down, place, semaphore.at[len(copies)]))
+        copies.append(fetch(rows, weights, place, semaphore.at[len(copies)]))
         if packed:
             extra = piece.shape[0] - 2 * joint_rank
             copy = pltpu.make_async_copy(
                 piece.at[pl.ds(2 * joint_rank, extra)],
-                refs[4].at[number],
+                refs[3].at[number],
                 semaphore.at[len(copies)],
             )
             copy.start()
             copies.append(copy)
     for copy in copies:
         copy.wait()
-    rows = tokens.shape[0]
-    features = frozen.shape[0]
-    second = second_document(kernel_marks(lengths), rows, seq_count)
-    values = tokens[...]
-    part[:, :features] = dot_nt(values, frozen[...])
-    first_low = dot_nt(values, down[:joint_rank])
-    second_low = dot_nt(values, down[joint_rank:])
-    part[:, features : features + joint_rank] = jnp.where(second, second_low, first_low)
+    keep = pltpu.make_async_copy(weights, matrix, semaphore.at[len(copies)])
+    keep.start()
+    part[...] = dot_nt(tokens[...], weights[...])
     if packed:
-        assemble_up(seq_count, refs[4], refs[3])
+        assemble_up(seq_count, refs[3], refs[2])
+    keep.wait()
 
 
 def rotated(values, cosines, sines):
     return values * cosines + pltpu.roll(values, values.shape[1] // 2, 1) * sines
 
 
-def qkv_kernel(lengths, mine, theirs, up_blocks, cosines, sines, queries, pairs, low_rank):
+def qkv_kernel(seq_count, lengths, mine, theirs, up_blocks, cosines, sines, queries, pairs, low_rank):
     rows = mine.shape[0]
     own_rows = queries.shape[0] // QHEADS
     query_columns = QHEADS * HEAD_WIDTH
     value_start = query_columns + HEAD_WIDTH
     features = value_start + HEAD_WIDTH
-    low_columns = slice(features, features + low_rank.shape[1])
+    joint_rank = low_rank.shape[1]
+    middle = features + joint_rank
     ends = kernel_marks(lengths)
+
+    def low_rows(picked, second):
+        first_low = mine[picked, features:middle] + theirs[picked, features:middle]
+        second_low = mine[picked, middle:] + theirs[picked, middle:]
+        return jnp.where(second, second_low, first_low).astype(jnp.bfloat16)
+
+    first = (lax.axis_index("seq") >= seq_count // 2).astype(jnp.int32)
     first_row = lax.axis_index("seq") * rows
     segments = row_segments(ends, row_positions(first_row, rows))
-    low = (mine[:, low_columns] + theirs[:, low_columns]).astype(jnp.bfloat16)
+    low = low_rows(slice(None), segments != first)
     low_rank[...] = low
     value_delta = jnp.zeros((rows, HEAD_WIDTH), jnp.float32)
     for document in range(SEGS):
@@ -268,7 +282,7 @@
     start = pl.multiple_of(lax.axis_index("tp") * own_rows, own_rows)
     own = pl.ds(start, own_rows)
     own_segments = row_segments(ends, row_positions(first_row + start, own_rows))
-    own_low = (mine[own, low_columns] + theirs[own, low_columns]).astype(jnp.bfloat16)
+    own_low = low_rows(own, own_segments != first)
     query_delta = jnp.zeros((own_rows, query_columns), jnp.float32)
     for document in range(SEGS):
         chosen = jnp.where(own_segments == document, own_low, jnp.zeros_like(own_low))
@@ -284,7 +298,19 @@
 
 def attention_kernel(block_count, unused, lengths, queries, incoming, cosines, sines, *refs):
     blocks = refs[:block_count]
-    output, query_grad, kept, sent, low_probs = refs[block_count + unused :]
+    output, query_grad, kept, sent, down_zeros, up_zeros = refs[block_count + unused : -4]
+    low_probs, down_blank, up_blank, semaphore = refs[-4:]
+    down_blank[...] = jnp.zeros_like(down_blank)
+    up_blank[...] = jnp.zeros_like(up_blank)
+    copies = []
+    for blank, zeros in ((down_blank, down_zeros), (up_blank, up_zeros)):
+        step = blank.shape[0]
+        for start in range(0, zeros.shape[0], step):
+            copy = pltpu.make_async_copy(
+                blank, zeros.at[pl.ds(start, step)], semaphore.at[len(copies)]
+            )
+            copy.start()
+            copies.append(copy)
     own_rows, query_columns = incoming.shape
     rows = blocks[0].shape[0]
     score_scale = HEAD_WIDTH ** (-0.5)
@@ -340,12 +366,28 @@
         query_grad[:, columns] = rotated(
             total[picked] * score_scale, cosines[own], -sines[own]
         ).astype(jnp.bfloat16)
+    for copy in copies:
+        copy.wait()
+
+
+def sum_kernel(kept, arrived, *sums):
+    for back, total in enumerate(sums):
+        total[...] = kept[back] + arrived[back]
+
+
+def pair_kernel(terms, cosines, sines, *refs):
+    parts, pair = refs[:terms], refs[-2]
+    own_rows = pair.shape[0]
+    total = sum(part[...] for part in parts)
+    own = pl.ds(pl.multiple_of(lax.axis_index("tp") * own_rows, own_rows), own_rows)
+    keys = rotated(total[:, :HEAD_WIDTH], cosines[own], -sines[own])
+    pair[:, :HEAD_WIDTH] = keys.astype(jnp.bfloat16)
+    pair[:, HEAD_WIDTH:] = total[:, HEAD_WIDTH:].astype(jnp.bfloat16)
 
 
 def rank_kernel(
-    unused, seq_count, lengths, own_query, other_query, own_pair, other_pair, low_rank, up_blocks, *refs
+    seq_count, lengths, own_query, other_query, own_pair, other_pair, low_rank, up_blocks, *refs
 ):
-    refs = refs[unused:]
     gradients, rank_grad = refs[:2]
     split_terms, (terms, blocks) = refs[2:-2], refs[-2:]
     own_rows, query_columns = own_query.shape
@@ -355,10 +397,12 @@
     other = pl.multiple_of(own_rows - start, own_rows)
     gradients[pl.ds(start, own_rows), :query_columns] = own_query[...]
     gradients[pl.ds(other, own_rows), :query_columns] = other_query[...]
-    gradients[pl.ds(start, own_rows), query_columns:] = own_pair[...]
-    gradients[pl.ds(other, own_rows), query_columns:] = other_pair[...]
+    value_start = query_columns + HEAD_WIDTH
+    features = value_start + HEAD_WIDTH
+    gradients[pl.ds(start, own_rows), query_columns:features] = own_pair[...]
+    gradients[pl.ds(other, own_rows), query_columns:features] = other_pair[...]
     query_grad = gradients[:, :query_columns]
-    value_grad = gradients[:, query_columns + HEAD_WIDTH :]
+    value_grad = gradients[:, value_start:features]
     low = low_rank[...]
     rank = low.shape[1] // 2
     segments = row_segments(kernel_marks(lengths), row_positions(seq_index * rows, rows))
@@ -374,7 +418,13 @@
         place = slice(document * rank, (document + 1) * rank)
         terms[place, :query_columns] = adapter_scale * query_terms[:rank]
         terms[place, query_columns:] = adapter_scale * value_terms[rank:]
-    rank_grad[...] = (adapter_scale * total).astype(jnp.bfloat16)
+    turned = (adapter_scale * total).astype(jnp.bfloat16)
+    rank_grad[...] = turned
+    second = segments != (seq_index >= seq_count // 2).astype(jnp.int32)
+    nothing = jnp.zeros_like(turned)
+    middle = features + low.shape[1]
+    gradients[:, features:middle] = jnp.where(second, nothing, turned)
+    gradients[:, middle:] = jnp.where(second, turned, nothing)
     held = blocks.shape[2]
     for holder in range(seq_count):
         blocks[holder] = terms[:, holder * held : (holder + 1) * held]
@@ -382,21 +432,8 @@
         block[...] = blocks[ring_index(seq_index + steps - seq_count, seq_count)]
 
 
-def token_kernel(seq_count, lengths, gradients, rank_grad, frozen, down, token_grad):
-    rows = gradients.shape[0]
-    joint_rank = down.shape[0] // 2
-    second = second_document(kernel_marks(lengths), rows, seq_count)
-    low = rank_grad[...]
-    nothing = jnp.zeros_like(low)
-    first_low = jnp.where(second, nothing, low)
-    second_low = jnp.where(second, low, nothing)
-    chunk = 512
-    for column in range(0, token_grad.shape[1], chunk):
-        columns = slice(column, column + chunk)
-        total = dot_nn(gradients[...], frozen[:, columns])
-        total += dot_nn(first_low, down[:joint_rank, columns])
-        total += dot_nn(second_low, down[joint_rank:, columns])
-        token_grad[:, columns] = total.astype(jnp.bfloat16)
+def token_kernel(gradients, matrix, token_grad):
+    token_grad[...] = dot_nn(gradients[...], matrix[...]).astype(jnp.bfloat16)
 
 
 def split_halves(terms, own, far):
@@ -490,6 +527,7 @@
     second_end = first_end + lengths[1]
     half_count = seq_count // 2
 
+    down_bank = adapter_down_weight[:, :, 0, :]
     plane_count = group_count * batch_count
     share = width // plane_count
     pieces, places = [], []
@@ -505,9 +543,18 @@
         and 4 * 2 * held_up <= down_width
     )
     if direct:
-        own_share = lax.dynamic_slice_in_dim(
-            frozen_qkv_matrix, (group_index * batch_count + batch_index) * share, share, axis=1
-        )
+        row_shapes = [(frozen_rows, share)]
+        row_shapes += [(SEGS, joint_rank, held_down)] * 2 + [(SEGS, low_width, held_up)] * 2
+        own_share, own_down, far_down, own_up, far_up, bank_rows = pl.pallas_call(
+            select_kernel,
+            out_shape=[jax.ShapeDtypeStruct(shape, bf16) for shape in row_shapes]
+            + [jax.ShapeDtypeStruct((2 * SEGS,), jnp.int32)],
+            in_specs=[in_smem()] * 2 + [in_place()] * 3,
+            out_specs=[in_place()] * 5 + [in_smem()],
+            scratch_shapes=[pltpu.SemaphoreType.DMA((1 + 4 * SEGS,))],
+            cost_estimate=cost(0, 4 * SEGS * joint_rank * held_down * 2),
+            name="select",
+        )(adapter_bank_row, document_adapter, frozen_qkv_matrix, down_bank, adapter_up_weight)
         pieces.append(frozen_qkv_matrix)
         places.append(frozen_place(seq_count, frozen_rows, None, 0, 0, 0))
         before = shift(own_share, "seq", 1)
@@ -537,21 +584,10 @@
                 )
     else:
         pieces.append(lax.all_gather(frozen_qkv_matrix, "seq", axis=0, tiled=True))
-        places.append(whole_place)
-
-    down_bank = adapter_down_weight[:, :, 0, :]
+        places.append(whole_place(0))
+
     column_blocks, up_blocks = None, None
     if direct:
-        row_shapes = [(SEGS, joint_rank, held_down)] * 2 + [(SEGS, low_width, held_up)] * 2
-        own_down, far_down, own_up, far_up = pl.pallas_call(
-            select_kernel,
-            out_shape=[jax.ShapeDtypeStruct(shape, bf16) for shape in row_shapes],
-            in_specs=[in_smem()] * 2 + [in_place()] * 2,
-            out_specs=[in_place()] * 4,
-            scratch_shapes=[pltpu.SemaphoreType.DMA((4 * SEGS,))],
-            cost_estimate=cost(0, 4 * SEGS * joint_rank * held_down * 2),
-            name="select",
-        )(adapter_bank_row, document_adapter, down_bank, adapter_up_weight)
         far_down = shift(far_down, "batch", 1)
         far_up = shift(far_up, "batch", 1)
         payload_rows = 2 * joint_rank + low_width // 2
@@ -560,12 +596,13 @@
             out_shape=[jax.ShapeDtypeStruct((payload_rows, down_width), bf16)] * seq_count
             + [jax.ShapeDtypeStruct((rows, down_width), bf16)] * seq_count,
             in_specs=[in_vmem()] * 5 + [in_place()],
-            out_specs=[in_vmem()] * (2 * seq_count),
+            out_specs=[by_block((payload_rows, down_width))] * seq_count
+            + [by_block((rows, down_width))] * seq_count,
             scratch_shapes=[
                 pltpu.VMEM((SEGS * joint_rank, down_width), bf16),
                 pltpu.VMEM((SEGS, low_width, 2 * held_up), bf16),
             ],
-            compiler_params=pltpu.CompilerParams(vmem_limit_bytes=8 * mebibyte),
+            compiler_params=pltpu.CompilerParams(vmem_limit_bytes=16 * mebibyte),
             cost_estimate=cost(0, 4 * rows * width),
             name="pack",
         )(own_down, far_down, own_up, far_up, local_tokens, before)
@@ -574,7 +611,7 @@
             shift(part, "seq", steps) if steps else part
             for steps, part in enumerate(packed[:seq_count])
         ]
-        down_places = [down_place(seq_count, down_width, steps) for steps in range(seq_count)]
+        down_places = [down_place(seq_count, features, down_width, steps) for steps in range(seq_count)]
     else:
         sample_rows = lookup_rows(adapter_bank_row, document_adapter)
         got_down = lax.all_to_all(
@@ -590,7 +627,7 @@
         first = (seq_index >= half_count).astype(jnp.int32)
         merged = jnp.transpose(all_down, (1, 0, 2)).reshape(SEGS * joint_rank, -1)
         down_parts = [lax.dynamic_slice_in_dim(merged, first * joint_rank, 2 * joint_rank)]
-        down_places = [whole_place]
+        down_places = [whole_place(features)]
         up_rows = jnp.transpose(all_up, (1, 0, 2)).reshape(SEGS, low_width, -1)
         is_query = jnp.arange(up_rows.shape[2]) < query_columns
         up_blocks = jnp.concatenate(
@@ -621,43 +658,38 @@
     cosines = jnp.cos(angles)
     sines = jnp.sin(angles) * signs[None, :]
 
-    sample_rows = lookup_rows(adapter_bank_row, document_adapter)
-    down_zeros = jnp.zeros((adapters, joint_rank, 1, held_down), f32)
-    up_zeros = jnp.zeros((adapters, low_width, held_up), f32)
-    early = [down_zeros, up_zeros, cosines, sines]
-    up_shape = jax.ShapeDtypeStruct((SEGS, joint_rank, query_columns + HEAD_WIDTH), bf16)
-    arrived = [pltpu.VMEM((seq_count, low_width // 2, down_width), bf16)] if direct else []
-    weight_bytes = 2 * width * (features + 2 * joint_rank)
-    part, frozen, down, *built = pl.pallas_call(
-        functools.partial(project_kernel, places, down_places, len(early), seq_count),
-        out_shape=[
-            jax.ShapeDtypeStruct((rows, features + 128), f32),
-            jax.ShapeDtypeStruct((features, width), bf16),
-            jax.ShapeDtypeStruct((2 * joint_rank, width), bf16),
-        ]
-        + ([up_shape] if direct else []),
-        in_specs=[in_smem(), in_vmem()]
-        + [in_place()] * (len(pieces) + len(down_parts) + len(early)),
-        out_specs=[in_vmem()] * (4 if direct else 3),
-        scratch_shapes=arrived
-        + [pltpu.SemaphoreType.DMA((len(pieces) + 2 * len(down_parts),))],
-        compiler_params=pltpu.CompilerParams(vmem_limit_bytes=12 * mebibyte),
-        cost_estimate=cost(
-            2 * rows * width * (features + 2 * joint_rank), weight_bytes + 2 * rows * width
-        ),
-        name="project",
-    )(document_lengths, local_tokens, *pieces, *down_parts, *early)
-    if direct:
-        up_blocks = built[0]
-
     column_parts = [
         shift(block, "seq", steps) if steps else block
         for steps, block in enumerate(column_blocks)
     ]
+    early = [cosines, sines] + ([column_parts[2]] if seq_count > 3 else [])
+    up_shape = (SEGS, joint_rank, query_columns + HEAD_WIDTH)
+    matrix_rows = features + 2 * joint_rank
+    arrived = [pltpu.VMEM((seq_count, low_width // 2, down_width), bf16)] if direct else []
+    part, matrix, *built = pl.pallas_call(
+        functools.partial(project_kernel, places, down_places, len(early), seq_count),
+        out_shape=[
+            jax.ShapeDtypeStruct((rows, matrix_rows), f32),
+            jax.ShapeDtypeStruct((matrix_rows, width), bf16),
+        ]
+        + ([jax.ShapeDtypeStruct(up_shape, bf16)] if direct else []),
+        in_specs=[in_vmem()] + [in_place()] * (len(pieces) + len(down_parts) + len(early)),
+        out_specs=[in_vmem(), in_place()] + ([by_block(up_shape)] if direct else []),
+        scratch_shapes=arrived
+        + [
+            pltpu.VMEM((matrix_rows, width), bf16),
+            pltpu.SemaphoreType.DMA((len(pieces) + 2 * len(down_parts) + 1,)),
+        ],
+        compiler_params=pltpu.CompilerParams(vmem_limit_bytes=20 * mebibyte),
+        cost_estimate=cost(2 * rows * width * matrix_rows, 2 * width * (matrix_rows + rows)),
+        name="project",
+    )(local_tokens, *pieces, *down_parts, *early)
+    if direct:
+        up_blocks = built[0]
 
     other_part = shift(part, "tp", 1)
     queries, pairs, low_rank = pl.pallas_call(
-        qkv_kernel,
+        functools.partial(qkv_kernel, seq_count),
         out_shape=(
             jax.ShapeDtypeStruct((QHEADS * own_rows, HEAD_WIDTH), bf16),
             jax.ShapeDtypeStruct((rows, 2 * HEAD_WIDTH), bf16),
@@ -673,21 +705,29 @@
     blocks = [pairs] + [push(pairs, "seq", back) for back in range(1, half_count + 1)]
     block_count = len(blocks)
     incoming = output_gradient[0]
-    early_columns = [column_parts[1], column_parts[-1]]
-    attention, query_grad, kept, sent = pl.pallas_call(
+    early_columns = [column_parts[1]]
+    blank_rows = 4
+    bank_shapes = [(adapters, joint_rank, 1, held_down), (adapters, low_width, held_up)]
+    attention, query_grad, kept, sent, down_zeros, up_zeros = pl.pallas_call(
         functools.partial(attention_kernel, block_count, len(early_columns)),
         out_shape=(
             jax.ShapeDtypeStruct((own_rows, query_columns), bf16),
             jax.ShapeDtypeStruct((own_rows, query_columns), bf16),
             jax.ShapeDtypeStruct((block_count, own_rows, 2 * HEAD_WIDTH), f32),
             jax.ShapeDtypeStruct((block_count, own_rows, 2 * HEAD_WIDTH), f32),
-        ),
+        )
+        + tuple(jax.ShapeDtypeStruct(shape, f32) for shape in bank_shapes),
         in_specs=[in_smem()]
         + [in_vmem()] * (4 + block_count)
         + [in_place()] * len(early_columns),
-        out_specs=(in_vmem(),) * 4,
-        scratch_shapes=[pltpu.VMEM((block_count, QHEADS * own_rows, rows), bf16)],
-        compiler_params=pltpu.CompilerParams(vmem_limit_bytes=(4 + 4 * block_count) * mebibyte),
+        out_specs=(in_vmem(),) * 4 + (in_place(),) * 2,
+        scratch_shapes=[
+            pltpu.VMEM((block_count, QHEADS * own_rows, rows), bf16),
+            pltpu.VMEM((blank_rows,) + bank_shapes[0][1:], f32),
+            pltpu.VMEM((blank_rows,) + bank_shapes[1][1:], f32),
+            pltpu.SemaphoreType.DMA((2 * adapters // blank_rows,)),
+        ],
+        compiler_params=pltpu.CompilerParams(vmem_limit_bytes=(8 + 4 * block_count) * mebibyte),
         cost_estimate=cost(
             10 * block_count * QHEADS * own_rows * rows * HEAD_WIDTH,
             4 * rows * features,
@@ -697,27 +737,43 @@
     )(document_lengths, queries, incoming, cosines, sines, *blocks, *early_columns)
 
     other_query = shift(query_grad, "tp", 1)
-    pair_sums = kept + shift(sent, "tp", 1)
-    own_sum = pair_sums[0]
-    for back in range(1, block_count):
-        own_sum = own_sum + push(pair_sums[back], "seq", -back)
-    own_place = tp_index * own_rows
-    own_cosines = lax.dynamic_slice_in_dim(cosines, own_place, own_rows)
-    own_sines = lax.dynamic_slice_in_dim(sines, own_place, own_rows)
-    key_grad = own_sum[:, :HEAD_WIDTH]
-    key_grad = key_grad * own_cosines - jnp.roll(key_grad, HEAD_WIDTH // 2, axis=1) * own_sines
-    pair_grad = jnp.concatenate([key_grad, own_sum[:, HEAD_WIDTH:]], axis=1).astype(bf16)
+    pair_sums = pl.pallas_call(
+        sum_kernel,
+        out_shape=[jax.ShapeDtypeStruct((own_rows, 2 * HEAD_WIDTH), f32)] * block_count,
+        in_specs=[in_vmem()] * 2,
+        out_specs=[in_vmem()] * block_count,
+        compiler_params=pltpu.CompilerParams(vmem_limit_bytes=8 * mebibyte),
+        cost_estimate=cost(0, 12 * block_count * own_rows * 2 * HEAD_WIDTH),
+        name="pair_sums",
+    )(kept, shift(sent, "tp", 1))
+    pair_terms = [pair_sums[0]]
+    pair_terms += [push(pair_sums[back], "seq", -back) for back in range(1, block_count)]
+    pair_grad, late_block = pl.pallas_call(
+        functools.partial(pair_kernel, block_count),
+        out_shape=[
+            jax.ShapeDtypeStruct((own_rows, 2 * HEAD_WIDTH), bf16),
+            jax.ShapeDtypeStruct((rows, down_width), bf16),
+        ],
+        in_specs=[in_vmem()] * (2 + block_count) + [in_place()],
+        out_specs=[in_vmem(), in_place()],
+        input_output_aliases={2 + block_count: 1},
+        compiler_params=pltpu.CompilerParams(vmem_limit_bytes=8 * mebibyte),
+        cost_estimate=cost(0, 12 * block_count * own_rows * 2 * HEAD_WIDTH),
+        name="pair_gradients",
+    )(cosines, sines, *pair_terms, column_blocks[-1])
+    column_parts[-1] = shift(late_block, "seq", seq_count - 1)
     other_pair = shift(pair_grad, "tp", 1)
 
     gradients, rank_grad, *up_split = pl.pallas_call(
-        functools.partial(rank_kernel, 0, seq_count),
+        functools.partial(rank_kernel, seq_count),
         out_shape=[
-            jax.ShapeDtypeStruct((rows, features), bf16),
+            jax.ShapeDtypeStruct((rows, matrix_rows), bf16),
             jax.ShapeDtypeStruct((rows, joint_rank), bf16),
         ]
         + [jax.ShapeDtypeStruct((SEGS * low_width, held_up * batch_count), f32)] * seq_count,
         in_specs=[in_smem()] + [in_vmem()] * 6,
-        out_specs=[in_vmem()] * (2 + seq_count),
+        out_specs=[by_block((rows, matrix_rows)), in_vmem()]
+        + [by_block((SEGS * low_width, held_up * batch_count))] * seq_count,
         scratch_shapes=[
             pltpu.VMEM((SEGS * low_width, features - HEAD_WIDTH), f32),
             pltpu.VMEM((seq_count, SEGS * low_width, held_up * batch_count), f32),
@@ -734,19 +790,22 @@
         shift(block, "seq", steps) if steps else block for steps, block in enumerate(up_split)
     ]
 
+    chunk = 512
     token_grad = pl.pallas_call(
-        functools.partial(token_kernel, seq_count),
+        token_kernel,
+        grid=(width // chunk,),
         out_shape=jax.ShapeDtypeStruct((rows, width), bf16),
-        in_specs=[in_smem()] + [in_vmem()] * 4,
-        out_specs=in_vmem(),
-        compiler_params=pltpu.CompilerParams(vmem_limit_bytes=8 * mebibyte),
-        cost_estimate=cost(
-            2 * rows * width * (features + 2 * joint_rank), weight_bytes + 2 * rows * width
-        ),
+        in_specs=[
+            pl.BlockSpec((rows, matrix_rows), lambda step: (0, 0)),
+            pl.BlockSpec((matrix_rows, chunk), lambda step: (0, step)),
+        ],
+        out_specs=pl.BlockSpec((rows, chunk), lambda step: (0, step)),
+        compiler_params=pltpu.CompilerParams(vmem_limit_bytes=12 * mebibyte),
+        cost_estimate=cost(2 * rows * width * matrix_rows, 2 * width * (matrix_rows + rows)),
         name="token_gradient",
-    )(document_lengths, gradients, rank_grad, frozen, down)
-
-    if batch_count == 2:
+    )(gradients, matrix)
+
+    if direct:
         term_shapes = [(SEGS * joint_rank, held_down)] * 2 + [(SEGS * low_width, held_up)] * 2
     else:
         term_shapes = [(SEGS * joint_rank, down_width), (SEGS * low_width, held_up * batch_count)]
@@ -762,10 +821,9 @@
         name="down_terms",
     )(document_lengths, *rank_parts, *column_parts, *up_sums)
 
-    if batch_count == 2:
+    if direct:
         bank_downs = [terms[0], shift(terms[1], "batch", 1)]
         bank_ups = [terms[2], shift(terms[3], "batch", 1)]
-        sample_rows = jnp.where(batch_index == 0, sample_rows, sample_rows[::-1])
     else:
         down_send = jnp.transpose(
             terms[0].reshape(SEGS * joint_rank, batch_count, held_down), (1, 0, 2)
@@ -778,7 +836,8 @@
         bank_downs = [back_down[batch] for batch in range(batch_count)]
         bank_ups = [back_up[batch] for batch in range(batch_count)]
 
-    bank_rows = sample_rows.reshape(-1)
+    if not direct:
+        bank_rows = sample_rows.reshape(-1)
 
     def whole(array):
         return pl.BlockSpec(array.shape, lambda step, bank: (0,) * array.ndim)

time: 204 us -> 222 us (1.088)
  waiting for transfers between devices: 75.5 us -> 99 us
  local copies, waits for them, and re-layouts: 28.6 us -> 14.9 us
  Pallas kernels: 40.2 us -> 52.6 us
  starting transfers between devices: 53.1 us -> 50.7 us
    ppermute x32, waiting for transfers between devices: 54 us -> 78.4 us  [shift(): lax.ppermute(value, axis, [(at, (at + steps) % count) for at in range(cou...]
    pallas_call x1, Pallas kernels: 15.3 us -> 26.4 us  [shards(): pl.pallas_call(select_kernel, out_shape=[jax.ShapeDtypeStruct(shape, bf16...]
    unnamed x79 -> x50, local copies, waits for them, and re-layouts: 20.6 us -> 13.6 us
    broadcast_in_dim x2 -> x0, local copies, waits for them, and re-layouts: 4.64 us -> none  [the longest x1 4.53 us: shards(): down_zeros = jnp.zeros((adapters, joint_rank, 1, held_down), f32)]
    pallas_call x1, Pallas kernels: 3.41 us -> 7.49 us  [shards(): pl.pallas_call(functools.partial(attention_kernel, block_count, len(early...]
    ppermute x32, starting transfers between devices: 44.9 us -> 41.1 us  [shift(): lax.ppermute(value, axis, [(at, (at + steps) % count) for at in range(cou...]
    pallas_call x1, Pallas kernels: 8.03 us -> 5.17 us  [shards(): pl.pallas_call(functools.partial(project_kernel, places, down_places, len...]
    pallas_call x3 -> x5, Pallas kernels: 6.51 us -> 7.29 us  [the longest x1 4.82 us: shards(): pl.pallas_call(token_kernel, grid=(width // chunk,), out_shape=jax.ShapeD...]
  transfers between devices with their start and end apart: 36 -> 36, of which waited for: 20 -> 20; matrix products, arithmetic and copies ran while one was open for 2% -> 2% of each run, Pallas kernels for 11% -> 4%
where the time goes in v5:
time: 222 us
  waiting for transfers between devices  99 us (45%)
  Pallas kernels  52.6 us (24%)
  starting transfers between devices  50.7 us (23%)
  local copies, waits for them, and re-layouts  14.9 us (7%)
  other arithmetic  2.44 us (1%)
    ppermute x32, waiting for transfers between devices, shift(): lax.ppermute(value, axis, [(at, (at + steps) % count) for at in range(cou...  78.4 us
    ppermute x32, starting transfers between devices, shift(): lax.ppermute(value, axis, [(at, (at + steps) % count) for at in range(cou...  41.1 us
    pallas_call x1, Pallas kernels, shards(): pl.pallas_call(select_kernel, out_shape=[jax.ShapeDtypeStruct(shape, bf16...  26.4 us
    ppermute x4, waiting for transfers between devices, push(): return lax.ppermute(value, axis, pairs)  20.6 us
    unnamed x50, local copies, waits for them, and re-layouts  13.6 us
    ppermute x4, starting transfers between devices, push(): return lax.ppermute(value, axis, pairs)  9.63 us
    pallas_call x1, Pallas kernels, shards(): pl.pallas_call(functools.partial(attention_kernel, block_count, len(early...  7.49 us
    pallas_call x1, Pallas kernels, shards(): pl.pallas_call(functools.partial(project_kernel, places, down_places, len...  5.17 us
  transfers between devices with their start and end apart: 36, of which 20 were waited for; matrix products, arithmetic and copies ran while one was open for 2% of the time, Pallas kernels for 4%

profile of v5, /device:TPU:0, one launch (start us, length us, event | category | flops | bytes accessed | tf_op | source)
XLA Modules:
  0.0 221.8 jit_solution(16405537423114397666)
XLA Ops:
  0.7 26.4 %select.1 = (bf16[192,896]{1,0:T(8,128)(2,1)}, bf16[3,64,448]{2,1,0:T(8,128)(2,1)}, bf16[3,64,448]{2,1,0:T(8,128)(2,1)}, bf16[3,32,80]{2,1,0:T(8,128)(2,1)}, bf16[3,32,80]{2,1,0:T(8,128)(2,1)}, /*index=5*/s32[6]{0:T(128)}) custom-call(s32[64]{0:T(128)} %bank_row.1, s32[2,3]{1,0:T(2,128)} %adapters.1, bf16[192,3584]{1,0:T(8,128)(2,1)} %refs_0_.1, ...), custom_call_target="tpu_custom_call" | custom-call | bytes 688128 | tf_op jit(solution)/shard_map/select/pallas_call | solution.py:548
  27.1 3.1 %collective-permute-start = (bf16[192,896]{1,0:T(8,128)(2,1)}, bf16[192,896]{1,0:T(8,128)(2,1)}, u32[]{:S(2)}, u32[]{:S(2)}) collective-permute-start(bf16[192,896]{1,0:T(8,128)(2,1)} %get-tuple-element.47), channel_id=1, source_target_pairs={{0,4},{4,8},{8,12},{12,0},{1,5},{5,9},{9,13},{13,1},{2,6},{6,10},{... | collective-permute-start | bytes 1032200 | tf_op jit(solution)/shard_map/ppermute | solution.py:23
  32.2 9.2 %collective-permute-done.refs_1_ = bf16[192,896]{1,0:T(8,128)(2,1)} collective-permute-done((bf16[192,896]{1,0:T(8,128)(2,1)}, bf16[192,896]{1,0:T(8,128)(2,1)}, u32[]{:S(2)}, u32[]{:S(2)}) %collective-permute-start) | collective-permute-done | bytes 344096 | tf_op jit(solution)/shard_map/ppermute | solution.py:23
  41.4 6.1 %collective-permute-done.4.refs_5_ = bf16[192,896]{1,0:T(8,128)(2,1)} collective-permute-done((bf16[192,896]{1,0:T(8,128)(2,1)}, bf16[192,896]{1,0:T(8,128)(2,1)}, u32[]{:S(2)}, u32[]{:S(2)}) %collective-permute-start.4) | collective-permute-done | bytes 344096 | tf_op jit(solution)/shard_map/ppermute | solution.py:23
  51.6 7.1 %collective-permute-done.13.far_up = bf16[3,32,80]{2,1,0:T(8,128)(2,1)S(1)} collective-permute-done((bf16[3,32,80]{2,1,0:T(8,128)(2,1)}, bf16[3,32,80]{2,1,0:T(8,128)(2,1)S(1)}, u32[]{:S(2)}, u32[]{:S(2)}) %collective-permute-start.13) | collective-permute-done | bytes 15392 | tf_op jit(solution)/shard_map/ppermute | solution.py:23
  60.8 4.4 %collective-permute-done.12.far_down = bf16[3,64,448]{2,1,0:T(8,128)(2,1)S(1)} collective-permute-done((bf16[3,64,448]{2,1,0:T(8,128)(2,1)}, bf16[3,64,448]{2,1,0:T(8,128)(2,1)S(1)}, u32[]{:S(2)}, u32[]{:S(2)}) %collective-permute-start.12) | collective-permute-done | bytes 172064 | tf_op jit(solution)/shard_map/ppermute | solution.py:23
  75.3 2.7 %collective-permute-start.14 = (bf16[144,896]{1,0:T(8,128)(2,1)S(1)}, bf16[144,896]{1,0:T(8,128)(2,1)S(1)}, u32[]{:S(2)}, u32[]{:S(2)}) collective-permute-start(bf16[144,896]{1,0:T(8,128)(2,1)S(1)} %get-tuple-element.53), channel_id=1, source_target_pairs={{0,4},{4,8},{8,12},{12,0},{1,5},{5,9},{9,13},{13,1},{2,6},{6,10},{... | collective-permute-start | bytes 774152 | tf_op jit(solution)/shard_map/ppermute | solution.py:23
  82.5 3.8 %collective-permute-done.14.refs_14_ = bf16[144,896]{1,0:T(8,128)(2,1)S(1)} collective-permute-done((bf16[144,896]{1,0:T(8,128)(2,1)S(1)}, bf16[144,896]{1,0:T(8,128)(2,1)S(1)}, u32[]{:S(2)}, u32[]{:S(2)}) %collective-permute-start.14) | collective-permute-done | bytes 258080 | tf_op jit(solution)/shard_map/ppermute | solution.py:23
  87.5 15.2 %collective-permute-done.15.refs_15_ = bf16[144,896]{1,0:T(8,128)(2,1)S(1)} collective-permute-done((bf16[144,896]{1,0:T(8,128)(2,1)S(1)}, bf16[144,896]{1,0:T(8,128)(2,1)S(1)}, u32[]{:S(2)}, u32[]{:S(2)}) %collective-permute-start.15) | collective-permute-done | bytes 258080 | tf_op jit(solution)/shard_map/ppermute | solution.py:23
  113.9 4.3 %collective-permute-done.17.refs_19_.refs_6_ = bf16[256,896]{1,0:T(8,128)(2,1)} collective-permute-done((bf16[256,896]{1,0:T(8,128)(2,1)}, bf16[256,896]{1,0:T(8,128)(2,1)}, u32[]{:S(2)}, u32[]{:S(2)}) %collective-permute-start.17) | collective-permute-done | bytes 458784 | tf_op jit(solution)/shard_map/ppermute | solution.py:23
  122.0 5.2 %project.1 = (f32[256,896]{1,0:T(8,128)S(1)}, bf16[896,3584]{1,0:T(8,128)(2,1)S(1)}, bf16[3,64,640]{2,1,0:T(8,128)(2,1)S(1)}) custom-call(bf16[256,3584]{1,0:T(8,128)(2,1)S(1)} %bitcast.8, bf16[192,3584]{1,0:T(8,128)(2,1)S(1)} %copy-done.1, bf16[192,896]{1,0:T(8,128)(2,1)} %collective-permute-done.refs_1_, bf16[192,896]{1,0:T(8,128)(2,1)} %collective-permute-done.1.refs_2_, ...), custom_call_target="tpu_custom_call" | custom-call | flops 1644167168 | bytes 8257536 | tf_op jit(solution)/shard_map/project/pallas_call | solution.py:669
  127.3 10.3 %collective-permute-start.21 = (bf16[256,896]{1,0:T(8,128)(2,1)S(1)}, bf16[256,896]{1,0:T(8,128)(2,1)S(1)}, u32[]{:S(2)}, u32[]{:S(2)}) collective-permute-start(bf16[256,896]{1,0:T(8,128)(2,1)S(1)} %copy-done.23), channel_id=1, source_target_pairs={{0,4},{4,8},{8,12},{12,0},{1,5},{5,9},{9,13},{13,1},{2,6},{6,10},{... | collective-permute-start | bytes 1376264 | tf_op jit(solution)/shard_map/ppermute | solution.py:23
  138.6 5.7 %collective-permute-start.20 = (bf16[256,256]{1,0:T(8,128)(2,1)S(1)}, bf16[256,256]{1,0:T(8,128)(2,1)S(1)}, u32[]{:S(2)}, u32[]{:S(2)}) collective-permute-start(bf16[256,256]{1,0:T(8,128)(2,1)S(1)} %get-tuple-element.60.refs_0_), channel_id=1, source_target_pairs={{0,8},{4,12},{1,9},{5,13},{2,10},{6,14},{3,11},{7,15},{16,24},{20,... | collective-permute-start | bytes 393224 | tf_op jit(solution)/shard_map/ppermute | solution.py:29
  145.7 2.7 %collective-permute-done.21.refs_3_.refs_5_ = bf16[256,896]{1,0:T(8,128)(2,1)S(1)} collective-permute-done((bf16[256,896]{1,0:T(8,128)(2,1)S(1)}, bf16[256,896]{1,0:T(8,128)(2,1)S(1)}, u32[]{:S(2)}, u32[]{:S(2)}) %collective-permute-start.21) | collective-permute-done | bytes 458784 | tf_op jit(solution)/shard_map/ppermute | solution.py:23
  148.4 2.9 %collective-permute-done.20.refs_2_ = bf16[256,256]{1,0:T(8,128)(2,1)S(1)} collective-permute-done((bf16[256,256]{1,0:T(8,128)(2,1)S(1)}, bf16[256,256]{1,0:T(8,128)(2,1)S(1)}, u32[]{:S(2)}, u32[]{:S(2)}) %collective-permute-start.20) | collective-permute-done | bytes 131104 | tf_op jit(solution)/shard_map/ppermute | solution.py:29
  153.6 7.5 %attention.1 = (bf16[128,512]{1,0:T(8,128)(2,1)}, bf16[128,512]{1,0:T(8,128)(2,1)S(1)}, f32[3,128,256]{2,1,0:T(8,128)S(1)}, f32[3,128,256]{2,1,0:T(8,128)S(1)}, ...) custom-call(s32[2,3]{1,0:T(2,128)S(1)} %copy-done.20, bf16[512,128]{1,0:T(8,128)(2,1)S(1)} %get-tuple-element.59.queries, ...), custom_call_target="tpu_custom_call" | custom-call | flops 503316480 | bytes 786432 | tf_op jit(solution)/shard_map/attention/pallas_call | solution.py:711
  165.5 7.9 %collective-permute-done.24.refs_1_ = f32[128,256]{1,0:T(8,128)S(1)} collective-permute-done((f32[128,256]{1,0:T(8,128)S(1)}, f32[128,256]{1,0:T(8,128)S(1)}, u32[]{:S(2)}, u32[]{:S(2)}) %collective-permute-start.24) | collective-permute-done | bytes 131104 | tf_op jit(solution)/shard_map/ppermute | solution.py:29
  173.4 7.5 %collective-permute-done.25.refs_2_ = f32[128,256]{1,0:T(8,128)S(1)} collective-permute-done((f32[128,256]{1,0:T(8,128)S(1)}, f32[128,256]{1,0:T(8,128)S(1)}, u32[]{:S(2)}, u32[]{:S(2)}) %collective-permute-start.25) | collective-permute-done | bytes 131104 | tf_op jit(solution)/shard_map/ppermute | solution.py:29
  184.8 2.5 %collective-permute-start.28 = (bf16[256,64]{1,0:T(8,128)(2,1)S(1)}, bf16[256,64]{1,0:T(8,128)(2,1)S(1)}, u32[]{:S(2)}, u32[]{:S(2)}) collective-permute-start(bf16[256,64]{1,0:T(8,128)(2,1)S(1)} %get-tuple-element.75.refs_0_), channel_id=1, source_target_pairs={{0,8},{4,12},{8,0},{12,4},{1,9},{5,13},{9,1},{13,5},{2,10},{6,14},... | collective-permute-start | bytes 98312 | tf_op jit(solution)/shard_map/ppermute | solution.py:23
  188.9 8.7 %collective-permute-done.29.refs_3_ = bf16[256,64]{1,0:T(8,128)(2,1)S(1)} collective-permute-done((bf16[256,64]{1,0:T(8,128)(2,1)S(1)}, bf16[256,64]{1,0:T(8,128)(2,1)S(1)}, u32[]{:S(2)}, u32[]{:S(2)}) %collective-permute-start.29) | collective-permute-done | bytes 32800 | tf_op jit(solution)/shard_map/ppermute | solution.py:23
  197.8 4.3 %collective-permute-done.28.refs_2_ = bf16[256,64]{1,0:T(8,128)(2,1)S(1)} collective-permute-done((bf16[256,64]{1,0:T(8,128)(2,1)S(1)}, bf16[256,64]{1,0:T(8,128)(2,1)S(1)}, u32[]{:S(2)}, u32[]{:S(2)}) %collective-permute-start.28) | collective-permute-done | bytes 32800 | tf_op jit(solution)/shard_map/ppermute | solution.py:23
  202.1 6.1 %collective-permute-done.27.refs_1_ = bf16[256,64]{1,0:T(8,128)(2,1)S(1)} collective-permute-done((bf16[256,64]{1,0:T(8,128)(2,1)S(1)}, bf16[256,64]{1,0:T(8,128)(2,1)S(1)}, u32[]{:S(2)}, u32[]{:S(2)}) %collective-permute-start.27) | collective-permute-done | bytes 32800 | tf_op jit(solution)/shard_map/ppermute | solution.py:23
  212.6 4.8 %token_gradient.1 = bf16[256,3584]{1,0:T(8,128)(2,1)} custom-call(bf16[256,896]{1,0:T(8,128)(2,1)S(1)} %get-tuple-element.72.gradients, bf16[896,3584]{1,0:T(8,128)(2,1)S(1)} %get-tuple-element.73.matrix), custom_call_target="tpu_custom_call" | custom-call | flops 1644167168 | bytes 8257536 | tf_op jit(solution)/shard_map/token_gradient/pallas_call | solution.py:794
  218.9 2.9 %bank_rows.1 = (f32[64,64,1,448]{3,2,1,0:T(1,128)}, f32[64,32,80]{2,1,0:T(8,128)}) custom-call(s32[6]{0:T(128)S(1)} %copy-done.21, f32[192,448]{1,0:T(8,128)S(1)} %get-tuple-element.82.refs_0_, f32[192,448]{1,0:T(8,128)S(1)} %collective-permute-done.34.refs_1_, ...), custom_call_target="tpu_custom_call", output_to_operand_aliasing={{0}: (5, {}), {1}: (6, {})} | custom-call | tf_op jit(solution)/shard_map/bank_rows/pallas_call | solution.py:845
  (115 shorter events, 58.5 us)
Async XLA Ops:
  27.1 14.4 %collective-permute-start = (bf16[192,896]{1,0:T(8,128)(2,1)}, bf16[192,896]{1,0:T(8,128)(2,1)}, u32[]{:S(2)}, u32[]{:S(2)}) collective-permute-start(bf16[192,896]{1,0:T(8,128)(2,1)} %get-tuple-element.47), channel_id=1, source_target_pairs={{0,4},{4,8},{8,12},{12,0},{1,5},{5,9},{9,13},{13,1},{2,6},{6,10},{... | collective-permute-start | bytes 1032200 | tf_op jit(solution)/shard_map/ppermute | solution.py:23
  30.1 17.4 %collective-permute-start.4 = (bf16[192,896]{1,0:T(8,128)(2,1)}, bf16[192,896]{1,0:T(8,128)(2,1)}, u32[]{:S(2)}, u32[]{:S(2)}) collective-permute-start(bf16[192,896]{1,0:T(8,128)(2,1)} %get-tuple-element.47), channel_id=1, source_target_pairs={{0,12},{4,0},{8,4},{12,8},{1,13},{5,1},{9,5},{13,9},{2,14},{6,2},{... | collective-permute-start | bytes 1032200 | tf_op jit(solution)/shard_map/ppermute | solution.py:23
  41.4 25.9 %collective-permute-start.8 = (bf16[192,896]{1,0:T(8,128)(2,1)}, bf16[192,896]{1,0:T(8,128)(2,1)S(1)}, u32[]{:S(2)}, u32[]{:S(2)}) collective-permute-start(bf16[192,896]{1,0:T(8,128)(2,1)} %collective-permute-done.refs_1_), channel_id=1, source_target_pairs={{0,4},{4,8},{8,12},{12,0},{1,5},{5,9},{9,13},{13,1},{2,6},{6,10},{... | collective-permute-start | bytes 1032200 | tf_op jit(solution)/shard_map/ppermute | solution.py:23
  47.6 27.8 %collective-permute-start.6 = (bf16[192,896]{1,0:T(8,128)(2,1)}, bf16[192,896]{1,0:T(8,128)(2,1)}, u32[]{:S(2)}, u32[]{:S(2)}) collective-permute-start(bf16[192,896]{1,0:T(8,128)(2,1)} %collective-permute-done.4.refs_5_), channel_id=1, source_target_pairs={{0,16},{16,0},{1,17},{17,1},{2,18},{18,2},{3,19},{19,3},{4,20},{20... | collective-permute-start | bytes 1032200 | tf_op jit(solution)/shard_map/ppermute | solution.py:23
  49.3 28.7 %collective-permute-start.5 = (bf16[192,896]{1,0:T(8,128)(2,1)}, bf16[192,896]{1,0:T(8,128)(2,1)}, u32[]{:S(2)}, u32[]{:S(2)}) collective-permute-start(bf16[192,896]{1,0:T(8,128)(2,1)} %collective-permute-done.4.refs_5_), channel_id=1, source_target_pairs={{0,2},{2,0},{1,3},{3,1},{4,6},{6,4},{5,7},{7,5},{8,10},{10,8},{9,1... | collective-permute-start | bytes 1032200 | tf_op jit(solution)/shard_map/ppermute | solution.py:23
  50.8 27.3 %collective-permute-start.2 = (bf16[192,896]{1,0:T(8,128)(2,1)}, bf16[192,896]{1,0:T(8,128)(2,1)}, u32[]{:S(2)}, u32[]{:S(2)}) collective-permute-start(bf16[192,896]{1,0:T(8,128)(2,1)} %collective-permute-done.refs_1_), channel_id=1, source_target_pairs={{0,16},{16,0},{1,17},{17,1},{2,18},{18,2},{3,19},{19,3},{4,20},{20... | collective-permute-start | bytes 1032200 | tf_op jit(solution)/shard_map/ppermute | solution.py:23
  65.8 15.9 %collective-permute-start.1 = (bf16[192,896]{1,0:T(8,128)(2,1)}, bf16[192,896]{1,0:T(8,128)(2,1)}, u32[]{:S(2)}, u32[]{:S(2)}) collective-permute-start(bf16[192,896]{1,0:T(8,128)(2,1)} %collective-permute-done.refs_1_), channel_id=1, source_target_pairs={{0,2},{2,0},{1,3},{3,1},{4,6},{6,4},{5,7},{7,5},{8,10},{10,8},{9,1... | collective-permute-start | bytes 1032200 | tf_op jit(solution)/shard_map/ppermute | solution.py:23
  67.3 38.9 %collective-permute-start.9 = (bf16[192,896]{1,0:T(8,128)(2,1)S(1)}, bf16[192,896]{1,0:T(8,128)(2,1)}, u32[]{:S(2)}, u32[]{:S(2)}) collective-permute-start(bf16[192,896]{1,0:T(8,128)(2,1)S(1)} %collective-permute-done.8.refs_0_.refs_9_), channel_id=1, source_target_pairs={{0,2},{2,0},{1,3},{3,1},{4,6},{6,4},{5,7},{7,5},{8,10},{10,8},{9,1... | collective-permute-start | bytes 1032200 | tf_op jit(solution)/shard_map/ppermute | solution.py:23
  75.3 11.0 %collective-permute-start.14 = (bf16[144,896]{1,0:T(8,128)(2,1)S(1)}, bf16[144,896]{1,0:T(8,128)(2,1)S(1)}, u32[]{:S(2)}, u32[]{:S(2)}) collective-permute-start(bf16[144,896]{1,0:T(8,128)(2,1)S(1)} %get-tuple-element.53), channel_id=1, source_target_pairs={{0,4},{4,8},{8,12},{12,0},{1,5},{5,9},{9,13},{13,1},{2,6},{6,10},{... | collective-permute-start | bytes 774152 | tf_op jit(solution)/shard_map/ppermute | solution.py:23
  78.0 24.8 %collective-permute-start.15 = (bf16[144,896]{1,0:T(8,128)(2,1)S(1)}, bf16[144,896]{1,0:T(8,128)(2,1)S(1)}, u32[]{:S(2)}, u32[]{:S(2)}) collective-permute-start(bf16[144,896]{1,0:T(8,128)(2,1)S(1)} %get-tuple-element.54), channel_id=1, source_target_pairs={{0,8},{4,12},{8,0},{12,4},{1,9},{5,13},{9,1},{13,5},{2,10},{6,14},... | collective-permute-start | bytes 774152 | tf_op jit(solution)/shard_map/ppermute | solution.py:23
  78.1 26.9 %collective-permute-start.16 = (bf16[144,896]{1,0:T(8,128)(2,1)S(1)}, bf16[144,896]{1,0:T(8,128)(2,1)S(1)}, u32[]{:S(2)}, u32[]{:S(2)}) collective-permute-start(bf16[144,896]{1,0:T(8,128)(2,1)S(1)} %get-tuple-element.55), channel_id=1, source_target_pairs={{0,12},{4,0},{8,4},{12,8},{1,13},{5,1},{9,5},{13,9},{2,14},{6,2},{... | collective-permute-start | bytes 774152 | tf_op jit(solution)/shard_map/ppermute | solution.py:23
  81.8 36.4 %collective-permute-start.17 = (bf16[256,896]{1,0:T(8,128)(2,1)}, bf16[256,896]{1,0:T(8,128)(2,1)}, u32[]{:S(2)}, u32[]{:S(2)}) collective-permute-start(bf16[256,896]{1,0:T(8,128)(2,1)} %get-tuple-element.56), channel_id=1, source_target_pairs={{0,8},{4,12},{8,0},{12,4},{1,9},{5,13},{9,1},{13,5},{2,10},{6,14},... | collective-permute-start | bytes 1376264 | tf_op jit(solution)/shard_map/ppermute | solution.py:23
  87.0 24.5 %collective-permute-start.10 = (bf16[192,896]{1,0:T(8,128)(2,1)S(1)}, bf16[192,896]{1,0:T(8,128)(2,1)}, u32[]{:S(2)}, u32[]{:S(2)}) collective-permute-start(bf16[192,896]{1,0:T(8,128)(2,1)S(1)} %collective-permute-done.8.refs_0_.refs_9_), channel_id=1, source_target_pairs={{0,16},{16,0},{1,17},{17,1},{2,18},{18,2},{3,19},{19,3},{4,20},{20... | collective-permute-start | bytes 1032200 | tf_op jit(solution)/shard_map/ppermute | solution.py:23
  106.2 11.9 %collective-permute-start.11 = (bf16[192,896]{1,0:T(8,128)(2,1)}, bf16[192,896]{1,0:T(8,128)(2,1)}, u32[]{:S(2)}, u32[]{:S(2)}) collective-permute-start(bf16[192,896]{1,0:T(8,128)(2,1)} %collective-permute-done.9.refs_10_), channel_id=1, source_target_pairs={{0,16},{16,0},{1,17},{17,1},{2,18},{18,2},{3,19},{19,3},{4,20},{20... | collective-permute-start | bytes 1032200 | tf_op jit(solution)/shard_map/ppermute | solution.py:23
  127.3 21.1 %collective-permute-start.21 = (bf16[256,896]{1,0:T(8,128)(2,1)S(1)}, bf16[256,896]{1,0:T(8,128)(2,1)S(1)}, u32[]{:S(2)}, u32[]{:S(2)}) collective-permute-start(bf16[256,896]{1,0:T(8,128)(2,1)S(1)} %copy-done.23), channel_id=1, source_target_pairs={{0,4},{4,8},{8,12},{12,0},{1,5},{5,9},{9,13},{13,1},{2,6},{6,10},{... | collective-permute-start | bytes 1376264 | tf_op jit(solution)/shard_map/ppermute | solution.py:23
  138.6 12.6 %collective-permute-start.20 = (bf16[256,256]{1,0:T(8,128)(2,1)S(1)}, bf16[256,256]{1,0:T(8,128)(2,1)S(1)}, u32[]{:S(2)}, u32[]{:S(2)}) collective-permute-start(bf16[256,256]{1,0:T(8,128)(2,1)S(1)} %get-tuple-element.60.refs_0_), channel_id=1, source_target_pairs={{0,8},{4,12},{1,9},{5,13},{2,10},{6,14},{3,11},{7,15},{16,24},{20,... | collective-permute-start | bytes 393224 | tf_op jit(solution)/shard_map/ppermute | solution.py:29
  162.9 10.5 %collective-permute-start.24 = (f32[128,256]{1,0:T(8,128)S(1)}, f32[128,256]{1,0:T(8,128)S(1)}, u32[]{:S(2)}, u32[]{:S(2)}) collective-permute-start(f32[128,256]{1,0:T(8,128)S(1)} %get-tuple-element.67), channel_id=1, source_target_pairs={{4,0},{8,4},{12,8},{5,1},{9,5},{13,9},{6,2},{10,6},{14,10},{7,3},{... | collective-permute-start | bytes 393224 | tf_op jit(solution)/shard_map/ppermute | solution.py:29
  164.2 16.7 %collective-permute-start.25 = (f32[128,256]{1,0:T(8,128)S(1)}, f32[128,256]{1,0:T(8,128)S(1)}, u32[]{:S(2)}, u32[]{:S(2)}) collective-permute-start(f32[128,256]{1,0:T(8,128)S(1)} %get-tuple-element.68), channel_id=1, source_target_pairs={{8,0},{12,4},{9,1},{13,5},{10,2},{14,6},{11,3},{15,7},{24,16},{28,... | collective-permute-start | bytes 393224 | tf_op jit(solution)/shard_map/ppermute | solution.py:29
  181.0 27.2 %collective-permute-start.30 = (bf16[256,896]{1,0:T(8,128)(2,1)S(1)}, bf16[256,896]{1,0:T(8,128)(2,1)S(1)}, u32[]{:S(2)}, u32[]{:S(2)}) collective-permute-start(bf16[256,896]{1,0:T(8,128)(2,1)S(1)} %get-tuple-element.77), channel_id=1, source_target_pairs={{0,12},{4,0},{8,4},{12,8},{1,13},{5,1},{9,5},{13,9},{2,14},{6,2},{... | collective-permute-start | bytes 1376264 | tf_op jit(solution)/shard_map/ppermute | solution.py:23
  183.8 13.7 %collective-permute-start.29 = (bf16[256,64]{1,0:T(8,128)(2,1)S(1)}, bf16[256,64]{1,0:T(8,128)(2,1)S(1)}, u32[]{:S(2)}, u32[]{:S(2)}) collective-permute-start(bf16[256,64]{1,0:T(8,128)(2,1)S(1)} %get-tuple-element.75.refs_0_), channel_id=1, source_target_pairs={{0,12},{4,0},{8,4},{12,8},{1,13},{5,1},{9,5},{13,9},{2,14},{6,2},{... | collective-permute-start | bytes 98312 | tf_op jit(solution)/shard_map/ppermute | solution.py:23
  184.8 17.3 %collective-permute-start.28 = (bf16[256,64]{1,0:T(8,128)(2,1)S(1)}, bf16[256,64]{1,0:T(8,128)(2,1)S(1)}, u32[]{:S(2)}, u32[]{:S(2)}) collective-permute-start(bf16[256,64]{1,0:T(8,128)(2,1)S(1)} %get-tuple-element.75.refs_0_), channel_id=1, source_target_pairs={{0,8},{4,12},{8,0},{12,4},{1,9},{5,13},{9,1},{13,5},{2,10},{6,14},... | collective-permute-start | bytes 98312 | tf_op jit(solution)/shard_map/ppermute | solution.py:23
  187.3 20.9 %collective-permute-start.31 = (f32[96,160]{1,0:T(8,128)S(1)}, f32[96,160]{1,0:T(8,128)S(1)}, u32[]{:S(2)}, u32[]{:S(2)}) collective-permute-start(f32[96,160]{1,0:T(8,128)S(1)} %get-tuple-element.79), channel_id=1, source_target_pairs={{0,4},{4,8},{8,12},{12,0},{1,5},{5,9},{9,13},{13,1},{2,6},{6,10},{... | collective-permute-start | bytes 184328 | tf_op jit(solution)/shard_map/ppermute | solution.py:23
  187.3 20.9 %collective-permute-start.32 = (f32[96,160]{1,0:T(8,128)S(1)}, f32[96,160]{1,0:T(8,128)S(1)}, u32[]{:S(2)}, u32[]{:S(2)}) collective-permute-start(f32[96,160]{1,0:T(8,128)S(1)} %get-tuple-element.80), channel_id=1, source_target_pairs={{0,8},{4,12},{8,0},{12,4},{1,9},{5,13},{9,1},{13,5},{2,10},{6,14},... | collective-permute-start | bytes 184328 | tf_op jit(solution)/shard_map/ppermute | solution.py:23
  197.5 10.7 %collective-permute-start.33 = (f32[96,160]{1,0:T(8,128)S(1)}, f32[96,160]{1,0:T(8,128)S(1)}, u32[]{:S(2)}, u32[]{:S(2)}) collective-permute-start(f32[96,160]{1,0:T(8,128)S(1)} %get-tuple-element.81), channel_id=1, source_target_pairs={{0,12},{4,0},{8,4},{12,8},{1,13},{5,1},{9,5},{13,9},{2,14},{6,2},{... | collective-permute-start | bytes 184328 | tf_op jit(solution)/shard_map/ppermute | solution.py:23
  (37 other events, 466.7 us)

commit v6 on v5

--- a/solution.py
+++ b/solution.py
@@ -128,31 +128,6 @@
         return row, 0
 
     return place
-
-
-def select_kernel(bank_row, adapters, frozen, down_bank, up_bank, *refs):
-    share, outputs, rows, semaphore = refs[0], refs[1:5], refs[5], refs[6]
-    batch = lax.axis_index("batch")
-    width = share.shape[1]
-    place = (lax.axis_index("groups") * 2 + batch) * width
-    copies = [
-        pltpu.make_async_copy(
-            frozen.at[:, pl.ds(pl.multiple_of(place, 128), width)], share, semaphore.at[0]
-        )
-    ]
-    copies[0].start()
-    for which, sample in enumerate((batch, 1 - batch)):
-        for document in range(SEGS):
-            row = bank_row[adapters[sample, document]]
-            rows[which * SEGS + document] = row
-            for source, target in ((down_bank, outputs[which]), (up_bank, outputs[2 + which])):
-                copy = pltpu.make_async_copy(
-                    source.at[row], target.at[document], semaphore.at[len(copies)]
-                )
-                copy.start()
-                copies.append(copy)
-    for copy in copies:
-        copy.wait()
 
 
 def pack_kernel(unused, seq_count, own_down, far_down, own_up, far_up, tokens, *refs):
@@ -298,19 +273,7 @@
 
 def attention_kernel(block_count, unused, lengths, queries, incoming, cosines, sines, *refs):
     blocks = refs[:block_count]
-    output, query_grad, kept, sent, down_zeros, up_zeros = refs[block_count + unused : -4]
-    low_probs, down_blank, up_blank, semaphore = refs[-4:]
-    down_blank[...] = jnp.zeros_like(down_blank)
-    up_blank[...] = jnp.zeros_like(up_blank)
-    copies = []
-    for blank, zeros in ((down_blank, down_zeros), (up_blank, up_zeros)):
-        step = blank.shape[0]
-        for start in range(0, zeros.shape[0], step):
-            copy = pltpu.make_async_copy(
-                blank, zeros.at[pl.ds(start, step)], semaphore.at[len(copies)]
-            )
-            copy.start()
-            copies.append(copy)
+    output, query_grad, kept, sent, low_probs = refs[block_count + unused :]
     own_rows, query_columns = incoming.shape
     rows = blocks[0].shape[0]
     score_scale = HEAD_WIDTH ** (-0.5)
@@ -366,8 +329,6 @@
         query_grad[:, columns] = rotated(
             total[picked] * score_scale, cosines[own], -sines[own]
         ).astype(jnp.bfloat16)
-    for copy in copies:
-        copy.wait()
 
 
 def sum_kernel(kept, arrived, *sums):
@@ -429,46 +390,108 @@
     for holder in range(seq_count):
         blocks[holder] = terms[:, holder * held : (holder + 1) * held]
     for steps, block in enumerate(split_terms):
-        block[...] = blocks[ring_index(seq_index + steps - seq_count, seq_count)]
+        mine = blocks[ring_index(seq_index + steps - seq_count, seq_count)]
+        if block.shape == mine.shape:
+            block[...] = mine
+            continue
+        tail = held - 128
+        count = 128 // tail
+        height = mine.shape[0] // count
+        first_low = mine.shape[0] + height
+        block[: mine.shape[0]] = mine[:, :128]
+        for part in range(count):
+            block[mine.shape[0] : first_low, part * tail : (part + 1) * tail] = mine[
+                part * height : (part + 1) * height, 128:
+            ]
+        block[first_low:, : low.shape[1]] = turned[: rows // 2].astype(jnp.float32)
+        block[first_low:, low.shape[1] :] = turned[rows // 2 :].astype(jnp.float32)
 
 
 def token_kernel(gradients, matrix, token_grad):
     token_grad[...] = dot_nn(gradients[...], matrix[...]).astype(jnp.bfloat16)
 
 
-def split_halves(terms, own, far):
-    held = own.shape[1]
-    left, right = terms[:, :held], terms[:, held:]
-    ahead = lax.axis_index("batch") == 0
-    own[...] = jnp.where(ahead, left, right)
-    far[...] = jnp.where(ahead, right, left)
-
-
 def down_kernel(block_count, lengths, *refs):
-    ranks = refs[:block_count]
-    columns = refs[block_count : 2 * block_count]
-    up_parts = refs[2 * block_count : 3 * block_count]
-    outputs = refs[3 * block_count :]
+    columns = refs[:block_count]
+    up_parts = refs[block_count : 2 * block_count]
+    packed = up_parts[0].shape != up_parts[1].shape
+    rank_count = 1 if packed else block_count
+    ranks = refs[2 * block_count : 2 * block_count + rank_count]
+    outputs = refs[2 * block_count + rank_count :]
     rows, joint_rank = ranks[0].shape
     ends = kernel_marks(lengths)
+    up_rows, up_width = up_parts[0].shape
+    lows, ups = [ranks[0][...]], [up_parts[0][...]]
+    for behind in range(1, block_count):
+        if not packed:
+            lows.append(ranks[behind][...])
+            ups.append(up_parts[behind][...])
+            continue
+        part = up_parts[behind]
+        count = 128 // (up_width - 128)
+        first_low = up_rows + up_rows // count
+        halves = [part[first_low:, :joint_rank], part[first_low:, joint_rank:]]
+        lows.append(jnp.concatenate(halves, axis=0).astype(jnp.bfloat16))
     all_terms = []
     for document in range(SEGS):
         total = jnp.zeros((joint_rank, columns[0].shape[1]), jnp.float32)
         for behind in range(block_count):
             holder = ring_index(lax.axis_index("seq") - behind, block_count)
             segments = row_segments(ends, row_positions(holder * rows, rows))
-            low = ranks[behind][...]
-            chosen = jnp.where(segments == document, low, jnp.zeros_like(low))
+            chosen = jnp.where(segments == document, lows[behind], jnp.zeros_like(lows[behind]))
             total += dot_tn(chosen, columns[behind][...])
         all_terms.append(total)
     down_terms = jnp.concatenate(all_terms, axis=0)
-    up_terms = sum(part[...] for part in up_parts)
-    if len(outputs) == 2:
+    if not packed:
         outputs[0][...] = down_terms
-        outputs[1][...] = up_terms
-    else:
-        split_halves(down_terms, *outputs[:2])
-        split_halves(up_terms, *outputs[2:])
+        outputs[1][...] = sum(ups)
+        return
+    own_down, far, own_up, up_terms = outputs
+    tail = up_width - 128
+    height = up_rows // (128 // tail)
+    up_terms[...] = ups[0]
+    for part in up_parts[1:]:
+        up_terms[:, :128] += part[:up_rows]
+        for piece in range(128 // tail):
+            up_terms[piece * height : (piece + 1) * height, 128:] += part[
+                up_rows : up_rows + height, piece * tail : (piece + 1) * tail
+            ]
+    held, held_up = own_down.shape[1], own_up.shape[1]
+    ahead = lax.axis_index("batch") == 0
+    own_down[...] = jnp.where(ahead, down_terms[:, :held], down_terms[:, held:])
+    far[:, :held] = jnp.where(ahead, down_terms[:, held:], down_terms[:, :held])
+    left, right = up_terms[:, :held_up], up_terms[:, held_up:]
+    own_up[...] = jnp.where(ahead, left, right)
+    far_up = jnp.where(ahead, right, left)
+    spare = far.shape[1] - held
+    far[:up_rows, held:] = far_up[:, :spare]
+    far[up_rows:, held : held + held_up - spare] = far_up[:, spare:]
+
+
+def packed_bank_kernel(bank_rows, own_down, far, own_up, down_zeros, up_zeros, down_out, up_out):
+    step = pl.program_id(0)
+    joint_rank, held = down_out.shape[1], down_out.shape[3]
+    low_width, held_up = up_out.shape[1:]
+    up_rows = own_up.shape[0]
+    spare = far.shape[1] - held
+    down_total = jnp.zeros((joint_rank, held), jnp.float32)
+    head = jnp.zeros((low_width, spare), jnp.float32)
+    rest = jnp.zeros((low_width, held_up - spare), jnp.float32)
+    for document in range(SEGS):
+        rows = slice(document * joint_rank, (document + 1) * joint_rank)
+        lows = slice(document * low_width, (document + 1) * low_width)
+        same = bank_rows[document] == bank_rows[step]
+        down_total += jnp.where(same, own_down[rows], 0.0)
+        head += jnp.where(same, own_up[lows, :spare], 0.0)
+        rest += jnp.where(same, own_up[lows, spare:], 0.0)
+        same = bank_rows[SEGS + document] == bank_rows[step]
+        down_total += jnp.where(same, far[rows, :held], 0.0)
+        head += jnp.where(same, far[lows, held:], 0.0)
+        lows = slice(up_rows + document * low_width, up_rows + (document + 1) * low_width)
+        rest += jnp.where(same, far[lows, held : held + held_up - spare], 0.0)
+    down_out[0, :, 0, :] = down_total
+    up_out[0, :, :spare] = head
+    up_out[0, :, spare:] = rest
 
 
 def bank_kernel(block_count, bank_rows, *refs):
@@ -526,35 +549,51 @@
     first_end = lengths[0]
     second_end = first_end + lengths[1]
     half_count = seq_count // 2
-
+    held_down = adapter_down_weight.shape[3]
+    held_up = adapter_up_weight.shape[2]
+    down_width = held_down * batch_count
+    up_width = held_up * batch_count
+
+    positions = seq_index * rows + jnp.arange(rows, dtype=jnp.int32)
+    inside = positions - jnp.where(
+        positions >= second_end, second_end, jnp.where(positions >= first_end, first_end, 0)
+    )
+    exponent = jnp.arange(HEAD_WIDTH // 2, dtype=f32) * (2.0 / HEAD_WIDTH)
+    inverse = jnp.power(jnp.float32(rope_base), -exponent)
+    angles = inside.astype(f32)[:, None] * jnp.concatenate([inverse, inverse])[None, :]
+    signs = jnp.where(jnp.arange(HEAD_WIDTH) < HEAD_WIDTH // 2, -1.0, 1.0).astype(f32)
+    cosines = jnp.cos(angles)
+    sines = jnp.sin(angles) * signs[None, :]
+
+    sample_rows = lookup_rows(adapter_bank_row, document_adapter)
+    bank_rows = sample_rows.reshape(-1)
+    if batch_count == 2:
+        own_bank = jnp.where(batch_index == 0, sample_rows[0], sample_rows[1])
+        far_bank = jnp.where(batch_index == 0, sample_rows[1], sample_rows[0])
+        bank_rows = jnp.concatenate([own_bank, far_bank])
     down_bank = adapter_down_weight[:, :, 0, :]
+    down_zeros = jnp.zeros((adapters, joint_rank, 1, held_down), f32)
+    up_zeros = jnp.zeros((adapters, low_width, held_up), f32)
+
     plane_count = group_count * batch_count
     share = width // plane_count
     pieces, places = [], []
-    held_down = adapter_down_weight.shape[3]
-    held_up = adapter_up_weight.shape[2]
-    down_width = held_down * batch_count
+    padded_down = (held_down + 127) // 128 * 128
     direct = (
         group_count == 2
         and batch_count == 2
         and share % 128 == 0
         and down_width % 128 == 0
         and frozen_rows % 16 == 0
-        and 4 * 2 * held_up <= down_width
+        and 4 * up_width <= down_width
+        and up_width > 128
+        and 128 % (up_width - 128) == 0
+        and 0 < held_up + held_down - padded_down <= padded_down - held_down
     )
     if direct:
-        row_shapes = [(frozen_rows, share)]
-        row_shapes += [(SEGS, joint_rank, held_down)] * 2 + [(SEGS, low_width, held_up)] * 2
-        own_share, own_down, far_down, own_up, far_up, bank_rows = pl.pallas_call(
-            select_kernel,
-            out_shape=[jax.ShapeDtypeStruct(shape, bf16) for shape in row_shapes]
-            + [jax.ShapeDtypeStruct((2 * SEGS,), jnp.int32)],
-            in_specs=[in_smem()] * 2 + [in_place()] * 3,
-            out_specs=[in_place()] * 5 + [in_smem()],
-            scratch_shapes=[pltpu.SemaphoreType.DMA((1 + 4 * SEGS,))],
-            cost_estimate=cost(0, 4 * SEGS * joint_rank * held_down * 2),
-            name="select",
-        )(adapter_bank_row, document_adapter, frozen_qkv_matrix, down_bank, adapter_up_weight)
+        own_share = lax.dynamic_slice_in_dim(
+            frozen_qkv_matrix, (group_index * batch_count + batch_index) * share, share, axis=1
+        )
         pieces.append(frozen_qkv_matrix)
         places.append(frozen_place(seq_count, frozen_rows, None, 0, 0, 0))
         before = shift(own_share, "seq", 1)
@@ -564,14 +603,11 @@
             before = shift(before, "seq", 1)
             arrivals.append((steps, before))
         for steps, here in arrivals:
-            if steps < seq_count - 1:
-                over_batch = shift(here, "batch", 1)
-                over_groups = shift(here, "groups", 1)
-                over_both = shift(over_batch, "groups", 1)
-            else:
-                over_groups = shift(here, "groups", 1)
-                over_batch = shift(here, "batch", 1)
-                over_both = shift(over_groups, "batch", 1)
+            over_batch = shift(here, "batch", 1)
+            over_groups = shift(here, "groups", 1)
+            over_both = lax.ppermute(
+                here, ("groups", "batch"), [(at, plane_count - 1 - at) for at in range(plane_count)]
+            )
             for value, batch_step, group_step in (
                 (here, 0, 0),
                 (over_batch, 1, 0),
@@ -588,14 +624,16 @@
 
     column_blocks, up_blocks = None, None
     if direct:
-        far_down = shift(far_down, "batch", 1)
-        far_up = shift(far_up, "batch", 1)
+        far_down = shift(down_bank[far_bank], "batch", 1)
+        far_up = shift(adapter_up_weight[far_bank], "batch", 1)
+        own_down, own_up = down_bank[own_bank], adapter_up_weight[own_bank]
+        early = [before, down_zeros, up_zeros, cosines, sines, bank_rows]
         payload_rows = 2 * joint_rank + low_width // 2
         packed = pl.pallas_call(
-            functools.partial(pack_kernel, 1, seq_count),
+            functools.partial(pack_kernel, len(early), seq_count),
             out_shape=[jax.ShapeDtypeStruct((payload_rows, down_width), bf16)] * seq_count
             + [jax.ShapeDtypeStruct((rows, down_width), bf16)] * seq_count,
-            in_specs=[in_vmem()] * 5 + [in_place()],
+            in_specs=[in_vmem()] * 5 + [in_place()] * len(early),
             out_specs=[by_block((payload_rows, down_width))] * seq_count
             + [by_block((rows, down_width))] * seq_count,
             scratch_shapes=[
@@ -605,7 +643,7 @@
             compiler_params=pltpu.CompilerParams(vmem_limit_bytes=16 * mebibyte),
             cost_estimate=cost(0, 4 * rows * width),
             name="pack",
-        )(own_down, far_down, own_up, far_up, local_tokens, before)
+        )(own_down, far_down, own_up, far_up, local_tokens, *early)
         column_blocks = packed[seq_count:]
         down_parts = [
             shift(part, "seq", steps) if steps else part
@@ -613,7 +651,7 @@
         ]
         down_places = [down_place(seq_count, features, down_width, steps) for steps in range(seq_count)]
     else:
-        sample_rows = lookup_rows(adapter_bank_row, document_adapter)
+        bank_rows = sample_rows.reshape(-1)
         got_down = lax.all_to_all(
             down_bank[sample_rows], "batch", split_axis=0, concat_axis=0, tiled=True
         )
@@ -647,22 +685,11 @@
             for steps in range(seq_count)
         ]
 
-    positions = seq_index * rows + jnp.arange(rows, dtype=jnp.int32)
-    inside = positions - jnp.where(
-        positions >= second_end, second_end, jnp.where(positions >= first_end, first_end, 0)
-    )
-    exponent = jnp.arange(HEAD_WIDTH // 2, dtype=f32) * (2.0 / HEAD_WIDTH)
-    inverse = jnp.power(jnp.float32(rope_base), -exponent)
-    angles = inside.astype(f32)[:, None] * jnp.concatenate([inverse, inverse])[None, :]
-    signs = jnp.where(jnp.arange(HEAD_WIDTH) < HEAD_WIDTH // 2, -1.0, 1.0).astype(f32)
-    cosines = jnp.cos(angles)
-    sines = jnp.sin(angles) * signs[None, :]
-
     column_parts = [
         shift(block, "seq", steps) if steps else block
         for steps, block in enumerate(column_blocks)
     ]
-    early = [cosines, sines] + ([column_parts[2]] if seq_count > 3 else [])
+    early = [column_parts[2]] if direct and seq_count > 3 else []
     up_shape = (SEGS, joint_rank, query_columns + HEAD_WIDTH)
     matrix_rows = features + 2 * joint_rank
     arrived = [pltpu.VMEM((seq_count, low_width // 2, down_width), bf16)] if direct else []
@@ -706,27 +733,19 @@
     block_count = len(blocks)
     incoming = output_gradient[0]
     early_columns = [column_parts[1]]
-    blank_rows = 4
-    bank_shapes = [(adapters, joint_rank, 1, held_down), (adapters, low_width, held_up)]
-    attention, query_grad, kept, sent, down_zeros, up_zeros = pl.pallas_call(
+    attention, query_grad, kept, sent = pl.pallas_call(
         functools.partial(attention_kernel, block_count, len(early_columns)),
         out_shape=(
             jax.ShapeDtypeStruct((own_rows, query_columns), bf16),
             jax.ShapeDtypeStruct((own_rows, query_columns), bf16),
             jax.ShapeDtypeStruct((block_count, own_rows, 2 * HEAD_WIDTH), f32),
             jax.ShapeDtypeStruct((block_count, own_rows, 2 * HEAD_WIDTH), f32),
-        )
-        + tuple(jax.ShapeDtypeStruct(shape, f32) for shape in bank_shapes),
+        ),
         in_specs=[in_smem()]
         + [in_vmem()] * (4 + block_count)
         + [in_place()] * len(early_columns),
-        out_specs=(in_vmem(),) * 4 + (in_place(),) * 2,
-        scratch_shapes=[
-            pltpu.VMEM((block_count, QHEADS * own_rows, rows), bf16),
-            pltpu.VMEM((blank_rows,) + bank_shapes[0][1:], f32),
-            pltpu.VMEM((blank_rows,) + bank_shapes[1][1:], f32),
-            pltpu.SemaphoreType.DMA((2 * adapters // blank_rows,)),
-        ],
+        out_specs=(in_vmem(),) * 4,
+        scratch_shapes=[pltpu.VMEM((block_count, QHEADS * own_rows, rows), bf16)],
         compiler_params=pltpu.CompilerParams(vmem_limit_bytes=(8 + 4 * block_count) * mebibyte),
         cost_estimate=cost(
             10 * block_count * QHEADS * own_rows * rows * HEAD_WIDTH,
@@ -764,16 +783,20 @@
     column_parts[-1] = shift(late_block, "seq", seq_count - 1)
     other_pair = shift(pair_grad, "tp", 1)
 
+    split_shapes = [(SEGS * low_width, up_width)] * seq_count
+    if direct:
+        sent_rows = SEGS * low_width * up_width // 128 + rows // 2
+        split_shapes[1:] = [(sent_rows, 128)] * (seq_count - 1)
     gradients, rank_grad, *up_split = pl.pallas_call(
         functools.partial(rank_kernel, seq_count),
         out_shape=[
             jax.ShapeDtypeStruct((rows, matrix_rows), bf16),
             jax.ShapeDtypeStruct((rows, joint_rank), bf16),
         ]
-        + [jax.ShapeDtypeStruct((SEGS * low_width, held_up * batch_count), f32)] * seq_count,
+        + [jax.ShapeDtypeStruct(shape, f32) for shape in split_shapes],
         in_specs=[in_smem()] + [in_vmem()] * 6,
         out_specs=[by_block((rows, matrix_rows)), in_vmem()]
-        + [by_block((SEGS * low_width, held_up * batch_count))] * seq_count,
+        + [by_block(shape) for shape in split_shapes],
         scratch_shapes=[
             pltpu.VMEM((SEGS * low_width, features - HEAD_WIDTH), f32),
             pltpu.VMEM((seq_count, SEGS * low_width, held_up * batch_count), f32),
@@ -785,7 +808,9 @@
         document_lengths, query_grad, other_query, pair_grad, other_pair, low_rank, up_blocks
     )
 
-    rank_parts = [rank_grad] + [shift(rank_grad, "seq", steps) for steps in range(1, seq_count)]
+    rank_parts = [rank_grad]
+    if not direct:
+        rank_parts += [shift(rank_grad, "seq", steps) for steps in range(1, seq_count)]
     up_sums = [
         shift(block, "seq", steps) if steps else block for steps, block in enumerate(up_split)
     ]
@@ -806,24 +831,25 @@
     )(gradients, matrix)
 
     if direct:
-        term_shapes = [(SEGS * joint_rank, held_down)] * 2 + [(SEGS * low_width, held_up)] * 2
+        term_shapes = [(SEGS * joint_rank, held_down), (SEGS * joint_rank, padded_down)]
+        term_shapes += [(SEGS * low_width, held_up)]
     else:
-        term_shapes = [(SEGS * joint_rank, down_width), (SEGS * low_width, held_up * batch_count)]
+        term_shapes = [(SEGS * joint_rank, down_width), (SEGS * low_width, up_width)]
     terms = pl.pallas_call(
         functools.partial(down_kernel, seq_count),
         out_shape=[jax.ShapeDtypeStruct(shape, f32) for shape in term_shapes],
-        in_specs=[in_smem()] + [in_vmem()] * (3 * seq_count),
+        in_specs=[in_smem()] + [in_vmem()] * (2 * seq_count + len(rank_parts)),
         out_specs=[in_vmem()] * len(term_shapes),
+        scratch_shapes=[pltpu.VMEM((SEGS * low_width, up_width), f32)] if direct else [],
         compiler_params=pltpu.CompilerParams(vmem_limit_bytes=8 * mebibyte),
         cost_estimate=cost(
             2 * seq_count * rows * SEGS * joint_rank * down_width, 2 * seq_count * rows * down_width
         ),
         name="down_terms",
-    )(document_lengths, *rank_parts, *column_parts, *up_sums)
+    )(document_lengths, *column_parts, *up_sums, *rank_parts)
 
     if direct:
-        bank_downs = [terms[0], shift(terms[1], "batch", 1)]
-        bank_ups = [terms[2], shift(terms[3], "batch", 1)]
+        bank_terms = [terms[0], shift(terms[1], "batch", 1), terms[2]]
     else:
         down_send = jnp.transpose(
             terms[0].reshape(SEGS * joint_rank, batch_count, held_down), (1, 0, 2)
@@ -835,15 +861,15 @@
         back_up = lax.all_to_all(up_send, "batch", split_axis=0, concat_axis=0, tiled=True)
         bank_downs = [back_down[batch] for batch in range(batch_count)]
         bank_ups = [back_up[batch] for batch in range(batch_count)]
-
-    if not direct:
-        bank_rows = sample_rows.reshape(-1)
+        bank_terms = bank_downs + bank_ups
+
 
     def whole(array):
         return pl.BlockSpec(array.shape, lambda step, bank: (0,) * array.ndim)
 
+    term_count = len(bank_terms)
     down_grad, up_grad = pl.pallas_call(
-        functools.partial(bank_kernel, batch_count),
+        packed_bank_kernel if direct else functools.partial(bank_kernel, batch_count),
         out_shape=(
             jax.ShapeDtypeStruct(down_zeros.shape, f32),
             jax.ShapeDtypeStruct(up_zeros.shape, f32),
@@ -851,7 +877,7 @@
         grid_spec=pltpu.PrefetchScalarGridSpec(
             num_scalar_prefetch=1,
             grid=(batch_count * SEGS,),
-            in_specs=[whole(array) for array in bank_downs + bank_ups] + [in_place()] * 2,
+            in_specs=[whole(array) for array in bank_terms] + [in_place()] * 2,
             out_specs=(
                 pl.BlockSpec(
                     (1, joint_rank, 1, held_down),
@@ -863,13 +889,12 @@
                 ),
             ),
         ),
-        input_output_aliases={1 + 2 * batch_count: 0, 2 + 2 * batch_count: 1},
+        input_output_aliases={1 + term_count: 0, 2 + term_count: 1},
         compiler_params=pltpu.CompilerParams(vmem_limit_bytes=16 * mebibyte),
         name="bank_rows",
     )(
         bank_rows,
-        *bank_downs,
-        *bank_ups,
+        *bank_terms,
         down_zeros,
         up_zeros,
     )

time: 222 us -> 166 us (0.75); the launches traced: 222 us -> 163 us
  Pallas kernels: 52.6 us -> 19.9 us
  waiting for transfers between devices: 99 us -> 76.3 us
  starting transfers between devices: 50.7 us -> 44 us
  local copies, waits for them, and re-layouts: 14.9 us -> 18.1 us
    pallas_call x3 -> x2, Pallas kernels: 30.4 us -> 3.37 us  [the longest x1 3.05 us: shards(): pl.pallas_call(packed_bank_kernel if direct else functools.partial(bank_k...]
    ppermute x32 -> x25, waiting for transfers between devices: 78.4 us -> 60.6 us  [shift(): lax.ppermute(value, axis, [(at, (at + steps) % count) for at in range(cou...]
    ppermute x32 -> x25, starting transfers between devices: 41.1 us -> 31.6 us  [shift(): lax.ppermute(value, axis, [(at, (at + steps) % count) for at in range(cou...]
    unnamed x50 -> x19, local copies, waits for them, and re-layouts: 13.6 us -> 4.54 us
    gather x0 -> x4, local copies, waits for them, and re-layouts: none -> 6.61 us  [the longest x2 3.31 us: shards(): own_down, own_up = (down_bank[own_bank], adapter_up_weight[own_bank])]
    ppermute x4, waiting for transfers between devices: 20.6 us -> 15.7 us  [push(): return lax.ppermute(value, axis, pairs)]
    broadcast_in_dim x0 -> x2, local copies, waits for them, and re-layouts: none -> 4.64 us  [the longest x1 4.53 us: shards(): down_zeros = jnp.zeros((adapters, joint_rank, 1, held_down), f32)]
    pallas_call x1, Pallas kernels: 7.49 us -> 3.43 us  [shards(): pl.pallas_call(functools.partial(attention_kernel, block_count, len(early...]
  transfers between devices with their start and end apart: 36 -> 32, of which waited for: 20 -> 17; matrix products, arithmetic and copies ran while one was open for 2% -> 10% of each run, Pallas kernels for 4% -> 5%
where the time goes in v6:
time: 166 us; the launch traced here: 163 us
  waiting for transfers between devices  76.3 us (46%)
  starting transfers between devices  44 us (27%)
  Pallas kernels  19.9 us (12%)
  local copies, waits for them, and re-layouts  18.1 us (11%)
  other arithmetic  2.41 us (1%)
  between operations  2.26 us (1%)
    ppermute x25, waiting for transfers between devices, shift(): lax.ppermute(value, axis, [(at, (at + steps) % count) for at in range(cou...  60.6 us
    ppermute x25, starting transfers between devices, shift(): lax.ppermute(value, axis, [(at, (at + steps) % count) for at in range(cou...  31.6 us
    ppermute x4, waiting for transfers between devices, push(): return lax.ppermute(value, axis, pairs)  15.7 us
    ppermute x4, starting transfers between devices, push(): return lax.ppermute(value, axis, pairs)  8.39 us
    pallas_call x1, Pallas kernels, shards(): pl.pallas_call(token_kernel, grid=(width // chunk,), out_shape=jax.ShapeD...  4.84 us
    unnamed x19, local copies, waits for them, and re-layouts  4.54 us
    broadcast_in_dim x1, local copies, waits for them, and re-layouts, shards(): down_zeros = jnp.zeros((adapters, joint_rank, 1, held_down), f32)  4.53 us
    ppermute x3, starting transfers between devices, shards(): lax.ppermute(here, ('groups', 'batch'), [(at, plane_count - 1 - at) for a...  4.04 us
  transfers between devices with their start and end apart: 32, of which 17 were waited for; matrix products, arithmetic and copies ran while one was open for 10% of the time, Pallas kernels for 5%

profile of v6, /device:TPU:0, one launch (start us, length us, event | category | flops | bytes accessed | tf_op | source)
XLA Modules:
  0.0 163.0 jit_solution(2998008581788309988)
XLA Ops:
  1.7 5.1 %collective-permute-start.4 = (bf16[192,896]{1,0:T(8,128)(2,1)S(1)}, bf16[192,896]{1,0:T(8,128)(2,1)S(1)}, u32[]{:S(2)}, u32[]{:S(2)}) collective-permute-start(bf16[192,896]{1,0:T(8,128)(2,1)S(1)} %constant_dynamic-slice_fusion.1), channel_id=1, source_target_pairs={{0,12},{4,0},{8,4},{12,8},{1,13},{5,1},{9,5},{13,9},{2,14},{6,2},{... | collective-permute-start | bytes 1032200 | tf_op jit(solution)/shard_map/ppermute | solution.py:23
  10.8 2.7 %gather_fusion.1 = bf16[3,64,448]{2,1,0:T(8,128)(2,1)S(1)} fusion(bf16[64,64,448]{2,1,0:T(8,128)(2,1)} %bitcast.19, s32[1024]{0:T(1024)S(1)} %pad_clamp_fusion), kind=kCustom, calls=%fused_computation.1 | custom fusion | bytes 344076 | tf_op jit(solution)/shard_map/gather | solution.py:627
  16.8 2.5 %collective-permute-start.7 = (bf16[192,896]{1,0:T(8,128)(2,1)S(1)}, bf16[192,896]{1,0:T(8,128)(2,1)S(1)}, u32[]{:S(2)}, u32[]{:S(2)}) collective-permute-start(bf16[192,896]{1,0:T(8,128)(2,1)S(1)} %collective-permute-done.4.refs_5_), channel_id=1, source_target_pairs={{0,18},{2,16},{16,2},{18,0},{1,19},{3,17},{17,3},{19,1},{4,22},{6,... | collective-permute-start | bytes 1032200 | tf_op jit(solution)/shard_map/ppermute | solution.py:608
  19.3 3.1 %collective-permute-done.refs_1_ = bf16[192,896]{1,0:T(8,128)(2,1)S(1)} collective-permute-done((bf16[192,896]{1,0:T(8,128)(2,1)S(1)}, bf16[192,896]{1,0:T(8,128)(2,1)S(1)}, u32[]{:S(2)}, u32[]{:S(2)}) %collective-permute-start) | collective-permute-done | bytes 344096 | tf_op jit(solution)/shard_map/ppermute | solution.py:23
  30.1 2.7 %gather_fusion = bf16[3,64,448]{2,1,0:T(8,128)(2,1)S(1)} fusion(bf16[64,64,448]{2,1,0:T(8,128)(2,1)} %bitcast.20, s32[1024]{0:T(1024)S(1)} %pad_clamp_fusion.1), kind=kCustom, calls=%fused_computation | custom fusion | bytes 344076 | tf_op jit(solution)/shard_map/gather | solution.py:629
  36.1 4.5 %broadcast_in_dim.47.refs_1_.down_zeros = f32[64,64,1,448]{3,2,1,0:T(1,128)S(1)} broadcast(f32[]{:T(128)} %constant.11.clone.1), dimensions={} | broadcast | bytes 7340036 | tf_op jit(solution)/shard_map/broadcast_in_dim | solution.py:575
  41.1 3.0 %copy-done.1 = f32[64,64,1,448]{3,2,1,0:T(1,128)} copy-done((f32[64,64,1,448]{3,2,1,0:T(1,128)}, f32[64,64,1,448]{3,2,1,0:T(1,128)S(1)}, u32[]{:S(2)}) %copy-start.1) | copy-done | bytes 7340056
  44.1 2.8 %collective-permute-start.15 = (bf16[144,896]{1,0:T(8,128)(2,1)S(1)}, bf16[144,896]{1,0:T(8,128)(2,1)S(1)}, u32[]{:S(2)}, u32[]{:S(2)}) collective-permute-start(bf16[144,896]{1,0:T(8,128)(2,1)S(1)} %get-tuple-element.40), channel_id=1, source_target_pairs={{0,8},{4,12},{8,0},{12,4},{1,9},{5,13},{9,1},{13,5},{2,10},{6,14},... | collective-permute-start | bytes 774152 | tf_op jit(solution)/shard_map/ppermute | solution.py:23
  47.1 3.0 %collective-permute-done.2.refs_3_ = bf16[192,896]{1,0:T(8,128)(2,1)S(1)} collective-permute-done((bf16[192,896]{1,0:T(8,128)(2,1)S(1)}, bf16[192,896]{1,0:T(8,128)(2,1)S(1)}, u32[]{:S(2)}, u32[]{:S(2)}) %collective-permute-start.2) | collective-permute-done | bytes 344096 | tf_op jit(solution)/shard_map/ppermute | solution.py:23
  52.2 3.0 %collective-permute-done.14.refs_14_ = bf16[144,896]{1,0:T(8,128)(2,1)S(1)} collective-permute-done((bf16[144,896]{1,0:T(8,128)(2,1)S(1)}, bf16[144,896]{1,0:T(8,128)(2,1)S(1)}, u32[]{:S(2)}, u32[]{:S(2)}) %collective-permute-start.14) | collective-permute-done | bytes 258080 | tf_op jit(solution)/shard_map/ppermute | solution.py:23
  55.6 16.8 %collective-permute-done.15.refs_15_ = bf16[144,896]{1,0:T(8,128)(2,1)S(1)} collective-permute-done((bf16[144,896]{1,0:T(8,128)(2,1)S(1)}, bf16[144,896]{1,0:T(8,128)(2,1)S(1)}, u32[]{:S(2)}, u32[]{:S(2)}) %collective-permute-start.15) | collective-permute-done | bytes 258080 | tf_op jit(solution)/shard_map/ppermute | solution.py:23
  72.4 5.7 %collective-permute-start.16 = (bf16[144,896]{1,0:T(8,128)(2,1)S(1)}, bf16[144,896]{1,0:T(8,128)(2,1)S(1)}, u32[]{:S(2)}, u32[]{:S(2)}) collective-permute-start(bf16[144,896]{1,0:T(8,128)(2,1)S(1)} %get-tuple-element.41), channel_id=1, source_target_pairs={{0,12},{4,0},{8,4},{12,8},{1,13},{5,1},{9,5},{13,9},{2,14},{6,2},{... | collective-permute-start | bytes 774152 | tf_op jit(solution)/shard_map/ppermute | solution.py:23
  78.1 8.7 %collective-permute-done.16.refs_16_ = bf16[144,896]{1,0:T(8,128)(2,1)S(1)} collective-permute-done((bf16[144,896]{1,0:T(8,128)(2,1)S(1)}, bf16[144,896]{1,0:T(8,128)(2,1)S(1)}, u32[]{:S(2)}, u32[]{:S(2)}) %collective-permute-start.16) | collective-permute-done | bytes 258080 | tf_op jit(solution)/shard_map/ppermute | solution.py:23
  86.8 3.8 %project.1 = (f32[256,896]{1,0:T(8,128)S(1)}, bf16[896,3584]{1,0:T(8,128)(2,1)S(1)}, bf16[3,64,640]{2,1,0:T(8,128)(2,1)S(1)}) custom-call(bf16[256,3584]{1,0:T(8,128)(2,1)S(1)} %bitcast.16, bf16[192,3584]{1,0:T(8,128)(2,1)S(1)} %copy-done.4, bf16[192,896]{1,0:T(8,128)(2,1)S(1)} %collective-permute-done.refs_1_, ...), custom_call_target="tpu_custom_call" | custom-call | flops 1644167168 | bytes 8257536 | tf_op jit(solution)/shard_map/project/pallas_call | solution.py:696
  95.8 4.3 %collective-permute-start.19 = (bf16[256,256]{1,0:T(8,128)(2,1)S(1)}, bf16[256,256]{1,0:T(8,128)(2,1)S(1)}, u32[]{:S(2)}, u32[]{:S(2)}) collective-permute-start(bf16[256,256]{1,0:T(8,128)(2,1)S(1)} %get-tuple-element.46.refs_0_), channel_id=1, source_target_pairs={{0,4},{4,8},{8,12},{1,5},{5,9},{9,13},{2,6},{6,10},{10,14},{3,7},{... | collective-permute-start | bytes 393224 | tf_op jit(solution)/shard_map/ppermute | solution.py:29
  100.1 5.3 %collective-permute-done.21.refs_3_.refs_1_ = bf16[256,896]{1,0:T(8,128)(2,1)S(1)} collective-permute-done((bf16[256,896]{1,0:T(8,128)(2,1)S(1)}, bf16[256,896]{1,0:T(8,128)(2,1)S(1)}, u32[]{:S(2)}, u32[]{:S(2)}) %collective-permute-start.21) | collective-permute-done | bytes 458784 | tf_op jit(solution)/shard_map/ppermute | solution.py:23
  107.5 3.4 %attention.1 = (bf16[128,512]{1,0:T(8,128)(2,1)}, bf16[128,512]{1,0:T(8,128)(2,1)S(1)}, f32[3,128,256]{2,1,0:T(8,128)S(1)}, f32[3,128,256]{2,1,0:T(8,128)S(1)}) custom-call(s32[2,3]{1,0:T(2,128)S(1)} %copy-done.7, bf16[512,128]{1,0:T(8,128)(2,1)S(1)} %get-tuple-element.45.queries, bf16[128,512]{1,0:T(8,128)(2,1)S(1)} %bitcast.17, ...), custom_call_target="tpu_custom_call" | custom-call | flops 503316480 | bytes 786432 | tf_op jit(solution)/shard_map/attention/pallas_call | solution.py:736
  115.3 6.1 %collective-permute-done.24.refs_1_ = f32[128,256]{1,0:T(8,128)S(1)} collective-permute-done((f32[128,256]{1,0:T(8,128)S(1)}, f32[128,256]{1,0:T(8,128)S(1)}, u32[]{:S(2)}, u32[]{:S(2)}) %collective-permute-start.24) | collective-permute-done | bytes 131104 | tf_op jit(solution)/shard_map/ppermute | solution.py:29
  121.4 7.5 %collective-permute-done.25.refs_2_ = f32[128,256]{1,0:T(8,128)S(1)} collective-permute-done((f32[128,256]{1,0:T(8,128)S(1)}, f32[128,256]{1,0:T(8,128)S(1)}, u32[]{:S(2)}, u32[]{:S(2)}) %collective-permute-start.25) | collective-permute-done | bytes 131104 | tf_op jit(solution)/shard_map/ppermute | solution.py:29
  136.4 7.9 %collective-permute-done.28.refs_5_ = f32[248,128]{1,0:T(8,128)S(1)} collective-permute-done((f32[248,128]{1,0:T(8,128)S(1)}, f32[248,128]{1,0:T(8,128)S(1)}, u32[]{:S(2)}, u32[]{:S(2)}) %collective-permute-start.28) | collective-permute-done | bytes 127008 | tf_op jit(solution)/shard_map/ppermute | solution.py:23
  144.3 4.6 %collective-permute-done.29.refs_6_ = f32[248,128]{1,0:T(8,128)S(1)} collective-permute-done((f32[248,128]{1,0:T(8,128)S(1)}, f32[248,128]{1,0:T(8,128)S(1)}, u32[]{:S(2)}, u32[]{:S(2)}) %collective-permute-start.29) | collective-permute-done | bytes 127008 | tf_op jit(solution)/shard_map/ppermute | solution.py:23
  151.8 4.8 %token_gradient.1 = bf16[256,3584]{1,0:T(8,128)(2,1)} custom-call(bf16[256,896]{1,0:T(8,128)(2,1)S(1)} %get-tuple-element.58.gradients, bf16[896,3584]{1,0:T(8,128)(2,1)S(1)} %get-tuple-element.59.matrix), custom_call_target="tpu_custom_call" | custom-call | flops 1644167168 | bytes 8257536 | tf_op jit(solution)/shard_map/token_gradient/pallas_call | solution.py:819
  156.6 3.3 %collective-permute-done.31.far = f32[192,512]{1,0:T(8,128)S(1)} collective-permute-done((f32[192,512]{1,0:T(8,128)S(1)}, f32[192,512]{1,0:T(8,128)S(1)}, u32[]{:S(2)}, u32[]{:S(2)}) %collective-permute-start.31) | collective-permute-done | bytes 393248 | tf_op jit(solution)/shard_map/ppermute | solution.py:23
  159.9 3.0 %bank_rows.1 = (f32[64,64,1,448]{3,2,1,0:T(1,128)}, f32[64,32,80]{2,1,0:T(8,128)}) custom-call(s32[6]{0:T(128)S(1)} %pad_add_fusion.refs_5_.bank_rows, f32[192,448]{1,0:T(8,128)S(1)} %get-tuple-element.67.own_down, f32[192,512]{1,0:T(8,128)S(1)} %collective-permute-done.31.far, ...), custom_call_target="tpu_custom_call", output_to_operand_aliasing={{0}: (4, {}), {1}: (5, {})} | custom-call | tf_op jit(solution)/shard_map/bank_rows/pallas_call | solution.py:871
  (88 shorter events, 42.8 us)
Async XLA Ops:
  1.7 15.1 %collective-permute-start.4 = (bf16[192,896]{1,0:T(8,128)(2,1)S(1)}, bf16[192,896]{1,0:T(8,128)(2,1)S(1)}, u32[]{:S(2)}, u32[]{:S(2)}) collective-permute-start(bf16[192,896]{1,0:T(8,128)(2,1)S(1)} %constant_dynamic-slice_fusion.1), channel_id=1, source_target_pairs={{0,12},{4,0},{8,4},{12,8},{1,13},{5,1},{9,5},{13,9},{2,14},{6,2},{... | collective-permute-start | bytes 1032200 | tf_op jit(solution)/shard_map/ppermute | solution.py:23
  6.8 15.6 %collective-permute-start = (bf16[192,896]{1,0:T(8,128)(2,1)S(1)}, bf16[192,896]{1,0:T(8,128)(2,1)S(1)}, u32[]{:S(2)}, u32[]{:S(2)}) collective-permute-start(bf16[192,896]{1,0:T(8,128)(2,1)S(1)} %constant_dynamic-slice_fusion.1), channel_id=1, source_target_pairs={{0,4},{4,8},{8,12},{12,0},{1,5},{5,9},{9,13},{13,1},{2,6},{6,10},{... | collective-permute-start | bytes 1032200 | tf_op jit(solution)/shard_map/ppermute | solution.py:23
  9.2 17.0 %collective-permute-start.13 = (bf16[3,32,80]{2,1,0:T(8,128)(2,1)S(1)}, bf16[3,32,80]{2,1,0:T(8,128)(2,1)S(1)}, u32[]{:S(2)}, u32[]{:S(2)}) collective-permute-start(bf16[3,32,80]{2,1,0:T(8,128)(2,1)S(1)} %gather_fusion.3), channel_id=1, source_target_pairs={{0,2},{2,0},{1,3},{3,1},{4,6},{6,4},{5,7},{7,5},{8,10},{10,8},{9,1... | collective-permute-start | bytes 46088 | tf_op jit(solution)/shard_map/ppermute | solution.py:23
  13.6 14.8 %collective-permute-start.12 = (bf16[3,64,448]{2,1,0:T(8,128)(2,1)S(1)}, bf16[3,64,448]{2,1,0:T(8,128)(2,1)S(1)}, u32[]{:S(2)}, u32[]{:S(2)}) collective-permute-start(bf16[3,64,448]{2,1,0:T(8,128)(2,1)S(1)} %gather_fusion.1), channel_id=1, source_target_pairs={{0,2},{2,0},{1,3},{3,1},{4,6},{6,4},{5,7},{7,5},{8,10},{10,8},{9,1... | collective-permute-start | bytes 516104 | tf_op jit(solution)/shard_map/ppermute | solution.py:23
  16.8 16.0 %collective-permute-start.7 = (bf16[192,896]{1,0:T(8,128)(2,1)S(1)}, bf16[192,896]{1,0:T(8,128)(2,1)S(1)}, u32[]{:S(2)}, u32[]{:S(2)}) collective-permute-start(bf16[192,896]{1,0:T(8,128)(2,1)S(1)} %collective-permute-done.4.refs_5_), channel_id=1, source_target_pairs={{0,18},{2,16},{16,2},{18,0},{1,19},{3,17},{17,3},{19,1},{4,22},{6,... | collective-permute-start | bytes 1032200 | tf_op jit(solution)/shard_map/ppermute | solution.py:608
  22.4 12.0 %collective-permute-start.8 = (bf16[192,896]{1,0:T(8,128)(2,1)S(1)}, bf16[192,896]{1,0:T(8,128)(2,1)S(1)}, u32[]{:S(2)}, u32[]{:S(2)}) collective-permute-start(bf16[192,896]{1,0:T(8,128)(2,1)S(1)} %collective-permute-done.refs_1_), channel_id=1, source_target_pairs={{0,4},{4,8},{8,12},{12,0},{1,5},{5,9},{9,13},{13,1},{2,6},{6,10},{... | collective-permute-start | bytes 1032200 | tf_op jit(solution)/shard_map/ppermute | solution.py:23
  24.7 19.4 %collective-permute-start.6 = (bf16[192,896]{1,0:T(8,128)(2,1)S(1)}, bf16[192,896]{1,0:T(8,128)(2,1)S(1)}, u32[]{:S(2)}, u32[]{:S(2)}) collective-permute-start(bf16[192,896]{1,0:T(8,128)(2,1)S(1)} %collective-permute-done.4.refs_5_), channel_id=1, source_target_pairs={{0,16},{16,0},{1,17},{17,1},{2,18},{18,2},{3,19},{19,3},{4,20},{20... | collective-permute-start | bytes 1032200 | tf_op jit(solution)/shard_map/ppermute | solution.py:23
  26.3 17.8 %collective-permute-start.5 = (bf16[192,896]{1,0:T(8,128)(2,1)S(1)}, bf16[192,896]{1,0:T(8,128)(2,1)S(1)}, u32[]{:S(2)}, u32[]{:S(2)}) collective-permute-start(bf16[192,896]{1,0:T(8,128)(2,1)S(1)} %collective-permute-done.4.refs_5_), channel_id=1, source_target_pairs={{0,2},{2,0},{1,3},{3,1},{4,6},{6,4},{5,7},{7,5},{8,10},{10,8},{9,1... | collective-permute-start | bytes 1032200 | tf_op jit(solution)/shard_map/ppermute | solution.py:23
  29.0 17.9 %collective-permute-start.3 = (bf16[192,896]{1,0:T(8,128)(2,1)S(1)}, bf16[192,896]{1,0:T(8,128)(2,1)S(1)}, u32[]{:S(2)}, u32[]{:S(2)}) collective-permute-start(bf16[192,896]{1,0:T(8,128)(2,1)S(1)} %collective-permute-done.refs_1_), channel_id=1, source_target_pairs={{0,18},{2,16},{16,2},{18,0},{1,19},{3,17},{17,3},{19,1},{4,22},{6,... | collective-permute-start | bytes 1032200 | tf_op jit(solution)/shard_map/ppermute | solution.py:608
  32.8 17.3 %collective-permute-start.2 = (bf16[192,896]{1,0:T(8,128)(2,1)S(1)}, bf16[192,896]{1,0:T(8,128)(2,1)S(1)}, u32[]{:S(2)}, u32[]{:S(2)}) collective-permute-start(bf16[192,896]{1,0:T(8,128)(2,1)S(1)} %collective-permute-done.refs_1_), channel_id=1, source_target_pairs={{0,16},{16,0},{1,17},{17,1},{2,18},{18,2},{3,19},{19,3},{4,20},{20... | collective-permute-start | bytes 1032200 | tf_op jit(solution)/shard_map/ppermute | solution.py:23
  34.4 16.8 %collective-permute-start.1 = (bf16[192,896]{1,0:T(8,128)(2,1)S(1)}, bf16[192,896]{1,0:T(8,128)(2,1)S(1)}, u32[]{:S(2)}, u32[]{:S(2)}) collective-permute-start(bf16[192,896]{1,0:T(8,128)(2,1)S(1)} %collective-permute-done.refs_1_), channel_id=1, source_target_pairs={{0,2},{2,0},{1,3},{3,1},{4,6},{6,4},{5,7},{7,5},{8,10},{10,8},{9,1... | collective-permute-start | bytes 1032200 | tf_op jit(solution)/shard_map/ppermute | solution.py:23
  44.1 28.3 %collective-permute-start.15 = (bf16[144,896]{1,0:T(8,128)(2,1)S(1)}, bf16[144,896]{1,0:T(8,128)(2,1)S(1)}, u32[]{:S(2)}, u32[]{:S(2)}) collective-permute-start(bf16[144,896]{1,0:T(8,128)(2,1)S(1)} %get-tuple-element.40), channel_id=1, source_target_pairs={{0,8},{4,12},{8,0},{12,4},{1,9},{5,13},{9,1},{13,5},{2,10},{6,14},... | collective-permute-start | bytes 774152 | tf_op jit(solution)/shard_map/ppermute | solution.py:23
  46.9 39.9 %collective-permute-start.17 = (bf16[256,896]{1,0:T(8,128)(2,1)S(1)}, bf16[256,896]{1,0:T(8,128)(2,1)S(1)}, u32[]{:S(2)}, u32[]{:S(2)}) collective-permute-start(bf16[256,896]{1,0:T(8,128)(2,1)S(1)} %get-tuple-element.42), channel_id=1, source_target_pairs={{0,8},{4,12},{8,0},{12,4},{1,9},{5,13},{9,1},{13,5},{2,10},{6,14},... | collective-permute-start | bytes 1376264 | tf_op jit(solution)/shard_map/ppermute | solution.py:23
  50.1 36.6 %collective-permute-start.11 = (bf16[192,896]{1,0:T(8,128)(2,1)S(1)}, bf16[192,896]{1,0:T(8,128)(2,1)S(1)}, u32[]{:S(2)}, u32[]{:S(2)}) collective-permute-start(bf16[192,896]{1,0:T(8,128)(2,1)S(1)} %collective-permute-done.8.refs_0_.refs_9_), channel_id=1, source_target_pairs={{0,18},{2,16},{16,2},{18,0},{1,19},{3,17},{17,3},{19,1},{4,22},{6,... | collective-permute-start | bytes 1032200 | tf_op jit(solution)/shard_map/ppermute | solution.py:608
  51.3 35.5 %collective-permute-start.10 = (bf16[192,896]{1,0:T(8,128)(2,1)S(1)}, bf16[192,896]{1,0:T(8,128)(2,1)S(1)}, u32[]{:S(2)}, u32[]{:S(2)}) collective-permute-start(bf16[192,896]{1,0:T(8,128)(2,1)S(1)} %collective-permute-done.8.refs_0_.refs_9_), channel_id=1, source_target_pairs={{0,16},{16,0},{1,17},{17,1},{2,18},{18,2},{3,19},{19,3},{4,20},{20... | collective-permute-start | bytes 1032200 | tf_op jit(solution)/shard_map/ppermute | solution.py:23
  55.1 31.7 %collective-permute-start.9 = (bf16[192,896]{1,0:T(8,128)(2,1)S(1)}, bf16[192,896]{1,0:T(8,128)(2,1)S(1)}, u32[]{:S(2)}, u32[]{:S(2)}) collective-permute-start(bf16[192,896]{1,0:T(8,128)(2,1)S(1)} %collective-permute-done.8.refs_0_.refs_9_), channel_id=1, source_target_pairs={{0,2},{2,0},{1,3},{3,1},{4,6},{6,4},{5,7},{7,5},{8,10},{10,8},{9,1... | collective-permute-start | bytes 1032200 | tf_op jit(solution)/shard_map/ppermute | solution.py:23
  72.4 14.4 %collective-permute-start.16 = (bf16[144,896]{1,0:T(8,128)(2,1)S(1)}, bf16[144,896]{1,0:T(8,128)(2,1)S(1)}, u32[]{:S(2)}, u32[]{:S(2)}) collective-permute-start(bf16[144,896]{1,0:T(8,128)(2,1)S(1)} %get-tuple-element.41), channel_id=1, source_target_pairs={{0,12},{4,0},{8,4},{12,8},{1,13},{5,1},{9,5},{13,9},{2,14},{6,2},{... | collective-permute-start | bytes 774152 | tf_op jit(solution)/shard_map/ppermute | solution.py:23
  90.8 14.7 %collective-permute-start.21 = (bf16[256,896]{1,0:T(8,128)(2,1)S(1)}, bf16[256,896]{1,0:T(8,128)(2,1)S(1)}, u32[]{:S(2)}, u32[]{:S(2)}) collective-permute-start(bf16[256,896]{1,0:T(8,128)(2,1)S(1)} %get-tuple-element.47), channel_id=1, source_target_pairs={{0,4},{4,8},{8,12},{12,0},{1,5},{5,9},{9,13},{13,1},{2,6},{6,10},{... | collective-permute-start | bytes 1376264 | tf_op jit(solution)/shard_map/ppermute | solution.py:23
  95.8 11.7 %collective-permute-start.19 = (bf16[256,256]{1,0:T(8,128)(2,1)S(1)}, bf16[256,256]{1,0:T(8,128)(2,1)S(1)}, u32[]{:S(2)}, u32[]{:S(2)}) collective-permute-start(bf16[256,256]{1,0:T(8,128)(2,1)S(1)} %get-tuple-element.46.refs_0_), channel_id=1, source_target_pairs={{0,4},{4,8},{8,12},{1,5},{5,9},{9,13},{2,6},{6,10},{10,14},{3,7},{... | collective-permute-start | bytes 393224 | tf_op jit(solution)/shard_map/ppermute | solution.py:29
  114.0 15.0 %collective-permute-start.25 = (f32[128,256]{1,0:T(8,128)S(1)}, f32[128,256]{1,0:T(8,128)S(1)}, u32[]{:S(2)}, u32[]{:S(2)}) collective-permute-start(f32[128,256]{1,0:T(8,128)S(1)} %get-tuple-element.54), channel_id=1, source_target_pairs={{8,0},{12,4},{9,1},{13,5},{10,2},{14,6},{11,3},{15,7},{24,16},{28,... | collective-permute-start | bytes 393224 | tf_op jit(solution)/shard_map/ppermute | solution.py:29
  129.0 20.3 %collective-permute-start.27 = (bf16[256,896]{1,0:T(8,128)(2,1)S(1)}, bf16[256,896]{1,0:T(8,128)(2,1)S(1)}, u32[]{:S(2)}, u32[]{:S(2)}) collective-permute-start(bf16[256,896]{1,0:T(8,128)(2,1)S(1)} %get-tuple-element.61), channel_id=1, source_target_pairs={{0,12},{4,0},{8,4},{12,8},{1,13},{5,1},{9,5},{13,9},{2,14},{6,2},{... | collective-permute-start | bytes 1376264 | tf_op jit(solution)/shard_map/ppermute | solution.py:23
  132.0 12.4 %collective-permute-start.28 = (f32[248,128]{1,0:T(8,128)S(1)}, f32[248,128]{1,0:T(8,128)S(1)}, u32[]{:S(2)}, u32[]{:S(2)}) collective-permute-start(f32[248,128]{1,0:T(8,128)S(1)} %get-tuple-element.63), channel_id=1, source_target_pairs={{0,4},{4,8},{8,12},{12,0},{1,5},{5,9},{9,13},{13,1},{2,6},{6,10},{... | collective-permute-start | bytes 380936 | tf_op jit(solution)/shard_map/ppermute | solution.py:23
  133.9 14.9 %collective-permute-start.29 = (f32[248,128]{1,0:T(8,128)S(1)}, f32[248,128]{1,0:T(8,128)S(1)}, u32[]{:S(2)}, u32[]{:S(2)}) collective-permute-start(f32[248,128]{1,0:T(8,128)S(1)} %get-tuple-element.64), channel_id=1, source_target_pairs={{0,8},{4,12},{8,0},{12,4},{1,9},{5,13},{9,1},{13,5},{2,10},{6,14},... | collective-permute-start | bytes 380936 | tf_op jit(solution)/shard_map/ppermute | solution.py:23
  133.9 15.4 %collective-permute-start.30 = (f32[248,128]{1,0:T(8,128)S(1)}, f32[248,128]{1,0:T(8,128)S(1)}, u32[]{:S(2)}, u32[]{:S(2)}) collective-permute-start(f32[248,128]{1,0:T(8,128)S(1)} %get-tuple-element.65), channel_id=1, source_target_pairs={{0,12},{4,0},{8,4},{12,8},{1,13},{5,1},{9,5},{13,9},{2,14},{6,2},{... | collective-permute-start | bytes 380936 | tf_op jit(solution)/shard_map/ppermute | solution.py:23
  (17 other events, 145.7 us)

commit v7 on v6

--- a/solution.py
+++ b/solution.py
@@ -130,13 +130,15 @@
     return place
 
 
-def pack_kernel(unused, seq_count, own_down, far_down, own_up, far_up, tokens, *refs):
-    refs = refs[unused:]
-    payloads, columns = refs[:seq_count], refs[seq_count : 2 * seq_count]
-    down, up = refs[2 * seq_count :]
+def pack_kernel(own_down, far_down, own_up, far_up, before, after, *refs):
+    plane, forward, payloads, (down, up) = refs[0], refs[1], refs[2:-2], refs[-2:]
     ahead = lax.axis_index("batch") == 0
     joint_rank, held = own_down.shape[1:]
     low_width, held_up = own_up.shape[1:]
+    frozen_rows = before.shape[0]
+    plane[:frozen_rows] = before[...]
+    plane[frozen_rows:] = after[...]
+    forward[:frozen_rows] = before[...]
     for document in range(SEGS):
         rows = slice(document * joint_rank, (document + 1) * joint_rank)
         down[rows, :held] = jnp.where(ahead, own_down[document], far_down[document])
@@ -144,21 +146,29 @@
         up[document, :, :held_up] = jnp.where(ahead, own_up[document], far_up[document])
         up[document, :, held_up:] = jnp.where(ahead, far_up[document], own_up[document])
     half, slot = low_width // 2, down.shape[1] // 4
-    for steps in range(seq_count):
+    targets = [(0, payloads[0], 0), (1, forward, frozen_rows)]
+    targets += [(steps + 2, payload, 0) for steps, payload in enumerate(payloads[1:])]
+    seq_count = len(targets)
+    for steps, payload, base in targets:
         target = ring_index(lax.axis_index("seq") + steps - seq_count, seq_count)
         first = (target >= seq_count // 2).astype(jnp.int32)
         start = pl.multiple_of(first * joint_rank, joint_rank)
-        payload = payloads[steps]
-        payload[: 2 * joint_rank] = down[pl.ds(start, 2 * joint_rank)]
+        payload[base : base + 2 * joint_rank] = down[pl.ds(start, 2 * joint_rank)]
+        base = base + 2 * joint_rank
         for index in range(2):
             block = up[first + index]
             for part in range(2):
                 column = (2 * index + part) * slot
-                payload[2 * joint_rank :, column : column + 2 * held_up] = block[
+                payload[base : base + half, column : column + 2 * held_up] = block[
                     part * half : (part + 1) * half
                 ]
-        width = columns[steps].shape[1]
-        columns[steps][...] = tokens[:, pl.ds(pl.multiple_of(target * width, 128), width)]
+
+
+def cut_kernel(unused, seq_count, tokens, *refs):
+    for steps, block in enumerate(refs[unused:]):
+        target = ring_index(lax.axis_index("seq") + steps - seq_count, seq_count)
+        width = block.shape[1]
+        block[...] = tokens[:, pl.ds(pl.multiple_of(target * width, 128), width)]
 
 
 def assemble_up(seq_count, arrived, up_blocks):
@@ -187,37 +197,29 @@
                     ]
 
 
-def project_kernel(frozen_places, down_places, unused, seq_count, tokens, *refs):
-    frozen_count, down_count = len(frozen_places), len(down_places)
-    frozen_pieces = refs[:frozen_count]
-    down_pieces = refs[frozen_count : frozen_count + down_count]
-    refs = refs[frozen_count + down_count + unused :]
-    packed = down_count > 1
+def project_kernel(array_count, entries, up_entries, unused, seq_count, tokens, *refs):
+    arrays = refs[:array_count]
+    refs = refs[array_count + unused :]
     part, matrix = refs[:2]
     weights, semaphore = refs[-2:]
-    features = part.shape[1] - 2 * ADAPTER_RANK * 2
     copies = []
-    for piece, place in zip(frozen_pieces, frozen_places):
+    for number, start, height, place in entries:
+        piece = arrays[number].at[pl.ds(start, height)]
         copies.append(fetch(piece, weights, place, semaphore.at[len(copies)]))
-    joint_rank = 2 * ADAPTER_RANK
-    for number, (piece, place) in enumerate(zip(down_pieces, down_places)):
-        rows = piece.at[pl.ds(0, 2 * joint_rank)] if packed else piece
-        copies.append(fetch(rows, weights, place, semaphore.at[len(copies)]))
-        if packed:
-            extra = piece.shape[0] - 2 * joint_rank
-            copy = pltpu.make_async_copy(
-                piece.at[pl.ds(2 * joint_rank, extra)],
-                refs[3].at[number],
-                semaphore.at[len(copies)],
-            )
-            copy.start()
-            copies.append(copy)
+    for number, start, slot in up_entries:
+        copy = pltpu.make_async_copy(
+            arrays[number].at[pl.ds(start, refs[3].shape[1])],
+            refs[3].at[slot],
+            semaphore.at[len(copies)],
+        )
+        copy.start()
+        copies.append(copy)
     for copy in copies:
         copy.wait()
     keep = pltpu.make_async_copy(weights, matrix, semaphore.at[len(copies)])
     keep.start()
     part[...] = dot_nt(tokens[...], weights[...])
-    if packed:
+    if up_entries:
         assemble_up(seq_count, refs[3], refs[2])
     keep.wait()
 
@@ -226,7 +228,8 @@
     return values * cosines + pltpu.roll(values, values.shape[1] // 2, 1) * sines
 
 
-def qkv_kernel(seq_count, lengths, mine, theirs, up_blocks, cosines, sines, queries, pairs, low_rank):
+def qkv_kernel(seq_count, unused, lengths, mine, theirs, up_blocks, cosines, sines, *refs):
+    queries, pairs, low_rank = refs[unused:]
     rows = mine.shape[0]
     own_rows = queries.shape[0] // QHEADS
     query_columns = QHEADS * HEAD_WIDTH
@@ -577,10 +580,11 @@
 
     plane_count = group_count * batch_count
     share = width // plane_count
-    pieces, places = [], []
     padded_down = (held_down + 127) // 128 * 128
     direct = (
         group_count == 2
+        and seq_count == 4
+        and share == down_width
         and batch_count == 2
         and share % 128 == 0
         and down_width % 128 == 0
@@ -590,66 +594,83 @@
         and 128 % (up_width - 128) == 0
         and 0 < held_up + held_down - padded_down <= padded_down - held_down
     )
+    up_entries = []
     if direct:
         own_share = lax.dynamic_slice_in_dim(
             frozen_qkv_matrix, (group_index * batch_count + batch_index) * share, share, axis=1
         )
-        pieces.append(frozen_qkv_matrix)
-        places.append(frozen_place(seq_count, frozen_rows, None, 0, 0, 0))
         before = shift(own_share, "seq", 1)
-        after = shift(own_share, "seq", seq_count - 1)
-        arrivals = [(1, before), (seq_count - 1, after)]
-        for steps in range(2, seq_count - 1):
-            before = shift(before, "seq", 1)
-            arrivals.append((steps, before))
-        for steps, here in arrivals:
-            over_batch = shift(here, "batch", 1)
-            over_groups = shift(here, "groups", 1)
-            over_both = lax.ppermute(
-                here, ("groups", "batch"), [(at, plane_count - 1 - at) for at in range(plane_count)]
-            )
-            for value, batch_step, group_step in (
-                (here, 0, 0),
-                (over_batch, 1, 0),
-                (over_groups, 0, 1),
-                (over_both, 1, 1),
-            ):
-                pieces.append(value)
-                places.append(
-                    frozen_place(seq_count, frozen_rows, share, steps, batch_step, group_step)
-                )
-    else:
-        pieces.append(lax.all_gather(frozen_qkv_matrix, "seq", axis=0, tiled=True))
-        places.append(whole_place(0))
-
-    column_blocks, up_blocks = None, None
-    if direct:
+        after = shift(own_share, "seq", 3)
         far_down = shift(down_bank[far_bank], "batch", 1)
         far_up = shift(adapter_up_weight[far_bank], "batch", 1)
         own_down, own_up = down_bank[own_bank], adapter_up_weight[own_bank]
-        early = [before, down_zeros, up_zeros, cosines, sines, bank_rows]
         payload_rows = 2 * joint_rank + low_width // 2
-        packed = pl.pallas_call(
-            functools.partial(pack_kernel, len(early), seq_count),
-            out_shape=[jax.ShapeDtypeStruct((payload_rows, down_width), bf16)] * seq_count
-            + [jax.ShapeDtypeStruct((rows, down_width), bf16)] * seq_count,
-            in_specs=[in_vmem()] * 5 + [in_place()] * len(early),
-            out_specs=[by_block((payload_rows, down_width))] * seq_count
-            + [by_block((rows, down_width))] * seq_count,
+        pack_shapes = [(2 * frozen_rows, share), (frozen_rows + payload_rows, share)]
+        pack_shapes += [(payload_rows, share)] * 3
+        plane, forward, payload, *payloads = pl.pallas_call(
+            pack_kernel,
+            out_shape=[jax.ShapeDtypeStruct(shape, bf16) for shape in pack_shapes],
+            in_specs=[in_vmem()] * 6,
+            out_specs=[by_block(shape) for shape in pack_shapes],
             scratch_shapes=[
                 pltpu.VMEM((SEGS * joint_rank, down_width), bf16),
                 pltpu.VMEM((SEGS, low_width, 2 * held_up), bf16),
             ],
             compiler_params=pltpu.CompilerParams(vmem_limit_bytes=16 * mebibyte),
+            cost_estimate=cost(0, 8 * frozen_rows * share),
+            name="pack",
+        )(own_down, far_down, own_up, far_up, before, after)
+
+        def over_plane(value):
+            over_both = [(at, plane_count - 1 - at) for at in range(plane_count)]
+            return [
+                shift(value, "batch", 1),
+                shift(value, "groups", 1),
+                lax.ppermute(value, ("groups", "batch"), over_both),
+            ]
+
+        plane_parts = over_plane(plane)
+        forward = shift(forward, "seq", 1)
+        middle = forward[:frozen_rows]
+        middle_parts = over_plane(middle)
+        payloads = [shift(part, "seq", steps + 2) for steps, part in enumerate(payloads)]
+        arrays = [frozen_qkv_matrix, before, after, forward, payload] + payloads
+        arrays += plane_parts + middle_parts
+
+        def frozen_at(behind, batch_step, group_step):
+            return frozen_place(seq_count, frozen_rows, share, behind, batch_step, group_step)
+
+        def down_at(behind):
+            return down_place(seq_count, features, down_width, behind)
+
+        entries = [
+            (0, 0, frozen_rows, frozen_place(seq_count, frozen_rows, None, 0, 0, 0)),
+            (1, 0, frozen_rows, frozen_at(1, 0, 0)),
+            (2, 0, frozen_rows, frozen_at(3, 0, 0)),
+            (3, 0, frozen_rows, frozen_at(2, 0, 0)),
+            (4, 0, 2 * joint_rank, down_at(0)),
+            (3, frozen_rows, 2 * joint_rank, down_at(1)),
+            (5, 0, 2 * joint_rank, down_at(2)),
+            (6, 0, 2 * joint_rank, down_at(3)),
+        ]
+        up_entries = [(4, 2 * joint_rank, 0), (3, frozen_rows + 2 * joint_rank, 1)]
+        up_entries += [(5, 2 * joint_rank, 2), (6, 2 * joint_rank, 3)]
+        for number, (batch_step, group_step) in enumerate(((1, 0), (0, 1), (1, 1))):
+            entries += [
+                (7 + number, 0, frozen_rows, frozen_at(1, batch_step, group_step)),
+                (7 + number, frozen_rows, frozen_rows, frozen_at(3, batch_step, group_step)),
+                (10 + number, 0, frozen_rows, frozen_at(2, batch_step, group_step)),
+            ]
+        early = [forward, down_zeros, up_zeros, cosines, sines, bank_rows]
+        column_blocks = pl.pallas_call(
+            functools.partial(cut_kernel, len(early), seq_count),
+            out_shape=[jax.ShapeDtypeStruct((rows, down_width), bf16)] * seq_count,
+            in_specs=[in_vmem()] + [in_place()] * len(early),
+            out_specs=[by_block((rows, down_width))] * seq_count,
+            compiler_params=pltpu.CompilerParams(vmem_limit_bytes=16 * mebibyte),
             cost_estimate=cost(0, 4 * rows * width),
-            name="pack",
-        )(own_down, far_down, own_up, far_up, local_tokens, *early)
-        column_blocks = packed[seq_count:]
-        down_parts = [
-            shift(part, "seq", steps) if steps else part
-            for steps, part in enumerate(packed[:seq_count])
-        ]
-        down_places = [down_place(seq_count, features, down_width, steps) for steps in range(seq_count)]
+            name="cut",
+        )(local_tokens, *early)
     else:
         bank_rows = sample_rows.reshape(-1)
         got_down = lax.all_to_all(
@@ -664,8 +685,14 @@
         all_up = lax.all_gather(up_block, "seq", axis=0)
         first = (seq_index >= half_count).astype(jnp.int32)
         merged = jnp.transpose(all_down, (1, 0, 2)).reshape(SEGS * joint_rank, -1)
-        down_parts = [lax.dynamic_slice_in_dim(merged, first * joint_rank, 2 * joint_rank)]
-        down_places = [whole_place(features)]
+        arrays = [
+            lax.all_gather(frozen_qkv_matrix, "seq", axis=0, tiled=True),
+            lax.dynamic_slice_in_dim(merged, first * joint_rank, 2 * joint_rank),
+        ]
+        entries = [
+            (0, 0, features, whole_place(0)),
+            (1, 0, 2 * joint_rank, whole_place(features)),
+        ]
         up_rows = jnp.transpose(all_up, (1, 0, 2)).reshape(SEGS, low_width, -1)
         is_query = jnp.arange(up_rows.shape[2]) < query_columns
         up_blocks = jnp.concatenate(
@@ -694,45 +721,47 @@
     matrix_rows = features + 2 * joint_rank
     arrived = [pltpu.VMEM((seq_count, low_width // 2, down_width), bf16)] if direct else []
     part, matrix, *built = pl.pallas_call(
-        functools.partial(project_kernel, places, down_places, len(early), seq_count),
+        functools.partial(
+            project_kernel, len(arrays), entries, up_entries, len(early), seq_count
+        ),
         out_shape=[
             jax.ShapeDtypeStruct((rows, matrix_rows), f32),
             jax.ShapeDtypeStruct((matrix_rows, width), bf16),
         ]
         + ([jax.ShapeDtypeStruct(up_shape, bf16)] if direct else []),
-        in_specs=[in_vmem()] + [in_place()] * (len(pieces) + len(down_parts) + len(early)),
+        in_specs=[in_vmem()] + [in_place()] * (len(arrays) + len(early)),
         out_specs=[in_vmem(), in_place()] + ([by_block(up_shape)] if direct else []),
         scratch_shapes=arrived
         + [
             pltpu.VMEM((matrix_rows, width), bf16),
-            pltpu.SemaphoreType.DMA((len(pieces) + 2 * len(down_parts) + 1,)),
+            pltpu.SemaphoreType.DMA((len(entries) + len(up_entries) + 1,)),
         ],
         compiler_params=pltpu.CompilerParams(vmem_limit_bytes=20 * mebibyte),
         cost_estimate=cost(2 * rows * width * matrix_rows, 2 * width * (matrix_rows + rows)),
         name="project",
-    )(local_tokens, *pieces, *down_parts, *early)
+    )(local_tokens, *arrays, *early)
     if direct:
         up_blocks = built[0]
 
     other_part = shift(part, "tp", 1)
     queries, pairs, low_rank = pl.pallas_call(
-        functools.partial(qkv_kernel, seq_count),
+        functools.partial(qkv_kernel, seq_count, 1),
         out_shape=(
             jax.ShapeDtypeStruct((QHEADS * own_rows, HEAD_WIDTH), bf16),
             jax.ShapeDtypeStruct((rows, 2 * HEAD_WIDTH), bf16),
             jax.ShapeDtypeStruct((rows, joint_rank), bf16),
         ),
-        in_specs=[in_smem()] + [in_vmem()] * 5,
+        in_specs=[in_smem()] + [in_vmem()] * 5 + [in_place()],
         out_specs=(in_vmem(),) * 3,
         compiler_params=pltpu.CompilerParams(vmem_limit_bytes=8 * mebibyte),
         cost_estimate=cost(2 * rows * 3 * 64 * 640, 8 * rows * features),
         name="qkv",
-    )(document_lengths, part, other_part, up_blocks, cosines, sines)
+    )(document_lengths, part, other_part, up_blocks, cosines, sines, column_parts[1])
 
     blocks = [pairs] + [push(pairs, "seq", back) for back in range(1, half_count + 1)]
     block_count = len(blocks)
     incoming = output_gradient[0]
-    early_columns = [column_parts[1]]
+    early_columns = []
     attention, query_grad, kept, sent = pl.pallas_call(
         functools.partial(attention_kernel, block_count, len(early_columns)),
         out_shape=(

time: 166 us -> 163 us (0.982)
  starting transfers between devices: 44 us -> 40.1 us
    ppermute x25 -> x22, waiting for transfers between devices: 60.6 us -> 52.1 us  [shift(): lax.ppermute(value, axis, [(at, (at + steps) % count) for at in range(cou...]
    ppermute x3 -> x2, waiting for transfers between devices: 0.01 us -> 6.78 us  [over_plane(): lax.ppermute(value, ('groups', 'batch'), over_both)]
    ppermute x25 -> x22, starting transfers between devices: 31.6 us -> 28.6 us  [shift(): lax.ppermute(value, axis, [(at, (at + steps) % count) for at in range(cou...]
    ppermute x4, starting transfers between devices: 8.39 us -> 6.52 us  [push(): return lax.ppermute(value, axis, pairs)]
    pallas_call x3 -> x4, Pallas kernels: 5.24 us -> 6.33 us  [the longest x1 3.77 us: shards(): pl.pallas_call(functools.partial(project_kernel, len(arrays), entries, up...]
    ppermute x3 -> x2, starting transfers between devices: 4.04 us -> 4.96 us  [over_plane(): lax.ppermute(value, ('groups', 'batch'), over_both)]
  transfers between devices with their start and end apart: 32 -> 28, of which waited for: 17 -> 20; matrix products, arithmetic and copies ran while one was open for 10% -> 10% of each run, Pallas kernels for 5% -> 4%
where the time goes in v7:
time: 163 us; the launch traced here: 161 us
  waiting for transfers between devices  75.8 us (47%)
  starting transfers between devices  40.1 us (25%)
  Pallas kernels  21 us (13%)
  local copies, waits for them, and re-layouts  19 us (12%)
  other arithmetic  2.42 us (1%)
  between operations  2.2 us (1%)
    ppermute x22, waiting for transfers between devices, shift(): lax.ppermute(value, axis, [(at, (at + steps) % count) for at in range(cou...  52.1 us
    ppermute x22, starting transfers between devices, shift(): lax.ppermute(value, axis, [(at, (at + steps) % count) for at in range(cou...  28.6 us
    ppermute x4, waiting for transfers between devices, push(): return lax.ppermute(value, axis, pairs)  16.9 us
    ppermute x2, waiting for transfers between devices, over_plane(): lax.ppermute(value, ('groups', 'batch'), over_both)  6.78 us
    ppermute x4, starting transfers between devices, push(): return lax.ppermute(value, axis, pairs)  6.52 us
    unnamed x19, local copies, waits for them, and re-layouts  5.42 us
    ppermute x2, starting transfers between devices, over_plane(): lax.ppermute(value, ('groups', 'batch'), over_both)  4.96 us
    pallas_call x1, Pallas kernels, shards(): pl.pallas_call(token_kernel, grid=(width // chunk,), out_shape=jax.ShapeD...  4.84 us
  transfers between devices with their start and end apart: 28, of which 20 were waited for; matrix products, arithmetic and copies ran while one was open for 10% of the time, Pallas kernels for 4%

profile of v7, /device:TPU:0, one launch (start us, length us, event | category | flops | bytes accessed | tf_op | source)
XLA Modules:
  0.0 160.5 jit_solution(16656428845583118788)
XLA Ops:
  1.7 5.1 %collective-permute-start.1 = (bf16[192,896]{1,0:T(8,128)(2,1)S(1)}, bf16[192,896]{1,0:T(8,128)(2,1)S(1)}, u32[]{:S(2)}, u32[]{:S(2)}) collective-permute-start(bf16[192,896]{1,0:T(8,128)(2,1)S(1)} %constant_dynamic-slice_fusion.1), channel_id=1, source_target_pairs={{0,12},{4,0},{8,4},{12,8},{1,13},{5,1},{9,5},{13,9},{2,14},{6,2},{... | collective-permute-start | bytes 1032200 | tf_op jit(solution)/shard_map/ppermute | solution.py:23
  8.7 2.7 %gather_fusion.1 = bf16[3,64,448]{2,1,0:T(8,128)(2,1)S(1)} fusion(bf16[64,64,448]{2,1,0:T(8,128)(2,1)} %bitcast.19, s32[1024]{0:T(1024)S(1)} %pad_clamp_fusion), kind=kCustom, calls=%fused_computation.1 | custom fusion | bytes 344076 | tf_op jit(solution)/shard_map/gather | solution.py:604
  14.7 2.7 %gather_fusion = bf16[3,64,448]{2,1,0:T(8,128)(2,1)S(1)} fusion(bf16[64,64,448]{2,1,0:T(8,128)(2,1)} %bitcast.20, s32[1024]{0:T(1024)S(1)} %pad_clamp_fusion.1), kind=kCustom, calls=%fused_computation | custom fusion | bytes 344076 | tf_op jit(solution)/shard_map/gather | solution.py:606
  18.4 4.0 %collective-permute-done.before.refs_1_ = bf16[192,896]{1,0:T(8,128)(2,1)S(1)} collective-permute-done((bf16[192,896]{1,0:T(8,128)(2,1)S(1)}, bf16[192,896]{1,0:T(8,128)(2,1)S(1)}, u32[]{:S(2)}, u32[]{:S(2)}) %collective-permute-start) | collective-permute-done | bytes 344096 | tf_op jit(solution)/shard_map/ppermute | solution.py:23
  28.0 2.4 %collective-permute-start.9 = (bf16[384,896]{1,0:T(8,128)(2,1)}, bf16[384,896]{1,0:T(8,128)(2,1)S(1)}, u32[]{:S(2)}, u32[]{:S(2)}) collective-permute-start(bf16[384,896]{1,0:T(8,128)(2,1)} %get-tuple-element.43), channel_id=1, source_target_pairs={{0,18},{2,16},{16,2},{18,0},{1,19},{3,17},{17,3},{19,1},{4,22},{6,... | collective-permute-start | bytes 2064392 | tf_op jit(solution)/shard_map/ppermute | solution.py:629
  34.3 9.5 %collective-permute-done.4.refs_0_.refs_3_ = bf16[336,896]{1,0:T(8,128)(2,1)S(1)} collective-permute-done((bf16[336,896]{1,0:T(8,128)(2,1)}, bf16[336,896]{1,0:T(8,128)(2,1)S(1)}, u32[]{:S(2)}, u32[]{:S(2)}) %collective-permute-start.4) | collective-permute-done | bytes 602144 | tf_op jit(solution)/shard_map/ppermute | solution.py:23
  44.6 4.5 %broadcast_in_dim.47.refs_1_.down_zeros = f32[64,64,1,448]{3,2,1,0:T(1,128)S(1)} broadcast(f32[]{:T(128)} %constant.11.clone.1), dimensions={} | broadcast | bytes 7340036 | tf_op jit(solution)/shard_map/broadcast_in_dim | solution.py:578
  49.3 3.2 %copy-done.1 = f32[64,64,1,448]{3,2,1,0:T(1,128)} copy-done((f32[64,64,1,448]{3,2,1,0:T(1,128)}, f32[64,64,1,448]{3,2,1,0:T(1,128)S(1)}, u32[]{:S(2)}) %copy-start.1) | copy-done | bytes 7340056
  52.8 10.0 %collective-permute-start.13 = (bf16[256,896]{1,0:T(8,128)(2,1)S(1)}, bf16[256,896]{1,0:T(8,128)(2,1)S(1)}, u32[]{:S(2)}, u32[]{:S(2)}) collective-permute-start(bf16[256,896]{1,0:T(8,128)(2,1)S(1)} %get-tuple-element.44), channel_id=1, source_target_pairs={{0,8},{4,12},{8,0},{12,4},{1,9},{5,13},{9,1},{13,5},{2,10},{6,14},... | collective-permute-start | bytes 1376264 | tf_op jit(solution)/shard_map/ppermute | solution.py:23
  62.8 2.5 %collective-permute-start.12 = (bf16[192,896]{1,0:T(8,128)(2,1)S(1)}, bf16[192,896]{1,0:T(8,128)(2,1)S(1)}, u32[]{:S(2)}, u32[]{:S(2)}) collective-permute-start(bf16[192,896]{1,0:T(8,128)(2,1)S(1)} %slice.32), channel_id=1, source_target_pairs={{0,18},{2,16},{16,2},{18,0},{1,19},{3,17},{17,3},{19,1},{4,22},{6,... | collective-permute-start | bytes 1032200 | tf_op jit(solution)/shard_map/ppermute | solution.py:629
  66.3 6.8 %collective-permute-done.12.refs_12_ = bf16[192,896]{1,0:T(8,128)(2,1)S(1)} collective-permute-done((bf16[192,896]{1,0:T(8,128)(2,1)S(1)}, bf16[192,896]{1,0:T(8,128)(2,1)S(1)}, u32[]{:S(2)}, u32[]{:S(2)}) %collective-permute-start.12) | collective-permute-done | bytes 344096 | tf_op jit(solution)/shard_map/ppermute | solution.py:629
  73.1 2.4 %collective-permute-done.11.refs_11_ = bf16[192,896]{1,0:T(8,128)(2,1)S(1)} collective-permute-done((bf16[192,896]{1,0:T(8,128)(2,1)S(1)}, bf16[192,896]{1,0:T(8,128)(2,1)S(1)}, u32[]{:S(2)}, u32[]{:S(2)}) %collective-permute-start.11) | collective-permute-done | bytes 344096 | tf_op jit(solution)/shard_map/ppermute | solution.py:23
  75.8 2.3 %collective-permute-done.13.refs_13_.refs_2_ = bf16[256,896]{1,0:T(8,128)(2,1)S(1)} collective-permute-done((bf16[256,896]{1,0:T(8,128)(2,1)S(1)}, bf16[256,896]{1,0:T(8,128)(2,1)S(1)}, u32[]{:S(2)}, u32[]{:S(2)}) %collective-permute-start.13) | collective-permute-done | bytes 458784 | tf_op jit(solution)/shard_map/ppermute | solution.py:23
  78.2 3.8 %project.1 = (f32[256,896]{1,0:T(8,128)S(1)}, bf16[896,3584]{1,0:T(8,128)(2,1)S(1)}, bf16[3,64,640]{2,1,0:T(8,128)(2,1)S(1)}) custom-call(bf16[256,3584]{1,0:T(8,128)(2,1)S(1)} %bitcast.16, bf16[192,3584]{1,0:T(8,128)(2,1)S(1)} %copy-done.4, bf16[192,896]{1,0:T(8,128)(2,1)S(1)} %collective-permute-done.before.refs_1_, ...), custom_call_target="tpu_custom_call" | custom-call | flops 1644167168 | bytes 8257536 | tf_op jit(solution)/shard_map/project/pallas_call | solution.py:723
  82.3 14.5 %collective-permute-done.15.refs_0_.refs_1_ = bf16[256,896]{1,0:T(8,128)(2,1)S(1)} collective-permute-done((bf16[256,896]{1,0:T(8,128)(2,1)S(1)}, bf16[256,896]{1,0:T(8,128)(2,1)S(1)}, u32[]{:S(2)}, u32[]{:S(2)}) %collective-permute-start.15) | collective-permute-done | bytes 458784 | tf_op jit(solution)/shard_map/ppermute | solution.py:23
  99.2 2.6 %collective-permute-start.16 = (bf16[256,256]{1,0:T(8,128)(2,1)S(1)}, bf16[256,256]{1,0:T(8,128)(2,1)S(1)}, u32[]{:S(2)}, u32[]{:S(2)}) collective-permute-start(bf16[256,256]{1,0:T(8,128)(2,1)S(1)} %get-tuple-element.49.refs_0_), channel_id=1, source_target_pairs={{0,4},{4,8},{8,12},{1,5},{5,9},{9,13},{2,6},{6,10},{10,14},{3,7},{... | collective-permute-start | bytes 393224 | tf_op jit(solution)/shard_map/ppermute | solution.py:29
  104.9 3.4 %attention.1 = (bf16[128,512]{1,0:T(8,128)(2,1)}, bf16[128,512]{1,0:T(8,128)(2,1)S(1)}, f32[3,128,256]{2,1,0:T(8,128)S(1)}, f32[3,128,256]{2,1,0:T(8,128)S(1)}) custom-call(s32[2,3]{1,0:T(2,128)S(1)} %copy-done.5, bf16[512,128]{1,0:T(8,128)(2,1)S(1)} %get-tuple-element.48.queries, bf16[128,512]{1,0:T(8,128)(2,1)S(1)} %bitcast.17, ...), custom_call_target="tpu_custom_call" | custom-call | flops 503316480 | bytes 786432 | tf_op jit(solution)/shard_map/attention/pallas_call | solution.py:765
  112.7 6.3 %collective-permute-done.20.refs_1_ = f32[128,256]{1,0:T(8,128)S(1)} collective-permute-done((f32[128,256]{1,0:T(8,128)S(1)}, f32[128,256]{1,0:T(8,128)S(1)}, u32[]{:S(2)}, u32[]{:S(2)}) %collective-permute-start.20) | collective-permute-done | bytes 131104 | tf_op jit(solution)/shard_map/ppermute | solution.py:29
  119.0 7.5 %collective-permute-done.21.refs_2_ = f32[128,256]{1,0:T(8,128)S(1)} collective-permute-done((f32[128,256]{1,0:T(8,128)S(1)}, f32[128,256]{1,0:T(8,128)S(1)}, u32[]{:S(2)}, u32[]{:S(2)}) %collective-permute-start.21) | collective-permute-done | bytes 131104 | tf_op jit(solution)/shard_map/ppermute | solution.py:29
  131.5 2.4 %collective-permute-start.26 = (f32[248,128]{1,0:T(8,128)S(1)}, f32[248,128]{1,0:T(8,128)S(1)}, u32[]{:S(2)}, u32[]{:S(2)}) collective-permute-start(f32[248,128]{1,0:T(8,128)S(1)} %get-tuple-element.67), channel_id=1, source_target_pairs={{0,12},{4,0},{8,4},{12,8},{1,13},{5,1},{9,5},{13,9},{2,14},{6,2},{... | collective-permute-start | bytes 380936 | tf_op jit(solution)/shard_map/ppermute | solution.py:23
  133.9 7.9 %collective-permute-done.24.refs_5_ = f32[248,128]{1,0:T(8,128)S(1)} collective-permute-done((f32[248,128]{1,0:T(8,128)S(1)}, f32[248,128]{1,0:T(8,128)S(1)}, u32[]{:S(2)}, u32[]{:S(2)}) %collective-permute-start.24) | collective-permute-done | bytes 127008 | tf_op jit(solution)/shard_map/ppermute | solution.py:23
  141.9 4.6 %collective-permute-done.25.refs_6_ = f32[248,128]{1,0:T(8,128)S(1)} collective-permute-done((f32[248,128]{1,0:T(8,128)S(1)}, f32[248,128]{1,0:T(8,128)S(1)}, u32[]{:S(2)}, u32[]{:S(2)}) %collective-permute-start.25) | collective-permute-done | bytes 127008 | tf_op jit(solution)/shard_map/ppermute | solution.py:23
  150.3 4.8 %token_gradient.1 = bf16[256,3584]{1,0:T(8,128)(2,1)} custom-call(bf16[256,896]{1,0:T(8,128)(2,1)S(1)} %get-tuple-element.60.gradients, bf16[896,3584]{1,0:T(8,128)(2,1)S(1)} %get-tuple-element.61.matrix), custom_call_target="tpu_custom_call" | custom-call | flops 1644167168 | bytes 8257536 | tf_op jit(solution)/shard_map/token_gradient/pallas_call | solution.py:848
  157.5 3.0 %bank_rows.1 = (f32[64,64,1,448]{3,2,1,0:T(1,128)}, f32[64,32,80]{2,1,0:T(8,128)}) custom-call(s32[6]{0:T(128)S(1)} %pad_add_fusion.refs_5_.bank_rows, f32[192,448]{1,0:T(8,128)S(1)} %get-tuple-element.69.own_down, f32[192,512]{1,0:T(8,128)S(1)} %collective-permute-done.27.far, ...), custom_call_target="tpu_custom_call", output_to_operand_aliasing={{0}: (4, {}), {1}: (5, {})} | custom-call | tf_op jit(solution)/shard_map/bank_rows/pallas_call | solution.py:900
  (82 shorter events, 39.1 us)
Async XLA Ops:
  1.7 16.7 %collective-permute-start.1 = (bf16[192,896]{1,0:T(8,128)(2,1)S(1)}, bf16[192,896]{1,0:T(8,128)(2,1)S(1)}, u32[]{:S(2)}, u32[]{:S(2)}) collective-permute-start(bf16[192,896]{1,0:T(8,128)(2,1)S(1)} %constant_dynamic-slice_fusion.1), channel_id=1, source_target_pairs={{0,12},{4,0},{8,4},{12,8},{1,13},{5,1},{9,5},{13,9},{2,14},{6,2},{... | collective-permute-start | bytes 1032200 | tf_op jit(solution)/shard_map/ppermute | solution.py:23
  6.8 15.6 %collective-permute-start = (bf16[192,896]{1,0:T(8,128)(2,1)S(1)}, bf16[192,896]{1,0:T(8,128)(2,1)S(1)}, u32[]{:S(2)}, u32[]{:S(2)}) collective-permute-start(bf16[192,896]{1,0:T(8,128)(2,1)S(1)} %constant_dynamic-slice_fusion.1), channel_id=1, source_target_pairs={{0,4},{4,8},{8,12},{12,0},{1,5},{5,9},{9,13},{13,1},{2,6},{6,10},{... | collective-permute-start | bytes 1032200 | tf_op jit(solution)/shard_map/ppermute | solution.py:23
  11.4 7.0 %collective-permute-start.2 = (bf16[3,64,448]{2,1,0:T(8,128)(2,1)S(1)}, bf16[3,64,448]{2,1,0:T(8,128)(2,1)S(1)}, u32[]{:S(2)}, u32[]{:S(2)}) collective-permute-start(bf16[3,64,448]{2,1,0:T(8,128)(2,1)S(1)} %gather_fusion.1), channel_id=1, source_target_pairs={{0,2},{2,0},{1,3},{3,1},{4,6},{6,4},{5,7},{7,5},{8,10},{10,8},{9,1... | collective-permute-start | bytes 516104 | tf_op jit(solution)/shard_map/ppermute | solution.py:23
  25.1 18.6 %collective-permute-start.4 = (bf16[336,896]{1,0:T(8,128)(2,1)}, bf16[336,896]{1,0:T(8,128)(2,1)S(1)}, u32[]{:S(2)}, u32[]{:S(2)}) collective-permute-start(bf16[336,896]{1,0:T(8,128)(2,1)} %get-tuple-element.39), channel_id=1, source_target_pairs={{0,4},{4,8},{8,12},{12,0},{1,5},{5,9},{9,13},{13,1},{2,6},{6,10},{... | collective-permute-start | bytes 1806344 | tf_op jit(solution)/shard_map/ppermute | solution.py:23
  28.0 37.3 %collective-permute-start.9 = (bf16[384,896]{1,0:T(8,128)(2,1)}, bf16[384,896]{1,0:T(8,128)(2,1)S(1)}, u32[]{:S(2)}, u32[]{:S(2)}) collective-permute-start(bf16[384,896]{1,0:T(8,128)(2,1)} %get-tuple-element.43), channel_id=1, source_target_pairs={{0,18},{2,16},{16,2},{18,0},{1,19},{3,17},{17,3},{19,1},{4,22},{6,... | collective-permute-start | bytes 2064392 | tf_op jit(solution)/shard_map/ppermute | solution.py:629
  30.5 35.3 %collective-permute-start.8 = (bf16[384,896]{1,0:T(8,128)(2,1)}, bf16[384,896]{1,0:T(8,128)(2,1)S(1)}, u32[]{:S(2)}, u32[]{:S(2)}) collective-permute-start(bf16[384,896]{1,0:T(8,128)(2,1)} %get-tuple-element.43), channel_id=1, source_target_pairs={{0,16},{16,0},{1,17},{17,1},{2,18},{18,2},{3,19},{19,3},{4,20},{20... | collective-permute-start | bytes 2064392 | tf_op jit(solution)/shard_map/ppermute | solution.py:23
  33.0 33.3 %collective-permute-start.7 = (bf16[384,896]{1,0:T(8,128)(2,1)}, bf16[384,896]{1,0:T(8,128)(2,1)S(1)}, u32[]{:S(2)}, u32[]{:S(2)}) collective-permute-start(bf16[384,896]{1,0:T(8,128)(2,1)} %get-tuple-element.43), channel_id=1, source_target_pairs={{0,2},{2,0},{1,3},{3,1},{4,6},{6,4},{5,7},{7,5},{8,10},{10,8},{9,1... | collective-permute-start | bytes 2064392 | tf_op jit(solution)/shard_map/ppermute | solution.py:23
  33.6 19.1 %collective-permute-start.5 = (bf16[144,896]{1,0:T(8,128)(2,1)}, bf16[144,896]{1,0:T(8,128)(2,1)S(1)}, u32[]{:S(2)}, u32[]{:S(2)}) collective-permute-start(bf16[144,896]{1,0:T(8,128)(2,1)} %copy-done.7), channel_id=1, source_target_pairs={{0,8},{4,12},{8,0},{12,4},{1,9},{5,13},{9,1},{13,5},{2,10},{6,14},... | collective-permute-start | bytes 774152 | tf_op jit(solution)/shard_map/ppermute | solution.py:23
  43.8 19.0 %collective-permute-start.6 = (bf16[144,896]{1,0:T(8,128)(2,1)}, bf16[144,896]{1,0:T(8,128)(2,1)S(1)}, u32[]{:S(2)}, u32[]{:S(2)}) collective-permute-start(bf16[144,896]{1,0:T(8,128)(2,1)} %copy-done.6), channel_id=1, source_target_pairs={{0,12},{4,0},{8,4},{12,8},{1,13},{5,1},{9,5},{13,9},{2,14},{6,2},{... | collective-permute-start | bytes 774152 | tf_op jit(solution)/shard_map/ppermute | solution.py:23
  52.8 25.4 %collective-permute-start.13 = (bf16[256,896]{1,0:T(8,128)(2,1)S(1)}, bf16[256,896]{1,0:T(8,128)(2,1)S(1)}, u32[]{:S(2)}, u32[]{:S(2)}) collective-permute-start(bf16[256,896]{1,0:T(8,128)(2,1)S(1)} %get-tuple-element.44), channel_id=1, source_target_pairs={{0,8},{4,12},{8,0},{12,4},{1,9},{5,13},{9,1},{13,5},{2,10},{6,14},... | collective-permute-start | bytes 1376264 | tf_op jit(solution)/shard_map/ppermute | solution.py:23
  62.8 10.3 %collective-permute-start.12 = (bf16[192,896]{1,0:T(8,128)(2,1)S(1)}, bf16[192,896]{1,0:T(8,128)(2,1)S(1)}, u32[]{:S(2)}, u32[]{:S(2)}) collective-permute-start(bf16[192,896]{1,0:T(8,128)(2,1)S(1)} %slice.32), channel_id=1, source_target_pairs={{0,18},{2,16},{16,2},{18,0},{1,19},{3,17},{17,3},{19,1},{4,22},{6,... | collective-permute-start | bytes 1032200 | tf_op jit(solution)/shard_map/ppermute | solution.py:629
  65.3 10.2 %collective-permute-start.11 = (bf16[192,896]{1,0:T(8,128)(2,1)S(1)}, bf16[192,896]{1,0:T(8,128)(2,1)S(1)}, u32[]{:S(2)}, u32[]{:S(2)}) collective-permute-start(bf16[192,896]{1,0:T(8,128)(2,1)S(1)} %slice.32), channel_id=1, source_target_pairs={{0,16},{16,0},{1,17},{17,1},{2,18},{18,2},{3,19},{19,3},{4,20},{20... | collective-permute-start | bytes 1032200 | tf_op jit(solution)/shard_map/ppermute | solution.py:23
  65.8 10.0 %collective-permute-start.10 = (bf16[192,896]{1,0:T(8,128)(2,1)S(1)}, bf16[192,896]{1,0:T(8,128)(2,1)S(1)}, u32[]{:S(2)}, u32[]{:S(2)}) collective-permute-start(bf16[192,896]{1,0:T(8,128)(2,1)S(1)} %slice.32), channel_id=1, source_target_pairs={{0,2},{2,0},{1,3},{3,1},{4,6},{6,4},{5,7},{7,5},{8,10},{10,8},{9,1... | collective-permute-start | bytes 1032200 | tf_op jit(solution)/shard_map/ppermute | solution.py:23
  82.0 14.8 %collective-permute-start.14 = (f32[256,896]{1,0:T(8,128)S(1)}, f32[256,896]{1,0:T(8,128)S(1)}, u32[]{:S(2)}, u32[]{:S(2)}) collective-permute-start(f32[256,896]{1,0:T(8,128)S(1)} %get-tuple-element.45.mine), channel_id=1, source_target_pairs={{0,1},{1,0},{2,3},{3,2},{4,5},{5,4},{6,7},{7,6},{8,9},{9,8},{10,11... | collective-permute-start | bytes 2752520 | tf_op jit(solution)/shard_map/ppermute | solution.py:23
  82.1 14.7 %collective-permute-start.15 = (bf16[256,896]{1,0:T(8,128)(2,1)S(1)}, bf16[256,896]{1,0:T(8,128)(2,1)S(1)}, u32[]{:S(2)}, u32[]{:S(2)}) collective-permute-start(bf16[256,896]{1,0:T(8,128)(2,1)S(1)} %get-tuple-element.47), channel_id=1, source_target_pairs={{0,4},{4,8},{8,12},{12,0},{1,5},{5,9},{9,13},{13,1},{2,6},{6,10},{... | collective-permute-start | bytes 1376264 | tf_op jit(solution)/shard_map/ppermute | solution.py:23
  97.9 4.9 %collective-permute-start.17 = (bf16[256,256]{1,0:T(8,128)(2,1)S(1)}, bf16[256,256]{1,0:T(8,128)(2,1)S(1)}, u32[]{:S(2)}, u32[]{:S(2)}) collective-permute-start(bf16[256,256]{1,0:T(8,128)(2,1)S(1)} %get-tuple-element.49.refs_0_), channel_id=1, source_target_pairs={{0,8},{4,12},{1,9},{5,13},{2,10},{6,14},{3,11},{7,15},{16,24},{20,... | collective-permute-start | bytes 393224 | tf_op jit(solution)/shard_map/ppermute | solution.py:29
  99.2 5.7 %collective-permute-start.16 = (bf16[256,256]{1,0:T(8,128)(2,1)S(1)}, bf16[256,256]{1,0:T(8,128)(2,1)S(1)}, u32[]{:S(2)}, u32[]{:S(2)}) collective-permute-start(bf16[256,256]{1,0:T(8,128)(2,1)S(1)} %get-tuple-element.49.refs_0_), channel_id=1, source_target_pairs={{0,4},{4,8},{8,12},{1,5},{5,9},{9,13},{2,6},{6,10},{10,14},{3,7},{... | collective-permute-start | bytes 393224 | tf_op jit(solution)/shard_map/ppermute | solution.py:29
  110.1 8.9 %collective-permute-start.20 = (f32[128,256]{1,0:T(8,128)S(1)}, f32[128,256]{1,0:T(8,128)S(1)}, u32[]{:S(2)}, u32[]{:S(2)}) collective-permute-start(f32[128,256]{1,0:T(8,128)S(1)} %get-tuple-element.55), channel_id=1, source_target_pairs={{4,0},{8,4},{12,8},{5,1},{9,5},{13,9},{6,2},{10,6},{14,10},{7,3},{... | collective-permute-start | bytes 393224 | tf_op jit(solution)/shard_map/ppermute | solution.py:29
  111.4 15.1 %collective-permute-start.21 = (f32[128,256]{1,0:T(8,128)S(1)}, f32[128,256]{1,0:T(8,128)S(1)}, u32[]{:S(2)}, u32[]{:S(2)}) collective-permute-start(f32[128,256]{1,0:T(8,128)S(1)} %get-tuple-element.56), channel_id=1, source_target_pairs={{8,0},{12,4},{9,1},{13,5},{10,2},{14,6},{11,3},{15,7},{24,16},{28,... | collective-permute-start | bytes 393224 | tf_op jit(solution)/shard_map/ppermute | solution.py:29
  126.6 20.3 %collective-permute-start.23 = (bf16[256,896]{1,0:T(8,128)(2,1)S(1)}, bf16[256,896]{1,0:T(8,128)(2,1)S(1)}, u32[]{:S(2)}, u32[]{:S(2)}) collective-permute-start(bf16[256,896]{1,0:T(8,128)(2,1)S(1)} %get-tuple-element.63), channel_id=1, source_target_pairs={{0,12},{4,0},{8,4},{12,8},{1,13},{5,1},{9,5},{13,9},{2,14},{6,2},{... | collective-permute-start | bytes 1376264 | tf_op jit(solution)/shard_map/ppermute | solution.py:23
  129.5 12.4 %collective-permute-start.24 = (f32[248,128]{1,0:T(8,128)S(1)}, f32[248,128]{1,0:T(8,128)S(1)}, u32[]{:S(2)}, u32[]{:S(2)}) collective-permute-start(f32[248,128]{1,0:T(8,128)S(1)} %get-tuple-element.65), channel_id=1, source_target_pairs={{0,4},{4,8},{8,12},{12,0},{1,5},{5,9},{9,13},{13,1},{2,6},{6,10},{... | collective-permute-start | bytes 380936 | tf_op jit(solution)/shard_map/ppermute | solution.py:23
  131.5 14.9 %collective-permute-start.25 = (f32[248,128]{1,0:T(8,128)S(1)}, f32[248,128]{1,0:T(8,128)S(1)}, u32[]{:S(2)}, u32[]{:S(2)}) collective-permute-start(f32[248,128]{1,0:T(8,128)S(1)} %get-tuple-element.66), channel_id=1, source_target_pairs={{0,8},{4,12},{8,0},{12,4},{1,9},{5,13},{9,1},{13,5},{2,10},{6,14},... | collective-permute-start | bytes 380936 | tf_op jit(solution)/shard_map/ppermute | solution.py:23
  131.5 15.4 %collective-permute-start.26 = (f32[248,128]{1,0:T(8,128)S(1)}, f32[248,128]{1,0:T(8,128)S(1)}, u32[]{:S(2)}, u32[]{:S(2)}) collective-permute-start(f32[248,128]{1,0:T(8,128)S(1)} %get-tuple-element.67), channel_id=1, source_target_pairs={{0,12},{4,0},{8,4},{12,8},{1,13},{5,1},{9,5},{13,9},{2,14},{6,2},{... | collective-permute-start | bytes 380936 | tf_op jit(solution)/shard_map/ppermute | solution.py:23
  148.7 8.7 %collective-permute-start.27 = (f32[192,512]{1,0:T(8,128)S(1)}, f32[192,512]{1,0:T(8,128)S(1)}, u32[]{:S(2)}, u32[]{:S(2)}) collective-permute-start(f32[192,512]{1,0:T(8,128)S(1)} %get-tuple-element.70), channel_id=1, source_target_pairs={{0,2},{2,0},{1,3},{3,1},{4,6},{6,4},{5,7},{7,5},{8,10},{10,8},{9,1... | collective-permute-start | bytes 1179656 | tf_op jit(solution)/shard_map/ppermute | solution.py:23
  (13 other events, 110.0 us)

commit v8 on v7

--- a/solution.py
+++ b/solution.py
@@ -130,45 +130,82 @@
     return place
 
 
-def pack_kernel(own_down, far_down, own_up, far_up, before, after, *refs):
-    plane, forward, payloads, (down, up) = refs[0], refs[1], refs[2:-2], refs[-2:]
+def join_kernel(before, after, plane):
+    rows = before.shape[0]
+    plane[:rows] = before[...]
+    plane[rows:] = after[...]
+
+
+def pass_kernel(*refs):
+    del refs
+
+
+def block_kernel(own_down, far_down, down):
     ahead = lax.axis_index("batch") == 0
     joint_rank, held = own_down.shape[1:]
-    low_width, held_up = own_up.shape[1:]
-    frozen_rows = before.shape[0]
-    plane[:frozen_rows] = before[...]
-    plane[frozen_rows:] = after[...]
-    forward[:frozen_rows] = before[...]
     for document in range(SEGS):
         rows = slice(document * joint_rank, (document + 1) * joint_rank)
         down[rows, :held] = jnp.where(ahead, own_down[document], far_down[document])
         down[rows, held:] = jnp.where(ahead, far_down[document], own_down[document])
+
+
+def target_of(steps, seq_count):
+    target = ring_index(lax.axis_index("seq") + steps - seq_count, seq_count)
+    return target, (target >= seq_count // 2).astype(jnp.int32)
+
+
+def pack_kernel(unused, down, *refs):
+    payloads = refs[unused:]
+    joint_rank = down.shape[0] // SEGS
+    for steps, payload in enumerate(payloads):
+        target, first = target_of(steps, len(payloads))
+        start = pl.multiple_of(first * joint_rank, joint_rank)
+        payload[...] = down[pl.ds(start, 2 * joint_rank)]
+
+
+def cut_kernel(unused, tokens, own_up, far_up, *refs):
+    blocks, up = refs[unused:-1], refs[-1]
+    ahead = lax.axis_index("batch") == 0
+    low_width, held_up = own_up.shape[1:]
+    for document in range(SEGS):
         up[document, :, :held_up] = jnp.where(ahead, own_up[document], far_up[document])
         up[document, :, held_up:] = jnp.where(ahead, far_up[document], own_up[document])
-    half, slot = low_width // 2, down.shape[1] // 4
-    targets = [(0, payloads[0], 0), (1, forward, frozen_rows)]
-    targets += [(steps + 2, payload, 0) for steps, payload in enumerate(payloads[1:])]
-    seq_count = len(targets)
-    for steps, payload, base in targets:
-        target = ring_index(lax.axis_index("seq") + steps - seq_count, seq_count)
-        first = (target >= seq_count // 2).astype(jnp.int32)
-        start = pl.multiple_of(first * joint_rank, joint_rank)
-        payload[base : base + 2 * joint_rank] = down[pl.ds(start, 2 * joint_rank)]
-        base = base + 2 * joint_rank
+    rows = tokens.shape[0]
+    half = low_width // 2
+    for steps, block in enumerate(blocks):
+        target, first = target_of(steps, len(blocks))
+        width = block.shape[1]
+        block[:rows] = tokens[:, pl.ds(pl.multiple_of(target * width, 128), width)]
+        slot = width // 4
         for index in range(2):
-            block = up[first + index]
+            rows_up = up[first + index]
             for part in range(2):
                 column = (2 * index + part) * slot
-                payload[base : base + half, column : column + 2 * held_up] = block[
+                block[rows:, column : column + 2 * held_up] = rows_up[
                     part * half : (part + 1) * half
                 ]
 
 
-def cut_kernel(unused, seq_count, tokens, *refs):
-    for steps, block in enumerate(refs[unused:]):
-        target = ring_index(lax.axis_index("seq") + steps - seq_count, seq_count)
-        width = block.shape[1]
-        block[...] = tokens[:, pl.ds(pl.multiple_of(target * width, 128), width)]
+def low_kernel(seq_count, lengths, down, *refs):
+    columns, (own, *sends) = refs[:seq_count], refs[seq_count:]
+    joint_rank = down.shape[0] // SEGS
+    rows = own.shape[0]
+    ends = kernel_marks(lengths)
+    for behind in range(seq_count):
+        holder = ring_index(lax.axis_index("seq") - behind, seq_count)
+        first = (holder >= seq_count // 2).astype(jnp.int32)
+        second = row_segments(ends, row_positions(holder * rows, rows)) != first
+        start = pl.multiple_of(first * joint_rank, joint_rank)
+        values = columns[behind][:rows]
+        first_low = dot_nt(values, down[pl.ds(start, joint_rank)])
+        start = pl.multiple_of(start + joint_rank, joint_rank)
+        second_low = dot_nt(values, down[pl.ds(start, joint_rank)])
+        low = jnp.where(second, second_low, first_low)
+        if behind == 0:
+            own[...] = low
+        else:
+            sends[behind - 1][:, :joint_rank] = low[: rows // 2]
+            sends[behind - 1][:, joint_rank:] = low[rows // 2 :]
 
 
 def assemble_up(seq_count, arrived, up_blocks):
@@ -197,15 +234,15 @@
                     ]
 
 
-def project_kernel(array_count, entries, up_entries, unused, seq_count, tokens, *refs):
-    arrays = refs[:array_count]
-    refs = refs[array_count + unused :]
+def project_kernel(array_count, entries, up_entries, low_count, seq_count, tokens, *refs):
+    arrays, lows = refs[:array_count], refs[array_count : array_count + low_count]
+    refs = refs[array_count + low_count :]
     part, matrix = refs[:2]
-    weights, semaphore = refs[-2:]
+    frozen, semaphore = refs[-2:]
     copies = []
     for number, start, height, place in entries:
         piece = arrays[number].at[pl.ds(start, height)]
-        copies.append(fetch(piece, weights, place, semaphore.at[len(copies)]))
+        copies.append(fetch(piece, frozen, place, semaphore.at[len(copies)]))
     for number, start, slot in up_entries:
         copy = pltpu.make_async_copy(
             arrays[number].at[pl.ds(start, refs[3].shape[1])],
@@ -216,9 +253,19 @@
         copies.append(copy)
     for copy in copies:
         copy.wait()
-    keep = pltpu.make_async_copy(weights, matrix, semaphore.at[len(copies)])
+    keep = pltpu.make_async_copy(frozen, matrix, semaphore.at[len(copies)])
     keep.start()
-    part[...] = dot_nt(tokens[...], weights[...])
+    features, rows = frozen.shape[0], tokens.shape[0]
+    part[:, :features] = dot_nt(tokens[...], frozen[...])
+    joint_rank = 2 * ADAPTER_RANK
+    middle = features + joint_rank
+    total = lows[0][...]
+    if low_count > 1:
+        upper = sum(low[:, :joint_rank] for low in lows[1:])
+        lower = sum(low[:, joint_rank:] for low in lows[1:])
+        total = total + jnp.concatenate([upper, lower], axis=0)
+    part[:, features:middle] = total
+    part[:, middle:] = jnp.zeros_like(total)
     if up_entries:
         assemble_up(seq_count, refs[3], refs[2])
     keep.wait()
@@ -228,26 +275,18 @@
     return values * cosines + pltpu.roll(values, values.shape[1] // 2, 1) * sines
 
 
-def qkv_kernel(seq_count, unused, lengths, mine, theirs, up_blocks, cosines, sines, *refs):
+def qkv_kernel(unused, lengths, mine, theirs, up_blocks, cosines, sines, *refs):
     queries, pairs, low_rank = refs[unused:]
     rows = mine.shape[0]
     own_rows = queries.shape[0] // QHEADS
     query_columns = QHEADS * HEAD_WIDTH
     value_start = query_columns + HEAD_WIDTH
     features = value_start + HEAD_WIDTH
-    joint_rank = low_rank.shape[1]
-    middle = features + joint_rank
+    middle = features + low_rank.shape[1]
     ends = kernel_marks(lengths)
-
-    def low_rows(picked, second):
-        first_low = mine[picked, features:middle] + theirs[picked, features:middle]
-        second_low = mine[picked, middle:] + theirs[picked, middle:]
-        return jnp.where(second, second_low, first_low).astype(jnp.bfloat16)
-
-    first = (lax.axis_index("seq") >= seq_count // 2).astype(jnp.int32)
     first_row = lax.axis_index("seq") * rows
     segments = row_segments(ends, row_positions(first_row, rows))
-    low = low_rows(slice(None), segments != first)
+    low = (mine[:, features:middle] + theirs[:, features:middle]).astype(jnp.bfloat16)
     low_rank[...] = low
     value_delta = jnp.zeros((rows, HEAD_WIDTH), jnp.float32)
     for document in range(SEGS):
@@ -260,7 +299,7 @@
     start = pl.multiple_of(lax.axis_index("tp") * own_rows, own_rows)
     own = pl.ds(start, own_rows)
     own_segments = row_segments(ends, row_positions(first_row + start, own_rows))
-    own_low = low_rows(own, own_segments != first)
+    own_low = (mine[own, features:middle] + theirs[own, features:middle]).astype(jnp.bfloat16)
     query_delta = jnp.zeros((own_rows, query_columns), jnp.float32)
     for document in range(SEGS):
         chosen = jnp.where(own_segments == document, own_low, jnp.zeros_like(own_low))
@@ -340,7 +379,7 @@
 
 
 def pair_kernel(terms, cosines, sines, *refs):
-    parts, pair = refs[:terms], refs[-2]
+    parts, pair = refs[:terms], refs[-1]
     own_rows = pair.shape[0]
     total = sum(part[...] for part in parts)
     own = pl.ds(pl.multiple_of(lax.axis_index("tp") * own_rows, own_rows), own_rows)
@@ -352,8 +391,8 @@
 def rank_kernel(
     seq_count, lengths, own_query, other_query, own_pair, other_pair, low_rank, up_blocks, *refs
 ):
-    gradients, rank_grad = refs[:2]
-    split_terms, (terms, blocks) = refs[2:-2], refs[-2:]
+    gradients, rank_grad, packed_grad = refs[:3]
+    split_terms, (terms, blocks) = refs[3:-2], refs[-2:]
     own_rows, query_columns = own_query.shape
     rows = low_rank.shape[0]
     seq_index = lax.axis_index("seq")
@@ -384,6 +423,8 @@
         terms[place, query_columns:] = adapter_scale * value_terms[rank:]
     turned = (adapter_scale * total).astype(jnp.bfloat16)
     rank_grad[...] = turned
+    packed_grad[:, : low.shape[1]] = turned[: rows // 2]
+    packed_grad[:, low.shape[1] :] = turned[rows // 2 :]
     second = segments != (seq_index >= seq_count // 2).astype(jnp.int32)
     nothing = jnp.zeros_like(turned)
     middle = features + low.shape[1]
@@ -400,41 +441,42 @@
         tail = held - 128
         count = 128 // tail
         height = mine.shape[0] // count
-        first_low = mine.shape[0] + height
         block[: mine.shape[0]] = mine[:, :128]
         for part in range(count):
-            block[mine.shape[0] : first_low, part * tail : (part + 1) * tail] = mine[
+            block[mine.shape[0] :, part * tail : (part + 1) * tail] = mine[
                 part * height : (part + 1) * height, 128:
             ]
-        block[first_low:, : low.shape[1]] = turned[: rows // 2].astype(jnp.float32)
-        block[first_low:, low.shape[1] :] = turned[rows // 2 :].astype(jnp.float32)
-
-
-def token_kernel(gradients, matrix, token_grad):
-    token_grad[...] = dot_nn(gradients[...], matrix[...]).astype(jnp.bfloat16)
+
+
+def token_kernel(places, gradients, matrix, *refs):
+    weights, (token_grad, down, semaphore) = refs[:-3], refs[-3:]
+    step = pl.program_id(0)
+    width = token_grad.shape[1]
+
+    @pl.when(step == 0)
+    def load():
+        copies = [
+            fetch(piece, down, place, semaphore.at[number])
+            for number, (piece, place) in enumerate(zip(weights, places))
+        ]
+        for copy in copies:
+            copy.wait()
+
+    features = matrix.shape[0]
+    total = dot_nn(gradients[:, :features], matrix[...])
+    columns = pl.ds(pl.multiple_of(step * width, 128), width)
+    total += dot_nn(gradients[:, features:], down[:, columns])
+    token_grad[...] = total.astype(jnp.bfloat16)
 
 
 def down_kernel(block_count, lengths, *refs):
-    columns = refs[:block_count]
-    up_parts = refs[block_count : 2 * block_count]
-    packed = up_parts[0].shape != up_parts[1].shape
-    rank_count = 1 if packed else block_count
-    ranks = refs[2 * block_count : 2 * block_count + rank_count]
-    outputs = refs[2 * block_count + rank_count :]
+    columns, ranks = refs[:block_count], refs[block_count : 2 * block_count]
+    outputs = refs[2 * block_count :]
     rows, joint_rank = ranks[0].shape
     ends = kernel_marks(lengths)
-    up_rows, up_width = up_parts[0].shape
-    lows, ups = [ranks[0][...]], [up_parts[0][...]]
-    for behind in range(1, block_count):
-        if not packed:
-            lows.append(ranks[behind][...])
-            ups.append(up_parts[behind][...])
-            continue
-        part = up_parts[behind]
-        count = 128 // (up_width - 128)
-        first_low = up_rows + up_rows // count
-        halves = [part[first_low:, :joint_rank], part[first_low:, joint_rank:]]
-        lows.append(jnp.concatenate(halves, axis=0).astype(jnp.bfloat16))
+    lows = [ranks[0][...]]
+    for part in ranks[1:]:
+        lows.append(jnp.concatenate([part[:, :joint_rank], part[:, joint_rank:]], axis=0))
     all_terms = []
     for document in range(SEGS):
         total = jnp.zeros((joint_rank, columns[0].shape[1]), jnp.float32)
@@ -442,59 +484,58 @@
             holder = ring_index(lax.axis_index("seq") - behind, block_count)
             segments = row_segments(ends, row_positions(holder * rows, rows))
             chosen = jnp.where(segments == document, lows[behind], jnp.zeros_like(lows[behind]))
-            total += dot_tn(chosen, columns[behind][...])
+            total += dot_tn(chosen, columns[behind][:rows])
         all_terms.append(total)
     down_terms = jnp.concatenate(all_terms, axis=0)
-    if not packed:
+    if len(outputs) == 1:
         outputs[0][...] = down_terms
-        outputs[1][...] = sum(ups)
         return
-    own_down, far, own_up, up_terms = outputs
+    own_down, far_down = outputs
+    held = own_down.shape[1]
+    ahead = lax.axis_index("batch") == 0
+    own_down[...] = jnp.where(ahead, down_terms[:, :held], down_terms[:, held:])
+    far_down[...] = jnp.where(ahead, down_terms[:, held:], down_terms[:, :held])
+
+
+def up_kernel(block_count, *refs):
+    up_parts, outputs = refs[:block_count], refs[block_count:]
+    if len(outputs) == 1:
+        outputs[0][...] = sum(part[...] for part in up_parts)
+        return
+    own_up, far_up, up_terms = outputs
+    up_rows, up_width = up_terms.shape
     tail = up_width - 128
     height = up_rows // (128 // tail)
-    up_terms[...] = ups[0]
+    up_terms[...] = up_parts[0][...]
     for part in up_parts[1:]:
         up_terms[:, :128] += part[:up_rows]
         for piece in range(128 // tail):
             up_terms[piece * height : (piece + 1) * height, 128:] += part[
-                up_rows : up_rows + height, piece * tail : (piece + 1) * tail
+                up_rows:, piece * tail : (piece + 1) * tail
             ]
-    held, held_up = own_down.shape[1], own_up.shape[1]
+    held_up = own_up.shape[1]
     ahead = lax.axis_index("batch") == 0
-    own_down[...] = jnp.where(ahead, down_terms[:, :held], down_terms[:, held:])
-    far[:, :held] = jnp.where(ahead, down_terms[:, held:], down_terms[:, :held])
     left, right = up_terms[:, :held_up], up_terms[:, held_up:]
     own_up[...] = jnp.where(ahead, left, right)
-    far_up = jnp.where(ahead, right, left)
-    spare = far.shape[1] - held
-    far[:up_rows, held:] = far_up[:, :spare]
-    far[up_rows:, held : held + held_up - spare] = far_up[:, spare:]
-
-
-def packed_bank_kernel(bank_rows, own_down, far, own_up, down_zeros, up_zeros, down_out, up_out):
+    far_up[...] = jnp.where(ahead, right, left)
+
+
+def packed_bank_kernel(
+    bank_rows, own_down, far_down, own_up, far_up, down_zeros, up_zeros, down_out, up_out
+):
     step = pl.program_id(0)
-    joint_rank, held = down_out.shape[1], down_out.shape[3]
-    low_width, held_up = up_out.shape[1:]
-    up_rows = own_up.shape[0]
-    spare = far.shape[1] - held
-    down_total = jnp.zeros((joint_rank, held), jnp.float32)
-    head = jnp.zeros((low_width, spare), jnp.float32)
-    rest = jnp.zeros((low_width, held_up - spare), jnp.float32)
-    for document in range(SEGS):
-        rows = slice(document * joint_rank, (document + 1) * joint_rank)
-        lows = slice(document * low_width, (document + 1) * low_width)
-        same = bank_rows[document] == bank_rows[step]
-        down_total += jnp.where(same, own_down[rows], 0.0)
-        head += jnp.where(same, own_up[lows, :spare], 0.0)
-        rest += jnp.where(same, own_up[lows, spare:], 0.0)
-        same = bank_rows[SEGS + document] == bank_rows[step]
-        down_total += jnp.where(same, far[rows, :held], 0.0)
-        head += jnp.where(same, far[lows, held:], 0.0)
-        lows = slice(up_rows + document * low_width, up_rows + (document + 1) * low_width)
-        rest += jnp.where(same, far[lows, held : held + held_up - spare], 0.0)
+    joint_rank, low_width = down_out.shape[1], up_out.shape[1]
+    down_total = jnp.zeros((joint_rank, down_out.shape[3]), jnp.float32)
+    up_total = jnp.zeros((low_width, up_out.shape[2]), jnp.float32)
+    for block, (down, up) in enumerate(((own_down, own_up), (far_down, far_up))):
+        for document in range(SEGS):
+            same = bank_rows[block * SEGS + document] == bank_rows[step]
+            rows = slice(document * joint_rank, (document + 1) * joint_rank)
+            lows = slice(document * low_width, (document + 1) * low_width)
+            down_total += jnp.where(same, down[rows], 0.0)
+            up_total += jnp.where(same, up[lows], 0.0)
     down_out[0, :, 0, :] = down_total
-    up_out[0, :, :spare] = head
-    up_out[0, :, spare:] = rest
+    up_out[0] = up_total
 
 
 def bank_kernel(block_count, bank_rows, *refs):
@@ -604,22 +645,24 @@
         far_down = shift(down_bank[far_bank], "batch", 1)
         far_up = shift(adapter_up_weight[far_bank], "batch", 1)
         own_down, own_up = down_bank[own_bank], adapter_up_weight[own_bank]
-        payload_rows = 2 * joint_rank + low_width // 2
-        pack_shapes = [(2 * frozen_rows, share), (frozen_rows + payload_rows, share)]
-        pack_shapes += [(payload_rows, share)] * 3
-        plane, forward, payload, *payloads = pl.pallas_call(
-            pack_kernel,
-            out_shape=[jax.ShapeDtypeStruct(shape, bf16) for shape in pack_shapes],
-            in_specs=[in_vmem()] * 6,
-            out_specs=[by_block(shape) for shape in pack_shapes],
-            scratch_shapes=[
-                pltpu.VMEM((SEGS * joint_rank, down_width), bf16),
-                pltpu.VMEM((SEGS, low_width, 2 * held_up), bf16),
-            ],
-            compiler_params=pltpu.CompilerParams(vmem_limit_bytes=16 * mebibyte),
+        down_block = pl.pallas_call(
+            block_kernel,
+            out_shape=jax.ShapeDtypeStruct((SEGS * joint_rank, down_width), bf16),
+            in_specs=[in_vmem()] * 2,
+            out_specs=in_vmem(),
+            compiler_params=pltpu.CompilerParams(vmem_limit_bytes=8 * mebibyte),
+            cost_estimate=cost(0, 4 * SEGS * joint_rank * down_width),
+            name="down_block",
+        )(own_down, far_down)
+        plane = pl.pallas_call(
+            join_kernel,
+            out_shape=jax.ShapeDtypeStruct((2 * frozen_rows, share), bf16),
+            in_specs=[in_vmem()] * 2,
+            out_specs=in_vmem(),
+            compiler_params=pltpu.CompilerParams(vmem_limit_bytes=8 * mebibyte),
             cost_estimate=cost(0, 8 * frozen_rows * share),
-            name="pack",
-        )(own_down, far_down, own_up, far_up, before, after)
+            name="join",
+        )(before, after)
 
         def over_plane(value):
             over_both = [(at, plane_count - 1 - at) for at in range(plane_count)]
@@ -630,47 +673,66 @@
             ]
 
         plane_parts = over_plane(plane)
-        forward = shift(forward, "seq", 1)
-        middle = forward[:frozen_rows]
+        middle = pl.pallas_call(
+            pass_kernel,
+            out_shape=jax.ShapeDtypeStruct((frozen_rows, share), bf16),
+            in_specs=[in_place()] * 3,
+            out_specs=in_place(),
+            input_output_aliases={0: 0},
+            name="pass_middle",
+        )(shift(before, "seq", 1), down_zeros, up_zeros)
         middle_parts = over_plane(middle)
-        payloads = [shift(part, "seq", steps + 2) for steps, part in enumerate(payloads)]
-        arrays = [frozen_qkv_matrix, before, after, forward, payload] + payloads
-        arrays += plane_parts + middle_parts
+
+        early = [before, cosines, sines, bank_rows]
+        block_rows = rows + low_width // 2
+        column_blocks = pl.pallas_call(
+            functools.partial(cut_kernel, len(early)),
+            out_shape=[jax.ShapeDtypeStruct((block_rows, down_width), bf16)] * seq_count,
+            in_specs=[in_vmem()] * 3 + [in_place()] * len(early),
+            out_specs=[by_block((block_rows, down_width))] * seq_count,
+            scratch_shapes=[pltpu.VMEM((SEGS, low_width, 2 * held_up), bf16)],
+            compiler_params=pltpu.CompilerParams(vmem_limit_bytes=16 * mebibyte),
+            cost_estimate=cost(0, 4 * rows * width),
+            name="cut",
+        )(local_tokens, own_up, far_up, *early)
+        column_parts = [
+            shift(block, "seq", steps) if steps else block
+            for steps, block in enumerate(column_blocks)
+        ]
+        low_shapes = [(rows, joint_rank)] + [(rows // 2, 2 * joint_rank)] * (seq_count - 1)
+        lows = pl.pallas_call(
+            functools.partial(low_kernel, seq_count),
+            out_shape=[jax.ShapeDtypeStruct(shape, f32) for shape in low_shapes],
+            in_specs=[in_smem()] + [in_vmem()] * (1 + seq_count),
+            out_specs=[in_vmem()] * seq_count,
+            compiler_params=pltpu.CompilerParams(vmem_limit_bytes=8 * mebibyte),
+            cost_estimate=cost(
+                4 * seq_count * rows * joint_rank * down_width, 2 * seq_count * rows * down_width
+            ),
+            name="low",
+        )(document_lengths, down_block, *column_parts)
+        lows = [lows[0]] + [
+            shift(low, "seq", seq_count - 1 - steps) for steps, low in enumerate(lows[1:])
+        ]
+        arrays = [frozen_qkv_matrix, before, after, middle] + plane_parts + middle_parts
+        arrays += column_parts
 
         def frozen_at(behind, batch_step, group_step):
             return frozen_place(seq_count, frozen_rows, share, behind, batch_step, group_step)
-
-        def down_at(behind):
-            return down_place(seq_count, features, down_width, behind)
 
         entries = [
             (0, 0, frozen_rows, frozen_place(seq_count, frozen_rows, None, 0, 0, 0)),
             (1, 0, frozen_rows, frozen_at(1, 0, 0)),
             (2, 0, frozen_rows, frozen_at(3, 0, 0)),
             (3, 0, frozen_rows, frozen_at(2, 0, 0)),
-            (4, 0, 2 * joint_rank, down_at(0)),
-            (3, frozen_rows, 2 * joint_rank, down_at(1)),
-            (5, 0, 2 * joint_rank, down_at(2)),
-            (6, 0, 2 * joint_rank, down_at(3)),
         ]
-        up_entries = [(4, 2 * joint_rank, 0), (3, frozen_rows + 2 * joint_rank, 1)]
-        up_entries += [(5, 2 * joint_rank, 2), (6, 2 * joint_rank, 3)]
         for number, (batch_step, group_step) in enumerate(((1, 0), (0, 1), (1, 1))):
             entries += [
-                (7 + number, 0, frozen_rows, frozen_at(1, batch_step, group_step)),
-                (7 + number, frozen_rows, frozen_rows, frozen_at(3, batch_step, group_step)),
-                (10 + number, 0, frozen_rows, frozen_at(2, batch_step, group_step)),
+                (4 + number, 0, frozen_rows, frozen_at(1, batch_step, group_step)),
+                (4 + number, frozen_rows, frozen_rows, frozen_at(3, batch_step, group_step)),
+                (7 + number, 0, frozen_rows, frozen_at(2, batch_step, group_step)),
             ]
-        early = [forward, down_zeros, up_zeros, cosines, sines, bank_rows]
-        column_blocks = pl.pallas_call(
-            functools.partial(cut_kernel, len(early), seq_count),
-            out_shape=[jax.ShapeDtypeStruct((rows, down_width), bf16)] * seq_count,
-            in_specs=[in_vmem()] + [in_place()] * len(early),
-            out_specs=[by_block((rows, down_width))] * seq_count,
-            compiler_params=pltpu.CompilerParams(vmem_limit_bytes=16 * mebibyte),
-            cost_estimate=cost(0, 4 * rows * width),
-            name="cut",
-        )(local_tokens, *early)
+        up_entries = [(10 + behind, rows, behind) for behind in range(seq_count)]
     else:
         bank_rows = sample_rows.reshape(-1)
         got_down = lax.all_to_all(
@@ -685,14 +747,19 @@
         all_up = lax.all_gather(up_block, "seq", axis=0)
         first = (seq_index >= half_count).astype(jnp.int32)
         merged = jnp.transpose(all_down, (1, 0, 2)).reshape(SEGS * joint_rank, -1)
-        arrays = [
-            lax.all_gather(frozen_qkv_matrix, "seq", axis=0, tiled=True),
-            lax.dynamic_slice_in_dim(merged, first * joint_rank, 2 * joint_rank),
+        pair_rows = lax.dynamic_slice_in_dim(merged, first * joint_rank, 2 * joint_rank)
+        arrays = [lax.all_gather(frozen_qkv_matrix, "seq", axis=0, tiled=True)]
+        entries = [(0, 0, features, whole_place(0))]
+        both_lows = lax.dot_general(
+            local_tokens, pair_rows, (((1,), (1,)), ((), ())), preferred_element_type=f32
+        )
+        segments = (positions >= first_end).astype(jnp.int32) + (positions >= second_end)
+        lows = [
+            jnp.where(
+                (segments == first)[:, None], both_lows[:, :joint_rank], both_lows[:, joint_rank:]
+            )
         ]
-        entries = [
-            (0, 0, features, whole_place(0)),
-            (1, 0, 2 * joint_rank, whole_place(features)),
-        ]
+        weight_parts, weight_places = [pair_rows], [whole_place(0)]
         up_rows = jnp.transpose(all_up, (1, 0, 2)).reshape(SEGS, low_width, -1)
         is_query = jnp.arange(up_rows.shape[2]) < query_columns
         up_blocks = jnp.concatenate(
@@ -712,56 +779,69 @@
             for steps in range(seq_count)
         ]
 
-    column_parts = [
-        shift(block, "seq", steps) if steps else block
-        for steps, block in enumerate(column_blocks)
-    ]
-    early = [column_parts[2]] if direct and seq_count > 3 else []
+    if not direct:
+        column_parts = [
+            shift(block, "seq", steps) if steps else block
+            for steps, block in enumerate(column_blocks)
+        ]
     up_shape = (SEGS, joint_rank, query_columns + HEAD_WIDTH)
-    matrix_rows = features + 2 * joint_rank
+    part_width = features + 2 * joint_rank
     arrived = [pltpu.VMEM((seq_count, low_width // 2, down_width), bf16)] if direct else []
     part, matrix, *built = pl.pallas_call(
         functools.partial(
-            project_kernel, len(arrays), entries, up_entries, len(early), seq_count
+            project_kernel, len(arrays), entries, up_entries, len(lows), seq_count
         ),
         out_shape=[
-            jax.ShapeDtypeStruct((rows, matrix_rows), f32),
-            jax.ShapeDtypeStruct((matrix_rows, width), bf16),
+            jax.ShapeDtypeStruct((rows, part_width), f32),
+            jax.ShapeDtypeStruct((features, width), bf16),
         ]
         + ([jax.ShapeDtypeStruct(up_shape, bf16)] if direct else []),
-        in_specs=[in_vmem()] + [in_place()] * (len(arrays) + len(early)),
+        in_specs=[in_vmem()] + [in_place()] * len(arrays) + [in_vmem()] * len(lows),
         out_specs=[in_vmem(), in_place()] + ([by_block(up_shape)] if direct else []),
         scratch_shapes=arrived
         + [
-            pltpu.VMEM((matrix_rows, width), bf16),
+            pltpu.VMEM((features, width), bf16),
             pltpu.SemaphoreType.DMA((len(entries) + len(up_entries) + 1,)),
         ],
         compiler_params=pltpu.CompilerParams(vmem_limit_bytes=20 * mebibyte),
-        cost_estimate=cost(2 * rows * width * matrix_rows, 2 * width * (matrix_rows + rows)),
+        cost_estimate=cost(2 * rows * width * features, 2 * width * (features + rows)),
         name="project",
-    )(local_tokens, *arrays, *early)
+    )(local_tokens, *arrays, *lows)
     if direct:
         up_blocks = built[0]
+        payloads = pl.pallas_call(
+            functools.partial(pack_kernel, 1),
+            out_shape=[jax.ShapeDtypeStruct((2 * joint_rank, down_width), bf16)] * seq_count,
+            in_specs=[in_vmem()] + [in_place()],
+            out_specs=[by_block((2 * joint_rank, down_width))] * seq_count,
+            compiler_params=pltpu.CompilerParams(vmem_limit_bytes=8 * mebibyte),
+            cost_estimate=cost(0, 16 * joint_rank * down_width),
+            name="pack",
+        )(down_block, part)
+        weight_parts = [
+            shift(part, "seq", steps) if steps else part for steps, part in enumerate(payloads)
+        ]
+        weight_places = [down_place(seq_count, 0, down_width, steps) for steps in range(seq_count)]
 
     other_part = shift(part, "tp", 1)
     queries, pairs, low_rank = pl.pallas_call(
-        functools.partial(qkv_kernel, seq_count, 1),
+        functools.partial(qkv_kernel, 0),
         out_shape=(
             jax.ShapeDtypeStruct((QHEADS * own_rows, HEAD_WIDTH), bf16),
             jax.ShapeDtypeStruct((rows, 2 * HEAD_WIDTH), bf16),
             jax.ShapeDtypeStruct((rows, joint_rank), bf16),
         ),
-        in_specs=[in_smem()] + [in_vmem()] * 5 + [in_place()],
+        in_specs=[in_smem()] + [in_vmem()] * 5,
         out_specs=(in_vmem(),) * 3,
         compiler_params=pltpu.CompilerParams(vmem_limit_bytes=8 * mebibyte),
         cost_estimate=cost(2 * rows * 3 * 64 * 640, 8 * rows * features),
         name="qkv",
-    )(document_lengths, part, other_part, up_blocks, cosines, sines, column_parts[1])
+    )(document_lengths, part, other_part, up_blocks, cosines, sines)
 
     blocks = [pairs] + [push(pairs, "seq", back) for back in range(1, half_count + 1)]
     block_count = len(blocks)
     incoming = output_gradient[0]
-    early_columns = []
+    early_columns = [weight_parts[1], weight_parts[-1]] if direct else []
     attention, query_grad, kept, sent = pl.pallas_call(
         functools.partial(attention_kernel, block_count, len(early_columns)),
         out_shape=(
@@ -796,35 +876,31 @@
     )(kept, shift(sent, "tp", 1))
     pair_terms = [pair_sums[0]]
     pair_terms += [push(pair_sums[back], "seq", -back) for back in range(1, block_count)]
-    pair_grad, late_block = pl.pallas_call(
+    pair_grad = pl.pallas_call(
         functools.partial(pair_kernel, block_count),
-        out_shape=[
-            jax.ShapeDtypeStruct((own_rows, 2 * HEAD_WIDTH), bf16),
-            jax.ShapeDtypeStruct((rows, down_width), bf16),
-        ],
-        in_specs=[in_vmem()] * (2 + block_count) + [in_place()],
-        out_specs=[in_vmem(), in_place()],
-        input_output_aliases={2 + block_count: 1},
+        out_shape=jax.ShapeDtypeStruct((own_rows, 2 * HEAD_WIDTH), bf16),
+        in_specs=[in_vmem()] * (2 + block_count),
+        out_specs=in_vmem(),
         compiler_params=pltpu.CompilerParams(vmem_limit_bytes=8 * mebibyte),
         cost_estimate=cost(0, 12 * block_count * own_rows * 2 * HEAD_WIDTH),
         name="pair_gradients",
-    )(cosines, sines, *pair_terms, column_blocks[-1])
-    column_parts[-1] = shift(late_block, "seq", seq_count - 1)
+    )(cosines, sines, *pair_terms)
     other_pair = shift(pair_grad, "tp", 1)
 
     split_shapes = [(SEGS * low_width, up_width)] * seq_count
     if direct:
-        sent_rows = SEGS * low_width * up_width // 128 + rows // 2
+        sent_rows = SEGS * low_width * up_width // 128
         split_shapes[1:] = [(sent_rows, 128)] * (seq_count - 1)
-    gradients, rank_grad, *up_split = pl.pallas_call(
+    gradients, rank_grad, packed_grad, *up_split = pl.pallas_call(
         functools.partial(rank_kernel, seq_count),
         out_shape=[
-            jax.ShapeDtypeStruct((rows, matrix_rows), bf16),
+            jax.ShapeDtypeStruct((rows, part_width), bf16),
             jax.ShapeDtypeStruct((rows, joint_rank), bf16),
+            jax.ShapeDtypeStruct((rows // 2, 2 * joint_rank), bf16),
         ]
         + [jax.ShapeDtypeStruct(shape, f32) for shape in split_shapes],
         in_specs=[in_smem()] + [in_vmem()] * 6,
-        out_specs=[by_block((rows, matrix_rows)), in_vmem()]
+        out_specs=[by_block((rows, part_width)), in_vmem(), in_vmem()]
         + [by_block(shape) for shape in split_shapes],
         scratch_shapes=[
             pltpu.VMEM((SEGS * low_width, features - HEAD_WIDTH), f32),
@@ -838,53 +914,65 @@
     )
 
     rank_parts = [rank_grad]
-    if not direct:
-        rank_parts += [shift(rank_grad, "seq", steps) for steps in range(1, seq_count)]
+    rank_parts += [shift(packed_grad, "seq", steps) for steps in range(1, seq_count)]
     up_sums = [
         shift(block, "seq", steps) if steps else block for steps, block in enumerate(up_split)
     ]
 
     chunk = 512
     token_grad = pl.pallas_call(
-        token_kernel,
+        functools.partial(token_kernel, weight_places),
         grid=(width // chunk,),
         out_shape=jax.ShapeDtypeStruct((rows, width), bf16),
         in_specs=[
-            pl.BlockSpec((rows, matrix_rows), lambda step: (0, 0)),
-            pl.BlockSpec((matrix_rows, chunk), lambda step: (0, step)),
+            pl.BlockSpec((rows, part_width), lambda step: (0, 0)),
+            pl.BlockSpec((features, chunk), lambda step: (0, step)),
+        ]
+        + [in_place()] * len(weight_parts),
+        out_specs=pl.BlockSpec((rows, chunk), lambda step: (0, step)),
+        scratch_shapes=[
+            pltpu.VMEM((2 * joint_rank, width), bf16),
+            pltpu.SemaphoreType.DMA((len(weight_parts),)),
         ],
-        out_specs=pl.BlockSpec((rows, chunk), lambda step: (0, step)),
         compiler_params=pltpu.CompilerParams(vmem_limit_bytes=12 * mebibyte),
-        cost_estimate=cost(2 * rows * width * matrix_rows, 2 * width * (matrix_rows + rows)),
+        cost_estimate=cost(2 * rows * width * part_width, 2 * width * (part_width + rows)),
         name="token_gradient",
-    )(gradients, matrix)
-
-    if direct:
-        term_shapes = [(SEGS * joint_rank, held_down), (SEGS * joint_rank, padded_down)]
-        term_shapes += [(SEGS * low_width, held_up)]
-    else:
-        term_shapes = [(SEGS * joint_rank, down_width), (SEGS * low_width, up_width)]
+    )(gradients, matrix, *weight_parts)
+
+    term_shapes = [(SEGS * joint_rank, held_down)] * 2
+    up_shapes = [(SEGS * low_width, held_up)] * 2
+    if not direct:
+        term_shapes = [(SEGS * joint_rank, down_width)]
+        up_shapes = [(SEGS * low_width, up_width)]
     terms = pl.pallas_call(
         functools.partial(down_kernel, seq_count),
         out_shape=[jax.ShapeDtypeStruct(shape, f32) for shape in term_shapes],
-        in_specs=[in_smem()] + [in_vmem()] * (2 * seq_count + len(rank_parts)),
+        in_specs=[in_smem()] + [in_vmem()] * (2 * seq_count),
         out_specs=[in_vmem()] * len(term_shapes),
-        scratch_shapes=[pltpu.VMEM((SEGS * low_width, up_width), f32)] if direct else [],
         compiler_params=pltpu.CompilerParams(vmem_limit_bytes=8 * mebibyte),
         cost_estimate=cost(
             2 * seq_count * rows * SEGS * joint_rank * down_width, 2 * seq_count * rows * down_width
         ),
         name="down_terms",
-    )(document_lengths, *column_parts, *up_sums, *rank_parts)
+    )(document_lengths, *column_parts, *rank_parts)
+    ups = pl.pallas_call(
+        functools.partial(up_kernel, seq_count),
+        out_shape=[jax.ShapeDtypeStruct(shape, f32) for shape in up_shapes],
+        in_specs=[in_vmem()] * seq_count,
+        out_specs=[in_vmem()] * len(up_shapes),
+        scratch_shapes=[pltpu.VMEM((SEGS * low_width, up_width), f32)] if direct else [],
+        compiler_params=pltpu.CompilerParams(vmem_limit_bytes=8 * mebibyte),
+        name="up_terms",
+    )(*up_sums)
 
     if direct:
-        bank_terms = [terms[0], shift(terms[1], "batch", 1), terms[2]]
+        bank_terms = [terms[0], shift(terms[1], "batch", 1), ups[0], shift(ups[1], "batch", 1)]
     else:
         down_send = jnp.transpose(
             terms[0].reshape(SEGS * joint_rank, batch_count, held_down), (1, 0, 2)
         )
         up_send = jnp.transpose(
-            terms[1].reshape(SEGS * low_width, batch_count, held_up), (1, 0, 2)
+            ups[0].reshape(SEGS * low_width, batch_count, held_up), (1, 0, 2)
         )
         back_down = lax.all_to_all(down_send, "batch", split_axis=0, concat_axis=0, tiled=True)
         back_up = lax.all_to_all(up_send, "batch", split_axis=0, concat_axis=0, tiled=True)

time: 163 us -> 195 us (1.20)
  starting transfers between devices: 40.1 us -> 62.1 us
  local copies, waits for them, and re-layouts: 19 us -> 27.4 us
  Pallas kernels: 21 us -> 25.4 us
    ppermute x22 -> x30, starting transfers between devices: 28.6 us -> 49.1 us  [shift(): lax.ppermute(value, axis, [(at, (at + steps) % count) for at in range(cou...]
    unnamed x19 -> x53, local copies, waits for them, and re-layouts: 5.42 us -> 12 us
    ppermute x22 -> x30, waiting for transfers between devices: 52.1 us -> 48.2 us  [shift(): lax.ppermute(value, axis, [(at, (at + steps) % count) for at in range(cou...]
    pallas_call x5 -> x10, Pallas kernels: 7.49 us -> 11 us  [the longest x1 4.9 us: shards(): pl.pallas_call(functools.partial(token_kernel, weight_places), grid=(widt...]
  transfers between devices with their start and end apart: 28 -> 36, of which waited for: 20 -> 17; matrix products, arithmetic and copies ran while one was open for 10% -> 9% of each run, Pallas kernels for 4% -> 7%
where the time goes in v8:
time: 195 us; the launch traced here: 194 us
  waiting for transfers between devices  74.5 us (38%)
  starting transfers between devices  62.1 us (32%)
  local copies, waits for them, and re-layouts  27.4 us (14%)
  Pallas kernels  25.4 us (13%)
  other arithmetic  2.42 us (1%)
  between operations  2.3 us (1%)
    ppermute x30, starting transfers between devices, shift(): lax.ppermute(value, axis, [(at, (at + steps) % count) for at in range(cou...  49.1 us
    ppermute x30, waiting for transfers between devices, shift(): lax.ppermute(value, axis, [(at, (at + steps) % count) for at in range(cou...  48.2 us
    ppermute x4, waiting for transfers between devices, push(): return lax.ppermute(value, axis, pairs)  18.1 us
    unnamed x53, local copies, waits for them, and re-layouts  12 us
    ppermute x2, waiting for transfers between devices, over_plane(): lax.ppermute(value, ('groups', 'batch'), over_both)  8.14 us
    ppermute x4, starting transfers between devices, push(): return lax.ppermute(value, axis, pairs)  8.02 us
    broadcast_in_dim x1, local copies, waits for them, and re-layouts, shards(): down_zeros = jnp.zeros((adapters, joint_rank, 1, held_down), f32)  5.42 us
    ppermute x2, starting transfers between devices, over_plane(): lax.ppermute(value, ('groups', 'batch'), over_both)  4.96 us
  transfers between devices with their start and end apart: 36, of which 17 were waited for; matrix products, arithmetic and copies ran while one was open for 9% of the time, Pallas kernels for 7%

profile of v8, /device:TPU:0, one launch (start us, length us, event | category | flops | bytes accessed | tf_op | source)
XLA Modules:
  0.0 194.1 jit_solution(213820335818777222)
XLA Ops:
  1.7 5.1 %collective-permute-start.1 = (bf16[192,896]{1,0:T(8,128)(2,1)S(1)}, bf16[192,896]{1,0:T(8,128)(2,1)S(1)}, u32[]{:S(2)}, u32[]{:S(2)}) collective-permute-start(bf16[192,896]{1,0:T(8,128)(2,1)S(1)} %constant_dynamic-slice_fusion.1), channel_id=1, source_target_pairs={{0,12},{4,0},{8,4},{12,8},{1,13},{5,1},{9,5},{13,9},{2,14},{6,2},{... | collective-permute-start | bytes 1032200 | tf_op jit(solution)/shard_map/ppermute | solution.py:23
  15.3 7.1 %collective-permute-done.before.refs_0_.refs_1_ = bf16[192,896]{1,0:T(8,128)(2,1)S(1)} collective-permute-done((bf16[192,896]{1,0:T(8,128)(2,1)S(1)}, bf16[192,896]{1,0:T(8,128)(2,1)S(1)}, u32[]{:S(2)}, u32[]{:S(2)}) %collective-permute-start) | collective-permute-done | bytes 344096 | tf_op jit(solution)/shard_map/ppermute | solution.py:23
  28.6 2.4 %collective-permute-start.5 = (bf16[384,896]{1,0:T(8,128)(2,1)}, bf16[384,896]{1,0:T(8,128)(2,1)}, u32[]{:S(2)}, u32[]{:S(2)}) collective-permute-start(bf16[384,896]{1,0:T(8,128)(2,1)} %join.1), channel_id=1, source_target_pairs={{0,18},{2,16},{16,2},{18,0},{1,19},{3,17},{17,3},{19,1},{4,22},{6,... | collective-permute-start | bytes 2064392 | tf_op jit(solution)/shard_map/ppermute | solution.py:672
  32.8 2.7 %gather_fusion.3 = bf16[3,64,448]{2,1,0:T(8,128)(2,1)S(1)} fusion(bf16[64,64,448]{2,1,0:T(8,128)(2,1)} %bitcast.19, s32[1024]{0:T(1024)S(1)} %pad_clamp_fusion), kind=kCustom, calls=%fused_computation.3 | custom fusion | bytes 344076 | tf_op jit(solution)/shard_map/gather | solution.py:645
  36.1 13.3 %collective-permute-done.13.far_down = bf16[3,64,448]{2,1,0:T(8,128)(2,1)S(1)} collective-permute-done((bf16[3,64,448]{2,1,0:T(8,128)(2,1)S(1)}, bf16[3,64,448]{2,1,0:T(8,128)(2,1)S(1)}, u32[]{:S(2)}, u32[]{:S(2)}) %collective-permute-start.13) | collective-permute-done | bytes 172064 | tf_op jit(solution)/shard_map/ppermute | solution.py:23
  53.0 9.4 %collective-permute-done.11.refs_2_.refs_12_ = bf16[272,896]{1,0:T(8,128)(2,1)S(1)} collective-permute-done((bf16[272,896]{1,0:T(8,128)(2,1)}, bf16[272,896]{1,0:T(8,128)(2,1)S(1)}, u32[]{:S(2)}, u32[]{:S(2)}) %collective-permute-start.11) | collective-permute-done | bytes 487456 | tf_op jit(solution)/shard_map/ppermute | solution.py:23
  64.0 2.7 %gather_fusion.2 = bf16[3,64,448]{2,1,0:T(8,128)(2,1)S(1)} fusion(bf16[64,64,448]{2,1,0:T(8,128)(2,1)} %bitcast.20, s32[1024]{0:T(1024)S(1)} %pad_clamp_fusion.1), kind=kCustom, calls=%fused_computation.2 | custom fusion | bytes 344076 | tf_op jit(solution)/shard_map/gather | solution.py:647
  70.8 10.5 %collective-permute-start.14 = (f32[128,128]{1,0:T(8,128)S(1)}, f32[128,128]{1,0:T(8,128)S(1)}, u32[]{:S(2)}, u32[]{:S(2)}) collective-permute-start(f32[128,128]{1,0:T(8,128)S(1)} %get-tuple-element.47), channel_id=1, source_target_pairs={{0,12},{4,0},{8,4},{12,8},{1,13},{5,1},{9,5},{13,9},{2,14},{6,2},{... | collective-permute-start | bytes 196616 | tf_op jit(solution)/shard_map/ppermute | solution.py:23
  84.1 3.9 %collective-permute-start.16 = (f32[128,128]{1,0:T(8,128)}, f32[128,128]{1,0:T(8,128)}, u32[]{:S(2)}, u32[]{:S(2)}) collective-permute-start(f32[128,128]{1,0:T(8,128)} %get-tuple-element.49), channel_id=1, source_target_pairs={{0,4},{4,8},{8,12},{12,0},{1,5},{5,9},{9,13},{13,1},{2,6},{6,10},{... | collective-permute-start | bytes 196616 | tf_op jit(solution)/shard_map/ppermute | solution.py:23
  89.0 5.4 %broadcast_in_dim.45.refs_1_.down_zeros = f32[64,64,1,448]{3,2,1,0:T(1,128)} broadcast(f32[]{:T(128)} %constant.10.clone.1), dimensions={} | broadcast | bytes 7340036 | tf_op jit(solution)/shard_map/broadcast_in_dim | solution.py:619
  94.5 2.5 %collective-permute-start.8 = (bf16[192,896]{1,0:T(8,128)(2,1)}, bf16[192,896]{1,0:T(8,128)(2,1)S(1)}, u32[]{:S(2)}, u32[]{:S(2)}) collective-permute-start(bf16[192,896]{1,0:T(8,128)(2,1)} %pass_middle.1.refs_3_), channel_id=1, source_target_pairs={{0,18},{2,16},{16,2},{18,0},{1,19},{3,17},{17,3},{19,1},{4,22},{6,... | collective-permute-start | bytes 1032200 | tf_op jit(solution)/shard_map/ppermute | solution.py:672
  98.0 8.1 %collective-permute-done.8.refs_9_ = bf16[192,896]{1,0:T(8,128)(2,1)S(1)} collective-permute-done((bf16[192,896]{1,0:T(8,128)(2,1)}, bf16[192,896]{1,0:T(8,128)(2,1)S(1)}, u32[]{:S(2)}, u32[]{:S(2)}) %collective-permute-start.8) | collective-permute-done | bytes 344096 | tf_op jit(solution)/shard_map/ppermute | solution.py:672
  106.2 3.5 %collective-permute-done.7.refs_8_ = bf16[192,896]{1,0:T(8,128)(2,1)S(1)} collective-permute-done((bf16[192,896]{1,0:T(8,128)(2,1)}, bf16[192,896]{1,0:T(8,128)(2,1)S(1)}, u32[]{:S(2)}, u32[]{:S(2)}) %collective-permute-start.7) | collective-permute-done | bytes 344096 | tf_op jit(solution)/shard_map/ppermute | solution.py:23
  117.1 4.9 %project.1 = (f32[256,896]{1,0:T(8,128)S(1)}, bf16[768,3584]{1,0:T(8,128)(2,1)S(1)}, bf16[3,64,640]{2,1,0:T(8,128)(2,1)S(1)}) custom-call(bf16[256,3584]{1,0:T(8,128)(2,1)S(1)} %bitcast.16, bf16[192,3584]{1,0:T(8,128)(2,1)S(1)} %copy-done.13, bf16[192,896]{1,0:T(8,128)(2,1)S(1)} %copy-done.10, bf16[192,896]{1,0:T(8,128)(2,1)S(1)} %copy-done.19, ...), custom_call_target="tpu_custom_call" | custom-call | flops 1409286144 | bytes 7340032 | tf_op jit(solution)/shard_map/project/pallas_call | solution.py:790
  122.5 3.5 %collective-permute-start.21 = (bf16[128,896]{1,0:T(8,128)(2,1)S(1)}, bf16[128,896]{1,0:T(8,128)(2,1)S(1)}, u32[]{:S(2)}, u32[]{:S(2)}) collective-permute-start(bf16[128,896]{1,0:T(8,128)(2,1)S(1)} %get-tuple-element.55), channel_id=1, source_target_pairs={{0,12},{4,0},{8,4},{12,8},{1,13},{5,1},{9,5},{13,9},{2,14},{6,2},{... | collective-permute-start | bytes 688136 | tf_op jit(solution)/shard_map/ppermute | solution.py:23
  128.4 4.1 %collective-permute-start.18 = (bf16[256,256]{1,0:T(8,128)(2,1)S(1)}, bf16[256,256]{1,0:T(8,128)(2,1)S(1)}, u32[]{:S(2)}, u32[]{:S(2)}) collective-permute-start(bf16[256,256]{1,0:T(8,128)(2,1)S(1)} %get-tuple-element.53.refs_0_), channel_id=1, source_target_pairs={{0,4},{4,8},{8,12},{1,5},{5,9},{9,13},{2,6},{6,10},{10,14},{3,7},{... | collective-permute-start | bytes 393224 | tf_op jit(solution)/shard_map/ppermute | solution.py:29
  132.5 2.7 %collective-permute-done.21.refs_4_.refs_3_ = bf16[128,896]{1,0:T(8,128)(2,1)S(1)} collective-permute-done((bf16[128,896]{1,0:T(8,128)(2,1)S(1)}, bf16[128,896]{1,0:T(8,128)(2,1)S(1)}, u32[]{:S(2)}, u32[]{:S(2)}) %collective-permute-start.21) | collective-permute-done | bytes 229408 | tf_op jit(solution)/shard_map/ppermute | solution.py:23
  138.6 3.4 %attention.1 = (bf16[128,512]{1,0:T(8,128)(2,1)}, bf16[128,512]{1,0:T(8,128)(2,1)S(1)}, f32[3,128,256]{2,1,0:T(8,128)S(1)}, f32[3,128,256]{2,1,0:T(8,128)S(1)}) custom-call(s32[2,3]{1,0:T(2,128)S(1)} %copy-done.24, bf16[512,128]{1,0:T(8,128)(2,1)S(1)} %get-tuple-element.52.queries, bf16[128,512]{1,0:T(8,128)(2,1)S(1)} %bitcast.17, ...), custom_call_target="tpu_custom_call" | custom-call | flops 503316480 | bytes 786432 | tf_op jit(solution)/shard_map/attention/pallas_call | solution.py:845
  146.6 7.2 %collective-permute-done.24.refs_1_ = f32[128,256]{1,0:T(8,128)S(1)} collective-permute-done((f32[128,256]{1,0:T(8,128)S(1)}, f32[128,256]{1,0:T(8,128)S(1)}, u32[]{:S(2)}, u32[]{:S(2)}) %collective-permute-start.24) | collective-permute-done | bytes 131104 | tf_op jit(solution)/shard_map/ppermute | solution.py:29
  153.8 7.5 %collective-permute-done.25.refs_2_ = f32[128,256]{1,0:T(8,128)S(1)} collective-permute-done((f32[128,256]{1,0:T(8,128)S(1)}, f32[128,256]{1,0:T(8,128)S(1)}, u32[]{:S(2)}, u32[]{:S(2)}) %collective-permute-start.25) | collective-permute-done | bytes 131104 | tf_op jit(solution)/shard_map/ppermute | solution.py:29
  166.1 2.9 %collective-permute-start.27 = (bf16[128,896]{1,0:T(8,128)(2,1)S(1)}, bf16[128,896]{1,0:T(8,128)(2,1)S(1)}, u32[]{:S(2)}, u32[]{:S(2)}) collective-permute-start(bf16[128,896]{1,0:T(8,128)(2,1)S(1)} %get-tuple-element.67), channel_id=1, source_target_pairs={{0,8},{4,12},{8,0},{12,4},{1,9},{5,13},{9,1},{13,5},{2,10},{6,14},... | collective-permute-start | bytes 688136 | tf_op jit(solution)/shard_map/ppermute | solution.py:23
  180.8 3.7 %collective-permute-done.33.refs_2_ = f32[120,128]{1,0:T(8,128)S(1)} collective-permute-done((f32[120,128]{1,0:T(8,128)S(1)}, f32[120,128]{1,0:T(8,128)S(1)}, u32[]{:S(2)}, u32[]{:S(2)}) %collective-permute-start.33) | collective-permute-done | bytes 61472 | tf_op jit(solution)/shard_map/ppermute | solution.py:23
  186.3 4.9 %token_gradient.1 = bf16[256,3584]{1,0:T(8,128)(2,1)} custom-call(bf16[256,896]{1,0:T(8,128)(2,1)S(1)} %get-tuple-element.64.gradients, bf16[768,3584]{1,0:T(8,128)(2,1)S(1)} %get-tuple-element.65.matrix, bf16[128,896]{1,0:T(8,128)(2,1)S(1)} %get-tuple-element.66.refs_0_, bf16[128,896]{1,0:T(8,128)(2,1)S(1)} %collective-permute-done.20.refs_3_.refs_1_, ...), custom_call_target="tpu_custom_call" | custom-call | flops 1644167168 | bytes 8257536 | tf_op jit(solution)/shard_map/token_gradient/pallas_call | solution.py:923
  191.2 2.9 %bank_rows.1 = (f32[64,64,1,448]{3,2,1,0:T(1,128)}, f32[64,32,80]{2,1,0:T(8,128)}) custom-call(s32[6]{0:T(128)S(1)} %pad_add_fusion.refs_3_.bank_rows, f32[192,448]{1,0:T(8,128)S(1)} %get-tuple-element.70.own_down, f32[192,448]{1,0:T(8,128)S(1)} %collective-permute-done.31.far_down, ...), custom_call_target="tpu_custom_call", output_to_operand_aliasing={{0}: (5, {}), {1}: (6, {})} | custom-call | tf_op jit(solution)/shard_map/bank_rows/pallas_call | solution.py:988
  (136 shorter events, 67.2 us)
Async XLA Ops:
  1.7 25.9 %collective-permute-start.1 = (bf16[192,896]{1,0:T(8,128)(2,1)S(1)}, bf16[192,896]{1,0:T(8,128)(2,1)S(1)}, u32[]{:S(2)}, u32[]{:S(2)}) collective-permute-start(bf16[192,896]{1,0:T(8,128)(2,1)S(1)} %constant_dynamic-slice_fusion.1), channel_id=1, source_target_pairs={{0,12},{4,0},{8,4},{12,8},{1,13},{5,1},{9,5},{13,9},{2,14},{6,2},{... | collective-permute-start | bytes 1032200 | tf_op jit(solution)/shard_map/ppermute | solution.py:23
  6.8 15.6 %collective-permute-start = (bf16[192,896]{1,0:T(8,128)(2,1)S(1)}, bf16[192,896]{1,0:T(8,128)(2,1)S(1)}, u32[]{:S(2)}, u32[]{:S(2)}) collective-permute-start(bf16[192,896]{1,0:T(8,128)(2,1)S(1)} %constant_dynamic-slice_fusion.1), channel_id=1, source_target_pairs={{0,4},{4,8},{8,12},{12,0},{1,5},{5,9},{9,13},{13,1},{2,6},{6,10},{... | collective-permute-start | bytes 1032200 | tf_op jit(solution)/shard_map/ppermute | solution.py:23
  25.4 27.2 %collective-permute-start.10 = (bf16[272,896]{1,0:T(8,128)(2,1)}, bf16[272,896]{1,0:T(8,128)(2,1)S(1)}, u32[]{:S(2)}, u32[]{:S(2)}) collective-permute-start(bf16[272,896]{1,0:T(8,128)(2,1)} %get-tuple-element.43), channel_id=1, source_target_pairs={{0,4},{4,8},{8,12},{12,0},{1,5},{5,9},{9,13},{13,1},{2,6},{6,10},{... | collective-permute-start | bytes 1462280 | tf_op jit(solution)/shard_map/ppermute | solution.py:23
  27.0 35.5 %collective-permute-start.11 = (bf16[272,896]{1,0:T(8,128)(2,1)}, bf16[272,896]{1,0:T(8,128)(2,1)S(1)}, u32[]{:S(2)}, u32[]{:S(2)}) collective-permute-start(bf16[272,896]{1,0:T(8,128)(2,1)} %get-tuple-element.44), channel_id=1, source_target_pairs={{0,8},{4,12},{8,0},{12,4},{1,9},{5,13},{9,1},{13,5},{2,10},{6,14},... | collective-permute-start | bytes 1462280 | tf_op jit(solution)/shard_map/ppermute | solution.py:23
  28.6 68.9 %collective-permute-start.5 = (bf16[384,896]{1,0:T(8,128)(2,1)}, bf16[384,896]{1,0:T(8,128)(2,1)}, u32[]{:S(2)}, u32[]{:S(2)}) collective-permute-start(bf16[384,896]{1,0:T(8,128)(2,1)} %join.1), channel_id=1, source_target_pairs={{0,18},{2,16},{16,2},{18,0},{1,19},{3,17},{17,3},{19,1},{4,22},{6,... | collective-permute-start | bytes 2064392 | tf_op jit(solution)/shard_map/ppermute | solution.py:672
  31.1 36.7 %collective-permute-start.12 = (bf16[272,896]{1,0:T(8,128)(2,1)}, bf16[272,896]{1,0:T(8,128)(2,1)S(1)}, u32[]{:S(2)}, u32[]{:S(2)}) collective-permute-start(bf16[272,896]{1,0:T(8,128)(2,1)} %get-tuple-element.45), channel_id=1, source_target_pairs={{0,12},{4,0},{8,4},{12,8},{1,13},{5,1},{9,5},{13,9},{2,14},{6,2},{... | collective-permute-start | bytes 1462280 | tf_op jit(solution)/shard_map/ppermute | solution.py:23
  35.5 13.9 %collective-permute-start.13 = (bf16[3,64,448]{2,1,0:T(8,128)(2,1)S(1)}, bf16[3,64,448]{2,1,0:T(8,128)(2,1)S(1)}, u32[]{:S(2)}, u32[]{:S(2)}) collective-permute-start(bf16[3,64,448]{2,1,0:T(8,128)(2,1)S(1)} %gather_fusion.3), channel_id=1, source_target_pairs={{0,2},{2,0},{1,3},{3,1},{4,6},{6,4},{5,7},{7,5},{8,10},{10,8},{9,1... | collective-permute-start | bytes 516104 | tf_op jit(solution)/shard_map/ppermute | solution.py:23
  50.1 31.2 %collective-permute-start.2 = (bf16[192,896]{1,0:T(8,128)(2,1)S(1)}, bf16[192,896]{1,0:T(8,128)(2,1)S(1)}, u32[]{:S(2)}, u32[]{:S(2)}) collective-permute-start(bf16[192,896]{1,0:T(8,128)(2,1)S(1)} %collective-permute-done.before.refs_0_.refs_1_), channel_id=1, source_target_pairs={{0,4},{4,8},{8,12},{12,0},{1,5},{5,9},{9,13},{13,1},{2,6},{6,10},{... | collective-permute-start | bytes 1032200 | tf_op jit(solution)/shard_map/ppermute | solution.py:23
  52.5 45.5 %collective-permute-start.4 = (bf16[384,896]{1,0:T(8,128)(2,1)}, bf16[384,896]{1,0:T(8,128)(2,1)}, u32[]{:S(2)}, u32[]{:S(2)}) collective-permute-start(bf16[384,896]{1,0:T(8,128)(2,1)} %join.1), channel_id=1, source_target_pairs={{0,16},{16,0},{1,17},{17,1},{2,18},{18,2},{3,19},{19,3},{4,20},{20... | collective-permute-start | bytes 2064392 | tf_op jit(solution)/shard_map/ppermute | solution.py:23
  62.5 35.6 %collective-permute-start.3 = (bf16[384,896]{1,0:T(8,128)(2,1)}, bf16[384,896]{1,0:T(8,128)(2,1)}, u32[]{:S(2)}, u32[]{:S(2)}) collective-permute-start(bf16[384,896]{1,0:T(8,128)(2,1)} %join.1), channel_id=1, source_target_pairs={{0,2},{2,0},{1,3},{3,1},{4,6},{6,4},{5,7},{7,5},{8,10},{10,8},{9,1... | collective-permute-start | bytes 2064392 | tf_op jit(solution)/shard_map/ppermute | solution.py:23
  70.8 13.2 %collective-permute-start.14 = (f32[128,128]{1,0:T(8,128)S(1)}, f32[128,128]{1,0:T(8,128)S(1)}, u32[]{:S(2)}, u32[]{:S(2)}) collective-permute-start(f32[128,128]{1,0:T(8,128)S(1)} %get-tuple-element.47), channel_id=1, source_target_pairs={{0,12},{4,0},{8,4},{12,8},{1,13},{5,1},{9,5},{13,9},{2,14},{6,2},{... | collective-permute-start | bytes 196616 | tf_op jit(solution)/shard_map/ppermute | solution.py:23
  81.3 13.1 %collective-permute-start.15 = (f32[128,128]{1,0:T(8,128)}, f32[128,128]{1,0:T(8,128)}, u32[]{:S(2)}, u32[]{:S(2)}) collective-permute-start(f32[128,128]{1,0:T(8,128)} %get-tuple-element.48), channel_id=1, source_target_pairs={{0,8},{4,12},{8,0},{12,4},{1,9},{5,13},{9,1},{13,5},{2,10},{6,14},... | collective-permute-start | bytes 196616 | tf_op jit(solution)/shard_map/ppermute | solution.py:23
  84.1 12.9 %collective-permute-start.16 = (f32[128,128]{1,0:T(8,128)}, f32[128,128]{1,0:T(8,128)}, u32[]{:S(2)}, u32[]{:S(2)}) collective-permute-start(f32[128,128]{1,0:T(8,128)} %get-tuple-element.49), channel_id=1, source_target_pairs={{0,4},{4,8},{8,12},{12,0},{1,5},{5,9},{9,13},{13,1},{2,6},{6,10},{... | collective-permute-start | bytes 196616 | tf_op jit(solution)/shard_map/ppermute | solution.py:23
  94.5 11.7 %collective-permute-start.8 = (bf16[192,896]{1,0:T(8,128)(2,1)}, bf16[192,896]{1,0:T(8,128)(2,1)S(1)}, u32[]{:S(2)}, u32[]{:S(2)}) collective-permute-start(bf16[192,896]{1,0:T(8,128)(2,1)} %pass_middle.1.refs_3_), channel_id=1, source_target_pairs={{0,18},{2,16},{16,2},{18,0},{1,19},{3,17},{17,3},{19,1},{4,22},{6,... | collective-permute-start | bytes 1032200 | tf_op jit(solution)/shard_map/ppermute | solution.py:672
  97.0 12.7 %collective-permute-start.7 = (bf16[192,896]{1,0:T(8,128)(2,1)}, bf16[192,896]{1,0:T(8,128)(2,1)S(1)}, u32[]{:S(2)}, u32[]{:S(2)}) collective-permute-start(bf16[192,896]{1,0:T(8,128)(2,1)} %pass_middle.1.refs_3_), channel_id=1, source_target_pairs={{0,16},{16,0},{1,17},{17,1},{2,18},{18,2},{3,19},{19,3},{4,20},{20... | collective-permute-start | bytes 1032200 | tf_op jit(solution)/shard_map/ppermute | solution.py:23
  97.5 12.3 %collective-permute-start.6 = (bf16[192,896]{1,0:T(8,128)(2,1)}, bf16[192,896]{1,0:T(8,128)(2,1)S(1)}, u32[]{:S(2)}, u32[]{:S(2)}) collective-permute-start(bf16[192,896]{1,0:T(8,128)(2,1)} %pass_middle.1.refs_3_), channel_id=1, source_target_pairs={{0,2},{2,0},{1,3},{3,1},{4,6},{6,4},{5,7},{7,5},{8,10},{10,8},{9,1... | collective-permute-start | bytes 1032200 | tf_op jit(solution)/shard_map/ppermute | solution.py:23
  122.2 10.3 %collective-permute-start.20 = (bf16[128,896]{1,0:T(8,128)(2,1)S(1)}, bf16[128,896]{1,0:T(8,128)(2,1)S(1)}, u32[]{:S(2)}, u32[]{:S(2)}) collective-permute-start(bf16[128,896]{1,0:T(8,128)(2,1)S(1)} %get-tuple-element.54), channel_id=1, source_target_pairs={{0,4},{4,8},{8,12},{12,0},{1,5},{5,9},{9,13},{13,1},{2,6},{6,10},{... | collective-permute-start | bytes 688136 | tf_op jit(solution)/shard_map/ppermute | solution.py:23
  122.5 12.7 %collective-permute-start.21 = (bf16[128,896]{1,0:T(8,128)(2,1)S(1)}, bf16[128,896]{1,0:T(8,128)(2,1)S(1)}, u32[]{:S(2)}, u32[]{:S(2)}) collective-permute-start(bf16[128,896]{1,0:T(8,128)(2,1)S(1)} %get-tuple-element.55), channel_id=1, source_target_pairs={{0,12},{4,0},{8,4},{12,8},{1,13},{5,1},{9,5},{13,9},{2,14},{6,2},{... | collective-permute-start | bytes 688136 | tf_op jit(solution)/shard_map/ppermute | solution.py:23
  128.4 10.3 %collective-permute-start.18 = (bf16[256,256]{1,0:T(8,128)(2,1)S(1)}, bf16[256,256]{1,0:T(8,128)(2,1)S(1)}, u32[]{:S(2)}, u32[]{:S(2)}) collective-permute-start(bf16[256,256]{1,0:T(8,128)(2,1)S(1)} %get-tuple-element.53.refs_0_), channel_id=1, source_target_pairs={{0,4},{4,8},{8,12},{1,5},{5,9},{9,13},{2,6},{6,10},{10,14},{3,7},{... | collective-permute-start | bytes 393224 | tf_op jit(solution)/shard_map/ppermute | solution.py:29
  143.8 10.0 %collective-permute-start.24 = (f32[128,256]{1,0:T(8,128)S(1)}, f32[128,256]{1,0:T(8,128)S(1)}, u32[]{:S(2)}, u32[]{:S(2)}) collective-permute-start(f32[128,256]{1,0:T(8,128)S(1)} %get-tuple-element.61), channel_id=1, source_target_pairs={{4,0},{8,4},{12,8},{5,1},{9,5},{13,9},{6,2},{10,6},{14,10},{7,3},{... | collective-permute-start | bytes 393224 | tf_op jit(solution)/shard_map/ppermute | solution.py:29
  145.1 16.2 %collective-permute-start.25 = (f32[128,256]{1,0:T(8,128)S(1)}, f32[128,256]{1,0:T(8,128)S(1)}, u32[]{:S(2)}, u32[]{:S(2)}) collective-permute-start(f32[128,256]{1,0:T(8,128)S(1)} %get-tuple-element.62), channel_id=1, source_target_pairs={{8,0},{12,4},{9,1},{13,5},{10,2},{14,6},{11,3},{15,7},{24,16},{28,... | collective-permute-start | bytes 393224 | tf_op jit(solution)/shard_map/ppermute | solution.py:29
  146.4 15.1 %collective-permute-start.22 = (bf16[128,512]{1,0:T(8,128)(2,1)S(1)}, bf16[128,512]{1,0:T(8,128)(2,1)S(1)}, u32[]{:S(2)}, u32[]{:S(2)}) collective-permute-start(bf16[128,512]{1,0:T(8,128)(2,1)S(1)} %get-tuple-element.57.own_query), channel_id=1, source_target_pairs={{0,1},{1,0},{2,3},{3,2},{4,5},{5,4},{6,7},{7,6},{8,9},{9,8},{10,11... | collective-permute-start | bytes 393224 | tf_op jit(solution)/shard_map/ppermute | solution.py:23
  166.1 20.2 %collective-permute-start.27 = (bf16[128,896]{1,0:T(8,128)(2,1)S(1)}, bf16[128,896]{1,0:T(8,128)(2,1)S(1)}, u32[]{:S(2)}, u32[]{:S(2)}) collective-permute-start(bf16[128,896]{1,0:T(8,128)(2,1)S(1)} %get-tuple-element.67), channel_id=1, source_target_pairs={{0,8},{4,12},{8,0},{12,4},{1,9},{5,13},{9,1},{13,5},{2,10},{6,14},... | collective-permute-start | bytes 688136 | tf_op jit(solution)/shard_map/ppermute | solution.py:23
  173.1 18.1 %collective-permute-start.31 = (f32[192,448]{1,0:T(8,128)S(1)}, f32[192,448]{1,0:T(8,128)S(1)}, u32[]{:S(2)}, u32[]{:S(2)}) collective-permute-start(f32[192,448]{1,0:T(8,128)S(1)} %get-tuple-element.71), channel_id=1, source_target_pairs={{0,2},{2,0},{1,3},{3,1},{4,6},{6,4},{5,7},{7,5},{8,10},{10,8},{9,1... | collective-permute-start | bytes 1032200 | tf_op jit(solution)/shard_map/ppermute | solution.py:23
  (38 other events, 454.5 us)

commit v9 on v8

--- a/solution.py
+++ b/solution.py
@@ -130,14 +130,11 @@
     return place
 
 
-def join_kernel(before, after, plane):
+def join_kernel(before, after, *refs):
+    plane = refs[-1]
     rows = before.shape[0]
     plane[:rows] = before[...]
     plane[rows:] = after[...]
-
-
-def pass_kernel(*refs):
-    del refs
 
 
 def block_kernel(own_down, far_down, down):
@@ -163,7 +160,7 @@
         payload[...] = down[pl.ds(start, 2 * joint_rank)]
 
 
-def cut_kernel(unused, tokens, own_up, far_up, *refs):
+def cut_kernel(unused, steps_of, seq_count, tokens, own_up, far_up, *refs):
     blocks, up = refs[unused:-1], refs[-1]
     ahead = lax.axis_index("batch") == 0
     low_width, held_up = own_up.shape[1:]
@@ -172,8 +169,8 @@
         up[document, :, held_up:] = jnp.where(ahead, far_up[document], own_up[document])
     rows = tokens.shape[0]
     half = low_width // 2
-    for steps, block in enumerate(blocks):
-        target, first = target_of(steps, len(blocks))
+    for steps, block in zip(steps_of, blocks):
+        target, first = target_of(steps, seq_count)
         width = block.shape[1]
         block[:rows] = tokens[:, pl.ds(pl.multiple_of(target * width, 128), width)]
         slot = width // 4
@@ -471,7 +468,7 @@
 
 def down_kernel(block_count, lengths, *refs):
     columns, ranks = refs[:block_count], refs[block_count : 2 * block_count]
-    outputs = refs[2 * block_count :]
+    outputs = refs[2 * block_count + 1 :]
     rows, joint_rank = ranks[0].shape
     ends = kernel_marks(lengths)
     lows = [ranks[0][...]]
@@ -673,32 +670,33 @@
             ]
 
         plane_parts = over_plane(plane)
-        middle = pl.pallas_call(
-            pass_kernel,
-            out_shape=jax.ShapeDtypeStruct((frozen_rows, share), bf16),
-            in_specs=[in_place()] * 3,
-            out_specs=in_place(),
-            input_output_aliases={0: 0},
-            name="pass_middle",
-        )(shift(before, "seq", 1), down_zeros, up_zeros)
+        middle = shift(before, "seq", 1)
         middle_parts = over_plane(middle)
 
-        early = [before, cosines, sines, bank_rows]
         block_rows = rows + low_width // 2
-        column_blocks = pl.pallas_call(
-            functools.partial(cut_kernel, len(early)),
-            out_shape=[jax.ShapeDtypeStruct((block_rows, down_width), bf16)] * seq_count,
-            in_specs=[in_vmem()] * 3 + [in_place()] * len(early),
-            out_specs=[by_block((block_rows, down_width))] * seq_count,
-            scratch_shapes=[pltpu.VMEM((SEGS, low_width, 2 * held_up), bf16)],
-            compiler_params=pltpu.CompilerParams(vmem_limit_bytes=16 * mebibyte),
-            cost_estimate=cost(0, 4 * rows * width),
-            name="cut",
-        )(local_tokens, own_up, far_up, *early)
-        column_parts = [
-            shift(block, "seq", steps) if steps else block
-            for steps, block in enumerate(column_blocks)
-        ]
+
+        def cut_columns(steps_of, early):
+            blocks = pl.pallas_call(
+                functools.partial(cut_kernel, len(early), steps_of, seq_count),
+                out_shape=[jax.ShapeDtypeStruct((block_rows, down_width), bf16)] * len(steps_of),
+                in_specs=[in_vmem()] * 3 + [in_place()] * len(early),
+                out_specs=[by_block((block_rows, down_width))] * len(steps_of),
+                scratch_shapes=[pltpu.VMEM((SEGS, low_width, 2 * held_up), bf16)],
+                compiler_params=pltpu.CompilerParams(vmem_limit_bytes=16 * mebibyte),
+                cost_estimate=cost(0, len(steps_of) * rows * width),
+                name="cut",
+            )(local_tokens, own_up, far_up, *early)
+            return [
+                shift(block, "seq", steps) if steps else block
+                for steps, block in zip(steps_of, blocks)
+            ]
+
+        near_before, near_after = cut_columns((1, 3), [plane, down_block])
+        own_columns, far_columns = cut_columns(
+            (0, 2),
+            [near_before, *plane_parts, down_zeros, up_zeros, cosines, sines, bank_rows],
+        )
+        column_parts = [own_columns, near_before, far_columns, near_after]
         low_shapes = [(rows, joint_rank)] + [(rows // 2, 2 * joint_rank)] * (seq_count - 1)
         lows = pl.pallas_call(
             functools.partial(low_kernel, seq_count),
@@ -944,17 +942,6 @@
     if not direct:
         term_shapes = [(SEGS * joint_rank, down_width)]
         up_shapes = [(SEGS * low_width, up_width)]
-    terms = pl.pallas_call(
-        functools.partial(down_kernel, seq_count),
-        out_shape=[jax.ShapeDtypeStruct(shape, f32) for shape in term_shapes],
-        in_specs=[in_smem()] + [in_vmem()] * (2 * seq_count),
-        out_specs=[in_vmem()] * len(term_shapes),
-        compiler_params=pltpu.CompilerParams(vmem_limit_bytes=8 * mebibyte),
-        cost_estimate=cost(
-            2 * seq_count * rows * SEGS * joint_rank * down_width, 2 * seq_count * rows * down_width
-        ),
-        name="down_terms",
-    )(document_lengths, *column_parts, *rank_parts)
     ups = pl.pallas_call(
         functools.partial(up_kernel, seq_count),
         out_shape=[jax.ShapeDtypeStruct(shape, f32) for shape in up_shapes],
@@ -964,7 +951,17 @@
         compiler_params=pltpu.CompilerParams(vmem_limit_bytes=8 * mebibyte),
         name="up_terms",
     )(*up_sums)
-
+    terms = pl.pallas_call(
+        functools.partial(down_kernel, seq_count),
+        out_shape=[jax.ShapeDtypeStruct(shape, f32) for shape in term_shapes],
+        in_specs=[in_smem()] + [in_vmem()] * (2 * seq_count) + [in_place()],
+        out_specs=[in_vmem()] * len(term_shapes),
+        compiler_params=pltpu.CompilerParams(vmem_limit_bytes=8 * mebibyte),
+        cost_estimate=cost(
+            2 * seq_count * rows * SEGS * joint_rank * down_width, 2 * seq_count * rows * down_width
+        ),
+        name="down_terms",
+    )(document_lengths, *column_parts, *rank_parts, ups[0])
     if direct:
         bank_terms = [terms[0], shift(terms[1], "batch", 1), ups[0], shift(ups[1], "batch", 1)]
     else:

time: 195 us -> 177 us (0.908)
  starting transfers between devices: 62.1 us -> 39.1 us
  waiting for transfers between devices: 74.5 us -> 86.1 us
  local copies, waits for them, and re-layouts: 27.4 us -> 22.6 us
    ppermute x30, starting transfers between devices: 49.1 us -> 28 us  [shift(): lax.ppermute(value, axis, [(at, (at + steps) % count) for at in range(cou...]
    ppermute x30, waiting for transfers between devices: 48.2 us -> 67.7 us  [shift(): lax.ppermute(value, axis, [(at, (at + steps) % count) for at in range(cou...]
    ppermute x2, waiting for transfers between devices: 8.14 us -> 0.01 us  [over_plane(): lax.ppermute(value, ('groups', 'batch'), over_both)]
    unnamed x53 -> x31, local copies, waits for them, and re-layouts: 12 us -> 6.88 us
  transfers between devices with their start and end apart: 36 -> 36, of which waited for: 17 -> 20; matrix products, arithmetic and copies ran while one was open for 9% -> 10% of each run, Pallas kernels for 7% -> 7%
where the time goes in v9:
time: 177 us; the launch traced here: 176 us
  waiting for transfers between devices  86.1 us (49%)
  starting transfers between devices  39.1 us (22%)
  Pallas kernels  23.8 us (13%)
  local copies, waits for them, and re-layouts  22.6 us (13%)
  other arithmetic  2.39 us (1%)
  between operations  2.21 us (1%)
    ppermute x30, waiting for transfers between devices, shift(): lax.ppermute(value, axis, [(at, (at + steps) % count) for at in range(cou...  67.7 us
    ppermute x30, starting transfers between devices, shift(): lax.ppermute(value, axis, [(at, (at + steps) % count) for at in range(cou...  28 us
    ppermute x4, waiting for transfers between devices, push(): return lax.ppermute(value, axis, pairs)  18.3 us
    ppermute x4, starting transfers between devices, push(): return lax.ppermute(value, axis, pairs)  7.03 us
    unnamed x31, local copies, waits for them, and re-layouts  6.88 us
    pallas_call x1, Pallas kernels, shards(): pl.pallas_call(functools.partial(token_kernel, weight_places), grid=(widt...  4.91 us
    broadcast_in_dim x1, local copies, waits for them, and re-layouts, shards(): down_zeros = jnp.zeros((adapters, joint_rank, 1, held_down), f32)  4.53 us
    ppermute x2, starting transfers between devices, over_plane(): lax.ppermute(value, ('groups', 'batch'), over_both)  4.1 us
  transfers between devices with their start and end apart: 36, of which 20 were waited for; matrix products, arithmetic and copies ran while one was open for 10% of the time, Pallas kernels for 7%

profile of v9, /device:TPU:0, one launch (start us, length us, event | category | flops | bytes accessed | tf_op | source)
XLA Modules:
  0.0 176.1 jit_solution(12686660313404384091)
XLA Ops:
  2.6 5.0 %collective-permute-start.1 = (bf16[192,896]{1,0:T(8,128)(2,1)}, bf16[192,896]{1,0:T(8,128)(2,1)S(1)}, u32[]{:S(2)}, u32[]{:S(2)}) collective-permute-start(bf16[192,896]{1,0:T(8,128)(2,1)} %constant_dynamic-slice_fusion.1), channel_id=1, source_target_pairs={{0,12},{4,0},{8,4},{12,8},{1,13},{5,1},{9,5},{13,9},{2,14},{6,2},{... | collective-permute-start | bytes 1032200 | tf_op jit(solution)/shard_map/ppermute | solution.py:23
  11.6 3.4 %gather_fusion.3 = bf16[3,64,448]{2,1,0:T(8,128)(2,1)} fusion(bf16[64,64,448]{2,1,0:T(8,128)(2,1)} %bitcast.20, s32[1024]{0:T(1024)S(1)} %pad_clamp_fusion), kind=kCustom, calls=%fused_computation.3 | custom fusion | bytes 344076 | tf_op jit(solution)/shard_map/gather | solution.py:642
  16.8 6.6 %collective-permute-done.before.refs_1_ = bf16[192,896]{1,0:T(8,128)(2,1)S(1)} collective-permute-done((bf16[192,896]{1,0:T(8,128)(2,1)}, bf16[192,896]{1,0:T(8,128)(2,1)S(1)}, u32[]{:S(2)}, u32[]{:S(2)}) %collective-permute-start) | collective-permute-done | bytes 344096 | tf_op jit(solution)/shard_map/ppermute | solution.py:23
  24.4 2.4 %collective-permute-start.5 = (bf16[384,896]{1,0:T(8,128)(2,1)}, bf16[384,896]{1,0:T(8,128)(2,1)}, u32[]{:S(2)}, u32[]{:S(2)}) collective-permute-start(bf16[384,896]{1,0:T(8,128)(2,1)} %join.1.refs_0_), channel_id=1, source_target_pairs={{0,18},{2,16},{16,2},{18,0},{1,19},{3,17},{17,3},{19,1},{4,22},{6,... | collective-permute-start | bytes 2064392 | tf_op jit(solution)/shard_map/ppermute | solution.py:669
  29.0 2.7 %gather_fusion.2 = bf16[3,64,448]{2,1,0:T(8,128)(2,1)S(1)} fusion(bf16[64,64,448]{2,1,0:T(8,128)(2,1)} %bitcast.21, s32[1024]{0:T(1024)S(1)} %pad_clamp_fusion.1), kind=kCustom, calls=%fused_computation.2 | custom fusion | bytes 344076 | tf_op jit(solution)/shard_map/gather | solution.py:644
  40.0 12.0 %collective-permute-done.11.refs_0_.refs_1_.refs_11_ = bf16[272,896]{1,0:T(8,128)(2,1)S(1)} collective-permute-done((bf16[272,896]{1,0:T(8,128)(2,1)}, bf16[272,896]{1,0:T(8,128)(2,1)S(1)}, u32[]{:S(2)}, u32[]{:S(2)}) %collective-permute-start.11) | collective-permute-done | bytes 487456 | tf_op jit(solution)/shard_map/ppermute | solution.py:23
  52.0 4.6 %collective-permute-done.4.refs_2_.refs_5_ = bf16[384,896]{1,0:T(8,128)(2,1)} collective-permute-done((bf16[384,896]{1,0:T(8,128)(2,1)}, bf16[384,896]{1,0:T(8,128)(2,1)}, u32[]{:S(2)}, u32[]{:S(2)}) %collective-permute-start.4) | collective-permute-done | bytes 688160 | tf_op jit(solution)/shard_map/ppermute | solution.py:23
  56.9 4.5 %broadcast_in_dim.47.refs_4_.down_zeros = f32[64,64,1,448]{3,2,1,0:T(1,128)S(1)} broadcast(f32[]{:T(128)} %constant.11.clone.1), dimensions={} | broadcast | bytes 7340036 | tf_op jit(solution)/shard_map/broadcast_in_dim | solution.py:616
  61.7 3.2 %copy-done.1 = f32[64,64,1,448]{3,2,1,0:T(1,128)} copy-done((f32[64,64,1,448]{3,2,1,0:T(1,128)}, f32[64,64,1,448]{3,2,1,0:T(1,128)S(1)}, u32[]{:S(2)}) %copy-start.1) | copy-done | bytes 7340056
  68.8 20.4 %collective-permute-done.12.refs_2_.refs_12_ = bf16[272,896]{1,0:T(8,128)(2,1)S(1)} collective-permute-done((bf16[272,896]{1,0:T(8,128)(2,1)S(1)}, bf16[272,896]{1,0:T(8,128)(2,1)S(1)}, u32[]{:S(2)}, u32[]{:S(2)}) %collective-permute-start.12) | collective-permute-done | bytes 487456 | tf_op jit(solution)/shard_map/ppermute | solution.py:23
  95.3 4.0 %collective-permute-done.15.refs_16_ = f32[128,128]{1,0:T(8,128)S(1)} collective-permute-done((f32[128,128]{1,0:T(8,128)S(1)}, f32[128,128]{1,0:T(8,128)S(1)}, u32[]{:S(2)}, u32[]{:S(2)}) %collective-permute-start.15) | collective-permute-done | bytes 65568 | tf_op jit(solution)/shard_map/ppermute | solution.py:23
  99.3 4.0 %project.1 = (f32[256,896]{1,0:T(8,128)S(1)}, bf16[768,3584]{1,0:T(8,128)(2,1)S(1)}, bf16[3,64,640]{2,1,0:T(8,128)(2,1)S(1)}) custom-call(bf16[256,3584]{1,0:T(8,128)(2,1)S(1)} %bitcast.17, bf16[192,3584]{1,0:T(8,128)(2,1)S(1)} %copy-done.4, bf16[192,896]{1,0:T(8,128)(2,1)S(1)} %copy-done.6, bf16[192,896]{1,0:T(8,128)(2,1)S(1)} %collective-permute-done.1.after.refs_2_, ...), custom_call_target="tpu_custom_call" | custom-call | flops 1409286144 | bytes 7340032 | tf_op jit(solution)/shard_map/project/pallas_call | solution.py:788
  103.5 3.8 %collective-permute-start.21 = (bf16[128,896]{1,0:T(8,128)(2,1)S(1)}, bf16[128,896]{1,0:T(8,128)(2,1)S(1)}, u32[]{:S(2)}, u32[]{:S(2)}) collective-permute-start(bf16[128,896]{1,0:T(8,128)(2,1)S(1)} %get-tuple-element.55), channel_id=1, source_target_pairs={{0,12},{4,0},{8,4},{12,8},{1,13},{5,1},{9,5},{13,9},{2,14},{6,2},{... | collective-permute-start | bytes 688136 | tf_op jit(solution)/shard_map/ppermute | solution.py:23
  110.2 2.6 %collective-permute-start.18 = (bf16[256,256]{1,0:T(8,128)(2,1)S(1)}, bf16[256,256]{1,0:T(8,128)(2,1)S(1)}, u32[]{:S(2)}, u32[]{:S(2)}) collective-permute-start(bf16[256,256]{1,0:T(8,128)(2,1)S(1)} %get-tuple-element.53.refs_0_), channel_id=1, source_target_pairs={{0,4},{4,8},{8,12},{1,5},{5,9},{9,13},{2,6},{6,10},{10,14},{3,7},{... | collective-permute-start | bytes 393224 | tf_op jit(solution)/shard_map/ppermute | solution.py:29
  113.8 2.7 %collective-permute-done.21.refs_4_.refs_3_ = bf16[128,896]{1,0:T(8,128)(2,1)S(1)} collective-permute-done((bf16[128,896]{1,0:T(8,128)(2,1)S(1)}, bf16[128,896]{1,0:T(8,128)(2,1)S(1)}, u32[]{:S(2)}, u32[]{:S(2)}) %collective-permute-start.21) | collective-permute-done | bytes 229408 | tf_op jit(solution)/shard_map/ppermute | solution.py:23
  117.3 2.6 %collective-permute-done.18.refs_1_ = bf16[256,256]{1,0:T(8,128)(2,1)S(1)} collective-permute-done((bf16[256,256]{1,0:T(8,128)(2,1)S(1)}, bf16[256,256]{1,0:T(8,128)(2,1)S(1)}, u32[]{:S(2)}, u32[]{:S(2)}) %collective-permute-start.18) | collective-permute-done | bytes 131104 | tf_op jit(solution)/shard_map/ppermute | solution.py:29
  119.9 3.4 %attention.1 = (bf16[128,512]{1,0:T(8,128)(2,1)}, bf16[128,512]{1,0:T(8,128)(2,1)S(1)}, f32[3,128,256]{2,1,0:T(8,128)S(1)}, f32[3,128,256]{2,1,0:T(8,128)S(1)}) custom-call(s32[2,3]{1,0:T(2,128)S(1)} %copy-done.12, bf16[512,128]{1,0:T(8,128)(2,1)S(1)} %get-tuple-element.52.queries, bf16[128,512]{1,0:T(8,128)(2,1)S(1)} %bitcast.18, ...), custom_call_target="tpu_custom_call" | custom-call | flops 503316480 | bytes 786432 | tf_op jit(solution)/shard_map/attention/pallas_call | solution.py:843
  127.9 7.3 %collective-permute-done.24.refs_1_ = f32[128,256]{1,0:T(8,128)S(1)} collective-permute-done((f32[128,256]{1,0:T(8,128)S(1)}, f32[128,256]{1,0:T(8,128)S(1)}, u32[]{:S(2)}, u32[]{:S(2)}) %collective-permute-start.24) | collective-permute-done | bytes 131104 | tf_op jit(solution)/shard_map/ppermute | solution.py:29
  135.3 7.5 %collective-permute-done.25.refs_2_ = f32[128,256]{1,0:T(8,128)S(1)} collective-permute-done((f32[128,256]{1,0:T(8,128)S(1)}, f32[128,256]{1,0:T(8,128)S(1)}, u32[]{:S(2)}, u32[]{:S(2)}) %collective-permute-start.25) | collective-permute-done | bytes 131104 | tf_op jit(solution)/shard_map/ppermute | solution.py:29
  145.7 3.7 %collective-permute-start.33 = (f32[120,128]{1,0:T(8,128)S(1)}, f32[120,128]{1,0:T(8,128)S(1)}, u32[]{:S(2)}, u32[]{:S(2)}) collective-permute-start(f32[120,128]{1,0:T(8,128)S(1)} %get-tuple-element.73), channel_id=1, source_target_pairs={{0,12},{4,0},{8,4},{12,8},{1,13},{5,1},{9,5},{13,9},{2,14},{6,2},{... | collective-permute-start | bytes 184328 | tf_op jit(solution)/shard_map/ppermute | solution.py:23
  154.6 5.9 %collective-permute-done.29.refs_6_ = bf16[128,128]{1,0:T(8,128)(2,1)S(1)} collective-permute-done((bf16[128,128]{1,0:T(8,128)(2,1)S(1)}, bf16[128,128]{1,0:T(8,128)(2,1)S(1)}, u32[]{:S(2)}, u32[]{:S(2)}) %collective-permute-start.29) | collective-permute-done | bytes 32800 | tf_op jit(solution)/shard_map/ppermute | solution.py:23
  164.5 2.9 %collective-permute-done.27.refs_2_ = bf16[128,896]{1,0:T(8,128)(2,1)S(1)} collective-permute-done((bf16[128,896]{1,0:T(8,128)(2,1)S(1)}, bf16[128,896]{1,0:T(8,128)(2,1)S(1)}, u32[]{:S(2)}, u32[]{:S(2)}) %collective-permute-start.27) | collective-permute-done | bytes 229408 | tf_op jit(solution)/shard_map/ppermute | solution.py:23
  167.4 4.9 %token_gradient.1 = bf16[256,3584]{1,0:T(8,128)(2,1)} custom-call(bf16[256,896]{1,0:T(8,128)(2,1)S(1)} %get-tuple-element.64.gradients, bf16[768,3584]{1,0:T(8,128)(2,1)S(1)} %get-tuple-element.65.matrix, bf16[128,896]{1,0:T(8,128)(2,1)S(1)} %get-tuple-element.66.refs_0_, bf16[128,896]{1,0:T(8,128)(2,1)S(1)} %collective-permute-done.20.refs_3_.refs_1_, ...), custom_call_target="tpu_custom_call" | custom-call | flops 1644167168 | bytes 8257536 | tf_op jit(solution)/shard_map/token_gradient/pallas_call | solution.py:921
  173.3 2.9 %bank_rows.1 = (f32[64,64,1,448]{3,2,1,0:T(1,128)}, f32[64,32,80]{2,1,0:T(8,128)}) custom-call(s32[6]{0:T(128)S(1)} %pad_add_fusion.refs_8_.bank_rows, f32[192,448]{1,0:T(8,128)S(1)} %get-tuple-element.75.own_down, f32[192,448]{1,0:T(8,128)S(1)} %collective-permute-done.34.far_down, ...), custom_call_target="tpu_custom_call", output_to_operand_aliasing={{0}: (5, {}), {1}: (6, {})} | custom-call | tf_op jit(solution)/shard_map/bank_rows/pallas_call | solution.py:985
  (114 shorter events, 50.5 us)
Async XLA Ops:
  2.6 14.2 %collective-permute-start.1 = (bf16[192,896]{1,0:T(8,128)(2,1)}, bf16[192,896]{1,0:T(8,128)(2,1)S(1)}, u32[]{:S(2)}, u32[]{:S(2)}) collective-permute-start(bf16[192,896]{1,0:T(8,128)(2,1)} %constant_dynamic-slice_fusion.1), channel_id=1, source_target_pairs={{0,12},{4,0},{8,4},{12,8},{1,13},{5,1},{9,5},{13,9},{2,14},{6,2},{... | collective-permute-start | bytes 1032200 | tf_op jit(solution)/shard_map/ppermute | solution.py:23
  7.6 15.8 %collective-permute-start = (bf16[192,896]{1,0:T(8,128)(2,1)}, bf16[192,896]{1,0:T(8,128)(2,1)S(1)}, u32[]{:S(2)}, u32[]{:S(2)}) collective-permute-start(bf16[192,896]{1,0:T(8,128)(2,1)} %constant_dynamic-slice_fusion.1), channel_id=1, source_target_pairs={{0,4},{4,8},{8,12},{12,0},{1,5},{5,9},{9,13},{13,1},{2,6},{6,10},{... | collective-permute-start | bytes 1032200 | tf_op jit(solution)/shard_map/ppermute | solution.py:23
  10.0 21.9 %collective-permute-start.9 = (bf16[3,32,80]{2,1,0:T(8,128)(2,1)S(1)}, bf16[3,32,80]{2,1,0:T(8,128)(2,1)S(1)}, u32[]{:S(2)}, u32[]{:S(2)}) collective-permute-start(bf16[3,32,80]{2,1,0:T(8,128)(2,1)S(1)} %gather_fusion.1), channel_id=1, source_target_pairs={{0,2},{2,0},{1,3},{3,1},{4,6},{6,4},{5,7},{7,5},{8,10},{10,8},{9,1... | collective-permute-start | bytes 46088 | tf_op jit(solution)/shard_map/ppermute | solution.py:23
  15.0 16.8 %collective-permute-start.10 = (bf16[3,64,448]{2,1,0:T(8,128)(2,1)}, bf16[3,64,448]{2,1,0:T(8,128)(2,1)S(1)}, u32[]{:S(2)}, u32[]{:S(2)}) collective-permute-start(bf16[3,64,448]{2,1,0:T(8,128)(2,1)} %gather_fusion.3), channel_id=1, source_target_pairs={{0,2},{2,0},{1,3},{3,1},{4,6},{6,4},{5,7},{7,5},{8,10},{10,8},{9,1... | collective-permute-start | bytes 516104 | tf_op jit(solution)/shard_map/ppermute | solution.py:23
  24.4 27.6 %collective-permute-start.5 = (bf16[384,896]{1,0:T(8,128)(2,1)}, bf16[384,896]{1,0:T(8,128)(2,1)}, u32[]{:S(2)}, u32[]{:S(2)}) collective-permute-start(bf16[384,896]{1,0:T(8,128)(2,1)} %join.1.refs_0_), channel_id=1, source_target_pairs={{0,18},{2,16},{16,2},{18,0},{1,19},{3,17},{17,3},{19,1},{4,22},{6,... | collective-permute-start | bytes 2064392 | tf_op jit(solution)/shard_map/ppermute | solution.py:669
  26.8 29.8 %collective-permute-start.4 = (bf16[384,896]{1,0:T(8,128)(2,1)}, bf16[384,896]{1,0:T(8,128)(2,1)}, u32[]{:S(2)}, u32[]{:S(2)}) collective-permute-start(bf16[384,896]{1,0:T(8,128)(2,1)} %join.1.refs_0_), channel_id=1, source_target_pairs={{0,16},{16,0},{1,17},{17,1},{2,18},{18,2},{3,19},{19,3},{4,20},{20... | collective-permute-start | bytes 2064392 | tf_op jit(solution)/shard_map/ppermute | solution.py:23
  27.3 29.4 %collective-permute-start.3 = (bf16[384,896]{1,0:T(8,128)(2,1)}, bf16[384,896]{1,0:T(8,128)(2,1)}, u32[]{:S(2)}, u32[]{:S(2)}) collective-permute-start(bf16[384,896]{1,0:T(8,128)(2,1)} %join.1.refs_0_), channel_id=1, source_target_pairs={{0,2},{2,0},{1,3},{3,1},{4,6},{6,4},{5,7},{7,5},{8,10},{10,8},{9,1... | collective-permute-start | bytes 2064392 | tf_op jit(solution)/shard_map/ppermute | solution.py:23
  35.8 16.2 %collective-permute-start.11 = (bf16[272,896]{1,0:T(8,128)(2,1)}, bf16[272,896]{1,0:T(8,128)(2,1)S(1)}, u32[]{:S(2)}, u32[]{:S(2)}) collective-permute-start(bf16[272,896]{1,0:T(8,128)(2,1)} %get-tuple-element.42), channel_id=1, source_target_pairs={{0,4},{4,8},{8,12},{12,0},{1,5},{5,9},{9,13},{13,1},{2,6},{6,10},{... | collective-permute-start | bytes 1462280 | tf_op jit(solution)/shard_map/ppermute | solution.py:23
  39.3 26.0 %collective-permute-start.2 = (bf16[192,896]{1,0:T(8,128)(2,1)}, bf16[192,896]{1,0:T(8,128)(2,1)S(1)}, u32[]{:S(2)}, u32[]{:S(2)}) collective-permute-start(bf16[192,896]{1,0:T(8,128)(2,1)} %copy-done.5), channel_id=1, source_target_pairs={{0,4},{4,8},{8,12},{12,0},{1,5},{5,9},{9,13},{13,1},{2,6},{6,10},{... | collective-permute-start | bytes 1032200 | tf_op jit(solution)/shard_map/ppermute | solution.py:23
  52.0 16.8 %collective-permute-start.13 = (bf16[272,896]{1,0:T(8,128)(2,1)}, bf16[272,896]{1,0:T(8,128)(2,1)S(1)}, u32[]{:S(2)}, u32[]{:S(2)}) collective-permute-start(bf16[272,896]{1,0:T(8,128)(2,1)} %copy-done.13), channel_id=1, source_target_pairs={{0,12},{4,0},{8,4},{12,8},{1,13},{5,1},{9,5},{13,9},{2,14},{6,2},{... | collective-permute-start | bytes 1462280 | tf_op jit(solution)/shard_map/ppermute | solution.py:23
  64.9 24.3 %collective-permute-start.12 = (bf16[272,896]{1,0:T(8,128)(2,1)S(1)}, bf16[272,896]{1,0:T(8,128)(2,1)S(1)}, u32[]{:S(2)}, u32[]{:S(2)}) collective-permute-start(bf16[272,896]{1,0:T(8,128)(2,1)S(1)} %get-tuple-element.44), channel_id=1, source_target_pairs={{0,8},{4,12},{8,0},{12,4},{1,9},{5,13},{9,1},{13,5},{2,10},{6,14},... | collective-permute-start | bytes 1462280 | tf_op jit(solution)/shard_map/ppermute | solution.py:23
  65.3 27.0 %collective-permute-start.8 = (bf16[192,896]{1,0:T(8,128)(2,1)S(1)}, bf16[192,896]{1,0:T(8,128)(2,1)S(1)}, u32[]{:S(2)}, u32[]{:S(2)}) collective-permute-start(bf16[192,896]{1,0:T(8,128)(2,1)S(1)} %collective-permute-done.2.refs_3_), channel_id=1, source_target_pairs={{0,18},{2,16},{16,2},{18,0},{1,19},{3,17},{17,3},{19,1},{4,22},{6,... | collective-permute-start | bytes 1032200 | tf_op jit(solution)/shard_map/ppermute | solution.py:669
  67.0 26.1 %collective-permute-start.7 = (bf16[192,896]{1,0:T(8,128)(2,1)S(1)}, bf16[192,896]{1,0:T(8,128)(2,1)S(1)}, u32[]{:S(2)}, u32[]{:S(2)}) collective-permute-start(bf16[192,896]{1,0:T(8,128)(2,1)S(1)} %collective-permute-done.2.refs_3_), channel_id=1, source_target_pairs={{0,16},{16,0},{1,17},{17,1},{2,18},{18,2},{3,19},{19,3},{4,20},{20... | collective-permute-start | bytes 1032200 | tf_op jit(solution)/shard_map/ppermute | solution.py:23
  68.3 24.8 %collective-permute-start.6 = (bf16[192,896]{1,0:T(8,128)(2,1)S(1)}, bf16[192,896]{1,0:T(8,128)(2,1)S(1)}, u32[]{:S(2)}, u32[]{:S(2)}) collective-permute-start(bf16[192,896]{1,0:T(8,128)(2,1)S(1)} %collective-permute-done.2.refs_3_), channel_id=1, source_target_pairs={{0,2},{2,0},{1,3},{3,1},{4,6},{6,4},{5,7},{7,5},{8,10},{10,8},{9,1... | collective-permute-start | bytes 1032200 | tf_op jit(solution)/shard_map/ppermute | solution.py:23
  103.5 10.3 %collective-permute-start.20 = (bf16[128,896]{1,0:T(8,128)(2,1)S(1)}, bf16[128,896]{1,0:T(8,128)(2,1)S(1)}, u32[]{:S(2)}, u32[]{:S(2)}) collective-permute-start(bf16[128,896]{1,0:T(8,128)(2,1)S(1)} %get-tuple-element.54), channel_id=1, source_target_pairs={{0,4},{4,8},{8,12},{12,0},{1,5},{5,9},{9,13},{13,1},{2,6},{6,10},{... | collective-permute-start | bytes 688136 | tf_op jit(solution)/shard_map/ppermute | solution.py:23
  103.5 13.0 %collective-permute-start.21 = (bf16[128,896]{1,0:T(8,128)(2,1)S(1)}, bf16[128,896]{1,0:T(8,128)(2,1)S(1)}, u32[]{:S(2)}, u32[]{:S(2)}) collective-permute-start(bf16[128,896]{1,0:T(8,128)(2,1)S(1)} %get-tuple-element.55), channel_id=1, source_target_pairs={{0,12},{4,0},{8,4},{12,8},{1,13},{5,1},{9,5},{13,9},{2,14},{6,2},{... | collective-permute-start | bytes 688136 | tf_op jit(solution)/shard_map/ppermute | solution.py:23
  110.2 9.7 %collective-permute-start.18 = (bf16[256,256]{1,0:T(8,128)(2,1)S(1)}, bf16[256,256]{1,0:T(8,128)(2,1)S(1)}, u32[]{:S(2)}, u32[]{:S(2)}) collective-permute-start(bf16[256,256]{1,0:T(8,128)(2,1)S(1)} %get-tuple-element.53.refs_0_), channel_id=1, source_target_pairs={{0,4},{4,8},{8,12},{1,5},{5,9},{9,13},{2,6},{6,10},{10,14},{3,7},{... | collective-permute-start | bytes 393224 | tf_op jit(solution)/shard_map/ppermute | solution.py:29
  125.1 10.1 %collective-permute-start.24 = (f32[128,256]{1,0:T(8,128)S(1)}, f32[128,256]{1,0:T(8,128)S(1)}, u32[]{:S(2)}, u32[]{:S(2)}) collective-permute-start(f32[128,256]{1,0:T(8,128)S(1)} %get-tuple-element.61), channel_id=1, source_target_pairs={{4,0},{8,4},{12,8},{5,1},{9,5},{13,9},{6,2},{10,6},{14,10},{7,3},{... | collective-permute-start | bytes 393224 | tf_op jit(solution)/shard_map/ppermute | solution.py:29
  126.4 16.4 %collective-permute-start.25 = (f32[128,256]{1,0:T(8,128)S(1)}, f32[128,256]{1,0:T(8,128)S(1)}, u32[]{:S(2)}, u32[]{:S(2)}) collective-permute-start(f32[128,256]{1,0:T(8,128)S(1)} %get-tuple-element.62), channel_id=1, source_target_pairs={{8,0},{12,4},{9,1},{13,5},{10,2},{14,6},{11,3},{15,7},{24,16},{28,... | collective-permute-start | bytes 393224 | tf_op jit(solution)/shard_map/ppermute | solution.py:29
  127.7 15.3 %collective-permute-start.22 = (bf16[128,512]{1,0:T(8,128)(2,1)S(1)}, bf16[128,512]{1,0:T(8,128)(2,1)S(1)}, u32[]{:S(2)}, u32[]{:S(2)}) collective-permute-start(bf16[128,512]{1,0:T(8,128)(2,1)S(1)} %get-tuple-element.57.own_query), channel_id=1, source_target_pairs={{0,1},{1,0},{2,3},{3,2},{4,5},{5,4},{6,7},{7,6},{8,9},{9,8},{10,11... | collective-permute-start | bytes 393224 | tf_op jit(solution)/shard_map/ppermute | solution.py:23
  150.1 10.5 %collective-permute-start.29 = (bf16[128,128]{1,0:T(8,128)(2,1)S(1)}, bf16[128,128]{1,0:T(8,128)(2,1)S(1)}, u32[]{:S(2)}, u32[]{:S(2)}) collective-permute-start(bf16[128,128]{1,0:T(8,128)(2,1)S(1)} %get-tuple-element.69), channel_id=1, source_target_pairs={{0,8},{4,12},{8,0},{12,4},{1,9},{5,13},{9,1},{13,5},{2,10},{6,14},... | collective-permute-start | bytes 98312 | tf_op jit(solution)/shard_map/ppermute | solution.py:23
  154.0 13.4 %collective-permute-start.27 = (bf16[128,896]{1,0:T(8,128)(2,1)S(1)}, bf16[128,896]{1,0:T(8,128)(2,1)S(1)}, u32[]{:S(2)}, u32[]{:S(2)}) collective-permute-start(bf16[128,896]{1,0:T(8,128)(2,1)S(1)} %get-tuple-element.67), channel_id=1, source_target_pairs={{0,8},{4,12},{8,0},{12,4},{1,9},{5,13},{9,1},{13,5},{2,10},{6,14},... | collective-permute-start | bytes 688136 | tf_op jit(solution)/shard_map/ppermute | solution.py:23
  162.4 10.9 %collective-permute-start.34 = (f32[192,448]{1,0:T(8,128)S(1)}, f32[192,448]{1,0:T(8,128)S(1)}, u32[]{:S(2)}, u32[]{:S(2)}) collective-permute-start(f32[192,448]{1,0:T(8,128)S(1)} %get-tuple-element.76), channel_id=1, source_target_pairs={{0,2},{2,0},{1,3},{3,1},{4,6},{6,4},{5,7},{7,5},{8,10},{10,8},{9,1... | collective-permute-start | bytes 1032200 | tf_op jit(solution)/shard_map/ppermute | solution.py:23
  164.0 9.3 %collective-permute-start.35 = (f32[96,80]{1,0:T(8,128)S(1)}, f32[96,80]{1,0:T(8,128)S(1)}, u32[]{:S(2)}, u32[]{:S(2)}) collective-permute-start(f32[96,80]{1,0:T(8,128)S(1)} %get-tuple-element.77), channel_id=1, source_target_pairs={{0,2},{2,0},{1,3},{3,1},{4,6},{6,4},{5,7},{7,5},{8,10},{10,8},{9,1... | collective-permute-start | bytes 92168 | tf_op jit(solution)/shard_map/ppermute | solution.py:23
  (27 other events, 264.6 us)

commit v10 on v7

--- a/solution.py
+++ b/solution.py
@@ -164,11 +164,15 @@
                 ]
 
 
-def cut_kernel(unused, seq_count, tokens, *refs):
-    for steps, block in enumerate(refs[unused:]):
+def cut_kernel(unused, seq_count, tokens, payload, *refs):
+    blocks = refs[unused:]
+    for steps, block in enumerate(blocks):
         target = ring_index(lax.axis_index("seq") + steps - seq_count, seq_count)
         width = block.shape[1]
-        block[...] = tokens[:, pl.ds(pl.multiple_of(target * width, 128), width)]
+        rows = block.shape[0] - tokens.shape[0]
+        if rows:
+            block[:rows] = payload[...]
+        block[rows:] = tokens[:, pl.ds(pl.multiple_of(target * width, 128), width)]
 
 
 def assemble_up(seq_count, arrived, up_blocks):
@@ -200,7 +204,7 @@
 def project_kernel(array_count, entries, up_entries, unused, seq_count, tokens, *refs):
     arrays = refs[:array_count]
     refs = refs[array_count + unused :]
-    part, matrix = refs[:2]
+    own_query, sent_query, rest, matrix = refs[:4]
     weights, semaphore = refs[-2:]
     copies = []
     for number, start, height, place in entries:
@@ -208,8 +212,8 @@
         copies.append(fetch(piece, weights, place, semaphore.at[len(copies)]))
     for number, start, slot in up_entries:
         copy = pltpu.make_async_copy(
-            arrays[number].at[pl.ds(start, refs[3].shape[1])],
-            refs[3].at[slot],
+            arrays[number].at[pl.ds(start, refs[5].shape[1])],
+            refs[5].at[slot],
             semaphore.at[len(copies)],
         )
         copy.start()
@@ -218,9 +222,15 @@
         copy.wait()
     keep = pltpu.make_async_copy(weights, matrix, semaphore.at[len(copies)])
     keep.start()
-    part[...] = dot_nt(tokens[...], weights[...])
+    part = dot_nt(tokens[...], weights[...])
+    own_rows, query_columns = own_query.shape
+    first = lax.axis_index("tp") == 0
+    upper, lower = part[:own_rows, :query_columns], part[own_rows:, :query_columns]
+    own_query[...] = jnp.where(first, upper, lower)
+    sent_query[...] = jnp.where(first, lower, upper)
+    rest[...] = part[:, query_columns:]
     if up_entries:
-        assemble_up(seq_count, refs[3], refs[2])
+        assemble_up(seq_count, refs[5], refs[4])
     keep.wait()
 
 
@@ -228,19 +238,17 @@
     return values * cosines + pltpu.roll(values, values.shape[1] // 2, 1) * sines
 
 
-def qkv_kernel(seq_count, unused, lengths, mine, theirs, up_blocks, cosines, sines, *refs):
+def qkv_kernel(
+    seq_count, unused, lengths, own_query, other_query, mine, theirs, up_blocks, cosines, sines, *refs
+):
     queries, pairs, low_rank = refs[unused:]
-    rows = mine.shape[0]
-    own_rows = queries.shape[0] // QHEADS
-    query_columns = QHEADS * HEAD_WIDTH
-    value_start = query_columns + HEAD_WIDTH
-    features = value_start + HEAD_WIDTH
-    joint_rank = low_rank.shape[1]
-    middle = features + joint_rank
+    rows, joint_rank = low_rank.shape
+    own_rows, query_columns = own_query.shape
+    start_low, middle = 2 * HEAD_WIDTH, 2 * HEAD_WIDTH + joint_rank
     ends = kernel_marks(lengths)
 
     def low_rows(picked, second):
-        first_low = mine[picked, features:middle] + theirs[picked, features:middle]
+        first_low = mine[picked, start_low:middle] + theirs[picked, start_low:middle]
         second_low = mine[picked, middle:] + theirs[picked, middle:]
         return jnp.where(second, second_low, first_low).astype(jnp.bfloat16)
 
@@ -253,9 +261,9 @@
     for document in range(SEGS):
         chosen = jnp.where(segments == document, low, jnp.zeros_like(low))
         value_delta += dot_nn(chosen, up_blocks[document, :, query_columns:])
-    keys = mine[:, query_columns:value_start] + theirs[:, query_columns:value_start]
+    keys = mine[:, :HEAD_WIDTH] + theirs[:, :HEAD_WIDTH]
     pairs[:, :HEAD_WIDTH] = rotated(keys, cosines[...], sines[...]).astype(jnp.bfloat16)
-    values = mine[:, value_start:features] + theirs[:, value_start:features]
+    values = mine[:, HEAD_WIDTH:start_low] + theirs[:, HEAD_WIDTH:start_low]
     pairs[:, HEAD_WIDTH:] = (values + adapter_scale * value_delta).astype(jnp.bfloat16)
     start = pl.multiple_of(lax.axis_index("tp") * own_rows, own_rows)
     own = pl.ds(start, own_rows)
@@ -265,7 +273,7 @@
     for document in range(SEGS):
         chosen = jnp.where(own_segments == document, own_low, jnp.zeros_like(own_low))
         query_delta += dot_nn(chosen, up_blocks[document, :, :query_columns])
-    projected = mine[own, :query_columns] + theirs[own, :query_columns]
+    projected = own_query[...] + other_query[...]
     projected = projected + adapter_scale * query_delta
     for head in range(QHEADS):
         turned = rotated(
@@ -334,13 +342,13 @@
         ).astype(jnp.bfloat16)
 
 
-def sum_kernel(kept, arrived, *sums):
-    for back, total in enumerate(sums):
+def sum_kernel(unused, kept, arrived, *refs):
+    for back, total in enumerate(refs[unused:]):
         total[...] = kept[back] + arrived[back]
 
 
 def pair_kernel(terms, cosines, sines, *refs):
-    parts, pair = refs[:terms], refs[-2]
+    parts, pair = refs[:terms], refs[-1]
     own_rows = pair.shape[0]
     total = sum(part[...] for part in parts)
     own = pl.ds(pl.multiple_of(lax.axis_index("tp") * own_rows, own_rows), own_rows)
@@ -442,7 +450,8 @@
             holder = ring_index(lax.axis_index("seq") - behind, block_count)
             segments = row_segments(ends, row_positions(holder * rows, rows))
             chosen = jnp.where(segments == document, lows[behind], jnp.zeros_like(lows[behind]))
-            total += dot_tn(chosen, columns[behind][...])
+            first_row = columns[behind].shape[0] - rows
+            total += dot_tn(chosen, columns[behind][first_row:])
         all_terms.append(total)
     down_terms = jnp.concatenate(all_terms, axis=0)
     if not packed:
@@ -633,9 +642,25 @@
         forward = shift(forward, "seq", 1)
         middle = forward[:frozen_rows]
         middle_parts = over_plane(middle)
-        payloads = [shift(part, "seq", steps + 2) for steps, part in enumerate(payloads)]
-        arrays = [frozen_qkv_matrix, before, after, forward, payload] + payloads
-        arrays += plane_parts + middle_parts
+        near_payload = shift(payloads[1], "seq", 3)
+        early = [plane, down_zeros, up_zeros, cosines, sines, bank_rows]
+        block_shapes = [(rows, down_width)] * seq_count
+        block_shapes[2] = (rows + payload_rows, down_width)
+        column_blocks = pl.pallas_call(
+            functools.partial(cut_kernel, len(early), seq_count),
+            out_shape=[jax.ShapeDtypeStruct(shape, bf16) for shape in block_shapes],
+            in_specs=[in_vmem()] * 2 + [in_place()] * len(early),
+            out_specs=[by_block(shape) for shape in block_shapes],
+            compiler_params=pltpu.CompilerParams(vmem_limit_bytes=16 * mebibyte),
+            cost_estimate=cost(0, 4 * rows * width),
+            name="cut",
+        )(local_tokens, payloads[0], *early)
+        column_parts = [
+            shift(block, "seq", steps) if steps else block
+            for steps, block in enumerate(column_blocks)
+        ]
+        arrays = [frozen_qkv_matrix, before, after, forward, payload]
+        arrays += [column_parts[2], near_payload] + plane_parts + middle_parts
 
         def frozen_at(behind, batch_step, group_step):
             return frozen_place(seq_count, frozen_rows, share, behind, batch_step, group_step)
@@ -661,16 +686,6 @@
                 (7 + number, frozen_rows, frozen_rows, frozen_at(3, batch_step, group_step)),
                 (10 + number, 0, frozen_rows, frozen_at(2, batch_step, group_step)),
             ]
-        early = [forward, down_zeros, up_zeros, cosines, sines, bank_rows]
-        column_blocks = pl.pallas_call(
-            functools.partial(cut_kernel, len(early), seq_count),
-            out_shape=[jax.ShapeDtypeStruct((rows, down_width), bf16)] * seq_count,
-            in_specs=[in_vmem()] + [in_place()] * len(early),
-            out_specs=[by_block((rows, down_width))] * seq_count,
-            compiler_params=pltpu.CompilerParams(vmem_limit_bytes=16 * mebibyte),
-            cost_estimate=cost(0, 4 * rows * width),
-            name="cut",
-        )(local_tokens, *early)
     else:
         bank_rows = sample_rows.reshape(-1)
         got_down = lax.all_to_all(
@@ -712,25 +727,27 @@
             for steps in range(seq_count)
         ]
 
-    column_parts = [
-        shift(block, "seq", steps) if steps else block
-        for steps, block in enumerate(column_blocks)
-    ]
-    early = [column_parts[2]] if direct and seq_count > 3 else []
+    if not direct:
+        column_parts = [
+            shift(block, "seq", steps) if steps else block
+            for steps, block in enumerate(column_blocks)
+        ]
     up_shape = (SEGS, joint_rank, query_columns + HEAD_WIDTH)
     matrix_rows = features + 2 * joint_rank
     arrived = [pltpu.VMEM((seq_count, low_width // 2, down_width), bf16)] if direct else []
-    part, matrix, *built = pl.pallas_call(
+    own_part, sent_part, rest_part, matrix, *built = pl.pallas_call(
         functools.partial(
-            project_kernel, len(arrays), entries, up_entries, len(early), seq_count
+            project_kernel, len(arrays), entries, up_entries, 0, seq_count
         ),
         out_shape=[
-            jax.ShapeDtypeStruct((rows, matrix_rows), f32),
+            jax.ShapeDtypeStruct((own_rows, query_columns), f32),
+            jax.ShapeDtypeStruct((own_rows, query_columns), f32),
+            jax.ShapeDtypeStruct((rows, matrix_rows - query_columns), f32),
             jax.ShapeDtypeStruct((matrix_rows, width), bf16),
         ]
         + ([jax.ShapeDtypeStruct(up_shape, bf16)] if direct else []),
-        in_specs=[in_vmem()] + [in_place()] * (len(arrays) + len(early)),
-        out_specs=[in_vmem(), in_place()] + ([by_block(up_shape)] if direct else []),
+        in_specs=[in_vmem()] + [in_place()] * len(arrays),
+        out_specs=[in_vmem()] * 3 + [in_place()] + ([by_block(up_shape)] if direct else []),
         scratch_shapes=arrived
         + [
             pltpu.VMEM((matrix_rows, width), bf16),
@@ -739,24 +756,28 @@
         compiler_params=pltpu.CompilerParams(vmem_limit_bytes=20 * mebibyte),
         cost_estimate=cost(2 * rows * width * matrix_rows, 2 * width * (matrix_rows + rows)),
         name="project",
-    )(local_tokens, *arrays, *early)
+    )(local_tokens, *arrays)
     if direct:
         up_blocks = built[0]
 
-    other_part = shift(part, "tp", 1)
+    other_part = shift(sent_part, "tp", 1)
+    other_rest = shift(rest_part, "tp", 1)
+    due = [column_parts[1]] if direct else []
     queries, pairs, low_rank = pl.pallas_call(
-        functools.partial(qkv_kernel, seq_count, 1),
+        functools.partial(qkv_kernel, seq_count, len(due)),
         out_shape=(
             jax.ShapeDtypeStruct((QHEADS * own_rows, HEAD_WIDTH), bf16),
             jax.ShapeDtypeStruct((rows, 2 * HEAD_WIDTH), bf16),
             jax.ShapeDtypeStruct((rows, joint_rank), bf16),
         ),
-        in_specs=[in_smem()] + [in_vmem()] * 5 + [in_place()],
+        in_specs=[in_smem()] + [in_vmem()] * 7 + [in_place()] * len(due),
         out_specs=(in_vmem(),) * 3,
         compiler_params=pltpu.CompilerParams(vmem_limit_bytes=8 * mebibyte),
         cost_estimate=cost(2 * rows * 3 * 64 * 640, 8 * rows * features),
         name="qkv",
-    )(document_lengths, part, other_part, up_blocks, cosines, sines, column_parts[1])
+    )(
+        document_lengths, own_part, other_part, rest_part, other_rest, up_blocks, cosines, sines, *due
+    )
 
     blocks = [pairs] + [push(pairs, "seq", back) for back in range(1, half_count + 1)]
     block_count = len(blocks)
@@ -785,31 +806,27 @@
     )(document_lengths, queries, incoming, cosines, sines, *blocks, *early_columns)
 
     other_query = shift(query_grad, "tp", 1)
+    due = [column_parts[-1]] if direct else []
     pair_sums = pl.pallas_call(
-        sum_kernel,
+        functools.partial(sum_kernel, len(due)),
         out_shape=[jax.ShapeDtypeStruct((own_rows, 2 * HEAD_WIDTH), f32)] * block_count,
-        in_specs=[in_vmem()] * 2,
+        in_specs=[in_vmem()] * 2 + [in_place()] * len(due),
         out_specs=[in_vmem()] * block_count,
         compiler_params=pltpu.CompilerParams(vmem_limit_bytes=8 * mebibyte),
         cost_estimate=cost(0, 12 * block_count * own_rows * 2 * HEAD_WIDTH),
         name="pair_sums",
-    )(kept, shift(sent, "tp", 1))
+    )(kept, shift(sent, "tp", 1), *due)
     pair_terms = [pair_sums[0]]
     pair_terms += [push(pair_sums[back], "seq", -back) for back in range(1, block_count)]
-    pair_grad, late_block = pl.pallas_call(
+    pair_grad = pl.pallas_call(
         functools.partial(pair_kernel, block_count),
-        out_shape=[
-            jax.ShapeDtypeStruct((own_rows, 2 * HEAD_WIDTH), bf16),
-            jax.ShapeDtypeStruct((rows, down_width), bf16),
-        ],
-        in_specs=[in_vmem()] * (2 + block_count) + [in_place()],
-        out_specs=[in_vmem(), in_place()],
-        input_output_aliases={2 + block_count: 1},
+        out_shape=jax.ShapeDtypeStruct((own_rows, 2 * HEAD_WIDTH), bf16),
+        in_specs=[in_vmem()] * (2 + block_count),
+        out_specs=in_vmem(),
         compiler_params=pltpu.CompilerParams(vmem_limit_bytes=8 * mebibyte),
         cost_estimate=cost(0, 12 * block_count * own_rows * 2 * HEAD_WIDTH),
         name="pair_gradients",
-    )(cosines, sines, *pair_terms, column_blocks[-1])
-    column_parts[-1] = shift(late_block, "seq", seq_count - 1)
+    )(cosines, sines, *pair_terms)
     other_pair = shift(pair_grad, "tp", 1)
 
     split_shapes = [(SEGS * low_width, up_width)] * seq_count

time: 163 us -> 182 us (1.12)
  starting transfers between devices: 40.1 us -> 70.1 us
  waiting for transfers between devices: 75.8 us -> 67.7 us
    ppermute x22, starting transfers between devices: 28.6 us -> 47.8 us  [shift(): lax.ppermute(value, axis, [(at, (at + steps) % count) for at in range(cou...]
    ppermute x4, starting transfers between devices: 6.52 us -> 17.5 us  [push(): return lax.ppermute(value, axis, pairs)]
    ppermute x22, waiting for transfers between devices: 52.1 us -> 44.6 us  [shift(): lax.ppermute(value, axis, [(at, (at + steps) % count) for at in range(cou...]
    ppermute x2, waiting for transfers between devices: 6.78 us -> 0.01 us  [over_plane(): lax.ppermute(value, ('groups', 'batch'), over_both)]
    ppermute x4, waiting for transfers between devices: 16.9 us -> 23 us  [push(): return lax.ppermute(value, axis, pairs)]
    unnamed x19 -> x15, local copies, waits for them, and re-layouts: 5.42 us -> 4.02 us
  transfers between devices with their start and end apart: 28 -> 28, of which waited for: 20 -> 13; matrix products, arithmetic and copies ran while one was open for 10% -> 9% of each run, Pallas kernels for 4% -> 7%
where the time goes in v10:
time: 182 us; the launch traced here: 181 us
  starting transfers between devices  70.1 us (39%)
  waiting for transfers between devices  67.7 us (37%)
  Pallas kernels  20.8 us (11%)
  local copies, waits for them, and re-layouts  17.6 us (10%)
  other arithmetic  2.41 us (1%)
  between operations  2.27 us (1%)
    ppermute x22, starting transfers between devices, shift(): lax.ppermute(value, axis, [(at, (at + steps) % count) for at in range(cou...  47.8 us
    ppermute x22, waiting for transfers between devices, shift(): lax.ppermute(value, axis, [(at, (at + steps) % count) for at in range(cou...  44.6 us
    ppermute x4, waiting for transfers between devices, push(): return lax.ppermute(value, axis, pairs)  23 us
    ppermute x4, starting transfers between devices, push(): return lax.ppermute(value, axis, pairs)  17.5 us
    ppermute x2, starting transfers between devices, over_plane(): lax.ppermute(value, ('groups', 'batch'), over_both)  4.82 us
    pallas_call x1, Pallas kernels, shards(): pl.pallas_call(token_kernel, grid=(width // chunk,), out_shape=jax.ShapeD...  4.82 us
    broadcast_in_dim x1, local copies, waits for them, and re-layouts, shards(): down_zeros = jnp.zeros((adapters, joint_rank, 1, held_down), f32)  4.53 us
    unnamed x15, local copies, waits for them, and re-layouts  4.02 us
  transfers between devices with their start and end apart: 28, of which 13 were waited for; matrix products, arithmetic and copies ran while one was open for 9% of the time, Pallas kernels for 7%

profile of v10, /device:TPU:0, one launch (start us, length us, event | category | flops | bytes accessed | tf_op | source)
XLA Modules:
  0.0 180.9 jit_solution(15943935240589669283)
XLA Ops:
  1.7 5.1 %collective-permute-start.1 = (bf16[192,896]{1,0:T(8,128)(2,1)S(1)}, bf16[192,896]{1,0:T(8,128)(2,1)S(1)}, u32[]{:S(2)}, u32[]{:S(2)}) collective-permute-start(bf16[192,896]{1,0:T(8,128)(2,1)S(1)} %constant_dynamic-slice_fusion.1), channel_id=1, source_target_pairs={{0,12},{4,0},{8,4},{12,8},{1,13},{5,1},{9,5},{13,9},{2,14},{6,2},{... | collective-permute-start | bytes 1032200 | tf_op jit(solution)/shard_map/ppermute | solution.py:23
  10.8 2.7 %gather_fusion.1 = bf16[3,64,448]{2,1,0:T(8,128)(2,1)S(1)} fusion(bf16[64,64,448]{2,1,0:T(8,128)(2,1)} %bitcast.19, s32[1024]{0:T(1024)S(1)} %pad_clamp_fusion), kind=kCustom, calls=%fused_computation.1 | custom fusion | bytes 344076 | tf_op jit(solution)/shard_map/gather | solution.py:613
  16.0 2.7 %gather_fusion = bf16[3,64,448]{2,1,0:T(8,128)(2,1)S(1)} fusion(bf16[64,64,448]{2,1,0:T(8,128)(2,1)} %bitcast.20, s32[1024]{0:T(1024)S(1)} %pad_clamp_fusion.1), kind=kCustom, calls=%fused_computation | custom fusion | bytes 344076 | tf_op jit(solution)/shard_map/gather | solution.py:615
  19.7 2.7 %collective-permute-done.before.refs_1_ = bf16[192,896]{1,0:T(8,128)(2,1)S(1)} collective-permute-done((bf16[192,896]{1,0:T(8,128)(2,1)S(1)}, bf16[192,896]{1,0:T(8,128)(2,1)S(1)}, u32[]{:S(2)}, u32[]{:S(2)}) %collective-permute-start) | collective-permute-done | bytes 344096 | tf_op jit(solution)/shard_map/ppermute | solution.py:23
  27.2 2.5 %collective-permute-start.9 = (bf16[384,896]{1,0:T(8,128)(2,1)S(1)}, bf16[384,896]{1,0:T(8,128)(2,1)S(1)}, u32[]{:S(2)}, u32[]{:S(2)}) collective-permute-start(bf16[384,896]{1,0:T(8,128)(2,1)S(1)} %get-tuple-element.42.refs_0_), channel_id=1, source_target_pairs={{0,18},{2,16},{16,2},{18,0},{1,19},{3,17},{17,3},{19,1},{4,22},{6,... | collective-permute-start | bytes 2064392 | tf_op jit(solution)/shard_map/ppermute | solution.py:638
  31.0 4.5 %broadcast_in_dim.47.refs_1_.down_zeros = f32[64,64,1,448]{3,2,1,0:T(1,128)S(1)} broadcast(f32[]{:T(128)} %constant.11.clone.1), dimensions={} | broadcast | bytes 7340036 | tf_op jit(solution)/shard_map/broadcast_in_dim | solution.py:587
  35.7 3.2 %copy-done.1 = f32[64,64,1,448]{3,2,1,0:T(1,128)} copy-done((f32[64,64,1,448]{3,2,1,0:T(1,128)}, f32[64,64,1,448]{3,2,1,0:T(1,128)S(1)}, u32[]{:S(2)}) %copy-start.1) | copy-done | bytes 7340056
  41.9 16.6 %collective-permute-done.6.refs_6_ = bf16[144,896]{1,0:T(8,128)(2,1)S(1)} collective-permute-done((bf16[144,896]{1,0:T(8,128)(2,1)S(1)}, bf16[144,896]{1,0:T(8,128)(2,1)S(1)}, u32[]{:S(2)}, u32[]{:S(2)}) %collective-permute-start.6) | collective-permute-done | bytes 258080 | tf_op jit(solution)/shard_map/ppermute | solution.py:23
  62.0 28.5 %collective-permute-start.15 = (bf16[256,896]{1,0:T(8,128)(2,1)S(1)}, bf16[256,896]{1,0:T(8,128)(2,1)S(1)}, u32[]{:S(2)}, u32[]{:S(2)}) collective-permute-start(bf16[256,896]{1,0:T(8,128)(2,1)S(1)} %get-tuple-element.49), channel_id=1, source_target_pairs={{0,4},{4,8},{8,12},{12,0},{1,5},{5,9},{9,13},{13,1},{2,6},{6,10},{... | collective-permute-start | bytes 1376264 | tf_op jit(solution)/shard_map/ppermute | solution.py:23
  90.5 3.8 %project.1 = (f32[128,512]{1,0:T(8,128)S(1)}, f32[128,512]{1,0:T(8,128)S(1)}, f32[256,384]{1,0:T(8,128)S(1)}, bf16[896,3584]{1,0:T(8,128)(2,1)S(1)}, bf16[3,64,640]{2,1,0:T(8,128)(2,1)S(1)}) custom-call(bf16[256,3584]{1,0:T(8,128)(2,1)S(1)} %bitcast.16, bf16[192,3584]{1,0:T(8,128)(2,1)S(1)} %copy-done.4, ...), custom_call_target="tpu_custom_call" | custom-call | flops 1644167168 | bytes 8257536 | tf_op jit(solution)/shard_map/project/pallas_call | solution.py:738
  94.9 4.7 %collective-permute-done.15.refs_0_.refs_1_ = bf16[256,896]{1,0:T(8,128)(2,1)S(1)} collective-permute-done((bf16[256,896]{1,0:T(8,128)(2,1)S(1)}, bf16[256,896]{1,0:T(8,128)(2,1)S(1)}, u32[]{:S(2)}, u32[]{:S(2)}) %collective-permute-start.15) | collective-permute-done | bytes 458784 | tf_op jit(solution)/shard_map/ppermute | solution.py:23
  100.7 12.6 %collective-permute-start.17 = (bf16[256,256]{1,0:T(8,128)(2,1)S(1)}, bf16[256,256]{1,0:T(8,128)(2,1)S(1)}, u32[]{:S(2)}, u32[]{:S(2)}) collective-permute-start(bf16[256,256]{1,0:T(8,128)(2,1)S(1)} %get-tuple-element.51.refs_0_), channel_id=1, source_target_pairs={{0,8},{4,12},{1,9},{5,13},{2,10},{6,14},{3,11},{7,15},{16,24},{20,... | collective-permute-start | bytes 393224 | tf_op jit(solution)/shard_map/ppermute | solution.py:29
  113.3 2.3 %collective-permute-start.16 = (bf16[256,256]{1,0:T(8,128)(2,1)S(1)}, bf16[256,256]{1,0:T(8,128)(2,1)S(1)}, u32[]{:S(2)}, u32[]{:S(2)}) collective-permute-start(bf16[256,256]{1,0:T(8,128)(2,1)S(1)} %get-tuple-element.51.refs_0_), channel_id=1, source_target_pairs={{0,4},{4,8},{8,12},{1,5},{5,9},{9,13},{2,6},{6,10},{10,14},{3,7},{... | collective-permute-start | bytes 393224 | tf_op jit(solution)/shard_map/ppermute | solution.py:29
  116.8 2.8 %collective-permute-done.16.refs_1_ = bf16[256,256]{1,0:T(8,128)(2,1)S(1)} collective-permute-done((bf16[256,256]{1,0:T(8,128)(2,1)S(1)}, bf16[256,256]{1,0:T(8,128)(2,1)S(1)}, u32[]{:S(2)}, u32[]{:S(2)}) %collective-permute-start.16) | collective-permute-done | bytes 131104 | tf_op jit(solution)/shard_map/ppermute | solution.py:29
  119.6 3.4 %attention.1 = (bf16[128,512]{1,0:T(8,128)(2,1)}, bf16[128,512]{1,0:T(8,128)(2,1)S(1)}, f32[3,128,256]{2,1,0:T(8,128)S(1)}, f32[3,128,256]{2,1,0:T(8,128)S(1)}) custom-call(s32[2,3]{1,0:T(2,128)S(1)} %copy-done.5, bf16[512,128]{1,0:T(8,128)(2,1)S(1)} %get-tuple-element.50.queries, bf16[128,512]{1,0:T(8,128)(2,1)S(1)} %bitcast.17, ...), custom_call_target="tpu_custom_call" | custom-call | flops 503316480 | bytes 786432 | tf_op jit(solution)/shard_map/attention/pallas_call | solution.py:786
  123.0 6.0 %collective-permute-done.20.refs_0_.refs_3_ = bf16[256,896]{1,0:T(8,128)(2,1)S(1)} collective-permute-done((bf16[256,896]{1,0:T(8,128)(2,1)S(1)}, bf16[256,896]{1,0:T(8,128)(2,1)S(1)}, u32[]{:S(2)}, u32[]{:S(2)}) %collective-permute-start.20) | collective-permute-done | bytes 458784 | tf_op jit(solution)/shard_map/ppermute | solution.py:23
  131.8 11.6 %collective-permute-done.21.refs_1_ = f32[128,256]{1,0:T(8,128)S(1)} collective-permute-done((f32[128,256]{1,0:T(8,128)S(1)}, f32[128,256]{1,0:T(8,128)S(1)}, u32[]{:S(2)}, u32[]{:S(2)}) %collective-permute-start.21) | collective-permute-done | bytes 131104 | tf_op jit(solution)/shard_map/ppermute | solution.py:29
  143.3 7.5 %collective-permute-done.22.refs_2_ = f32[128,256]{1,0:T(8,128)S(1)} collective-permute-done((f32[128,256]{1,0:T(8,128)S(1)}, f32[128,256]{1,0:T(8,128)S(1)}, u32[]{:S(2)}, u32[]{:S(2)}) %collective-permute-start.22) | collective-permute-done | bytes 131104 | tf_op jit(solution)/shard_map/ppermute | solution.py:29
  153.8 3.7 %collective-permute-start.26 = (f32[248,128]{1,0:T(8,128)S(1)}, f32[248,128]{1,0:T(8,128)S(1)}, u32[]{:S(2)}, u32[]{:S(2)}) collective-permute-start(f32[248,128]{1,0:T(8,128)S(1)} %get-tuple-element.67), channel_id=1, source_target_pairs={{0,12},{4,0},{8,4},{12,8},{1,13},{5,1},{9,5},{13,9},{2,14},{6,2},{... | collective-permute-start | bytes 380936 | tf_op jit(solution)/shard_map/ppermute | solution.py:23
  157.5 4.4 %collective-permute-done.24.refs_5_ = f32[248,128]{1,0:T(8,128)S(1)} collective-permute-done((f32[248,128]{1,0:T(8,128)S(1)}, f32[248,128]{1,0:T(8,128)S(1)}, u32[]{:S(2)}, u32[]{:S(2)}) %collective-permute-start.24) | collective-permute-done | bytes 127008 | tf_op jit(solution)/shard_map/ppermute | solution.py:23
  161.8 4.5 %collective-permute-done.25.refs_6_ = f32[248,128]{1,0:T(8,128)S(1)} collective-permute-done((f32[248,128]{1,0:T(8,128)S(1)}, f32[248,128]{1,0:T(8,128)S(1)}, u32[]{:S(2)}, u32[]{:S(2)}) %collective-permute-start.25) | collective-permute-done | bytes 127008 | tf_op jit(solution)/shard_map/ppermute | solution.py:23
  169.5 4.8 %token_gradient.1 = bf16[256,3584]{1,0:T(8,128)(2,1)} custom-call(bf16[256,896]{1,0:T(8,128)(2,1)S(1)} %get-tuple-element.61.gradients, bf16[896,3584]{1,0:T(8,128)(2,1)S(1)} %get-tuple-element.62.matrix), custom_call_target="tpu_custom_call" | custom-call | flops 1644167168 | bytes 8257536 | tf_op jit(solution)/shard_map/token_gradient/pallas_call | solution.py:865
  174.3 3.6 %collective-permute-done.27.far = f32[192,512]{1,0:T(8,128)S(1)} collective-permute-done((f32[192,512]{1,0:T(8,128)S(1)}, f32[192,512]{1,0:T(8,128)S(1)}, u32[]{:S(2)}, u32[]{:S(2)}) %collective-permute-start.27) | collective-permute-done | bytes 393248 | tf_op jit(solution)/shard_map/ppermute | solution.py:23
  177.9 3.0 %bank_rows.1 = (f32[64,64,1,448]{3,2,1,0:T(1,128)}, f32[64,32,80]{2,1,0:T(8,128)}) custom-call(s32[6]{0:T(128)S(1)} %pad_add_fusion.refs_5_.bank_rows, f32[192,448]{1,0:T(8,128)S(1)} %get-tuple-element.69.own_down, f32[192,512]{1,0:T(8,128)S(1)} %collective-permute-done.27.far, ...), custom_call_target="tpu_custom_call", output_to_operand_aliasing={{0}: (4, {}), {1}: (5, {})} | custom-call | tf_op jit(solution)/shard_map/bank_rows/pallas_call | solution.py:917
  (78 shorter events, 31.3 us)
Async XLA Ops:
  1.7 18.0 %collective-permute-start.1 = (bf16[192,896]{1,0:T(8,128)(2,1)S(1)}, bf16[192,896]{1,0:T(8,128)(2,1)S(1)}, u32[]{:S(2)}, u32[]{:S(2)}) collective-permute-start(bf16[192,896]{1,0:T(8,128)(2,1)S(1)} %constant_dynamic-slice_fusion.1), channel_id=1, source_target_pairs={{0,12},{4,0},{8,4},{12,8},{1,13},{5,1},{9,5},{13,9},{2,14},{6,2},{... | collective-permute-start | bytes 1032200 | tf_op jit(solution)/shard_map/ppermute | solution.py:23
  6.8 15.6 %collective-permute-start = (bf16[192,896]{1,0:T(8,128)(2,1)S(1)}, bf16[192,896]{1,0:T(8,128)(2,1)S(1)}, u32[]{:S(2)}, u32[]{:S(2)}) collective-permute-start(bf16[192,896]{1,0:T(8,128)(2,1)S(1)} %constant_dynamic-slice_fusion.1), channel_id=1, source_target_pairs={{0,4},{4,8},{8,12},{12,0},{1,5},{5,9},{9,13},{13,1},{2,6},{6,10},{... | collective-permute-start | bytes 1032200 | tf_op jit(solution)/shard_map/ppermute | solution.py:23
  9.2 9.5 %collective-permute-start.3 = (bf16[3,32,80]{2,1,0:T(8,128)(2,1)S(1)}, bf16[3,32,80]{2,1,0:T(8,128)(2,1)S(1)}, u32[]{:S(2)}, u32[]{:S(2)}) collective-permute-start(bf16[3,32,80]{2,1,0:T(8,128)(2,1)S(1)} %gather_fusion.3), channel_id=1, source_target_pairs={{0,2},{2,0},{1,3},{3,1},{4,6},{6,4},{5,7},{7,5},{8,10},{10,8},{9,1... | collective-permute-start | bytes 46088 | tf_op jit(solution)/shard_map/ppermute | solution.py:23
  13.6 6.1 %collective-permute-start.2 = (bf16[3,64,448]{2,1,0:T(8,128)(2,1)S(1)}, bf16[3,64,448]{2,1,0:T(8,128)(2,1)S(1)}, u32[]{:S(2)}, u32[]{:S(2)}) collective-permute-start(bf16[3,64,448]{2,1,0:T(8,128)(2,1)S(1)} %gather_fusion.1), channel_id=1, source_target_pairs={{0,2},{2,0},{1,3},{3,1},{4,6},{6,4},{5,7},{7,5},{8,10},{10,8},{9,1... | collective-permute-start | bytes 516104 | tf_op jit(solution)/shard_map/ppermute | solution.py:23
  23.5 16.6 %collective-permute-start.4 = (bf16[336,896]{1,0:T(8,128)(2,1)}, bf16[336,896]{1,0:T(8,128)(2,1)S(1)}, u32[]{:S(2)}, u32[]{:S(2)}) collective-permute-start(bf16[336,896]{1,0:T(8,128)(2,1)} %get-tuple-element.39), channel_id=1, source_target_pairs={{0,4},{4,8},{8,12},{12,0},{1,5},{5,9},{9,13},{13,1},{2,6},{6,10},{... | collective-permute-start | bytes 1806344 | tf_op jit(solution)/shard_map/ppermute | solution.py:23
  27.2 33.6 %collective-permute-start.9 = (bf16[384,896]{1,0:T(8,128)(2,1)S(1)}, bf16[384,896]{1,0:T(8,128)(2,1)S(1)}, u32[]{:S(2)}, u32[]{:S(2)}) collective-permute-start(bf16[384,896]{1,0:T(8,128)(2,1)S(1)} %get-tuple-element.42.refs_0_), channel_id=1, source_target_pairs={{0,18},{2,16},{16,2},{18,0},{1,19},{3,17},{17,3},{19,1},{4,22},{6,... | collective-permute-start | bytes 2064392 | tf_op jit(solution)/shard_map/ppermute | solution.py:638
  29.7 31.6 %collective-permute-start.8 = (bf16[384,896]{1,0:T(8,128)(2,1)S(1)}, bf16[384,896]{1,0:T(8,128)(2,1)S(1)}, u32[]{:S(2)}, u32[]{:S(2)}) collective-permute-start(bf16[384,896]{1,0:T(8,128)(2,1)S(1)} %get-tuple-element.42.refs_0_), channel_id=1, source_target_pairs={{0,16},{16,0},{1,17},{17,1},{2,18},{18,2},{3,19},{19,3},{4,20},{20... | collective-permute-start | bytes 2064392 | tf_op jit(solution)/shard_map/ppermute | solution.py:23
  38.9 51.5 %collective-permute-start.5 = (bf16[400,896]{1,0:T(8,128)(2,1)S(1)}, bf16[400,896]{1,0:T(8,128)(2,1)S(1)}, u32[]{:S(2)}, u32[]{:S(2)}) collective-permute-start(bf16[400,896]{1,0:T(8,128)(2,1)S(1)} %get-tuple-element.43), channel_id=1, source_target_pairs={{0,8},{4,12},{8,0},{12,4},{1,9},{5,13},{9,1},{13,5},{2,10},{6,14},... | collective-permute-start | bytes 2150408 | tf_op jit(solution)/shard_map/ppermute | solution.py:23
  39.6 22.4 %collective-permute-start.7 = (bf16[384,896]{1,0:T(8,128)(2,1)S(1)}, bf16[384,896]{1,0:T(8,128)(2,1)S(1)}, u32[]{:S(2)}, u32[]{:S(2)}) collective-permute-start(bf16[384,896]{1,0:T(8,128)(2,1)S(1)} %get-tuple-element.42.refs_0_), channel_id=1, source_target_pairs={{0,2},{2,0},{1,3},{3,1},{4,6},{6,4},{5,7},{7,5},{8,10},{10,8},{9,1... | collective-permute-start | bytes 2064392 | tf_op jit(solution)/shard_map/ppermute | solution.py:23
  40.1 18.3 %collective-permute-start.6 = (bf16[144,896]{1,0:T(8,128)(2,1)S(1)}, bf16[144,896]{1,0:T(8,128)(2,1)S(1)}, u32[]{:S(2)}, u32[]{:S(2)}) collective-permute-start(bf16[144,896]{1,0:T(8,128)(2,1)S(1)} %get-tuple-element.44), channel_id=1, source_target_pairs={{0,12},{4,0},{8,4},{12,8},{1,13},{5,1},{9,5},{13,9},{2,14},{6,2},{... | collective-permute-start | bytes 774152 | tf_op jit(solution)/shard_map/ppermute | solution.py:23
  58.5 32.0 %collective-permute-start.12 = (bf16[192,896]{1,0:T(8,128)(2,1)S(1)}, bf16[192,896]{1,0:T(8,128)(2,1)S(1)}, u32[]{:S(2)}, u32[]{:S(2)}) collective-permute-start(bf16[192,896]{1,0:T(8,128)(2,1)S(1)} %slice.32), channel_id=1, source_target_pairs={{0,18},{2,16},{16,2},{18,0},{1,19},{3,17},{17,3},{19,1},{4,22},{6,... | collective-permute-start | bytes 1032200 | tf_op jit(solution)/shard_map/ppermute | solution.py:638
  60.8 29.7 %collective-permute-start.11 = (bf16[192,896]{1,0:T(8,128)(2,1)S(1)}, bf16[192,896]{1,0:T(8,128)(2,1)S(1)}, u32[]{:S(2)}, u32[]{:S(2)}) collective-permute-start(bf16[192,896]{1,0:T(8,128)(2,1)S(1)} %slice.32), channel_id=1, source_target_pairs={{0,16},{16,0},{1,17},{17,1},{2,18},{18,2},{3,19},{19,3},{4,20},{20... | collective-permute-start | bytes 1032200 | tf_op jit(solution)/shard_map/ppermute | solution.py:23
  61.3 29.2 %collective-permute-start.10 = (bf16[192,896]{1,0:T(8,128)(2,1)S(1)}, bf16[192,896]{1,0:T(8,128)(2,1)S(1)}, u32[]{:S(2)}, u32[]{:S(2)}) collective-permute-start(bf16[192,896]{1,0:T(8,128)(2,1)S(1)} %slice.32), channel_id=1, source_target_pairs={{0,2},{2,0},{1,3},{3,1},{4,6},{6,4},{5,7},{7,5},{8,10},{10,8},{9,1... | collective-permute-start | bytes 1032200 | tf_op jit(solution)/shard_map/ppermute | solution.py:23
  62.0 37.6 %collective-permute-start.15 = (bf16[256,896]{1,0:T(8,128)(2,1)S(1)}, bf16[256,896]{1,0:T(8,128)(2,1)S(1)}, u32[]{:S(2)}, u32[]{:S(2)}) collective-permute-start(bf16[256,896]{1,0:T(8,128)(2,1)S(1)} %get-tuple-element.49), channel_id=1, source_target_pairs={{0,4},{4,8},{8,12},{12,0},{1,5},{5,9},{9,13},{13,1},{2,6},{6,10},{... | collective-permute-start | bytes 1376264 | tf_op jit(solution)/shard_map/ppermute | solution.py:23
  100.7 16.1 %collective-permute-start.17 = (bf16[256,256]{1,0:T(8,128)(2,1)S(1)}, bf16[256,256]{1,0:T(8,128)(2,1)S(1)}, u32[]{:S(2)}, u32[]{:S(2)}) collective-permute-start(bf16[256,256]{1,0:T(8,128)(2,1)S(1)} %get-tuple-element.51.refs_0_), channel_id=1, source_target_pairs={{0,8},{4,12},{1,9},{5,13},{2,10},{6,14},{3,11},{7,15},{16,24},{20,... | collective-permute-start | bytes 393224 | tf_op jit(solution)/shard_map/ppermute | solution.py:29
  113.3 6.3 %collective-permute-start.16 = (bf16[256,256]{1,0:T(8,128)(2,1)S(1)}, bf16[256,256]{1,0:T(8,128)(2,1)S(1)}, u32[]{:S(2)}, u32[]{:S(2)}) collective-permute-start(bf16[256,256]{1,0:T(8,128)(2,1)S(1)} %get-tuple-element.51.refs_0_), channel_id=1, source_target_pairs={{0,4},{4,8},{8,12},{1,5},{5,9},{9,13},{2,6},{6,10},{10,14},{3,7},{... | collective-permute-start | bytes 393224 | tf_op jit(solution)/shard_map/ppermute | solution.py:29
  115.6 13.4 %collective-permute-start.20 = (bf16[256,896]{1,0:T(8,128)(2,1)S(1)}, bf16[256,896]{1,0:T(8,128)(2,1)S(1)}, u32[]{:S(2)}, u32[]{:S(2)}) collective-permute-start(bf16[256,896]{1,0:T(8,128)(2,1)S(1)} %get-tuple-element.56), channel_id=1, source_target_pairs={{0,12},{4,0},{8,4},{12,8},{1,13},{5,1},{9,5},{13,9},{2,14},{6,2},{... | collective-permute-start | bytes 1376264 | tf_op jit(solution)/shard_map/ppermute | solution.py:23
  129.1 14.2 %collective-permute-start.21 = (f32[128,256]{1,0:T(8,128)S(1)}, f32[128,256]{1,0:T(8,128)S(1)}, u32[]{:S(2)}, u32[]{:S(2)}) collective-permute-start(f32[128,256]{1,0:T(8,128)S(1)} %get-tuple-element.58), channel_id=1, source_target_pairs={{4,0},{8,4},{12,8},{5,1},{9,5},{13,9},{6,2},{10,6},{14,10},{7,3},{... | collective-permute-start | bytes 393224 | tf_op jit(solution)/shard_map/ppermute | solution.py:29
  130.4 20.5 %collective-permute-start.22 = (f32[128,256]{1,0:T(8,128)S(1)}, f32[128,256]{1,0:T(8,128)S(1)}, u32[]{:S(2)}, u32[]{:S(2)}) collective-permute-start(f32[128,256]{1,0:T(8,128)S(1)} %get-tuple-element.59), channel_id=1, source_target_pairs={{8,0},{12,4},{9,1},{13,5},{10,2},{14,6},{11,3},{15,7},{24,16},{28,... | collective-permute-start | bytes 393224 | tf_op jit(solution)/shard_map/ppermute | solution.py:29
  131.7 19.4 %collective-permute-start.18 = (bf16[128,512]{1,0:T(8,128)(2,1)S(1)}, bf16[128,512]{1,0:T(8,128)(2,1)S(1)}, u32[]{:S(2)}, u32[]{:S(2)}) collective-permute-start(bf16[128,512]{1,0:T(8,128)(2,1)S(1)} %get-tuple-element.53.own_query), channel_id=1, source_target_pairs={{0,1},{1,0},{2,3},{3,2},{4,5},{5,4},{6,7},{7,6},{8,9},{9,8},{10,11... | collective-permute-start | bytes 393224 | tf_op jit(solution)/shard_map/ppermute | solution.py:23
  153.6 8.2 %collective-permute-start.24 = (f32[248,128]{1,0:T(8,128)S(1)}, f32[248,128]{1,0:T(8,128)S(1)}, u32[]{:S(2)}, u32[]{:S(2)}) collective-permute-start(f32[248,128]{1,0:T(8,128)S(1)} %get-tuple-element.65), channel_id=1, source_target_pairs={{0,4},{4,8},{8,12},{12,0},{1,5},{5,9},{9,13},{13,1},{2,6},{6,10},{... | collective-permute-start | bytes 380936 | tf_op jit(solution)/shard_map/ppermute | solution.py:23
  153.7 12.7 %collective-permute-start.25 = (f32[248,128]{1,0:T(8,128)S(1)}, f32[248,128]{1,0:T(8,128)S(1)}, u32[]{:S(2)}, u32[]{:S(2)}) collective-permute-start(f32[248,128]{1,0:T(8,128)S(1)} %get-tuple-element.66), channel_id=1, source_target_pairs={{0,8},{4,12},{8,0},{12,4},{1,9},{5,13},{9,1},{13,5},{2,10},{6,14},... | collective-permute-start | bytes 380936 | tf_op jit(solution)/shard_map/ppermute | solution.py:23
  153.8 12.6 %collective-permute-start.26 = (f32[248,128]{1,0:T(8,128)S(1)}, f32[248,128]{1,0:T(8,128)S(1)}, u32[]{:S(2)}, u32[]{:S(2)}) collective-permute-start(f32[248,128]{1,0:T(8,128)S(1)} %get-tuple-element.67), channel_id=1, source_target_pairs={{0,12},{4,0},{8,4},{12,8},{1,13},{5,1},{9,5},{13,9},{2,14},{6,2},{... | collective-permute-start | bytes 380936 | tf_op jit(solution)/shard_map/ppermute | solution.py:23
  168.2 9.6 %collective-permute-start.27 = (f32[192,512]{1,0:T(8,128)S(1)}, f32[192,512]{1,0:T(8,128)S(1)}, u32[]{:S(2)}, u32[]{:S(2)}) collective-permute-start(f32[192,512]{1,0:T(8,128)S(1)} %get-tuple-element.70), channel_id=1, source_target_pairs={{0,2},{2,0},{1,3},{3,1},{4,6},{6,4},{5,7},{7,5},{8,10},{10,8},{9,1... | collective-permute-start | bytes 1179656 | tf_op jit(solution)/shard_map/ppermute | solution.py:23
  (11 other events, 131.5 us)

commit v11 on v7

--- a/solution.py
+++ b/solution.py
@@ -200,7 +200,7 @@
 def project_kernel(array_count, entries, up_entries, unused, seq_count, tokens, *refs):
     arrays = refs[:array_count]
     refs = refs[array_count + unused :]
-    part, matrix = refs[:2]
+    own_query, sent_query, rest, matrix = refs[:4]
     weights, semaphore = refs[-2:]
     copies = []
     for number, start, height, place in entries:
@@ -208,8 +208,8 @@
         copies.append(fetch(piece, weights, place, semaphore.at[len(copies)]))
     for number, start, slot in up_entries:
         copy = pltpu.make_async_copy(
-            arrays[number].at[pl.ds(start, refs[3].shape[1])],
-            refs[3].at[slot],
+            arrays[number].at[pl.ds(start, refs[5].shape[1])],
+            refs[5].at[slot],
             semaphore.at[len(copies)],
         )
         copy.start()
@@ -218,9 +218,15 @@
         copy.wait()
     keep = pltpu.make_async_copy(weights, matrix, semaphore.at[len(copies)])
     keep.start()
-    part[...] = dot_nt(tokens[...], weights[...])
+    part = dot_nt(tokens[...], weights[...])
+    own_rows, query_columns = own_query.shape
+    first = lax.axis_index("tp") == 0
+    upper, lower = part[:own_rows, :query_columns], part[own_rows:, :query_columns]
+    own_query[...] = jnp.where(first, upper, lower)
+    sent_query[...] = jnp.where(first, lower, upper)
+    rest[...] = part[:, query_columns:]
     if up_entries:
-        assemble_up(seq_count, refs[3], refs[2])
+        assemble_up(seq_count, refs[5], refs[4])
     keep.wait()
 
 
@@ -228,19 +234,17 @@
     return values * cosines + pltpu.roll(values, values.shape[1] // 2, 1) * sines
 
 
-def qkv_kernel(seq_count, unused, lengths, mine, theirs, up_blocks, cosines, sines, *refs):
+def qkv_kernel(
+    seq_count, unused, lengths, own_query, other_query, mine, theirs, up_blocks, cosines, sines, *refs
+):
     queries, pairs, low_rank = refs[unused:]
-    rows = mine.shape[0]
-    own_rows = queries.shape[0] // QHEADS
-    query_columns = QHEADS * HEAD_WIDTH
-    value_start = query_columns + HEAD_WIDTH
-    features = value_start + HEAD_WIDTH
-    joint_rank = low_rank.shape[1]
-    middle = features + joint_rank
+    rows, joint_rank = low_rank.shape
+    own_rows, query_columns = own_query.shape
+    start_low, middle = 2 * HEAD_WIDTH, 2 * HEAD_WIDTH + joint_rank
     ends = kernel_marks(lengths)
 
     def low_rows(picked, second):
-        first_low = mine[picked, features:middle] + theirs[picked, features:middle]
+        first_low = mine[picked, start_low:middle] + theirs[picked, start_low:middle]
         second_low = mine[picked, middle:] + theirs[picked, middle:]
         return jnp.where(second, second_low, first_low).astype(jnp.bfloat16)
 
@@ -253,9 +257,9 @@
     for document in range(SEGS):
         chosen = jnp.where(segments == document, low, jnp.zeros_like(low))
         value_delta += dot_nn(chosen, up_blocks[document, :, query_columns:])
-    keys = mine[:, query_columns:value_start] + theirs[:, query_columns:value_start]
+    keys = mine[:, :HEAD_WIDTH] + theirs[:, :HEAD_WIDTH]
     pairs[:, :HEAD_WIDTH] = rotated(keys, cosines[...], sines[...]).astype(jnp.bfloat16)
-    values = mine[:, value_start:features] + theirs[:, value_start:features]
+    values = mine[:, HEAD_WIDTH:start_low] + theirs[:, HEAD_WIDTH:start_low]
     pairs[:, HEAD_WIDTH:] = (values + adapter_scale * value_delta).astype(jnp.bfloat16)
     start = pl.multiple_of(lax.axis_index("tp") * own_rows, own_rows)
     own = pl.ds(start, own_rows)
@@ -265,7 +269,7 @@
     for document in range(SEGS):
         chosen = jnp.where(own_segments == document, own_low, jnp.zeros_like(own_low))
         query_delta += dot_nn(chosen, up_blocks[document, :, :query_columns])
-    projected = mine[own, :query_columns] + theirs[own, :query_columns]
+    projected = own_query[...] + other_query[...]
     projected = projected + adapter_scale * query_delta
     for head in range(QHEADS):
         turned = rotated(
@@ -410,7 +414,8 @@
         block[first_low:, low.shape[1] :] = turned[rows // 2 :].astype(jnp.float32)
 
 
-def token_kernel(gradients, matrix, token_grad):
+def token_kernel(gradients, matrix, *refs):
+    token_grad = refs[2]
     token_grad[...] = dot_nn(gradients[...], matrix[...]).astype(jnp.bfloat16)
 
 
@@ -661,7 +666,7 @@
                 (7 + number, frozen_rows, frozen_rows, frozen_at(3, batch_step, group_step)),
                 (10 + number, 0, frozen_rows, frozen_at(2, batch_step, group_step)),
             ]
-        early = [forward, down_zeros, up_zeros, cosines, sines, bank_rows]
+        early = [forward, cosines, sines, bank_rows]
         column_blocks = pl.pallas_call(
             functools.partial(cut_kernel, len(early), seq_count),
             out_shape=[jax.ShapeDtypeStruct((rows, down_width), bf16)] * seq_count,
@@ -720,17 +725,19 @@
     up_shape = (SEGS, joint_rank, query_columns + HEAD_WIDTH)
     matrix_rows = features + 2 * joint_rank
     arrived = [pltpu.VMEM((seq_count, low_width // 2, down_width), bf16)] if direct else []
-    part, matrix, *built = pl.pallas_call(
+    own_part, sent_part, rest_part, matrix, *built = pl.pallas_call(
         functools.partial(
             project_kernel, len(arrays), entries, up_entries, len(early), seq_count
         ),
         out_shape=[
-            jax.ShapeDtypeStruct((rows, matrix_rows), f32),
+            jax.ShapeDtypeStruct((own_rows, query_columns), f32),
+            jax.ShapeDtypeStruct((own_rows, query_columns), f32),
+            jax.ShapeDtypeStruct((rows, matrix_rows - query_columns), f32),
             jax.ShapeDtypeStruct((matrix_rows, width), bf16),
         ]
         + ([jax.ShapeDtypeStruct(up_shape, bf16)] if direct else []),
         in_specs=[in_vmem()] + [in_place()] * (len(arrays) + len(early)),
-        out_specs=[in_vmem(), in_place()] + ([by_block(up_shape)] if direct else []),
+        out_specs=[in_vmem()] * 3 + [in_place()] + ([by_block(up_shape)] if direct else []),
         scratch_shapes=arrived
         + [
             pltpu.VMEM((matrix_rows, width), bf16),
@@ -743,7 +750,8 @@
     if direct:
         up_blocks = built[0]
 
-    other_part = shift(part, "tp", 1)
+    other_part = shift(sent_part, "tp", 1)
+    other_rest = shift(rest_part, "tp", 1)
     queries, pairs, low_rank = pl.pallas_call(
         functools.partial(qkv_kernel, seq_count, 1),
         out_shape=(
@@ -751,12 +759,15 @@
             jax.ShapeDtypeStruct((rows, 2 * HEAD_WIDTH), bf16),
             jax.ShapeDtypeStruct((rows, joint_rank), bf16),
         ),
-        in_specs=[in_smem()] + [in_vmem()] * 5 + [in_place()],
+        in_specs=[in_smem()] + [in_vmem()] * 7 + [in_place()],
         out_specs=(in_vmem(),) * 3,
         compiler_params=pltpu.CompilerParams(vmem_limit_bytes=8 * mebibyte),
         cost_estimate=cost(2 * rows * 3 * 64 * 640, 8 * rows * features),
         name="qkv",
-    )(document_lengths, part, other_part, up_blocks, cosines, sines, column_parts[1])
+    )(
+        document_lengths, own_part, other_part, rest_part, other_rest, up_blocks, cosines, sines,
+        column_parts[1],
+    )
 
     blocks = [pairs] + [push(pairs, "seq", back) for back in range(1, half_count + 1)]
     block_count = len(blocks)
@@ -845,19 +856,30 @@
     ]
 
     chunk = 512
-    token_grad = pl.pallas_call(
+    token_grad, down_zeros, up_zeros = pl.pallas_call(
         token_kernel,
         grid=(width // chunk,),
-        out_shape=jax.ShapeDtypeStruct((rows, width), bf16),
+        out_shape=[
+            jax.ShapeDtypeStruct((rows, width), bf16),
+            jax.ShapeDtypeStruct(down_zeros.shape, f32),
+            jax.ShapeDtypeStruct(up_zeros.shape, f32),
+        ],
         in_specs=[
             pl.BlockSpec((rows, matrix_rows), lambda step: (0, 0)),
             pl.BlockSpec((matrix_rows, chunk), lambda step: (0, step)),
+            in_place(),
+            in_place(),
         ],
-        out_specs=pl.BlockSpec((rows, chunk), lambda step: (0, step)),
+        out_specs=[
+            pl.BlockSpec((rows, chunk), lambda step: (0, step)),
+            in_place(),
+            in_place(),
+        ],
+        input_output_aliases={2: 1, 3: 2},
         compiler_params=pltpu.CompilerParams(vmem_limit_bytes=12 * mebibyte),
         cost_estimate=cost(2 * rows * width * matrix_rows, 2 * width * (matrix_rows + rows)),
         name="token_gradient",
-    )(gradients, matrix)
+    )(gradients, matrix, down_zeros, up_zeros)
 
     if direct:
         term_shapes = [(SEGS * joint_rank, held_down), (SEGS * joint_rank, padded_down)]

time: 163 us -> 166 us (1.018); the launches traced: 161 us -> 166 us
  local copies, waits for them, and re-layouts: 19 us -> 22.6 us
  starting transfers between devices: 40.1 us -> 42 us
    ppermute x2, waiting for transfers between devices: 6.78 us -> 0.01 us  [over_plane(): lax.ppermute(value, ('groups', 'batch'), over_both)]
    ppermute x22 -> x23, waiting for transfers between devices: 52.1 us -> 57.7 us  [shift(): lax.ppermute(value, axis, [(at, (at + steps) % count) for at in range(cou...]
    ppermute x22 -> x23, starting transfers between devices: 28.6 us -> 31.8 us  [shift(): lax.ppermute(value, axis, [(at, (at + steps) % count) for at in range(cou...]
    unnamed x19 -> x25, local copies, waits for them, and re-layouts: 5.42 us -> 5.65 us
  transfers between devices with their start and end apart: 28 -> 29, of which waited for: 20 -> 20; matrix products, arithmetic and copies ran while one was open for 10% -> 11% of each run, Pallas kernels for 4% -> 7%
where the time goes in v11:
time: 166 us
  waiting for transfers between devices  74.8 us (45%)
  starting transfers between devices  42 us (25%)
  local copies, waits for them, and re-layouts  22.6 us (14%)
  Pallas kernels  21.6 us (13%)
  other arithmetic  2.5 us (2%)
  between operations  2.13 us (1%)
    ppermute x23, waiting for transfers between devices, shift(): lax.ppermute(value, axis, [(at, (at + steps) % count) for at in range(cou...  57.7 us
    ppermute x23, starting transfers between devices, shift(): lax.ppermute(value, axis, [(at, (at + steps) % count) for at in range(cou...  31.8 us
    ppermute x4, waiting for transfers between devices, push(): return lax.ppermute(value, axis, pairs)  17.1 us
    unnamed x25, local copies, waits for them, and re-layouts  5.65 us
    broadcast_in_dim x1, local copies, waits for them, and re-layouts, shards(): down_zeros = jnp.zeros((adapters, joint_rank, 1, held_down), f32)  5.41 us
    ppermute x4, starting transfers between devices, push(): return lax.ppermute(value, axis, pairs)  5.34 us
    ppermute x2, starting transfers between devices, over_plane(): lax.ppermute(value, ('groups', 'batch'), over_both)  4.89 us
    pallas_call x1, Pallas kernels, shards(): pl.pallas_call(token_kernel, grid=(width // chunk,), out_shape=[jax.Shape...  4.82 us
  transfers between devices with their start and end apart: 29, of which 20 were waited for; matrix products, arithmetic and copies ran while one was open for 11% of the time, Pallas kernels for 7%

profile of v11, /device:TPU:0, one launch (start us, length us, event | category | flops | bytes accessed | tf_op | source)
XLA Modules:
  0.0 165.7 jit_solution(18446253803253889077)
XLA Ops:
  2.6 5.0 %collective-permute-start.1 = (bf16[192,896]{1,0:T(8,128)(2,1)}, bf16[192,896]{1,0:T(8,128)(2,1)S(1)}, u32[]{:S(2)}, u32[]{:S(2)}) collective-permute-start(bf16[192,896]{1,0:T(8,128)(2,1)} %constant_dynamic-slice_fusion.1), channel_id=1, source_target_pairs={{0,12},{4,0},{8,4},{12,8},{1,13},{5,1},{9,5},{13,9},{2,14},{6,2},{... | collective-permute-start | bytes 1032200 | tf_op jit(solution)/shard_map/ppermute | solution.py:23
  9.5 3.4 %gather_fusion.1 = bf16[3,64,448]{2,1,0:T(8,128)(2,1)} fusion(bf16[64,64,448]{2,1,0:T(8,128)(2,1)} %bitcast.18, s32[1024]{0:T(1024)S(1)} %pad_clamp_fusion), kind=kCustom, calls=%fused_computation.1 | custom fusion | bytes 344076 | tf_op jit(solution)/shard_map/gather | solution.py:609
  16.1 2.7 %gather_fusion = bf16[3,64,448]{2,1,0:T(8,128)(2,1)S(1)} fusion(bf16[64,64,448]{2,1,0:T(8,128)(2,1)} %bitcast.19, s32[1024]{0:T(1024)S(1)} %pad_clamp_fusion.1), kind=kCustom, calls=%fused_computation | custom fusion | bytes 344076 | tf_op jit(solution)/shard_map/gather | solution.py:611
  20.0 3.4 %collective-permute-done.before.refs_1_ = bf16[192,896]{1,0:T(8,128)(2,1)S(1)} collective-permute-done((bf16[192,896]{1,0:T(8,128)(2,1)}, bf16[192,896]{1,0:T(8,128)(2,1)S(1)}, u32[]{:S(2)}, u32[]{:S(2)}) %collective-permute-start) | collective-permute-done | bytes 344096 | tf_op jit(solution)/shard_map/ppermute | solution.py:23
  30.3 2.4 %collective-permute-start.9 = (bf16[384,896]{1,0:T(8,128)(2,1)}, bf16[384,896]{1,0:T(8,128)(2,1)}, u32[]{:S(2)}, u32[]{:S(2)}) collective-permute-start(bf16[384,896]{1,0:T(8,128)(2,1)} %copy-done.8), channel_id=1, source_target_pairs={{0,18},{2,16},{16,2},{18,0},{1,19},{3,17},{17,3},{19,1},{4,22},{6,... | collective-permute-start | bytes 2064392 | tf_op jit(solution)/shard_map/ppermute | solution.py:634
  36.7 9.4 %collective-permute-done.4.refs_0_.refs_3_ = bf16[336,896]{1,0:T(8,128)(2,1)S(1)} collective-permute-done((bf16[336,896]{1,0:T(8,128)(2,1)}, bf16[336,896]{1,0:T(8,128)(2,1)S(1)}, u32[]{:S(2)}, u32[]{:S(2)}) %collective-permute-start.4) | collective-permute-done | bytes 602144 | tf_op jit(solution)/shard_map/ppermute | solution.py:23
  46.9 8.2 %collective-permute-done.5.refs_5_ = bf16[144,896]{1,0:T(8,128)(2,1)S(1)} collective-permute-done((bf16[144,896]{1,0:T(8,128)(2,1)}, bf16[144,896]{1,0:T(8,128)(2,1)S(1)}, u32[]{:S(2)}, u32[]{:S(2)}) %collective-permute-start.5) | collective-permute-done | bytes 258080 | tf_op jit(solution)/shard_map/ppermute | solution.py:23
  57.2 2.1 %collective-permute-done.6.refs_6_ = bf16[144,896]{1,0:T(8,128)(2,1)S(1)} collective-permute-done((bf16[144,896]{1,0:T(8,128)(2,1)}, bf16[144,896]{1,0:T(8,128)(2,1)S(1)}, u32[]{:S(2)}, u32[]{:S(2)}) %collective-permute-start.6) | collective-permute-done | bytes 258080 | tf_op jit(solution)/shard_map/ppermute | solution.py:23
  59.3 2.4 %collective-permute-start.12 = (bf16[192,896]{1,0:T(8,128)(2,1)S(1)}, bf16[192,896]{1,0:T(8,128)(2,1)S(1)}, u32[]{:S(2)}, u32[]{:S(2)}) collective-permute-start(bf16[192,896]{1,0:T(8,128)(2,1)S(1)} %slice.32), channel_id=1, source_target_pairs={{0,18},{2,16},{16,2},{18,0},{1,19},{3,17},{17,3},{19,1},{4,22},{6,... | collective-permute-start | bytes 1032200 | tf_op jit(solution)/shard_map/ppermute | solution.py:634
  62.3 2.5 %collective-permute-done.8.refs_8_ = bf16[384,896]{1,0:T(8,128)(2,1)} collective-permute-done((bf16[384,896]{1,0:T(8,128)(2,1)}, bf16[384,896]{1,0:T(8,128)(2,1)}, u32[]{:S(2)}, u32[]{:S(2)}) %collective-permute-start.8) | collective-permute-done | bytes 688160 | tf_op jit(solution)/shard_map/ppermute | solution.py:23
  66.2 10.0 %collective-permute-start.16 = (bf16[256,896]{1,0:T(8,128)(2,1)S(1)}, bf16[256,896]{1,0:T(8,128)(2,1)S(1)}, u32[]{:S(2)}, u32[]{:S(2)}) collective-permute-start(bf16[256,896]{1,0:T(8,128)(2,1)S(1)} %get-tuple-element.54), channel_id=1, source_target_pairs={{0,4},{4,8},{8,12},{12,0},{1,5},{5,9},{9,13},{13,1},{2,6},{6,10},{... | collective-permute-start | bytes 1376264 | tf_op jit(solution)/shard_map/ppermute | solution.py:23
  77.2 13.2 %collective-permute-done.13.refs_13_.refs_2_ = bf16[256,896]{1,0:T(8,128)(2,1)S(1)} collective-permute-done((bf16[256,896]{1,0:T(8,128)(2,1)S(1)}, bf16[256,896]{1,0:T(8,128)(2,1)S(1)}, u32[]{:S(2)}, u32[]{:S(2)}) %collective-permute-start.13) | collective-permute-done | bytes 458784 | tf_op jit(solution)/shard_map/ppermute | solution.py:23
  92.3 4.7 %project.1 = (f32[128,512]{1,0:T(8,128)S(1)}, f32[128,512]{1,0:T(8,128)S(1)}, f32[256,384]{1,0:T(8,128)S(1)}, bf16[896,3584]{1,0:T(8,128)(2,1)S(1)}, bf16[3,64,640]{2,1,0:T(8,128)(2,1)S(1)}) custom-call(bf16[256,3584]{1,0:T(8,128)(2,1)S(1)} %bitcast.16, bf16[192,3584]{1,0:T(8,128)(2,1)S(1)} %copy-done.2, bf16[192,896]{1,0:T(8,128)(2,1)S(1)} %copy-done.4, ...), custom_call_target="tpu_custom_call" | custom-call | flops 1644167168 | bytes 8257536 | tf_op jit(solution)/shard_map/project/pallas_call | solution.py:728
  103.0 2.6 %collective-permute-done.18.refs_2_ = bf16[256,256]{1,0:T(8,128)(2,1)S(1)} collective-permute-done((bf16[256,256]{1,0:T(8,128)(2,1)S(1)}, bf16[256,256]{1,0:T(8,128)(2,1)S(1)}, u32[]{:S(2)}, u32[]{:S(2)}) %collective-permute-start.18) | collective-permute-done | bytes 131104 | tf_op jit(solution)/shard_map/ppermute | solution.py:29
  105.6 2.1 %collective-permute-done.17.refs_1_ = bf16[256,256]{1,0:T(8,128)(2,1)S(1)} collective-permute-done((bf16[256,256]{1,0:T(8,128)(2,1)S(1)}, bf16[256,256]{1,0:T(8,128)(2,1)S(1)}, u32[]{:S(2)}, u32[]{:S(2)}) %collective-permute-start.17) | collective-permute-done | bytes 131104 | tf_op jit(solution)/shard_map/ppermute | solution.py:29
  107.7 3.4 %attention.1 = (bf16[128,512]{1,0:T(8,128)(2,1)}, bf16[128,512]{1,0:T(8,128)(2,1)S(1)}, f32[3,128,256]{2,1,0:T(8,128)S(1)}, f32[3,128,256]{2,1,0:T(8,128)S(1)}) custom-call(s32[2,3]{1,0:T(2,128)S(1)} %copy-done.7, bf16[512,128]{1,0:T(8,128)(2,1)S(1)} %get-tuple-element.55.queries, bf16[128,512]{1,0:T(8,128)(2,1)S(1)} %bitcast.17, ...), custom_call_target="tpu_custom_call" | custom-call | flops 503316480 | bytes 786432 | tf_op jit(solution)/shard_map/attention/pallas_call | solution.py:776
  115.5 5.6 %collective-permute-done.21.refs_1_ = f32[128,256]{1,0:T(8,128)S(1)} collective-permute-done((f32[128,256]{1,0:T(8,128)S(1)}, f32[128,256]{1,0:T(8,128)S(1)}, u32[]{:S(2)}, u32[]{:S(2)}) %collective-permute-start.21) | collective-permute-done | bytes 131104 | tf_op jit(solution)/shard_map/ppermute | solution.py:29
  121.1 6.8 %collective-permute-done.22.refs_2_ = f32[128,256]{1,0:T(8,128)S(1)} collective-permute-done((f32[128,256]{1,0:T(8,128)S(1)}, f32[128,256]{1,0:T(8,128)S(1)}, u32[]{:S(2)}, u32[]{:S(2)}) %collective-permute-start.22) | collective-permute-done | bytes 131104 | tf_op jit(solution)/shard_map/ppermute | solution.py:29
  132.9 2.4 %collective-permute-start.27 = (f32[248,128]{1,0:T(8,128)S(1)}, f32[248,128]{1,0:T(8,128)S(1)}, u32[]{:S(2)}, u32[]{:S(2)}) collective-permute-start(f32[248,128]{1,0:T(8,128)S(1)} %get-tuple-element.75), channel_id=1, source_target_pairs={{0,12},{4,0},{8,4},{12,8},{1,13},{5,1},{9,5},{13,9},{2,14},{6,2},{... | collective-permute-start | bytes 380936 | tf_op jit(solution)/shard_map/ppermute | solution.py:23
  135.3 7.9 %collective-permute-done.25.refs_5_ = f32[248,128]{1,0:T(8,128)S(1)} collective-permute-done((f32[248,128]{1,0:T(8,128)S(1)}, f32[248,128]{1,0:T(8,128)S(1)}, u32[]{:S(2)}, u32[]{:S(2)}) %collective-permute-start.25) | collective-permute-done | bytes 127008 | tf_op jit(solution)/shard_map/ppermute | solution.py:23
  143.2 4.1 %collective-permute-done.26.refs_6_ = f32[248,128]{1,0:T(8,128)S(1)} collective-permute-done((f32[248,128]{1,0:T(8,128)S(1)}, f32[248,128]{1,0:T(8,128)S(1)}, u32[]{:S(2)}, u32[]{:S(2)}) %collective-permute-start.26) | collective-permute-done | bytes 127008 | tf_op jit(solution)/shard_map/ppermute | solution.py:23
  152.4 5.4 %broadcast_in_dim.51.clone.refs_0_ = f32[64,64,1,448]{3,2,1,0:T(1,128)} broadcast(f32[]{:T(128)} %constant.41.clone.1), dimensions={} | broadcast | bytes 7340036 | tf_op jit(solution)/shard_map/broadcast_in_dim | solution.py:583
  157.8 4.8 %token_gradient.1 = (bf16[256,3584]{1,0:T(8,128)(2,1)}, f32[64,64,1,448]{3,2,1,0:T(1,128)}, f32[64,32,80]{2,1,0:T(8,128)}) custom-call(bf16[256,896]{1,0:T(8,128)(2,1)S(1)} %get-tuple-element.67.gradients, bf16[896,3584]{1,0:T(8,128)(2,1)S(1)} %get-tuple-element.68.matrix, ...), custom_call_target="tpu_custom_call", output_to_operand_aliasing={{1}: (2, {}), {2}: (3, {})} | custom-call | flops 1644167168 | bytes 8257536 | tf_op jit(solution)/shard_map/token_gradient/pallas_call | solution.py:859
  162.7 3.0 %bank_rows.1 = (f32[64,64,1,448]{3,2,1,0:T(1,128)}, f32[64,32,80]{2,1,0:T(8,128)}) custom-call(s32[6]{0:T(128)S(1)} %pad_add_fusion.refs_3_.bank_rows, f32[192,448]{1,0:T(8,128)S(1)} %get-tuple-element.77.own_down, f32[192,512]{1,0:T(8,128)S(1)} %collective-permute-done.28.far, ...), custom_call_target="tpu_custom_call", output_to_operand_aliasing={{0}: (4, {}), {1}: (5, {})} | custom-call | tf_op jit(solution)/shard_map/bank_rows/pallas_call | solution.py:922
  (90 shorter events, 45.6 us)
Async XLA Ops:
  2.6 17.4 %collective-permute-start.1 = (bf16[192,896]{1,0:T(8,128)(2,1)}, bf16[192,896]{1,0:T(8,128)(2,1)S(1)}, u32[]{:S(2)}, u32[]{:S(2)}) collective-permute-start(bf16[192,896]{1,0:T(8,128)(2,1)} %constant_dynamic-slice_fusion.1), channel_id=1, source_target_pairs={{0,12},{4,0},{8,4},{12,8},{1,13},{5,1},{9,5},{13,9},{2,14},{6,2},{... | collective-permute-start | bytes 1032200 | tf_op jit(solution)/shard_map/ppermute | solution.py:23
  7.6 15.8 %collective-permute-start = (bf16[192,896]{1,0:T(8,128)(2,1)}, bf16[192,896]{1,0:T(8,128)(2,1)S(1)}, u32[]{:S(2)}, u32[]{:S(2)}) collective-permute-start(bf16[192,896]{1,0:T(8,128)(2,1)} %constant_dynamic-slice_fusion.1), channel_id=1, source_target_pairs={{0,4},{4,8},{8,12},{12,0},{1,5},{5,9},{9,13},{13,1},{2,6},{6,10},{... | collective-permute-start | bytes 1032200 | tf_op jit(solution)/shard_map/ppermute | solution.py:23
  12.9 7.1 %collective-permute-start.2 = (bf16[3,64,448]{2,1,0:T(8,128)(2,1)}, bf16[3,64,448]{2,1,0:T(8,128)(2,1)S(1)}, u32[]{:S(2)}, u32[]{:S(2)}) collective-permute-start(bf16[3,64,448]{2,1,0:T(8,128)(2,1)} %gather_fusion.1), channel_id=1, source_target_pairs={{0,2},{2,0},{1,3},{3,1},{4,6},{6,4},{5,7},{7,5},{8,10},{10,8},{9,1... | collective-permute-start | bytes 516104 | tf_op jit(solution)/shard_map/ppermute | solution.py:23
  14.9 5.0 %collective-permute-start.3 = (bf16[3,32,80]{2,1,0:T(8,128)(2,1)S(1)}, bf16[3,32,80]{2,1,0:T(8,128)(2,1)S(1)}, u32[]{:S(2)}, u32[]{:S(2)}) collective-permute-start(bf16[3,32,80]{2,1,0:T(8,128)(2,1)S(1)} %gather_fusion.3), channel_id=1, source_target_pairs={{0,2},{2,0},{1,3},{3,1},{4,6},{6,4},{5,7},{7,5},{8,10},{10,8},{9,1... | collective-permute-start | bytes 46088 | tf_op jit(solution)/shard_map/ppermute | solution.py:23
  27.5 18.6 %collective-permute-start.4 = (bf16[336,896]{1,0:T(8,128)(2,1)}, bf16[336,896]{1,0:T(8,128)(2,1)S(1)}, u32[]{:S(2)}, u32[]{:S(2)}) collective-permute-start(bf16[336,896]{1,0:T(8,128)(2,1)} %get-tuple-element.44), channel_id=1, source_target_pairs={{0,4},{4,8},{8,12},{12,0},{1,5},{5,9},{9,13},{13,1},{2,6},{6,10},{... | collective-permute-start | bytes 1806344 | tf_op jit(solution)/shard_map/ppermute | solution.py:23
  30.3 31.4 %collective-permute-start.9 = (bf16[384,896]{1,0:T(8,128)(2,1)}, bf16[384,896]{1,0:T(8,128)(2,1)}, u32[]{:S(2)}, u32[]{:S(2)}) collective-permute-start(bf16[384,896]{1,0:T(8,128)(2,1)} %copy-done.8), channel_id=1, source_target_pairs={{0,18},{2,16},{16,2},{18,0},{1,19},{3,17},{17,3},{19,1},{4,22},{6,... | collective-permute-start | bytes 2064392 | tf_op jit(solution)/shard_map/ppermute | solution.py:634
  32.8 32.0 %collective-permute-start.8 = (bf16[384,896]{1,0:T(8,128)(2,1)}, bf16[384,896]{1,0:T(8,128)(2,1)}, u32[]{:S(2)}, u32[]{:S(2)}) collective-permute-start(bf16[384,896]{1,0:T(8,128)(2,1)} %copy-done.8), channel_id=1, source_target_pairs={{0,16},{16,0},{1,17},{17,1},{2,18},{18,2},{3,19},{19,3},{4,20},{20... | collective-permute-start | bytes 2064392 | tf_op jit(solution)/shard_map/ppermute | solution.py:23
  35.4 30.8 %collective-permute-start.7 = (bf16[384,896]{1,0:T(8,128)(2,1)}, bf16[384,896]{1,0:T(8,128)(2,1)S(1)}, u32[]{:S(2)}, u32[]{:S(2)}) collective-permute-start(bf16[384,896]{1,0:T(8,128)(2,1)} %copy-done.8), channel_id=1, source_target_pairs={{0,2},{2,0},{1,3},{3,1},{4,6},{6,4},{5,7},{7,5},{8,10},{10,8},{9,1... | collective-permute-start | bytes 2064392 | tf_op jit(solution)/shard_map/ppermute | solution.py:23
  36.0 19.0 %collective-permute-start.5 = (bf16[144,896]{1,0:T(8,128)(2,1)}, bf16[144,896]{1,0:T(8,128)(2,1)S(1)}, u32[]{:S(2)}, u32[]{:S(2)}) collective-permute-start(bf16[144,896]{1,0:T(8,128)(2,1)} %copy-done.10), channel_id=1, source_target_pairs={{0,8},{4,12},{8,0},{12,4},{1,9},{5,13},{9,1},{13,5},{2,10},{6,14},... | collective-permute-start | bytes 774152 | tf_op jit(solution)/shard_map/ppermute | solution.py:23
  46.1 13.2 %collective-permute-start.6 = (bf16[144,896]{1,0:T(8,128)(2,1)}, bf16[144,896]{1,0:T(8,128)(2,1)S(1)}, u32[]{:S(2)}, u32[]{:S(2)}) collective-permute-start(bf16[144,896]{1,0:T(8,128)(2,1)} %copy-done.9), channel_id=1, source_target_pairs={{0,12},{4,0},{8,4},{12,8},{1,13},{5,1},{9,5},{13,9},{2,14},{6,2},{... | collective-permute-start | bytes 774152 | tf_op jit(solution)/shard_map/ppermute | solution.py:23
  55.1 35.2 %collective-permute-start.13 = (bf16[256,896]{1,0:T(8,128)(2,1)S(1)}, bf16[256,896]{1,0:T(8,128)(2,1)S(1)}, u32[]{:S(2)}, u32[]{:S(2)}) collective-permute-start(bf16[256,896]{1,0:T(8,128)(2,1)S(1)} %get-tuple-element.49), channel_id=1, source_target_pairs={{0,8},{4,12},{8,0},{12,4},{1,9},{5,13},{9,1},{13,5},{2,10},{6,14},... | collective-permute-start | bytes 1376264 | tf_op jit(solution)/shard_map/ppermute | solution.py:23
  59.3 16.9 %collective-permute-start.12 = (bf16[192,896]{1,0:T(8,128)(2,1)S(1)}, bf16[192,896]{1,0:T(8,128)(2,1)S(1)}, u32[]{:S(2)}, u32[]{:S(2)}) collective-permute-start(bf16[192,896]{1,0:T(8,128)(2,1)S(1)} %slice.32), channel_id=1, source_target_pairs={{0,18},{2,16},{16,2},{18,0},{1,19},{3,17},{17,3},{19,1},{4,22},{6,... | collective-permute-start | bytes 1032200 | tf_op jit(solution)/shard_map/ppermute | solution.py:634
  61.8 15.2 %collective-permute-start.11 = (bf16[192,896]{1,0:T(8,128)(2,1)S(1)}, bf16[192,896]{1,0:T(8,128)(2,1)S(1)}, u32[]{:S(2)}, u32[]{:S(2)}) collective-permute-start(bf16[192,896]{1,0:T(8,128)(2,1)S(1)} %slice.32), channel_id=1, source_target_pairs={{0,16},{16,0},{1,17},{17,1},{2,18},{18,2},{3,19},{19,3},{4,20},{20... | collective-permute-start | bytes 1032200 | tf_op jit(solution)/shard_map/ppermute | solution.py:23
  64.8 12.4 %collective-permute-start.10 = (bf16[192,896]{1,0:T(8,128)(2,1)S(1)}, bf16[192,896]{1,0:T(8,128)(2,1)S(1)}, u32[]{:S(2)}, u32[]{:S(2)}) collective-permute-start(bf16[192,896]{1,0:T(8,128)(2,1)S(1)} %slice.32), channel_id=1, source_target_pairs={{0,2},{2,0},{1,3},{3,1},{4,6},{6,4},{5,7},{7,5},{8,10},{10,8},{9,1... | collective-permute-start | bytes 1032200 | tf_op jit(solution)/shard_map/ppermute | solution.py:23
  66.2 31.3 %collective-permute-start.16 = (bf16[256,896]{1,0:T(8,128)(2,1)S(1)}, bf16[256,896]{1,0:T(8,128)(2,1)S(1)}, u32[]{:S(2)}, u32[]{:S(2)}) collective-permute-start(bf16[256,896]{1,0:T(8,128)(2,1)S(1)} %get-tuple-element.54), channel_id=1, source_target_pairs={{0,4},{4,8},{8,12},{12,0},{1,5},{5,9},{9,13},{13,1},{2,6},{6,10},{... | collective-permute-start | bytes 1376264 | tf_op jit(solution)/shard_map/ppermute | solution.py:23
  100.2 5.3 %collective-permute-start.18 = (bf16[256,256]{1,0:T(8,128)(2,1)S(1)}, bf16[256,256]{1,0:T(8,128)(2,1)S(1)}, u32[]{:S(2)}, u32[]{:S(2)}) collective-permute-start(bf16[256,256]{1,0:T(8,128)(2,1)S(1)} %get-tuple-element.56.refs_0_), channel_id=1, source_target_pairs={{0,8},{4,12},{1,9},{5,13},{2,10},{6,14},{3,11},{7,15},{16,24},{20,... | collective-permute-start | bytes 393224 | tf_op jit(solution)/shard_map/ppermute | solution.py:29
  101.7 6.0 %collective-permute-start.17 = (bf16[256,256]{1,0:T(8,128)(2,1)S(1)}, bf16[256,256]{1,0:T(8,128)(2,1)S(1)}, u32[]{:S(2)}, u32[]{:S(2)}) collective-permute-start(bf16[256,256]{1,0:T(8,128)(2,1)S(1)} %get-tuple-element.56.refs_0_), channel_id=1, source_target_pairs={{0,4},{4,8},{8,12},{1,5},{5,9},{9,13},{2,6},{6,10},{10,14},{3,7},{... | collective-permute-start | bytes 393224 | tf_op jit(solution)/shard_map/ppermute | solution.py:29
  112.9 8.2 %collective-permute-start.21 = (f32[128,256]{1,0:T(8,128)S(1)}, f32[128,256]{1,0:T(8,128)S(1)}, u32[]{:S(2)}, u32[]{:S(2)}) collective-permute-start(f32[128,256]{1,0:T(8,128)S(1)} %get-tuple-element.62), channel_id=1, source_target_pairs={{4,0},{8,4},{12,8},{5,1},{9,5},{13,9},{6,2},{10,6},{14,10},{7,3},{... | collective-permute-start | bytes 393224 | tf_op jit(solution)/shard_map/ppermute | solution.py:29
  114.2 13.7 %collective-permute-start.22 = (f32[128,256]{1,0:T(8,128)S(1)}, f32[128,256]{1,0:T(8,128)S(1)}, u32[]{:S(2)}, u32[]{:S(2)}) collective-permute-start(f32[128,256]{1,0:T(8,128)S(1)} %get-tuple-element.63), channel_id=1, source_target_pairs={{8,0},{12,4},{9,1},{13,5},{10,2},{14,6},{11,3},{15,7},{24,16},{28,... | collective-permute-start | bytes 393224 | tf_op jit(solution)/shard_map/ppermute | solution.py:29
  128.0 20.0 %collective-permute-start.24 = (bf16[256,896]{1,0:T(8,128)(2,1)S(1)}, bf16[256,896]{1,0:T(8,128)(2,1)S(1)}, u32[]{:S(2)}, u32[]{:S(2)}) collective-permute-start(bf16[256,896]{1,0:T(8,128)(2,1)S(1)} %get-tuple-element.71), channel_id=1, source_target_pairs={{0,12},{4,0},{8,4},{12,8},{1,13},{5,1},{9,5},{13,9},{2,14},{6,2},{... | collective-permute-start | bytes 1376264 | tf_op jit(solution)/shard_map/ppermute | solution.py:23
  130.9 12.4 %collective-permute-start.25 = (f32[248,128]{1,0:T(8,128)S(1)}, f32[248,128]{1,0:T(8,128)S(1)}, u32[]{:S(2)}, u32[]{:S(2)}) collective-permute-start(f32[248,128]{1,0:T(8,128)S(1)} %get-tuple-element.73), channel_id=1, source_target_pairs={{0,4},{4,8},{8,12},{12,0},{1,5},{5,9},{9,13},{13,1},{2,6},{6,10},{... | collective-permute-start | bytes 380936 | tf_op jit(solution)/shard_map/ppermute | solution.py:23
  132.9 14.5 %collective-permute-start.26 = (f32[248,128]{1,0:T(8,128)S(1)}, f32[248,128]{1,0:T(8,128)S(1)}, u32[]{:S(2)}, u32[]{:S(2)}) collective-permute-start(f32[248,128]{1,0:T(8,128)S(1)} %get-tuple-element.74), channel_id=1, source_target_pairs={{0,8},{4,12},{8,0},{12,4},{1,9},{5,13},{9,1},{13,5},{2,10},{6,14},... | collective-permute-start | bytes 380936 | tf_op jit(solution)/shard_map/ppermute | solution.py:23
  132.9 15.1 %collective-permute-start.27 = (f32[248,128]{1,0:T(8,128)S(1)}, f32[248,128]{1,0:T(8,128)S(1)}, u32[]{:S(2)}, u32[]{:S(2)}) collective-permute-start(f32[248,128]{1,0:T(8,128)S(1)} %get-tuple-element.75), channel_id=1, source_target_pairs={{0,12},{4,0},{8,4},{12,8},{1,13},{5,1},{9,5},{13,9},{2,14},{6,2},{... | collective-permute-start | bytes 380936 | tf_op jit(solution)/shard_map/ppermute | solution.py:23
  149.8 12.9 %collective-permute-start.28 = (f32[192,512]{1,0:T(8,128)S(1)}, f32[192,512]{1,0:T(8,128)S(1)}, u32[]{:S(2)}, u32[]{:S(2)}) collective-permute-start(f32[192,512]{1,0:T(8,128)S(1)} %get-tuple-element.78), channel_id=1, source_target_pairs={{0,2},{2,0},{1,3},{3,1},{4,6},{6,4},{5,7},{7,5},{8,10},{10,8},{9,1... | collective-permute-start | bytes 1179656 | tf_op jit(solution)/shard_map/ppermute | solution.py:23
  (17 other events, 152.7 us)

commit v12 on v11

--- a/solution.py
+++ b/solution.py
@@ -164,6 +164,26 @@
                 ]
 
 
+def pass_kernel(*refs):
+    del refs
+
+
+def pass_after(value, *earlier):
+    return pl.pallas_call(
+        pass_kernel,
+        out_shape=jax.ShapeDtypeStruct(value.shape, value.dtype),
+        in_specs=[in_place()] * (1 + len(earlier)),
+        out_specs=in_place(),
+        input_output_aliases={0: 0},
+        name="pass_after",
+    )(value, *earlier)
+
+
+def pick_kernel(forward, *refs):
+    middle = refs[-1]
+    middle[...] = forward[: middle.shape[0]]
+
+
 def cut_kernel(unused, seq_count, tokens, *refs):
     for steps, block in enumerate(refs[unused:]):
         target = ring_index(lax.axis_index("seq") + steps - seq_count, seq_count)
@@ -338,13 +358,13 @@
         ).astype(jnp.bfloat16)
 
 
-def sum_kernel(kept, arrived, *sums):
-    for back, total in enumerate(sums):
+def sum_kernel(unused, kept, arrived, *refs):
+    for back, total in enumerate(refs[unused:]):
         total[...] = kept[back] + arrived[back]
 
 
 def pair_kernel(terms, cosines, sines, *refs):
-    parts, pair = refs[:terms], refs[-2]
+    parts, pair = refs[:terms], refs[-1]
     own_rows = pair.shape[0]
     total = sum(part[...] for part in parts)
     own = pl.ds(pl.multiple_of(lax.axis_index("tp") * own_rows, own_rows), own_rows)
@@ -414,8 +434,7 @@
         block[first_low:, low.shape[1] :] = turned[rows // 2 :].astype(jnp.float32)
 
 
-def token_kernel(gradients, matrix, *refs):
-    token_grad = refs[2]
+def token_kernel(gradients, matrix, token_grad):
     token_grad[...] = dot_nn(gradients[...], matrix[...]).astype(jnp.bfloat16)
 
 
@@ -636,7 +655,15 @@
 
         plane_parts = over_plane(plane)
         forward = shift(forward, "seq", 1)
-        middle = forward[:frozen_rows]
+        middle = pl.pallas_call(
+            pick_kernel,
+            out_shape=jax.ShapeDtypeStruct((frozen_rows, share), bf16),
+            in_specs=[in_vmem()] + [in_place()] * 2,
+            out_specs=in_vmem(),
+            compiler_params=pltpu.CompilerParams(vmem_limit_bytes=8 * mebibyte),
+            cost_estimate=cost(0, 4 * frozen_rows * share),
+            name="pick",
+        )(forward, down_zeros, up_zeros)
         middle_parts = over_plane(middle)
         payloads = [shift(part, "seq", steps + 2) for steps, part in enumerate(payloads)]
         arrays = [frozen_qkv_matrix, before, after, forward, payload] + payloads
@@ -666,7 +693,7 @@
                 (7 + number, frozen_rows, frozen_rows, frozen_at(3, batch_step, group_step)),
                 (10 + number, 0, frozen_rows, frozen_at(2, batch_step, group_step)),
             ]
-        early = [forward, cosines, sines, bank_rows]
+        early = [forward, *plane_parts, *payloads, cosines, sines, bank_rows]
         column_blocks = pl.pallas_call(
             functools.partial(cut_kernel, len(early), seq_count),
             out_shape=[jax.ShapeDtypeStruct((rows, down_width), bf16)] * seq_count,
@@ -717,10 +744,14 @@
             for steps in range(seq_count)
         ]
 
-    column_parts = [
-        shift(block, "seq", steps) if steps else block
-        for steps, block in enumerate(column_blocks)
-    ]
+    if direct:
+        column_parts = [column_blocks[0], None, shift(column_blocks[2], "seq", 2), None]
+        column_parts[1] = shift(pass_after(column_blocks[1], column_parts[2]), "seq", 1)
+    else:
+        column_parts = [
+            shift(block, "seq", steps) if steps else block
+            for steps, block in enumerate(column_blocks)
+        ]
     early = [column_parts[2]] if direct and seq_count > 3 else []
     up_shape = (SEGS, joint_rank, query_columns + HEAD_WIDTH)
     matrix_rows = features + 2 * joint_rank
@@ -771,6 +802,8 @@
 
     blocks = [pairs] + [push(pairs, "seq", back) for back in range(1, half_count + 1)]
     block_count = len(blocks)
+    if direct:
+        column_parts[3] = shift(pass_after(column_blocks[3], *blocks[1:]), "seq", 3)
     incoming = output_gradient[0]
     early_columns = []
     attention, query_grad, kept, sent = pl.pallas_call(
@@ -796,31 +829,27 @@
     )(document_lengths, queries, incoming, cosines, sines, *blocks, *early_columns)
 
     other_query = shift(query_grad, "tp", 1)
+    due = [column_parts[-1]] if direct else []
     pair_sums = pl.pallas_call(
-        sum_kernel,
+        functools.partial(sum_kernel, len(due)),
         out_shape=[jax.ShapeDtypeStruct((own_rows, 2 * HEAD_WIDTH), f32)] * block_count,
-        in_specs=[in_vmem()] * 2,
+        in_specs=[in_vmem()] * 2 + [in_place()] * len(due),
         out_specs=[in_vmem()] * block_count,
         compiler_params=pltpu.CompilerParams(vmem_limit_bytes=8 * mebibyte),
         cost_estimate=cost(0, 12 * block_count * own_rows * 2 * HEAD_WIDTH),
         name="pair_sums",
-    )(kept, shift(sent, "tp", 1))
+    )(kept, shift(sent, "tp", 1), *due)
     pair_terms = [pair_sums[0]]
     pair_terms += [push(pair_sums[back], "seq", -back) for back in range(1, block_count)]
-    pair_grad, late_block = pl.pallas_call(
+    pair_grad = pl.pallas_call(
         functools.partial(pair_kernel, block_count),
-        out_shape=[
-            jax.ShapeDtypeStruct((own_rows, 2 * HEAD_WIDTH), bf16),
-            jax.ShapeDtypeStruct((rows, down_width), bf16),
-        ],
-        in_specs=[in_vmem()] * (2 + block_count) + [in_place()],
-        out_specs=[in_vmem(), in_place()],
-        input_output_aliases={2 + block_count: 1},
+        out_shape=jax.ShapeDtypeStruct((own_rows, 2 * HEAD_WIDTH), bf16),
+        in_specs=[in_vmem()] * (2 + block_count),
+        out_specs=in_vmem(),
         compiler_params=pltpu.CompilerParams(vmem_limit_bytes=8 * mebibyte),
         cost_estimate=cost(0, 12 * block_count * own_rows * 2 * HEAD_WIDTH),
         name="pair_gradients",
-    )(cosines, sines, *pair_terms, column_blocks[-1])
-    column_parts[-1] = shift(late_block, "seq", seq_count - 1)
+    )(cosines, sines, *pair_terms)
     other_pair = shift(pair_grad, "tp", 1)
 
     split_shapes = [(SEGS * low_width, up_width)] * seq_count
@@ -856,30 +885,19 @@
     ]
 
     chunk = 512
-    token_grad, down_zeros, up_zeros = pl.pallas_call(
+    token_grad = pl.pallas_call(
         token_kernel,
         grid=(width // chunk,),
-        out_shape=[
-            jax.ShapeDtypeStruct((rows, width), bf16),
-            jax.ShapeDtypeStruct(down_zeros.shape, f32),
-            jax.ShapeDtypeStruct(up_zeros.shape, f32),
-        ],
+        out_shape=jax.ShapeDtypeStruct((rows, width), bf16),
         in_specs=[
             pl.BlockSpec((rows, matrix_rows), lambda step: (0, 0)),
             pl.BlockSpec((matrix_rows, chunk), lambda step: (0, step)),
-            in_place(),
-            in_place(),
         ],
-        out_specs=[
-            pl.BlockSpec((rows, chunk), lambda step: (0, step)),
-            in_place(),
-            in_place(),
-        ],
-        input_output_aliases={2: 1, 3: 2},
+        out_specs=pl.BlockSpec((rows, chunk), lambda step: (0, step)),
         compiler_params=pltpu.CompilerParams(vmem_limit_bytes=12 * mebibyte),
         cost_estimate=cost(2 * rows * width * matrix_rows, 2 * width * (matrix_rows + rows)),
         name="token_gradient",
-    )(gradients, matrix, down_zeros, up_zeros)
+    )(gradients, matrix)
 
     if direct:
         term_shapes = [(SEGS * joint_rank, held_down), (SEGS * joint_rank, padded_down)]

time: 166 us -> 179 us (1.078)
  local copies, waits for them, and re-layouts: 22.6 us -> 35 us
  starting transfers between devices: 42 us -> 36.4 us
  waiting for transfers between devices: 74.8 us -> 78 us
  Pallas kernels: 21.6 us -> 23.7 us
    unnamed x25 -> x63, local copies, waits for them, and re-layouts: 5.65 us -> 20 us
    ppermute x23, starting transfers between devices: 31.8 us -> 22 us  [shift(): lax.ppermute(value, axis, [(at, (at + steps) % count) for at in range(cou...]
    ppermute x23, waiting for transfers between devices: 57.7 us -> 63 us  [shift(): lax.ppermute(value, axis, [(at, (at + steps) % count) for at in range(cou...]
    ppermute x4, starting transfers between devices: 5.34 us -> 9.45 us  [push(): return lax.ppermute(value, axis, pairs)]
    ppermute x4, waiting for transfers between devices: 17.1 us -> 14.1 us  [push(): return lax.ppermute(value, axis, pairs)]
    pallas_call x3 -> x6, Pallas kernels: 4.95 us -> 5.8 us  [the longest x1 4.82 us: shards(): pl.pallas_call(token_kernel, grid=(width // chunk,), out_shape=jax.ShapeD...]
  transfers between devices with their start and end apart: 29 -> 29, of which waited for: 20 -> 18; matrix products, arithmetic and copies ran while one was open for 11% -> 9% of each run, Pallas kernels for 7% -> 8%
where the time goes in v12:
time: 179 us; the launch traced here: 178 us
  waiting for transfers between devices  78 us (44%)
  starting transfers between devices  36.4 us (20%)
  local copies, waits for them, and re-layouts  35 us (20%)
  Pallas kernels  23.7 us (13%)
  other arithmetic  2.32 us (1%)
  between operations  2.22 us (1%)
    ppermute x23, waiting for transfers between devices, shift(): lax.ppermute(value, axis, [(at, (at + steps) % count) for at in range(cou...  63 us
    ppermute x23, starting transfers between devices, shift(): lax.ppermute(value, axis, [(at, (at + steps) % count) for at in range(cou...  22 us
    unnamed x63, local copies, waits for them, and re-layouts  20 us
    ppermute x4, waiting for transfers between devices, push(): return lax.ppermute(value, axis, pairs)  14.1 us
    ppermute x4, starting transfers between devices, push(): return lax.ppermute(value, axis, pairs)  9.45 us
    pallas_call x1, Pallas kernels, shards(): pl.pallas_call(functools.partial(project_kernel, len(arrays), entries, up...  5.13 us
    ppermute x2, starting transfers between devices, over_plane(): lax.ppermute(value, ('groups', 'batch'), over_both)  4.89 us
    pallas_call x1, Pallas kernels, shards(): pl.pallas_call(token_kernel, grid=(width // chunk,), out_shape=jax.ShapeD...  4.82 us
  transfers between devices with their start and end apart: 29, of which 18 were waited for; matrix products, arithmetic and copies ran while one was open for 9% of the time, Pallas kernels for 8%

profile of v12, /device:TPU:0, one launch (start us, length us, event | category | flops | bytes accessed | tf_op | source)
XLA Modules:
  0.0 177.6 jit_solution(14600389254186076601)
XLA Ops:
  2.6 5.0 %collective-permute-start.1 = (bf16[192,896]{1,0:T(8,128)(2,1)}, bf16[192,896]{1,0:T(8,128)(2,1)S(1)}, u32[]{:S(2)}, u32[]{:S(2)}) collective-permute-start(bf16[192,896]{1,0:T(8,128)(2,1)} %constant_dynamic-slice_fusion.1), channel_id=1, source_target_pairs={{0,12},{4,0},{8,4},{12,8},{1,13},{5,1},{9,5},{13,9},{2,14},{6,2},{... | collective-permute-start | bytes 1032200 | tf_op jit(solution)/shard_map/ppermute | solution.py:23
  11.6 3.4 %gather_fusion.1 = bf16[3,64,448]{2,1,0:T(8,128)(2,1)} fusion(bf16[64,64,448]{2,1,0:T(8,128)(2,1)} %bitcast.19, s32[1024]{0:T(1024)S(1)} %pad_clamp_fusion), kind=kCustom, calls=%fused_computation.1 | custom fusion | bytes 344076 | tf_op jit(solution)/shard_map/gather | solution.py:628
  16.8 2.7 %gather_fusion = bf16[3,64,448]{2,1,0:T(8,128)(2,1)S(1)} fusion(bf16[64,64,448]{2,1,0:T(8,128)(2,1)} %bitcast.20, s32[1024]{0:T(1024)S(1)} %pad_clamp_fusion.1), kind=kCustom, calls=%fused_computation | custom fusion | bytes 344076 | tf_op jit(solution)/shard_map/gather | solution.py:630
  33.8 22.0 %collective-permute-done.5.refs_4_.refs_5_ = bf16[144,896]{1,0:T(8,128)(2,1)S(1)} collective-permute-done((bf16[144,896]{1,0:T(8,128)(2,1)}, bf16[144,896]{1,0:T(8,128)(2,1)S(1)}, u32[]{:S(2)}, u32[]{:S(2)}) %collective-permute-start.5) | collective-permute-done | bytes 258080 | tf_op jit(solution)/shard_map/ppermute | solution.py:23
  56.4 6.2 %collective-permute-done.6.refs_5_.refs_6_ = bf16[144,896]{1,0:T(8,128)(2,1)S(1)} collective-permute-done((bf16[144,896]{1,0:T(8,128)(2,1)}, bf16[144,896]{1,0:T(8,128)(2,1)S(1)}, u32[]{:S(2)}, u32[]{:S(2)}) %collective-permute-start.6) | collective-permute-done | bytes 258080 | tf_op jit(solution)/shard_map/ppermute | solution.py:23
  64.7 4.5 %broadcast_in_dim.47.refs_0_.down_zeros = f32[64,64,1,448]{3,2,1,0:T(1,128)S(1)} broadcast(f32[]{:T(128)} %constant.11.clone.1), dimensions={} | broadcast | bytes 7340036 | tf_op jit(solution)/shard_map/broadcast_in_dim | solution.py:602
  70.2 2.6 %copy-done.1 = f32[64,64,1,448]{3,2,1,0:T(1,128)} copy-done((f32[64,64,1,448]{3,2,1,0:T(1,128)}, f32[64,64,1,448]{3,2,1,0:T(1,128)S(1)}, u32[]{:S(2)}) %copy-start.1) | copy-done | bytes 7340056
  76.3 7.8 %collective-permute-done.13.refs_13_.refs_1_.refs_2_ = bf16[256,896]{1,0:T(8,128)(2,1)} collective-permute-done((bf16[256,896]{1,0:T(8,128)(2,1)S(1)}, bf16[256,896]{1,0:T(8,128)(2,1)}, u32[]{:S(2)}, u32[]{:S(2)}) %collective-permute-start.13) | collective-permute-done | bytes 458784 | tf_op jit(solution)/shard_map/ppermute | solution.py:23
  85.0 3.9 %collective-permute-done.11.refs_11_ = bf16[192,896]{1,0:T(8,128)(2,1)} collective-permute-done((bf16[192,896]{1,0:T(8,128)(2,1)}, bf16[192,896]{1,0:T(8,128)(2,1)}, u32[]{:S(2)}, u32[]{:S(2)}) %collective-permute-start.11) | collective-permute-done | bytes 344096 | tf_op jit(solution)/shard_map/ppermute | solution.py:23
  95.3 5.1 %project.1 = (f32[128,512]{1,0:T(8,128)S(1)}, f32[128,512]{1,0:T(8,128)S(1)}, f32[256,384]{1,0:T(8,128)S(1)}, bf16[896,3584]{1,0:T(8,128)(2,1)S(1)}, bf16[3,64,640]{2,1,0:T(8,128)(2,1)S(1)}) custom-call(bf16[256,3584]{1,0:T(8,128)(2,1)S(1)} %bitcast.16, bf16[192,3584]{1,0:T(8,128)(2,1)S(1)} %copy-done.9, bf16[192,896]{1,0:T(8,128)(2,1)S(1)} %copy-done.13, ...), custom_call_target="tpu_custom_call" | custom-call | flops 1644167168 | bytes 8257536 | tf_op jit(solution)/shard_map/project/pallas_call | solution.py:759
  100.4 2.7 %copy-done.4 = bf16[896,3584]{1,0:T(8,128)(2,1)} copy-done((bf16[896,3584]{1,0:T(8,128)(2,1)}, bf16[896,3584]{1,0:T(8,128)(2,1)S(1)}, u32[]{:S(2)}) %copy-start.4) | copy-done | bytes 6422552
  107.0 3.7 %collective-permute-start.18 = (bf16[256,256]{1,0:T(8,128)(2,1)S(1)}, bf16[256,256]{1,0:T(8,128)(2,1)S(1)}, u32[]{:S(2)}, u32[]{:S(2)}) collective-permute-start(bf16[256,256]{1,0:T(8,128)(2,1)S(1)} %get-tuple-element.51.refs_0_), channel_id=1, source_target_pairs={{0,8},{4,12},{1,9},{5,13},{2,10},{6,14},{3,11},{7,15},{16,24},{20,... | collective-permute-start | bytes 393224 | tf_op jit(solution)/shard_map/ppermute | solution.py:29
  110.7 3.2 %collective-permute-start.17 = (bf16[256,256]{1,0:T(8,128)(2,1)S(1)}, bf16[256,256]{1,0:T(8,128)(2,1)S(1)}, u32[]{:S(2)}, u32[]{:S(2)}) collective-permute-start(bf16[256,256]{1,0:T(8,128)(2,1)S(1)} %get-tuple-element.51.refs_0_), channel_id=1, source_target_pairs={{0,4},{4,8},{8,12},{1,5},{5,9},{9,13},{2,6},{6,10},{10,14},{3,7},{... | collective-permute-start | bytes 393224 | tf_op jit(solution)/shard_map/ppermute | solution.py:29
  113.9 2.7 %collective-permute-done.17.refs_1_ = bf16[256,256]{1,0:T(8,128)(2,1)S(1)} collective-permute-done((bf16[256,256]{1,0:T(8,128)(2,1)S(1)}, bf16[256,256]{1,0:T(8,128)(2,1)S(1)}, u32[]{:S(2)}, u32[]{:S(2)}) %collective-permute-start.17) | collective-permute-done | bytes 131104 | tf_op jit(solution)/shard_map/ppermute | solution.py:29
  117.3 4.4 %collective-permute-start.21 = (bf16[256,896]{1,0:T(8,128)(2,1)}, bf16[256,896]{1,0:T(8,128)(2,1)S(1)}, u32[]{:S(2)}, u32[]{:S(2)}) collective-permute-start(bf16[256,896]{1,0:T(8,128)(2,1)} %pass_after.3), channel_id=1, source_target_pairs={{0,12},{4,0},{8,4},{12,8},{1,13},{5,1},{9,5},{13,9},{2,14},{6,2},{... | collective-permute-start | bytes 1376264 | tf_op jit(solution)/shard_map/ppermute | solution.py:23
  124.3 3.4 %attention.1 = (bf16[128,512]{1,0:T(8,128)(2,1)}, bf16[128,512]{1,0:T(8,128)(2,1)S(1)}, f32[3,128,256]{2,1,0:T(8,128)S(1)}, f32[3,128,256]{2,1,0:T(8,128)S(1)}) custom-call(s32[2,3]{1,0:T(2,128)S(1)} %copy-done.28, bf16[512,128]{1,0:T(8,128)(2,1)S(1)} %get-tuple-element.50.queries, bf16[128,512]{1,0:T(8,128)(2,1)S(1)} %bitcast.17, ...), custom_call_target="tpu_custom_call" | custom-call | flops 503316480 | bytes 786432 | tf_op jit(solution)/shard_map/attention/pallas_call | solution.py:809
  134.7 5.3 %collective-permute-done.22.refs_1_ = f32[128,256]{1,0:T(8,128)S(1)} collective-permute-done((f32[128,256]{1,0:T(8,128)S(1)}, f32[128,256]{1,0:T(8,128)S(1)}, u32[]{:S(2)}, u32[]{:S(2)}) %collective-permute-start.22) | collective-permute-done | bytes 131104 | tf_op jit(solution)/shard_map/ppermute | solution.py:29
  140.0 6.1 %collective-permute-done.23.refs_2_ = f32[128,256]{1,0:T(8,128)S(1)} collective-permute-done((f32[128,256]{1,0:T(8,128)S(1)}, f32[128,256]{1,0:T(8,128)S(1)}, u32[]{:S(2)}, u32[]{:S(2)}) %collective-permute-start.23) | collective-permute-done | bytes 131104 | tf_op jit(solution)/shard_map/ppermute | solution.py:29
  149.0 3.7 %collective-permute-start.27 = (f32[248,128]{1,0:T(8,128)S(1)}, f32[248,128]{1,0:T(8,128)S(1)}, u32[]{:S(2)}, u32[]{:S(2)}) collective-permute-start(f32[248,128]{1,0:T(8,128)S(1)} %get-tuple-element.67), channel_id=1, source_target_pairs={{0,12},{4,0},{8,4},{12,8},{1,13},{5,1},{9,5},{13,9},{2,14},{6,2},{... | collective-permute-start | bytes 380936 | tf_op jit(solution)/shard_map/ppermute | solution.py:23
  152.7 4.4 %collective-permute-done.25.refs_5_ = f32[248,128]{1,0:T(8,128)S(1)} collective-permute-done((f32[248,128]{1,0:T(8,128)S(1)}, f32[248,128]{1,0:T(8,128)S(1)}, u32[]{:S(2)}, u32[]{:S(2)}) %collective-permute-start.25) | collective-permute-done | bytes 127008 | tf_op jit(solution)/shard_map/ppermute | solution.py:23
  157.1 4.5 %collective-permute-done.26.refs_6_ = f32[248,128]{1,0:T(8,128)S(1)} collective-permute-done((f32[248,128]{1,0:T(8,128)S(1)}, f32[248,128]{1,0:T(8,128)S(1)}, u32[]{:S(2)}, u32[]{:S(2)}) %collective-permute-start.26) | collective-permute-done | bytes 127008 | tf_op jit(solution)/shard_map/ppermute | solution.py:23
  166.5 4.8 %token_gradient.1 = bf16[256,3584]{1,0:T(8,128)(2,1)} custom-call(bf16[256,896]{1,0:T(8,128)(2,1)S(1)} %get-tuple-element.61.gradients, bf16[896,3584]{1,0:T(8,128)(2,1)S(1)} %copy-done.5), custom_call_target="tpu_custom_call" | custom-call | flops 1644167168 | bytes 8257536 | tf_op jit(solution)/shard_map/token_gradient/pallas_call | solution.py:888
  171.3 3.3 %collective-permute-done.28.far = f32[192,512]{1,0:T(8,128)S(1)} collective-permute-done((f32[192,512]{1,0:T(8,128)S(1)}, f32[192,512]{1,0:T(8,128)S(1)}, u32[]{:S(2)}, u32[]{:S(2)}) %collective-permute-start.28) | collective-permute-done | bytes 393248 | tf_op jit(solution)/shard_map/ppermute | solution.py:23
  174.6 3.0 %bank_rows.1 = (f32[64,64,1,448]{3,2,1,0:T(1,128)}, f32[64,32,80]{2,1,0:T(8,128)}) custom-call(s32[6]{0:T(128)S(1)} %pad_add_fusion.refs_8_.bank_rows, f32[192,448]{1,0:T(8,128)S(1)} %get-tuple-element.69.own_down, f32[192,512]{1,0:T(8,128)S(1)} %collective-permute-done.28.far, ...), custom_call_target="tpu_custom_call", output_to_operand_aliasing={{0}: (4, {}), {1}: (5, {})} | custom-call | tf_op jit(solution)/shard_map/bank_rows/pallas_call | solution.py:940
  (130 shorter events, 56.9 us)
Async XLA Ops:
  2.6 18.7 %collective-permute-start.1 = (bf16[192,896]{1,0:T(8,128)(2,1)}, bf16[192,896]{1,0:T(8,128)(2,1)S(1)}, u32[]{:S(2)}, u32[]{:S(2)}) collective-permute-start(bf16[192,896]{1,0:T(8,128)(2,1)} %constant_dynamic-slice_fusion.1), channel_id=1, source_target_pairs={{0,12},{4,0},{8,4},{12,8},{1,13},{5,1},{9,5},{13,9},{2,14},{6,2},{... | collective-permute-start | bytes 1032200 | tf_op jit(solution)/shard_map/ppermute | solution.py:23
  7.6 15.8 %collective-permute-start = (bf16[192,896]{1,0:T(8,128)(2,1)}, bf16[192,896]{1,0:T(8,128)(2,1)S(1)}, u32[]{:S(2)}, u32[]{:S(2)}) collective-permute-start(bf16[192,896]{1,0:T(8,128)(2,1)} %constant_dynamic-slice_fusion.1), channel_id=1, source_target_pairs={{0,4},{4,8},{8,12},{12,0},{1,5},{5,9},{9,13},{13,1},{2,6},{6,10},{... | collective-permute-start | bytes 1032200 | tf_op jit(solution)/shard_map/ppermute | solution.py:23
  10.0 9.5 %collective-permute-start.3 = (bf16[3,32,80]{2,1,0:T(8,128)(2,1)S(1)}, bf16[3,32,80]{2,1,0:T(8,128)(2,1)S(1)}, u32[]{:S(2)}, u32[]{:S(2)}) collective-permute-start(bf16[3,32,80]{2,1,0:T(8,128)(2,1)S(1)} %gather_fusion.3), channel_id=1, source_target_pairs={{0,2},{2,0},{1,3},{3,1},{4,6},{6,4},{5,7},{7,5},{8,10},{10,8},{9,1... | collective-permute-start | bytes 46088 | tf_op jit(solution)/shard_map/ppermute | solution.py:23
  15.0 6.3 %collective-permute-start.2 = (bf16[3,64,448]{2,1,0:T(8,128)(2,1)}, bf16[3,64,448]{2,1,0:T(8,128)(2,1)S(1)}, u32[]{:S(2)}, u32[]{:S(2)}) collective-permute-start(bf16[3,64,448]{2,1,0:T(8,128)(2,1)} %gather_fusion.1), channel_id=1, source_target_pairs={{0,2},{2,0},{1,3},{3,1},{4,6},{6,4},{5,7},{7,5},{8,10},{10,8},{9,1... | collective-permute-start | bytes 516104 | tf_op jit(solution)/shard_map/ppermute | solution.py:23
  25.5 37.0 %collective-permute-start.9 = (bf16[384,896]{1,0:T(8,128)(2,1)}, bf16[384,896]{1,0:T(8,128)(2,1)}, u32[]{:S(2)}, u32[]{:S(2)}) collective-permute-start(bf16[384,896]{1,0:T(8,128)(2,1)} %get-tuple-element.43), channel_id=1, source_target_pairs={{0,18},{2,16},{16,2},{18,0},{1,19},{3,17},{17,3},{19,1},{4,22},{6,... | collective-permute-start | bytes 2064392 | tf_op jit(solution)/shard_map/ppermute | solution.py:653
  28.0 34.6 %collective-permute-start.8 = (bf16[384,896]{1,0:T(8,128)(2,1)}, bf16[384,896]{1,0:T(8,128)(2,1)}, u32[]{:S(2)}, u32[]{:S(2)}) collective-permute-start(bf16[384,896]{1,0:T(8,128)(2,1)} %get-tuple-element.43), channel_id=1, source_target_pairs={{0,16},{16,0},{1,17},{17,1},{2,18},{18,2},{3,19},{19,3},{4,20},{20... | collective-permute-start | bytes 2064392 | tf_op jit(solution)/shard_map/ppermute | solution.py:23
  28.5 34.1 %collective-permute-start.7 = (bf16[384,896]{1,0:T(8,128)(2,1)}, bf16[384,896]{1,0:T(8,128)(2,1)}, u32[]{:S(2)}, u32[]{:S(2)}) collective-permute-start(bf16[384,896]{1,0:T(8,128)(2,1)} %get-tuple-element.43), channel_id=1, source_target_pairs={{0,2},{2,0},{1,3},{3,1},{4,6},{6,4},{5,7},{7,5},{8,10},{10,8},{9,1... | collective-permute-start | bytes 2064392 | tf_op jit(solution)/shard_map/ppermute | solution.py:23
  29.6 26.2 %collective-permute-start.5 = (bf16[144,896]{1,0:T(8,128)(2,1)}, bf16[144,896]{1,0:T(8,128)(2,1)S(1)}, u32[]{:S(2)}, u32[]{:S(2)}) collective-permute-start(bf16[144,896]{1,0:T(8,128)(2,1)} %get-tuple-element.41), channel_id=1, source_target_pairs={{0,8},{4,12},{8,0},{12,4},{1,9},{5,13},{9,1},{13,5},{2,10},{6,14},... | collective-permute-start | bytes 774152 | tf_op jit(solution)/shard_map/ppermute | solution.py:23
  30.3 32.2 %collective-permute-start.4 = (bf16[336,896]{1,0:T(8,128)(2,1)}, bf16[336,896]{1,0:T(8,128)(2,1)S(1)}, u32[]{:S(2)}, u32[]{:S(2)}) collective-permute-start(bf16[336,896]{1,0:T(8,128)(2,1)} %get-tuple-element.39), channel_id=1, source_target_pairs={{0,4},{4,8},{8,12},{12,0},{1,5},{5,9},{9,13},{13,1},{2,6},{6,10},{... | collective-permute-start | bytes 1806344 | tf_op jit(solution)/shard_map/ppermute | solution.py:23
  55.8 6.8 %collective-permute-start.6 = (bf16[144,896]{1,0:T(8,128)(2,1)}, bf16[144,896]{1,0:T(8,128)(2,1)S(1)}, u32[]{:S(2)}, u32[]{:S(2)}) collective-permute-start(bf16[144,896]{1,0:T(8,128)(2,1)} %copy-done.29), channel_id=1, source_target_pairs={{0,12},{4,0},{8,4},{12,8},{1,13},{5,1},{9,5},{13,9},{2,14},{6,2},{... | collective-permute-start | bytes 774152 | tf_op jit(solution)/shard_map/ppermute | solution.py:23
  63.6 20.5 %collective-permute-start.13 = (bf16[256,896]{1,0:T(8,128)(2,1)S(1)}, bf16[256,896]{1,0:T(8,128)(2,1)}, u32[]{:S(2)}, u32[]{:S(2)}) collective-permute-start(bf16[256,896]{1,0:T(8,128)(2,1)S(1)} %get-tuple-element.44), channel_id=1, source_target_pairs={{0,8},{4,12},{8,0},{12,4},{1,9},{5,13},{9,1},{13,5},{2,10},{6,14},... | collective-permute-start | bytes 1376264 | tf_op jit(solution)/shard_map/ppermute | solution.py:23
  72.8 12.2 %collective-permute-start.12 = (bf16[192,896]{1,0:T(8,128)(2,1)}, bf16[192,896]{1,0:T(8,128)(2,1)}, u32[]{:S(2)}, u32[]{:S(2)}) collective-permute-start(bf16[192,896]{1,0:T(8,128)(2,1)} %pick.1), channel_id=1, source_target_pairs={{0,18},{2,16},{16,2},{18,0},{1,19},{3,17},{17,3},{19,1},{4,22},{6,... | collective-permute-start | bytes 1032200 | tf_op jit(solution)/shard_map/ppermute | solution.py:653
  75.2 13.7 %collective-permute-start.11 = (bf16[192,896]{1,0:T(8,128)(2,1)}, bf16[192,896]{1,0:T(8,128)(2,1)}, u32[]{:S(2)}, u32[]{:S(2)}) collective-permute-start(bf16[192,896]{1,0:T(8,128)(2,1)} %pick.1), channel_id=1, source_target_pairs={{0,16},{16,0},{1,17},{17,1},{2,18},{18,2},{3,19},{19,3},{4,20},{20... | collective-permute-start | bytes 1032200 | tf_op jit(solution)/shard_map/ppermute | solution.py:23
  75.7 13.2 %collective-permute-start.10 = (bf16[192,896]{1,0:T(8,128)(2,1)}, bf16[192,896]{1,0:T(8,128)(2,1)}, u32[]{:S(2)}, u32[]{:S(2)}) collective-permute-start(bf16[192,896]{1,0:T(8,128)(2,1)} %pick.1), channel_id=1, source_target_pairs={{0,2},{2,0},{1,3},{3,1},{4,6},{6,4},{5,7},{7,5},{8,10},{10,8},{9,1... | collective-permute-start | bytes 1032200 | tf_op jit(solution)/shard_map/ppermute | solution.py:23
  84.1 21.0 %collective-permute-start.16 = (bf16[256,896]{1,0:T(8,128)(2,1)}, bf16[256,896]{1,0:T(8,128)(2,1)S(1)}, u32[]{:S(2)}, u32[]{:S(2)}) collective-permute-start(bf16[256,896]{1,0:T(8,128)(2,1)} %pass_after.2), channel_id=1, source_target_pairs={{0,4},{4,8},{8,12},{12,0},{1,5},{5,9},{9,13},{13,1},{2,6},{6,10},{... | collective-permute-start | bytes 1376264 | tf_op jit(solution)/shard_map/ppermute | solution.py:23
  107.0 6.9 %collective-permute-start.18 = (bf16[256,256]{1,0:T(8,128)(2,1)S(1)}, bf16[256,256]{1,0:T(8,128)(2,1)S(1)}, u32[]{:S(2)}, u32[]{:S(2)}) collective-permute-start(bf16[256,256]{1,0:T(8,128)(2,1)S(1)} %get-tuple-element.51.refs_0_), channel_id=1, source_target_pairs={{0,8},{4,12},{1,9},{5,13},{2,10},{6,14},{3,11},{7,15},{16,24},{20,... | collective-permute-start | bytes 393224 | tf_op jit(solution)/shard_map/ppermute | solution.py:29
  117.3 14.7 %collective-permute-start.21 = (bf16[256,896]{1,0:T(8,128)(2,1)}, bf16[256,896]{1,0:T(8,128)(2,1)S(1)}, u32[]{:S(2)}, u32[]{:S(2)}) collective-permute-start(bf16[256,896]{1,0:T(8,128)(2,1)} %pass_after.3), channel_id=1, source_target_pairs={{0,12},{4,0},{8,4},{12,8},{1,13},{5,1},{9,5},{13,9},{2,14},{6,2},{... | collective-permute-start | bytes 1376264 | tf_op jit(solution)/shard_map/ppermute | solution.py:23
  132.0 8.0 %collective-permute-start.22 = (f32[128,256]{1,0:T(8,128)S(1)}, f32[128,256]{1,0:T(8,128)S(1)}, u32[]{:S(2)}, u32[]{:S(2)}) collective-permute-start(f32[128,256]{1,0:T(8,128)S(1)} %get-tuple-element.58), channel_id=1, source_target_pairs={{4,0},{8,4},{12,8},{5,1},{9,5},{13,9},{6,2},{10,6},{14,10},{7,3},{... | collective-permute-start | bytes 393224 | tf_op jit(solution)/shard_map/ppermute | solution.py:29
  133.3 12.8 %collective-permute-start.23 = (f32[128,256]{1,0:T(8,128)S(1)}, f32[128,256]{1,0:T(8,128)S(1)}, u32[]{:S(2)}, u32[]{:S(2)}) collective-permute-start(f32[128,256]{1,0:T(8,128)S(1)} %get-tuple-element.59), channel_id=1, source_target_pairs={{8,0},{12,4},{9,1},{13,5},{10,2},{14,6},{11,3},{15,7},{24,16},{28,... | collective-permute-start | bytes 393224 | tf_op jit(solution)/shard_map/ppermute | solution.py:29
  134.6 11.7 %collective-permute-start.19 = (bf16[128,512]{1,0:T(8,128)(2,1)S(1)}, bf16[128,512]{1,0:T(8,128)(2,1)S(1)}, u32[]{:S(2)}, u32[]{:S(2)}) collective-permute-start(bf16[128,512]{1,0:T(8,128)(2,1)S(1)} %get-tuple-element.53.own_query), channel_id=1, source_target_pairs={{0,1},{1,0},{2,3},{3,2},{4,5},{5,4},{6,7},{7,6},{8,9},{9,8},{10,11... | collective-permute-start | bytes 393224 | tf_op jit(solution)/shard_map/ppermute | solution.py:23
  148.9 8.2 %collective-permute-start.25 = (f32[248,128]{1,0:T(8,128)S(1)}, f32[248,128]{1,0:T(8,128)S(1)}, u32[]{:S(2)}, u32[]{:S(2)}) collective-permute-start(f32[248,128]{1,0:T(8,128)S(1)} %get-tuple-element.65), channel_id=1, source_target_pairs={{0,4},{4,8},{8,12},{12,0},{1,5},{5,9},{9,13},{13,1},{2,6},{6,10},{... | collective-permute-start | bytes 380936 | tf_op jit(solution)/shard_map/ppermute | solution.py:23
  148.9 12.7 %collective-permute-start.26 = (f32[248,128]{1,0:T(8,128)S(1)}, f32[248,128]{1,0:T(8,128)S(1)}, u32[]{:S(2)}, u32[]{:S(2)}) collective-permute-start(f32[248,128]{1,0:T(8,128)S(1)} %get-tuple-element.66), channel_id=1, source_target_pairs={{0,8},{4,12},{8,0},{12,4},{1,9},{5,13},{9,1},{13,5},{2,10},{6,14},... | collective-permute-start | bytes 380936 | tf_op jit(solution)/shard_map/ppermute | solution.py:23
  149.0 12.6 %collective-permute-start.27 = (f32[248,128]{1,0:T(8,128)S(1)}, f32[248,128]{1,0:T(8,128)S(1)}, u32[]{:S(2)}, u32[]{:S(2)}) collective-permute-start(f32[248,128]{1,0:T(8,128)S(1)} %get-tuple-element.67), channel_id=1, source_target_pairs={{0,12},{4,0},{8,4},{12,8},{1,13},{5,1},{9,5},{13,9},{2,14},{6,2},{... | collective-permute-start | bytes 380936 | tf_op jit(solution)/shard_map/ppermute | solution.py:23
  165.0 9.6 %collective-permute-start.28 = (f32[192,512]{1,0:T(8,128)S(1)}, f32[192,512]{1,0:T(8,128)S(1)}, u32[]{:S(2)}, u32[]{:S(2)}) collective-permute-start(f32[192,512]{1,0:T(8,128)S(1)} %get-tuple-element.70), channel_id=1, source_target_pairs={{0,2},{2,0},{1,3},{3,1},{4,6},{6,4},{5,7},{7,5},{8,10},{10,8},{9,1... | collective-permute-start | bytes 1179656 | tf_op jit(solution)/shard_map/ppermute | solution.py:23
  (36 other events, 239.3 us)

commit v13 on v7

--- a/solution.py
+++ b/solution.py
@@ -164,6 +164,21 @@
                 ]
 
 
+def pass_kernel(*refs):
+    del refs
+
+
+def pass_after(value, *earlier):
+    return pl.pallas_call(
+        pass_kernel,
+        out_shape=jax.ShapeDtypeStruct(value.shape, value.dtype),
+        in_specs=[in_place()] * (1 + len(earlier)),
+        out_specs=in_place(),
+        input_output_aliases={0: 0},
+        name="pass_after",
+    )(value, *earlier)
+
+
 def cut_kernel(unused, seq_count, tokens, *refs):
     for steps, block in enumerate(refs[unused:]):
         target = ring_index(lax.axis_index("seq") + steps - seq_count, seq_count)
@@ -334,8 +349,8 @@
         ).astype(jnp.bfloat16)
 
 
-def sum_kernel(kept, arrived, *sums):
-    for back, total in enumerate(sums):
+def sum_kernel(unused, kept, arrived, *refs):
+    for back, total in enumerate(refs[unused:]):
         total[...] = kept[back] + arrived[back]
 
 
@@ -616,7 +631,7 @@
                 pltpu.VMEM((SEGS * joint_rank, down_width), bf16),
                 pltpu.VMEM((SEGS, low_width, 2 * held_up), bf16),
             ],
-            compiler_params=pltpu.CompilerParams(vmem_limit_bytes=16 * mebibyte),
+            compiler_params=pltpu.CompilerParams(vmem_limit_bytes=8 * mebibyte),
             cost_estimate=cost(0, 8 * frozen_rows * share),
             name="pack",
         )(own_down, far_down, own_up, far_up, before, after)
@@ -667,7 +682,7 @@
             out_shape=[jax.ShapeDtypeStruct((rows, down_width), bf16)] * seq_count,
             in_specs=[in_vmem()] + [in_place()] * len(early),
             out_specs=[by_block((rows, down_width))] * seq_count,
-            compiler_params=pltpu.CompilerParams(vmem_limit_bytes=16 * mebibyte),
+            compiler_params=pltpu.CompilerParams(vmem_limit_bytes=8 * mebibyte),
             cost_estimate=cost(0, 4 * rows * width),
             name="cut",
         )(local_tokens, *early)
@@ -736,7 +751,7 @@
             pltpu.VMEM((matrix_rows, width), bf16),
             pltpu.SemaphoreType.DMA((len(entries) + len(up_entries) + 1,)),
         ],
-        compiler_params=pltpu.CompilerParams(vmem_limit_bytes=20 * mebibyte),
+        compiler_params=pltpu.CompilerParams(vmem_limit_bytes=12 * mebibyte),
         cost_estimate=cost(2 * rows * width * matrix_rows, 2 * width * (matrix_rows + rows)),
         name="project",
     )(local_tokens, *arrays, *early)
@@ -745,21 +760,22 @@
 
     other_part = shift(part, "tp", 1)
     queries, pairs, low_rank = pl.pallas_call(
-        functools.partial(qkv_kernel, seq_count, 1),
+        functools.partial(qkv_kernel, seq_count, 0),
         out_shape=(
             jax.ShapeDtypeStruct((QHEADS * own_rows, HEAD_WIDTH), bf16),
             jax.ShapeDtypeStruct((rows, 2 * HEAD_WIDTH), bf16),
             jax.ShapeDtypeStruct((rows, joint_rank), bf16),
         ),
-        in_specs=[in_smem()] + [in_vmem()] * 5 + [in_place()],
+        in_specs=[in_smem()] + [in_vmem()] * 5,
         out_specs=(in_vmem(),) * 3,
         compiler_params=pltpu.CompilerParams(vmem_limit_bytes=8 * mebibyte),
         cost_estimate=cost(2 * rows * 3 * 64 * 640, 8 * rows * features),
         name="qkv",
-    )(document_lengths, part, other_part, up_blocks, cosines, sines, column_parts[1])
+    )(document_lengths, part, other_part, up_blocks, cosines, sines)
 
     blocks = [pairs] + [push(pairs, "seq", back) for back in range(1, half_count + 1)]
     block_count = len(blocks)
+    column_parts[1] = shift(pass_after(column_blocks[1], *blocks[1:]), "seq", 1)
     incoming = output_gradient[0]
     early_columns = []
     attention, query_grad, kept, sent = pl.pallas_call(
@@ -785,15 +801,16 @@
     )(document_lengths, queries, incoming, cosines, sines, *blocks, *early_columns)
 
     other_query = shift(query_grad, "tp", 1)
+    due = [column_parts[1]]
     pair_sums = pl.pallas_call(
-        sum_kernel,
+        functools.partial(sum_kernel, len(due)),
         out_shape=[jax.ShapeDtypeStruct((own_rows, 2 * HEAD_WIDTH), f32)] * block_count,
-        in_specs=[in_vmem()] * 2,
+        in_specs=[in_vmem()] * 2 + [in_place()] * len(due),
         out_specs=[in_vmem()] * block_count,
         compiler_params=pltpu.CompilerParams(vmem_limit_bytes=8 * mebibyte),
         cost_estimate=cost(0, 12 * block_count * own_rows * 2 * HEAD_WIDTH),
         name="pair_sums",
-    )(kept, shift(sent, "tp", 1))
+    )(kept, shift(sent, "tp", 1), *due)
     pair_terms = [pair_sums[0]]
     pair_terms += [push(pair_sums[back], "seq", -back) for back in range(1, block_count)]
     pair_grad, late_block = pl.pallas_call(
@@ -919,7 +936,7 @@
             ),
         ),
         input_output_aliases={1 + term_count: 0, 2 + term_count: 1},
-        compiler_params=pltpu.CompilerParams(vmem_limit_bytes=16 * mebibyte),
+        compiler_params=pltpu.CompilerParams(vmem_limit_bytes=8 * mebibyte),
         name="bank_rows",
     )(
         bank_rows,

time: 163 us -> 160 us (0.982)
  waiting for transfers between devices: 75.8 us -> 59.6 us
  local copies, waits for them, and re-layouts: 19 us -> 26.8 us
  starting transfers between devices: 40.1 us -> 45.1 us
    ppermute x22, waiting for transfers between devices: 52.1 us -> 40.1 us  [shift(): lax.ppermute(value, axis, [(at, (at + steps) % count) for at in range(cou...]
    unnamed x19 -> x37, local copies, waits for them, and re-layouts: 5.42 us -> 13.2 us
    ppermute x22, starting transfers between devices: 28.6 us -> 31.9 us  [shift(): lax.ppermute(value, axis, [(at, (at + steps) % count) for at in range(cou...]
    ppermute x4, waiting for transfers between devices: 16.9 us -> 14 us  [push(): return lax.ppermute(value, axis, pairs)]
    ppermute x4, starting transfers between devices: 6.52 us -> 8.26 us  [push(): return lax.ppermute(value, axis, pairs)]
  transfers between devices with their start and end apart: 28 -> 28, of which waited for: 20 -> 17; matrix products, arithmetic and copies ran while one was open for 10% -> 10% of each run, Pallas kernels for 4% -> 6%
where the time goes in v13:
time: 160 us; the launch traced here: 158 us
  waiting for transfers between devices  59.6 us (37%)
  starting transfers between devices  45.1 us (28%)
  local copies, waits for them, and re-layouts  26.8 us (17%)
  Pallas kernels  21.9 us (14%)
  other arithmetic  2.42 us (2%)
  between operations  2.22 us (1%)
    ppermute x22, waiting for transfers between devices, shift(): lax.ppermute(value, axis, [(at, (at + steps) % count) for at in range(cou...  40.1 us
    ppermute x22, starting transfers between devices, shift(): lax.ppermute(value, axis, [(at, (at + steps) % count) for at in range(cou...  31.9 us
    ppermute x4, waiting for transfers between devices, push(): return lax.ppermute(value, axis, pairs)  14 us
    unnamed x37, local copies, waits for them, and re-layouts  13.2 us
    ppermute x4, starting transfers between devices, push(): return lax.ppermute(value, axis, pairs)  8.26 us
    ppermute x2, waiting for transfers between devices, over_plane(): lax.ppermute(value, ('groups', 'batch'), over_both)  5.55 us
    ppermute x2, starting transfers between devices, over_plane(): lax.ppermute(value, ('groups', 'batch'), over_both)  4.96 us
    pallas_call x1, Pallas kernels, shards(): pl.pallas_call(token_kernel, grid=(width // chunk,), out_shape=jax.ShapeD...  4.84 us
  transfers between devices with their start and end apart: 28, of which 17 were waited for; matrix products, arithmetic and copies ran while one was open for 10% of the time, Pallas kernels for 6%

profile of v13, /device:TPU:0, one launch (start us, length us, event | category | flops | bytes accessed | tf_op | source)
XLA Modules:
  0.0 158.0 jit_solution(1291393761277379407)
XLA Ops:
  1.7 5.1 %collective-permute-start.1 = (bf16[192,896]{1,0:T(8,128)(2,1)S(1)}, bf16[192,896]{1,0:T(8,128)(2,1)S(1)}, u32[]{:S(2)}, u32[]{:S(2)}) collective-permute-start(bf16[192,896]{1,0:T(8,128)(2,1)S(1)} %constant_dynamic-slice_fusion.1), channel_id=1, source_target_pairs={{0,12},{4,0},{8,4},{12,8},{1,13},{5,1},{9,5},{13,9},{2,14},{6,2},{... | collective-permute-start | bytes 1032200 | tf_op jit(solution)/shard_map/ppermute | solution.py:23
  8.7 2.7 %gather_fusion.1 = bf16[3,64,448]{2,1,0:T(8,128)(2,1)S(1)} fusion(bf16[64,64,448]{2,1,0:T(8,128)(2,1)} %bitcast.19, s32[1024]{0:T(1024)S(1)} %pad_clamp_fusion), kind=kCustom, calls=%fused_computation.1 | custom fusion | bytes 344076 | tf_op jit(solution)/shard_map/gather | solution.py:619
  14.7 2.7 %gather_fusion = bf16[3,64,448]{2,1,0:T(8,128)(2,1)S(1)} fusion(bf16[64,64,448]{2,1,0:T(8,128)(2,1)} %bitcast.20, s32[1024]{0:T(1024)S(1)} %pad_clamp_fusion.1), kind=kCustom, calls=%fused_computation | custom fusion | bytes 344076 | tf_op jit(solution)/shard_map/gather | solution.py:621
  18.4 4.0 %collective-permute-done.before.refs_1_ = bf16[192,896]{1,0:T(8,128)(2,1)S(1)} collective-permute-done((bf16[192,896]{1,0:T(8,128)(2,1)S(1)}, bf16[192,896]{1,0:T(8,128)(2,1)S(1)}, u32[]{:S(2)}, u32[]{:S(2)}) %collective-permute-start) | collective-permute-done | bytes 344096 | tf_op jit(solution)/shard_map/ppermute | solution.py:23
  32.9 9.2 %collective-permute-done.4.refs_0_.refs_3_ = bf16[336,896]{1,0:T(8,128)(2,1)S(1)} collective-permute-done((bf16[336,896]{1,0:T(8,128)(2,1)S(1)}, bf16[336,896]{1,0:T(8,128)(2,1)S(1)}, u32[]{:S(2)}, u32[]{:S(2)}) %collective-permute-start.4) | collective-permute-done | bytes 602144 | tf_op jit(solution)/shard_map/ppermute | solution.py:23
  42.9 4.5 %broadcast_in_dim.47.refs_1_.down_zeros = f32[64,64,1,448]{3,2,1,0:T(1,128)S(1)} broadcast(f32[]{:T(128)} %constant.11.clone.1), dimensions={} | broadcast | bytes 7340036 | tf_op jit(solution)/shard_map/broadcast_in_dim | solution.py:593
  47.6 3.2 %copy-done.1 = f32[64,64,1,448]{3,2,1,0:T(1,128)} copy-done((f32[64,64,1,448]{3,2,1,0:T(1,128)}, f32[64,64,1,448]{3,2,1,0:T(1,128)S(1)}, u32[]{:S(2)}) %copy-start.1) | copy-done | bytes 7340056
  52.4 10.2 %collective-permute-start.13 = (bf16[256,896]{1,0:T(8,128)(2,1)S(1)}, bf16[256,896]{1,0:T(8,128)(2,1)S(1)}, u32[]{:S(2)}, u32[]{:S(2)}) collective-permute-start(bf16[256,896]{1,0:T(8,128)(2,1)S(1)} %get-tuple-element.44), channel_id=1, source_target_pairs={{0,8},{4,12},{8,0},{12,4},{1,9},{5,13},{9,1},{13,5},{2,10},{6,14},... | collective-permute-start | bytes 1376264 | tf_op jit(solution)/shard_map/ppermute | solution.py:23
  62.7 2.5 %collective-permute-start.12 = (bf16[192,896]{1,0:T(8,128)(2,1)S(1)}, bf16[192,896]{1,0:T(8,128)(2,1)S(1)}, u32[]{:S(2)}, u32[]{:S(2)}) collective-permute-start(bf16[192,896]{1,0:T(8,128)(2,1)S(1)} %slice.32), channel_id=1, source_target_pairs={{0,18},{2,16},{16,2},{18,0},{1,19},{3,17},{17,3},{19,1},{4,22},{6,... | collective-permute-start | bytes 1032200 | tf_op jit(solution)/shard_map/ppermute | solution.py:644
  66.2 5.5 %collective-permute-done.12.refs_12_ = bf16[192,896]{1,0:T(8,128)(2,1)S(1)} collective-permute-done((bf16[192,896]{1,0:T(8,128)(2,1)S(1)}, bf16[192,896]{1,0:T(8,128)(2,1)S(1)}, u32[]{:S(2)}, u32[]{:S(2)}) %collective-permute-start.12) | collective-permute-done | bytes 344096 | tf_op jit(solution)/shard_map/ppermute | solution.py:644
  71.8 3.6 %collective-permute-done.11.refs_11_ = bf16[192,896]{1,0:T(8,128)(2,1)S(1)} collective-permute-done((bf16[192,896]{1,0:T(8,128)(2,1)S(1)}, bf16[192,896]{1,0:T(8,128)(2,1)S(1)}, u32[]{:S(2)}, u32[]{:S(2)}) %collective-permute-start.11) | collective-permute-done | bytes 344096 | tf_op jit(solution)/shard_map/ppermute | solution.py:23
  76.5 4.7 %project.1 = (f32[256,896]{1,0:T(8,128)S(1)}, bf16[896,3584]{1,0:T(8,128)(2,1)S(1)}, bf16[3,64,640]{2,1,0:T(8,128)(2,1)S(1)}) custom-call(bf16[256,3584]{1,0:T(8,128)(2,1)S(1)} %bitcast.16, bf16[192,3584]{1,0:T(8,128)(2,1)S(1)} %copy-done.6, bf16[192,896]{1,0:T(8,128)(2,1)S(1)} %collective-permute-done.before.refs_1_, ...), custom_call_target="tpu_custom_call" | custom-call | flops 1644167168 | bytes 8257536 | tf_op jit(solution)/shard_map/project/pallas_call | solution.py:738
  81.3 2.7 %copy-done.4 = bf16[896,3584]{1,0:T(8,128)(2,1)} copy-done((bf16[896,3584]{1,0:T(8,128)(2,1)}, bf16[896,3584]{1,0:T(8,128)(2,1)S(1)}, u32[]{:S(2)}) %copy-start.4) | copy-done | bytes 6422552
  89.0 4.2 %collective-permute-start.15 = (bf16[256,256]{1,0:T(8,128)(2,1)S(1)}, bf16[256,256]{1,0:T(8,128)(2,1)S(1)}, u32[]{:S(2)}, u32[]{:S(2)}) collective-permute-start(bf16[256,256]{1,0:T(8,128)(2,1)S(1)} %get-tuple-element.48.refs_0_), channel_id=1, source_target_pairs={{0,4},{4,8},{8,12},{1,5},{5,9},{9,13},{2,6},{6,10},{10,14},{3,7},{... | collective-permute-start | bytes 393224 | tf_op jit(solution)/shard_map/ppermute | solution.py:29
  96.7 3.3 %collective-permute-start.19 = (bf16[256,896]{1,0:T(8,128)(2,1)}, bf16[256,896]{1,0:T(8,128)(2,1)S(1)}, u32[]{:S(2)}, u32[]{:S(2)}) collective-permute-start(bf16[256,896]{1,0:T(8,128)(2,1)} %pass_after.1), channel_id=1, source_target_pairs={{0,4},{4,8},{8,12},{12,0},{1,5},{5,9},{9,13},{13,1},{2,6},{6,10},{... | collective-permute-start | bytes 1376264 | tf_op jit(solution)/shard_map/ppermute | solution.py:23
  103.6 3.4 %attention.1 = (bf16[128,512]{1,0:T(8,128)(2,1)}, bf16[128,512]{1,0:T(8,128)(2,1)S(1)}, f32[3,128,256]{2,1,0:T(8,128)S(1)}, f32[3,128,256]{2,1,0:T(8,128)S(1)}) custom-call(s32[2,3]{1,0:T(2,128)S(1)} %copy-done.14, bf16[512,128]{1,0:T(8,128)(2,1)S(1)} %get-tuple-element.47.queries, bf16[128,512]{1,0:T(8,128)(2,1)S(1)} %bitcast.17, ...), custom_call_target="tpu_custom_call" | custom-call | flops 503316480 | bytes 786432 | tf_op jit(solution)/shard_map/attention/pallas_call | solution.py:781
  108.7 2.6 %collective-permute-done.19.refs_0_.refs_1_ = bf16[256,896]{1,0:T(8,128)(2,1)S(1)} collective-permute-done((bf16[256,896]{1,0:T(8,128)(2,1)}, bf16[256,896]{1,0:T(8,128)(2,1)S(1)}, u32[]{:S(2)}, u32[]{:S(2)}) %collective-permute-start.19) | collective-permute-done | bytes 458784 | tf_op jit(solution)/shard_map/ppermute | solution.py:23
  113.9 4.7 %collective-permute-done.20.refs_1_ = f32[128,256]{1,0:T(8,128)S(1)} collective-permute-done((f32[128,256]{1,0:T(8,128)S(1)}, f32[128,256]{1,0:T(8,128)S(1)}, u32[]{:S(2)}, u32[]{:S(2)}) %collective-permute-start.20) | collective-permute-done | bytes 131104 | tf_op jit(solution)/shard_map/ppermute | solution.py:29
  118.6 7.2 %collective-permute-done.21.refs_2_ = f32[128,256]{1,0:T(8,128)S(1)} collective-permute-done((f32[128,256]{1,0:T(8,128)S(1)}, f32[128,256]{1,0:T(8,128)S(1)}, u32[]{:S(2)}, u32[]{:S(2)}) %collective-permute-start.21) | collective-permute-done | bytes 131104 | tf_op jit(solution)/shard_map/ppermute | solution.py:29
  133.2 5.4 %collective-permute-done.24.refs_5_ = f32[248,128]{1,0:T(8,128)S(1)} collective-permute-done((f32[248,128]{1,0:T(8,128)S(1)}, f32[248,128]{1,0:T(8,128)S(1)}, u32[]{:S(2)}, u32[]{:S(2)}) %collective-permute-start.24) | collective-permute-done | bytes 127008 | tf_op jit(solution)/shard_map/ppermute | solution.py:23
  138.6 5.4 %collective-permute-done.25.refs_6_ = f32[248,128]{1,0:T(8,128)S(1)} collective-permute-done((f32[248,128]{1,0:T(8,128)S(1)}, f32[248,128]{1,0:T(8,128)S(1)}, u32[]{:S(2)}, u32[]{:S(2)}) %collective-permute-start.25) | collective-permute-done | bytes 127008 | tf_op jit(solution)/shard_map/ppermute | solution.py:23
  147.5 4.8 %token_gradient.1 = bf16[256,3584]{1,0:T(8,128)(2,1)} custom-call(bf16[256,896]{1,0:T(8,128)(2,1)S(1)} %get-tuple-element.60.gradients, bf16[896,3584]{1,0:T(8,128)(2,1)S(1)} %copy-done.5), custom_call_target="tpu_custom_call" | custom-call | flops 1644167168 | bytes 8257536 | tf_op jit(solution)/shard_map/token_gradient/pallas_call | solution.py:865
  152.3 2.7 %collective-permute-done.27.far = f32[192,512]{1,0:T(8,128)S(1)} collective-permute-done((f32[192,512]{1,0:T(8,128)S(1)}, f32[192,512]{1,0:T(8,128)S(1)}, u32[]{:S(2)}, u32[]{:S(2)}) %collective-permute-start.27) | collective-permute-done | bytes 393248 | tf_op jit(solution)/shard_map/ppermute | solution.py:23
  155.0 3.0 %bank_rows.1 = (f32[64,64,1,448]{3,2,1,0:T(1,128)}, f32[64,32,80]{2,1,0:T(8,128)}) custom-call(s32[6]{0:T(128)S(1)} %pad_add_fusion.refs_5_.bank_rows, f32[192,448]{1,0:T(8,128)S(1)} %get-tuple-element.69.own_down, f32[192,512]{1,0:T(8,128)S(1)} %collective-permute-done.27.far, ...), custom_call_target="tpu_custom_call", output_to_operand_aliasing={{0}: (4, {}), {1}: (5, {})} | custom-call | tf_op jit(solution)/shard_map/bank_rows/pallas_call | solution.py:917
  (101 shorter events, 48.2 us)
Async XLA Ops:
  1.7 16.7 %collective-permute-start.1 = (bf16[192,896]{1,0:T(8,128)(2,1)S(1)}, bf16[192,896]{1,0:T(8,128)(2,1)S(1)}, u32[]{:S(2)}, u32[]{:S(2)}) collective-permute-start(bf16[192,896]{1,0:T(8,128)(2,1)S(1)} %constant_dynamic-slice_fusion.1), channel_id=1, source_target_pairs={{0,12},{4,0},{8,4},{12,8},{1,13},{5,1},{9,5},{13,9},{2,14},{6,2},{... | collective-permute-start | bytes 1032200 | tf_op jit(solution)/shard_map/ppermute | solution.py:23
  6.8 15.6 %collective-permute-start = (bf16[192,896]{1,0:T(8,128)(2,1)S(1)}, bf16[192,896]{1,0:T(8,128)(2,1)S(1)}, u32[]{:S(2)}, u32[]{:S(2)}) collective-permute-start(bf16[192,896]{1,0:T(8,128)(2,1)S(1)} %constant_dynamic-slice_fusion.1), channel_id=1, source_target_pairs={{0,4},{4,8},{8,12},{12,0},{1,5},{5,9},{9,13},{13,1},{2,6},{6,10},{... | collective-permute-start | bytes 1032200 | tf_op jit(solution)/shard_map/ppermute | solution.py:23
  11.4 7.0 %collective-permute-start.2 = (bf16[3,64,448]{2,1,0:T(8,128)(2,1)S(1)}, bf16[3,64,448]{2,1,0:T(8,128)(2,1)S(1)}, u32[]{:S(2)}, u32[]{:S(2)}) collective-permute-start(bf16[3,64,448]{2,1,0:T(8,128)(2,1)S(1)} %gather_fusion.1), channel_id=1, source_target_pairs={{0,2},{2,0},{1,3},{3,1},{4,6},{6,4},{5,7},{7,5},{8,10},{10,8},{9,1... | collective-permute-start | bytes 516104 | tf_op jit(solution)/shard_map/ppermute | solution.py:23
  13.5 4.8 %collective-permute-start.3 = (bf16[3,32,80]{2,1,0:T(8,128)(2,1)S(1)}, bf16[3,32,80]{2,1,0:T(8,128)(2,1)S(1)}, u32[]{:S(2)}, u32[]{:S(2)}) collective-permute-start(bf16[3,32,80]{2,1,0:T(8,128)(2,1)S(1)} %gather_fusion.3), channel_id=1, source_target_pairs={{0,2},{2,0},{1,3},{3,1},{4,6},{6,4},{5,7},{7,5},{8,10},{10,8},{9,1... | collective-permute-start | bytes 46088 | tf_op jit(solution)/shard_map/ppermute | solution.py:23
  23.7 18.4 %collective-permute-start.4 = (bf16[336,896]{1,0:T(8,128)(2,1)S(1)}, bf16[336,896]{1,0:T(8,128)(2,1)S(1)}, u32[]{:S(2)}, u32[]{:S(2)}) collective-permute-start(bf16[336,896]{1,0:T(8,128)(2,1)S(1)} %get-tuple-element.39), channel_id=1, source_target_pairs={{0,4},{4,8},{8,12},{12,0},{1,5},{5,9},{9,13},{13,1},{2,6},{6,10},{... | collective-permute-start | bytes 1806344 | tf_op jit(solution)/shard_map/ppermute | solution.py:23
  26.6 38.6 %collective-permute-start.9 = (bf16[384,896]{1,0:T(8,128)(2,1)}, bf16[384,896]{1,0:T(8,128)(2,1)}, u32[]{:S(2)}, u32[]{:S(2)}) collective-permute-start(bf16[384,896]{1,0:T(8,128)(2,1)} %get-tuple-element.43), channel_id=1, source_target_pairs={{0,18},{2,16},{16,2},{18,0},{1,19},{3,17},{17,3},{19,1},{4,22},{6,... | collective-permute-start | bytes 2064392 | tf_op jit(solution)/shard_map/ppermute | solution.py:644
  29.1 36.7 %collective-permute-start.8 = (bf16[384,896]{1,0:T(8,128)(2,1)}, bf16[384,896]{1,0:T(8,128)(2,1)}, u32[]{:S(2)}, u32[]{:S(2)}) collective-permute-start(bf16[384,896]{1,0:T(8,128)(2,1)} %get-tuple-element.43), channel_id=1, source_target_pairs={{0,16},{16,0},{1,17},{17,1},{2,18},{18,2},{3,19},{19,3},{4,20},{20... | collective-permute-start | bytes 2064392 | tf_op jit(solution)/shard_map/ppermute | solution.py:23
  31.6 34.6 %collective-permute-start.7 = (bf16[384,896]{1,0:T(8,128)(2,1)}, bf16[384,896]{1,0:T(8,128)(2,1)S(1)}, u32[]{:S(2)}, u32[]{:S(2)}) collective-permute-start(bf16[384,896]{1,0:T(8,128)(2,1)} %get-tuple-element.43), channel_id=1, source_target_pairs={{0,2},{2,0},{1,3},{3,1},{4,6},{6,4},{5,7},{7,5},{8,10},{10,8},{9,1... | collective-permute-start | bytes 2064392 | tf_op jit(solution)/shard_map/ppermute | solution.py:23
  32.2 20.2 %collective-permute-start.5 = (bf16[144,896]{1,0:T(8,128)(2,1)}, bf16[144,896]{1,0:T(8,128)(2,1)S(1)}, u32[]{:S(2)}, u32[]{:S(2)}) collective-permute-start(bf16[144,896]{1,0:T(8,128)(2,1)} %get-tuple-element.41), channel_id=1, source_target_pairs={{0,8},{4,12},{8,0},{12,4},{1,9},{5,13},{9,1},{13,5},{2,10},{6,14},... | collective-permute-start | bytes 774152 | tf_op jit(solution)/shard_map/ppermute | solution.py:23
  42.1 20.5 %collective-permute-start.6 = (bf16[144,896]{1,0:T(8,128)(2,1)}, bf16[144,896]{1,0:T(8,128)(2,1)S(1)}, u32[]{:S(2)}, u32[]{:S(2)}) collective-permute-start(bf16[144,896]{1,0:T(8,128)(2,1)} %get-tuple-element.42), channel_id=1, source_target_pairs={{0,12},{4,0},{8,4},{12,8},{1,13},{5,1},{9,5},{13,9},{2,14},{6,2},{... | collective-permute-start | bytes 774152 | tf_op jit(solution)/shard_map/ppermute | solution.py:23
  52.4 24.1 %collective-permute-start.13 = (bf16[256,896]{1,0:T(8,128)(2,1)S(1)}, bf16[256,896]{1,0:T(8,128)(2,1)S(1)}, u32[]{:S(2)}, u32[]{:S(2)}) collective-permute-start(bf16[256,896]{1,0:T(8,128)(2,1)S(1)} %get-tuple-element.44), channel_id=1, source_target_pairs={{0,8},{4,12},{8,0},{12,4},{1,9},{5,13},{9,1},{13,5},{2,10},{6,14},... | collective-permute-start | bytes 1376264 | tf_op jit(solution)/shard_map/ppermute | solution.py:23
  62.7 9.1 %collective-permute-start.12 = (bf16[192,896]{1,0:T(8,128)(2,1)S(1)}, bf16[192,896]{1,0:T(8,128)(2,1)S(1)}, u32[]{:S(2)}, u32[]{:S(2)}) collective-permute-start(bf16[192,896]{1,0:T(8,128)(2,1)S(1)} %slice.32), channel_id=1, source_target_pairs={{0,18},{2,16},{16,2},{18,0},{1,19},{3,17},{17,3},{19,1},{4,22},{6,... | collective-permute-start | bytes 1032200 | tf_op jit(solution)/shard_map/ppermute | solution.py:644
  65.2 10.2 %collective-permute-start.11 = (bf16[192,896]{1,0:T(8,128)(2,1)S(1)}, bf16[192,896]{1,0:T(8,128)(2,1)S(1)}, u32[]{:S(2)}, u32[]{:S(2)}) collective-permute-start(bf16[192,896]{1,0:T(8,128)(2,1)S(1)} %slice.32), channel_id=1, source_target_pairs={{0,16},{16,0},{1,17},{17,1},{2,18},{18,2},{3,19},{19,3},{4,20},{20... | collective-permute-start | bytes 1032200 | tf_op jit(solution)/shard_map/ppermute | solution.py:23
  65.7 9.7 %collective-permute-start.10 = (bf16[192,896]{1,0:T(8,128)(2,1)S(1)}, bf16[192,896]{1,0:T(8,128)(2,1)S(1)}, u32[]{:S(2)}, u32[]{:S(2)}) collective-permute-start(bf16[192,896]{1,0:T(8,128)(2,1)S(1)} %slice.32), channel_id=1, source_target_pairs={{0,2},{2,0},{1,3},{3,1},{4,6},{6,4},{5,7},{7,5},{8,10},{10,8},{9,1... | collective-permute-start | bytes 1032200 | tf_op jit(solution)/shard_map/ppermute | solution.py:23
  87.6 6.4 %collective-permute-start.16 = (bf16[256,256]{1,0:T(8,128)(2,1)S(1)}, bf16[256,256]{1,0:T(8,128)(2,1)S(1)}, u32[]{:S(2)}, u32[]{:S(2)}) collective-permute-start(bf16[256,256]{1,0:T(8,128)(2,1)S(1)} %get-tuple-element.48.refs_0_), channel_id=1, source_target_pairs={{0,8},{4,12},{1,9},{5,13},{2,10},{6,14},{3,11},{7,15},{16,24},{20,... | collective-permute-start | bytes 393224 | tf_op jit(solution)/shard_map/ppermute | solution.py:29
  89.0 7.0 %collective-permute-start.15 = (bf16[256,256]{1,0:T(8,128)(2,1)S(1)}, bf16[256,256]{1,0:T(8,128)(2,1)S(1)}, u32[]{:S(2)}, u32[]{:S(2)}) collective-permute-start(bf16[256,256]{1,0:T(8,128)(2,1)S(1)} %get-tuple-element.48.refs_0_), channel_id=1, source_target_pairs={{0,4},{4,8},{8,12},{1,5},{5,9},{9,13},{2,6},{6,10},{10,14},{3,7},{... | collective-permute-start | bytes 393224 | tf_op jit(solution)/shard_map/ppermute | solution.py:29
  96.7 14.6 %collective-permute-start.19 = (bf16[256,896]{1,0:T(8,128)(2,1)}, bf16[256,896]{1,0:T(8,128)(2,1)S(1)}, u32[]{:S(2)}, u32[]{:S(2)}) collective-permute-start(bf16[256,896]{1,0:T(8,128)(2,1)} %pass_after.1), channel_id=1, source_target_pairs={{0,4},{4,8},{8,12},{12,0},{1,5},{5,9},{9,13},{13,1},{2,6},{6,10},{... | collective-permute-start | bytes 1376264 | tf_op jit(solution)/shard_map/ppermute | solution.py:23
  111.3 7.3 %collective-permute-start.20 = (f32[128,256]{1,0:T(8,128)S(1)}, f32[128,256]{1,0:T(8,128)S(1)}, u32[]{:S(2)}, u32[]{:S(2)}) collective-permute-start(f32[128,256]{1,0:T(8,128)S(1)} %get-tuple-element.55), channel_id=1, source_target_pairs={{4,0},{8,4},{12,8},{5,1},{9,5},{13,9},{6,2},{10,6},{14,10},{7,3},{... | collective-permute-start | bytes 393224 | tf_op jit(solution)/shard_map/ppermute | solution.py:29
  112.6 13.2 %collective-permute-start.21 = (f32[128,256]{1,0:T(8,128)S(1)}, f32[128,256]{1,0:T(8,128)S(1)}, u32[]{:S(2)}, u32[]{:S(2)}) collective-permute-start(f32[128,256]{1,0:T(8,128)S(1)} %get-tuple-element.56), channel_id=1, source_target_pairs={{8,0},{12,4},{9,1},{13,5},{10,2},{14,6},{11,3},{15,7},{24,16},{28,... | collective-permute-start | bytes 393224 | tf_op jit(solution)/shard_map/ppermute | solution.py:29
  125.9 18.1 %collective-permute-start.23 = (bf16[256,896]{1,0:T(8,128)(2,1)S(1)}, bf16[256,896]{1,0:T(8,128)(2,1)S(1)}, u32[]{:S(2)}, u32[]{:S(2)}) collective-permute-start(bf16[256,896]{1,0:T(8,128)(2,1)S(1)} %get-tuple-element.63), channel_id=1, source_target_pairs={{0,12},{4,0},{8,4},{12,8},{1,13},{5,1},{9,5},{13,9},{2,14},{6,2},{... | collective-permute-start | bytes 1376264 | tf_op jit(solution)/shard_map/ppermute | solution.py:23
  128.8 9.8 %collective-permute-start.24 = (f32[248,128]{1,0:T(8,128)S(1)}, f32[248,128]{1,0:T(8,128)S(1)}, u32[]{:S(2)}, u32[]{:S(2)}) collective-permute-start(f32[248,128]{1,0:T(8,128)S(1)} %get-tuple-element.65), channel_id=1, source_target_pairs={{0,4},{4,8},{8,12},{12,0},{1,5},{5,9},{9,13},{13,1},{2,6},{6,10},{... | collective-permute-start | bytes 380936 | tf_op jit(solution)/shard_map/ppermute | solution.py:23
  130.8 13.2 %collective-permute-start.25 = (f32[248,128]{1,0:T(8,128)S(1)}, f32[248,128]{1,0:T(8,128)S(1)}, u32[]{:S(2)}, u32[]{:S(2)}) collective-permute-start(f32[248,128]{1,0:T(8,128)S(1)} %get-tuple-element.66), channel_id=1, source_target_pairs={{0,8},{4,12},{8,0},{12,4},{1,9},{5,13},{9,1},{13,5},{2,10},{6,14},... | collective-permute-start | bytes 380936 | tf_op jit(solution)/shard_map/ppermute | solution.py:23
  130.8 13.2 %collective-permute-start.26 = (f32[248,128]{1,0:T(8,128)S(1)}, f32[248,128]{1,0:T(8,128)S(1)}, u32[]{:S(2)}, u32[]{:S(2)}) collective-permute-start(f32[248,128]{1,0:T(8,128)S(1)} %get-tuple-element.67), channel_id=1, source_target_pairs={{0,12},{4,0},{8,4},{12,8},{1,13},{5,1},{9,5},{13,9},{2,14},{6,2},{... | collective-permute-start | bytes 380936 | tf_op jit(solution)/shard_map/ppermute | solution.py:23
  145.9 9.1 %collective-permute-start.27 = (f32[192,512]{1,0:T(8,128)S(1)}, f32[192,512]{1,0:T(8,128)S(1)}, u32[]{:S(2)}, u32[]{:S(2)}) collective-permute-start(f32[192,512]{1,0:T(8,128)S(1)} %get-tuple-element.70), channel_id=1, source_target_pairs={{0,2},{2,0},{1,3},{3,1},{4,6},{6,4},{5,7},{7,5},{8,10},{10,8},{9,1... | collective-permute-start | bytes 1179656 | tf_op jit(solution)/shard_map/ppermute | solution.py:23
  (22 other events, 190.5 us)

commit v14 on v13

--- a/solution.py
+++ b/solution.py
@@ -172,7 +172,7 @@
     return pl.pallas_call(
         pass_kernel,
         out_shape=jax.ShapeDtypeStruct(value.shape, value.dtype),
-        in_specs=[in_place()] * (1 + len(earlier)),
+        in_specs=[in_place()] + [in_vmem()] * len(earlier),
         out_specs=in_place(),
         input_output_aliases={0: 0},
         name="pass_after",
@@ -631,7 +631,7 @@
                 pltpu.VMEM((SEGS * joint_rank, down_width), bf16),
                 pltpu.VMEM((SEGS, low_width, 2 * held_up), bf16),
             ],
-            compiler_params=pltpu.CompilerParams(vmem_limit_bytes=8 * mebibyte),
+            compiler_params=pltpu.CompilerParams(vmem_limit_bytes=16 * mebibyte),
             cost_estimate=cost(0, 8 * frozen_rows * share),
             name="pack",
         )(own_down, far_down, own_up, far_up, before, after)
@@ -682,7 +682,7 @@
             out_shape=[jax.ShapeDtypeStruct((rows, down_width), bf16)] * seq_count,
             in_specs=[in_vmem()] + [in_place()] * len(early),
             out_specs=[by_block((rows, down_width))] * seq_count,
-            compiler_params=pltpu.CompilerParams(vmem_limit_bytes=8 * mebibyte),
+            compiler_params=pltpu.CompilerParams(vmem_limit_bytes=16 * mebibyte),
             cost_estimate=cost(0, 4 * rows * width),
             name="cut",
         )(local_tokens, *early)
@@ -751,7 +751,7 @@
             pltpu.VMEM((matrix_rows, width), bf16),
             pltpu.SemaphoreType.DMA((len(entries) + len(up_entries) + 1,)),
         ],
-        compiler_params=pltpu.CompilerParams(vmem_limit_bytes=12 * mebibyte),
+        compiler_params=pltpu.CompilerParams(vmem_limit_bytes=20 * mebibyte),
         cost_estimate=cost(2 * rows * width * matrix_rows, 2 * width * (matrix_rows + rows)),
         name="project",
     )(local_tokens, *arrays, *early)
@@ -936,7 +936,7 @@
             ),
         ),
         input_output_aliases={1 + term_count: 0, 2 + term_count: 1},
-        compiler_params=pltpu.CompilerParams(vmem_limit_bytes=8 * mebibyte),
+        compiler_params=pltpu.CompilerParams(vmem_limit_bytes=16 * mebibyte),
         name="bank_rows",
     )(
         bank_rows,

time: 160 us -> 160 us (level)
  no operation moved by 1% of the time
where the time goes in v14:
time: 160 us; the launch traced here: 159 us
  waiting for transfers between devices  60.3 us (38%)
  starting transfers between devices  45 us (28%)
  local copies, waits for them, and re-layouts  26 us (16%)
  Pallas kernels  22.9 us (14%)
  other arithmetic  2.42 us (2%)
  between operations  2.22 us (1%)
    ppermute x22, waiting for transfers between devices, shift(): lax.ppermute(value, axis, [(at, (at + steps) % count) for at in range(cou...  39.7 us
    ppermute x22, starting transfers between devices, shift(): lax.ppermute(value, axis, [(at, (at + steps) % count) for at in range(cou...  32.6 us
    ppermute x4, waiting for transfers between devices, push(): return lax.ppermute(value, axis, pairs)  14.3 us
    unnamed x37, local copies, waits for them, and re-layouts  12.4 us
    ppermute x4, starting transfers between devices, push(): return lax.ppermute(value, axis, pairs)  7.48 us
    ppermute x2, waiting for transfers between devices, over_plane(): lax.ppermute(value, ('groups', 'batch'), over_both)  6.33 us
    ppermute x2, starting transfers between devices, over_plane(): lax.ppermute(value, ('groups', 'batch'), over_both)  4.96 us
    pallas_call x1, Pallas kernels, shards(): pl.pallas_call(token_kernel, grid=(width // chunk,), out_shape=jax.ShapeD...  4.84 us
  transfers between devices with their start and end apart: 28, of which 17 were waited for; matrix products, arithmetic and copies ran while one was open for 10% of the time, Pallas kernels for 6%

profile of v14, /device:TPU:0, one launch (start us, length us, event | category | flops | bytes accessed | tf_op | source)
XLA Modules:
  0.0 158.9 jit_solution(2037376615759716322)
XLA Ops:
  1.7 5.1 %collective-permute-start.1 = (bf16[192,896]{1,0:T(8,128)(2,1)S(1)}, bf16[192,896]{1,0:T(8,128)(2,1)S(1)}, u32[]{:S(2)}, u32[]{:S(2)}) collective-permute-start(bf16[192,896]{1,0:T(8,128)(2,1)S(1)} %constant_dynamic-slice_fusion.1), channel_id=1, source_target_pairs={{0,12},{4,0},{8,4},{12,8},{1,13},{5,1},{9,5},{13,9},{2,14},{6,2},{... | collective-permute-start | bytes 1032200 | tf_op jit(solution)/shard_map/ppermute | solution.py:23
  8.7 2.7 %gather_fusion.1 = bf16[3,64,448]{2,1,0:T(8,128)(2,1)S(1)} fusion(bf16[64,64,448]{2,1,0:T(8,128)(2,1)} %bitcast.19, s32[1024]{0:T(1024)S(1)} %pad_clamp_fusion), kind=kCustom, calls=%fused_computation.1 | custom fusion | bytes 344076 | tf_op jit(solution)/shard_map/gather | solution.py:619
  14.7 2.7 %gather_fusion = bf16[3,64,448]{2,1,0:T(8,128)(2,1)S(1)} fusion(bf16[64,64,448]{2,1,0:T(8,128)(2,1)} %bitcast.20, s32[1024]{0:T(1024)S(1)} %pad_clamp_fusion.1), kind=kCustom, calls=%fused_computation | custom fusion | bytes 344076 | tf_op jit(solution)/shard_map/gather | solution.py:621
  18.4 4.0 %collective-permute-done.before.refs_1_ = bf16[192,896]{1,0:T(8,128)(2,1)S(1)} collective-permute-done((bf16[192,896]{1,0:T(8,128)(2,1)S(1)}, bf16[192,896]{1,0:T(8,128)(2,1)S(1)}, u32[]{:S(2)}, u32[]{:S(2)}) %collective-permute-start) | collective-permute-done | bytes 344096 | tf_op jit(solution)/shard_map/ppermute | solution.py:23
  32.9 9.2 %collective-permute-done.4.refs_0_.refs_3_ = bf16[336,896]{1,0:T(8,128)(2,1)S(1)} collective-permute-done((bf16[336,896]{1,0:T(8,128)(2,1)S(1)}, bf16[336,896]{1,0:T(8,128)(2,1)S(1)}, u32[]{:S(2)}, u32[]{:S(2)}) %collective-permute-start.4) | collective-permute-done | bytes 602144 | tf_op jit(solution)/shard_map/ppermute | solution.py:23
  42.9 4.5 %broadcast_in_dim.47.refs_1_.down_zeros = f32[64,64,1,448]{3,2,1,0:T(1,128)S(1)} broadcast(f32[]{:T(128)} %constant.11.clone.1), dimensions={} | broadcast | bytes 7340036 | tf_op jit(solution)/shard_map/broadcast_in_dim | solution.py:593
  47.6 3.2 %copy-done.1 = f32[64,64,1,448]{3,2,1,0:T(1,128)} copy-done((f32[64,64,1,448]{3,2,1,0:T(1,128)}, f32[64,64,1,448]{3,2,1,0:T(1,128)S(1)}, u32[]{:S(2)}) %copy-start.1) | copy-done | bytes 7340056
  51.6 10.2 %collective-permute-start.13 = (bf16[256,896]{1,0:T(8,128)(2,1)S(1)}, bf16[256,896]{1,0:T(8,128)(2,1)S(1)}, u32[]{:S(2)}, u32[]{:S(2)}) collective-permute-start(bf16[256,896]{1,0:T(8,128)(2,1)S(1)} %get-tuple-element.44), channel_id=1, source_target_pairs={{0,8},{4,12},{8,0},{12,4},{1,9},{5,13},{9,1},{13,5},{2,10},{6,14},... | collective-permute-start | bytes 1376264 | tf_op jit(solution)/shard_map/ppermute | solution.py:23
  61.9 2.5 %collective-permute-start.12 = (bf16[192,896]{1,0:T(8,128)(2,1)S(1)}, bf16[192,896]{1,0:T(8,128)(2,1)S(1)}, u32[]{:S(2)}, u32[]{:S(2)}) collective-permute-start(bf16[192,896]{1,0:T(8,128)(2,1)S(1)} %slice.32), channel_id=1, source_target_pairs={{0,18},{2,16},{16,2},{18,0},{1,19},{3,17},{17,3},{19,1},{4,22},{6,... | collective-permute-start | bytes 1032200 | tf_op jit(solution)/shard_map/ppermute | solution.py:644
  65.5 6.3 %collective-permute-done.12.refs_12_ = bf16[192,896]{1,0:T(8,128)(2,1)S(1)} collective-permute-done((bf16[192,896]{1,0:T(8,128)(2,1)S(1)}, bf16[192,896]{1,0:T(8,128)(2,1)S(1)}, u32[]{:S(2)}, u32[]{:S(2)}) %collective-permute-start.12) | collective-permute-done | bytes 344096 | tf_op jit(solution)/shard_map/ppermute | solution.py:644
  71.8 2.8 %collective-permute-done.11.refs_11_ = bf16[192,896]{1,0:T(8,128)(2,1)S(1)} collective-permute-done((bf16[192,896]{1,0:T(8,128)(2,1)S(1)}, bf16[192,896]{1,0:T(8,128)(2,1)S(1)}, u32[]{:S(2)}, u32[]{:S(2)}) %collective-permute-start.11) | collective-permute-done | bytes 344096 | tf_op jit(solution)/shard_map/ppermute | solution.py:23
  76.5 4.7 %project.1 = (f32[256,896]{1,0:T(8,128)S(1)}, bf16[896,3584]{1,0:T(8,128)(2,1)S(1)}, bf16[3,64,640]{2,1,0:T(8,128)(2,1)S(1)}) custom-call(bf16[256,3584]{1,0:T(8,128)(2,1)S(1)} %bitcast.16, bf16[192,3584]{1,0:T(8,128)(2,1)S(1)} %copy-done.6, bf16[192,896]{1,0:T(8,128)(2,1)S(1)} %collective-permute-done.before.refs_1_, ...), custom_call_target="tpu_custom_call" | custom-call | flops 1644167168 | bytes 8257536 | tf_op jit(solution)/shard_map/project/pallas_call | solution.py:738
  81.3 2.7 %copy-done.4 = bf16[896,3584]{1,0:T(8,128)(2,1)} copy-done((bf16[896,3584]{1,0:T(8,128)(2,1)}, bf16[896,3584]{1,0:T(8,128)(2,1)S(1)}, u32[]{:S(2)}) %copy-start.4) | copy-done | bytes 6422552
  84.0 2.5 %collective-permute-done.14.theirs = f32[256,896]{1,0:T(8,128)S(1)} collective-permute-done((f32[256,896]{1,0:T(8,128)S(1)}, f32[256,896]{1,0:T(8,128)S(1)}, u32[]{:S(2)}, u32[]{:S(2)}) %collective-permute-start.14) | collective-permute-done | bytes 917536 | tf_op jit(solution)/shard_map/ppermute | solution.py:23
  89.0 3.5 %collective-permute-start.15 = (bf16[256,256]{1,0:T(8,128)(2,1)S(1)}, bf16[256,256]{1,0:T(8,128)(2,1)S(1)}, u32[]{:S(2)}, u32[]{:S(2)}) collective-permute-start(bf16[256,256]{1,0:T(8,128)(2,1)S(1)} %get-tuple-element.48.refs_0_), channel_id=1, source_target_pairs={{0,4},{4,8},{8,12},{1,5},{5,9},{9,13},{2,6},{6,10},{10,14},{3,7},{... | collective-permute-start | bytes 393224 | tf_op jit(solution)/shard_map/ppermute | solution.py:29
  96.9 4.0 %collective-permute-start.19 = (bf16[256,896]{1,0:T(8,128)(2,1)}, bf16[256,896]{1,0:T(8,128)(2,1)S(1)}, u32[]{:S(2)}, u32[]{:S(2)}) collective-permute-start(bf16[256,896]{1,0:T(8,128)(2,1)} %pass_after.1), channel_id=1, source_target_pairs={{0,4},{4,8},{8,12},{12,0},{1,5},{5,9},{9,13},{13,1},{2,6},{6,10},{... | collective-permute-start | bytes 1376264 | tf_op jit(solution)/shard_map/ppermute | solution.py:23
  104.5 3.4 %attention.1 = (bf16[128,512]{1,0:T(8,128)(2,1)}, bf16[128,512]{1,0:T(8,128)(2,1)S(1)}, f32[3,128,256]{2,1,0:T(8,128)S(1)}, f32[3,128,256]{2,1,0:T(8,128)S(1)}) custom-call(s32[2,3]{1,0:T(2,128)S(1)} %copy-done.14, bf16[512,128]{1,0:T(8,128)(2,1)S(1)} %get-tuple-element.47.queries, bf16[128,512]{1,0:T(8,128)(2,1)S(1)} %bitcast.17, ...), custom_call_target="tpu_custom_call" | custom-call | flops 503316480 | bytes 786432 | tf_op jit(solution)/shard_map/attention/pallas_call | solution.py:781
  114.4 4.3 %collective-permute-done.20.refs_1_ = f32[128,256]{1,0:T(8,128)S(1)} collective-permute-done((f32[128,256]{1,0:T(8,128)S(1)}, f32[128,256]{1,0:T(8,128)S(1)}, u32[]{:S(2)}, u32[]{:S(2)}) %collective-permute-start.20) | collective-permute-done | bytes 131104 | tf_op jit(solution)/shard_map/ppermute | solution.py:29
  118.7 8.0 %collective-permute-done.21.refs_2_ = f32[128,256]{1,0:T(8,128)S(1)} collective-permute-done((f32[128,256]{1,0:T(8,128)S(1)}, f32[128,256]{1,0:T(8,128)S(1)}, u32[]{:S(2)}, u32[]{:S(2)}) %collective-permute-start.21) | collective-permute-done | bytes 131104 | tf_op jit(solution)/shard_map/ppermute | solution.py:29
  134.1 3.7 %collective-permute-done.24.refs_5_ = f32[248,128]{1,0:T(8,128)S(1)} collective-permute-done((f32[248,128]{1,0:T(8,128)S(1)}, f32[248,128]{1,0:T(8,128)S(1)}, u32[]{:S(2)}, u32[]{:S(2)}) %collective-permute-start.24) | collective-permute-done | bytes 127008 | tf_op jit(solution)/shard_map/ppermute | solution.py:23
  137.8 6.8 %collective-permute-done.25.refs_6_ = f32[248,128]{1,0:T(8,128)S(1)} collective-permute-done((f32[248,128]{1,0:T(8,128)S(1)}, f32[248,128]{1,0:T(8,128)S(1)}, u32[]{:S(2)}, u32[]{:S(2)}) %collective-permute-start.25) | collective-permute-done | bytes 127008 | tf_op jit(solution)/shard_map/ppermute | solution.py:23
  148.1 4.8 %token_gradient.1 = bf16[256,3584]{1,0:T(8,128)(2,1)} custom-call(bf16[256,896]{1,0:T(8,128)(2,1)S(1)} %get-tuple-element.60.gradients, bf16[896,3584]{1,0:T(8,128)(2,1)S(1)} %copy-done.5), custom_call_target="tpu_custom_call" | custom-call | flops 1644167168 | bytes 8257536 | tf_op jit(solution)/shard_map/token_gradient/pallas_call | solution.py:865
  153.0 2.9 %collective-permute-done.27.far = f32[192,512]{1,0:T(8,128)S(1)} collective-permute-done((f32[192,512]{1,0:T(8,128)S(1)}, f32[192,512]{1,0:T(8,128)S(1)}, u32[]{:S(2)}, u32[]{:S(2)}) %collective-permute-start.27) | collective-permute-done | bytes 393248 | tf_op jit(solution)/shard_map/ppermute | solution.py:23
  155.8 3.0 %bank_rows.1 = (f32[64,64,1,448]{3,2,1,0:T(1,128)}, f32[64,32,80]{2,1,0:T(8,128)}) custom-call(s32[6]{0:T(128)S(1)} %pad_add_fusion.refs_5_.bank_rows, f32[192,448]{1,0:T(8,128)S(1)} %get-tuple-element.69.own_down, f32[192,512]{1,0:T(8,128)S(1)} %collective-permute-done.27.far, ...), custom_call_target="tpu_custom_call", output_to_operand_aliasing={{0}: (4, {}), {1}: (5, {})} | custom-call | tf_op jit(solution)/shard_map/bank_rows/pallas_call | solution.py:917
  (101 shorter events, 48.8 us)
Async XLA Ops:
  1.7 16.7 %collective-permute-start.1 = (bf16[192,896]{1,0:T(8,128)(2,1)S(1)}, bf16[192,896]{1,0:T(8,128)(2,1)S(1)}, u32[]{:S(2)}, u32[]{:S(2)}) collective-permute-start(bf16[192,896]{1,0:T(8,128)(2,1)S(1)} %constant_dynamic-slice_fusion.1), channel_id=1, source_target_pairs={{0,12},{4,0},{8,4},{12,8},{1,13},{5,1},{9,5},{13,9},{2,14},{6,2},{... | collective-permute-start | bytes 1032200 | tf_op jit(solution)/shard_map/ppermute | solution.py:23
  6.8 15.6 %collective-permute-start = (bf16[192,896]{1,0:T(8,128)(2,1)S(1)}, bf16[192,896]{1,0:T(8,128)(2,1)S(1)}, u32[]{:S(2)}, u32[]{:S(2)}) collective-permute-start(bf16[192,896]{1,0:T(8,128)(2,1)S(1)} %constant_dynamic-slice_fusion.1), channel_id=1, source_target_pairs={{0,4},{4,8},{8,12},{12,0},{1,5},{5,9},{9,13},{13,1},{2,6},{6,10},{... | collective-permute-start | bytes 1032200 | tf_op jit(solution)/shard_map/ppermute | solution.py:23
  11.4 7.0 %collective-permute-start.2 = (bf16[3,64,448]{2,1,0:T(8,128)(2,1)S(1)}, bf16[3,64,448]{2,1,0:T(8,128)(2,1)S(1)}, u32[]{:S(2)}, u32[]{:S(2)}) collective-permute-start(bf16[3,64,448]{2,1,0:T(8,128)(2,1)S(1)} %gather_fusion.1), channel_id=1, source_target_pairs={{0,2},{2,0},{1,3},{3,1},{4,6},{6,4},{5,7},{7,5},{8,10},{10,8},{9,1... | collective-permute-start | bytes 516104 | tf_op jit(solution)/shard_map/ppermute | solution.py:23
  13.5 4.8 %collective-permute-start.3 = (bf16[3,32,80]{2,1,0:T(8,128)(2,1)S(1)}, bf16[3,32,80]{2,1,0:T(8,128)(2,1)S(1)}, u32[]{:S(2)}, u32[]{:S(2)}) collective-permute-start(bf16[3,32,80]{2,1,0:T(8,128)(2,1)S(1)} %gather_fusion.3), channel_id=1, source_target_pairs={{0,2},{2,0},{1,3},{3,1},{4,6},{6,4},{5,7},{7,5},{8,10},{10,8},{9,1... | collective-permute-start | bytes 46088 | tf_op jit(solution)/shard_map/ppermute | solution.py:23
  23.7 18.4 %collective-permute-start.4 = (bf16[336,896]{1,0:T(8,128)(2,1)S(1)}, bf16[336,896]{1,0:T(8,128)(2,1)S(1)}, u32[]{:S(2)}, u32[]{:S(2)}) collective-permute-start(bf16[336,896]{1,0:T(8,128)(2,1)S(1)} %get-tuple-element.39), channel_id=1, source_target_pairs={{0,4},{4,8},{8,12},{12,0},{1,5},{5,9},{9,13},{13,1},{2,6},{6,10},{... | collective-permute-start | bytes 1806344 | tf_op jit(solution)/shard_map/ppermute | solution.py:23
  26.6 37.8 %collective-permute-start.9 = (bf16[384,896]{1,0:T(8,128)(2,1)}, bf16[384,896]{1,0:T(8,128)(2,1)}, u32[]{:S(2)}, u32[]{:S(2)}) collective-permute-start(bf16[384,896]{1,0:T(8,128)(2,1)} %get-tuple-element.43), channel_id=1, source_target_pairs={{0,18},{2,16},{16,2},{18,0},{1,19},{3,17},{17,3},{19,1},{4,22},{6,... | collective-permute-start | bytes 2064392 | tf_op jit(solution)/shard_map/ppermute | solution.py:644
  29.1 35.9 %collective-permute-start.8 = (bf16[384,896]{1,0:T(8,128)(2,1)}, bf16[384,896]{1,0:T(8,128)(2,1)}, u32[]{:S(2)}, u32[]{:S(2)}) collective-permute-start(bf16[384,896]{1,0:T(8,128)(2,1)} %get-tuple-element.43), channel_id=1, source_target_pairs={{0,16},{16,0},{1,17},{17,1},{2,18},{18,2},{3,19},{19,3},{4,20},{20... | collective-permute-start | bytes 2064392 | tf_op jit(solution)/shard_map/ppermute | solution.py:23
  31.6 33.9 %collective-permute-start.7 = (bf16[384,896]{1,0:T(8,128)(2,1)}, bf16[384,896]{1,0:T(8,128)(2,1)S(1)}, u32[]{:S(2)}, u32[]{:S(2)}) collective-permute-start(bf16[384,896]{1,0:T(8,128)(2,1)} %get-tuple-element.43), channel_id=1, source_target_pairs={{0,2},{2,0},{1,3},{3,1},{4,6},{6,4},{5,7},{7,5},{8,10},{10,8},{9,1... | collective-permute-start | bytes 2064392 | tf_op jit(solution)/shard_map/ppermute | solution.py:23
  32.2 19.4 %collective-permute-start.5 = (bf16[144,896]{1,0:T(8,128)(2,1)}, bf16[144,896]{1,0:T(8,128)(2,1)S(1)}, u32[]{:S(2)}, u32[]{:S(2)}) collective-permute-start(bf16[144,896]{1,0:T(8,128)(2,1)} %get-tuple-element.41), channel_id=1, source_target_pairs={{0,8},{4,12},{8,0},{12,4},{1,9},{5,13},{9,1},{13,5},{2,10},{6,14},... | collective-permute-start | bytes 774152 | tf_op jit(solution)/shard_map/ppermute | solution.py:23
  42.1 19.8 %collective-permute-start.6 = (bf16[144,896]{1,0:T(8,128)(2,1)}, bf16[144,896]{1,0:T(8,128)(2,1)S(1)}, u32[]{:S(2)}, u32[]{:S(2)}) collective-permute-start(bf16[144,896]{1,0:T(8,128)(2,1)} %get-tuple-element.42), channel_id=1, source_target_pairs={{0,12},{4,0},{8,4},{12,8},{1,13},{5,1},{9,5},{13,9},{2,14},{6,2},{... | collective-permute-start | bytes 774152 | tf_op jit(solution)/shard_map/ppermute | solution.py:23
  51.6 24.9 %collective-permute-start.13 = (bf16[256,896]{1,0:T(8,128)(2,1)S(1)}, bf16[256,896]{1,0:T(8,128)(2,1)S(1)}, u32[]{:S(2)}, u32[]{:S(2)}) collective-permute-start(bf16[256,896]{1,0:T(8,128)(2,1)S(1)} %get-tuple-element.44), channel_id=1, source_target_pairs={{0,8},{4,12},{8,0},{12,4},{1,9},{5,13},{9,1},{13,5},{2,10},{6,14},... | collective-permute-start | bytes 1376264 | tf_op jit(solution)/shard_map/ppermute | solution.py:23
  61.9 9.9 %collective-permute-start.12 = (bf16[192,896]{1,0:T(8,128)(2,1)S(1)}, bf16[192,896]{1,0:T(8,128)(2,1)S(1)}, u32[]{:S(2)}, u32[]{:S(2)}) collective-permute-start(bf16[192,896]{1,0:T(8,128)(2,1)S(1)} %slice.32), channel_id=1, source_target_pairs={{0,18},{2,16},{16,2},{18,0},{1,19},{3,17},{17,3},{19,1},{4,22},{6,... | collective-permute-start | bytes 1032200 | tf_op jit(solution)/shard_map/ppermute | solution.py:644
  64.4 10.2 %collective-permute-start.11 = (bf16[192,896]{1,0:T(8,128)(2,1)S(1)}, bf16[192,896]{1,0:T(8,128)(2,1)S(1)}, u32[]{:S(2)}, u32[]{:S(2)}) collective-permute-start(bf16[192,896]{1,0:T(8,128)(2,1)S(1)} %slice.32), channel_id=1, source_target_pairs={{0,16},{16,0},{1,17},{17,1},{2,18},{18,2},{3,19},{19,3},{4,20},{20... | collective-permute-start | bytes 1032200 | tf_op jit(solution)/shard_map/ppermute | solution.py:23
  64.9 9.7 %collective-permute-start.10 = (bf16[192,896]{1,0:T(8,128)(2,1)S(1)}, bf16[192,896]{1,0:T(8,128)(2,1)S(1)}, u32[]{:S(2)}, u32[]{:S(2)}) collective-permute-start(bf16[192,896]{1,0:T(8,128)(2,1)S(1)} %slice.32), channel_id=1, source_target_pairs={{0,2},{2,0},{1,3},{3,1},{4,6},{6,4},{5,7},{7,5},{8,10},{10,8},{9,1... | collective-permute-start | bytes 1032200 | tf_op jit(solution)/shard_map/ppermute | solution.py:23
  87.6 5.6 %collective-permute-start.16 = (bf16[256,256]{1,0:T(8,128)(2,1)S(1)}, bf16[256,256]{1,0:T(8,128)(2,1)S(1)}, u32[]{:S(2)}, u32[]{:S(2)}) collective-permute-start(bf16[256,256]{1,0:T(8,128)(2,1)S(1)} %get-tuple-element.48.refs_0_), channel_id=1, source_target_pairs={{0,8},{4,12},{1,9},{5,13},{2,10},{6,14},{3,11},{7,15},{16,24},{20,... | collective-permute-start | bytes 393224 | tf_op jit(solution)/shard_map/ppermute | solution.py:29
  89.0 6.2 %collective-permute-start.15 = (bf16[256,256]{1,0:T(8,128)(2,1)S(1)}, bf16[256,256]{1,0:T(8,128)(2,1)S(1)}, u32[]{:S(2)}, u32[]{:S(2)}) collective-permute-start(bf16[256,256]{1,0:T(8,128)(2,1)S(1)} %get-tuple-element.48.refs_0_), channel_id=1, source_target_pairs={{0,4},{4,8},{8,12},{1,5},{5,9},{9,13},{2,6},{6,10},{10,14},{3,7},{... | collective-permute-start | bytes 393224 | tf_op jit(solution)/shard_map/ppermute | solution.py:29
  96.9 14.9 %collective-permute-start.19 = (bf16[256,896]{1,0:T(8,128)(2,1)}, bf16[256,896]{1,0:T(8,128)(2,1)S(1)}, u32[]{:S(2)}, u32[]{:S(2)}) collective-permute-start(bf16[256,896]{1,0:T(8,128)(2,1)} %pass_after.1), channel_id=1, source_target_pairs={{0,4},{4,8},{8,12},{12,0},{1,5},{5,9},{9,13},{13,1},{2,6},{6,10},{... | collective-permute-start | bytes 1376264 | tf_op jit(solution)/shard_map/ppermute | solution.py:23
  111.8 6.9 %collective-permute-start.20 = (f32[128,256]{1,0:T(8,128)S(1)}, f32[128,256]{1,0:T(8,128)S(1)}, u32[]{:S(2)}, u32[]{:S(2)}) collective-permute-start(f32[128,256]{1,0:T(8,128)S(1)} %get-tuple-element.55), channel_id=1, source_target_pairs={{4,0},{8,4},{12,8},{5,1},{9,5},{13,9},{6,2},{10,6},{14,10},{7,3},{... | collective-permute-start | bytes 393224 | tf_op jit(solution)/shard_map/ppermute | solution.py:29
  113.1 13.5 %collective-permute-start.21 = (f32[128,256]{1,0:T(8,128)S(1)}, f32[128,256]{1,0:T(8,128)S(1)}, u32[]{:S(2)}, u32[]{:S(2)}) collective-permute-start(f32[128,256]{1,0:T(8,128)S(1)} %get-tuple-element.56), channel_id=1, source_target_pairs={{8,0},{12,4},{9,1},{13,5},{10,2},{14,6},{11,3},{15,7},{24,16},{28,... | collective-permute-start | bytes 393224 | tf_op jit(solution)/shard_map/ppermute | solution.py:29
  126.8 17.9 %collective-permute-start.23 = (bf16[256,896]{1,0:T(8,128)(2,1)S(1)}, bf16[256,896]{1,0:T(8,128)(2,1)S(1)}, u32[]{:S(2)}, u32[]{:S(2)}) collective-permute-start(bf16[256,896]{1,0:T(8,128)(2,1)S(1)} %get-tuple-element.63), channel_id=1, source_target_pairs={{0,12},{4,0},{8,4},{12,8},{1,13},{5,1},{9,5},{13,9},{2,14},{6,2},{... | collective-permute-start | bytes 1376264 | tf_op jit(solution)/shard_map/ppermute | solution.py:23
  129.7 8.2 %collective-permute-start.24 = (f32[248,128]{1,0:T(8,128)S(1)}, f32[248,128]{1,0:T(8,128)S(1)}, u32[]{:S(2)}, u32[]{:S(2)}) collective-permute-start(f32[248,128]{1,0:T(8,128)S(1)} %get-tuple-element.65), channel_id=1, source_target_pairs={{0,4},{4,8},{8,12},{12,0},{1,5},{5,9},{9,13},{13,1},{2,6},{6,10},{... | collective-permute-start | bytes 380936 | tf_op jit(solution)/shard_map/ppermute | solution.py:23
  131.7 13.0 %collective-permute-start.25 = (f32[248,128]{1,0:T(8,128)S(1)}, f32[248,128]{1,0:T(8,128)S(1)}, u32[]{:S(2)}, u32[]{:S(2)}) collective-permute-start(f32[248,128]{1,0:T(8,128)S(1)} %get-tuple-element.66), channel_id=1, source_target_pairs={{0,8},{4,12},{8,0},{12,4},{1,9},{5,13},{9,1},{13,5},{2,10},{6,14},... | collective-permute-start | bytes 380936 | tf_op jit(solution)/shard_map/ppermute | solution.py:23
  131.7 13.0 %collective-permute-start.26 = (f32[248,128]{1,0:T(8,128)S(1)}, f32[248,128]{1,0:T(8,128)S(1)}, u32[]{:S(2)}, u32[]{:S(2)}) collective-permute-start(f32[248,128]{1,0:T(8,128)S(1)} %get-tuple-element.67), channel_id=1, source_target_pairs={{0,12},{4,0},{8,4},{12,8},{1,13},{5,1},{9,5},{13,9},{2,14},{6,2},{... | collective-permute-start | bytes 380936 | tf_op jit(solution)/shard_map/ppermute | solution.py:23
  146.6 9.3 %collective-permute-start.27 = (f32[192,512]{1,0:T(8,128)S(1)}, f32[192,512]{1,0:T(8,128)S(1)}, u32[]{:S(2)}, u32[]{:S(2)}) collective-permute-start(f32[192,512]{1,0:T(8,128)S(1)} %get-tuple-element.70), channel_id=1, source_target_pairs={{0,2},{2,0},{1,3},{3,1},{4,6},{6,4},{5,7},{7,5},{8,10},{10,8},{9,1... | collective-permute-start | bytes 1179656 | tf_op jit(solution)/shard_map/ppermute | solution.py:23
  (22 other events, 215.8 us)

commit v15 on v14

--- a/solution.py
+++ b/solution.py
@@ -175,6 +175,7 @@
         in_specs=[in_place()] + [in_vmem()] * len(earlier),
         out_specs=in_place(),
         input_output_aliases={0: 0},
+        compiler_params=pltpu.CompilerParams(vmem_limit_bytes=2 * mebibyte),
         name="pass_after",
     )(value, *earlier)
 

time: 160 us -> 155 us (0.969)
  local copies, waits for them, and re-layouts: 26 us -> 19 us
  waiting for transfers between devices: 60.3 us -> 65.5 us
  Pallas kernels: 22.9 us -> 21 us
    unnamed x37 -> x19, local copies, waits for them, and re-layouts: 12.4 us -> 5.42 us
    ppermute x22, waiting for transfers between devices: 39.7 us -> 43.6 us  [shift(): lax.ppermute(value, axis, [(at, (at + steps) % count) for at in range(cou...]
  transfers between devices with their start and end apart: 28 -> 28, of which waited for: 17 -> 20; matrix products, arithmetic and copies ran while one was open for 10% -> 10% of each run, Pallas kernels for 6% -> 6%
where the time goes in v15:
time: 155 us; the launch traced here: 154 us
  waiting for transfers between devices  65.5 us (42%)
  starting transfers between devices  44.3 us (29%)
  Pallas kernels  21 us (14%)
  local copies, waits for them, and re-layouts  19 us (12%)
  other arithmetic  2.42 us (2%)
  between operations  2.2 us (1%)
    ppermute x22, waiting for transfers between devices, shift(): lax.ppermute(value, axis, [(at, (at + steps) % count) for at in range(cou...  43.6 us
    ppermute x22, starting transfers between devices, shift(): lax.ppermute(value, axis, [(at, (at + steps) % count) for at in range(cou...  32.2 us
    ppermute x4, waiting for transfers between devices, push(): return lax.ppermute(value, axis, pairs)  15.2 us
    ppermute x4, starting transfers between devices, push(): return lax.ppermute(value, axis, pairs)  7.14 us
    ppermute x2, waiting for transfers between devices, over_plane(): lax.ppermute(value, ('groups', 'batch'), over_both)  6.78 us
    unnamed x19, local copies, waits for them, and re-layouts  5.42 us
    ppermute x2, starting transfers between devices, over_plane(): lax.ppermute(value, ('groups', 'batch'), over_both)  4.96 us
    pallas_call x1, Pallas kernels, shards(): pl.pallas_call(token_kernel, grid=(width // chunk,), out_shape=jax.ShapeD...  4.84 us
  transfers between devices with their start and end apart: 28, of which 20 were waited for; matrix products, arithmetic and copies ran while one was open for 10% of the time, Pallas kernels for 6%

profile of v15, /device:TPU:0, one launch (start us, length us, event | category | flops | bytes accessed | tf_op | source)
XLA Modules:
  0.0 154.4 jit_solution(87561573628027328)
XLA Ops:
  1.7 5.1 %collective-permute-start.1 = (bf16[192,896]{1,0:T(8,128)(2,1)S(1)}, bf16[192,896]{1,0:T(8,128)(2,1)S(1)}, u32[]{:S(2)}, u32[]{:S(2)}) collective-permute-start(bf16[192,896]{1,0:T(8,128)(2,1)S(1)} %constant_dynamic-slice_fusion.1), channel_id=1, source_target_pairs={{0,12},{4,0},{8,4},{12,8},{1,13},{5,1},{9,5},{13,9},{2,14},{6,2},{... | collective-permute-start | bytes 1032200 | tf_op jit(solution)/shard_map/ppermute | solution.py:23
  8.7 2.7 %gather_fusion.1 = bf16[3,64,448]{2,1,0:T(8,128)(2,1)S(1)} fusion(bf16[64,64,448]{2,1,0:T(8,128)(2,1)} %bitcast.19, s32[1024]{0:T(1024)S(1)} %pad_clamp_fusion), kind=kCustom, calls=%fused_computation.1 | custom fusion | bytes 344076 | tf_op jit(solution)/shard_map/gather | solution.py:620
  14.7 2.7 %gather_fusion = bf16[3,64,448]{2,1,0:T(8,128)(2,1)S(1)} fusion(bf16[64,64,448]{2,1,0:T(8,128)(2,1)} %bitcast.20, s32[1024]{0:T(1024)S(1)} %pad_clamp_fusion.1), kind=kCustom, calls=%fused_computation | custom fusion | bytes 344076 | tf_op jit(solution)/shard_map/gather | solution.py:622
  18.4 4.0 %collective-permute-done.before.refs_1_ = bf16[192,896]{1,0:T(8,128)(2,1)S(1)} collective-permute-done((bf16[192,896]{1,0:T(8,128)(2,1)S(1)}, bf16[192,896]{1,0:T(8,128)(2,1)S(1)}, u32[]{:S(2)}, u32[]{:S(2)}) %collective-permute-start) | collective-permute-done | bytes 344096 | tf_op jit(solution)/shard_map/ppermute | solution.py:23
  34.3 9.5 %collective-permute-done.4.refs_0_.refs_3_ = bf16[336,896]{1,0:T(8,128)(2,1)S(1)} collective-permute-done((bf16[336,896]{1,0:T(8,128)(2,1)}, bf16[336,896]{1,0:T(8,128)(2,1)S(1)}, u32[]{:S(2)}, u32[]{:S(2)}) %collective-permute-start.4) | collective-permute-done | bytes 602144 | tf_op jit(solution)/shard_map/ppermute | solution.py:23
  44.6 4.5 %broadcast_in_dim.47.refs_1_.down_zeros = f32[64,64,1,448]{3,2,1,0:T(1,128)S(1)} broadcast(f32[]{:T(128)} %constant.11.clone.1), dimensions={} | broadcast | bytes 7340036 | tf_op jit(solution)/shard_map/broadcast_in_dim | solution.py:594
  49.3 3.2 %copy-done.1 = f32[64,64,1,448]{3,2,1,0:T(1,128)} copy-done((f32[64,64,1,448]{3,2,1,0:T(1,128)}, f32[64,64,1,448]{3,2,1,0:T(1,128)S(1)}, u32[]{:S(2)}) %copy-start.1) | copy-done | bytes 7340056
  52.8 10.0 %collective-permute-start.13 = (bf16[256,896]{1,0:T(8,128)(2,1)S(1)}, bf16[256,896]{1,0:T(8,128)(2,1)S(1)}, u32[]{:S(2)}, u32[]{:S(2)}) collective-permute-start(bf16[256,896]{1,0:T(8,128)(2,1)S(1)} %get-tuple-element.44), channel_id=1, source_target_pairs={{0,8},{4,12},{8,0},{12,4},{1,9},{5,13},{9,1},{13,5},{2,10},{6,14},... | collective-permute-start | bytes 1376264 | tf_op jit(solution)/shard_map/ppermute | solution.py:23
  62.8 2.5 %collective-permute-start.12 = (bf16[192,896]{1,0:T(8,128)(2,1)S(1)}, bf16[192,896]{1,0:T(8,128)(2,1)S(1)}, u32[]{:S(2)}, u32[]{:S(2)}) collective-permute-start(bf16[192,896]{1,0:T(8,128)(2,1)S(1)} %slice.32), channel_id=1, source_target_pairs={{0,18},{2,16},{16,2},{18,0},{1,19},{3,17},{17,3},{19,1},{4,22},{6,... | collective-permute-start | bytes 1032200 | tf_op jit(solution)/shard_map/ppermute | solution.py:645
  66.3 6.8 %collective-permute-done.12.refs_12_ = bf16[192,896]{1,0:T(8,128)(2,1)S(1)} collective-permute-done((bf16[192,896]{1,0:T(8,128)(2,1)S(1)}, bf16[192,896]{1,0:T(8,128)(2,1)S(1)}, u32[]{:S(2)}, u32[]{:S(2)}) %collective-permute-start.12) | collective-permute-done | bytes 344096 | tf_op jit(solution)/shard_map/ppermute | solution.py:645
  78.2 3.8 %project.1 = (f32[256,896]{1,0:T(8,128)S(1)}, bf16[896,3584]{1,0:T(8,128)(2,1)S(1)}, bf16[3,64,640]{2,1,0:T(8,128)(2,1)S(1)}) custom-call(bf16[256,3584]{1,0:T(8,128)(2,1)S(1)} %bitcast.16, bf16[192,3584]{1,0:T(8,128)(2,1)S(1)} %copy-done.4, bf16[192,896]{1,0:T(8,128)(2,1)S(1)} %collective-permute-done.before.refs_1_, ...), custom_call_target="tpu_custom_call" | custom-call | flops 1644167168 | bytes 8257536 | tf_op jit(solution)/shard_map/project/pallas_call | solution.py:739
  82.1 2.5 %collective-permute-done.14.theirs = f32[256,896]{1,0:T(8,128)S(1)} collective-permute-done((f32[256,896]{1,0:T(8,128)S(1)}, f32[256,896]{1,0:T(8,128)S(1)}, u32[]{:S(2)}, u32[]{:S(2)}) %collective-permute-start.14) | collective-permute-done | bytes 917536 | tf_op jit(solution)/shard_map/ppermute | solution.py:23
  87.1 3.1 %collective-permute-start.15 = (bf16[256,256]{1,0:T(8,128)(2,1)S(1)}, bf16[256,256]{1,0:T(8,128)(2,1)S(1)}, u32[]{:S(2)}, u32[]{:S(2)}) collective-permute-start(bf16[256,256]{1,0:T(8,128)(2,1)S(1)} %get-tuple-element.48.refs_0_), channel_id=1, source_target_pairs={{0,4},{4,8},{8,12},{1,5},{5,9},{9,13},{2,6},{6,10},{10,14},{3,7},{... | collective-permute-start | bytes 393224 | tf_op jit(solution)/shard_map/ppermute | solution.py:29
  90.4 2.7 %collective-permute-done.15.refs_1_ = bf16[256,256]{1,0:T(8,128)(2,1)S(1)} collective-permute-done((bf16[256,256]{1,0:T(8,128)(2,1)S(1)}, bf16[256,256]{1,0:T(8,128)(2,1)S(1)}, u32[]{:S(2)}, u32[]{:S(2)}) %collective-permute-start.15) | collective-permute-done | bytes 131104 | tf_op jit(solution)/shard_map/ppermute | solution.py:29
  93.1 3.8 %collective-permute-start.19 = (bf16[256,896]{1,0:T(8,128)(2,1)S(1)}, bf16[256,896]{1,0:T(8,128)(2,1)S(1)}, u32[]{:S(2)}, u32[]{:S(2)}) collective-permute-start(bf16[256,896]{1,0:T(8,128)(2,1)S(1)} %pass_after.1), channel_id=1, source_target_pairs={{0,4},{4,8},{8,12},{12,0},{1,5},{5,9},{9,13},{13,1},{2,6},{6,10},{... | collective-permute-start | bytes 1376264 | tf_op jit(solution)/shard_map/ppermute | solution.py:23
  96.9 3.4 %attention.1 = (bf16[128,512]{1,0:T(8,128)(2,1)}, bf16[128,512]{1,0:T(8,128)(2,1)S(1)}, f32[3,128,256]{2,1,0:T(8,128)S(1)}, f32[3,128,256]{2,1,0:T(8,128)S(1)}) custom-call(s32[2,3]{1,0:T(2,128)S(1)} %copy-done.5, bf16[512,128]{1,0:T(8,128)(2,1)S(1)} %get-tuple-element.47.queries, bf16[128,512]{1,0:T(8,128)(2,1)S(1)} %bitcast.17, ...), custom_call_target="tpu_custom_call" | custom-call | flops 503316480 | bytes 786432 | tf_op jit(solution)/shard_map/attention/pallas_call | solution.py:782
  102.1 5.2 %collective-permute-done.19.refs_0_.refs_1_ = bf16[256,896]{1,0:T(8,128)(2,1)S(1)} collective-permute-done((bf16[256,896]{1,0:T(8,128)(2,1)S(1)}, bf16[256,896]{1,0:T(8,128)(2,1)S(1)}, u32[]{:S(2)}, u32[]{:S(2)}) %collective-permute-start.19) | collective-permute-done | bytes 458784 | tf_op jit(solution)/shard_map/ppermute | solution.py:23
  109.9 5.2 %collective-permute-done.20.refs_1_ = f32[128,256]{1,0:T(8,128)S(1)} collective-permute-done((f32[128,256]{1,0:T(8,128)S(1)}, f32[128,256]{1,0:T(8,128)S(1)}, u32[]{:S(2)}, u32[]{:S(2)}) %collective-permute-start.20) | collective-permute-done | bytes 131104 | tf_op jit(solution)/shard_map/ppermute | solution.py:29
  115.1 7.1 %collective-permute-done.21.refs_2_ = f32[128,256]{1,0:T(8,128)S(1)} collective-permute-done((f32[128,256]{1,0:T(8,128)S(1)}, f32[128,256]{1,0:T(8,128)S(1)}, u32[]{:S(2)}, u32[]{:S(2)}) %collective-permute-start.21) | collective-permute-done | bytes 131104 | tf_op jit(solution)/shard_map/ppermute | solution.py:29
  129.6 3.7 %collective-permute-done.24.refs_5_ = f32[248,128]{1,0:T(8,128)S(1)} collective-permute-done((f32[248,128]{1,0:T(8,128)S(1)}, f32[248,128]{1,0:T(8,128)S(1)}, u32[]{:S(2)}, u32[]{:S(2)}) %collective-permute-start.24) | collective-permute-done | bytes 127008 | tf_op jit(solution)/shard_map/ppermute | solution.py:23
  133.3 6.2 %collective-permute-done.25.refs_6_ = f32[248,128]{1,0:T(8,128)S(1)} collective-permute-done((f32[248,128]{1,0:T(8,128)S(1)}, f32[248,128]{1,0:T(8,128)S(1)}, u32[]{:S(2)}, u32[]{:S(2)}) %collective-permute-start.25) | collective-permute-done | bytes 127008 | tf_op jit(solution)/shard_map/ppermute | solution.py:23
  142.9 4.8 %token_gradient.1 = bf16[256,3584]{1,0:T(8,128)(2,1)} custom-call(bf16[256,896]{1,0:T(8,128)(2,1)S(1)} %get-tuple-element.60.gradients, bf16[896,3584]{1,0:T(8,128)(2,1)S(1)} %get-tuple-element.61.matrix), custom_call_target="tpu_custom_call" | custom-call | flops 1644167168 | bytes 8257536 | tf_op jit(solution)/shard_map/token_gradient/pallas_call | solution.py:866
  147.8 3.6 %collective-permute-done.27.far = f32[192,512]{1,0:T(8,128)S(1)} collective-permute-done((f32[192,512]{1,0:T(8,128)S(1)}, f32[192,512]{1,0:T(8,128)S(1)}, u32[]{:S(2)}, u32[]{:S(2)}) %collective-permute-start.27) | collective-permute-done | bytes 393248 | tf_op jit(solution)/shard_map/ppermute | solution.py:23
  151.4 3.0 %bank_rows.1 = (f32[64,64,1,448]{3,2,1,0:T(1,128)}, f32[64,32,80]{2,1,0:T(8,128)}) custom-call(s32[6]{0:T(128)S(1)} %pad_add_fusion.refs_5_.bank_rows, f32[192,448]{1,0:T(8,128)S(1)} %get-tuple-element.69.own_down, f32[192,512]{1,0:T(8,128)S(1)} %collective-permute-done.27.far, ...), custom_call_target="tpu_custom_call", output_to_operand_aliasing={{0}: (4, {}), {1}: (5, {})} | custom-call | tf_op jit(solution)/shard_map/bank_rows/pallas_call | solution.py:918
  (83 shorter events, 43.0 us)
Async XLA Ops:
  1.7 16.7 %collective-permute-start.1 = (bf16[192,896]{1,0:T(8,128)(2,1)S(1)}, bf16[192,896]{1,0:T(8,128)(2,1)S(1)}, u32[]{:S(2)}, u32[]{:S(2)}) collective-permute-start(bf16[192,896]{1,0:T(8,128)(2,1)S(1)} %constant_dynamic-slice_fusion.1), channel_id=1, source_target_pairs={{0,12},{4,0},{8,4},{12,8},{1,13},{5,1},{9,5},{13,9},{2,14},{6,2},{... | collective-permute-start | bytes 1032200 | tf_op jit(solution)/shard_map/ppermute | solution.py:23
  6.8 15.6 %collective-permute-start = (bf16[192,896]{1,0:T(8,128)(2,1)S(1)}, bf16[192,896]{1,0:T(8,128)(2,1)S(1)}, u32[]{:S(2)}, u32[]{:S(2)}) collective-permute-start(bf16[192,896]{1,0:T(8,128)(2,1)S(1)} %constant_dynamic-slice_fusion.1), channel_id=1, source_target_pairs={{0,4},{4,8},{8,12},{12,0},{1,5},{5,9},{9,13},{13,1},{2,6},{6,10},{... | collective-permute-start | bytes 1032200 | tf_op jit(solution)/shard_map/ppermute | solution.py:23
  11.4 7.0 %collective-permute-start.2 = (bf16[3,64,448]{2,1,0:T(8,128)(2,1)S(1)}, bf16[3,64,448]{2,1,0:T(8,128)(2,1)S(1)}, u32[]{:S(2)}, u32[]{:S(2)}) collective-permute-start(bf16[3,64,448]{2,1,0:T(8,128)(2,1)S(1)} %gather_fusion.1), channel_id=1, source_target_pairs={{0,2},{2,0},{1,3},{3,1},{4,6},{6,4},{5,7},{7,5},{8,10},{10,8},{9,1... | collective-permute-start | bytes 516104 | tf_op jit(solution)/shard_map/ppermute | solution.py:23
  13.5 4.8 %collective-permute-start.3 = (bf16[3,32,80]{2,1,0:T(8,128)(2,1)S(1)}, bf16[3,32,80]{2,1,0:T(8,128)(2,1)S(1)}, u32[]{:S(2)}, u32[]{:S(2)}) collective-permute-start(bf16[3,32,80]{2,1,0:T(8,128)(2,1)S(1)} %gather_fusion.3), channel_id=1, source_target_pairs={{0,2},{2,0},{1,3},{3,1},{4,6},{6,4},{5,7},{7,5},{8,10},{10,8},{9,1... | collective-permute-start | bytes 46088 | tf_op jit(solution)/shard_map/ppermute | solution.py:23
  25.1 18.6 %collective-permute-start.4 = (bf16[336,896]{1,0:T(8,128)(2,1)}, bf16[336,896]{1,0:T(8,128)(2,1)S(1)}, u32[]{:S(2)}, u32[]{:S(2)}) collective-permute-start(bf16[336,896]{1,0:T(8,128)(2,1)} %get-tuple-element.39), channel_id=1, source_target_pairs={{0,4},{4,8},{8,12},{12,0},{1,5},{5,9},{9,13},{13,1},{2,6},{6,10},{... | collective-permute-start | bytes 1806344 | tf_op jit(solution)/shard_map/ppermute | solution.py:23
  28.0 37.3 %collective-permute-start.9 = (bf16[384,896]{1,0:T(8,128)(2,1)}, bf16[384,896]{1,0:T(8,128)(2,1)S(1)}, u32[]{:S(2)}, u32[]{:S(2)}) collective-permute-start(bf16[384,896]{1,0:T(8,128)(2,1)} %get-tuple-element.43), channel_id=1, source_target_pairs={{0,18},{2,16},{16,2},{18,0},{1,19},{3,17},{17,3},{19,1},{4,22},{6,... | collective-permute-start | bytes 2064392 | tf_op jit(solution)/shard_map/ppermute | solution.py:645
  30.5 35.3 %collective-permute-start.8 = (bf16[384,896]{1,0:T(8,128)(2,1)}, bf16[384,896]{1,0:T(8,128)(2,1)S(1)}, u32[]{:S(2)}, u32[]{:S(2)}) collective-permute-start(bf16[384,896]{1,0:T(8,128)(2,1)} %get-tuple-element.43), channel_id=1, source_target_pairs={{0,16},{16,0},{1,17},{17,1},{2,18},{18,2},{3,19},{19,3},{4,20},{20... | collective-permute-start | bytes 2064392 | tf_op jit(solution)/shard_map/ppermute | solution.py:23
  33.0 33.3 %collective-permute-start.7 = (bf16[384,896]{1,0:T(8,128)(2,1)}, bf16[384,896]{1,0:T(8,128)(2,1)S(1)}, u32[]{:S(2)}, u32[]{:S(2)}) collective-permute-start(bf16[384,896]{1,0:T(8,128)(2,1)} %get-tuple-element.43), channel_id=1, source_target_pairs={{0,2},{2,0},{1,3},{3,1},{4,6},{6,4},{5,7},{7,5},{8,10},{10,8},{9,1... | collective-permute-start | bytes 2064392 | tf_op jit(solution)/shard_map/ppermute | solution.py:23
  33.6 19.1 %collective-permute-start.5 = (bf16[144,896]{1,0:T(8,128)(2,1)}, bf16[144,896]{1,0:T(8,128)(2,1)S(1)}, u32[]{:S(2)}, u32[]{:S(2)}) collective-permute-start(bf16[144,896]{1,0:T(8,128)(2,1)} %copy-done.7), channel_id=1, source_target_pairs={{0,8},{4,12},{8,0},{12,4},{1,9},{5,13},{9,1},{13,5},{2,10},{6,14},... | collective-permute-start | bytes 774152 | tf_op jit(solution)/shard_map/ppermute | solution.py:23
  43.8 19.0 %collective-permute-start.6 = (bf16[144,896]{1,0:T(8,128)(2,1)}, bf16[144,896]{1,0:T(8,128)(2,1)S(1)}, u32[]{:S(2)}, u32[]{:S(2)}) collective-permute-start(bf16[144,896]{1,0:T(8,128)(2,1)} %copy-done.6), channel_id=1, source_target_pairs={{0,12},{4,0},{8,4},{12,8},{1,13},{5,1},{9,5},{13,9},{2,14},{6,2},{... | collective-permute-start | bytes 774152 | tf_op jit(solution)/shard_map/ppermute | solution.py:23
  52.8 25.4 %collective-permute-start.13 = (bf16[256,896]{1,0:T(8,128)(2,1)S(1)}, bf16[256,896]{1,0:T(8,128)(2,1)S(1)}, u32[]{:S(2)}, u32[]{:S(2)}) collective-permute-start(bf16[256,896]{1,0:T(8,128)(2,1)S(1)} %get-tuple-element.44), channel_id=1, source_target_pairs={{0,8},{4,12},{8,0},{12,4},{1,9},{5,13},{9,1},{13,5},{2,10},{6,14},... | collective-permute-start | bytes 1376264 | tf_op jit(solution)/shard_map/ppermute | solution.py:23
  62.8 10.3 %collective-permute-start.12 = (bf16[192,896]{1,0:T(8,128)(2,1)S(1)}, bf16[192,896]{1,0:T(8,128)(2,1)S(1)}, u32[]{:S(2)}, u32[]{:S(2)}) collective-permute-start(bf16[192,896]{1,0:T(8,128)(2,1)S(1)} %slice.32), channel_id=1, source_target_pairs={{0,18},{2,16},{16,2},{18,0},{1,19},{3,17},{17,3},{19,1},{4,22},{6,... | collective-permute-start | bytes 1032200 | tf_op jit(solution)/shard_map/ppermute | solution.py:645
  65.3 10.2 %collective-permute-start.11 = (bf16[192,896]{1,0:T(8,128)(2,1)S(1)}, bf16[192,896]{1,0:T(8,128)(2,1)S(1)}, u32[]{:S(2)}, u32[]{:S(2)}) collective-permute-start(bf16[192,896]{1,0:T(8,128)(2,1)S(1)} %slice.32), channel_id=1, source_target_pairs={{0,16},{16,0},{1,17},{17,1},{2,18},{18,2},{3,19},{19,3},{4,20},{20... | collective-permute-start | bytes 1032200 | tf_op jit(solution)/shard_map/ppermute | solution.py:23
  65.8 10.0 %collective-permute-start.10 = (bf16[192,896]{1,0:T(8,128)(2,1)S(1)}, bf16[192,896]{1,0:T(8,128)(2,1)S(1)}, u32[]{:S(2)}, u32[]{:S(2)}) collective-permute-start(bf16[192,896]{1,0:T(8,128)(2,1)S(1)} %slice.32), channel_id=1, source_target_pairs={{0,2},{2,0},{1,3},{3,1},{4,6},{6,4},{5,7},{7,5},{8,10},{10,8},{9,1... | collective-permute-start | bytes 1032200 | tf_op jit(solution)/shard_map/ppermute | solution.py:23
  85.6 4.8 %collective-permute-start.16 = (bf16[256,256]{1,0:T(8,128)(2,1)S(1)}, bf16[256,256]{1,0:T(8,128)(2,1)S(1)}, u32[]{:S(2)}, u32[]{:S(2)}) collective-permute-start(bf16[256,256]{1,0:T(8,128)(2,1)S(1)} %get-tuple-element.48.refs_0_), channel_id=1, source_target_pairs={{0,8},{4,12},{1,9},{5,13},{2,10},{6,14},{3,11},{7,15},{16,24},{20,... | collective-permute-start | bytes 393224 | tf_op jit(solution)/shard_map/ppermute | solution.py:29
  87.1 6.0 %collective-permute-start.15 = (bf16[256,256]{1,0:T(8,128)(2,1)S(1)}, bf16[256,256]{1,0:T(8,128)(2,1)S(1)}, u32[]{:S(2)}, u32[]{:S(2)}) collective-permute-start(bf16[256,256]{1,0:T(8,128)(2,1)S(1)} %get-tuple-element.48.refs_0_), channel_id=1, source_target_pairs={{0,4},{4,8},{8,12},{1,5},{5,9},{9,13},{2,6},{6,10},{10,14},{3,7},{... | collective-permute-start | bytes 393224 | tf_op jit(solution)/shard_map/ppermute | solution.py:29
  93.1 14.2 %collective-permute-start.19 = (bf16[256,896]{1,0:T(8,128)(2,1)S(1)}, bf16[256,896]{1,0:T(8,128)(2,1)S(1)}, u32[]{:S(2)}, u32[]{:S(2)}) collective-permute-start(bf16[256,896]{1,0:T(8,128)(2,1)S(1)} %pass_after.1), channel_id=1, source_target_pairs={{0,4},{4,8},{8,12},{12,0},{1,5},{5,9},{9,13},{13,1},{2,6},{6,10},{... | collective-permute-start | bytes 1376264 | tf_op jit(solution)/shard_map/ppermute | solution.py:23
  107.3 7.8 %collective-permute-start.20 = (f32[128,256]{1,0:T(8,128)S(1)}, f32[128,256]{1,0:T(8,128)S(1)}, u32[]{:S(2)}, u32[]{:S(2)}) collective-permute-start(f32[128,256]{1,0:T(8,128)S(1)} %get-tuple-element.55), channel_id=1, source_target_pairs={{4,0},{8,4},{12,8},{5,1},{9,5},{13,9},{6,2},{10,6},{14,10},{7,3},{... | collective-permute-start | bytes 393224 | tf_op jit(solution)/shard_map/ppermute | solution.py:29
  108.6 13.6 %collective-permute-start.21 = (f32[128,256]{1,0:T(8,128)S(1)}, f32[128,256]{1,0:T(8,128)S(1)}, u32[]{:S(2)}, u32[]{:S(2)}) collective-permute-start(f32[128,256]{1,0:T(8,128)S(1)} %get-tuple-element.56), channel_id=1, source_target_pairs={{8,0},{12,4},{9,1},{13,5},{10,2},{14,6},{11,3},{15,7},{24,16},{28,... | collective-permute-start | bytes 393224 | tf_op jit(solution)/shard_map/ppermute | solution.py:29
  122.3 17.3 %collective-permute-start.23 = (bf16[256,896]{1,0:T(8,128)(2,1)S(1)}, bf16[256,896]{1,0:T(8,128)(2,1)S(1)}, u32[]{:S(2)}, u32[]{:S(2)}) collective-permute-start(bf16[256,896]{1,0:T(8,128)(2,1)S(1)} %get-tuple-element.63), channel_id=1, source_target_pairs={{0,12},{4,0},{8,4},{12,8},{1,13},{5,1},{9,5},{13,9},{2,14},{6,2},{... | collective-permute-start | bytes 1376264 | tf_op jit(solution)/shard_map/ppermute | solution.py:23
  125.2 8.2 %collective-permute-start.24 = (f32[248,128]{1,0:T(8,128)S(1)}, f32[248,128]{1,0:T(8,128)S(1)}, u32[]{:S(2)}, u32[]{:S(2)}) collective-permute-start(f32[248,128]{1,0:T(8,128)S(1)} %get-tuple-element.65), channel_id=1, source_target_pairs={{0,4},{4,8},{8,12},{12,0},{1,5},{5,9},{9,13},{13,1},{2,6},{6,10},{... | collective-permute-start | bytes 380936 | tf_op jit(solution)/shard_map/ppermute | solution.py:23
  127.2 12.4 %collective-permute-start.25 = (f32[248,128]{1,0:T(8,128)S(1)}, f32[248,128]{1,0:T(8,128)S(1)}, u32[]{:S(2)}, u32[]{:S(2)}) collective-permute-start(f32[248,128]{1,0:T(8,128)S(1)} %get-tuple-element.66), channel_id=1, source_target_pairs={{0,8},{4,12},{8,0},{12,4},{1,9},{5,13},{9,1},{13,5},{2,10},{6,14},... | collective-permute-start | bytes 380936 | tf_op jit(solution)/shard_map/ppermute | solution.py:23
  127.2 12.4 %collective-permute-start.26 = (f32[248,128]{1,0:T(8,128)S(1)}, f32[248,128]{1,0:T(8,128)S(1)}, u32[]{:S(2)}, u32[]{:S(2)}) collective-permute-start(f32[248,128]{1,0:T(8,128)S(1)} %get-tuple-element.67), channel_id=1, source_target_pairs={{0,12},{4,0},{8,4},{12,8},{1,13},{5,1},{9,5},{13,9},{2,14},{6,2},{... | collective-permute-start | bytes 380936 | tf_op jit(solution)/shard_map/ppermute | solution.py:23
  141.4 10.0 %collective-permute-start.27 = (f32[192,512]{1,0:T(8,128)S(1)}, f32[192,512]{1,0:T(8,128)S(1)}, u32[]{:S(2)}, u32[]{:S(2)}) collective-permute-start(f32[192,512]{1,0:T(8,128)S(1)} %get-tuple-element.70), channel_id=1, source_target_pairs={{0,2},{2,0},{1,3},{3,1},{4,6},{6,4},{5,7},{7,5},{8,10},{10,8},{9,1... | collective-permute-start | bytes 1179656 | tf_op jit(solution)/shard_map/ppermute | solution.py:23
  (13 other events, 87.5 us)

commit v16 on v15

--- a/solution.py
+++ b/solution.py
@@ -350,8 +350,8 @@
         ).astype(jnp.bfloat16)
 
 
-def sum_kernel(unused, kept, arrived, *refs):
-    for back, total in enumerate(refs[unused:]):
+def sum_kernel(kept, arrived, *sums):
+    for back, total in enumerate(sums):
         total[...] = kept[back] + arrived[back]
 
 
@@ -802,16 +802,15 @@
     )(document_lengths, queries, incoming, cosines, sines, *blocks, *early_columns)
 
     other_query = shift(query_grad, "tp", 1)
-    due = [column_parts[1]]
     pair_sums = pl.pallas_call(
-        functools.partial(sum_kernel, len(due)),
+        sum_kernel,
         out_shape=[jax.ShapeDtypeStruct((own_rows, 2 * HEAD_WIDTH), f32)] * block_count,
-        in_specs=[in_vmem()] * 2 + [in_place()] * len(due),
+        in_specs=[in_vmem()] * 2,
         out_specs=[in_vmem()] * block_count,
         compiler_params=pltpu.CompilerParams(vmem_limit_bytes=8 * mebibyte),
         cost_estimate=cost(0, 12 * block_count * own_rows * 2 * HEAD_WIDTH),
         name="pair_sums",
-    )(kept, shift(sent, "tp", 1), *due)
+    )(kept, shift(sent, "tp", 1))
     pair_terms = [pair_sums[0]]
     pair_terms += [push(pair_sums[back], "seq", -back) for back in range(1, block_count)]
     pair_grad, late_block = pl.pallas_call(
@@ -820,13 +819,13 @@
             jax.ShapeDtypeStruct((own_rows, 2 * HEAD_WIDTH), bf16),
             jax.ShapeDtypeStruct((rows, down_width), bf16),
         ],
-        in_specs=[in_vmem()] * (2 + block_count) + [in_place()],
+        in_specs=[in_vmem()] * (2 + block_count) + [in_place()] * 2,
         out_specs=[in_vmem(), in_place()],
         input_output_aliases={2 + block_count: 1},
         compiler_params=pltpu.CompilerParams(vmem_limit_bytes=8 * mebibyte),
         cost_estimate=cost(0, 12 * block_count * own_rows * 2 * HEAD_WIDTH),
         name="pair_gradients",
-    )(cosines, sines, *pair_terms, column_blocks[-1])
+    )(cosines, sines, *pair_terms, column_blocks[-1], column_parts[1])
     column_parts[-1] = shift(late_block, "seq", seq_count - 1)
     other_pair = shift(pair_grad, "tp", 1)
 

time: 155 us -> 157 us (1.013)
  waiting for transfers between devices: 65.5 us -> 67.5 us
    ppermute x22, waiting for transfers between devices: 43.6 us -> 49.6 us  [shift(): lax.ppermute(value, axis, [(at, (at + steps) % count) for at in range(cou...]
    ppermute x4, waiting for transfers between devices: 15.2 us -> 11.1 us  [push(): return lax.ppermute(value, axis, pairs)]
  transfers between devices with their start and end apart: 28 -> 28, of which waited for: 20 -> 20; matrix products, arithmetic and copies ran while one was open for 10% -> 10% of each run, Pallas kernels for 6% -> 4%
where the time goes in v16:
time: 157 us; the launch traced here: 156 us
  waiting for transfers between devices  67.5 us (43%)
  starting transfers between devices  44.3 us (28%)
  Pallas kernels  21 us (13%)
  local copies, waits for them, and re-layouts  19 us (12%)
  other arithmetic  2.42 us (2%)
  between operations  2.2 us (1%)
    ppermute x22, waiting for transfers between devices, shift(): lax.ppermute(value, axis, [(at, (at + steps) % count) for at in range(cou...  49.6 us
    ppermute x22, starting transfers between devices, shift(): lax.ppermute(value, axis, [(at, (at + steps) % count) for at in range(cou...  32.2 us
    ppermute x4, waiting for transfers between devices, push(): return lax.ppermute(value, axis, pairs)  11.1 us
    ppermute x4, starting transfers between devices, push(): return lax.ppermute(value, axis, pairs)  7.14 us
    ppermute x2, waiting for transfers between devices, over_plane(): lax.ppermute(value, ('groups', 'batch'), over_both)  6.78 us
    unnamed x19, local copies, waits for them, and re-layouts  5.42 us
    ppermute x2, starting transfers between devices, over_plane(): lax.ppermute(value, ('groups', 'batch'), over_both)  4.96 us
    pallas_call x1, Pallas kernels, shards(): pl.pallas_call(token_kernel, grid=(width // chunk,), out_shape=jax.ShapeD...  4.84 us
  transfers between devices with their start and end apart: 28, of which 20 were waited for; matrix products, arithmetic and copies ran while one was open for 10% of the time, Pallas kernels for 4%

profile of v16, /device:TPU:0, one launch (start us, length us, event | category | flops | bytes accessed | tf_op | source)
XLA Modules:
  0.0 156.4 jit_solution(1779056015747879600)
XLA Ops:
  1.7 5.1 %collective-permute-start.1 = (bf16[192,896]{1,0:T(8,128)(2,1)S(1)}, bf16[192,896]{1,0:T(8,128)(2,1)S(1)}, u32[]{:S(2)}, u32[]{:S(2)}) collective-permute-start(bf16[192,896]{1,0:T(8,128)(2,1)S(1)} %constant_dynamic-slice_fusion.1), channel_id=1, source_target_pairs={{0,12},{4,0},{8,4},{12,8},{1,13},{5,1},{9,5},{13,9},{2,14},{6,2},{... | collective-permute-start | bytes 1032200 | tf_op jit(solution)/shard_map/ppermute | solution.py:23
  8.7 2.7 %gather_fusion.1 = bf16[3,64,448]{2,1,0:T(8,128)(2,1)S(1)} fusion(bf16[64,64,448]{2,1,0:T(8,128)(2,1)} %bitcast.19, s32[1024]{0:T(1024)S(1)} %pad_clamp_fusion), kind=kCustom, calls=%fused_computation.1 | custom fusion | bytes 344076 | tf_op jit(solution)/shard_map/gather | solution.py:620
  14.7 2.7 %gather_fusion = bf16[3,64,448]{2,1,0:T(8,128)(2,1)S(1)} fusion(bf16[64,64,448]{2,1,0:T(8,128)(2,1)} %bitcast.20, s32[1024]{0:T(1024)S(1)} %pad_clamp_fusion.1), kind=kCustom, calls=%fused_computation | custom fusion | bytes 344076 | tf_op jit(solution)/shard_map/gather | solution.py:622
  18.4 4.0 %collective-permute-done.before.refs_1_ = bf16[192,896]{1,0:T(8,128)(2,1)S(1)} collective-permute-done((bf16[192,896]{1,0:T(8,128)(2,1)S(1)}, bf16[192,896]{1,0:T(8,128)(2,1)S(1)}, u32[]{:S(2)}, u32[]{:S(2)}) %collective-permute-start) | collective-permute-done | bytes 344096 | tf_op jit(solution)/shard_map/ppermute | solution.py:23
  34.3 9.5 %collective-permute-done.4.refs_0_.refs_3_ = bf16[336,896]{1,0:T(8,128)(2,1)S(1)} collective-permute-done((bf16[336,896]{1,0:T(8,128)(2,1)}, bf16[336,896]{1,0:T(8,128)(2,1)S(1)}, u32[]{:S(2)}, u32[]{:S(2)}) %collective-permute-start.4) | collective-permute-done | bytes 602144 | tf_op jit(solution)/shard_map/ppermute | solution.py:23
  44.6 4.5 %broadcast_in_dim.47.refs_1_.down_zeros = f32[64,64,1,448]{3,2,1,0:T(1,128)S(1)} broadcast(f32[]{:T(128)} %constant.11.clone.1), dimensions={} | broadcast | bytes 7340036 | tf_op jit(solution)/shard_map/broadcast_in_dim | solution.py:594
  49.3 3.2 %copy-done.1 = f32[64,64,1,448]{3,2,1,0:T(1,128)} copy-done((f32[64,64,1,448]{3,2,1,0:T(1,128)}, f32[64,64,1,448]{3,2,1,0:T(1,128)S(1)}, u32[]{:S(2)}) %copy-start.1) | copy-done | bytes 7340056
  52.8 10.0 %collective-permute-start.13 = (bf16[256,896]{1,0:T(8,128)(2,1)S(1)}, bf16[256,896]{1,0:T(8,128)(2,1)S(1)}, u32[]{:S(2)}, u32[]{:S(2)}) collective-permute-start(bf16[256,896]{1,0:T(8,128)(2,1)S(1)} %get-tuple-element.44), channel_id=1, source_target_pairs={{0,8},{4,12},{8,0},{12,4},{1,9},{5,13},{9,1},{13,5},{2,10},{6,14},... | collective-permute-start | bytes 1376264 | tf_op jit(solution)/shard_map/ppermute | solution.py:23
  62.8 2.5 %collective-permute-start.12 = (bf16[192,896]{1,0:T(8,128)(2,1)S(1)}, bf16[192,896]{1,0:T(8,128)(2,1)S(1)}, u32[]{:S(2)}, u32[]{:S(2)}) collective-permute-start(bf16[192,896]{1,0:T(8,128)(2,1)S(1)} %slice.32), channel_id=1, source_target_pairs={{0,18},{2,16},{16,2},{18,0},{1,19},{3,17},{17,3},{19,1},{4,22},{6,... | collective-permute-start | bytes 1032200 | tf_op jit(solution)/shard_map/ppermute | solution.py:645
  66.3 6.8 %collective-permute-done.12.refs_12_ = bf16[192,896]{1,0:T(8,128)(2,1)S(1)} collective-permute-done((bf16[192,896]{1,0:T(8,128)(2,1)S(1)}, bf16[192,896]{1,0:T(8,128)(2,1)S(1)}, u32[]{:S(2)}, u32[]{:S(2)}) %collective-permute-start.12) | collective-permute-done | bytes 344096 | tf_op jit(solution)/shard_map/ppermute | solution.py:645
  78.2 3.8 %project.1 = (f32[256,896]{1,0:T(8,128)S(1)}, bf16[896,3584]{1,0:T(8,128)(2,1)S(1)}, bf16[3,64,640]{2,1,0:T(8,128)(2,1)S(1)}) custom-call(bf16[256,3584]{1,0:T(8,128)(2,1)S(1)} %bitcast.16, bf16[192,3584]{1,0:T(8,128)(2,1)S(1)} %copy-done.4, bf16[192,896]{1,0:T(8,128)(2,1)S(1)} %collective-permute-done.before.refs_1_, ...), custom_call_target="tpu_custom_call" | custom-call | flops 1644167168 | bytes 8257536 | tf_op jit(solution)/shard_map/project/pallas_call | solution.py:739
  82.1 2.5 %collective-permute-done.14.theirs = f32[256,896]{1,0:T(8,128)S(1)} collective-permute-done((f32[256,896]{1,0:T(8,128)S(1)}, f32[256,896]{1,0:T(8,128)S(1)}, u32[]{:S(2)}, u32[]{:S(2)}) %collective-permute-start.14) | collective-permute-done | bytes 917536 | tf_op jit(solution)/shard_map/ppermute | solution.py:23
  87.1 3.1 %collective-permute-start.15 = (bf16[256,256]{1,0:T(8,128)(2,1)S(1)}, bf16[256,256]{1,0:T(8,128)(2,1)S(1)}, u32[]{:S(2)}, u32[]{:S(2)}) collective-permute-start(bf16[256,256]{1,0:T(8,128)(2,1)S(1)} %get-tuple-element.48.refs_0_), channel_id=1, source_target_pairs={{0,4},{4,8},{8,12},{1,5},{5,9},{9,13},{2,6},{6,10},{10,14},{3,7},{... | collective-permute-start | bytes 393224 | tf_op jit(solution)/shard_map/ppermute | solution.py:29
  90.4 2.7 %collective-permute-done.15.refs_1_ = bf16[256,256]{1,0:T(8,128)(2,1)S(1)} collective-permute-done((bf16[256,256]{1,0:T(8,128)(2,1)S(1)}, bf16[256,256]{1,0:T(8,128)(2,1)S(1)}, u32[]{:S(2)}, u32[]{:S(2)}) %collective-permute-start.15) | collective-permute-done | bytes 131104 | tf_op jit(solution)/shard_map/ppermute | solution.py:29
  93.1 3.4 %attention.1 = (bf16[128,512]{1,0:T(8,128)(2,1)}, bf16[128,512]{1,0:T(8,128)(2,1)S(1)}, f32[3,128,256]{2,1,0:T(8,128)S(1)}, f32[3,128,256]{2,1,0:T(8,128)S(1)}) custom-call(s32[2,3]{1,0:T(2,128)S(1)} %copy-done.5, bf16[512,128]{1,0:T(8,128)(2,1)S(1)} %get-tuple-element.47.queries, bf16[128,512]{1,0:T(8,128)(2,1)S(1)} %bitcast.17, ...), custom_call_target="tpu_custom_call" | custom-call | flops 503316480 | bytes 786432 | tf_op jit(solution)/shard_map/attention/pallas_call | solution.py:782
  96.5 3.8 %collective-permute-start.21 = (bf16[256,896]{1,0:T(8,128)(2,1)S(1)}, bf16[256,896]{1,0:T(8,128)(2,1)S(1)}, u32[]{:S(2)}, u32[]{:S(2)}) collective-permute-start(bf16[256,896]{1,0:T(8,128)(2,1)S(1)} %pass_after.1), channel_id=1, source_target_pairs={{0,4},{4,8},{8,12},{12,0},{1,5},{5,9},{9,13},{13,1},{2,6},{6,10},{... | collective-permute-start | bytes 1376264 | tf_op jit(solution)/shard_map/ppermute | solution.py:23
  103.0 9.2 %collective-permute-done.21.refs_4_.refs_1_ = bf16[256,896]{1,0:T(8,128)(2,1)S(1)} collective-permute-done((bf16[256,896]{1,0:T(8,128)(2,1)S(1)}, bf16[256,896]{1,0:T(8,128)(2,1)S(1)}, u32[]{:S(2)}, u32[]{:S(2)}) %collective-permute-start.21) | collective-permute-done | bytes 458784 | tf_op jit(solution)/shard_map/ppermute | solution.py:23
  112.2 2.6 %collective-permute-done.19.refs_1_ = f32[128,256]{1,0:T(8,128)S(1)} collective-permute-done((f32[128,256]{1,0:T(8,128)S(1)}, f32[128,256]{1,0:T(8,128)S(1)}, u32[]{:S(2)}, u32[]{:S(2)}) %collective-permute-start.19) | collective-permute-done | bytes 131104 | tf_op jit(solution)/shard_map/ppermute | solution.py:29
  114.8 5.6 %collective-permute-done.20.refs_2_ = f32[128,256]{1,0:T(8,128)S(1)} collective-permute-done((f32[128,256]{1,0:T(8,128)S(1)}, f32[128,256]{1,0:T(8,128)S(1)}, u32[]{:S(2)}, u32[]{:S(2)}) %collective-permute-start.20) | collective-permute-done | bytes 131104 | tf_op jit(solution)/shard_map/ppermute | solution.py:29
  127.9 7.9 %collective-permute-done.24.refs_5_ = f32[248,128]{1,0:T(8,128)S(1)} collective-permute-done((f32[248,128]{1,0:T(8,128)S(1)}, f32[248,128]{1,0:T(8,128)S(1)}, u32[]{:S(2)}, u32[]{:S(2)}) %collective-permute-start.24) | collective-permute-done | bytes 127008 | tf_op jit(solution)/shard_map/ppermute | solution.py:23
  135.8 3.8 %collective-permute-done.25.refs_6_ = f32[248,128]{1,0:T(8,128)S(1)} collective-permute-done((f32[248,128]{1,0:T(8,128)S(1)}, f32[248,128]{1,0:T(8,128)S(1)}, u32[]{:S(2)}, u32[]{:S(2)}) %collective-permute-start.25) | collective-permute-done | bytes 127008 | tf_op jit(solution)/shard_map/ppermute | solution.py:23
  144.6 4.8 %token_gradient.1 = bf16[256,3584]{1,0:T(8,128)(2,1)} custom-call(bf16[256,896]{1,0:T(8,128)(2,1)S(1)} %get-tuple-element.60.gradients, bf16[896,3584]{1,0:T(8,128)(2,1)S(1)} %get-tuple-element.61.matrix), custom_call_target="tpu_custom_call" | custom-call | flops 1644167168 | bytes 8257536 | tf_op jit(solution)/shard_map/token_gradient/pallas_call | solution.py:865
  149.5 3.9 %collective-permute-done.27.far = f32[192,512]{1,0:T(8,128)S(1)} collective-permute-done((f32[192,512]{1,0:T(8,128)S(1)}, f32[192,512]{1,0:T(8,128)S(1)}, u32[]{:S(2)}, u32[]{:S(2)}) %collective-permute-start.27) | collective-permute-done | bytes 393248 | tf_op jit(solution)/shard_map/ppermute | solution.py:23
  153.4 3.0 %bank_rows.1 = (f32[64,64,1,448]{3,2,1,0:T(1,128)}, f32[64,32,80]{2,1,0:T(8,128)}) custom-call(s32[6]{0:T(128)S(1)} %pad_add_fusion.refs_5_.bank_rows, f32[192,448]{1,0:T(8,128)S(1)} %get-tuple-element.69.own_down, f32[192,512]{1,0:T(8,128)S(1)} %collective-permute-done.27.far, ...), custom_call_target="tpu_custom_call", output_to_operand_aliasing={{0}: (4, {}), {1}: (5, {})} | custom-call | tf_op jit(solution)/shard_map/bank_rows/pallas_call | solution.py:917
  (83 shorter events, 42.9 us)
Async XLA Ops:
  1.7 16.7 %collective-permute-start.1 = (bf16[192,896]{1,0:T(8,128)(2,1)S(1)}, bf16[192,896]{1,0:T(8,128)(2,1)S(1)}, u32[]{:S(2)}, u32[]{:S(2)}) collective-permute-start(bf16[192,896]{1,0:T(8,128)(2,1)S(1)} %constant_dynamic-slice_fusion.1), channel_id=1, source_target_pairs={{0,12},{4,0},{8,4},{12,8},{1,13},{5,1},{9,5},{13,9},{2,14},{6,2},{... | collective-permute-start | bytes 1032200 | tf_op jit(solution)/shard_map/ppermute | solution.py:23
  6.8 15.6 %collective-permute-start = (bf16[192,896]{1,0:T(8,128)(2,1)S(1)}, bf16[192,896]{1,0:T(8,128)(2,1)S(1)}, u32[]{:S(2)}, u32[]{:S(2)}) collective-permute-start(bf16[192,896]{1,0:T(8,128)(2,1)S(1)} %constant_dynamic-slice_fusion.1), channel_id=1, source_target_pairs={{0,4},{4,8},{8,12},{12,0},{1,5},{5,9},{9,13},{13,1},{2,6},{6,10},{... | collective-permute-start | bytes 1032200 | tf_op jit(solution)/shard_map/ppermute | solution.py:23
  11.4 7.0 %collective-permute-start.2 = (bf16[3,64,448]{2,1,0:T(8,128)(2,1)S(1)}, bf16[3,64,448]{2,1,0:T(8,128)(2,1)S(1)}, u32[]{:S(2)}, u32[]{:S(2)}) collective-permute-start(bf16[3,64,448]{2,1,0:T(8,128)(2,1)S(1)} %gather_fusion.1), channel_id=1, source_target_pairs={{0,2},{2,0},{1,3},{3,1},{4,6},{6,4},{5,7},{7,5},{8,10},{10,8},{9,1... | collective-permute-start | bytes 516104 | tf_op jit(solution)/shard_map/ppermute | solution.py:23
  13.5 4.8 %collective-permute-start.3 = (bf16[3,32,80]{2,1,0:T(8,128)(2,1)S(1)}, bf16[3,32,80]{2,1,0:T(8,128)(2,1)S(1)}, u32[]{:S(2)}, u32[]{:S(2)}) collective-permute-start(bf16[3,32,80]{2,1,0:T(8,128)(2,1)S(1)} %gather_fusion.3), channel_id=1, source_target_pairs={{0,2},{2,0},{1,3},{3,1},{4,6},{6,4},{5,7},{7,5},{8,10},{10,8},{9,1... | collective-permute-start | bytes 46088 | tf_op jit(solution)/shard_map/ppermute | solution.py:23
  25.1 18.6 %collective-permute-start.4 = (bf16[336,896]{1,0:T(8,128)(2,1)}, bf16[336,896]{1,0:T(8,128)(2,1)S(1)}, u32[]{:S(2)}, u32[]{:S(2)}) collective-permute-start(bf16[336,896]{1,0:T(8,128)(2,1)} %get-tuple-element.39), channel_id=1, source_target_pairs={{0,4},{4,8},{8,12},{12,0},{1,5},{5,9},{9,13},{13,1},{2,6},{6,10},{... | collective-permute-start | bytes 1806344 | tf_op jit(solution)/shard_map/ppermute | solution.py:23
  28.0 37.3 %collective-permute-start.9 = (bf16[384,896]{1,0:T(8,128)(2,1)}, bf16[384,896]{1,0:T(8,128)(2,1)S(1)}, u32[]{:S(2)}, u32[]{:S(2)}) collective-permute-start(bf16[384,896]{1,0:T(8,128)(2,1)} %get-tuple-element.43), channel_id=1, source_target_pairs={{0,18},{2,16},{16,2},{18,0},{1,19},{3,17},{17,3},{19,1},{4,22},{6,... | collective-permute-start | bytes 2064392 | tf_op jit(solution)/shard_map/ppermute | solution.py:645
  30.5 35.3 %collective-permute-start.8 = (bf16[384,896]{1,0:T(8,128)(2,1)}, bf16[384,896]{1,0:T(8,128)(2,1)S(1)}, u32[]{:S(2)}, u32[]{:S(2)}) collective-permute-start(bf16[384,896]{1,0:T(8,128)(2,1)} %get-tuple-element.43), channel_id=1, source_target_pairs={{0,16},{16,0},{1,17},{17,1},{2,18},{18,2},{3,19},{19,3},{4,20},{20... | collective-permute-start | bytes 2064392 | tf_op jit(solution)/shard_map/ppermute | solution.py:23
  33.0 33.3 %collective-permute-start.7 = (bf16[384,896]{1,0:T(8,128)(2,1)}, bf16[384,896]{1,0:T(8,128)(2,1)S(1)}, u32[]{:S(2)}, u32[]{:S(2)}) collective-permute-start(bf16[384,896]{1,0:T(8,128)(2,1)} %get-tuple-element.43), channel_id=1, source_target_pairs={{0,2},{2,0},{1,3},{3,1},{4,6},{6,4},{5,7},{7,5},{8,10},{10,8},{9,1... | collective-permute-start | bytes 2064392 | tf_op jit(solution)/shard_map/ppermute | solution.py:23
  33.6 19.1 %collective-permute-start.5 = (bf16[144,896]{1,0:T(8,128)(2,1)}, bf16[144,896]{1,0:T(8,128)(2,1)S(1)}, u32[]{:S(2)}, u32[]{:S(2)}) collective-permute-start(bf16[144,896]{1,0:T(8,128)(2,1)} %copy-done.7), channel_id=1, source_target_pairs={{0,8},{4,12},{8,0},{12,4},{1,9},{5,13},{9,1},{13,5},{2,10},{6,14},... | collective-permute-start | bytes 774152 | tf_op jit(solution)/shard_map/ppermute | solution.py:23
  43.8 19.0 %collective-permute-start.6 = (bf16[144,896]{1,0:T(8,128)(2,1)}, bf16[144,896]{1,0:T(8,128)(2,1)S(1)}, u32[]{:S(2)}, u32[]{:S(2)}) collective-permute-start(bf16[144,896]{1,0:T(8,128)(2,1)} %copy-done.6), channel_id=1, source_target_pairs={{0,12},{4,0},{8,4},{12,8},{1,13},{5,1},{9,5},{13,9},{2,14},{6,2},{... | collective-permute-start | bytes 774152 | tf_op jit(solution)/shard_map/ppermute | solution.py:23
  52.8 25.4 %collective-permute-start.13 = (bf16[256,896]{1,0:T(8,128)(2,1)S(1)}, bf16[256,896]{1,0:T(8,128)(2,1)S(1)}, u32[]{:S(2)}, u32[]{:S(2)}) collective-permute-start(bf16[256,896]{1,0:T(8,128)(2,1)S(1)} %get-tuple-element.44), channel_id=1, source_target_pairs={{0,8},{4,12},{8,0},{12,4},{1,9},{5,13},{9,1},{13,5},{2,10},{6,14},... | collective-permute-start | bytes 1376264 | tf_op jit(solution)/shard_map/ppermute | solution.py:23
  62.8 10.3 %collective-permute-start.12 = (bf16[192,896]{1,0:T(8,128)(2,1)S(1)}, bf16[192,896]{1,0:T(8,128)(2,1)S(1)}, u32[]{:S(2)}, u32[]{:S(2)}) collective-permute-start(bf16[192,896]{1,0:T(8,128)(2,1)S(1)} %slice.32), channel_id=1, source_target_pairs={{0,18},{2,16},{16,2},{18,0},{1,19},{3,17},{17,3},{19,1},{4,22},{6,... | collective-permute-start | bytes 1032200 | tf_op jit(solution)/shard_map/ppermute | solution.py:645
  65.3 10.2 %collective-permute-start.11 = (bf16[192,896]{1,0:T(8,128)(2,1)S(1)}, bf16[192,896]{1,0:T(8,128)(2,1)S(1)}, u32[]{:S(2)}, u32[]{:S(2)}) collective-permute-start(bf16[192,896]{1,0:T(8,128)(2,1)S(1)} %slice.32), channel_id=1, source_target_pairs={{0,16},{16,0},{1,17},{17,1},{2,18},{18,2},{3,19},{19,3},{4,20},{20... | collective-permute-start | bytes 1032200 | tf_op jit(solution)/shard_map/ppermute | solution.py:23
  65.8 10.0 %collective-permute-start.10 = (bf16[192,896]{1,0:T(8,128)(2,1)S(1)}, bf16[192,896]{1,0:T(8,128)(2,1)S(1)}, u32[]{:S(2)}, u32[]{:S(2)}) collective-permute-start(bf16[192,896]{1,0:T(8,128)(2,1)S(1)} %slice.32), channel_id=1, source_target_pairs={{0,2},{2,0},{1,3},{3,1},{4,6},{6,4},{5,7},{7,5},{8,10},{10,8},{9,1... | collective-permute-start | bytes 1032200 | tf_op jit(solution)/shard_map/ppermute | solution.py:23
  85.6 4.8 %collective-permute-start.16 = (bf16[256,256]{1,0:T(8,128)(2,1)S(1)}, bf16[256,256]{1,0:T(8,128)(2,1)S(1)}, u32[]{:S(2)}, u32[]{:S(2)}) collective-permute-start(bf16[256,256]{1,0:T(8,128)(2,1)S(1)} %get-tuple-element.48.refs_0_), channel_id=1, source_target_pairs={{0,8},{4,12},{1,9},{5,13},{2,10},{6,14},{3,11},{7,15},{16,24},{20,... | collective-permute-start | bytes 393224 | tf_op jit(solution)/shard_map/ppermute | solution.py:29
  87.1 6.0 %collective-permute-start.15 = (bf16[256,256]{1,0:T(8,128)(2,1)S(1)}, bf16[256,256]{1,0:T(8,128)(2,1)S(1)}, u32[]{:S(2)}, u32[]{:S(2)}) collective-permute-start(bf16[256,256]{1,0:T(8,128)(2,1)S(1)} %get-tuple-element.48.refs_0_), channel_id=1, source_target_pairs={{0,4},{4,8},{8,12},{1,5},{5,9},{9,13},{2,6},{6,10},{10,14},{3,7},{... | collective-permute-start | bytes 393224 | tf_op jit(solution)/shard_map/ppermute | solution.py:29
  96.5 15.7 %collective-permute-start.21 = (bf16[256,896]{1,0:T(8,128)(2,1)S(1)}, bf16[256,896]{1,0:T(8,128)(2,1)S(1)}, u32[]{:S(2)}, u32[]{:S(2)}) collective-permute-start(bf16[256,896]{1,0:T(8,128)(2,1)S(1)} %pass_after.1), channel_id=1, source_target_pairs={{0,4},{4,8},{8,12},{12,0},{1,5},{5,9},{9,13},{13,1},{2,6},{6,10},{... | collective-permute-start | bytes 1376264 | tf_op jit(solution)/shard_map/ppermute | solution.py:23
  100.4 14.4 %collective-permute-start.19 = (f32[128,256]{1,0:T(8,128)S(1)}, f32[128,256]{1,0:T(8,128)S(1)}, u32[]{:S(2)}, u32[]{:S(2)}) collective-permute-start(f32[128,256]{1,0:T(8,128)S(1)} %get-tuple-element.54), channel_id=1, source_target_pairs={{4,0},{8,4},{12,8},{5,1},{9,5},{13,9},{6,2},{10,6},{14,10},{7,3},{... | collective-permute-start | bytes 393224 | tf_op jit(solution)/shard_map/ppermute | solution.py:29
  101.7 18.7 %collective-permute-start.20 = (f32[128,256]{1,0:T(8,128)S(1)}, f32[128,256]{1,0:T(8,128)S(1)}, u32[]{:S(2)}, u32[]{:S(2)}) collective-permute-start(f32[128,256]{1,0:T(8,128)S(1)} %get-tuple-element.55), channel_id=1, source_target_pairs={{8,0},{12,4},{9,1},{13,5},{10,2},{14,6},{11,3},{15,7},{24,16},{28,... | collective-permute-start | bytes 393224 | tf_op jit(solution)/shard_map/ppermute | solution.py:29
  120.5 20.7 %collective-permute-start.23 = (bf16[256,896]{1,0:T(8,128)(2,1)S(1)}, bf16[256,896]{1,0:T(8,128)(2,1)S(1)}, u32[]{:S(2)}, u32[]{:S(2)}) collective-permute-start(bf16[256,896]{1,0:T(8,128)(2,1)S(1)} %get-tuple-element.63), channel_id=1, source_target_pairs={{0,12},{4,0},{8,4},{12,8},{1,13},{5,1},{9,5},{13,9},{2,14},{6,2},{... | collective-permute-start | bytes 1376264 | tf_op jit(solution)/shard_map/ppermute | solution.py:23
  123.5 12.3 %collective-permute-start.24 = (f32[248,128]{1,0:T(8,128)S(1)}, f32[248,128]{1,0:T(8,128)S(1)}, u32[]{:S(2)}, u32[]{:S(2)}) collective-permute-start(f32[248,128]{1,0:T(8,128)S(1)} %get-tuple-element.65), channel_id=1, source_target_pairs={{0,4},{4,8},{8,12},{12,0},{1,5},{5,9},{9,13},{13,1},{2,6},{6,10},{... | collective-permute-start | bytes 380936 | tf_op jit(solution)/shard_map/ppermute | solution.py:23
  125.4 14.2 %collective-permute-start.25 = (f32[248,128]{1,0:T(8,128)S(1)}, f32[248,128]{1,0:T(8,128)S(1)}, u32[]{:S(2)}, u32[]{:S(2)}) collective-permute-start(f32[248,128]{1,0:T(8,128)S(1)} %get-tuple-element.66), channel_id=1, source_target_pairs={{0,8},{4,12},{8,0},{12,4},{1,9},{5,13},{9,1},{13,5},{2,10},{6,14},... | collective-permute-start | bytes 380936 | tf_op jit(solution)/shard_map/ppermute | solution.py:23
  125.4 15.8 %collective-permute-start.26 = (f32[248,128]{1,0:T(8,128)S(1)}, f32[248,128]{1,0:T(8,128)S(1)}, u32[]{:S(2)}, u32[]{:S(2)}) collective-permute-start(f32[248,128]{1,0:T(8,128)S(1)} %get-tuple-element.67), channel_id=1, source_target_pairs={{0,12},{4,0},{8,4},{12,8},{1,13},{5,1},{9,5},{13,9},{2,14},{6,2},{... | collective-permute-start | bytes 380936 | tf_op jit(solution)/shard_map/ppermute | solution.py:23
  143.1 10.3 %collective-permute-start.27 = (f32[192,512]{1,0:T(8,128)S(1)}, f32[192,512]{1,0:T(8,128)S(1)}, u32[]{:S(2)}, u32[]{:S(2)}) collective-permute-start(f32[192,512]{1,0:T(8,128)S(1)} %get-tuple-element.70), channel_id=1, source_target_pairs={{0,2},{2,0},{1,3},{3,1},{4,6},{6,4},{5,7},{7,5},{8,10},{10,8},{9,1... | collective-permute-start | bytes 1179656 | tf_op jit(solution)/shard_map/ppermute | solution.py:23
  (13 other events, 85.8 us)

commit v17 on v15

--- a/solution.py
+++ b/solution.py
@@ -677,7 +677,7 @@
                 (7 + number, frozen_rows, frozen_rows, frozen_at(3, batch_step, group_step)),
                 (10 + number, 0, frozen_rows, frozen_at(2, batch_step, group_step)),
             ]
-        early = [forward, down_zeros, up_zeros, cosines, sines, bank_rows]
+        early = [forward, cosines, sines, bank_rows]
         column_blocks = pl.pallas_call(
             functools.partial(cut_kernel, len(early), seq_count),
             out_shape=[jax.ShapeDtypeStruct((rows, down_width), bf16)] * seq_count,
@@ -778,7 +778,7 @@
     block_count = len(blocks)
     column_parts[1] = shift(pass_after(column_blocks[1], *blocks[1:]), "seq", 1)
     incoming = output_gradient[0]
-    early_columns = []
+    early_columns = [down_zeros, up_zeros]
     attention, query_grad, kept, sent = pl.pallas_call(
         functools.partial(attention_kernel, block_count, len(early_columns)),
         out_shape=(

time: 155 us -> 162 us (1.045)
  waiting for transfers between devices: 65.5 us -> 72.9 us
  starting transfers between devices: 44.3 us -> 40.4 us
  local copies, waits for them, and re-layouts: 19 us -> 20.8 us
    ppermute x22, waiting for transfers between devices: 43.6 us -> 56.2 us  [shift(): lax.ppermute(value, axis, [(at, (at + steps) % count) for at in range(cou...]
    ppermute x22, starting transfers between devices: 32.2 us -> 25 us  [shift(): lax.ppermute(value, axis, [(at, (at + steps) % count) for at in range(cou...]
    ppermute x4, waiting for transfers between devices: 15.2 us -> 11.6 us  [push(): return lax.ppermute(value, axis, pairs)]
    ppermute x4, starting transfers between devices: 7.14 us -> 10.5 us  [push(): return lax.ppermute(value, axis, pairs)]
    ppermute x2, waiting for transfers between devices: 6.78 us -> 5.1 us  [over_plane(): lax.ppermute(value, ('groups', 'batch'), over_both)]
    unnamed x19 -> x29, local copies, waits for them, and re-layouts: 5.42 us -> 5.67 us
  transfers between devices with their start and end apart: 28 -> 28, of which waited for: 20 -> 21; matrix products, arithmetic and copies ran while one was open for 10% -> 10% of each run, Pallas kernels for 6% -> 6%
where the time goes in v17:
time: 162 us; the launch traced here: 160 us
  waiting for transfers between devices  72.9 us (45%)
  starting transfers between devices  40.4 us (25%)
  Pallas kernels  21.6 us (13%)
  local copies, waits for them, and re-layouts  20.8 us (13%)
  other arithmetic  2.5 us (2%)
  between operations  2.18 us (1%)
    ppermute x22, waiting for transfers between devices, shift(): lax.ppermute(value, axis, [(at, (at + steps) % count) for at in range(cou...  56.2 us
    ppermute x22, starting transfers between devices, shift(): lax.ppermute(value, axis, [(at, (at + steps) % count) for at in range(cou...  25 us
    ppermute x4, waiting for transfers between devices, push(): return lax.ppermute(value, axis, pairs)  11.6 us
    ppermute x4, starting transfers between devices, push(): return lax.ppermute(value, axis, pairs)  10.5 us
    unnamed x29, local copies, waits for them, and re-layouts  5.67 us
    ppermute x2, waiting for transfers between devices, over_plane(): lax.ppermute(value, ('groups', 'batch'), over_both)  5.1 us
    ppermute x2, starting transfers between devices, over_plane(): lax.ppermute(value, ('groups', 'batch'), over_both)  4.89 us
    pallas_call x1, Pallas kernels, shards(): pl.pallas_call(token_kernel, grid=(width // chunk,), out_shape=jax.ShapeD...  4.82 us
  transfers between devices with their start and end apart: 28, of which 21 were waited for; matrix products, arithmetic and copies ran while one was open for 10% of the time, Pallas kernels for 6%

profile of v17, /device:TPU:0, one launch (start us, length us, event | category | flops | bytes accessed | tf_op | source)
XLA Modules:
  0.0 160.5 jit_solution(6902493161572836250)
XLA Ops:
  2.6 5.0 %collective-permute-start.1 = (bf16[192,896]{1,0:T(8,128)(2,1)}, bf16[192,896]{1,0:T(8,128)(2,1)S(1)}, u32[]{:S(2)}, u32[]{:S(2)}) collective-permute-start(bf16[192,896]{1,0:T(8,128)(2,1)} %constant_dynamic-slice_fusion.1), channel_id=1, source_target_pairs={{0,12},{4,0},{8,4},{12,8},{1,13},{5,1},{9,5},{13,9},{2,14},{6,2},{... | collective-permute-start | bytes 1032200 | tf_op jit(solution)/shard_map/ppermute | solution.py:23
  9.5 3.4 %gather_fusion.1 = bf16[3,64,448]{2,1,0:T(8,128)(2,1)} fusion(bf16[64,64,448]{2,1,0:T(8,128)(2,1)} %bitcast.19, s32[1024]{0:T(1024)S(1)} %pad_clamp_fusion), kind=kCustom, calls=%fused_computation.1 | custom fusion | bytes 344076 | tf_op jit(solution)/shard_map/gather | solution.py:620
  16.1 2.7 %gather_fusion = bf16[3,64,448]{2,1,0:T(8,128)(2,1)S(1)} fusion(bf16[64,64,448]{2,1,0:T(8,128)(2,1)} %bitcast.20, s32[1024]{0:T(1024)S(1)} %pad_clamp_fusion.1), kind=kCustom, calls=%fused_computation | custom fusion | bytes 344076 | tf_op jit(solution)/shard_map/gather | solution.py:622
  20.0 3.4 %collective-permute-done.before.refs_1_ = bf16[192,896]{1,0:T(8,128)(2,1)S(1)} collective-permute-done((bf16[192,896]{1,0:T(8,128)(2,1)}, bf16[192,896]{1,0:T(8,128)(2,1)S(1)}, u32[]{:S(2)}, u32[]{:S(2)}) %collective-permute-start) | collective-permute-done | bytes 344096 | tf_op jit(solution)/shard_map/ppermute | solution.py:23
  36.7 9.4 %collective-permute-done.4.refs_0_.refs_3_ = bf16[336,896]{1,0:T(8,128)(2,1)S(1)} collective-permute-done((bf16[336,896]{1,0:T(8,128)(2,1)}, bf16[336,896]{1,0:T(8,128)(2,1)S(1)}, u32[]{:S(2)}, u32[]{:S(2)}) %collective-permute-start.4) | collective-permute-done | bytes 602144 | tf_op jit(solution)/shard_map/ppermute | solution.py:23
  46.9 8.2 %collective-permute-done.5.refs_5_ = bf16[144,896]{1,0:T(8,128)(2,1)S(1)} collective-permute-done((bf16[144,896]{1,0:T(8,128)(2,1)}, bf16[144,896]{1,0:T(8,128)(2,1)S(1)}, u32[]{:S(2)}, u32[]{:S(2)}) %collective-permute-start.5) | collective-permute-done | bytes 258080 | tf_op jit(solution)/shard_map/ppermute | solution.py:23
  62.3 2.5 %collective-permute-done.8.refs_8_ = bf16[384,896]{1,0:T(8,128)(2,1)} collective-permute-done((bf16[384,896]{1,0:T(8,128)(2,1)}, bf16[384,896]{1,0:T(8,128)(2,1)}, u32[]{:S(2)}, u32[]{:S(2)}) %collective-permute-start.8) | collective-permute-done | bytes 688160 | tf_op jit(solution)/shard_map/ppermute | solution.py:23
  66.2 5.1 %collective-permute-done.12.refs_12_ = bf16[192,896]{1,0:T(8,128)(2,1)S(1)} collective-permute-done((bf16[192,896]{1,0:T(8,128)(2,1)S(1)}, bf16[192,896]{1,0:T(8,128)(2,1)S(1)}, u32[]{:S(2)}, u32[]{:S(2)}) %collective-permute-start.12) | collective-permute-done | bytes 344096 | tf_op jit(solution)/shard_map/ppermute | solution.py:645
  71.3 5.7 %collective-permute-done.11.refs_11_ = bf16[192,896]{1,0:T(8,128)(2,1)S(1)} collective-permute-done((bf16[192,896]{1,0:T(8,128)(2,1)S(1)}, bf16[192,896]{1,0:T(8,128)(2,1)S(1)}, u32[]{:S(2)}, u32[]{:S(2)}) %collective-permute-start.11) | collective-permute-done | bytes 344096 | tf_op jit(solution)/shard_map/ppermute | solution.py:23
  77.2 3.3 %collective-permute-done.13.refs_13_.refs_2_ = bf16[256,896]{1,0:T(8,128)(2,1)S(1)} collective-permute-done((bf16[256,896]{1,0:T(8,128)(2,1)S(1)}, bf16[256,896]{1,0:T(8,128)(2,1)S(1)}, u32[]{:S(2)}, u32[]{:S(2)}) %collective-permute-start.13) | collective-permute-done | bytes 458784 | tf_op jit(solution)/shard_map/ppermute | solution.py:23
  82.4 4.7 %project.1 = (f32[256,896]{1,0:T(8,128)S(1)}, bf16[896,3584]{1,0:T(8,128)(2,1)S(1)}, bf16[3,64,640]{2,1,0:T(8,128)(2,1)S(1)}) custom-call(bf16[256,3584]{1,0:T(8,128)(2,1)S(1)} %bitcast.16, bf16[192,3584]{1,0:T(8,128)(2,1)S(1)} %copy-done.4, bf16[192,896]{1,0:T(8,128)(2,1)S(1)} %copy-done.6, bf16[192,896]{1,0:T(8,128)(2,1)S(1)} %collective-permute-done.1.after.refs_2_, ...), custom_call_target="tpu_custom_call" | custom-call | flops 1644167168 | bytes 8257536 | tf_op jit(solution)/shard_map/project/pallas_call | solution.py:739
  87.2 2.5 %collective-permute-done.14.theirs = f32[256,896]{1,0:T(8,128)S(1)} collective-permute-done((f32[256,896]{1,0:T(8,128)S(1)}, f32[256,896]{1,0:T(8,128)S(1)}, u32[]{:S(2)}, u32[]{:S(2)}) %collective-permute-start.14) | collective-permute-done | bytes 917536 | tf_op jit(solution)/shard_map/ppermute | solution.py:23
  92.2 6.5 %collective-permute-start.15 = (bf16[256,256]{1,0:T(8,128)(2,1)S(1)}, bf16[256,256]{1,0:T(8,128)(2,1)S(1)}, u32[]{:S(2)}, u32[]{:S(2)}) collective-permute-start(bf16[256,256]{1,0:T(8,128)(2,1)S(1)} %get-tuple-element.48.refs_0_), channel_id=1, source_target_pairs={{0,4},{4,8},{8,12},{1,5},{5,9},{9,13},{2,6},{6,10},{10,14},{3,7},{... | collective-permute-start | bytes 393224 | tf_op jit(solution)/shard_map/ppermute | solution.py:29
  98.7 2.7 %collective-permute-done.15.refs_1_ = bf16[256,256]{1,0:T(8,128)(2,1)S(1)} collective-permute-done((bf16[256,256]{1,0:T(8,128)(2,1)S(1)}, bf16[256,256]{1,0:T(8,128)(2,1)S(1)}, u32[]{:S(2)}, u32[]{:S(2)}) %collective-permute-start.15) | collective-permute-done | bytes 131104 | tf_op jit(solution)/shard_map/ppermute | solution.py:29
  101.5 2.5 %collective-permute-start.19 = (bf16[256,896]{1,0:T(8,128)(2,1)S(1)}, bf16[256,896]{1,0:T(8,128)(2,1)S(1)}, u32[]{:S(2)}, u32[]{:S(2)}) collective-permute-start(bf16[256,896]{1,0:T(8,128)(2,1)S(1)} %pass_after.1), channel_id=1, source_target_pairs={{0,4},{4,8},{8,12},{12,0},{1,5},{5,9},{9,13},{13,1},{2,6},{6,10},{... | collective-permute-start | bytes 1376264 | tf_op jit(solution)/shard_map/ppermute | solution.py:23
  104.1 4.5 %broadcast_in_dim.50.refs_3_.down_zeros = f32[64,64,1,448]{3,2,1,0:T(1,128)S(1)} broadcast(f32[]{:T(128)} %constant.41.clone.1), dimensions={} | broadcast | bytes 7340036 | tf_op jit(solution)/shard_map/broadcast_in_dim | solution.py:594
  108.7 3.4 %attention.1 = (bf16[128,512]{1,0:T(8,128)(2,1)}, bf16[128,512]{1,0:T(8,128)(2,1)S(1)}, f32[3,128,256]{2,1,0:T(8,128)S(1)}, f32[3,128,256]{2,1,0:T(8,128)S(1)}) custom-call(s32[2,3]{1,0:T(2,128)S(1)} %copy-done.10, bf16[512,128]{1,0:T(8,128)(2,1)S(1)} %get-tuple-element.47.queries, bf16[128,512]{1,0:T(8,128)(2,1)S(1)} %bitcast.17, ...), custom_call_target="tpu_custom_call" | custom-call | flops 503316480 | bytes 786432 | tf_op jit(solution)/shard_map/attention/pallas_call | solution.py:782
  118.8 6.1 %collective-permute-done.20.refs_1_ = f32[128,256]{1,0:T(8,128)S(1)} collective-permute-done((f32[128,256]{1,0:T(8,128)S(1)}, f32[128,256]{1,0:T(8,128)S(1)}, u32[]{:S(2)}, u32[]{:S(2)}) %collective-permute-start.20) | collective-permute-done | bytes 131104 | tf_op jit(solution)/shard_map/ppermute | solution.py:29
  124.9 2.8 %collective-permute-done.21.refs_2_ = f32[128,256]{1,0:T(8,128)S(1)} collective-permute-done((f32[128,256]{1,0:T(8,128)S(1)}, f32[128,256]{1,0:T(8,128)S(1)}, u32[]{:S(2)}, u32[]{:S(2)}) %collective-permute-start.21) | collective-permute-done | bytes 131104 | tf_op jit(solution)/shard_map/ppermute | solution.py:29
  133.5 2.8 %collective-permute-start.26 = (f32[248,128]{1,0:T(8,128)S(1)}, f32[248,128]{1,0:T(8,128)S(1)}, u32[]{:S(2)}, u32[]{:S(2)}) collective-permute-start(f32[248,128]{1,0:T(8,128)S(1)} %get-tuple-element.67), channel_id=1, source_target_pairs={{0,12},{4,0},{8,4},{12,8},{1,13},{5,1},{9,5},{13,9},{2,14},{6,2},{... | collective-permute-start | bytes 380936 | tf_op jit(solution)/shard_map/ppermute | solution.py:23
  136.4 5.0 %collective-permute-done.24.refs_5_ = f32[248,128]{1,0:T(8,128)S(1)} collective-permute-done((f32[248,128]{1,0:T(8,128)S(1)}, f32[248,128]{1,0:T(8,128)S(1)}, u32[]{:S(2)}, u32[]{:S(2)}) %collective-permute-start.24) | collective-permute-done | bytes 127008 | tf_op jit(solution)/shard_map/ppermute | solution.py:23
  141.4 6.4 %collective-permute-done.25.refs_6_ = f32[248,128]{1,0:T(8,128)S(1)} collective-permute-done((f32[248,128]{1,0:T(8,128)S(1)}, f32[248,128]{1,0:T(8,128)S(1)}, u32[]{:S(2)}, u32[]{:S(2)}) %collective-permute-start.25) | collective-permute-done | bytes 127008 | tf_op jit(solution)/shard_map/ppermute | solution.py:23
  151.2 4.8 %token_gradient.1 = bf16[256,3584]{1,0:T(8,128)(2,1)} custom-call(bf16[256,896]{1,0:T(8,128)(2,1)S(1)} %get-tuple-element.60.gradients, bf16[896,3584]{1,0:T(8,128)(2,1)S(1)} %get-tuple-element.61.matrix), custom_call_target="tpu_custom_call" | custom-call | flops 1644167168 | bytes 8257536 | tf_op jit(solution)/shard_map/token_gradient/pallas_call | solution.py:866
  157.4 3.0 %bank_rows.1 = (f32[64,64,1,448]{3,2,1,0:T(1,128)}, f32[64,32,80]{2,1,0:T(8,128)}) custom-call(s32[6]{0:T(128)S(1)} %pad_add_fusion.refs_3_.bank_rows, f32[192,448]{1,0:T(8,128)S(1)} %get-tuple-element.69.own_down, f32[192,512]{1,0:T(8,128)S(1)} %collective-permute-done.27.far, ...), custom_call_target="tpu_custom_call", output_to_operand_aliasing={{0}: (4, {}), {1}: (5, {})} | custom-call | tf_op jit(solution)/shard_map/bank_rows/pallas_call | solution.py:918
  (93 shorter events, 51.7 us)
Async XLA Ops:
  2.6 17.4 %collective-permute-start.1 = (bf16[192,896]{1,0:T(8,128)(2,1)}, bf16[192,896]{1,0:T(8,128)(2,1)S(1)}, u32[]{:S(2)}, u32[]{:S(2)}) collective-permute-start(bf16[192,896]{1,0:T(8,128)(2,1)} %constant_dynamic-slice_fusion.1), channel_id=1, source_target_pairs={{0,12},{4,0},{8,4},{12,8},{1,13},{5,1},{9,5},{13,9},{2,14},{6,2},{... | collective-permute-start | bytes 1032200 | tf_op jit(solution)/shard_map/ppermute | solution.py:23
  7.6 15.8 %collective-permute-start = (bf16[192,896]{1,0:T(8,128)(2,1)}, bf16[192,896]{1,0:T(8,128)(2,1)S(1)}, u32[]{:S(2)}, u32[]{:S(2)}) collective-permute-start(bf16[192,896]{1,0:T(8,128)(2,1)} %constant_dynamic-slice_fusion.1), channel_id=1, source_target_pairs={{0,4},{4,8},{8,12},{12,0},{1,5},{5,9},{9,13},{13,1},{2,6},{6,10},{... | collective-permute-start | bytes 1032200 | tf_op jit(solution)/shard_map/ppermute | solution.py:23
  12.9 7.1 %collective-permute-start.2 = (bf16[3,64,448]{2,1,0:T(8,128)(2,1)}, bf16[3,64,448]{2,1,0:T(8,128)(2,1)S(1)}, u32[]{:S(2)}, u32[]{:S(2)}) collective-permute-start(bf16[3,64,448]{2,1,0:T(8,128)(2,1)} %gather_fusion.1), channel_id=1, source_target_pairs={{0,2},{2,0},{1,3},{3,1},{4,6},{6,4},{5,7},{7,5},{8,10},{10,8},{9,1... | collective-permute-start | bytes 516104 | tf_op jit(solution)/shard_map/ppermute | solution.py:23
  14.9 5.0 %collective-permute-start.3 = (bf16[3,32,80]{2,1,0:T(8,128)(2,1)S(1)}, bf16[3,32,80]{2,1,0:T(8,128)(2,1)S(1)}, u32[]{:S(2)}, u32[]{:S(2)}) collective-permute-start(bf16[3,32,80]{2,1,0:T(8,128)(2,1)S(1)} %gather_fusion.3), channel_id=1, source_target_pairs={{0,2},{2,0},{1,3},{3,1},{4,6},{6,4},{5,7},{7,5},{8,10},{10,8},{9,1... | collective-permute-start | bytes 46088 | tf_op jit(solution)/shard_map/ppermute | solution.py:23
  27.5 18.6 %collective-permute-start.4 = (bf16[336,896]{1,0:T(8,128)(2,1)}, bf16[336,896]{1,0:T(8,128)(2,1)S(1)}, u32[]{:S(2)}, u32[]{:S(2)}) collective-permute-start(bf16[336,896]{1,0:T(8,128)(2,1)} %get-tuple-element.39), channel_id=1, source_target_pairs={{0,4},{4,8},{8,12},{12,0},{1,5},{5,9},{9,13},{13,1},{2,6},{6,10},{... | collective-permute-start | bytes 1806344 | tf_op jit(solution)/shard_map/ppermute | solution.py:23
  30.3 31.4 %collective-permute-start.9 = (bf16[384,896]{1,0:T(8,128)(2,1)}, bf16[384,896]{1,0:T(8,128)(2,1)}, u32[]{:S(2)}, u32[]{:S(2)}) collective-permute-start(bf16[384,896]{1,0:T(8,128)(2,1)} %copy-done.11), channel_id=1, source_target_pairs={{0,18},{2,16},{16,2},{18,0},{1,19},{3,17},{17,3},{19,1},{4,22},{6,... | collective-permute-start | bytes 2064392 | tf_op jit(solution)/shard_map/ppermute | solution.py:645
  32.8 32.0 %collective-permute-start.8 = (bf16[384,896]{1,0:T(8,128)(2,1)}, bf16[384,896]{1,0:T(8,128)(2,1)}, u32[]{:S(2)}, u32[]{:S(2)}) collective-permute-start(bf16[384,896]{1,0:T(8,128)(2,1)} %copy-done.11), channel_id=1, source_target_pairs={{0,16},{16,0},{1,17},{17,1},{2,18},{18,2},{3,19},{19,3},{4,20},{20... | collective-permute-start | bytes 2064392 | tf_op jit(solution)/shard_map/ppermute | solution.py:23
  35.4 30.8 %collective-permute-start.7 = (bf16[384,896]{1,0:T(8,128)(2,1)}, bf16[384,896]{1,0:T(8,128)(2,1)S(1)}, u32[]{:S(2)}, u32[]{:S(2)}) collective-permute-start(bf16[384,896]{1,0:T(8,128)(2,1)} %copy-done.11), channel_id=1, source_target_pairs={{0,2},{2,0},{1,3},{3,1},{4,6},{6,4},{5,7},{7,5},{8,10},{10,8},{9,1... | collective-permute-start | bytes 2064392 | tf_op jit(solution)/shard_map/ppermute | solution.py:23
  36.0 19.0 %collective-permute-start.5 = (bf16[144,896]{1,0:T(8,128)(2,1)}, bf16[144,896]{1,0:T(8,128)(2,1)S(1)}, u32[]{:S(2)}, u32[]{:S(2)}) collective-permute-start(bf16[144,896]{1,0:T(8,128)(2,1)} %copy-done.13), channel_id=1, source_target_pairs={{0,8},{4,12},{8,0},{12,4},{1,9},{5,13},{9,1},{13,5},{2,10},{6,14},... | collective-permute-start | bytes 774152 | tf_op jit(solution)/shard_map/ppermute | solution.py:23
  46.1 13.2 %collective-permute-start.6 = (bf16[144,896]{1,0:T(8,128)(2,1)}, bf16[144,896]{1,0:T(8,128)(2,1)S(1)}, u32[]{:S(2)}, u32[]{:S(2)}) collective-permute-start(bf16[144,896]{1,0:T(8,128)(2,1)} %copy-done.12), channel_id=1, source_target_pairs={{0,12},{4,0},{8,4},{12,8},{1,13},{5,1},{9,5},{13,9},{2,14},{6,2},{... | collective-permute-start | bytes 774152 | tf_op jit(solution)/shard_map/ppermute | solution.py:23
  55.1 25.4 %collective-permute-start.13 = (bf16[256,896]{1,0:T(8,128)(2,1)S(1)}, bf16[256,896]{1,0:T(8,128)(2,1)S(1)}, u32[]{:S(2)}, u32[]{:S(2)}) collective-permute-start(bf16[256,896]{1,0:T(8,128)(2,1)S(1)} %get-tuple-element.44), channel_id=1, source_target_pairs={{0,8},{4,12},{8,0},{12,4},{1,9},{5,13},{9,1},{13,5},{2,10},{6,14},... | collective-permute-start | bytes 1376264 | tf_op jit(solution)/shard_map/ppermute | solution.py:23
  59.3 12.0 %collective-permute-start.12 = (bf16[192,896]{1,0:T(8,128)(2,1)S(1)}, bf16[192,896]{1,0:T(8,128)(2,1)S(1)}, u32[]{:S(2)}, u32[]{:S(2)}) collective-permute-start(bf16[192,896]{1,0:T(8,128)(2,1)S(1)} %slice.32), channel_id=1, source_target_pairs={{0,18},{2,16},{16,2},{18,0},{1,19},{3,17},{17,3},{19,1},{4,22},{6,... | collective-permute-start | bytes 1032200 | tf_op jit(solution)/shard_map/ppermute | solution.py:645
  61.8 15.2 %collective-permute-start.11 = (bf16[192,896]{1,0:T(8,128)(2,1)S(1)}, bf16[192,896]{1,0:T(8,128)(2,1)S(1)}, u32[]{:S(2)}, u32[]{:S(2)}) collective-permute-start(bf16[192,896]{1,0:T(8,128)(2,1)S(1)} %slice.32), channel_id=1, source_target_pairs={{0,16},{16,0},{1,17},{17,1},{2,18},{18,2},{3,19},{19,3},{4,20},{20... | collective-permute-start | bytes 1032200 | tf_op jit(solution)/shard_map/ppermute | solution.py:23
  64.8 12.4 %collective-permute-start.10 = (bf16[192,896]{1,0:T(8,128)(2,1)S(1)}, bf16[192,896]{1,0:T(8,128)(2,1)S(1)}, u32[]{:S(2)}, u32[]{:S(2)}) collective-permute-start(bf16[192,896]{1,0:T(8,128)(2,1)S(1)} %slice.32), channel_id=1, source_target_pairs={{0,2},{2,0},{1,3},{3,1},{4,6},{6,4},{5,7},{7,5},{8,10},{10,8},{9,1... | collective-permute-start | bytes 1032200 | tf_op jit(solution)/shard_map/ppermute | solution.py:23
  90.8 8.0 %collective-permute-start.16 = (bf16[256,256]{1,0:T(8,128)(2,1)S(1)}, bf16[256,256]{1,0:T(8,128)(2,1)S(1)}, u32[]{:S(2)}, u32[]{:S(2)}) collective-permute-start(bf16[256,256]{1,0:T(8,128)(2,1)S(1)} %get-tuple-element.48.refs_0_), channel_id=1, source_target_pairs={{0,8},{4,12},{1,9},{5,13},{2,10},{6,14},{3,11},{7,15},{16,24},{20,... | collective-permute-start | bytes 393224 | tf_op jit(solution)/shard_map/ppermute | solution.py:29
  92.2 9.2 %collective-permute-start.15 = (bf16[256,256]{1,0:T(8,128)(2,1)S(1)}, bf16[256,256]{1,0:T(8,128)(2,1)S(1)}, u32[]{:S(2)}, u32[]{:S(2)}) collective-permute-start(bf16[256,256]{1,0:T(8,128)(2,1)S(1)} %get-tuple-element.48.refs_0_), channel_id=1, source_target_pairs={{0,4},{4,8},{8,12},{1,5},{5,9},{9,13},{2,6},{6,10},{10,14},{3,7},{... | collective-permute-start | bytes 393224 | tf_op jit(solution)/shard_map/ppermute | solution.py:29
  101.5 14.7 %collective-permute-start.19 = (bf16[256,896]{1,0:T(8,128)(2,1)S(1)}, bf16[256,896]{1,0:T(8,128)(2,1)S(1)}, u32[]{:S(2)}, u32[]{:S(2)}) collective-permute-start(bf16[256,896]{1,0:T(8,128)(2,1)S(1)} %pass_after.1), channel_id=1, source_target_pairs={{0,4},{4,8},{8,12},{12,0},{1,5},{5,9},{9,13},{13,1},{2,6},{6,10},{... | collective-permute-start | bytes 1376264 | tf_op jit(solution)/shard_map/ppermute | solution.py:23
  116.2 8.7 %collective-permute-start.20 = (f32[128,256]{1,0:T(8,128)S(1)}, f32[128,256]{1,0:T(8,128)S(1)}, u32[]{:S(2)}, u32[]{:S(2)}) collective-permute-start(f32[128,256]{1,0:T(8,128)S(1)} %get-tuple-element.55), channel_id=1, source_target_pairs={{4,0},{8,4},{12,8},{5,1},{9,5},{13,9},{6,2},{10,6},{14,10},{7,3},{... | collective-permute-start | bytes 393224 | tf_op jit(solution)/shard_map/ppermute | solution.py:29
  117.5 10.2 %collective-permute-start.21 = (f32[128,256]{1,0:T(8,128)S(1)}, f32[128,256]{1,0:T(8,128)S(1)}, u32[]{:S(2)}, u32[]{:S(2)}) collective-permute-start(f32[128,256]{1,0:T(8,128)S(1)} %get-tuple-element.56), channel_id=1, source_target_pairs={{8,0},{12,4},{9,1},{13,5},{10,2},{14,6},{11,3},{15,7},{24,16},{28,... | collective-permute-start | bytes 393224 | tf_op jit(solution)/shard_map/ppermute | solution.py:29
  127.8 19.9 %collective-permute-start.23 = (bf16[256,896]{1,0:T(8,128)(2,1)S(1)}, bf16[256,896]{1,0:T(8,128)(2,1)S(1)}, u32[]{:S(2)}, u32[]{:S(2)}) collective-permute-start(bf16[256,896]{1,0:T(8,128)(2,1)S(1)} %get-tuple-element.63), channel_id=1, source_target_pairs={{0,12},{4,0},{8,4},{12,8},{1,13},{5,1},{9,5},{13,9},{2,14},{6,2},{... | collective-permute-start | bytes 1376264 | tf_op jit(solution)/shard_map/ppermute | solution.py:23
  130.9 10.4 %collective-permute-start.24 = (f32[248,128]{1,0:T(8,128)S(1)}, f32[248,128]{1,0:T(8,128)S(1)}, u32[]{:S(2)}, u32[]{:S(2)}) collective-permute-start(f32[248,128]{1,0:T(8,128)S(1)} %get-tuple-element.65), channel_id=1, source_target_pairs={{0,4},{4,8},{8,12},{12,0},{1,5},{5,9},{9,13},{13,1},{2,6},{6,10},{... | collective-permute-start | bytes 380936 | tf_op jit(solution)/shard_map/ppermute | solution.py:23
  132.7 15.0 %collective-permute-start.25 = (f32[248,128]{1,0:T(8,128)S(1)}, f32[248,128]{1,0:T(8,128)S(1)}, u32[]{:S(2)}, u32[]{:S(2)}) collective-permute-start(f32[248,128]{1,0:T(8,128)S(1)} %get-tuple-element.66), channel_id=1, source_target_pairs={{0,8},{4,12},{8,0},{12,4},{1,9},{5,13},{9,1},{13,5},{2,10},{6,14},... | collective-permute-start | bytes 380936 | tf_op jit(solution)/shard_map/ppermute | solution.py:23
  133.5 14.2 %collective-permute-start.26 = (f32[248,128]{1,0:T(8,128)S(1)}, f32[248,128]{1,0:T(8,128)S(1)}, u32[]{:S(2)}, u32[]{:S(2)}) collective-permute-start(f32[248,128]{1,0:T(8,128)S(1)} %get-tuple-element.67), channel_id=1, source_target_pairs={{0,12},{4,0},{8,4},{12,8},{1,13},{5,1},{9,5},{13,9},{2,14},{6,2},{... | collective-permute-start | bytes 380936 | tf_op jit(solution)/shard_map/ppermute | solution.py:23
  149.6 7.8 %collective-permute-start.27 = (f32[192,512]{1,0:T(8,128)S(1)}, f32[192,512]{1,0:T(8,128)S(1)}, u32[]{:S(2)}, u32[]{:S(2)}) collective-permute-start(f32[192,512]{1,0:T(8,128)S(1)} %get-tuple-element.70), channel_id=1, source_target_pairs={{0,2},{2,0},{1,3},{3,1},{4,6},{6,4},{5,7},{7,5},{8,10},{10,8},{9,1... | collective-permute-start | bytes 1179656 | tf_op jit(solution)/shard_map/ppermute | solution.py:23
  (18 other events, 138.5 us)
